TPU v7x, 32 devices: a whole 2x2x4 slice. The times are simulated.
32 devices in a mesh: dp: 4 (over y, x), ctx: 8 (over z, core).
Axes of the slice: x: 2, y: 2, z: 4, core: 2. Of those that a mesh axis runs over, the one named last changes fastest.
Arguments:
- hyena_q: bfloat16 [4096, 4096], P(('dp', 'ctx')), parts along dimension 0, may hold values from -6 to 6
- hyena_k: bfloat16 [4096, 4096], P(('dp', 'ctx')), parts along dimension 0, may hold values from -6 to 6
- hyena_v: bfloat16 [4096, 4096], P(('dp', 'ctx')), parts along dimension 0, may hold values from -6 to 6
- short_filter: float32 [3, 3, 4096], replicated, may hold values from -3.5 to 3.5
- residue: float32 [4096, 16], P('ctx'), may hold values from -0.09375 to 0.09375
- decay_rate: float32 [4096, 16], P('ctx'), may hold values from 0.00024414062 to 0.034
- att_query: bfloat16 [4096, 4096], P(('dp', 'ctx')), parts along dimension 0, may hold values from -32 to 32
- att_key: bfloat16 [4096, 4096], P(('dp', 'ctx')), parts along dimension 0, may hold values from -6 to 6
- att_value: bfloat16 [4096, 4096], P(('dp', 'ctx')), parts along dimension 0, may hold values from -6 to 6
Outputs:
- hyena_out: bfloat16 [4096, 4096], P(('dp', 'ctx')), parts along dimension 0
- att_out: bfloat16 [4096, 4096], P(('dp', 'ctx')), parts along dimension 0
There are 4 independent parts, one for each index of `dp`. A program takes and returns all parts, laid end to end along the dimension named above; an argument that names none is the same for every part. Nothing has to cross between parts.
All inputs are finite; a program needn't handle non-finite values.
Results may differ from a plain program's by a relative error of at most 0.0058.
Values may be sent and summed in bfloat16 or wider, within the bound.
No kernel may reach another device: no remote copies, remote signals or barrier semaphores. Data moves between devices by JAX's collectives and lax.ppermute only.
A program may use at most 128 MiB of HBM per device.

v0:
```python
import math

import jax
import jax.numpy as jnp
from jax import lax
from jax.sharding import PartitionSpec as P

HEAD_DIM = 128


HIGHEST = lax.Precision.HIGHEST


def causal_taps(rim_rows, feature, tap_weights):
    values = feature.astype(jnp.float32)
    padded = jnp.concatenate([rim_rows, values], 0)
    length = values.shape[0]
    taps_count = tap_weights.shape[0]
    result = tap_weights[0] * padded[taps_count - 1 : taps_count - 1 + length]
    for offset in range(1, taps_count):
        result = (
            result
            + tap_weights[offset]
            * padded[taps_count - 1 - offset : taps_count - 1 - offset + length]
        )
    return result


def dft_tables(first_size, second_size):
    total_size = first_size * second_size
    outer = jnp.arange(first_size, dtype=jnp.int32)
    inner = jnp.arange(first_size // 2, dtype=jnp.int32)
    later = jnp.arange(second_size, dtype=jnp.int32)
    angle_one = (outer[:, None] * inner[None, :] % first_size).astype(jnp.float32) * (
        2.0 * math.pi / first_size
    )
    angle_two = (later[:, None] * later[None, :] % second_size).astype(jnp.float32) * (
        2.0 * math.pi / second_size
    )
    angle_twist = (outer[:, None] * later[None, :] % total_size).astype(jnp.float32) * (
        2.0 * math.pi / total_size
    )
    return (
        jnp.cos(angle_one),
        jnp.sin(angle_one),
        jnp.cos(angle_two),
        jnp.sin(angle_two),
        jnp.cos(angle_twist)[:, :, None],
        jnp.sin(angle_twist)[:, :, None],
    )


def forward_dft(signal, tables):
    cos_one, sin_one, cos_two, sin_two, cos_twist, sin_twist = tables
    part_re = jnp.einsum("kn,nmc->kmc", cos_one, signal, precision=HIGHEST)
    part_im = -jnp.einsum("kn,nmc->kmc", sin_one, signal, precision=HIGHEST)
    turned_re = part_re * cos_twist + part_im * sin_twist
    turned_im = part_im * cos_twist - part_re * sin_twist
    spec_re = jnp.einsum("kmc,mj->kjc", turned_re, cos_two, precision=HIGHEST) + jnp.einsum(
        "kmc,mj->kjc", turned_im, sin_two, precision=HIGHEST
    )
    spec_im = jnp.einsum("kmc,mj->kjc", turned_im, cos_two, precision=HIGHEST) - jnp.einsum(
        "kmc,mj->kjc", turned_re, sin_two, precision=HIGHEST
    )
    return (spec_re, spec_im)


def inverse_dft(spec_re, spec_im, tables, total_size):
    cos_one, sin_one, cos_two, sin_two, cos_twist, sin_twist = tables
    back_re = jnp.einsum("kjc,jm->kmc", spec_re, cos_two, precision=HIGHEST) - jnp.einsum(
        "kjc,jm->kmc", spec_im, sin_two, precision=HIGHEST
    )
    back_im = jnp.einsum("kjc,jm->kmc", spec_im, cos_two, precision=HIGHEST) + jnp.einsum(
        "kjc,jm->kmc", spec_re, sin_two, precision=HIGHEST
    )
    twist_re = back_re * cos_twist - back_im * sin_twist
    twist_im = back_im * cos_twist + back_re * sin_twist
    result = jnp.einsum("kn,kmc->nmc", cos_one, twist_re, precision=HIGHEST) - jnp.einsum(
        "kn,kmc->nmc", sin_one, twist_im, precision=HIGHEST
    )
    return result / total_size


def long_conv(product, residue, decay_rate):
    length, channels = product.shape
    block_width = min(128, channels)
    block_count = channels // block_width
    total_size = 2 * length
    low_bits = (total_size & -total_size).bit_length() - 1
    first_size = 2 ** (low_bits // 2)
    second_size = total_size // first_size
    half_first = first_size // 2
    tables = dft_tables(first_size, second_size)
    time_index = jnp.arange(length, dtype=jnp.float32)[:, None]

    def one_block(items):
        piece_in, residue_piece, rate_piece = items
        kernel = jnp.zeros((length, block_width), jnp.float32)
        for mode_index in range(residue_piece.shape[1]):
            kernel = kernel + residue_piece[:, mode_index] * jnp.exp(
                -rate_piece[:, mode_index] * time_index
            )
        signal = piece_in.astype(jnp.float32).reshape(half_first, second_size, block_width)
        signal_re, signal_im = forward_dft(signal, tables)
        kernel_re, kernel_im = forward_dft(
            kernel.reshape(half_first, second_size, block_width), tables
        )
        joint_re = signal_re * kernel_re - signal_im * kernel_im
        joint_im = signal_re * kernel_im + signal_im * kernel_re
        return inverse_dft(joint_re, joint_im, tables, total_size).reshape(length, block_width)

    blocks_in = product.reshape(length, block_count, block_width).transpose(1, 0, 2)
    residue_blocks = residue.reshape(block_count, block_width, residue.shape[1])
    rate_blocks = decay_rate.reshape(block_count, block_width, decay_rate.shape[1])
    results = lax.map(one_block, (blocks_in, residue_blocks, rate_blocks))
    return results.transpose(1, 0, 2).reshape(length, channels)


def attend(pieces):
    length = pieces[0].shape[0]
    head_count = pieces[0].shape[2]
    head_width = pieces[0].shape[3]
    query_all = pieces[0].reshape(length, head_count, head_width)
    key_all = pieces[1].reshape(length, head_count, head_width)
    value_all = pieces[2].reshape(length, head_count, head_width)
    block_rows = min(length, max(512, length // 8))
    score_scale = head_width ** (-0.5)
    out_blocks = []
    for block_index in range(length // block_rows):
        start_row = block_index * block_rows
        key_end = start_row + block_rows
        query_block = query_all[start_row:key_end]
        scores = (
            jnp.einsum(
                "qhd,khd->hqk", query_block, key_all[:key_end], preferred_element_type=jnp.float32
            )
            * score_scale
        )
        query_pos = start_row + jnp.arange(block_rows, dtype=jnp.int32)[:, None]
        key_pos = jnp.arange(key_end, dtype=jnp.int32)[None, :]
        scores = jnp.where((key_pos <= query_pos)[None, :, :], scores, -jnp.inf)
        row_max = jnp.max(scores, axis=2, keepdims=True)
        expo_scores = jnp.exp(scores - row_max)
        denominator = jnp.sum(expo_scores, axis=2)
        weights = expo_scores.astype(jnp.bfloat16)
        mixed_out = jnp.einsum(
            "hqk,khd->qhd", weights, value_all[:key_end], preferred_element_type=jnp.float32
        )
        mixed_out = mixed_out / denominator.T[:, :, None]
        out_blocks.append(mixed_out.astype(jnp.bfloat16))
    attended = jnp.concatenate(out_blocks, 0).reshape(length, 1, head_count, head_width)
    return lax.all_to_all(attended, "ctx", split_axis=0, concat_axis=1, tiled=True)


def local(
    hyena_q, hyena_k, hyena_v, short_filter, residue, decay_rate, att_query, att_key, att_value
):
    seq_rows = hyena_q.shape[0]
    devices = lax.axis_size("ctx")
    channels = hyena_q.shape[1] // devices
    rim_count = short_filter.shape[1] - 1
    relaid = (
        lax.all_to_all(hyena_q, "ctx", split_axis=1, concat_axis=0, tiled=True),
        lax.all_to_all(hyena_k, "ctx", split_axis=1, concat_axis=0, tiled=True),
        lax.all_to_all(hyena_v, "ctx", split_axis=1, concat_axis=0, tiled=True),
    )
    offset = lax.axis_index("ctx") * channels
    local_taps = lax.dynamic_slice_in_dim(short_filter, offset, channels, 2)
    zero_rim = jnp.zeros((rim_count, channels), jnp.float32)
    query_mix = causal_taps(zero_rim, relaid[0], local_taps[0])
    key_mix = causal_taps(zero_rim, relaid[1], local_taps[1])
    value_mix = causal_taps(zero_rim, relaid[2], local_taps[2])
    product = lax.optimization_barrier((key_mix * value_mix).astype(jnp.bfloat16))
    smoothed = lax.optimization_barrier(
        long_conv(product, residue, decay_rate).astype(jnp.bfloat16)
    )
    outgoing = (query_mix * smoothed.astype(jnp.float32)).astype(jnp.bfloat16)
    returned = lax.all_to_all(outgoing, "ctx", split_axis=0, concat_axis=1, tiled=True)
    head_groups = att_query.shape[1] // (devices * HEAD_DIM)
    query_four = att_query.reshape(seq_rows, devices, head_groups, HEAD_DIM)
    key_four = att_key.reshape(seq_rows, devices, head_groups, HEAD_DIM)
    value_four = att_value.reshape(seq_rows, devices, head_groups, HEAD_DIM)
    attended = attend(
        (
            lax.all_to_all(query_four, "ctx", split_axis=1, concat_axis=0, tiled=True),
            lax.all_to_all(key_four, "ctx", split_axis=1, concat_axis=0, tiled=True),
            lax.all_to_all(value_four, "ctx", split_axis=1, concat_axis=0, tiled=True),
        )
    )
    att_out = attended.reshape(seq_rows, att_query.shape[1])
    return (returned, att_out)


def solution(mesh):
    placed = (
        P(("dp", "ctx"), None),
        P(("dp", "ctx"), None),
        P(("dp", "ctx"), None),
        P(),
        P("ctx", None),
        P("ctx", None),
        P(("dp", "ctx"), None),
        P(("dp", "ctx"), None),
        P(("dp", "ctx"), None),
    )
    return jax.shard_map(
        local,
        mesh=mesh,
        in_specs=placed,
        out_specs=(P(("dp", "ctx"), None), P(("dp", "ctx"), None)),
        check_vma=False,
    )
```

profile of v0, /device:TPU:0, one launch (start us, length us, event | category | flops | bytes accessed | tf_op | source)
XLA Modules:
  0.0 393.7 jit_solution(4542768714001126562)
XLA Ops:
  0.6 2.4 copy.149
  3.0 6.3 %all-to-all-start.2 = ((bf16[128,8,512]{0,2,1:T(8,128)(2,1)}), bf16[128,8,512]{0,2,1:T(8,128)(2,1)S(1)}, u32[]{:S(2)}, u32[]{:S(2)}) async-start(bf16[128,8,512]{0,2,1:T(8,128)(2,1)} %bitcast.13), calls=%async_computation.2 | async-start | bytes 2097152 | tf_op jit(solution)/shard_map/all_to_all | solution.py:165
  10.6 25.3 %all-to-all-done.2 = bf16[128,8,512]{0,2,1:T(8,128)(2,1)S(1)} async-done(((bf16[128,8,512]{0,2,1:T(8,128)(2,1)}), bf16[128,8,512]{0,2,1:T(8,128)(2,1)S(1)}, u32[]{:S(2)}, u32[]{:S(2)}) %all-to-all-start.2) | async-done | bytes 1048608 | tf_op jit(solution)/shard_map/all_to_all | solution.py:165
  35.9 3.6 all-to-all-start.1
  40.8 25.2 %all-to-all-done.1 = bf16[128,8,512]{0,2,1:T(8,128)(2,1)S(1)} async-done(((bf16[128,8,512]{0,2,1:T(8,128)(2,1)}), bf16[128,8,512]{0,2,1:T(8,128)(2,1)S(1)}, u32[]{:S(2)}, u32[]{:S(2)}) %all-to-all-start.1) | async-done | bytes 1048608 | tf_op jit(solution)/shard_map/all_to_all | solution.py:164
  67.0 3.6 all-to-all-start
  73.5 23.6 %all-to-all-done = bf16[128,8,512]{0,2,1:T(8,128)(2,1)S(1)} async-done(((bf16[128,8,512]{0,2,1:T(8,128)(2,1)}), bf16[128,8,512]{0,2,1:T(8,128)(2,1)S(1)}, u32[]{:S(2)}, u32[]{:S(2)}) %all-to-all-start) | async-done | bytes 1048608 | tf_op jit(solution)/shard_map/all_to_all | solution.py:163
  97.0 3.6 all-to-all-start.4
  100.6 2.3 copy.161
  102.9 2.3 copy.162
  105.2 21.9 %all-to-all-done.4 = bf16[128,8,4,128]{3,0,2,1:T(8,128)(2,1)S(1)} async-done(((bf16[128,8,4,128]{3,0,2,1:T(8,128)(2,1)}), bf16[128,8,4,128]{3,0,2,1:T(8,128)(2,1)S(1)}, u32[]{:S(2)}, u32[]{:S(2)}) %all-to-all-start.4) | async-done | bytes 1048608 | tf_op jit(solution)/shard_map/all_to_all | solution.py:185
  128.1 3.6 all-to-all-start.5
  139.0 1.9 copy.150
  140.9 2.7 convert_bitcast_fusion.1
  143.7 2.9 copy.148
  146.6 5.2 %multiply_convert_fusion.1 = bf16[1024,512]{1,0:T(8,128)(2,1)} fusion(f32[1024,512]{1,0:T(8,128)S(1)} %bitcast.295, f32[1024,512]{1,0:T(8,128)} %bitcast.296, f32[512]{0:T(512)S(1)} %bitcast.326, f32[512]{0:T(512)S(1)} %bitcast.321, f32[512]{0:T(512)S(1)} %bitcast.322, f32[512]{0:T(512)S(1)} %bitcast.323, f32[512]{0:T(512)S(1)} %bitcast.324, ...), kind=kLoop, calls=%fused_computation.251 | loop fusion | flops 6291456 | bytes 5255168 | tf_op jit(solution)/shard_map/convert_element_type | solution.py:173
  153.2 4.9 %all-to-all-done.5 = bf16[128,8,4,128]{3,0,2,1:T(8,128)(2,1)S(1)} async-done(((bf16[128,8,4,128]{3,0,2,1:T(8,128)(2,1)}), bf16[128,8,4,128]{3,0,2,1:T(8,128)(2,1)S(1)}, u32[]{:S(2)}, u32[]{:S(2)}) %all-to-all-start.5) | async-done | bytes 1048608 | tf_op jit(solution)/shard_map/all_to_all | solution.py:186
  158.2 4.3 %all-to-all-start.6 = ((bf16[128,8,4,128]{3,0,2,1:T(8,128)(2,1)}), bf16[128,8,4,128]{3,0,2,1:T(8,128)(2,1)}, u32[]{:S(2)}, u32[]{:S(2)}) async-start(bf16[128,8,4,128]{3,0,2,1:T(8,128)(2,1)} %copy.165), calls=%async_computation.6 | async-start | bytes 2097152 | tf_op jit(solution)/shard_map/all_to_all | solution.py:187
  162.4 153.6 %while.12 = (s32[]{:T(128)}, bf16[4,1024,128]{1,2,0:T(8,128)(2,1)}, bf16[4,1024,128]{1,2,0:T(8,128)(2,1)S(1)}, f32[4,128,16]{1,0,2:T(4,128)S(1)}, f32[4,128,16]{1,0,2:T(4,128)S(1)}, /*index=5*/s32[]{:T(128)}) while((s32[]{:T(128)}, bf16[4,1024,128]{1,2,0:T(8,128)(2,1)}, bf16[4,1024,128]{1,2,0:T(8,128)(2,1)S(1)}, ...), condition=%wide.region_1.2_spmd.clone.clone, body=%wide.region_0.1_spmd.clone.clone.sunk | while | flops 2739775488 | bytes 67572384 | solution.py:115
  182.1 3.3 fusion.301
  187.2 2.7 multiply_subtract_fusion.5
  195.2 1.8 convolution_add_fusion.6
  198.8 1.8 convolution_subtract_fusion.5
  202.3 2.1 multiply_subtract_fusion.6
  213.5 3.3 fusion.301
  218.6 2.7 multiply_subtract_fusion.5
  223.0 1.8 convolution_add_fusion.7
  226.6 1.8 convolution_add_fusion.6
  230.2 1.8 convolution_subtract_fusion.5
  233.7 2.1 multiply_subtract_fusion.6
  244.9 3.3 fusion.301
  250.0 2.7 multiply_subtract_fusion.5
  258.0 1.8 convolution_add_fusion.6
  265.1 2.1 multiply_subtract_fusion.6
  276.3 3.3 fusion.301
  281.4 2.7 multiply_subtract_fusion.5
  285.8 1.8 convolution_add_fusion.7
  293.0 1.8 convolution_subtract_fusion.5
  296.6 2.1 multiply_subtract_fusion.6
  316.1 2.0 slice.306
  322.3 1.9 copy.146
  324.3 2.2 fusion.216
  329.9 4.9 %all-to-all-start.3 = ((bf16[8,128,512]{2,1,0:T(8,128)(2,1)}), bf16[8,128,512]{2,1,0:T(8,128)(2,1)S(1)}, u32[]{:S(2)}, u32[]{:S(2)}) async-start(bf16[8,128,512]{2,1,0:T(8,128)(2,1)} %bitcast.301), calls=%async_computation.3 | async-start | bytes 2097152 | tf_op jit(solution)/shard_map/all_to_all | solution.py:178
  342.4 2.3 fusion.188
  344.7 2.5 divide_convert_fusion
  349.1 12.3 %all-to-all-done.3 = bf16[8,128,512]{2,1,0:T(8,128)(2,1)S(1)} async-done(((bf16[8,128,512]{2,1,0:T(8,128)(2,1)}), bf16[8,128,512]{2,1,0:T(8,128)(2,1)S(1)}, u32[]{:S(2)}, u32[]{:S(2)}) %all-to-all-start.3) | async-done | bytes 1048608 | tf_op jit(solution)/shard_map/all_to_all | solution.py:178
  361.4 3.6 all-to-all-start.7
  367.0 24.5 %all-to-all-done.7 = bf16[1024,1,4,128]{3,2,1,0:T(4,128)(2,1)S(1)} async-done(((bf16[1024,1,4,128]{3,2,1,0:T(4,128)(2,1)}), bf16[1024,1,4,128]{3,2,1,0:T(4,128)(2,1)S(1)}, u32[]{:S(2)}, u32[]{:S(2)}) %all-to-all-start.7) | async-done | bytes 1048608 | tf_op jit(solution)/shard_map/all_to_all | solution.py:152
  (202 shorter events, 114.9 us)
Async XLA Ops:
  0.6 8.7 %copy-start.13 = (bf16[128,4096]{1,0:T(8,128)(2,1)S(1)}, bf16[128,4096]{1,0:T(8,128)(2,1)}, u32[]{:S(2)}) copy-start(bf16[128,4096]{1,0:T(8,128)(2,1)} %param.12) | copy-start | bytes 3145732
  3.0 32.9 %all-to-all-start.2 = ((bf16[128,8,512]{0,2,1:T(8,128)(2,1)}), bf16[128,8,512]{0,2,1:T(8,128)(2,1)S(1)}, u32[]{:S(2)}, u32[]{:S(2)}) async-start(bf16[128,8,512]{0,2,1:T(8,128)(2,1)} %bitcast.13), calls=%async_computation.2 | async-start | bytes 2097152 | tf_op jit(solution)/shard_map/all_to_all | solution.py:165
  9.3 30.2 %copy-start.14 = (bf16[128,4096]{1,0:T(8,128)(2,1)S(1)}, bf16[128,4096]{1,0:T(8,128)(2,1)}, u32[]{:S(2)}) copy-start(bf16[128,4096]{1,0:T(8,128)(2,1)} %param.11) | copy-start | bytes 3145732
  35.9 30.1 %all-to-all-start.1 = ((bf16[128,8,512]{0,2,1:T(8,128)(2,1)}), bf16[128,8,512]{0,2,1:T(8,128)(2,1)S(1)}, u32[]{:S(2)}, u32[]{:S(2)}) async-start(bf16[128,8,512]{0,2,1:T(8,128)(2,1)} %bitcast.7), calls=%async_computation.1 | async-start | bytes 2097152 | tf_op jit(solution)/shard_map/all_to_all | solution.py:164
  66.0 1.0 copy-start.6
  67.0 30.1 %all-to-all-start = ((bf16[128,8,512]{0,2,1:T(8,128)(2,1)}), bf16[128,8,512]{0,2,1:T(8,128)(2,1)S(1)}, u32[]{:S(2)}, u32[]{:S(2)}) async-start(bf16[128,8,512]{0,2,1:T(8,128)(2,1)} %bitcast.1), calls=%async_computation | async-start | bytes 2097152 | tf_op jit(solution)/shard_map/all_to_all | solution.py:163
  97.0 5.8 %copy-start.4 = (bf16[128,8,512]{0,2,1:T(8,128)(2,1)}, bf16[128,8,512]{0,2,1:T(8,128)(2,1)S(1)}, u32[]{:S(2)}) copy-start(bf16[128,8,512]{0,2,1:T(8,128)(2,1)S(1)} %all-to-all-done) | copy-start | bytes 3145732
  97.0 30.1 %all-to-all-start.4 = ((bf16[128,8,4,128]{3,0,2,1:T(8,128)(2,1)}), bf16[128,8,4,128]{3,0,2,1:T(8,128)(2,1)S(1)}, u32[]{:S(2)}, u32[]{:S(2)}) async-start(bf16[128,8,4,128]{3,0,2,1:T(8,128)(2,1)} %copy.159), calls=%async_computation.4 | async-start | bytes 2097152 | tf_op jit(solution)/shard_map/all_to_all | solution.py:185
  102.9 28.8 %copy-start.16 = (f32[512,16]{0,1:T(8,128)S(1)}, f32[512,16]{0,1:T(8,128)}, u32[]{:S(2)}) copy-start(f32[512,16]{0,1:T(8,128)} %param.15) | copy-start | bytes 98308
  102.9 28.8 %copy-start.17 = (f32[512,16]{0,1:T(8,128)S(1)}, f32[512,16]{0,1:T(8,128)}, u32[]{:S(2)}) copy-start(f32[512,16]{0,1:T(8,128)} %param.16) | copy-start | bytes 98308
  127.1 1.0 copy-start.8
  128.1 30.1 %all-to-all-start.5 = ((bf16[128,8,4,128]{3,0,2,1:T(8,128)(2,1)}), bf16[128,8,4,128]{3,0,2,1:T(8,128)(2,1)S(1)}, u32[]{:S(2)}, u32[]{:S(2)}) async-start(bf16[128,8,4,128]{3,0,2,1:T(8,128)(2,1)} %copy.162), calls=%async_computation.5 | async-start | bytes 2097152 | tf_op jit(solution)/shard_map/all_to_all | solution.py:186
  158.2 4.3 %copy-start = (bf16[128,8,4,128]{3,0,2,1:T(8,128)(2,1)}, bf16[128,8,4,128]{3,0,2,1:T(8,128)(2,1)S(1)}, u32[]{:S(2)}) copy-start(bf16[128,8,4,128]{3,0,2,1:T(8,128)(2,1)S(1)} %all-to-all-done.5) | copy-start | bytes 3145732
  158.2 171.8 %all-to-all-start.6 = ((bf16[128,8,4,128]{3,0,2,1:T(8,128)(2,1)}), bf16[128,8,4,128]{3,0,2,1:T(8,128)(2,1)}, u32[]{:S(2)}, u32[]{:S(2)}) async-start(bf16[128,8,4,128]{3,0,2,1:T(8,128)(2,1)} %copy.165), calls=%async_computation.6 | async-start | bytes 2097152 | tf_op jit(solution)/shard_map/all_to_all | solution.py:187
  181.9 3.5 copy-start.1
  185.4 1.7 copy-start.21
  211.1 2.3 copy-start.2
  213.3 3.5 copy-start.1
  216.8 1.7 copy-start.21
  242.5 2.3 copy-start.2
  244.7 3.5 copy-start.1
  248.2 1.7 copy-start.21
  273.9 2.3 copy-start.2
  276.1 3.5 copy-start.1
  279.6 1.7 copy-start.21
  305.3 2.3 copy-start.2
  316.1 3.4 copy-start.15
  318.1 2.7 copy-start.5
  324.2 3.1 copy-start.9
  324.3 3.9 copy-start.7
  324.3 3.9 copy-start.18
  324.3 3.9 copy-start.19
  324.3 3.9 copy-start.20
  329.9 6.1 %copy-start.10 = (bf16[4,128,1,4,128]{4,1,3,0,2:T(8,128)(2,1)S(1)}, bf16[4,128,1,4,128]{4,1,3,0,2:T(8,128)(2,1)}, u32[]{:S(2)}) copy-start(bf16[4,128,1,4,128]{4,1,3,0,2:T(8,128)(2,1)} %get-tuple-element.361) | copy-start | bytes 1572868
  329.9 31.5 %all-to-all-start.3 = ((bf16[8,128,512]{2,1,0:T(8,128)(2,1)}), bf16[8,128,512]{2,1,0:T(8,128)(2,1)S(1)}, u32[]{:S(2)}, u32[]{:S(2)}) async-start(bf16[8,128,512]{2,1,0:T(8,128)(2,1)} %bitcast.301), calls=%async_computation.3 | async-start | bytes 2097152 | tf_op jit(solution)/shard_map/all_to_all | solution.py:178
  334.8 1.3 copy-start.11
  334.8 1.4 copy-start.12
  337.9 1.5 copy-start.3
  361.4 30.1 %all-to-all-start.7 = ((bf16[1024,1,4,128]{3,2,1,0:T(4,128)(2,1)}), bf16[1024,1,4,128]{3,2,1,0:T(4,128)(2,1)S(1)}, u32[]{:S(2)}, u32[]{:S(2)}) async-start(bf16[1024,1,4,128]{3,2,1,0:T(4,128)(2,1)} %copy.171), calls=%async_computation.7 | async-start | bytes 2097152 | tf_op jit(solution)/shard_map/all_to_all | solution.py:152
where the time goes:
time: 399 us; the launch traced here: 394 us
  waiting for transfers between devices  138 us (35%)
  matrix products  125 us (31%)
  local copies, waits for them, and re-layouts  49.7 us (12%)
  starting transfers between devices  33.2 us (8%)
  loops' own time  28.9 us (7%)
  other arithmetic  18 us (5%)
    another operation x1, loops' own time, long_conv(): results = lax.map(one_block, (blocks_in, residue_blocks, rate_blocks))  28.9 us
    all_to_all x1, waiting for transfers between devices, local(): lax.all_to_all(hyena_v, 'ctx', split_axis=1, concat_axis=0, tiled=True)  25.3 us
    all_to_all x1, waiting for transfers between devices, local(): lax.all_to_all(hyena_k, 'ctx', split_axis=1, concat_axis=0, tiled=True)  25.2 us
    all_to_all x1, waiting for transfers between devices, attend(): lax.all_to_all(attended, 'ctx', split_axis=0, concat_axis=1, tiled=True)  24.5 us
    all_to_all x1, waiting for transfers between devices, local(): lax.all_to_all(hyena_q, 'ctx', split_axis=1, concat_axis=0, tiled=True)  23.6 us
    all_to_all x1, waiting for transfers between devices, local(): lax.all_to_all(query_four, 'ctx', split_axis=1, concat_axis=0, tiled=True)  21.9 us
    dot_general x8, matrix products, forward_dft(): part_im = -jnp.einsum('kn,nmc->kmc', sin_one, signal, precision=HIGHEST)  16 us
    dot_general x8, matrix products, forward_dft(): jnp.einsum('kmc,mj->kjc', turned_re, sin_two, precision=HIGHEST)  15.8 us
  transfers between devices with their start and end apart: 8, of which 7 were waited for; matrix products, arithmetic and copies ran while one was open for 47% of the time, Pallas kernels for 0%

commit v1 on v0

v1 whole, which is shorter than its diff:
```python
import functools
import math

import jax
import jax.numpy as jnp
from jax import lax
from jax.experimental import pallas as pl
from jax.experimental.pallas import tpu as pltpu
from jax.sharding import PartitionSpec as P

HEAD_DIM = 128
LANES = 128
SUBLANES = 8
CHUNKS = 4
NEGATIVE = -1e30
EXP_SCALE = HEAD_DIM**-0.5 * math.log2(math.e)
VMEM_LIMIT = 40 * 1024 * 1024


def params(**kwargs):
    return pltpu.CompilerParams(vmem_limit_bytes=VMEM_LIMIT, **kwargs)


def to_positions(source_ref, scratch_ref, first):
    rows, columns = source_ref.shape
    step = 16
    for start in range(0, rows, step):
        for block in range(columns // LANES):
            piece = source_ref[start : start + step, block * LANES : (block + 1) * LANES]
            scratch_ref[pl.ds((first + start) * SUBLANES + block, step, SUBLANES), :] = piece.astype(
                jnp.float32
            )


def rim_to_positions(rim_ref, first_row, scratch_ref):
    taps = 2
    for block in range(rim_ref.shape[1] // LANES):
        piece = rim_ref[first_row : first_row + taps, block * LANES : (block + 1) * LANES]
        scratch_ref[pl.ds(block, taps, SUBLANES), :] = piece


def vector_at(ref, position):
    return ref[pl.ds(pl.multiple_of(position * SUBLANES, SUBLANES), SUBLANES), :]


def state_kernel(modes, k_ref, v_ref, rim_ref, taps_ref, par_ref, p_ref, s_ref, k_scr, v_scr):
    rows = k_ref.shape[0]
    to_positions(k_ref, k_scr, 2)
    to_positions(v_ref, v_scr, 2)
    rim_to_positions(rim_ref, 2, k_scr)
    rim_to_positions(rim_ref, 4, v_scr)
    decay = [
        jnp.exp(-par_ref[pl.ds(mode, SUBLANES, 2 * modes), :]) for mode in range(modes)
    ]
    k_taps = [taps_ref[3 + tap] for tap in range(3)]
    v_taps = [taps_ref[6 + tap] for tap in range(3)]

    def body(position, carry):
        k_two, k_one, v_two, v_one, states = carry
        k_now = vector_at(k_scr, position + 2)
        v_now = vector_at(v_scr, position + 2)
        k_mix = k_taps[0] * k_now + k_taps[1] * k_one + k_taps[2] * k_two
        v_mix = v_taps[0] * v_now + v_taps[1] * v_one + v_taps[2] * v_two
        product = (k_mix * v_mix).astype(jnp.bfloat16).astype(jnp.float32)
        p_ref[pl.ds(pl.multiple_of(position * SUBLANES, SUBLANES), SUBLANES), :] = product
        states = tuple(state * rate + product for state, rate in zip(states, decay))
        return (k_one, k_now, v_one, v_now, states)

    zero = jnp.zeros((SUBLANES, LANES), jnp.float32)
    start = (
        vector_at(k_scr, 0),
        vector_at(k_scr, 1),
        vector_at(v_scr, 0),
        vector_at(v_scr, 1),
        (zero,) * modes,
    )
    states = lax.fori_loop(0, rows, body, start, unroll=4)[4]
    for mode in range(modes):
        s_ref[pl.ds(mode, SUBLANES, modes), :] = states[mode]


def output_kernel(
    modes, q_ref, p_ref, rim_ref, taps_ref, par_ref, carry_ref, out_ref, q_scr, out_scr
):
    rows = q_ref.shape[0]
    to_positions(q_ref, q_scr, 2)
    rim_to_positions(rim_ref, 0, q_scr)
    decay = [
        jnp.exp(-par_ref[pl.ds(mode, SUBLANES, 2 * modes), :]) for mode in range(modes)
    ]
    residue = [par_ref[pl.ds(modes + mode, SUBLANES, 2 * modes), :] for mode in range(modes)]
    q_taps = [taps_ref[tap] for tap in range(3)]

    def body(position, carry):
        q_two, q_one, states = carry
        q_now = vector_at(q_scr, position + 2)
        product = vector_at(p_ref, position)
        q_mix = q_taps[0] * q_now + q_taps[1] * q_one + q_taps[2] * q_two
        states = tuple(state * rate + product for state, rate in zip(states, decay))
        terms = [state * weight for state, weight in zip(states, residue)]
        while len(terms) > 1:
            terms = [left + right for left, right in zip(terms[::2], terms[1::2])]
        smoothed = terms[0].astype(jnp.bfloat16).astype(jnp.float32)
        out_scr[pl.ds(pl.multiple_of(position * SUBLANES, SUBLANES), SUBLANES), :] = q_mix * smoothed
        return (q_one, q_now, states)

    start = (
        vector_at(q_scr, 0),
        vector_at(q_scr, 1),
        tuple(carry_ref[pl.ds(mode, SUBLANES, modes), :] for mode in range(modes)),
    )
    lax.fori_loop(0, rows, body, start, unroll=4)
    step = 16
    for first in range(0, rows, step):
        for block in range(q_ref.shape[1] // LANES):
            piece = out_scr[pl.ds(first * SUBLANES + block, step, SUBLANES), :]
            out_ref[first : first + step, block * LANES : (block + 1) * LANES] = piece.astype(
                out_ref.dtype
            )


def convolve(hyena_q, hyena_k, hyena_v, short_filter, residue, decay_rate):
    rows, channels = hyena_q.shape
    devices = lax.axis_size("ctx")
    modes = residue.shape[1]
    own_blocks = residue.shape[0] // LANES
    blocks = channels // LANES
    groups = blocks // SUBLANES
    width = SUBLANES * LANES
    group_rows = SUBLANES * modes

    def by_blocks(array):
        return array.reshape(own_blocks, LANES, modes).transpose(0, 2, 1)

    rim = jnp.concatenate([hyena_q[rows - 2 :], hyena_k[rows - 2 :], hyena_v[rows - 2 :]], 0)
    rim = lax.ppermute(rim, "ctx", [(index, index + 1) for index in range(devices - 1)])
    rim = jnp.pad(rim.astype(jnp.float32), ((0, 2), (0, 0)))
    own_rate = by_blocks(decay_rate)
    own_par = jnp.concatenate([own_rate, by_blocks(residue)], 1).reshape(
        own_blocks * 2 * modes, LANES
    )
    par = lax.all_gather(own_par, "ctx", axis=0, tiled=True)
    taps = short_filter.reshape(9, blocks, LANES)

    def wide(index):
        return (0, index)

    feature_spec = pl.BlockSpec((rows, width), wide)
    rim_spec = pl.BlockSpec((8, width), wide)
    taps_spec = pl.BlockSpec((9, SUBLANES, LANES), lambda index: (0, index, 0))
    par_spec = pl.BlockSpec((2 * group_rows, LANES), lambda index: (index, 0))
    state_spec = pl.BlockSpec((group_rows, LANES), lambda index: (index, 0))
    product_spec = pl.BlockSpec((rows * SUBLANES, LANES), lambda index: (index, 0))
    padded = pltpu.VMEM(((rows + 2) * SUBLANES, LANES), jnp.float32)
    product, state = pl.pallas_call(
        functools.partial(state_kernel, modes),
        grid=(groups,),
        in_specs=[feature_spec, feature_spec, rim_spec, taps_spec, par_spec],
        out_specs=[product_spec, state_spec],
        out_shape=[
            jax.ShapeDtypeStruct((groups * rows * SUBLANES, LANES), jnp.float32),
            jax.ShapeDtypeStruct((groups * group_rows, LANES), jnp.float32),
        ],
        scratch_shapes=[padded, padded],
        compiler_params=params(),
        cost_estimate=pl.CostEstimate(
            flops=4 * 10**9, bytes_accessed=8 * 2**20, transcendentals=0
        ),
        name="conv_state",
    )(hyena_k, hyena_v, rim, taps, par)
    arrived = lax.all_to_all(state, "ctx", split_axis=0, concat_axis=0, tiled=True).reshape(
        devices, own_blocks, modes, LANES
    )
    chunk_decay = jnp.exp(-own_rate * rows)
    entering = [jnp.zeros((own_blocks, modes, LANES), jnp.float32)]
    for index in range(devices - 1):
        entering.append(entering[-1] * chunk_decay + arrived[index])
    entering = jnp.stack(entering).reshape(devices * own_blocks * modes, LANES)
    carry = lax.all_to_all(entering, "ctx", split_axis=0, concat_axis=0, tiled=True)
    return pl.pallas_call(
        functools.partial(output_kernel, modes),
        grid=(groups,),
        in_specs=[feature_spec, product_spec, rim_spec, taps_spec, par_spec, state_spec],
        out_specs=feature_spec,
        out_shape=jax.ShapeDtypeStruct((rows, channels), jnp.bfloat16),
        scratch_shapes=[padded, pltpu.VMEM((rows * SUBLANES, LANES), jnp.float32)],
        compiler_params=params(),
        cost_estimate=pl.CostEstimate(
            flops=6 * 10**9, bytes_accessed=8 * 2**20, transcendentals=0
        ),
        name="conv_output",
    )(hyena_q, product, rim, taps, par, carry)


def head_slice(head):
    return pl.ds(pl.multiple_of(head * HEAD_DIM, HEAD_DIM), HEAD_DIM)


def lane_index(rows):
    return lax.broadcasted_iota(jnp.int32, (rows, LANES), 1)


def soft(query, keys, values, mask=None):
    scores = lax.dot_general(
        query, keys, (((1,), (1,)), ((), ())), preferred_element_type=jnp.float32
    )
    if mask is not None:
        scores = jnp.where(mask, scores, NEGATIVE)
    top = jnp.max(scores, axis=1, keepdims=True) * EXP_SCALE
    expo = jnp.exp2(scores * EXP_SCALE - top)
    total = jnp.sum(expo, axis=1, keepdims=True)
    mixed = jnp.dot(expo.astype(jnp.bfloat16), values, preferred_element_type=jnp.float32)
    return mixed / total, top + jnp.log2(total)


def partial_kernel(slots, role_ref, q_ref, k_ref, v_ref, kp_ref, vp_ref, g_ref, gp_ref, *rest):
    remote_refs = rest[:slots]
    own_ref, lse_ref = rest[slots : slots + 2]
    back_refs = rest[slots + 2 : 2 * slots + 2]
    rows, width = q_ref.shape
    heads = width // HEAD_DIM
    odd = role_ref[0] == 1
    gathered = role_ref[1] == 1

    def key_value(head, with_quad):
        cut = head_slice(head)
        keys = [kp_ref[:, cut], k_ref[:, cut]]
        values = [vp_ref[:, cut], v_ref[:, cut]]
        if with_quad:
            keys = [g_ref[0, :, cut], gp_ref[0, :, cut]] + keys
            values = [g_ref[1, :, cut], gp_ref[1, :, cut]] + values
        return jnp.concatenate(keys, 0), jnp.concatenate(values, 0)

    def run(with_quad):
        key_count = rows * (4 if with_quad else 2)
        row = lax.broadcasted_iota(jnp.int32, (rows, key_count), 0)
        column = lax.broadcasted_iota(jnp.int32, (rows, key_count), 1) - (key_count - 2 * rows)
        partner_limit = jnp.where(odd, rows, 0)
        mask = (column < partner_limit) | ((column >= rows) & (column - rows <= row))
        lanes = lane_index(rows)

        def own_body(head, sums):
            keys, values = key_value(head, with_quad)
            mixed, lse = soft(q_ref[:, head_slice(head)], keys, values, mask)
            own_ref[:, head_slice(head)] = mixed
            return jnp.where(lanes == head, lse, sums)

        lse_ref[...] = lax.fori_loop(
            0, heads, own_body, jnp.zeros((rows, LANES), jnp.float32)
        )

        for slot in range(slots):

            @pl.when(role_ref[2 + slot] == 1)
            def _():
                def remote_body(head, sums):
                    keys, values = key_value(head, with_quad)
                    mixed, lse = soft(remote_refs[slot][:, head_slice(head)], keys, values)
                    back_refs[slot][:, head_slice(head)] = mixed.astype(jnp.bfloat16)
                    first = lse.astype(jnp.bfloat16).astype(jnp.float32)
                    second = (lse - first).astype(jnp.bfloat16).astype(jnp.float32)
                    third = lse - first - second
                    sums = jnp.where(lanes == head, first, sums)
                    sums = jnp.where(lanes == heads + head, second, sums)
                    return jnp.where(lanes == 2 * heads + head, third, sums)

                sums = lax.fori_loop(
                    0, heads, remote_body, jnp.zeros((rows, LANES), jnp.float32)
                )
                back_refs[slot][:, width:] = sums.astype(jnp.bfloat16)

    @pl.when(gathered)
    def _():
        run(True)

    @pl.when(jnp.logical_not(gathered))
    def _():
        run(False)


def merge_kernel(slots, heads, role_ref, *refs):
    own_ref, lse_ref = refs[:2]
    back_refs = refs[2 : 2 + slots]
    out_ref = refs[-1]
    rows = own_ref.shape[0]
    width = heads * HEAD_DIM
    lanes = lane_index(rows)

    def body(head, nothing):
        cut = head_slice(head)
        mixed = [own_ref[:, cut]]
        sums = [jnp.sum(jnp.where(lanes == head, lse_ref[...], 0.0), axis=1, keepdims=True)]
        mine = (lanes == head) | (lanes == heads + head) | (lanes == 2 * heads + head)
        for slot in range(slots):
            valid = role_ref[2 + slots + slot] == 1
            tail = back_refs[slot][:, width:].astype(jnp.float32)
            lse = jnp.sum(jnp.where(mine, tail, 0.0), axis=1, keepdims=True)
            sums.append(jnp.where(valid, lse, NEGATIVE))
            mixed.append(back_refs[slot][:, cut].astype(jnp.float32))
        top = functools.reduce(jnp.maximum, sums)
        weights = [jnp.exp2(part - top) for part in sums]
        total = functools.reduce(jnp.add, weights)
        result = functools.reduce(
            jnp.add, [part * (weight / total) for part, weight in zip(mixed, weights)]
        )
        out_ref[:, cut] = result.astype(out_ref.dtype)
        return nothing

    lax.fori_loop(0, heads, body, 0)


def query_moves(devices):
    quads = devices // 4
    moves = []
    for distance in range(1, quads):
        for half in range(2):
            moves.append(
                [
                    (4 * quad + 2 * half + core, 4 * (quad - distance) + 2 + core)
                    for quad in range(distance, quads)
                    for core in range(2)
                ]
            )
    if not moves:
        moves.append([])
    moves[0] = moves[0] + [(devices - 2 + core, devices - 4 + core) for core in range(2)]
    return moves


def attend(query, key, value):
    rows, columns = query.shape
    devices = lax.axis_size("ctx")
    quads = devices // 4
    me = lax.axis_index("ctx")
    moves = query_moves(devices)
    slots = len(moves)
    width = columns // CHUNKS
    heads = width // HEAD_DIM

    def flag(members):
        table = [1 if index in members else 0 for index in range(devices)]
        return jnp.asarray(table, jnp.int32)[me]

    gathers = [
        (4 * quad + core, 4 * quad + 2 + core) for quad in range(quads - 1) for core in range(2)
    ]
    gather_swap = [
        (4 * quad + 2 + core, 4 * quad + 3 - core) for quad in range(quads - 1) for core in range(2)
    ]
    swap = [(index, index ^ 1) for index in range(devices)]
    role = jnp.stack(
        [me % 2, flag([target for _, target in gathers])]
        + [flag([target for _, target in pairs]) for pairs in moves]
        + [flag([source for source, _ in pairs]) for pairs in moves]
    ).astype(jnp.int32)
    key_swapped = lax.ppermute(key, "ctx", swap)
    value_swapped = lax.ppermute(value, "ctx", swap)
    smem = pl.BlockSpec(memory_space=pltpu.SMEM)
    result = None
    for chunk in range(CHUNKS):
        cut = slice(chunk * width, (chunk + 1) * width)
        both = jnp.stack([key[:, cut], value[:, cut]])
        from_below = lax.ppermute(both, "ctx", gathers)
        from_below_swapped = lax.ppermute(from_below, "ctx", gather_swap)
        query_cut = query[:, cut]
        remote = [lax.ppermute(query_cut, "ctx", pairs) for pairs in moves]
        here = pl.BlockSpec((rows, width), lambda step, chunk=chunk: (0, chunk))
        alone = pl.BlockSpec((rows, width), lambda step: (0, 0))
        quad_spec = pl.BlockSpec((2, rows, width), lambda step: (0, 0, 0))
        lse_spec = pl.BlockSpec((rows, LANES), lambda step: (0, 0))
        back_spec = pl.BlockSpec((rows, width + LANES), lambda step: (0, 0))
        outs = pl.pallas_call(
            functools.partial(partial_kernel, slots),
            grid=(1,),
            in_specs=[smem] + [here] * 5 + [quad_spec] * 2 + [alone] * slots,
            out_specs=[alone, lse_spec] + [back_spec] * slots,
            out_shape=[
                jax.ShapeDtypeStruct((rows, width), jnp.float32),
                jax.ShapeDtypeStruct((rows, LANES), jnp.float32),
            ]
            + [jax.ShapeDtypeStruct((rows, width + LANES), jnp.bfloat16)] * slots,
            compiler_params=params(),
            cost_estimate=pl.CostEstimate(
                flops=3 * 10**9, bytes_accessed=4 * 2**20, transcendentals=0
            ),
            name="att_partial",
        )(role, query, key, value, key_swapped, value_swapped, from_below, from_below_swapped, *remote)
        back = [
            lax.ppermute(part, "ctx", [(target, source) for source, target in pairs])
            for part, pairs in zip(outs[2:], moves)
        ]
        operands = [role, outs[0], outs[1], *back]
        specs = [smem, alone, lse_spec] + [back_spec] * slots
        aliases = {}
        if result is not None:
            aliases = {len(operands): 0}
            operands.append(result)
            specs.append(pl.BlockSpec(memory_space=pl.ANY))
        result = pl.pallas_call(
            functools.partial(merge_kernel, slots, heads),
            grid=(1,),
            in_specs=specs,
            out_specs=here,
            out_shape=jax.ShapeDtypeStruct((rows, columns), jnp.bfloat16),
            input_output_aliases=aliases,
            compiler_params=params(),
            cost_estimate=pl.CostEstimate(
                flops=10**9, bytes_accessed=2 * 2**20, transcendentals=0
            ),
            name="att_merge",
        )(*operands)
    return result


def local(
    hyena_q, hyena_k, hyena_v, short_filter, residue, decay_rate, att_query, att_key, att_value
):
    att_out = attend(att_query, att_key, att_value)
    hyena_out = convolve(hyena_q, hyena_k, hyena_v, short_filter, residue, decay_rate)
    return (hyena_out, att_out)


def solution(mesh):
    rows = P(("dp", "ctx"), None)
    shared = P("ctx", None)
    return jax.shard_map(
        local,
        mesh=mesh,
        in_specs=(rows, rows, rows, P(), shared, shared, rows, rows, rows),
        out_specs=(rows, rows),
        check_vma=False,
    )
```

time: 399 us -> 211 us (0.53)
  the two profiles are of different devices: /device:TPU:0 before, /device:TPU:10 now
where the time goes in v1:
time: 211 us; the launch traced here: 209 us
  Pallas kernels  73.6 us (35%)
  starting transfers between devices  53.8 us (25%)
  local copies, waits for them, and re-layouts  36.1 us (17%)
  waiting for transfers between devices  20.4 us (10%)
  blocking collectives  16.8 us (8%)
  other arithmetic  7.38 us (3%)
    pallas_call x4, Pallas kernels, attend(): pl.pallas_call(functools.partial(partial_kernel, slots), grid=(1,), in_sp...  48.2 us
    unnamed x95, local copies, waits for them, and re-layouts  21.2 us
    ppermute x4, waiting for transfers between devices, attend(): from_below = lax.ppermute(both, 'ctx', gathers)  19.8 us
    all_gather x1, blocking collectives, convolve(): par = lax.all_gather(own_par, 'ctx', axis=0, tiled=True)  16.8 us
    ppermute x8, starting transfers between devices, attend(): lax.ppermute(part, 'ctx', [(target, source) for source, target in pairs])  16.5 us
    pallas_call x4, Pallas kernels, attend(): pl.pallas_call(functools.partial(merge_kernel, slots, heads), grid=(1,),...  11.7 us
    ppermute x8, starting transfers between devices, attend(): remote = [lax.ppermute(query_cut, 'ctx', pairs) for pairs in moves]  10.3 us
    ppermute x4, starting transfers between devices, attend(): from_below_swapped = lax.ppermute(from_below, 'ctx', gather_swap)  8.27 us
  transfers between devices with their start and end apart: 29, of which 3 were waited for; matrix products, arithmetic and copies ran while one was open for 12% of the time, Pallas kernels for 34%

profile of v1, /device:TPU:10, one launch (start us, length us, event | category | flops | bytes accessed | tf_op | source)
XLA Modules:
  0.0 209.4 jit_solution(15666651708310755896)
XLA Ops:
  0.7 2.3 %fusion = (bf16[128,1024]{1,0:T(8,128)(2,1)}, bf16[128,1024]{1,0:T(8,128)(2,1)}, bf16[128,1024]{1,0:T(8,128)(2,1)}, bf16[128,1024]{1,0:T(8,128)(2,1)}) fusion(bf16[128,4096]{1,0:T(8,128)(2,1)} %q_ref.9), kind=kLoop, calls=%fused_computation.33 | loop fusion | bytes 2097152 | tf_op jit(solution)/shard_map/slice | solution.py:365
  3.0 1.3 collective-permute-start.23
  4.3 1.3 collective-permute-start.24
  9.4 2.1 %collective-permute-start = (bf16[6,4096]{1,0:T(8,128)(2,1)}, bf16[6,4096]{1,0:T(8,128)(2,1)S(1)}, u32[]{:S(2)}, u32[]{:S(2)}) collective-permute-start(bf16[6,4096]{1,0:T(8,128)(2,1)} %pad_maximum_fusion.4), channel_id=1, source_target_pairs={{0,1},{1,2},{2,3},{3,4},{4,5},{5,6},{6,7},{8,9},{9,10},{10,11},{11... | collective-permute-start | bytes 147464 | tf_op jit(solution)/shard_map/ppermute | solution.py:136
  13.4 16.8 %all_gather.3.par_ref = f32[1024,128]{1,0:T(8,128)S(1)} all-gather(f32[128,128]{1,0:T(8,128)S(1)} %bitcast.107), channel_id=1, replica_groups=mesh['dp'=4,'ctx'=8] {'ctx'}, dimensions={0}, use_global_device_ids=true | all-gather | bytes 589824 | tf_op jit(solution)/shard_map/all_gather | solution.py:142
  32.2 1.3 collective-permute-start.21
  34.8 1.2 copy-done.11
  36.0 5.5 %conv_state.1 = (f32[4096,128]{1,0:T(8,128)S(1)}, f32[512,128]{1,0:T(8,128)}) custom-call(bf16[128,4096]{1,0:T(8,128)(2,1)S(1)} %copy-done.10, bf16[128,4096]{1,0:T(8,128)(2,1)S(1)} %copy-done.11, f32[8,4096]{1,0:T(8,128)S(1)} %pad_convert_fusion.rim_ref, f32[9,32,128]{2,1,0:T(8,128)S(1)} %reshape.66.taps_ref, f32[1024,128]{1,0:T(8,128)S(1)} %all_gather.3.par_ref), custom_call_target="tpu_custom_call" | custom-call | flops 4000000000 | bytes 8388608 | tf_op jit(solution)/shard_map/conv_state/pallas_call | solution.py:155
  41.6 1.3 copy-done.35
  42.9 7.5 %all-to-all-start = ((f32[8,64,128]{2,1,0:T(8,128)}), f32[8,64,128]{2,1,0:T(8,128)}, u32[]{:S(2)}, u32[]{:S(2)}) async-start(f32[8,64,128]{2,1,0:T(8,128)} %bitcast.3), calls=%async_computation | async-start | bytes 524288 | tf_op jit(solution)/shard_map/all_to_all | solution.py:171
  50.4 1.9 pad_maximum_fusion.2
  52.3 2.0 pad_maximum_fusion.1
  54.2 1.9 pad_maximum_fusion
  59.2 3.2 %stack.75.role_ref = s32[6]{0:T(128)S(1)} concatenate(s32[1]{0:T(128)} %bitcast.19, s32[1]{0:T(128)} %dynamic_slice.15, s32[1]{0:T(128)} %dynamic_slice.16, s32[1]{0:T(128)} %dynamic_slice.15, s32[1]{0:T(128)} %dynamic_slice.18, s32[1]{0:T(128)} %dynamic_slice.19), dimensions={0} | concatenate | bytes 48 | tf_op jit(solution)/shard_map/stack | solution.py:351
  63.3 1.3 collective-permute-start.15
  64.6 1.3 collective-permute-start.9
  67.2 2.0 collective-permute-start.22
  70.4 9.9 %collective-permute-done.15.g_ref = bf16[2,128,1024]{2,1,0:T(8,128)(2,1)} collective-permute-done((bf16[2,128,1024]{2,1,0:T(8,128)(2,1)}, bf16[2,128,1024]{2,1,0:T(8,128)(2,1)}, u32[]{:S(2)}, u32[]{:S(2)}) %collective-permute-start.15) | collective-permute-done | bytes 524320 | tf_op jit(solution)/shard_map/ppermute | solution.py:363
  80.3 1.3 collective-permute-start.3
  81.6 9.9 %collective-permute-done.9.g_ref = bf16[2,128,1024]{2,1,0:T(8,128)(2,1)} collective-permute-done((bf16[2,128,1024]{2,1,0:T(8,128)(2,1)}, bf16[2,128,1024]{2,1,0:T(8,128)(2,1)}, u32[]{:S(2)}, u32[]{:S(2)}) %collective-permute-start.9) | collective-permute-done | bytes 524320 | tf_op jit(solution)/shard_map/ppermute | solution.py:363
  91.5 1.9 collective-permute-start.16
  95.2 3.4 %all-to-all-start.1 = ((f32[8,64,128]{2,1,0:T(8,128)}), f32[8,64,128]{2,1,0:T(8,128)S(1)}, u32[]{:S(2)}, u32[]{:S(2)}) async-start(f32[8,64,128]{2,1,0:T(8,128)} %bitcast_dynamic-update-slice_fusion), calls=%async_computation.1 | async-start | bytes 524288 | tf_op jit(solution)/shard_map/all_to_all | solution.py:179
  98.7 1.3 collective-permute-start.17
  100.0 1.3 collective-permute-start.18
  101.3 2.4 %collective-permute-start.10 = (bf16[2,128,1024]{2,1,0:T(8,128)(2,1)}, bf16[2,128,1024]{2,1,0:T(8,128)(2,1)S(1)}, u32[]{:S(2)}, u32[]{:S(2)}) collective-permute-start(bf16[2,128,1024]{2,1,0:T(8,128)(2,1)} %collective-permute-done.9.g_ref), channel_id=1, source_target_pairs={{2,3},{3,2},{10,11},{11,10},{18,19},{19,18},{26,27},{27,26}} | collective-permute-start | bytes 1572872 | tf_op jit(solution)/shard_map/ppermute | solution.py:364
  104.6 11.6 %att_partial.7 = (f32[128,1024]{1,0:T(8,128)S(1)}, f32[128,128]{1,0:T(8,128)S(1)}, bf16[128,1152]{1,0:T(8,128)(2,1)S(1)}, bf16[128,1152]{1,0:T(8,128)(2,1)S(1)}) custom-call(s32[6]{0:T(128)S(1)} %stack.75.role_ref, bf16[128,4096]{1,0:T(8,128)(2,1)S(1)} %copy-done.1, bf16[128,4096]{1,0:T(8,128)(2,1)S(1)} %copy-done.2, bf16[128,4096]{1,0:T(8,128)(2,1)S(1)} %copy-done.3, ...), custom_call_target="tpu_custom_call" | custom-call | flops 3000000000 | bytes 4194304 | tf_op jit(solution)/shard_map/att_partial/pallas_call | solution.py:372
  118.2 1.3 collective-permute-start.11
  119.5 1.3 collective-permute-start.12
  120.8 1.3 collective-permute-start.5
  122.1 1.9 collective-permute-start.4
  124.0 12.2 %att_partial.6 = (f32[128,1024]{1,0:T(8,128)S(1)}, f32[128,128]{1,0:T(8,128)S(1)}, bf16[128,1152]{1,0:T(8,128)(2,1)S(1)}, bf16[128,1152]{1,0:T(8,128)(2,1)}) custom-call(s32[6]{0:T(128)S(1)} %stack.75.role_ref, bf16[128,4096]{1,0:T(8,128)(2,1)S(1)} %copy-done.1, bf16[128,4096]{1,0:T(8,128)(2,1)S(1)} %copy-done.2, bf16[128,4096]{1,0:T(8,128)(2,1)S(1)} %copy-done.3, ...), custom_call_target="tpu_custom_call" | custom-call | flops 3000000000 | bytes 4194304 | tf_op jit(solution)/shard_map/att_partial/pallas_call | solution.py:372
  137.1 1.3 collective-permute-start.6
  138.4 1.3 collective-permute-start.25
  139.7 5.5 %collective-permute-start.26 = (bf16[128,1152]{1,0:T(8,128)(2,1)S(1)}, bf16[128,1152]{1,0:T(8,128)(2,1)S(1)}, u32[]{:S(2)}, u32[]{:S(2)}) collective-permute-start(bf16[128,1152]{1,0:T(8,128)(2,1)S(1)} %get-tuple-element.37), channel_id=1, source_target_pairs={{2,6},{3,7},{10,14},{11,15},{18,22},{19,23},{26,30},{27,31}} | collective-permute-start | bytes 884744 | tf_op jit(solution)/shard_map/ppermute | solution.py:389
  145.2 1.9 collective-permute-start.19
  147.0 12.2 %att_partial.5 = (f32[128,1024]{1,0:T(8,128)S(1)}, f32[128,128]{1,0:T(8,128)S(1)}, bf16[128,1152]{1,0:T(8,128)(2,1)}, bf16[128,1152]{1,0:T(8,128)(2,1)}) custom-call(s32[6]{0:T(128)S(1)} %stack.75.role_ref, bf16[128,4096]{1,0:T(8,128)(2,1)S(1)} %copy-done.1, bf16[128,4096]{1,0:T(8,128)(2,1)S(1)} %copy-done.2, bf16[128,4096]{1,0:T(8,128)(2,1)S(1)} %copy-done.3, ...), custom_call_target="tpu_custom_call" | custom-call | flops 3000000000 | bytes 4194304 | tf_op jit(solution)/shard_map/att_partial/pallas_call | solution.py:372
  160.0 2.0 collective-permute-start.20
  162.0 2.0 collective-permute-start.13
  164.0 12.2 %att_partial.4 = (f32[128,1024]{1,0:T(8,128)S(1)}, f32[128,128]{1,0:T(8,128)S(1)}, bf16[128,1152]{1,0:T(8,128)(2,1)}, bf16[128,1152]{1,0:T(8,128)(2,1)}) custom-call(s32[6]{0:T(128)S(1)} %stack.75.role_ref, bf16[128,4096]{1,0:T(8,128)(2,1)S(1)} %copy-done.1, bf16[128,4096]{1,0:T(8,128)(2,1)S(1)} %copy-done.2, bf16[128,4096]{1,0:T(8,128)(2,1)S(1)} %copy-done.3, ...), custom_call_target="tpu_custom_call" | custom-call | flops 3000000000 | bytes 4194304 | tf_op jit(solution)/shard_map/att_partial/pallas_call | solution.py:372
  178.4 1.3 collective-permute-start.14
  180.4 1.3 collective-permute-start.7
  182.4 1.3 collective-permute-start.8
  187.8 1.6 copy-done.36
  189.4 8.2 %conv_output.1 = bf16[128,4096]{1,0:T(8,128)(2,1)} custom-call(bf16[128,4096]{1,0:T(8,128)(2,1)S(1)} %copy-done.12, f32[4096,128]{1,0:T(8,128)S(1)} %copy-done.36, f32[8,4096]{1,0:T(8,128)S(1)} %copy-done.9, f32[9,32,128]{2,1,0:T(8,128)S(1)} %copy-done.7, f32[1024,128]{1,0:T(8,128)S(1)} %copy-done.5, f32[512,128]{1,0:T(8,128)S(1)} %bitcast.106), custom_call_target="tpu_custom_call" | custom-call | flops 6000000000 | bytes 8388608 | tf_op jit(solution)/shard_map/conv_output/pallas_call | solution.py:180
  197.6 2.7 %att_merge.4.refs_4_ = bf16[128,4096]{1,0:T(8,128)(2,1)} custom-call(s32[6]{0:T(128)S(1)} %stack.75.role_ref, f32[128,1024]{1,0:T(8,128)S(1)} %copy-done.32, f32[128,128]{1,0:T(8,128)S(1)} %copy-done.34, bf16[128,1152]{1,0:T(8,128)(2,1)S(1)} %copy-done.14, bf16[128,1152]{1,0:T(8,128)(2,1)S(1)} %copy-done.18), custom_call_target="tpu_custom_call" | custom-call | flops 1000000000 | bytes 2097152 | tf_op jit(solution)/shard_map/att_merge/pallas_call | solution.py:399
  200.3 3.2 %att_merge.5.refs_4_ = bf16[128,4096]{1,0:T(8,128)(2,1)} custom-call(s32[6]{0:T(128)S(1)} %stack.75.role_ref, f32[128,1024]{1,0:T(8,128)S(1)} %copy-done.22, f32[128,128]{1,0:T(8,128)S(1)} %get-tuple-element.31.refs_1_, bf16[128,1152]{1,0:T(8,128)(2,1)S(1)} %copy-done.16, ...), custom_call_target="tpu_custom_call", output_to_operand_aliasing={{}: (5, {})} | custom-call | flops 1000000000 | bytes 2097152 | tf_op jit(solution)/shard_map/att_merge/pallas_call | solution.py:399
  203.5 3.2 %att_merge.6.refs_4_ = bf16[128,4096]{1,0:T(8,128)(2,1)} custom-call(s32[6]{0:T(128)S(1)} %stack.75.role_ref, f32[128,1024]{1,0:T(8,128)S(1)} %copy-done.24, f32[128,128]{1,0:T(8,128)S(1)} %copy-done.28, bf16[128,1152]{1,0:T(8,128)(2,1)} %collective-permute-done.13.refs_2_, ...), custom_call_target="tpu_custom_call", output_to_operand_aliasing={{}: (5, {})} | custom-call | flops 1000000000 | bytes 2097152 | tf_op jit(solution)/shard_map/att_merge/pallas_call | solution.py:399
  206.7 2.7 %att_merge.7 = bf16[128,4096]{1,0:T(8,128)(2,1)} custom-call(s32[6]{0:T(128)S(1)} %stack.75.role_ref, f32[128,1024]{1,0:T(8,128)S(1)} %copy-done.26, f32[128,128]{1,0:T(8,128)S(1)} %copy-done.30, bf16[128,1152]{1,0:T(8,128)(2,1)S(1)} %collective-permute-done.7.refs_2_, ...), custom_call_target="tpu_custom_call", output_to_operand_aliasing={{}: (5, {})} | custom-call | flops 1000000000 | bytes 2097152 | tf_op jit(solution)/shard_map/att_merge/pallas_call | solution.py:399
  (139 shorter events, 29.3 us)
Async XLA Ops:
  0.6 12.8 %copy-start = (f32[512,16]{0,1:T(8,128)S(1)}, f32[512,16]{0,1:T(8,128)}, u32[]{:S(2)}) copy-start(f32[512,16]{0,1:T(8,128)} %param.19) | copy-start | bytes 98308
  0.6 4.9 %copy-start.2 = (bf16[128,4096]{1,0:T(8,128)(2,1)S(1)}, bf16[128,4096]{1,0:T(8,128)(2,1)}, u32[]{:S(2)}) copy-start(bf16[128,4096]{1,0:T(8,128)(2,1)} %k_ref.9) | copy-start | bytes 3145732
  0.7 5.0 %copy-start.3 = (bf16[128,4096]{1,0:T(8,128)(2,1)S(1)}, bf16[128,4096]{1,0:T(8,128)(2,1)}, u32[]{:S(2)}) copy-start(bf16[128,4096]{1,0:T(8,128)(2,1)} %v_ref.9) | copy-start | bytes 3145732
  3.0 60.3 %collective-permute-start.23 = (bf16[128,1024]{1,0:T(8,128)(2,1)}, bf16[128,1024]{1,0:T(8,128)(2,1)S(1)}, u32[]{:S(2)}, u32[]{:S(2)}) collective-permute-start(bf16[128,1024]{1,0:T(8,128)(2,1)} %get-tuple-element.44), channel_id=1, source_target_pairs={{4,2},{5,3},{6,4},{7,5},{12,10},{13,11},{14,12},{15,13},{20,18},{2... | collective-permute-start | bytes 786440 | tf_op jit(solution)/shard_map/ppermute | solution.py:366
  4.3 60.3 %collective-permute-start.24 = (bf16[128,1024]{1,0:T(8,128)(2,1)}, bf16[128,1024]{1,0:T(8,128)(2,1)}, u32[]{:S(2)}, u32[]{:S(2)}) collective-permute-start(bf16[128,1024]{1,0:T(8,128)(2,1)} %get-tuple-element.44), channel_id=1, source_target_pairs={{6,2},{7,3},{14,10},{15,11},{22,18},{23,19},{30,26},{31,27}} | collective-permute-start | bytes 786440 | tf_op jit(solution)/shard_map/ppermute | solution.py:366
  5.6 94.4 %collective-permute-start.1 = (bf16[128,4096]{1,0:T(8,128)(2,1)S(1)}, bf16[128,4096]{1,0:T(8,128)(2,1)}, u32[]{:S(2)}, u32[]{:S(2)}) collective-permute-start(bf16[128,4096]{1,0:T(8,128)(2,1)S(1)} %copy-done.2), channel_id=1, source_target_pairs={{0,1},{1,0},{2,3},{3,2},{4,5},{5,4},{6,7},{7,6},{8,9},{9,8},{10,11... | collective-permute-start | bytes 3145736 | tf_op jit(solution)/shard_map/ppermute | solution.py:356
  5.7 95.6 %collective-permute-start.2 = (bf16[128,4096]{1,0:T(8,128)(2,1)S(1)}, bf16[128,4096]{1,0:T(8,128)(2,1)}, u32[]{:S(2)}, u32[]{:S(2)}) collective-permute-start(bf16[128,4096]{1,0:T(8,128)(2,1)S(1)} %copy-done.3), channel_id=1, source_target_pairs={{0,1},{1,0},{2,3},{3,2},{4,5},{5,4},{6,7},{7,6},{8,9},{9,8},{10,11... | collective-permute-start | bytes 3145736 | tf_op jit(solution)/shard_map/ppermute | solution.py:357
  9.4 22.8 %collective-permute-start = (bf16[6,4096]{1,0:T(8,128)(2,1)}, bf16[6,4096]{1,0:T(8,128)(2,1)S(1)}, u32[]{:S(2)}, u32[]{:S(2)}) collective-permute-start(bf16[6,4096]{1,0:T(8,128)(2,1)} %pad_maximum_fusion.4), channel_id=1, source_target_pairs={{0,1},{1,2},{2,3},{3,4},{4,5},{5,6},{6,7},{8,9},{9,10},{10,11},{11... | collective-permute-start | bytes 147464 | tf_op jit(solution)/shard_map/ppermute | solution.py:136
  30.3 11.3 %copy-start.4 = (f32[1024,128]{1,0:T(8,128)}, f32[1024,128]{1,0:T(8,128)S(1)}, u32[]{:S(2)}) copy-start(f32[1024,128]{1,0:T(8,128)S(1)} %all_gather.3.par_ref) | copy-start | bytes 1572868
  32.2 9.3 %copy-start.6 = (f32[9,32,128]{2,1,0:T(8,128)}, f32[9,32,128]{2,1,0:T(8,128)S(1)}, u32[]{:S(2)}) copy-start(f32[9,32,128]{2,1,0:T(8,128)S(1)} %reshape.66.taps_ref) | copy-start | bytes 442372
  32.2 34.9 %collective-permute-start.21 = (bf16[2,128,1024]{2,1,0:T(8,128)(2,1)}, bf16[2,128,1024]{2,1,0:T(8,128)(2,1)}, u32[]{:S(2)}, u32[]{:S(2)}) collective-permute-start(bf16[2,128,1024]{2,1,0:T(8,128)(2,1)} %pad_maximum_fusion.3), channel_id=1, source_target_pairs={{0,2},{1,3},{8,10},{9,11},{16,18},{17,19},{24,26},{25,27}} | collective-permute-start | bytes 1572872 | tf_op jit(solution)/shard_map/ppermute | solution.py:363
  36.0 5.5 %copy-start.8 = (f32[8,4096]{1,0:T(8,128)}, f32[8,4096]{1,0:T(8,128)S(1)}, u32[]{:S(2)}) copy-start(f32[8,4096]{1,0:T(8,128)S(1)} %pad_convert_fusion.rim_ref) | copy-start | bytes 393220
  42.9 13.9 %copy-start.43 = (s32[8]{0:T(128)S(1)}, s32[8]{0:T(128)}, u32[]{:S(2)}) copy-start(s32[8]{0:T(128)} %constant.36.clone) | copy-start | bytes 100
  42.9 14.5 %copy-start.42 = (s32[8]{0:T(128)S(1)}, s32[8]{0:T(128)}, u32[]{:S(2)}) copy-start(s32[8]{0:T(128)} %constant.37.clone) | copy-start | bytes 100
  42.9 15.1 %copy-start.41 = (s32[8]{0:T(128)S(1)}, s32[8]{0:T(128)}, u32[]{:S(2)}) copy-start(s32[8]{0:T(128)} %constant.38.clone) | copy-start | bytes 100
  42.9 15.7 %copy-start.40 = (s32[8]{0:T(128)S(1)}, s32[8]{0:T(128)}, u32[]{:S(2)}) copy-start(s32[8]{0:T(128)} %constant.39.clone) | copy-start | bytes 100
  42.9 19.5 %all-to-all-start = ((f32[8,64,128]{2,1,0:T(8,128)}), f32[8,64,128]{2,1,0:T(8,128)}, u32[]{:S(2)}, u32[]{:S(2)}) async-start(f32[8,64,128]{2,1,0:T(8,128)} %bitcast.3), calls=%async_computation | async-start | bytes 524288 | tf_op jit(solution)/shard_map/all_to_all | solution.py:171
  52.3 51.4 %copy-start.1 = (bf16[128,4096]{1,0:T(8,128)(2,1)S(1)}, bf16[128,4096]{1,0:T(8,128)(2,1)}, u32[]{:S(2)}) copy-start(bf16[128,4096]{1,0:T(8,128)(2,1)} %q_ref.9) | copy-start | bytes 3145732
  63.3 32.0 %copy-start.19 = (bf16[128,1024]{1,0:T(8,128)(2,1)}, bf16[128,1024]{1,0:T(8,128)(2,1)S(1)}, u32[]{:S(2)}) copy-start(bf16[128,1024]{1,0:T(8,128)(2,1)S(1)} %collective-permute-done.23.rest_0_) | copy-start | bytes 786436
  63.3 17.0 %collective-permute-start.15 = (bf16[2,128,1024]{2,1,0:T(8,128)(2,1)}, bf16[2,128,1024]{2,1,0:T(8,128)(2,1)}, u32[]{:S(2)}, u32[]{:S(2)}) collective-permute-start(bf16[2,128,1024]{2,1,0:T(8,128)(2,1)} %pad_maximum_fusion.2), channel_id=1, source_target_pairs={{0,2},{1,3},{8,10},{9,11},{16,18},{17,19},{24,26},{25,27}} | collective-permute-start | bytes 1572872 | tf_op jit(solution)/shard_map/ppermute | solution.py:363
  64.6 26.9 %collective-permute-start.9 = (bf16[2,128,1024]{2,1,0:T(8,128)(2,1)}, bf16[2,128,1024]{2,1,0:T(8,128)(2,1)}, u32[]{:S(2)}, u32[]{:S(2)}) collective-permute-start(bf16[2,128,1024]{2,1,0:T(8,128)(2,1)} %pad_maximum_fusion.1), channel_id=1, source_target_pairs={{0,2},{1,3},{8,10},{9,11},{16,18},{17,19},{24,26},{25,27}} | collective-permute-start | bytes 1572872 | tf_op jit(solution)/shard_map/ppermute | solution.py:363
  67.2 31.5 %collective-permute-start.22 = (bf16[2,128,1024]{2,1,0:T(8,128)(2,1)}, bf16[2,128,1024]{2,1,0:T(8,128)(2,1)}, u32[]{:S(2)}, u32[]{:S(2)}) collective-permute-start(bf16[2,128,1024]{2,1,0:T(8,128)(2,1)} %collective-permute-done.21.g_ref), channel_id=1, source_target_pairs={{2,3},{3,2},{10,11},{11,10},{18,19},{19,18},{26,27},{27,26}} | collective-permute-start | bytes 1572872 | tf_op jit(solution)/shard_map/ppermute | solution.py:364
  80.3 40.5 %collective-permute-start.3 = (bf16[2,128,1024]{2,1,0:T(8,128)(2,1)}, bf16[2,128,1024]{2,1,0:T(8,128)(2,1)}, u32[]{:S(2)}, u32[]{:S(2)}) collective-permute-start(bf16[2,128,1024]{2,1,0:T(8,128)(2,1)} %pad_maximum_fusion), channel_id=1, source_target_pairs={{0,2},{1,3},{8,10},{9,11},{16,18},{17,19},{24,26},{25,27}} | collective-permute-start | bytes 1572872 | tf_op jit(solution)/shard_map/ppermute | solution.py:363
  91.5 30.6 %collective-permute-start.16 = (bf16[2,128,1024]{2,1,0:T(8,128)(2,1)}, bf16[2,128,1024]{2,1,0:T(8,128)(2,1)}, u32[]{:S(2)}, u32[]{:S(2)}) collective-permute-start(bf16[2,128,1024]{2,1,0:T(8,128)(2,1)} %collective-permute-done.15.g_ref), channel_id=1, source_target_pairs={{2,3},{3,2},{10,11},{11,10},{18,19},{19,18},{26,27},{27,26}} | collective-permute-start | bytes 1572872 | tf_op jit(solution)/shard_map/ppermute | solution.py:364
  95.2 88.5 %all-to-all-start.1 = ((f32[8,64,128]{2,1,0:T(8,128)}), f32[8,64,128]{2,1,0:T(8,128)S(1)}, u32[]{:S(2)}, u32[]{:S(2)}) async-start(f32[8,64,128]{2,1,0:T(8,128)} %bitcast_dynamic-update-slice_fusion), calls=%async_computation.1 | async-start | bytes 524288 | tf_op jit(solution)/shard_map/all_to_all | solution.py:179
  98.7 19.5 %collective-permute-start.17 = (bf16[128,1024]{1,0:T(8,128)(2,1)}, bf16[128,1024]{1,0:T(8,128)(2,1)S(1)}, u32[]{:S(2)}, u32[]{:S(2)}) collective-permute-start(bf16[128,1024]{1,0:T(8,128)(2,1)} %get-tuple-element.45), channel_id=1, source_target_pairs={{4,2},{5,3},{6,4},{7,5},{12,10},{13,11},{14,12},{15,13},{20,18},{2... | collective-permute-start | bytes 786440 | tf_op jit(solution)/shard_map/ppermute | solution.py:366
  100.0 19.5 %collective-permute-start.18 = (bf16[128,1024]{1,0:T(8,128)(2,1)}, bf16[128,1024]{1,0:T(8,128)(2,1)S(1)}, u32[]{:S(2)}, u32[]{:S(2)}) collective-permute-start(bf16[128,1024]{1,0:T(8,128)(2,1)} %get-tuple-element.45), channel_id=1, source_target_pairs={{6,2},{7,3},{14,10},{15,11},{22,18},{23,19},{30,26},{31,27}} | collective-permute-start | bytes 786440 | tf_op jit(solution)/shard_map/ppermute | solution.py:366
  101.3 43.9 %collective-permute-start.10 = (bf16[2,128,1024]{2,1,0:T(8,128)(2,1)}, bf16[2,128,1024]{2,1,0:T(8,128)(2,1)S(1)}, u32[]{:S(2)}, u32[]{:S(2)}) collective-permute-start(bf16[2,128,1024]{2,1,0:T(8,128)(2,1)} %collective-permute-done.9.g_ref), channel_id=1, source_target_pairs={{2,3},{3,2},{10,11},{11,10},{18,19},{19,18},{26,27},{27,26}} | collective-permute-start | bytes 1572872 | tf_op jit(solution)/shard_map/ppermute | solution.py:364
  104.6 13.5 %copy-start.38 = (bf16[128,1024]{1,0:T(8,128)(2,1)S(1)}, bf16[128,1024]{1,0:T(8,128)(2,1)}, u32[]{:S(2)}) copy-start(bf16[128,1024]{1,0:T(8,128)(2,1)} %get-tuple-element.46) | copy-start | bytes 786436
  104.6 16.2 %copy-start.37 = (bf16[128,1024]{1,0:T(8,128)(2,1)S(1)}, bf16[128,1024]{1,0:T(8,128)(2,1)}, u32[]{:S(2)}) copy-start(bf16[128,1024]{1,0:T(8,128)(2,1)} %get-tuple-element.47) | copy-start | bytes 786436
  118.2 18.9 %collective-permute-start.11 = (bf16[128,1024]{1,0:T(8,128)(2,1)S(1)}, bf16[128,1024]{1,0:T(8,128)(2,1)S(1)}, u32[]{:S(2)}, u32[]{:S(2)}) collective-permute-start(bf16[128,1024]{1,0:T(8,128)(2,1)S(1)} %copy-done.38), channel_id=1, source_target_pairs={{4,2},{5,3},{6,4},{7,5},{12,10},{13,11},{14,12},{15,13},{20,18},{2... | collective-permute-start | bytes 786440 | tf_op jit(solution)/shard_map/ppermute | solution.py:366
  119.5 18.9 %collective-permute-start.12 = (bf16[128,1024]{1,0:T(8,128)(2,1)S(1)}, bf16[128,1024]{1,0:T(8,128)(2,1)S(1)}, u32[]{:S(2)}, u32[]{:S(2)}) collective-permute-start(bf16[128,1024]{1,0:T(8,128)(2,1)S(1)} %copy-done.38), channel_id=1, source_target_pairs={{6,2},{7,3},{14,10},{15,11},{22,18},{23,19},{30,26},{31,27}} | collective-permute-start | bytes 786440 | tf_op jit(solution)/shard_map/ppermute | solution.py:366
  120.8 18.9 %collective-permute-start.5 = (bf16[128,1024]{1,0:T(8,128)(2,1)S(1)}, bf16[128,1024]{1,0:T(8,128)(2,1)S(1)}, u32[]{:S(2)}, u32[]{:S(2)}) collective-permute-start(bf16[128,1024]{1,0:T(8,128)(2,1)S(1)} %copy-done.37), channel_id=1, source_target_pairs={{4,2},{5,3},{6,4},{7,5},{12,10},{13,11},{14,12},{15,13},{20,18},{2... | collective-permute-start | bytes 786440 | tf_op jit(solution)/shard_map/ppermute | solution.py:366
  122.1 39.9 %collective-permute-start.4 = (bf16[2,128,1024]{2,1,0:T(8,128)(2,1)}, bf16[2,128,1024]{2,1,0:T(8,128)(2,1)S(1)}, u32[]{:S(2)}, u32[]{:S(2)}) collective-permute-start(bf16[2,128,1024]{2,1,0:T(8,128)(2,1)} %collective-permute-done.3.g_ref), channel_id=1, source_target_pairs={{2,3},{3,2},{10,11},{11,10},{18,19},{19,18},{26,27},{27,26}} | collective-permute-start | bytes 1572872 | tf_op jit(solution)/shard_map/ppermute | solution.py:364
  137.1 22.9 %collective-permute-start.6 = (bf16[128,1024]{1,0:T(8,128)(2,1)S(1)}, bf16[128,1024]{1,0:T(8,128)(2,1)S(1)}, u32[]{:S(2)}, u32[]{:S(2)}) collective-permute-start(bf16[128,1024]{1,0:T(8,128)(2,1)S(1)} %copy-done.37), channel_id=1, source_target_pairs={{6,2},{7,3},{14,10},{15,11},{22,18},{23,19},{30,26},{31,27}} | collective-permute-start | bytes 786440 | tf_op jit(solution)/shard_map/ppermute | solution.py:366
  138.4 39.3 %collective-permute-start.25 = (bf16[128,1152]{1,0:T(8,128)(2,1)S(1)}, bf16[128,1152]{1,0:T(8,128)(2,1)S(1)}, u32[]{:S(2)}, u32[]{:S(2)}) collective-permute-start(bf16[128,1152]{1,0:T(8,128)(2,1)S(1)} %get-tuple-element.36), channel_id=1, source_target_pairs={{2,4},{3,5},{4,6},{5,7},{10,12},{11,13},{12,14},{13,15},{18,20},{1... | collective-permute-start | bytes 884744 | tf_op jit(solution)/shard_map/ppermute | solution.py:389
  139.7 40.0 %collective-permute-start.26 = (bf16[128,1152]{1,0:T(8,128)(2,1)S(1)}, bf16[128,1152]{1,0:T(8,128)(2,1)S(1)}, u32[]{:S(2)}, u32[]{:S(2)}) collective-permute-start(bf16[128,1152]{1,0:T(8,128)(2,1)S(1)} %get-tuple-element.37), channel_id=1, source_target_pairs={{2,6},{3,7},{10,14},{11,15},{18,22},{19,23},{26,30},{27,31}} | collective-permute-start | bytes 884744 | tf_op jit(solution)/shard_map/ppermute | solution.py:389
  145.2 36.5 %collective-permute-start.19 = (bf16[128,1152]{1,0:T(8,128)(2,1)S(1)}, bf16[128,1152]{1,0:T(8,128)(2,1)S(1)}, u32[]{:S(2)}, u32[]{:S(2)}) collective-permute-start(bf16[128,1152]{1,0:T(8,128)(2,1)S(1)} %get-tuple-element.32), channel_id=1, source_target_pairs={{2,4},{3,5},{4,6},{5,7},{10,12},{11,13},{12,14},{13,15},{18,20},{1... | collective-permute-start | bytes 884744 | tf_op jit(solution)/shard_map/ppermute | solution.py:389
  160.0 16.2 %copy-start.27 = (f32[128,128]{1,0:T(8,128)}, f32[128,128]{1,0:T(8,128)S(1)}, u32[]{:S(2)}) copy-start(f32[128,128]{1,0:T(8,128)S(1)} %get-tuple-element.27.refs_1_) | copy-start | bytes 196612
  160.0 40.3 %collective-permute-start.20 = (bf16[128,1152]{1,0:T(8,128)(2,1)}, bf16[128,1152]{1,0:T(8,128)(2,1)}, u32[]{:S(2)}, u32[]{:S(2)}) collective-permute-start(bf16[128,1152]{1,0:T(8,128)(2,1)} %get-tuple-element.33), channel_id=1, source_target_pairs={{2,6},{3,7},{10,14},{11,15},{18,22},{19,23},{26,30},{27,31}} | collective-permute-start | bytes 884744 | tf_op jit(solution)/shard_map/ppermute | solution.py:389
  162.0 41.5 %collective-permute-start.13 = (bf16[128,1152]{1,0:T(8,128)(2,1)}, bf16[128,1152]{1,0:T(8,128)(2,1)}, u32[]{:S(2)}, u32[]{:S(2)}) collective-permute-start(bf16[128,1152]{1,0:T(8,128)(2,1)} %get-tuple-element.28), channel_id=1, source_target_pairs={{2,4},{3,5},{4,6},{5,7},{10,12},{11,13},{12,14},{13,15},{18,20},{1... | collective-permute-start | bytes 884744 | tf_op jit(solution)/shard_map/ppermute | solution.py:389
  178.4 25.1 %collective-permute-start.14 = (bf16[128,1152]{1,0:T(8,128)(2,1)}, bf16[128,1152]{1,0:T(8,128)(2,1)S(1)}, u32[]{:S(2)}, u32[]{:S(2)}) collective-permute-start(bf16[128,1152]{1,0:T(8,128)(2,1)} %get-tuple-element.29), channel_id=1, source_target_pairs={{2,6},{3,7},{10,14},{11,15},{18,22},{19,23},{26,30},{27,31}} | collective-permute-start | bytes 884744 | tf_op jit(solution)/shard_map/ppermute | solution.py:389
  180.4 26.3 %collective-permute-start.7 = (bf16[128,1152]{1,0:T(8,128)(2,1)}, bf16[128,1152]{1,0:T(8,128)(2,1)S(1)}, u32[]{:S(2)}, u32[]{:S(2)}) collective-permute-start(bf16[128,1152]{1,0:T(8,128)(2,1)} %get-tuple-element.24), channel_id=1, source_target_pairs={{2,4},{3,5},{4,6},{5,7},{10,12},{11,13},{12,14},{13,15},{18,20},{1... | collective-permute-start | bytes 884744 | tf_op jit(solution)/shard_map/ppermute | solution.py:389
  182.4 24.3 %collective-permute-start.8 = (bf16[128,1152]{1,0:T(8,128)(2,1)}, bf16[128,1152]{1,0:T(8,128)(2,1)S(1)}, u32[]{:S(2)}, u32[]{:S(2)}) collective-permute-start(bf16[128,1152]{1,0:T(8,128)(2,1)} %get-tuple-element.25), channel_id=1, source_target_pairs={{2,6},{3,7},{10,14},{11,15},{18,22},{19,23},{26,30},{27,31}} | collective-permute-start | bytes 884744 | tf_op jit(solution)/shard_map/ppermute | solution.py:389
  189.4 8.2 %copy-start.14 = (bf16[128,1152]{1,0:T(8,128)(2,1)S(1)}, bf16[128,1152]{1,0:T(8,128)(2,1)}, u32[]{:S(2)}) copy-start(bf16[128,1152]{1,0:T(8,128)(2,1)} %copy-done.13) | copy-start | bytes 884740
  189.4 8.2 %copy-start.18 = (bf16[128,1152]{1,0:T(8,128)(2,1)S(1)}, bf16[128,1152]{1,0:T(8,128)(2,1)}, u32[]{:S(2)}) copy-start(bf16[128,1152]{1,0:T(8,128)(2,1)} %copy-done.17) | copy-start | bytes 884740
  189.4 8.2 %copy-start.32 = (f32[128,1024]{1,0:T(8,128)S(1)}, f32[128,1024]{1,0:T(8,128)}, u32[]{:S(2)}) copy-start(f32[128,1024]{1,0:T(8,128)} %copy-done.31) | copy-start | bytes 1572868
  189.4 8.2 %copy-start.34 = (f32[128,128]{1,0:T(8,128)S(1)}, f32[128,128]{1,0:T(8,128)}, u32[]{:S(2)}) copy-start(f32[128,128]{1,0:T(8,128)} %copy-done.33) | copy-start | bytes 196612
  (25 other events, 39.2 us)

commit v2 on v0

v2 whole, which is shorter than its diff:
```python
import functools
import math

import jax
import jax.numpy as jnp
from jax import lax
from jax.experimental import pallas as pl
from jax.experimental.pallas import tpu as pltpu
from jax.sharding import PartitionSpec as P

HEAD_DIM = 128
LANES = 128
SUBLANES = 8
TAPS = 3
CHUNKS = 4
UNROLL = 2
NEGATIVE = -1e30
EXP_SCALE = HEAD_DIM**-0.5 * math.log2(math.e)
VMEM_LIMIT = 56 * 1024 * 1024


def params(**kwargs):
    return pltpu.CompilerParams(vmem_limit_bytes=VMEM_LIMIT, **kwargs)


def cost(microseconds):
    return pl.CostEstimate(
        flops=microseconds * 10**9, bytes_accessed=2**20, transcendentals=0
    )


def block_lanes(block):
    return slice(block * LANES, (block + 1) * LANES)


def segment_size(modes, own_blocks, blocks):
    return 2 * modes + 2 * TAPS * blocks // own_blocks


def rim_pack_kernel(modes, rate_ref, residue_ref, q_ref, k_ref, v_ref, out_ref):
    own_blocks = rate_ref.shape[0] // LANES
    blocks = q_ref.shape[1] // LANES
    share = 2 * TAPS * blocks // own_blocks
    size = 2 * modes + share
    for block in range(own_blocks):
        rows = slice(block * LANES, (block + 1) * LANES)
        fill = jnp.zeros((LANES, LANES - 2 * modes), jnp.float32)
        both = jnp.concatenate([rate_ref[rows, :], residue_ref[rows, :], fill], 1)
        out_ref[block * size : block * size + 2 * modes, :] = jnp.transpose(both)[: 2 * modes]
    for feature, ref in enumerate((q_ref, k_ref, v_ref)):
        last = ref[...].astype(jnp.float32)[ref.shape[0] - 2 :]
        for row in range(2):
            for block in range(blocks):
                place = (2 * feature + row) * blocks + block
                target = place // share * size + 2 * modes + place % share
                out_ref[target : target + 1, :] = last[row : row + 1, block_lanes(block)]


def rim_rows(shared_ref, modes, own_blocks, blocks, feature, block):
    me = lax.axis_index("ctx")
    share = 2 * TAPS * blocks // own_blocks
    size = 2 * modes + share
    before = jnp.maximum(me - 1, 0) * own_blocks
    rows = []
    for row in range(2):
        place = (2 * feature + row) * blocks + block
        target = (before + place // share) * size + 2 * modes + place % share
        rows.append(jnp.where(me == 0, 0.0, shared_ref[pl.ds(target, 1), :]))
    return rows


def short_mix(feature, rim, taps):
    two_before, one_before = rim
    row = lax.broadcasted_iota(jnp.int32, feature.shape, 0)
    one = jnp.where(row == 0, one_before, pltpu.roll(feature, 1, 0))
    two = jnp.where(row == 0, two_before, jnp.where(row == 1, one_before, pltpu.roll(feature, 2, 0)))
    return taps[0] * feature + taps[1] * one + taps[2] * two


def tap_rows(taps_ref, feature, lanes):
    return [taps_ref[feature, pl.ds(tap, 1), lanes] for tap in range(TAPS)]


def state_kernel(
    modes, own_blocks, blocks, k_ref, v_ref, shared_ref, taps_ref, y_ref, s_ref, p_scr, y_scr
):
    group = pl.program_id(0)
    rows = k_ref.shape[0]
    size = segment_size(modes, own_blocks, blocks)
    for block in range(SUBLANES):
        lanes = block_lanes(block)
        mixes = [
            short_mix(
                ref[:, lanes].astype(jnp.float32),
                rim_rows(
                    shared_ref, modes, own_blocks, blocks, feature, group * SUBLANES + block
                ),
                tap_rows(taps_ref, feature, lanes),
            )
            for feature, ref in ((1, k_ref), (2, v_ref))
        ]
        product = (mixes[0] * mixes[1]).astype(jnp.bfloat16).astype(jnp.float32)
        p_scr[pl.ds(block, rows, SUBLANES), :] = product
    first = group * SUBLANES * size
    decay = [
        jnp.exp(-shared_ref[pl.ds(first + mode, SUBLANES, size), :]) for mode in range(modes)
    ]
    residue = [
        shared_ref[pl.ds(first + modes + mode, SUBLANES, size), :] for mode in range(modes)
    ]

    def body(position, states):
        here = pl.ds(pl.multiple_of(position * SUBLANES, SUBLANES), SUBLANES)
        product = p_scr[here, :]
        states = tuple(state * rate + product for state, rate in zip(states, decay))
        terms = [state * weight for state, weight in zip(states, residue)]
        while len(terms) > 1:
            terms = [left + right for left, right in zip(terms[::2], terms[1::2])]
        y_scr[here, :] = terms[0]
        return states

    zero = jnp.zeros((SUBLANES, LANES), jnp.float32)
    states = lax.fori_loop(0, rows, body, (zero,) * modes, unroll=4)
    for mode in range(modes):
        s_ref[pl.ds(mode, SUBLANES, modes), :] = states[mode]
    for block in range(SUBLANES):
        y_ref[:, block_lanes(block)] = y_scr[pl.ds(block, rows, SUBLANES), :]


def output_kernel(
    modes, own_blocks, blocks, devices, q_ref, y_ref, shared_ref, state_ref, taps_ref, out_ref
):
    group = pl.program_id(0)
    me = lax.axis_index("ctx")
    rows = q_ref.shape[0]
    size = segment_size(modes, own_blocks, blocks)
    step = lax.broadcasted_iota(jnp.int32, (SUBLANES, LANES), 0).astype(jnp.float32) + 1.0

    def body(block, nothing):
        place = group * SUBLANES + block
        lanes = pl.ds(pl.multiple_of(block * LANES, LANES), LANES)
        rate = shared_ref[pl.ds(pl.multiple_of(place * size, SUBLANES), modes), :]
        residue = shared_ref[pl.ds(pl.multiple_of(place * size + modes, SUBLANES), modes), :]
        chunk_decay = jnp.exp(-rate * rows)
        entering = jnp.zeros((modes, LANES), jnp.float32)
        for device in range(devices - 1):
            start = pl.multiple_of((device * blocks + place) * modes, SUBLANES)
            after = entering * chunk_decay + state_ref[pl.ds(start, modes), :]
            entering = jnp.where(device < me, after, entering)
        weighted = residue * entering
        eight = jnp.exp(-rate * SUBLANES)
        terms = [
            weighted[mode : mode + 1] * jnp.exp(-rate[mode : mode + 1] * step)
            for mode in range(modes)
        ]
        eights = [jnp.broadcast_to(eight[mode : mode + 1], terms[0].shape) for mode in range(modes)]
        added = []
        for start in range(0, rows, SUBLANES):
            sums = list(terms)
            while len(sums) > 1:
                sums = [left + right for left, right in zip(sums[::2], sums[1::2])]
            added.append(sums[0])
            if start + SUBLANES < rows:
                terms = [term * decay for term, decay in zip(terms, eights)]
        smoothed = y_ref[:, lanes] + jnp.concatenate(added, 0)
        smoothed = smoothed.astype(jnp.bfloat16).astype(jnp.float32)
        mix = short_mix(
            q_ref[:, lanes].astype(jnp.float32),
            rim_rows(shared_ref, modes, own_blocks, blocks, 0, place),
            tap_rows(taps_ref, 0, lanes),
        )
        out_ref[:, lanes] = (mix * smoothed).astype(out_ref.dtype)
        return nothing

    lax.fori_loop(0, SUBLANES, body, 0)


def convolve(hyena_q, hyena_k, hyena_v, short_filter, residue, decay_rate):
    rows, channels = hyena_q.shape
    devices = lax.axis_size("ctx")
    modes = residue.shape[1]
    own_blocks = residue.shape[0] // LANES
    blocks = channels // LANES
    groups = blocks // SUBLANES
    width = SUBLANES * LANES
    size = segment_size(modes, own_blocks, blocks)
    end = rows // 16 - 1
    last_spec = pl.BlockSpec((16, channels), lambda step: (end, 0))
    own_spec = pl.BlockSpec(residue.shape, lambda step: (0, 0))
    own_shared = pl.pallas_call(
        functools.partial(rim_pack_kernel, modes),
        grid=(1,),
        in_specs=[own_spec] * 2 + [last_spec] * 3,
        out_specs=pl.BlockSpec((own_blocks * size, LANES), lambda step: (0, 0)),
        out_shape=jax.ShapeDtypeStruct((own_blocks * size, LANES), jnp.float32),
        compiler_params=params(),
        cost_estimate=cost(1),
        name="conv_pack",
    )(decay_rate, residue, hyena_q, hyena_k, hyena_v)
    shared = lax.all_gather(own_shared, "ctx", axis=0, tiled=True)
    feature_spec = pl.BlockSpec((rows, width), lambda group: (0, group))
    shared_spec = pl.BlockSpec((blocks * size, LANES), lambda group: (0, 0))
    taps_spec = pl.BlockSpec((TAPS, TAPS, width), lambda group: (0, 0, group))
    positions = pltpu.VMEM((rows * SUBLANES, LANES), jnp.float32)
    local_result, state = pl.pallas_call(
        functools.partial(state_kernel, modes, own_blocks, blocks),
        grid=(groups,),
        in_specs=[feature_spec, feature_spec, shared_spec, taps_spec],
        out_specs=[
            feature_spec,
            pl.BlockSpec((SUBLANES * modes, LANES), lambda group: (group, 0)),
        ],
        out_shape=[
            jax.ShapeDtypeStruct((rows, channels), jnp.float32),
            jax.ShapeDtypeStruct((blocks * modes, LANES), jnp.float32),
        ],
        scratch_shapes=[positions, positions],
        compiler_params=params(),
        cost_estimate=cost(8),
        name="conv_state",
    )(hyena_k, hyena_v, shared, short_filter)
    states = lax.all_gather(state, "ctx", axis=0, tiled=True)
    return pl.pallas_call(
        functools.partial(output_kernel, modes, own_blocks, blocks, devices),
        grid=(groups,),
        in_specs=[
            feature_spec,
            feature_spec,
            shared_spec,
            pl.BlockSpec(states.shape, lambda group: (0, 0)),
            taps_spec,
        ],
        out_specs=feature_spec,
        out_shape=jax.ShapeDtypeStruct((rows, channels), jnp.bfloat16),
        compiler_params=params(),
        cost_estimate=cost(5),
        name="conv_output",
    )(hyena_q, local_result, shared, states, short_filter)


def head_slice(head, rows=HEAD_DIM):
    return pl.ds(pl.multiple_of(head * rows, rows), rows)


def among(me, members):
    return functools.reduce(jnp.logical_or, [me == member for member in members])


def plan_moves(devices):
    quads = devices // 4
    transfers = [[(devices - 1, devices - 3)]]
    for distance in range(1, quads):
        if distance > len(transfers):
            transfers.append([])
        for quad in range(distance, quads):
            target = 4 * (quad - distance) + 2
            transfers[distance - 1] += [(4 * quad, target), (4 * quad + 2, target + 1)]
    return transfers


def soft(query, keys, values, mask=None):
    scores = lax.dot_general(
        query, keys, (((1,), (1,)), ((), ())), preferred_element_type=jnp.float32
    )
    if mask is not None:
        scores = jnp.where(mask, scores, NEGATIVE)
    top = jnp.max(scores, axis=1, keepdims=True) * EXP_SCALE
    expo = jnp.exp2(scores * EXP_SCALE - top).astype(jnp.bfloat16)
    mixed = jnp.dot(expo, values, preferred_element_type=jnp.float32)
    total = mixed[:, HEAD_DIM:]
    return mixed[:, :HEAD_DIM] / total, top + jnp.log2(total)


def key_pack_kernel(k_ref, v_ref, *outs):
    heads = outs[0].shape[0] // 2 // HEAD_DIM
    for index, out in enumerate(outs):
        for which, ref in enumerate((k_ref, v_ref)):
            for head in range(heads):
                row = (which * heads + head) * HEAD_DIM
                out[row : row + HEAD_DIM, :] = ref[:, block_lanes(index * heads + head)]


def query_pack_kernel(q_ref, qs_ref, *outs):
    rows = q_ref.shape[0]
    heads = outs[0].shape[0] // 2 // rows
    odd = lax.axis_index("ctx") % 2
    for index, out in enumerate(outs):
        for head in range(heads):
            for ref, half in ((q_ref, odd), (qs_ref, 1 - odd)):
                place = pl.ds(pl.multiple_of((2 * head + half) * rows, rows), rows)
                out[place, :] = ref[:, block_lanes(index * heads + head)]


def tail_rows(heads):
    return -(-3 * heads // 16) * 16


def partial_kernel(transfers, upper, heads, *refs):
    count = len(transfers)
    q_ref, k_ref, v_ref, kp_ref, vp_ref, g_ref, gp_ref = refs[:7]
    ask_refs = refs[7 : 7 + count]
    own_ref, lse_ref = refs[7 + count : 9 + count]
    answer_refs = refs[9 + count :]
    me = lax.axis_index("ctx")
    rows = q_ref.shape[0]
    tail = tail_rows(heads)

    def key_value(head, with_quad):
        cut = head_slice(head)
        keys = [kp_ref[:, cut], k_ref[:, cut]]
        values = [vp_ref[:, cut], v_ref[:, cut]]
        if with_quad:
            value_cut = head_slice(heads + head)
            keys = [g_ref[cut, :], gp_ref[cut, :]] + keys
            values = [g_ref[value_cut, :], gp_ref[value_cut, :]] + values
        values = jnp.concatenate(values, 0)
        return jnp.concatenate(keys, 0), jnp.concatenate([values, jnp.ones_like(values)], 1)

    def run(with_quad):
        key_count = rows * (4 if with_quad else 2)
        row = lax.broadcasted_iota(jnp.int32, (rows, key_count), 0)
        column = lax.broadcasted_iota(jnp.int32, (rows, key_count), 1)
        column = column - (key_count - 2 * rows)
        partner_limit = jnp.where(me % 2 == 1, rows, 0)
        mask = (column < partner_limit) | ((column >= rows) & (column - rows <= row))
        lanes = lax.broadcasted_iota(jnp.int32, (rows, LANES), 1)

        def own_body(head, sums):
            keys, values = key_value(head, with_quad)
            mixed, lse = soft(q_ref[:, head_slice(head)], keys, values, mask)
            own_ref[:, head_slice(head)] = mixed
            return jnp.where(lanes == head, lse, sums)

        zeros = jnp.zeros((rows, LANES), jnp.float32)
        lse_ref[...] = lax.fori_loop(0, heads, own_body, zeros, unroll=UNROLL)

        def answer(index):
            lanes = lax.broadcasted_iota(jnp.int32, (2 * rows, LANES), 1)

            def body(head, sums):
                keys, values = key_value(head, with_quad)
                place = head_slice(head, 2 * rows)
                mixed, lse = soft(ask_refs[index][place, :], keys, values)
                answer_refs[index][place, :] = mixed.astype(jnp.bfloat16)
                first = lse.astype(jnp.bfloat16).astype(jnp.float32)
                second = (lse - first).astype(jnp.bfloat16).astype(jnp.float32)
                sums = jnp.where(lanes == head, first, sums)
                sums = jnp.where(lanes == heads + head, second, sums)
                return jnp.where(lanes == 2 * heads + head, lse - first - second, sums)

            zeros = jnp.zeros((2 * rows, LANES), jnp.float32)
            sums = lax.fori_loop(0, heads, body, zeros, unroll=UNROLL)
            for half in range(2):
                part = jnp.transpose(sums[half * rows : (half + 1) * rows])[:tail]
                start = 2 * heads * rows + half * tail
                answer_refs[index][start : start + tail, :] = part.astype(jnp.bfloat16)

        for index, pairs in enumerate(transfers):
            asked = [target for _, target in pairs if (target in upper) == with_quad]
            if asked:
                pl.when(among(me, asked))(functools.partial(answer, index))

    if upper:
        pl.when(among(me, upper))(functools.partial(run, True))
        pl.when(jnp.logical_not(among(me, upper)))(functools.partial(run, False))
    else:
        run(False)


def merge_kernel(transfers, heads, chunks, onto, *refs):
    per_chunk = 2 + 2 * len(transfers)
    out_ref = refs[-1]
    me = lax.axis_index("ctx")
    odd = me % 2
    rows = out_ref.shape[0]
    tail = tail_rows(heads)
    returned = [[source for source, _ in pairs] for pairs in transfers]
    with_partner = [members + [member ^ 1 for member in members] for members in returned]
    answered = among(me, sorted(set(sum(with_partner, []))))
    for position in range(chunks):
        own_ref, lse_ref, *others = refs[position * per_chunk : (position + 1) * per_chunk]
        base = position * heads * HEAD_DIM

        @pl.when(answered)
        def _():
            valid, sums = [], []
            for index, ref in enumerate(others):
                members = returned[index // 2]
                if index % 2:
                    members = [member ^ 1 for member in members]
                valid.append(among(me, members))
                start = pl.multiple_of(2 * heads * rows + odd * tail, 16)
                part = ref[pl.ds(start, tail), :].astype(jnp.float32)
                part = part[:heads] + part[heads : 2 * heads] + part[2 * heads : 3 * heads]
                fill = jnp.zeros((LANES - heads, rows), jnp.float32)
                sums.append(jnp.transpose(jnp.concatenate([part, fill], 0)))
            for head in range(heads):
                cut = block_lanes(head)
                logs = [lse_ref[:, head : head + 1]]
                mixed = [own_ref[:, cut]]
                for index, ref in enumerate(others):
                    logs.append(jnp.where(valid[index], sums[index][:, head : head + 1], NEGATIVE))
                    place = pl.ds(pl.multiple_of((2 * head + odd) * rows, rows), rows)
                    part = ref[place, :].astype(jnp.float32)
                    mixed.append(jnp.where(valid[index], part, 0.0))
                top = functools.reduce(jnp.maximum, logs)
                weights = [jnp.exp2(part - top) for part in logs]
                total = functools.reduce(jnp.add, weights)
                terms = [part * (weight / total) for part, weight in zip(mixed, weights)]
                out_ref[:, base + head * HEAD_DIM : base + (head + 1) * HEAD_DIM] = (
                    functools.reduce(jnp.add, terms).astype(out_ref.dtype)
                )

        @pl.when(jnp.logical_not(answered))
        def _():
            out_ref[:, base : base + heads * HEAD_DIM] = own_ref[...].astype(out_ref.dtype)


def attend(query, key, value):
    rows, columns = query.shape
    devices = lax.axis_size("ctx")
    quads = devices // 4
    transfers = plan_moves(devices)
    width = columns // CHUNKS
    heads = width // HEAD_DIM
    upper = [4 * quad + 2 + core for quad in range(quads - 1) for core in range(2)]
    gathers = [(who - 2, who) for who in upper]
    swap = [(index, index ^ 1) for index in range(devices)]

    def whole(shape):
        return pl.BlockSpec(shape, lambda step: (0,) * len(shape))

    def chunk_spec(chunk):
        return pl.BlockSpec((rows, width), lambda step: (0, chunk))

    query_swapped = lax.ppermute(query, "ctx", swap)
    key_swapped = lax.ppermute(key, "ctx", swap)
    value_swapped = lax.ppermute(value, "ctx", swap)
    kv_shape = (2 * width, HEAD_DIM)
    key_packs = pl.pallas_call(
        key_pack_kernel,
        grid=(1,),
        in_specs=[whole((rows, columns))] * 2,
        out_specs=[whole(kv_shape)] * CHUNKS,
        out_shape=[jax.ShapeDtypeStruct(kv_shape, jnp.bfloat16)] * CHUNKS,
        compiler_params=params(),
        cost_estimate=cost(3),
        name="key_pack",
    )(key, value)
    ask_shape = (2 * heads * rows, HEAD_DIM)
    query_packs = pl.pallas_call(
        query_pack_kernel,
        grid=(1,),
        in_specs=[whole((rows, columns))] * 2,
        out_specs=[whole(ask_shape)] * CHUNKS,
        out_shape=[jax.ShapeDtypeStruct(ask_shape, jnp.bfloat16)] * CHUNKS,
        compiler_params=params(),
        cost_estimate=cost(3),
        name="query_pack",
    )(query, query_swapped)
    asks, quad_kv = [], []
    for chunk in range(CHUNKS):
        arrived = lax.ppermute(key_packs[chunk], "ctx", gathers)
        asks.append([lax.ppermute(query_packs[chunk], "ctx", pairs) for pairs in transfers])
        quad_kv.append([arrived, lax.ppermute(arrived, "ctx", swap)])

    answer_shape = (2 * heads * rows + 2 * tail_rows(heads), HEAD_DIM)
    parts = []
    for chunk in range(CHUNKS):
        own, lse, *answers = pl.pallas_call(
            functools.partial(partial_kernel, transfers, upper, heads),
            grid=(1,),
            in_specs=[chunk_spec(chunk)] * 5
            + [whole(kv_shape)] * 2
            + [whole(ask_shape)] * len(transfers),
            out_specs=[whole((rows, width)), whole((rows, LANES))]
            + [whole(answer_shape)] * len(transfers),
            out_shape=[
                jax.ShapeDtypeStruct((rows, width), jnp.float32),
                jax.ShapeDtypeStruct((rows, LANES), jnp.float32),
            ]
            + [jax.ShapeDtypeStruct(answer_shape, jnp.bfloat16)] * len(transfers),
            compiler_params=params(),
            cost_estimate=cost(4),
            name="att_partial",
        )(query, key, value, key_swapped, value_swapped, *quad_kv[chunk], *asks[chunk])
        parts.append([own, lse])
        for answer, pairs in zip(answers, transfers):
            back = lax.ppermute(answer, "ctx", [(target, source) for source, target in pairs])
            parts[-1] += [back, lax.ppermute(back, "ctx", swap)]

    def merge(result, first, count):
        operands = sum(parts[first : first + count], [])
        specs = [whole(operand.shape) for operand in operands]
        aliases = {}
        if result is not None:
            aliases = {len(operands): 0}
            operands.append(result)
            specs.append(pl.BlockSpec(memory_space=pl.ANY))
        return pl.pallas_call(
            functools.partial(merge_kernel, transfers, heads, count, result is not None),
            grid=(1,),
            in_specs=specs,
            out_specs=pl.BlockSpec((rows, count * width), lambda step: (0, first // count)),
            out_shape=jax.ShapeDtypeStruct((rows, columns), jnp.bfloat16),
            input_output_aliases=aliases,
            compiler_params=params(),
            cost_estimate=cost(2),
            name="att_merge",
        )(*operands)

    if CHUNKS == 1:
        return merge(None, 0, 1)
    result = merge(None, 0, CHUNKS - 1)
    return merge(result, CHUNKS - 1, 1)


def local(
    hyena_q, hyena_k, hyena_v, short_filter, residue, decay_rate, att_query, att_key, att_value
):
    att_out = attend(att_query, att_key, att_value)
    hyena_out = convolve(hyena_q, hyena_k, hyena_v, short_filter, residue, decay_rate)
    return (hyena_out, att_out)


def solution(mesh):
    rows = P(("dp", "ctx"), None)
    shared = P("ctx", None)
    return jax.shard_map(
        local,
        mesh=mesh,
        in_specs=(rows, rows, rows, P(), shared, shared, rows, rows, rows),
        out_specs=(rows, rows),
        check_vma=False,
    )
```

time: 399 us -> 183 us (0.46)
  the two profiles are of different devices: /device:TPU:0 before, /device:TPU:17 now
where the time goes in v2:
time: 183 us; the launch traced here: 181 us
  starting transfers between devices  69.8 us (38%)
  Pallas kernels  60.7 us (33%)
  waiting for transfers between devices  29.1 us (16%)
  between operations  14.4 us (8%)
  local copies, waits for them, and re-layouts  7.46 us (4%)
    ppermute x4, starting transfers between devices, attend(): quad_kv.append([arrived, lax.ppermute(arrived, 'ctx', swap)])  30 us
    pallas_call x4, Pallas kernels, attend(): pl.pallas_call(functools.partial(partial_kernel, transfers, upper, heads)...  26.6 us
    all_gather x1, waiting for transfers between devices, convolve(): shared = lax.all_gather(own_shared, 'ctx', axis=0, tiled=True)  23.3 us
    ppermute x4, starting transfers between devices, attend(): parts[-1] += [back, lax.ppermute(back, 'ctx', swap)]  20.3 us
    pallas_call x1, Pallas kernels, convolve(): pl.pallas_call(functools.partial(state_kernel, modes, own_blocks, blocks)...  10.2 us
    ppermute x4, starting transfers between devices, attend(): lax.ppermute(answer, 'ctx', [(target, source) for source, target in pairs])  7.99 us
    pallas_call x2, Pallas kernels, merge(): pl.pallas_call(functools.partial(merge_kernel, transfers, heads, count, r...  7.66 us
    pallas_call x1, Pallas kernels, convolve(): pl.pallas_call(functools.partial(output_kernel, modes, own_blocks, blocks...  7.58 us
  transfers between devices with their start and end apart: 25, of which 4 were waited for; matrix products, arithmetic and copies ran while one was open for 0% of the time, Pallas kernels for 28%

profile of v2, /device:TPU:17, one launch (start us, length us, event | category | flops | bytes accessed | tf_op | source)
XLA Modules:
  0.0 181.5 jit_solution(4148869443768153448)
XLA Ops:
  7.2 1.6 copy.12.rate_ref
  8.8 1.6 copy.13.residue_ref
  10.4 2.1 %conv_pack.1 = f32[320,128]{1,0:T(8,128)} custom-call(f32[512,16]{1,0:T(8,128)} %copy.12.rate_ref, f32[512,16]{1,0:T(8,128)} %copy.13.residue_ref, bf16[128,4096]{1,0:T(8,128)(2,1)} %q_ref.4, bf16[128,4096]{1,0:T(8,128)(2,1)} %k_ref.4, bf16[128,4096]{1,0:T(8,128)(2,1)} %v_ref.4), custom_call_target="tpu_custom_call" | custom-call | flops 1000000000 | bytes 1048576 | tf_op jit(solution)/shard_map/conv_pack/pallas_call | solution.py:190
  12.5 0.0 all-gather.5.cloned.1.call-start
  12.6 3.4 %key_pack.1 = (bf16[2048,128]{1,0:T(8,128)(2,1)}, bf16[2048,128]{1,0:T(8,128)(2,1)}, bf16[2048,128]{1,0:T(8,128)(2,1)}, bf16[2048,128]{1,0:T(8,128)(2,1)}) custom-call(bf16[128,4096]{1,0:T(8,128)(2,1)} %refs_1_.7, bf16[128,4096]{1,0:T(8,128)(2,1)} %refs_2_.7), custom_call_target="tpu_custom_call" | custom-call | flops 3000000000 | bytes 1048576 | tf_op jit(solution)/shard_map/key_pack/pallas_call | solution.py:440
  15.9 1.5 collective-permute-start.8
  17.4 0.7 collective-permute-start.4
  18.1 0.1 collective-permute-start
  18.1 0.4 collective-permute-start.1
  18.6 1.5 collective-permute-start.13
  20.0 1.5 collective-permute-start.18
  21.5 23.3 %all-gather.3.cloned.1.call-done.shared_ref = f32[2560,128]{1,0:T(8,128)} async-done(((f32[320,128]{1,0:T(8,128)}), f32[2560,128]{1,0:T(8,128)}) %all-gather.3.cloned.1.call-update) | async-done | bytes 1310736 | tf_op jit(solution)/shard_map/all_gather | solution.py:200
  44.8 10.2 %conv_state.1 = (f32[128,4096]{1,0:T(8,128)}, f32[512,128]{1,0:T(8,128)}) custom-call(bf16[128,4096]{1,0:T(8,128)(2,1)} %k_ref.4, bf16[128,4096]{1,0:T(8,128)(2,1)} %v_ref.4, f32[2560,128]{1,0:T(8,128)} %all-gather.3.cloned.1.call-done.shared_ref, f32[3,3,4096]{2,1,0:T(4,128)} %taps_ref.3), custom_call_target="tpu_custom_call" | custom-call | flops 8000000000 | bytes 1048576 | tf_op jit(solution)/shard_map/conv_state/pallas_call | solution.py:205
  55.0 0.7 collective-permute-start.2
  55.7 0.3 collective-permute-start.9
  56.0 3.3 %query_pack.1 = (bf16[2048,128]{1,0:T(8,128)(2,1)}, bf16[2048,128]{1,0:T(8,128)(2,1)}, bf16[2048,128]{1,0:T(8,128)(2,1)}, bf16[2048,128]{1,0:T(8,128)(2,1)}) custom-call(bf16[128,4096]{1,0:T(8,128)(2,1)} %refs_0_.7, bf16[128,4096]{1,0:T(8,128)(2,1)} %collective-permute-done.4.qs_ref), custom_call_target="tpu_custom_call" | custom-call | flops 3000000000 | bytes 1048576 | tf_op jit(solution)/shard_map/query_pack/pallas_call | solution.py:451
  59.3 1.3 collective-permute-start.10
  60.6 9.6 %collective-permute-start.14 = (bf16[2048,128]{1,0:T(8,128)(2,1)}, bf16[2048,128]{1,0:T(8,128)(2,1)S(1)}, u32[]{:S(2)}, u32[]{:S(2)}) collective-permute-start(bf16[2048,128]{1,0:T(8,128)(2,1)} %collective-permute-done.13.refs_5_), channel_id=1, source_target_pairs={{0,1},{1,0},{2,3},{3,2},{4,5},{5,4},{6,7},{7,6},{8,9},{9,8},{10,11... | collective-permute-start | bytes 1572872 | tf_op jit(solution)/shard_map/ppermute | solution.py:465
  70.2 1.3 collective-permute-start.15
  71.5 19.9 %collective-permute-start.19 = (bf16[2048,128]{1,0:T(8,128)(2,1)}, bf16[2048,128]{1,0:T(8,128)(2,1)S(1)}, u32[]{:S(2)}, u32[]{:S(2)}) collective-permute-start(bf16[2048,128]{1,0:T(8,128)(2,1)} %collective-permute-done.18.refs_5_), channel_id=1, source_target_pairs={{0,1},{1,0},{2,3},{3,2},{4,5},{5,4},{6,7},{7,6},{8,9},{9,8},{10,11... | collective-permute-start | bytes 1572872 | tf_op jit(solution)/shard_map/ppermute | solution.py:465
  91.5 0.1 collective-permute-start.3
  91.6 1.4 collective-permute-start.20
  93.0 6.7 %att_partial.5 = (f32[128,1024]{1,0:T(8,128)}, f32[128,128]{1,0:T(8,128)}, bf16[2112,128]{1,0:T(8,128)(2,1)}) custom-call(bf16[128,4096]{1,0:T(8,128)(2,1)} %refs_0_.7, bf16[128,4096]{1,0:T(8,128)(2,1)} %refs_1_.7, bf16[128,4096]{1,0:T(8,128)(2,1)} %refs_2_.7, bf16[128,4096]{1,0:T(8,128)(2,1)} %collective-permute-done.refs_3_, ...), custom_call_target="tpu_custom_call" | custom-call | flops 4000000000 | bytes 1048576 | tf_op jit(solution)/shard_map/att_partial/pallas_call | solution.py:470
  99.7 1.3 collective-permute-start.5
  101.0 4.0 %collective-permute-start.11 = (bf16[2112,128]{1,0:T(8,128)(2,1)}, bf16[2112,128]{1,0:T(8,128)(2,1)S(1)}, u32[]{:S(2)}, u32[]{:S(2)}) collective-permute-start(bf16[2112,128]{1,0:T(8,128)(2,1)} %get-tuple-element.35), channel_id=1, source_target_pairs={{5,7},{2,4},{3,6},{13,15},{10,12},{11,14},{21,23},{18,20},{19,22},... | collective-permute-start | bytes 1622024 | tf_op jit(solution)/shard_map/ppermute | solution.py:489
  105.1 6.7 %att_partial.6 = (f32[128,1024]{1,0:T(8,128)}, f32[128,128]{1,0:T(8,128)}, bf16[2112,128]{1,0:T(8,128)(2,1)}) custom-call(bf16[128,4096]{1,0:T(8,128)(2,1)} %refs_0_.7, bf16[128,4096]{1,0:T(8,128)(2,1)} %refs_1_.7, bf16[128,4096]{1,0:T(8,128)(2,1)} %refs_2_.7, bf16[128,4096]{1,0:T(8,128)(2,1)} %collective-permute-done.refs_3_, ...), custom_call_target="tpu_custom_call" | custom-call | flops 4000000000 | bytes 1048576 | tf_op jit(solution)/shard_map/att_partial/pallas_call | solution.py:470
  111.8 1.3 collective-permute-start.16
  113.1 0.8 copy-done.19
  113.9 6.7 %att_partial.7 = (f32[128,1024]{1,0:T(8,128)}, f32[128,128]{1,0:T(8,128)}, bf16[2112,128]{1,0:T(8,128)(2,1)}) custom-call(bf16[128,4096]{1,0:T(8,128)(2,1)} %refs_0_.7, bf16[128,4096]{1,0:T(8,128)(2,1)} %refs_1_.7, bf16[128,4096]{1,0:T(8,128)(2,1)} %refs_2_.7, bf16[128,4096]{1,0:T(8,128)(2,1)} %collective-permute-done.refs_3_, ...), custom_call_target="tpu_custom_call" | custom-call | flops 4000000000 | bytes 1048576 | tf_op jit(solution)/shard_map/att_partial/pallas_call | solution.py:470
  120.6 1.3 collective-permute-start.21
  121.9 0.1 collective-permute-done.5.refs_7_
  122.1 0.6 copy-done.13
  122.7 0.8 copy-done.17
  123.6 6.6 %att_partial.4 = (f32[128,1024]{1,0:T(8,128)}, f32[128,128]{1,0:T(8,128)}, bf16[2112,128]{1,0:T(8,128)(2,1)}) custom-call(bf16[128,4096]{1,0:T(8,128)(2,1)} %refs_0_.7, bf16[128,4096]{1,0:T(8,128)(2,1)} %refs_1_.7, bf16[128,4096]{1,0:T(8,128)(2,1)} %refs_2_.7, bf16[128,4096]{1,0:T(8,128)(2,1)} %collective-permute-done.refs_3_, ...), custom_call_target="tpu_custom_call" | custom-call | flops 4000000000 | bytes 1048576 | tf_op jit(solution)/shard_map/att_partial/pallas_call | solution.py:470
  130.2 1.3 collective-permute-start.6
  131.5 2.5 %collective-permute-start.12 = (bf16[2112,128]{1,0:T(8,128)(2,1)S(1)}, bf16[2112,128]{1,0:T(8,128)(2,1)S(1)}, u32[]{:S(2)}, u32[]{:S(2)}) collective-permute-start(bf16[2112,128]{1,0:T(8,128)(2,1)S(1)} %collective-permute-done.11.refs_2_), channel_id=1, source_target_pairs={{0,1},{1,0},{2,3},{3,2},{4,5},{5,4},{6,7},{7,6},{8,9},{9,8},{10,11... | collective-permute-start | bytes 1622024 | tf_op jit(solution)/shard_map/ppermute | solution.py:490
  134.1 0.1 collective-permute-start.17
  134.2 2.7 %collective-permute-done.21.refs_10_ = bf16[2112,128]{1,0:T(8,128)(2,1)S(1)} collective-permute-done((bf16[2112,128]{1,0:T(8,128)(2,1)}, bf16[2112,128]{1,0:T(8,128)(2,1)S(1)}, u32[]{:S(2)}, u32[]{:S(2)}) %collective-permute-start.21) | collective-permute-done | bytes 540704 | tf_op jit(solution)/shard_map/ppermute | solution.py:489
  136.9 8.8 %collective-permute-start.22 = (bf16[2112,128]{1,0:T(8,128)(2,1)S(1)}, bf16[2112,128]{1,0:T(8,128)(2,1)S(1)}, u32[]{:S(2)}, u32[]{:S(2)}) collective-permute-start(bf16[2112,128]{1,0:T(8,128)(2,1)S(1)} %collective-permute-done.21.refs_10_), channel_id=1, source_target_pairs={{0,1},{1,0},{2,3},{3,2},{4,5},{5,4},{6,7},{7,6},{8,9},{9,8},{10,11... | collective-permute-start | bytes 1622024 | tf_op jit(solution)/shard_map/ppermute | solution.py:490
  145.8 2.7 %collective-permute-done.6.refs_2_ = bf16[2112,128]{1,0:T(8,128)(2,1)S(1)} collective-permute-done((bf16[2112,128]{1,0:T(8,128)(2,1)}, bf16[2112,128]{1,0:T(8,128)(2,1)S(1)}, u32[]{:S(2)}, u32[]{:S(2)}) %collective-permute-start.6) | collective-permute-done | bytes 540704 | tf_op jit(solution)/shard_map/ppermute | solution.py:489
  148.5 8.8 %collective-permute-start.7 = (bf16[2112,128]{1,0:T(8,128)(2,1)S(1)}, bf16[2112,128]{1,0:T(8,128)(2,1)S(1)}, u32[]{:S(2)}, u32[]{:S(2)}) collective-permute-start(bf16[2112,128]{1,0:T(8,128)(2,1)S(1)} %collective-permute-done.6.refs_2_), channel_id=1, source_target_pairs={{0,1},{1,0},{2,3},{3,2},{4,5},{5,4},{6,7},{7,6},{8,9},{9,8},{10,11... | collective-permute-start | bytes 1622024 | tf_op jit(solution)/shard_map/ppermute | solution.py:490
  157.4 0.7 copy-done.7
  158.1 0.2 copy-done.8
  158.4 0.2 copy-done.10
  158.6 4.9 %att_merge.2.refs_4_ = bf16[128,4096]{1,0:T(8,128)(2,1)} custom-call(f32[128,1024]{1,0:T(8,128)} %get-tuple-element.33.refs_0_, f32[128,128]{1,0:T(8,128)} %get-tuple-element.34.refs_1_, bf16[2112,128]{1,0:T(8,128)(2,1)} %copy-done.3, bf16[2112,128]{1,0:T(8,128)(2,1)} %copy-done.7, f32[128,1024]{1,0:T(8,128)} %get-tuple-element.38.refs_4_, ...), custom_call_target="tpu_custom_call" | custom-call | flops 2000000000 | bytes 1048576 | tf_op jit(solution)/shard_map/att_merge/pallas_call | solution.py:500
  163.4 0.8 copy-done.9
  164.3 2.8 %att_merge.3 = bf16[128,4096]{1,0:T(8,128)(2,1)} custom-call(f32[128,1024]{1,0:T(8,128)} %get-tuple-element.28.refs_0_, f32[128,128]{1,0:T(8,128)} %get-tuple-element.29.refs_1_, bf16[2112,128]{1,0:T(8,128)(2,1)} %copy-done.6, bf16[2112,128]{1,0:T(8,128)(2,1)} %copy-done.9, bf16[128,4096]{1,0:T(8,128)(2,1)} %att_merge.2.refs_4_), custom_call_target="tpu_custom_call", output_to_operand_aliasing={{}: (4, {})} | custom-call | flops 2000000000 | bytes 1048576 | tf_op jit(solution)/shard_map/att_merge/pallas_call | solution.py:500
  167.1 7.6 %conv_output.1 = bf16[128,4096]{1,0:T(8,128)(2,1)} custom-call(bf16[128,4096]{1,0:T(8,128)(2,1)} %q_ref.4, f32[128,4096]{1,0:T(8,128)} %get-tuple-element.24.y_ref, f32[2560,128]{1,0:T(8,128)} %all-gather.3.cloned.1.call-done.shared_ref, f32[4096,128]{1,0:T(8,128)} %all-gather.5.cloned.1.call-done.state_ref, f32[3,3,4096]{2,1,0:T(4,128)} %taps_ref.3), custom_call_target="tpu_custom_call" | custom-call | flops 5000000000 | bytes 1048576 | tf_op jit(solution)/shard_map/conv_output/pallas_call | solution.py:223
  (59 shorter events, 0.2 us)
Async XLA Ops:
  7.2 37.6 %all-gather.3.cloned.1.call-start = ((), (), s32[]{:S(2)}) async-start(), calls=%async_computation | async-start | bytes 1474560 | tf_op jit(solution)/shard_map/all_gather | solution.py:200
  12.5 4.9 %copy-start = (bf16[128,4096]{1,0:T(8,128)(2,1)S(1)}, bf16[128,4096]{1,0:T(8,128)(2,1)}, u32[]{:S(2)}) copy-start(bf16[128,4096]{1,0:T(8,128)(2,1)} %refs_0_.7) | copy-start | bytes 3145732
  12.5 5.6 %copy-start.1 = (bf16[128,4096]{1,0:T(8,128)(2,1)S(1)}, bf16[128,4096]{1,0:T(8,128)(2,1)}, u32[]{:S(2)}) copy-start(bf16[128,4096]{1,0:T(8,128)(2,1)} %refs_1_.7) | copy-start | bytes 3145732
  12.5 5.6 %copy-start.2 = (bf16[128,4096]{1,0:T(8,128)(2,1)S(1)}, bf16[128,4096]{1,0:T(8,128)(2,1)}, u32[]{:S(2)}) copy-start(bf16[128,4096]{1,0:T(8,128)(2,1)} %refs_2_.7) | copy-start | bytes 3145732
  12.5 154.5 %all-gather.5.cloned.1.call-start = ((), (), s32[]{:S(2)}) async-start(), calls=%async_computation.1 | async-start | bytes 2359296 | tf_op jit(solution)/shard_map/all_gather | solution.py:222
  15.9 4.1 %collective-permute-start.8 = (bf16[2048,128]{1,0:T(8,128)(2,1)}, bf16[2048,128]{1,0:T(8,128)(2,1)}, u32[]{:S(2)}, u32[]{:S(2)}) collective-permute-start(bf16[2048,128]{1,0:T(8,128)(2,1)} %get-tuple-element.31), channel_id=1, source_target_pairs={{0,2},{1,3},{8,10},{9,11},{16,18},{17,19},{24,26},{25,27}} | collective-permute-start | bytes 1572872 | tf_op jit(solution)/shard_map/ppermute | solution.py:463
  17.4 38.3 %collective-permute-start.4 = (bf16[128,4096]{1,0:T(8,128)(2,1)S(1)}, bf16[128,4096]{1,0:T(8,128)(2,1)}, u32[]{:S(2)}, u32[]{:S(2)}) collective-permute-start(bf16[128,4096]{1,0:T(8,128)(2,1)S(1)} %copy-done), channel_id=1, source_target_pairs={{0,1},{1,0},{2,3},{3,2},{4,5},{5,4},{6,7},{7,6},{8,9},{9,8},{10,11... | collective-permute-start | bytes 3145736 | tf_op jit(solution)/shard_map/ppermute | solution.py:436
  18.1 53.5 %collective-permute-start = (bf16[128,4096]{1,0:T(8,128)(2,1)S(1)}, bf16[128,4096]{1,0:T(8,128)(2,1)}, u32[]{:S(2)}, u32[]{:S(2)}) collective-permute-start(bf16[128,4096]{1,0:T(8,128)(2,1)S(1)} %copy-done.1), channel_id=1, source_target_pairs={{0,1},{1,0},{2,3},{3,2},{4,5},{5,4},{6,7},{7,6},{8,9},{9,8},{10,11... | collective-permute-start | bytes 3145736 | tf_op jit(solution)/shard_map/ppermute | solution.py:437
  18.1 73.4 %collective-permute-start.1 = (bf16[128,4096]{1,0:T(8,128)(2,1)S(1)}, bf16[128,4096]{1,0:T(8,128)(2,1)}, u32[]{:S(2)}, u32[]{:S(2)}) collective-permute-start(bf16[128,4096]{1,0:T(8,128)(2,1)S(1)} %copy-done.2), channel_id=1, source_target_pairs={{0,1},{1,0},{2,3},{3,2},{4,5},{5,4},{6,7},{7,6},{8,9},{9,8},{10,11... | collective-permute-start | bytes 3145736 | tf_op jit(solution)/shard_map/ppermute | solution.py:438
  18.6 36.4 %collective-permute-start.13 = (bf16[2048,128]{1,0:T(8,128)(2,1)}, bf16[2048,128]{1,0:T(8,128)(2,1)}, u32[]{:S(2)}, u32[]{:S(2)}) collective-permute-start(bf16[2048,128]{1,0:T(8,128)(2,1)} %get-tuple-element.36), channel_id=1, source_target_pairs={{0,2},{1,3},{8,10},{9,11},{16,18},{17,19},{24,26},{25,27}} | collective-permute-start | bytes 1572872 | tf_op jit(solution)/shard_map/ppermute | solution.py:463
  20.0 39.3 %collective-permute-start.18 = (bf16[2048,128]{1,0:T(8,128)(2,1)}, bf16[2048,128]{1,0:T(8,128)(2,1)}, u32[]{:S(2)}, u32[]{:S(2)}) collective-permute-start(bf16[2048,128]{1,0:T(8,128)(2,1)} %get-tuple-element.41), channel_id=1, source_target_pairs={{0,2},{1,3},{8,10},{9,11},{16,18},{17,19},{24,26},{25,27}} | collective-permute-start | bytes 1572872 | tf_op jit(solution)/shard_map/ppermute | solution.py:463
  55.0 5.6 %collective-permute-start.2 = (bf16[2048,128]{1,0:T(8,128)(2,1)}, bf16[2048,128]{1,0:T(8,128)(2,1)S(1)}, u32[]{:S(2)}, u32[]{:S(2)}) collective-permute-start(bf16[2048,128]{1,0:T(8,128)(2,1)} %get-tuple-element.26), channel_id=1, source_target_pairs={{0,2},{1,3},{8,10},{9,11},{16,18},{17,19},{24,26},{25,27}} | collective-permute-start | bytes 1572872 | tf_op jit(solution)/shard_map/ppermute | solution.py:463
  55.7 14.5 %collective-permute-start.9 = (bf16[2048,128]{1,0:T(8,128)(2,1)}, bf16[2048,128]{1,0:T(8,128)(2,1)S(1)}, u32[]{:S(2)}, u32[]{:S(2)}) collective-permute-start(bf16[2048,128]{1,0:T(8,128)(2,1)} %collective-permute-done.8.refs_5_), channel_id=1, source_target_pairs={{0,1},{1,0},{2,3},{3,2},{4,5},{5,4},{6,7},{7,6},{8,9},{9,8},{10,11... | collective-permute-start | bytes 1572872 | tf_op jit(solution)/shard_map/ppermute | solution.py:465
  59.3 32.3 %collective-permute-start.10 = (bf16[2048,128]{1,0:T(8,128)(2,1)}, bf16[2048,128]{1,0:T(8,128)(2,1)S(1)}, u32[]{:S(2)}, u32[]{:S(2)}) collective-permute-start(bf16[2048,128]{1,0:T(8,128)(2,1)} %get-tuple-element.32), channel_id=1, source_target_pairs={{7,5},{4,2},{6,3},{15,13},{12,10},{14,11},{23,21},{20,18},{22,19},... | collective-permute-start | bytes 1572872 | tf_op jit(solution)/shard_map/ppermute | solution.py:464
  60.6 39.1 %copy-start.11 = (bf16[2048,128]{1,0:T(8,128)(2,1)}, bf16[2048,128]{1,0:T(8,128)(2,1)S(1)}, u32[]{:S(2)}) copy-start(bf16[2048,128]{1,0:T(8,128)(2,1)S(1)} %collective-permute-done.2.refs_5_) | copy-start | bytes 1572868
  60.6 39.1 %collective-permute-start.14 = (bf16[2048,128]{1,0:T(8,128)(2,1)}, bf16[2048,128]{1,0:T(8,128)(2,1)S(1)}, u32[]{:S(2)}, u32[]{:S(2)}) collective-permute-start(bf16[2048,128]{1,0:T(8,128)(2,1)} %collective-permute-done.13.refs_5_), channel_id=1, source_target_pairs={{0,1},{1,0},{2,3},{3,2},{4,5},{5,4},{6,7},{7,6},{8,9},{9,8},{10,11... | collective-permute-start | bytes 1572872 | tf_op jit(solution)/shard_map/ppermute | solution.py:465
  70.2 22.8 %copy-start.16 = (bf16[2048,128]{1,0:T(8,128)(2,1)}, bf16[2048,128]{1,0:T(8,128)(2,1)S(1)}, u32[]{:S(2)}) copy-start(bf16[2048,128]{1,0:T(8,128)(2,1)S(1)} %collective-permute-done.9.refs_6_) | copy-start | bytes 1572868
  70.2 30.8 %collective-permute-start.15 = (bf16[2048,128]{1,0:T(8,128)(2,1)}, bf16[2048,128]{1,0:T(8,128)(2,1)S(1)}, u32[]{:S(2)}, u32[]{:S(2)}) collective-permute-start(bf16[2048,128]{1,0:T(8,128)(2,1)} %get-tuple-element.37), channel_id=1, source_target_pairs={{7,5},{4,2},{6,3},{15,13},{12,10},{14,11},{23,21},{20,18},{22,19},... | collective-permute-start | bytes 1572872 | tf_op jit(solution)/shard_map/ppermute | solution.py:464
  71.5 40.2 %collective-permute-start.19 = (bf16[2048,128]{1,0:T(8,128)(2,1)}, bf16[2048,128]{1,0:T(8,128)(2,1)S(1)}, u32[]{:S(2)}, u32[]{:S(2)}) collective-permute-start(bf16[2048,128]{1,0:T(8,128)(2,1)} %collective-permute-done.18.refs_5_), channel_id=1, source_target_pairs={{0,1},{1,0},{2,3},{3,2},{4,5},{5,4},{6,7},{7,6},{8,9},{9,8},{10,11... | collective-permute-start | bytes 1572872 | tf_op jit(solution)/shard_map/ppermute | solution.py:465
  91.5 30.5 %collective-permute-start.3 = (bf16[2048,128]{1,0:T(8,128)(2,1)S(1)}, bf16[2048,128]{1,0:T(8,128)(2,1)S(1)}, u32[]{:S(2)}, u32[]{:S(2)}) collective-permute-start(bf16[2048,128]{1,0:T(8,128)(2,1)S(1)} %collective-permute-done.2.refs_5_), channel_id=1, source_target_pairs={{0,1},{1,0},{2,3},{3,2},{4,5},{5,4},{6,7},{7,6},{8,9},{9,8},{10,11... | collective-permute-start | bytes 1572872 | tf_op jit(solution)/shard_map/ppermute | solution.py:465
  91.6 1.4 copy-start.20
  91.6 8.1 %copy-start.12 = (bf16[2048,128]{1,0:T(8,128)(2,1)S(1)}, bf16[2048,128]{1,0:T(8,128)(2,1)}, u32[]{:S(2)}) copy-start(bf16[2048,128]{1,0:T(8,128)(2,1)} %get-tuple-element.27) | copy-start | bytes 1572868
  91.6 21.5 %collective-permute-start.20 = (bf16[2048,128]{1,0:T(8,128)(2,1)}, bf16[2048,128]{1,0:T(8,128)(2,1)S(1)}, u32[]{:S(2)}, u32[]{:S(2)}) collective-permute-start(bf16[2048,128]{1,0:T(8,128)(2,1)} %get-tuple-element.42), channel_id=1, source_target_pairs={{7,5},{4,2},{6,3},{15,13},{12,10},{14,11},{23,21},{20,18},{22,19},... | collective-permute-start | bytes 1572872 | tf_op jit(solution)/shard_map/ppermute | solution.py:464
  99.7 5.4 %copy-start.15 = (bf16[2048,128]{1,0:T(8,128)(2,1)}, bf16[2048,128]{1,0:T(8,128)(2,1)S(1)}, u32[]{:S(2)}) copy-start(bf16[2048,128]{1,0:T(8,128)(2,1)S(1)} %collective-permute-done.14.refs_6_) | copy-start | bytes 1572868
  99.7 22.4 %collective-permute-start.5 = (bf16[2048,128]{1,0:T(8,128)(2,1)S(1)}, bf16[2048,128]{1,0:T(8,128)(2,1)S(1)}, u32[]{:S(2)}, u32[]{:S(2)}) collective-permute-start(bf16[2048,128]{1,0:T(8,128)(2,1)S(1)} %copy-done.12), channel_id=1, source_target_pairs={{7,5},{4,2},{6,3},{15,13},{12,10},{14,11},{23,21},{20,18},{22,19},... | collective-permute-start | bytes 1572872 | tf_op jit(solution)/shard_map/ppermute | solution.py:464
  101.0 4.1 %copy-start.18 = (bf16[2048,128]{1,0:T(8,128)(2,1)}, bf16[2048,128]{1,0:T(8,128)(2,1)S(1)}, u32[]{:S(2)}) copy-start(bf16[2048,128]{1,0:T(8,128)(2,1)S(1)} %collective-permute-done.15.refs_7_) | copy-start | bytes 1572868
  101.0 30.5 %collective-permute-start.11 = (bf16[2112,128]{1,0:T(8,128)(2,1)}, bf16[2112,128]{1,0:T(8,128)(2,1)S(1)}, u32[]{:S(2)}, u32[]{:S(2)}) collective-permute-start(bf16[2112,128]{1,0:T(8,128)(2,1)} %get-tuple-element.35), channel_id=1, source_target_pairs={{5,7},{2,4},{3,6},{13,15},{10,12},{11,14},{21,23},{18,20},{19,22},... | collective-permute-start | bytes 1622024 | tf_op jit(solution)/shard_map/ppermute | solution.py:489
  111.8 1.3 copy-start.14
  111.8 22.3 %collective-permute-start.16 = (bf16[2112,128]{1,0:T(8,128)(2,1)}, bf16[2112,128]{1,0:T(8,128)(2,1)S(1)}, u32[]{:S(2)}, u32[]{:S(2)}) collective-permute-start(bf16[2112,128]{1,0:T(8,128)(2,1)} %get-tuple-element.40), channel_id=1, source_target_pairs={{5,7},{2,4},{3,6},{13,15},{10,12},{11,14},{21,23},{18,20},{19,22},... | collective-permute-start | bytes 1622024 | tf_op jit(solution)/shard_map/ppermute | solution.py:489
  113.1 0.8 copy-start.19
  120.6 16.3 %collective-permute-start.21 = (bf16[2112,128]{1,0:T(8,128)(2,1)}, bf16[2112,128]{1,0:T(8,128)(2,1)S(1)}, u32[]{:S(2)}, u32[]{:S(2)}) collective-permute-start(bf16[2112,128]{1,0:T(8,128)(2,1)} %get-tuple-element.45), channel_id=1, source_target_pairs={{5,7},{2,4},{3,6},{13,15},{10,12},{11,14},{21,23},{18,20},{19,22},... | collective-permute-start | bytes 1622024 | tf_op jit(solution)/shard_map/ppermute | solution.py:489
  121.9 0.8 copy-start.13
  122.7 0.8 copy-start.17
  130.2 18.3 %collective-permute-start.6 = (bf16[2112,128]{1,0:T(8,128)(2,1)}, bf16[2112,128]{1,0:T(8,128)(2,1)S(1)}, u32[]{:S(2)}, u32[]{:S(2)}) collective-permute-start(bf16[2112,128]{1,0:T(8,128)(2,1)} %get-tuple-element.30), channel_id=1, source_target_pairs={{5,7},{2,4},{3,6},{13,15},{10,12},{11,14},{21,23},{18,20},{19,22},... | collective-permute-start | bytes 1622024 | tf_op jit(solution)/shard_map/ppermute | solution.py:489
  131.5 25.9 %copy-start.3 = (bf16[2112,128]{1,0:T(8,128)(2,1)}, bf16[2112,128]{1,0:T(8,128)(2,1)S(1)}, u32[]{:S(2)}) copy-start(bf16[2112,128]{1,0:T(8,128)(2,1)S(1)} %collective-permute-done.11.refs_2_) | copy-start | bytes 1622020
  131.5 25.8 %collective-permute-start.12 = (bf16[2112,128]{1,0:T(8,128)(2,1)S(1)}, bf16[2112,128]{1,0:T(8,128)(2,1)S(1)}, u32[]{:S(2)}, u32[]{:S(2)}) collective-permute-start(bf16[2112,128]{1,0:T(8,128)(2,1)S(1)} %collective-permute-done.11.refs_2_), channel_id=1, source_target_pairs={{0,1},{1,0},{2,3},{3,2},{4,5},{5,4},{6,7},{7,6},{8,9},{9,8},{10,11... | collective-permute-start | bytes 1622024 | tf_op jit(solution)/shard_map/ppermute | solution.py:490
  134.0 23.3 %copy-start.4 = (bf16[2112,128]{1,0:T(8,128)(2,1)}, bf16[2112,128]{1,0:T(8,128)(2,1)S(1)}, u32[]{:S(2)}) copy-start(bf16[2112,128]{1,0:T(8,128)(2,1)S(1)} %collective-permute-done.16.refs_6_) | copy-start | bytes 1622020
  134.1 23.3 %collective-permute-start.17 = (bf16[2112,128]{1,0:T(8,128)(2,1)S(1)}, bf16[2112,128]{1,0:T(8,128)(2,1)S(1)}, u32[]{:S(2)}, u32[]{:S(2)}) collective-permute-start(bf16[2112,128]{1,0:T(8,128)(2,1)S(1)} %collective-permute-done.16.refs_6_), channel_id=1, source_target_pairs={{0,1},{1,0},{2,3},{3,2},{4,5},{5,4},{6,7},{7,6},{8,9},{9,8},{10,11... | collective-permute-start | bytes 1622024 | tf_op jit(solution)/shard_map/ppermute | solution.py:490
  136.9 20.5 %copy-start.5 = (bf16[2112,128]{1,0:T(8,128)(2,1)}, bf16[2112,128]{1,0:T(8,128)(2,1)S(1)}, u32[]{:S(2)}) copy-start(bf16[2112,128]{1,0:T(8,128)(2,1)S(1)} %collective-permute-done.21.refs_10_) | copy-start | bytes 1622020
  136.9 20.4 %collective-permute-start.22 = (bf16[2112,128]{1,0:T(8,128)(2,1)S(1)}, bf16[2112,128]{1,0:T(8,128)(2,1)S(1)}, u32[]{:S(2)}, u32[]{:S(2)}) collective-permute-start(bf16[2112,128]{1,0:T(8,128)(2,1)S(1)} %collective-permute-done.21.refs_10_), channel_id=1, source_target_pairs={{0,1},{1,0},{2,3},{3,2},{4,5},{5,4},{6,7},{7,6},{8,9},{9,8},{10,11... | collective-permute-start | bytes 1622024 | tf_op jit(solution)/shard_map/ppermute | solution.py:490
  148.5 14.9 %copy-start.6 = (bf16[2112,128]{1,0:T(8,128)(2,1)}, bf16[2112,128]{1,0:T(8,128)(2,1)S(1)}, u32[]{:S(2)}) copy-start(bf16[2112,128]{1,0:T(8,128)(2,1)S(1)} %collective-permute-done.6.refs_2_) | copy-start | bytes 1622020
  148.5 14.9 %collective-permute-start.7 = (bf16[2112,128]{1,0:T(8,128)(2,1)S(1)}, bf16[2112,128]{1,0:T(8,128)(2,1)S(1)}, u32[]{:S(2)}, u32[]{:S(2)}) collective-permute-start(bf16[2112,128]{1,0:T(8,128)(2,1)S(1)} %collective-permute-done.6.refs_2_), channel_id=1, source_target_pairs={{0,1},{1,0},{2,3},{3,2},{4,5},{5,4},{6,7},{7,6},{8,9},{9,8},{10,11... | collective-permute-start | bytes 1622024 | tf_op jit(solution)/shard_map/ppermute | solution.py:490
  157.3 0.8 copy-start.7
  157.3 1.0 copy-start.8
  157.4 1.2 copy-start.10
  163.4 0.8 copy-start.9
Sparse Core Ops, SparseCore 0:
  12.6 32.1 all-gather.2
  55.1 44.2 all-gather.4

commit v3 on v2

v3 whole, which is shorter than its diff:
```python
import functools
import math

import jax
import jax.numpy as jnp
from jax import lax
from jax.experimental import pallas as pl
from jax.experimental.pallas import tpu as pltpu
from jax.sharding import PartitionSpec as P

HEAD_DIM = 128
LANES = 128
SUBLANES = 8
TAPS = 3
HEADS_PER_STEP = 4
CHUNK_STEPS = (2, 2, 2, 2)
TAIL = 16
NEGATIVE = -1e30
EXP_SCALE = HEAD_DIM**-0.5 * math.log2(math.e)
VMEM_LIMIT = 60 * 1024 * 1024


def params(**kwargs):
    return pltpu.CompilerParams(vmem_limit_bytes=VMEM_LIMIT, **kwargs)


def cost(microseconds):
    return pl.CostEstimate(
        flops=microseconds * 10**8, bytes_accessed=2**16, transcendentals=0
    )


def block_lanes(block):
    return slice(block * LANES, (block + 1) * LANES)


def conv_pack_kernel(rate_ref, residue_ref, q_ref, k_ref, v_ref, par_ref, rim_ref):
    modes = rate_ref.shape[0]
    for block in range(rate_ref.shape[1] // LANES):
        for which, ref in enumerate((rate_ref, residue_ref)):
            start = (2 * block + which) * modes
            for device in range(par_ref.shape[0]):
                par_ref[device, start : start + modes, :] = ref[:, block_lanes(block)]
    for feature, ref in enumerate((q_ref, k_ref, v_ref)):
        last = ref[...].astype(jnp.float32)[ref.shape[0] - 2 :]
        rim_ref[2 * feature : 2 * feature + 2, :] = last
    rim_ref[2 * TAPS :, :] = jnp.zeros((2, rim_ref.shape[1]), jnp.float32)


def rim_rows(rim_ref, feature, lanes):
    return [rim_ref[pl.ds(2 * feature + row, 1), lanes] for row in range(2)]


def short_mix(feature, rim, taps):
    two_before, one_before = rim
    row = lax.broadcasted_iota(jnp.int32, feature.shape, 0)
    one = jnp.where(row == 0, one_before, pltpu.roll(feature, 1, 0))
    two = jnp.where(row == 0, two_before, jnp.where(row == 1, one_before, pltpu.roll(feature, 2, 0)))
    return taps[0] * feature + taps[1] * one + taps[2] * two


def tap_rows(taps_ref, feature, lanes):
    return [taps_ref[feature, pl.ds(tap, 1), lanes] for tap in range(TAPS)]


def state_kernel(modes, k_ref, v_ref, rim_ref, par_ref, taps_ref, y_ref, s_ref, p_scr, y_scr):
    rows = k_ref.shape[0]
    for block in range(SUBLANES):
        lanes = block_lanes(block)
        mixes = [
            short_mix(
                ref[:, lanes].astype(jnp.float32),
                rim_rows(rim_ref, feature, lanes),
                tap_rows(taps_ref, feature, lanes),
            )
            for feature, ref in ((1, k_ref), (2, v_ref))
        ]
        product = (mixes[0] * mixes[1]).astype(jnp.bfloat16).astype(jnp.float32)
        p_scr[pl.ds(block, rows, SUBLANES), :] = product
    decay = [jnp.exp(-par_ref[pl.ds(mode, SUBLANES, 2 * modes), :]) for mode in range(modes)]
    residue = [par_ref[pl.ds(modes + mode, SUBLANES, 2 * modes), :] for mode in range(modes)]

    def body(position, states):
        here = pl.ds(pl.multiple_of(position * SUBLANES, SUBLANES), SUBLANES)
        product = p_scr[here, :]
        states = tuple(state * rate + product for state, rate in zip(states, decay))
        terms = [state * weight for state, weight in zip(states, residue)]
        while len(terms) > 1:
            terms = [left + right for left, right in zip(terms[::2], terms[1::2])]
        y_scr[here, :] = terms[0]
        return states

    zero = jnp.zeros((SUBLANES, LANES), jnp.float32)
    states = lax.fori_loop(0, rows, body, (zero,) * modes, unroll=4)
    for mode in range(modes):
        s_ref[pl.ds(mode, SUBLANES, modes), :] = states[mode]
    for block in range(SUBLANES):
        y_ref[:, block_lanes(block)] = y_scr[pl.ds(block, rows, SUBLANES), :]


def output_kernel(modes, q_ref, y_ref, rim_ref, par_ref, state_ref, taps_ref, out_ref):
    me = lax.axis_index("ctx")
    rows = q_ref.shape[0]
    step = lax.broadcasted_iota(jnp.int32, (SUBLANES, LANES), 0).astype(jnp.float32) + 1.0

    def body(block, nothing):
        lanes = pl.ds(pl.multiple_of(block * LANES, LANES), LANES)
        rate = par_ref[pl.ds(pl.multiple_of(2 * block * modes, SUBLANES), modes), :]
        residue = par_ref[pl.ds(pl.multiple_of((2 * block + 1) * modes, SUBLANES), modes), :]
        chunk_decay = jnp.exp(-rate * rows)
        entering = jnp.zeros((modes, LANES), jnp.float32)
        for device in range(state_ref.shape[0] - 1):
            start = pl.multiple_of(block * modes, SUBLANES)
            after = entering * chunk_decay + state_ref[device, pl.ds(start, modes), :]
            entering = jnp.where(device < me, after, entering)
        weighted = residue * entering
        eight = jnp.exp(-rate * SUBLANES)
        terms = [
            weighted[mode : mode + 1] * jnp.exp(-rate[mode : mode + 1] * step)
            for mode in range(modes)
        ]
        eights = [jnp.broadcast_to(eight[mode : mode + 1], terms[0].shape) for mode in range(modes)]
        added = []
        for start in range(0, rows, SUBLANES):
            sums = list(terms)
            while len(sums) > 1:
                sums = [left + right for left, right in zip(sums[::2], sums[1::2])]
            added.append(sums[0])
            if start + SUBLANES < rows:
                terms = [term * decay for term, decay in zip(terms, eights)]
        smoothed = y_ref[:, lanes] + jnp.concatenate(added, 0)
        smoothed = smoothed.astype(jnp.bfloat16).astype(jnp.float32)
        mix = short_mix(
            q_ref[:, lanes].astype(jnp.float32),
            rim_rows(rim_ref, 0, lanes),
            tap_rows(taps_ref, 0, lanes),
        )
        out_ref[:, lanes] = (mix * smoothed).astype(out_ref.dtype)
        return nothing

    lax.fori_loop(0, SUBLANES, body, 0)


def convolve(hyena_q, hyena_k, hyena_v, short_filter, residue, decay_rate):
    rows, channels = hyena_q.shape
    devices = lax.axis_size("ctx")
    modes = residue.shape[1]
    own_blocks = residue.shape[0] // LANES
    blocks = channels // LANES
    groups = blocks // SUBLANES
    width = SUBLANES * LANES
    end = rows // 16 - 1
    par_rows = 2 * own_blocks * modes
    own_par, rim = pl.pallas_call(
        conv_pack_kernel,
        grid=(1,),
        in_specs=[pl.BlockSpec((modes, residue.shape[0]), lambda step: (0, 0))] * 2
        + [pl.BlockSpec((16, channels), lambda step: (end, 0))] * 3,
        out_specs=[
            pl.BlockSpec((devices, par_rows, LANES), lambda step: (0, 0, 0)),
            pl.BlockSpec((8, channels), lambda step: (0, 0)),
        ],
        out_shape=[
            jax.ShapeDtypeStruct((devices, par_rows, LANES), jnp.float32),
            jax.ShapeDtypeStruct((8, channels), jnp.float32),
        ],
        compiler_params=params(),
        cost_estimate=cost(1),
        name="conv_pack",
    )(decay_rate.T, residue.T, hyena_q, hyena_k, hyena_v)
    par = lax.all_to_all(own_par, "ctx", split_axis=0, concat_axis=0, tiled=True)
    par = par.reshape(devices * par_rows, LANES)
    rim = lax.ppermute(rim, "ctx", [(index, index + 1) for index in range(devices - 1)])
    feature_spec = pl.BlockSpec((rows, width), lambda group: (0, group))
    rim_spec = pl.BlockSpec((8, width), lambda group: (0, group))
    par_spec = pl.BlockSpec((2 * SUBLANES * modes, LANES), lambda group: (group, 0))
    taps_spec = pl.BlockSpec((TAPS, TAPS, width), lambda group: (0, 0, group))
    positions = pltpu.VMEM((rows * SUBLANES, LANES), jnp.float32)
    local_result, state = pl.pallas_call(
        functools.partial(state_kernel, modes),
        grid=(groups,),
        in_specs=[feature_spec, feature_spec, rim_spec, par_spec, taps_spec],
        out_specs=[
            feature_spec,
            pl.BlockSpec((SUBLANES * modes, LANES), lambda group: (group, 0)),
        ],
        out_shape=[
            jax.ShapeDtypeStruct((rows, channels), jnp.float32),
            jax.ShapeDtypeStruct((blocks * modes, LANES), jnp.float32),
        ],
        scratch_shapes=[positions, positions],
        compiler_params=params(),
        cost_estimate=cost(8),
        name="conv_state",
    )(hyena_k, hyena_v, rim, par, short_filter)
    states = lax.all_gather(state, "ctx", axis=0, tiled=True)
    states = states.reshape(devices, blocks * modes, LANES)
    return pl.pallas_call(
        functools.partial(output_kernel, modes),
        grid=(groups,),
        in_specs=[
            feature_spec,
            feature_spec,
            rim_spec,
            par_spec,
            pl.BlockSpec((devices, SUBLANES * modes, LANES), lambda group: (0, group, 0)),
            taps_spec,
        ],
        out_specs=feature_spec,
        out_shape=jax.ShapeDtypeStruct((rows, channels), jnp.bfloat16),
        compiler_params=params(),
        cost_estimate=cost(5),
        name="conv_output",
    )(hyena_q, local_result, rim, par, states, short_filter)


def among(me, members):
    return functools.reduce(jnp.logical_or, [me == member for member in members])


def plan_moves(devices):
    quads = devices // 4
    transfers = [[(devices - 1, devices - 3)]]
    for distance in range(1, quads):
        if distance > len(transfers):
            transfers.append([])
        for quad in range(distance, quads):
            target = 4 * (quad - distance) + 2
            transfers[distance - 1] += [(4 * quad, target), (4 * quad + 2, target + 1)]
    return transfers


def soft(query, keys, values, mask=None):
    scores = lax.dot_general(
        query, keys, (((1,), (1,)), ((), ())), preferred_element_type=jnp.float32
    )
    if mask is not None:
        scores = jnp.where(mask, scores, NEGATIVE)
    top = jnp.max(scores, axis=1, keepdims=True) * EXP_SCALE
    expo = jnp.exp2(scores * EXP_SCALE - top).astype(jnp.bfloat16)
    mixed = jnp.dot(expo, values, preferred_element_type=jnp.float32)
    total = mixed[:, HEAD_DIM:]
    return mixed[:, :HEAD_DIM] / total, top + jnp.log2(total)


def pack_kernel(gathers, askers, widths, starts, q_ref, qs_ref, k_ref, v_ref, *rest):
    count = len(widths)
    key_outs, query_outs, sems = rest[:count], rest[count : 2 * count], rest[-1]
    me = lax.axis_index("ctx")
    odd = me % 2
    rows = q_ref.shape[0]

    def run(pairs):
        copies = [
            pltpu.make_async_copy(source, target, sems.at[index])
            for index, (source, target) in enumerate(pairs)
        ]
        for copy in copies:
            copy.start()
        for copy in copies:
            copy.wait()

    def cut(ref, chunk):
        return ref.at[:, pl.ds(starts[chunk], widths[chunk])]

    if gathers:

        @pl.when(among(me, gathers))
        def _():
            run(
                [
                    (cut(ref, chunk), key_outs[chunk].at[which])
                    for chunk in range(count)
                    for which, ref in enumerate((k_ref, v_ref))
                ]
            )

    @pl.when(among(me, askers))
    def _():
        run(
            [
                (cut(ref, chunk), query_outs[chunk].at[half])
                for chunk in range(count)
                for ref, half in ((q_ref, odd), (qs_ref, 1 - odd))
            ]
        )


def spread(rows_of_heads, count):
    lanes = lax.broadcasted_iota(jnp.int32, rows_of_heads[0].shape, 1)
    sums = jnp.zeros_like(rows_of_heads[0])
    for index, column in enumerate(rows_of_heads):
        sums = jnp.where(lanes == index, column, sums)
    return jnp.transpose(sums)[:count]


def partial_kernel(transfers, upper, *refs):
    count = len(transfers)
    q_ref, k_ref, v_ref, kp_ref, vp_ref, g_ref, gp_ref = refs[:7]
    ask_refs = refs[7 : 7 + count]
    own_ref, lse_ref = refs[7 + count : 9 + count]
    answer_refs = refs[9 + count :]
    me = lax.axis_index("ctx")
    rows = q_ref.shape[0]
    heads = q_ref.shape[1] // HEAD_DIM
    half_rows = heads * rows + TAIL

    def key_value(head, with_quad):
        cut = block_lanes(head)
        keys = [kp_ref[:, cut], k_ref[:, cut]]
        values = [vp_ref[:, cut], v_ref[:, cut]]
        if with_quad:
            keys = [g_ref[0, :, cut], gp_ref[0, :, cut]] + keys
            values = [g_ref[1, :, cut], gp_ref[1, :, cut]] + values
        values = jnp.concatenate(values, 0)
        return jnp.concatenate(keys, 0), jnp.concatenate([values, jnp.ones_like(values)], 1)

    def run(with_quad):
        key_count = rows * (4 if with_quad else 2)
        row = lax.broadcasted_iota(jnp.int32, (rows, key_count), 0)
        column = lax.broadcasted_iota(jnp.int32, (rows, key_count), 1)
        column = column - (key_count - 2 * rows)
        partner_limit = jnp.where(me % 2 == 1, rows, 0)
        mask = (column < partner_limit) | ((column >= rows) & (column - rows <= row))
        sums = []
        for head in range(heads):
            keys, values = key_value(head, with_quad)
            mixed, lse = soft(q_ref[:, block_lanes(head)], keys, values, mask)
            own_ref[:, block_lanes(head)] = mixed
            sums.append(lse)
        lse_ref[...] = spread(sums, SUBLANES)

        def answer(index):
            sums = [[], []]
            for head in range(heads):
                keys, values = key_value(head, with_quad)
                query = ask_refs[index][:, :, block_lanes(head)].reshape(2 * rows, HEAD_DIM)
                mixed, lse = soft(query, keys, values)
                first = lse.astype(jnp.bfloat16).astype(jnp.float32)
                second = (lse - first).astype(jnp.bfloat16).astype(jnp.float32)
                for half in range(2):
                    cut = slice(half * rows, (half + 1) * rows)
                    start = half * half_rows + head * rows
                    answer_refs[index][start : start + rows, :] = mixed[cut].astype(jnp.bfloat16)
                    sums[half] += [first[cut], second[cut], (lse - first - second)[cut]]
            for half in range(2):
                start = half * half_rows + heads * rows
                tail = spread(sums[half], TAIL).astype(jnp.bfloat16)
                answer_refs[index][start : start + TAIL, :] = tail

        for index, pairs in enumerate(transfers):
            asked = [target for _, target in pairs if (target in upper) == with_quad]
            if asked:
                pl.when(among(me, asked))(functools.partial(answer, index))

    if upper:
        pl.when(among(me, upper))(functools.partial(run, True))
        pl.when(jnp.logical_not(among(me, upper)))(functools.partial(run, False))
    else:
        run(False)


def merge_kernel(transfers, me_ref, own_ref, lse_ref, *refs):
    others = refs[: 2 * len(transfers)]
    out_ref = refs[-1]
    me = me_ref[0]
    rows, width = out_ref.shape
    heads = width // HEAD_DIM
    returned = []
    for pairs in transfers:
        members = [source for source, _ in pairs]
        returned += [members, [member ^ 1 for member in members]]
    answered = among(me, sorted(set(sum(returned, []))))

    def columns(part):
        fill = jnp.zeros((LANES - part.shape[0], rows), jnp.float32)
        return jnp.transpose(jnp.concatenate([part, fill], 0))

    @pl.when(answered)
    def _():
        own_sums = columns(lse_ref[...])
        valid = [among(me, members) for members in returned]
        sums = [columns(ref[heads * rows :, :].astype(jnp.float32)) for ref in others]
        for head in range(heads):
            cut = block_lanes(head)
            logs = [own_sums[:, head : head + 1]]
            mixed = [own_ref[:, cut]]
            for index, ref in enumerate(others):
                parts = [sums[index][:, 3 * head + part : 3 * head + part + 1] for part in range(3)]
                logs.append(jnp.where(valid[index], parts[0] + parts[1] + parts[2], NEGATIVE))
                part = ref[head * rows : (head + 1) * rows, :].astype(jnp.float32)
                mixed.append(jnp.where(valid[index], part, 0.0))
            top = functools.reduce(jnp.maximum, logs)
            weights = [jnp.exp2(part - top) for part in logs]
            total = functools.reduce(jnp.add, weights)
            terms = [part * (weight / total) for part, weight in zip(mixed, weights)]
            out_ref[:, cut] = functools.reduce(jnp.add, terms).astype(out_ref.dtype)

    @pl.when(jnp.logical_not(answered))
    def _():
        out_ref[...] = own_ref[...].astype(out_ref.dtype)


def after(array, *others):
    return lax.optimization_barrier((array, *others))[0]


def attend(query, key, value):
    rows, columns = query.shape
    devices = lax.axis_size("ctx")
    quads = devices // 4
    transfers = plan_moves(devices)
    step_width = HEADS_PER_STEP * HEAD_DIM
    chunks = len(CHUNK_STEPS)
    first_steps = [sum(CHUNK_STEPS[:chunk]) for chunk in range(chunks)]
    widths = [steps * step_width for steps in CHUNK_STEPS]
    starts = [step * step_width for step in first_steps]
    upper = [4 * quad + 2 + core for quad in range(quads - 1) for core in range(2)]
    gathers = [(who - 2, who) for who in upper]
    askers = sorted({source for pairs in transfers for source, _ in pairs})
    swap = [(index, index ^ 1) for index in range(devices)]
    me = lax.axis_index("ctx").astype(jnp.int32).reshape(1)

    query_swapped = lax.ppermute(query, "ctx", swap)
    key_swapped = lax.ppermute(key, "ctx", swap)
    value_swapped = lax.ppermute(value, "ctx", swap)

    def pack(members):
        hbm = pl.BlockSpec(memory_space=pl.ANY)
        shapes = [
            jax.ShapeDtypeStruct((2, rows, widths[chunk]), jnp.bfloat16) for chunk in members
        ]
        outs = pl.pallas_call(
            functools.partial(
                pack_kernel,
                [source for source, _ in gathers],
                askers,
                [widths[chunk] for chunk in members],
                [starts[chunk] for chunk in members],
            ),
            in_specs=[hbm] * 4,
            out_specs=[hbm] * (2 * len(members)),
            out_shape=shapes * 2,
            scratch_shapes=[pltpu.SemaphoreType.DMA((2 * len(members),))],
            compiler_params=params(),
            cost_estimate=cost(1),
            name="att_pack",
        )(query, query_swapped, key, value)
        return list(zip(outs[: len(members)], outs[len(members) :]))

    packs = pack([0]) + (pack(list(range(1, chunks))) if chunks > 1 else [])
    asks, quad_kv = [], []
    for chunk in range(chunks):
        key_pack, query_pack = packs[chunk]
        if chunk:
            key_pack = after(key_pack, quad_kv[-1][0])
            query_pack = after(query_pack, *asks[-1])
        arrived = lax.ppermute(key_pack, "ctx", gathers)
        asks.append([lax.ppermute(query_pack, "ctx", pairs) for pairs in transfers])
        quad_kv.append([arrived, lax.ppermute(arrived, "ctx", swap)])

    half_rows = HEADS_PER_STEP * rows + TAIL
    result = None
    for chunk in range(chunks):
        steps, first = CHUNK_STEPS[chunk], first_steps[chunk]
        whole_spec = pl.BlockSpec((rows, step_width), lambda step, first=first: (0, first + step))
        chunk_spec = pl.BlockSpec((rows, step_width), lambda step: (0, step))
        pair_spec = pl.BlockSpec((2, rows, step_width), lambda step: (0, 0, step))
        lse_spec = pl.BlockSpec((SUBLANES, LANES), lambda step: (step, 0))
        answer_spec = pl.BlockSpec((2 * half_rows, LANES), lambda step: (step, 0))
        answer_shape = jax.ShapeDtypeStruct((2 * half_rows * steps, LANES), jnp.bfloat16)
        own, lse, *answers = pl.pallas_call(
            functools.partial(partial_kernel, transfers, upper),
            grid=(steps,),
            in_specs=[whole_spec] * 5 + [pair_spec] * (2 + len(transfers)),
            out_specs=[chunk_spec, lse_spec] + [answer_spec] * len(transfers),
            out_shape=[
                jax.ShapeDtypeStruct((rows, widths[chunk]), jnp.float32),
                jax.ShapeDtypeStruct((SUBLANES * steps, LANES), jnp.float32),
            ]
            + [answer_shape] * len(transfers),
            compiler_params=params(),
            cost_estimate=cost(4),
            name="att_partial",
        )(query, key, value, key_swapped, value_swapped, *quad_kv[chunk], *asks[chunk])
        operands = [me, own, lse]
        for answer, pairs in zip(answers, transfers):
            back = lax.ppermute(answer, "ctx", [(target, source) for source, target in pairs])
            operands += [back, lax.ppermute(back, "ctx", swap)]

        def shifted(step, me_ref, first=first):
            return (0, first + step)

        half_spec = pl.BlockSpec(
            (half_rows, LANES), lambda step, me_ref: (2 * step + me_ref[0] % 2, 0)
        )
        specs = [
            pl.BlockSpec((rows, step_width), lambda step, me_ref: (0, step)),
            pl.BlockSpec((SUBLANES, LANES), lambda step, me_ref: (step, 0)),
        ] + [half_spec] * (2 * len(transfers))
        aliases = {}
        if result is not None:
            aliases = {len(operands): 0}
            operands.append(result)
            specs.append(pl.BlockSpec(memory_space=pl.ANY))
        result = pl.pallas_call(
            functools.partial(merge_kernel, transfers),
            grid_spec=pltpu.PrefetchScalarGridSpec(
                num_scalar_prefetch=1,
                grid=(steps,),
                in_specs=specs,
                out_specs=pl.BlockSpec((rows, step_width), shifted),
            ),
            out_shape=jax.ShapeDtypeStruct((rows, columns), jnp.bfloat16),
            input_output_aliases=aliases,
            compiler_params=params(),
            cost_estimate=cost(2),
            name="att_merge",
        )(*operands)
    return result


def local(
    hyena_q, hyena_k, hyena_v, short_filter, residue, decay_rate, att_query, att_key, att_value
):
    att_out = attend(att_query, att_key, att_value)
    hyena_out = convolve(hyena_q, hyena_k, hyena_v, short_filter, residue, decay_rate)
    return (hyena_out, att_out)


def solution(mesh):
    rows = P(("dp", "ctx"), None)
    shared = P("ctx", None)
    return jax.shard_map(
        local,
        mesh=mesh,
        in_specs=(rows, rows, rows, P(), shared, shared, rows, rows, rows),
        out_specs=(rows, rows),
        check_vma=False,
    )
```

time: 183 us -> 232 us (1.27)
  starting transfers between devices: 69.8 us -> 127 us
  Pallas kernels: 60.7 us -> 54.3 us
    ppermute x1, starting transfers between devices: 0.06 us -> 59.1 us  [attend(): key_swapped = lax.ppermute(key, 'ctx', swap)]
    ppermute x12 -> x13, waiting for transfers between devices: 0.18 us -> 26.2 us  [the longest x4 22.7 us: attend(): asks.append([lax.ppermute(query_pack, 'ctx', pairs) for pairs in transfers])]
    ppermute x4, starting transfers between devices: 30 us -> 5.15 us  [attend(): quad_kv.append([arrived, lax.ppermute(arrived, 'ctx', swap)])]
    all_gather x1 -> x0, waiting for transfers between devices: 23.3 us -> none  [convolve(): shared = lax.all_gather(own_shared, 'ctx', axis=0, tiled=True)]
    ppermute x12 -> x13, starting transfers between devices: 30.6 us -> 51.4 us  [the longest x4 37.6 us: attend(): operands += [back, lax.ppermute(back, 'ctx', swap)]]
    pallas_call x11 -> x13, Pallas kernels: 60.7 us -> 54.3 us  [the longest x4 19.2 us: attend(): pl.pallas_call(functools.partial(partial_kernel, transfers, upper), grid=...]
    ppermute x4, waiting for transfers between devices: 5.5 us -> 0.01 us  [attend(): lax.ppermute(answer, 'ctx', [(target, source) for source, target in pairs])]
    all_to_all x0 -> x1, starting transfers between devices: none -> 4.96 us  [convolve(): lax.all_to_all(own_par, 'ctx', split_axis=0, concat_axis=0, tiled=True)]
  transfers between devices with their start and end apart: 25 -> 26, of which waited for: 4 -> 4; matrix products, arithmetic and copies ran while one was open for 0% -> 0% of each run, Pallas kernels for 28% -> 22%
where the time goes in v3:
time: 232 us
  starting transfers between devices  127 us (55%)
  Pallas kernels  54.3 us (23%)
  waiting for transfers between devices  29.3 us (13%)
  between operations  14.3 us (6%)
  local copies, waits for them, and re-layouts  6.9 us (3%)
    ppermute x1, starting transfers between devices, attend(): key_swapped = lax.ppermute(key, 'ctx', swap)  59.1 us
    ppermute x4, starting transfers between devices, attend(): operands += [back, lax.ppermute(back, 'ctx', swap)]  37.6 us
    ppermute x4, waiting for transfers between devices, attend(): asks.append([lax.ppermute(query_pack, 'ctx', pairs) for pairs in transfers])  22.7 us
    pallas_call x4, Pallas kernels, attend(): pl.pallas_call(functools.partial(partial_kernel, transfers, upper), grid=...  19.2 us
    pallas_call x4, Pallas kernels, attend(): pl.pallas_call(functools.partial(merge_kernel, transfers), grid_spec=pltp...  16.6 us
    pallas_call x1, Pallas kernels, convolve(): pl.pallas_call(functools.partial(state_kernel, modes), grid=(groups,), in...  9.63 us
    unnamed x38, local copies, waits for them, and re-layouts  6.9 us
    pallas_call x1, Pallas kernels, convolve(): pl.pallas_call(functools.partial(output_kernel, modes), grid=(groups,), i...  6.74 us
  transfers between devices with their start and end apart: 26, of which 4 were waited for; matrix products, arithmetic and copies ran while one was open for 0% of the time, Pallas kernels for 22%

profile of v3, /device:TPU:17, one launch (start us, length us, event | category | flops | bytes accessed | tf_op | source)
XLA Modules:
  0.0 231.5 jit_solution(6700604673753010820)
XLA Ops:
  7.2 0.7 collective-permute-start.3
  7.9 1.9 conv_pack.1
  9.8 5.0 %all-to-all-start = ((f32[8,128,128]{2,1,0:T(8,128)}), f32[8,128,128]{2,1,0:T(8,128)S(1)}, u32[]{:S(2)}, u32[]{:S(2)}) async-start(f32[8,128,128]{2,1,0:T(8,128)} %get-tuple-element.33), calls=%async_computation | async-start | bytes 1048576 | tf_op jit(solution)/shard_map/all_to_all | solution.py:171
  14.8 3.3 %collective-permute-start = (f32[8,4096]{1,0:T(8,128)}, f32[8,4096]{1,0:T(8,128)S(1)}, u32[]{:S(2)}, u32[]{:S(2)}) collective-permute-start(f32[8,4096]{1,0:T(8,128)} %get-tuple-element.32), channel_id=1, source_target_pairs={{0,1},{1,2},{2,3},{3,4},{4,5},{5,6},{6,7},{8,9},{9,10},{10,11},{11... | collective-permute-start | bytes 393224 | tf_op jit(solution)/shard_map/ppermute | solution.py:173
  18.2 1.0 copy-done.4
  19.1 0.7 collective-permute-start.4
  19.8 3.5 %collective-permute-done.rim_ref = f32[8,4096]{1,0:T(8,128)S(1)} collective-permute-done((f32[8,4096]{1,0:T(8,128)}, f32[8,4096]{1,0:T(8,128)S(1)}, u32[]{:S(2)}, u32[]{:S(2)}) %collective-permute-start) | collective-permute-done | bytes 131104 | tf_op jit(solution)/shard_map/ppermute | solution.py:173
  23.3 3.0 %all-to-all-done = f32[8,128,128]{2,1,0:T(8,128)S(1)} async-done(((f32[8,128,128]{2,1,0:T(8,128)}), f32[8,128,128]{2,1,0:T(8,128)S(1)}, u32[]{:S(2)}, u32[]{:S(2)}) %all-to-all-start) | async-done | bytes 524320 | tf_op jit(solution)/shard_map/all_to_all | solution.py:171
  26.4 0.9 copy-done.5
  27.3 9.6 %conv_state.1 = (f32[128,4096]{1,0:T(8,128)}, f32[512,128]{1,0:T(8,128)}) custom-call(bf16[128,4096]{1,0:T(8,128)(2,1)} %k_ref.5, bf16[128,4096]{1,0:T(8,128)(2,1)} %v_ref.5, f32[8,4096]{1,0:T(8,128)} %copy-done.18, f32[1024,128]{1,0:T(8,128)} %bitcast.6, f32[3,3,4096]{2,1,0:T(4,128)} %taps_ref.3), custom_call_target="tpu_custom_call" | custom-call | flops 800000000 | bytes 65536 | tf_op jit(solution)/shard_map/conv_state/pallas_call | solution.py:179
  36.9 1.4 collective-permute-start.9
  38.4 0.1 att_pack.2
  38.5 1.5 collective-permute-start.5
  40.0 59.1 %collective-permute-start.1 = (bf16[128,4096]{1,0:T(8,128)(2,1)S(1)}, bf16[128,4096]{1,0:T(8,128)(2,1)S(1)}, u32[]{:S(2)}, u32[]{:S(2)}) collective-permute-start(bf16[128,4096]{1,0:T(8,128)(2,1)S(1)} %copy-done), channel_id=1, source_target_pairs={{0,1},{1,0},{2,3},{3,2},{4,5},{5,4},{6,7},{7,6},{8,9},{9,8},{10,11... | collective-permute-start | bytes 3145736 | tf_op jit(solution)/shard_map/ppermute | solution.py:425
  99.1 1.3 collective-permute-start.10
  100.4 1.5 collective-permute-start.6
  101.9 0.0 collective-permute-start.2
  101.9 12.2 %collective-permute-done.10.refs_7_ = bf16[2,128,1024]{2,1,0:T(8,128)(2,1)S(1)} collective-permute-done((bf16[2,128,1024]{2,1,0:T(8,128)(2,1)}, bf16[2,128,1024]{2,1,0:T(8,128)(2,1)S(1)}, u32[]{:S(2)}, u32[]{:S(2)}) %collective-permute-start.10) | collective-permute-done | bytes 524320 | tf_op jit(solution)/shard_map/ppermute | solution.py:459
  114.1 1.3 collective-permute-start.11
  115.4 1.5 collective-permute-start.7
  116.9 1.6 collective-permute-start.21
  118.5 0.1 collective-permute-start.18
  118.6 10.5 %collective-permute-done.11.refs_7_ = bf16[2,128,1024]{2,1,0:T(8,128)(2,1)S(1)} collective-permute-done((bf16[2,128,1024]{2,1,0:T(8,128)(2,1)}, bf16[2,128,1024]{2,1,0:T(8,128)(2,1)S(1)}, u32[]{:S(2)}, u32[]{:S(2)}) %collective-permute-start.11) | collective-permute-done | bytes 524320 | tf_op jit(solution)/shard_map/ppermute | solution.py:459
  129.1 1.0 copy-done.3
  130.1 1.3 collective-permute-start.12
  131.4 3.4 %collective-permute-start.8 = (bf16[2,128,1024]{2,1,0:T(8,128)(2,1)}, bf16[2,128,1024]{2,1,0:T(8,128)(2,1)}, u32[]{:S(2)}, u32[]{:S(2)}) collective-permute-start(bf16[2,128,1024]{2,1,0:T(8,128)(2,1)} %collective-permute-done.7.refs_5_), channel_id=1, source_target_pairs={{0,1},{1,0},{2,3},{3,2},{4,5},{5,4},{6,7},{7,6},{8,9},{9,8},{10,11... | collective-permute-start | bytes 1572872 | tf_op jit(solution)/shard_map/ppermute | solution.py:460
  134.9 4.8 %att_partial.7 = (f32[128,1024]{1,0:T(8,128)}, f32[16,128]{1,0:T(8,128)}, bf16[2112,128]{1,0:T(8,128)(2,1)}) custom-call(bf16[128,4096]{1,0:T(8,128)(2,1)} %refs_0_.7, bf16[128,4096]{1,0:T(8,128)(2,1)} %refs_1_.7, bf16[128,4096]{1,0:T(8,128)(2,1)} %refs_2_.7, bf16[128,4096]{1,0:T(8,128)(2,1)} %copy-done.2, bf16[128,4096]{1,0:T(8,128)(2,1)} %copy-done.3, ...), custom_call_target="tpu_custom_call" | custom-call | flops 400000000 | bytes 65536 | tf_op jit(solution)/shard_map/att_partial/pallas_call | solution.py:472
  139.7 1.3 collective-permute-start.22
  141.0 0.8 copy-done.17
  141.8 4.8 %att_partial.6 = (f32[128,1024]{1,0:T(8,128)}, f32[16,128]{1,0:T(8,128)}, bf16[2112,128]{1,0:T(8,128)(2,1)}) custom-call(bf16[128,4096]{1,0:T(8,128)(2,1)} %refs_0_.7, bf16[128,4096]{1,0:T(8,128)(2,1)} %refs_1_.7, bf16[128,4096]{1,0:T(8,128)(2,1)} %refs_2_.7, bf16[128,4096]{1,0:T(8,128)(2,1)} %copy-done.2, bf16[128,4096]{1,0:T(8,128)(2,1)} %copy-done.3, ...), custom_call_target="tpu_custom_call" | custom-call | flops 400000000 | bytes 65536 | tf_op jit(solution)/shard_map/att_partial/pallas_call | solution.py:472
  146.6 1.3 collective-permute-start.19
  147.9 0.8 copy-done.16
  148.7 4.8 %att_partial.5 = (f32[128,1024]{1,0:T(8,128)}, f32[16,128]{1,0:T(8,128)}, bf16[2112,128]{1,0:T(8,128)(2,1)}) custom-call(bf16[128,4096]{1,0:T(8,128)(2,1)} %refs_0_.7, bf16[128,4096]{1,0:T(8,128)(2,1)} %refs_1_.7, bf16[128,4096]{1,0:T(8,128)(2,1)} %refs_2_.7, bf16[128,4096]{1,0:T(8,128)(2,1)} %copy-done.2, bf16[128,4096]{1,0:T(8,128)(2,1)} %copy-done.3, ...), custom_call_target="tpu_custom_call" | custom-call | flops 400000000 | bytes 65536 | tf_op jit(solution)/shard_map/att_partial/pallas_call | solution.py:472
  153.5 1.5 collective-permute-start.16
  155.1 0.8 copy-done.15
  155.9 4.8 %att_partial.4 = (f32[128,1024]{1,0:T(8,128)}, f32[16,128]{1,0:T(8,128)}, bf16[2112,128]{1,0:T(8,128)(2,1)}) custom-call(bf16[128,4096]{1,0:T(8,128)(2,1)} %refs_0_.7, bf16[128,4096]{1,0:T(8,128)(2,1)} %refs_1_.7, bf16[128,4096]{1,0:T(8,128)(2,1)} %refs_2_.7, bf16[128,4096]{1,0:T(8,128)(2,1)} %copy-done.2, bf16[128,4096]{1,0:T(8,128)(2,1)} %copy-done.3, ...), custom_call_target="tpu_custom_call" | custom-call | flops 400000000 | bytes 65536 | tf_op jit(solution)/shard_map/att_partial/pallas_call | solution.py:472
  160.7 1.3 collective-permute-start.13
  162.0 3.1 %collective-permute-start.23 = (bf16[2112,128]{1,0:T(8,128)(2,1)S(1)}, bf16[2112,128]{1,0:T(8,128)(2,1)}, u32[]{:S(2)}, u32[]{:S(2)}) collective-permute-start(bf16[2112,128]{1,0:T(8,128)(2,1)S(1)} %collective-permute-done.22.refs_0_), channel_id=1, source_target_pairs={{0,1},{1,0},{2,3},{3,2},{4,5},{5,4},{6,7},{7,6},{8,9},{9,8},{10,11... | collective-permute-start | bytes 1622024 | tf_op jit(solution)/shard_map/ppermute | solution.py:489
  165.1 11.6 %collective-permute-start.20 = (bf16[2112,128]{1,0:T(8,128)(2,1)S(1)}, bf16[2112,128]{1,0:T(8,128)(2,1)}, u32[]{:S(2)}, u32[]{:S(2)}) collective-permute-start(bf16[2112,128]{1,0:T(8,128)(2,1)S(1)} %collective-permute-done.19.refs_0_), channel_id=1, source_target_pairs={{0,1},{1,0},{2,3},{3,2},{4,5},{5,4},{6,7},{7,6},{8,9},{9,8},{10,11... | collective-permute-start | bytes 1622024 | tf_op jit(solution)/shard_map/ppermute | solution.py:489
  176.7 11.6 %collective-permute-start.17 = (bf16[2112,128]{1,0:T(8,128)(2,1)S(1)}, bf16[2112,128]{1,0:T(8,128)(2,1)S(1)}, u32[]{:S(2)}, u32[]{:S(2)}) collective-permute-start(bf16[2112,128]{1,0:T(8,128)(2,1)S(1)} %collective-permute-done.16.refs_0_), channel_id=1, source_target_pairs={{0,1},{1,0},{2,3},{3,2},{4,5},{5,4},{6,7},{7,6},{8,9},{9,8},{10,11... | collective-permute-start | bytes 1622024 | tf_op jit(solution)/shard_map/ppermute | solution.py:489
  188.3 11.4 %collective-permute-start.14 = (bf16[2112,128]{1,0:T(8,128)(2,1)S(1)}, bf16[2112,128]{1,0:T(8,128)(2,1)S(1)}, u32[]{:S(2)}, u32[]{:S(2)}) collective-permute-start(bf16[2112,128]{1,0:T(8,128)(2,1)S(1)} %collective-permute-done.13.refs_0_), channel_id=1, source_target_pairs={{0,1},{1,0},{2,3},{3,2},{4,5},{5,4},{6,7},{7,6},{8,9},{9,8},{10,11... | collective-permute-start | bytes 1622024 | tf_op jit(solution)/shard_map/ppermute | solution.py:489
  199.7 4.1 %att_merge.4.refs_2_ = bf16[128,4096]{1,0:T(8,128)(2,1)} custom-call(s32[1]{0:T(128)} %bitcast.4.me_ref, f32[128,1024]{1,0:T(8,128)} %get-tuple-element.59.own_ref, f32[16,128]{1,0:T(8,128)} %get-tuple-element.60.lse_ref, bf16[2112,128]{1,0:T(8,128)(2,1)} %copy-done.6, bf16[2112,128]{1,0:T(8,128)(2,1)} %collective-permute-done.23.refs_1_), custom_call_target="tpu_custom_call" | custom-call | flops 200000000 | bytes 65536 | tf_op jit(solution)/shard_map/att_merge/pallas_call | solution.py:506
  203.8 4.2 %att_merge.5.refs_2_ = bf16[128,4096]{1,0:T(8,128)(2,1)} custom-call(s32[1]{0:T(128)} %bitcast.4.me_ref, f32[128,1024]{1,0:T(8,128)} %get-tuple-element.56.own_ref, f32[16,128]{1,0:T(8,128)} %get-tuple-element.57.lse_ref, bf16[2112,128]{1,0:T(8,128)(2,1)} %copy-done.7, ...), custom_call_target="tpu_custom_call", output_to_operand_aliasing={{}: (5, {})} | custom-call | flops 200000000 | bytes 65536 | tf_op jit(solution)/shard_map/att_merge/pallas_call | solution.py:506
  208.0 0.8 copy-done.11
  208.8 4.1 %att_merge.6.refs_2_ = bf16[128,4096]{1,0:T(8,128)(2,1)} custom-call(s32[1]{0:T(128)} %bitcast.4.me_ref, f32[128,1024]{1,0:T(8,128)} %get-tuple-element.53.own_ref, f32[16,128]{1,0:T(8,128)} %get-tuple-element.54.lse_ref, bf16[2112,128]{1,0:T(8,128)(2,1)} %copy-done.8, bf16[2112,128]{1,0:T(8,128)(2,1)} %copy-done.11, ...), custom_call_target="tpu_custom_call", output_to_operand_aliasing={{}: (5, {})} | custom-call | flops 200000000 | bytes 65536 | tf_op jit(solution)/shard_map/att_merge/pallas_call | solution.py:506
  213.0 6.7 %conv_output.1 = bf16[128,4096]{1,0:T(8,128)(2,1)} custom-call(bf16[128,4096]{1,0:T(8,128)(2,1)} %q_ref.5, f32[128,4096]{1,0:T(8,128)} %get-tuple-element.34.y_ref, f32[8,4096]{1,0:T(8,128)} %copy-done.18, f32[1024,128]{1,0:T(8,128)} %bitcast.7, f32[8,512,128]{2,1,0:T(8,128)} %bitcast.5, f32[3,3,4096]{2,1,0:T(4,128)} %taps_ref.3), custom_call_target="tpu_custom_call" | custom-call | flops 500000000 | bytes 65536 | tf_op jit(solution)/shard_map/conv_output/pallas_call | solution.py:198
  219.7 0.8 copy-done.10
  220.5 4.1 %att_merge.7 = bf16[128,4096]{1,0:T(8,128)(2,1)} custom-call(s32[1]{0:T(128)} %bitcast.4.me_ref, f32[128,1024]{1,0:T(8,128)} %get-tuple-element.50.own_ref, f32[16,128]{1,0:T(8,128)} %get-tuple-element.51.lse_ref, bf16[2112,128]{1,0:T(8,128)(2,1)} %copy-done.9, bf16[2112,128]{1,0:T(8,128)(2,1)} %copy-done.10, ...), custom_call_target="tpu_custom_call", output_to_operand_aliasing={{}: (5, {})} | custom-call | flops 200000000 | bytes 65536 | tf_op jit(solution)/shard_map/att_merge/pallas_call | solution.py:506
  (56 shorter events, 0.2 us)
Async XLA Ops:
  7.2 11.0 %collective-permute-start.3 = (bf16[128,4096]{1,0:T(8,128)(2,1)}, bf16[128,4096]{1,0:T(8,128)(2,1)S(1)}, u32[]{:S(2)}, u32[]{:S(2)}) collective-permute-start(bf16[128,4096]{1,0:T(8,128)(2,1)} %refs_0_.7), channel_id=1, source_target_pairs={{0,1},{1,0},{2,3},{3,2},{4,5},{5,4},{6,7},{7,6},{8,9},{9,8},{10,11... | collective-permute-start | bytes 3145736 | tf_op jit(solution)/shard_map/ppermute | solution.py:424
  9.8 16.5 %all-to-all-start = ((f32[8,128,128]{2,1,0:T(8,128)}), f32[8,128,128]{2,1,0:T(8,128)S(1)}, u32[]{:S(2)}, u32[]{:S(2)}) async-start(f32[8,128,128]{2,1,0:T(8,128)} %get-tuple-element.33), calls=%async_computation | async-start | bytes 1048576 | tf_op jit(solution)/shard_map/all_to_all | solution.py:171
  14.8 198.2 %all-gather.2.cloned.1.call-start = ((), (), s32[]{:S(2)}) async-start(), calls=%async_computation.1 | async-start | bytes 2359296 | tf_op jit(solution)/shard_map/all_gather | solution.py:196
  14.8 8.5 %collective-permute-start = (f32[8,4096]{1,0:T(8,128)}, f32[8,4096]{1,0:T(8,128)S(1)}, u32[]{:S(2)}, u32[]{:S(2)}) collective-permute-start(f32[8,4096]{1,0:T(8,128)} %get-tuple-element.32), channel_id=1, source_target_pairs={{0,1},{1,2},{2,3},{3,4},{4,5},{5,6},{6,7},{8,9},{9,10},{10,11},{11... | collective-permute-start | bytes 393224 | tf_op jit(solution)/shard_map/ppermute | solution.py:173
  18.1 1.0 copy-start.4
  19.1 19.4 %collective-permute-start.4 = (bf16[2,128,1024]{2,1,0:T(8,128)(2,1)}, bf16[2,128,1024]{2,1,0:T(8,128)(2,1)S(1)}, u32[]{:S(2)}, u32[]{:S(2)}) collective-permute-start(bf16[2,128,1024]{2,1,0:T(8,128)(2,1)} %get-tuple-element.39), channel_id=1, source_target_pairs={{0,2},{1,3},{8,10},{9,11},{16,18},{17,19},{24,26},{25,27}} | collective-permute-start | bytes 1572872 | tf_op jit(solution)/shard_map/ppermute | solution.py:458
  23.3 3.0 %copy-start.18 = (f32[8,4096]{1,0:T(8,128)}, f32[8,4096]{1,0:T(8,128)S(1)}, u32[]{:S(2)}) copy-start(f32[8,4096]{1,0:T(8,128)S(1)} %collective-permute-done.rim_ref) | copy-start | bytes 393220
  26.4 0.9 copy-start.5
  36.9 3.1 %copy-start = (bf16[128,4096]{1,0:T(8,128)(2,1)S(1)}, bf16[128,4096]{1,0:T(8,128)(2,1)}, u32[]{:S(2)}) copy-start(bf16[128,4096]{1,0:T(8,128)(2,1)} %refs_1_.7) | copy-start | bytes 3145732
  36.9 64.9 %copy-start.1 = (bf16[128,4096]{1,0:T(8,128)(2,1)S(1)}, bf16[128,4096]{1,0:T(8,128)(2,1)}, u32[]{:S(2)}) copy-start(bf16[128,4096]{1,0:T(8,128)(2,1)} %refs_2_.7) | copy-start | bytes 3145732
  36.9 62.1 %collective-permute-start.9 = (bf16[2,128,1024]{2,1,0:T(8,128)(2,1)}, bf16[2,128,1024]{2,1,0:T(8,128)(2,1)}, u32[]{:S(2)}, u32[]{:S(2)}) collective-permute-start(bf16[2,128,1024]{2,1,0:T(8,128)(2,1)} %get-tuple-element.46), channel_id=1, source_target_pairs={{7,5},{4,2},{6,3},{15,13},{12,10},{14,11},{23,21},{20,18},{22,19},... | collective-permute-start | bytes 1572872 | tf_op jit(solution)/shard_map/ppermute | solution.py:459
  38.5 96.3 %copy-start.12 = (bf16[2,128,1024]{2,1,0:T(8,128)(2,1)}, bf16[2,128,1024]{2,1,0:T(8,128)(2,1)S(1)}, u32[]{:S(2)}) copy-start(bf16[2,128,1024]{2,1,0:T(8,128)(2,1)S(1)} %collective-permute-done.4.refs_5_) | copy-start | bytes 1572868
  38.5 61.9 %collective-permute-start.5 = (bf16[2,128,1024]{2,1,0:T(8,128)(2,1)}, bf16[2,128,1024]{2,1,0:T(8,128)(2,1)}, u32[]{:S(2)}, u32[]{:S(2)}) collective-permute-start(bf16[2,128,1024]{2,1,0:T(8,128)(2,1)} %get-tuple-element.40), channel_id=1, source_target_pairs={{0,2},{1,3},{8,10},{9,11},{16,18},{17,19},{24,26},{25,27}} | collective-permute-start | bytes 1572872 | tf_op jit(solution)/shard_map/ppermute | solution.py:458
  40.0 78.5 %collective-permute-start.1 = (bf16[128,4096]{1,0:T(8,128)(2,1)S(1)}, bf16[128,4096]{1,0:T(8,128)(2,1)S(1)}, u32[]{:S(2)}, u32[]{:S(2)}) collective-permute-start(bf16[128,4096]{1,0:T(8,128)(2,1)S(1)} %copy-done), channel_id=1, source_target_pairs={{0,1},{1,0},{2,3},{3,2},{4,5},{5,4},{6,7},{7,6},{8,9},{9,8},{10,11... | collective-permute-start | bytes 3145736 | tf_op jit(solution)/shard_map/ppermute | solution.py:425
  99.1 15.0 %collective-permute-start.10 = (bf16[2,128,1024]{2,1,0:T(8,128)(2,1)}, bf16[2,128,1024]{2,1,0:T(8,128)(2,1)S(1)}, u32[]{:S(2)}, u32[]{:S(2)}) collective-permute-start(bf16[2,128,1024]{2,1,0:T(8,128)(2,1)} %get-tuple-element.47), channel_id=1, source_target_pairs={{7,5},{4,2},{6,3},{15,13},{12,10},{14,11},{23,21},{20,18},{22,19},... | collective-permute-start | bytes 1572872 | tf_op jit(solution)/shard_map/ppermute | solution.py:459
  100.4 15.0 %collective-permute-start.6 = (bf16[2,128,1024]{2,1,0:T(8,128)(2,1)}, bf16[2,128,1024]{2,1,0:T(8,128)(2,1)}, u32[]{:S(2)}, u32[]{:S(2)}) collective-permute-start(bf16[2,128,1024]{2,1,0:T(8,128)(2,1)} %get-tuple-element.41), channel_id=1, source_target_pairs={{0,2},{1,3},{8,10},{9,11},{16,18},{17,19},{24,26},{25,27}} | collective-permute-start | bytes 1572872 | tf_op jit(solution)/shard_map/ppermute | solution.py:458
  101.9 27.2 %collective-permute-start.2 = (bf16[128,4096]{1,0:T(8,128)(2,1)S(1)}, bf16[128,4096]{1,0:T(8,128)(2,1)S(1)}, u32[]{:S(2)}, u32[]{:S(2)}) collective-permute-start(bf16[128,4096]{1,0:T(8,128)(2,1)S(1)} %copy-done.1), channel_id=1, source_target_pairs={{0,1},{1,0},{2,3},{3,2},{4,5},{5,4},{6,7},{7,6},{8,9},{9,8},{10,11... | collective-permute-start | bytes 3145736 | tf_op jit(solution)/shard_map/ppermute | solution.py:426
  114.1 17.3 %copy-start.13 = (bf16[2,128,1024]{2,1,0:T(8,128)(2,1)}, bf16[2,128,1024]{2,1,0:T(8,128)(2,1)S(1)}, u32[]{:S(2)}) copy-start(bf16[2,128,1024]{2,1,0:T(8,128)(2,1)S(1)} %collective-permute-done.10.refs_7_) | copy-start | bytes 1572868
  114.1 15.0 %collective-permute-start.11 = (bf16[2,128,1024]{2,1,0:T(8,128)(2,1)}, bf16[2,128,1024]{2,1,0:T(8,128)(2,1)S(1)}, u32[]{:S(2)}, u32[]{:S(2)}) collective-permute-start(bf16[2,128,1024]{2,1,0:T(8,128)(2,1)} %get-tuple-element.48), channel_id=1, source_target_pairs={{7,5},{4,2},{6,3},{15,13},{12,10},{14,11},{23,21},{20,18},{22,19},... | collective-permute-start | bytes 1572872 | tf_op jit(solution)/shard_map/ppermute | solution.py:459
  115.4 16.0 %collective-permute-start.7 = (bf16[2,128,1024]{2,1,0:T(8,128)(2,1)}, bf16[2,128,1024]{2,1,0:T(8,128)(2,1)}, u32[]{:S(2)}, u32[]{:S(2)}) collective-permute-start(bf16[2,128,1024]{2,1,0:T(8,128)(2,1)} %get-tuple-element.42), channel_id=1, source_target_pairs={{0,2},{1,3},{8,10},{9,11},{16,18},{17,19},{24,26},{25,27}} | collective-permute-start | bytes 1572872 | tf_op jit(solution)/shard_map/ppermute | solution.py:458
  116.9 18.0 %collective-permute-start.21 = (bf16[2,128,1024]{2,1,0:T(8,128)(2,1)S(1)}, bf16[2,128,1024]{2,1,0:T(8,128)(2,1)}, u32[]{:S(2)}, u32[]{:S(2)}) collective-permute-start(bf16[2,128,1024]{2,1,0:T(8,128)(2,1)S(1)} %collective-permute-done.4.refs_5_), channel_id=1, source_target_pairs={{0,1},{1,0},{2,3},{3,2},{4,5},{5,4},{6,7},{7,6},{8,9},{9,8},{10,11... | collective-permute-start | bytes 1572872 | tf_op jit(solution)/shard_map/ppermute | solution.py:460
  118.5 16.3 %copy-start.2 = (bf16[128,4096]{1,0:T(8,128)(2,1)}, bf16[128,4096]{1,0:T(8,128)(2,1)S(1)}, u32[]{:S(2)}) copy-start(bf16[128,4096]{1,0:T(8,128)(2,1)S(1)} %collective-permute-done.1.refs_3_) | copy-start | bytes 3145732
  118.5 22.5 %collective-permute-start.18 = (bf16[2,128,1024]{2,1,0:T(8,128)(2,1)}, bf16[2,128,1024]{2,1,0:T(8,128)(2,1)S(1)}, u32[]{:S(2)}, u32[]{:S(2)}) collective-permute-start(bf16[2,128,1024]{2,1,0:T(8,128)(2,1)} %collective-permute-done.5.refs_5_), channel_id=1, source_target_pairs={{0,1},{1,0},{2,3},{3,2},{4,5},{5,4},{6,7},{7,6},{8,9},{9,8},{10,11... | collective-permute-start | bytes 1572872 | tf_op jit(solution)/shard_map/ppermute | solution.py:460
  129.1 2.3 %copy-start.14 = (bf16[2,128,1024]{2,1,0:T(8,128)(2,1)}, bf16[2,128,1024]{2,1,0:T(8,128)(2,1)S(1)}, u32[]{:S(2)}) copy-start(bf16[2,128,1024]{2,1,0:T(8,128)(2,1)S(1)} %collective-permute-done.11.refs_7_) | copy-start | bytes 1572868
  129.1 18.8 %collective-permute-start.15 = (bf16[2,128,1024]{2,1,0:T(8,128)(2,1)}, bf16[2,128,1024]{2,1,0:T(8,128)(2,1)S(1)}, u32[]{:S(2)}, u32[]{:S(2)}) collective-permute-start(bf16[2,128,1024]{2,1,0:T(8,128)(2,1)} %collective-permute-done.6.refs_5_), channel_id=1, source_target_pairs={{0,1},{1,0},{2,3},{3,2},{4,5},{5,4},{6,7},{7,6},{8,9},{9,8},{10,11... | collective-permute-start | bytes 1572872 | tf_op jit(solution)/shard_map/ppermute | solution.py:460
  129.1 1.0 copy-start.3
  130.1 24.9 %collective-permute-start.12 = (bf16[2,128,1024]{2,1,0:T(8,128)(2,1)}, bf16[2,128,1024]{2,1,0:T(8,128)(2,1)S(1)}, u32[]{:S(2)}, u32[]{:S(2)}) collective-permute-start(bf16[2,128,1024]{2,1,0:T(8,128)(2,1)} %get-tuple-element.49), channel_id=1, source_target_pairs={{7,5},{4,2},{6,3},{15,13},{12,10},{14,11},{23,21},{20,18},{22,19},... | collective-permute-start | bytes 1572872 | tf_op jit(solution)/shard_map/ppermute | solution.py:459
  131.4 23.7 %collective-permute-start.8 = (bf16[2,128,1024]{2,1,0:T(8,128)(2,1)}, bf16[2,128,1024]{2,1,0:T(8,128)(2,1)}, u32[]{:S(2)}, u32[]{:S(2)}) collective-permute-start(bf16[2,128,1024]{2,1,0:T(8,128)(2,1)} %collective-permute-done.7.refs_5_), channel_id=1, source_target_pairs={{0,1},{1,0},{2,3},{3,2},{4,5},{5,4},{6,7},{7,6},{8,9},{9,8},{10,11... | collective-permute-start | bytes 1572872 | tf_op jit(solution)/shard_map/ppermute | solution.py:460
  139.7 22.3 %collective-permute-start.22 = (bf16[2112,128]{1,0:T(8,128)(2,1)}, bf16[2112,128]{1,0:T(8,128)(2,1)S(1)}, u32[]{:S(2)}, u32[]{:S(2)}) collective-permute-start(bf16[2112,128]{1,0:T(8,128)(2,1)} %get-tuple-element.61), channel_id=1, source_target_pairs={{5,7},{2,4},{3,6},{13,15},{10,12},{11,14},{21,23},{18,20},{19,22},... | collective-permute-start | bytes 1622024 | tf_op jit(solution)/shard_map/ppermute | solution.py:488
  141.0 0.8 copy-start.17
  146.6 18.5 %collective-permute-start.19 = (bf16[2112,128]{1,0:T(8,128)(2,1)}, bf16[2112,128]{1,0:T(8,128)(2,1)S(1)}, u32[]{:S(2)}, u32[]{:S(2)}) collective-permute-start(bf16[2112,128]{1,0:T(8,128)(2,1)} %get-tuple-element.58), channel_id=1, source_target_pairs={{5,7},{2,4},{3,6},{13,15},{10,12},{11,14},{21,23},{18,20},{19,22},... | collective-permute-start | bytes 1622024 | tf_op jit(solution)/shard_map/ppermute | solution.py:488
  147.9 0.8 copy-start.16
  153.5 23.2 %collective-permute-start.16 = (bf16[2112,128]{1,0:T(8,128)(2,1)}, bf16[2112,128]{1,0:T(8,128)(2,1)S(1)}, u32[]{:S(2)}, u32[]{:S(2)}) collective-permute-start(bf16[2112,128]{1,0:T(8,128)(2,1)} %get-tuple-element.55), channel_id=1, source_target_pairs={{5,7},{2,4},{3,6},{13,15},{10,12},{11,14},{21,23},{18,20},{19,22},... | collective-permute-start | bytes 1622024 | tf_op jit(solution)/shard_map/ppermute | solution.py:488
  155.0 0.9 copy-start.15
  160.7 27.6 %collective-permute-start.13 = (bf16[2112,128]{1,0:T(8,128)(2,1)}, bf16[2112,128]{1,0:T(8,128)(2,1)S(1)}, u32[]{:S(2)}, u32[]{:S(2)}) collective-permute-start(bf16[2112,128]{1,0:T(8,128)(2,1)} %get-tuple-element.52), channel_id=1, source_target_pairs={{5,7},{2,4},{3,6},{13,15},{10,12},{11,14},{21,23},{18,20},{19,22},... | collective-permute-start | bytes 1622024 | tf_op jit(solution)/shard_map/ppermute | solution.py:488
  162.0 37.7 %copy-start.6 = (bf16[2112,128]{1,0:T(8,128)(2,1)}, bf16[2112,128]{1,0:T(8,128)(2,1)S(1)}, u32[]{:S(2)}) copy-start(bf16[2112,128]{1,0:T(8,128)(2,1)S(1)} %collective-permute-done.22.refs_0_) | copy-start | bytes 1622020
  162.0 37.7 %collective-permute-start.23 = (bf16[2112,128]{1,0:T(8,128)(2,1)S(1)}, bf16[2112,128]{1,0:T(8,128)(2,1)}, u32[]{:S(2)}, u32[]{:S(2)}) collective-permute-start(bf16[2112,128]{1,0:T(8,128)(2,1)S(1)} %collective-permute-done.22.refs_0_), channel_id=1, source_target_pairs={{0,1},{1,0},{2,3},{3,2},{4,5},{5,4},{6,7},{7,6},{8,9},{9,8},{10,11... | collective-permute-start | bytes 1622024 | tf_op jit(solution)/shard_map/ppermute | solution.py:489
  165.1 38.7 %copy-start.7 = (bf16[2112,128]{1,0:T(8,128)(2,1)}, bf16[2112,128]{1,0:T(8,128)(2,1)S(1)}, u32[]{:S(2)}) copy-start(bf16[2112,128]{1,0:T(8,128)(2,1)S(1)} %collective-permute-done.19.refs_0_) | copy-start | bytes 1622020
  165.1 38.7 %collective-permute-start.20 = (bf16[2112,128]{1,0:T(8,128)(2,1)S(1)}, bf16[2112,128]{1,0:T(8,128)(2,1)}, u32[]{:S(2)}, u32[]{:S(2)}) collective-permute-start(bf16[2112,128]{1,0:T(8,128)(2,1)S(1)} %collective-permute-done.19.refs_0_), channel_id=1, source_target_pairs={{0,1},{1,0},{2,3},{3,2},{4,5},{5,4},{6,7},{7,6},{8,9},{9,8},{10,11... | collective-permute-start | bytes 1622024 | tf_op jit(solution)/shard_map/ppermute | solution.py:489
  176.7 31.3 %copy-start.8 = (bf16[2112,128]{1,0:T(8,128)(2,1)}, bf16[2112,128]{1,0:T(8,128)(2,1)S(1)}, u32[]{:S(2)}) copy-start(bf16[2112,128]{1,0:T(8,128)(2,1)S(1)} %collective-permute-done.16.refs_0_) | copy-start | bytes 1622020
  176.7 31.3 %collective-permute-start.17 = (bf16[2112,128]{1,0:T(8,128)(2,1)S(1)}, bf16[2112,128]{1,0:T(8,128)(2,1)S(1)}, u32[]{:S(2)}, u32[]{:S(2)}) collective-permute-start(bf16[2112,128]{1,0:T(8,128)(2,1)S(1)} %collective-permute-done.16.refs_0_), channel_id=1, source_target_pairs={{0,1},{1,0},{2,3},{3,2},{4,5},{5,4},{6,7},{7,6},{8,9},{9,8},{10,11... | collective-permute-start | bytes 1622024 | tf_op jit(solution)/shard_map/ppermute | solution.py:489
  188.3 19.7 %copy-start.9 = (bf16[2112,128]{1,0:T(8,128)(2,1)}, bf16[2112,128]{1,0:T(8,128)(2,1)S(1)}, u32[]{:S(2)}) copy-start(bf16[2112,128]{1,0:T(8,128)(2,1)S(1)} %collective-permute-done.13.refs_0_) | copy-start | bytes 1622020
  188.3 31.4 %collective-permute-start.14 = (bf16[2112,128]{1,0:T(8,128)(2,1)S(1)}, bf16[2112,128]{1,0:T(8,128)(2,1)S(1)}, u32[]{:S(2)}, u32[]{:S(2)}) collective-permute-start(bf16[2112,128]{1,0:T(8,128)(2,1)S(1)} %collective-permute-done.13.refs_0_), channel_id=1, source_target_pairs={{0,1},{1,0},{2,3},{3,2},{4,5},{5,4},{6,7},{7,6},{8,9},{9,8},{10,11... | collective-permute-start | bytes 1622024 | tf_op jit(solution)/shard_map/ppermute | solution.py:489
  208.0 0.8 copy-start.11
  219.7 0.8 copy-start.10
Sparse Core Ops, SparseCore 0:
  37.0 42.1 all-gather.1

commit v4 on v3

--- a/solution.py
+++ b/solution.py
@@ -11,13 +11,13 @@
 HEAD_DIM = 128
 LANES = 128
 SUBLANES = 8
+TAIL = 4 * SUBLANES
 TAPS = 3
 HEADS_PER_STEP = 4
 CHUNK_STEPS = (2, 2, 2, 2)
-TAIL = 16
 NEGATIVE = -1e30
 EXP_SCALE = HEAD_DIM**-0.5 * math.log2(math.e)
-VMEM_LIMIT = 60 * 1024 * 1024
+VMEM_LIMIT = 255 * 1024 * 256
 
 
 def params(**kwargs):
@@ -26,7 +26,7 @@
 
 def cost(microseconds):
     return pl.CostEstimate(
-        flops=microseconds * 10**8, bytes_accessed=2**16, transcendentals=0
+        flops=microseconds * 10**9, bytes_accessed=2**20, transcendentals=0
     )
 
 
@@ -141,7 +141,7 @@
     lax.fori_loop(0, SUBLANES, body, 0)
 
 
-def convolve(hyena_q, hyena_k, hyena_v, short_filter, residue, decay_rate):
+def convolution(hyena_q, hyena_k, hyena_v, short_filter, residue, decay_rate):
     rows, channels = hyena_q.shape
     devices = lax.axis_size("ctx")
     modes = residue.shape[1]
@@ -151,67 +151,74 @@
     width = SUBLANES * LANES
     end = rows // 16 - 1
     par_rows = 2 * own_blocks * modes
-    own_par, rim = pl.pallas_call(
-        conv_pack_kernel,
-        grid=(1,),
-        in_specs=[pl.BlockSpec((modes, residue.shape[0]), lambda step: (0, 0))] * 2
-        + [pl.BlockSpec((16, channels), lambda step: (end, 0))] * 3,
-        out_specs=[
-            pl.BlockSpec((devices, par_rows, LANES), lambda step: (0, 0, 0)),
-            pl.BlockSpec((8, channels), lambda step: (0, 0)),
-        ],
-        out_shape=[
-            jax.ShapeDtypeStruct((devices, par_rows, LANES), jnp.float32),
-            jax.ShapeDtypeStruct((8, channels), jnp.float32),
-        ],
-        compiler_params=params(),
-        cost_estimate=cost(1),
-        name="conv_pack",
-    )(decay_rate.T, residue.T, hyena_q, hyena_k, hyena_v)
-    par = lax.all_to_all(own_par, "ctx", split_axis=0, concat_axis=0, tiled=True)
-    par = par.reshape(devices * par_rows, LANES)
-    rim = lax.ppermute(rim, "ctx", [(index, index + 1) for index in range(devices - 1)])
     feature_spec = pl.BlockSpec((rows, width), lambda group: (0, group))
     rim_spec = pl.BlockSpec((8, width), lambda group: (0, group))
     par_spec = pl.BlockSpec((2 * SUBLANES * modes, LANES), lambda group: (group, 0))
     taps_spec = pl.BlockSpec((TAPS, TAPS, width), lambda group: (0, 0, group))
     positions = pltpu.VMEM((rows * SUBLANES, LANES), jnp.float32)
-    local_result, state = pl.pallas_call(
-        functools.partial(state_kernel, modes),
-        grid=(groups,),
-        in_specs=[feature_spec, feature_spec, rim_spec, par_spec, taps_spec],
-        out_specs=[
-            feature_spec,
-            pl.BlockSpec((SUBLANES * modes, LANES), lambda group: (group, 0)),
-        ],
-        out_shape=[
-            jax.ShapeDtypeStruct((rows, channels), jnp.float32),
-            jax.ShapeDtypeStruct((blocks * modes, LANES), jnp.float32),
-        ],
-        scratch_shapes=[positions, positions],
-        compiler_params=params(),
-        cost_estimate=cost(8),
-        name="conv_state",
-    )(hyena_k, hyena_v, rim, par, short_filter)
-    states = lax.all_gather(state, "ctx", axis=0, tiled=True)
-    states = states.reshape(devices, blocks * modes, LANES)
-    return pl.pallas_call(
-        functools.partial(output_kernel, modes),
-        grid=(groups,),
-        in_specs=[
-            feature_spec,
-            feature_spec,
-            rim_spec,
-            par_spec,
-            pl.BlockSpec((devices, SUBLANES * modes, LANES), lambda group: (0, group, 0)),
-            taps_spec,
-        ],
-        out_specs=feature_spec,
-        out_shape=jax.ShapeDtypeStruct((rows, channels), jnp.bfloat16),
-        compiler_params=params(),
-        cost_estimate=cost(5),
-        name="conv_output",
-    )(hyena_q, local_result, rim, par, states, short_filter)
+
+    def first_part(token):
+        own_par, rim = pl.pallas_call(
+            conv_pack_kernel,
+            grid=(1,),
+            in_specs=[pl.BlockSpec((modes, residue.shape[0]), lambda step: (0, 0))] * 2
+            + [pl.BlockSpec((16, channels), lambda step: (end, 0))] * 3,
+            out_specs=[
+                pl.BlockSpec((devices, par_rows, LANES), lambda step: (0, 0, 0)),
+                pl.BlockSpec((8, channels), lambda step: (0, 0)),
+            ],
+            out_shape=[
+                jax.ShapeDtypeStruct((devices, par_rows, LANES), jnp.float32),
+                jax.ShapeDtypeStruct((8, channels), jnp.float32),
+            ],
+            compiler_params=params(),
+            cost_estimate=cost(1),
+            name="conv_pack",
+        )(after(decay_rate.T, token), residue.T, hyena_q, hyena_k, hyena_v)
+        par = lax.all_to_all(own_par, "ctx", split_axis=0, concat_axis=0, tiled=True)
+        par = par.reshape(devices * par_rows, LANES)
+        rim = lax.ppermute(rim, "ctx", [(index, index + 1) for index in range(devices - 1)])
+        local_result, state = pl.pallas_call(
+            functools.partial(state_kernel, modes),
+            grid=(groups,),
+            in_specs=[feature_spec, feature_spec, rim_spec, par_spec, taps_spec],
+            out_specs=[
+                feature_spec,
+                pl.BlockSpec((SUBLANES * modes, LANES), lambda group: (group, 0)),
+            ],
+            out_shape=[
+                jax.ShapeDtypeStruct((rows, channels), jnp.float32),
+                jax.ShapeDtypeStruct((blocks * modes, LANES), jnp.float32),
+            ],
+            scratch_shapes=[positions, positions],
+            compiler_params=params(),
+            cost_estimate=cost(9),
+            name="conv_state",
+        )(hyena_k, hyena_v, rim, par, short_filter)
+        return local_result, state, rim, par
+
+    def last_part(local_result, state, rim, par):
+        states = lax.all_gather(state, "ctx", axis=0, tiled=True)
+        states = states.reshape(devices, blocks * modes, LANES)
+        return pl.pallas_call(
+            functools.partial(output_kernel, modes),
+            grid=(groups,),
+            in_specs=[
+                feature_spec,
+                feature_spec,
+                rim_spec,
+                par_spec,
+                pl.BlockSpec((devices, SUBLANES * modes, LANES), lambda group: (0, group, 0)),
+                taps_spec,
+            ],
+            out_specs=feature_spec,
+            out_shape=jax.ShapeDtypeStruct((rows, channels), jnp.bfloat16),
+            compiler_params=params(),
+            cost_estimate=cost(6),
+            name="conv_output",
+        )(hyena_q, local_result, rim, par, states, short_filter)
+
+    return first_part, last_part
 
 
 def among(me, members):
@@ -245,20 +252,27 @@
 
 def pack_kernel(gathers, askers, widths, starts, q_ref, qs_ref, k_ref, v_ref, *rest):
     count = len(widths)
-    key_outs, query_outs, sems = rest[:count], rest[count : 2 * count], rest[-1]
+    key_outs, query_outs = rest[:count], rest[count : 2 * count]
+    stages, in_sems, out_sems = rest[2 * count : 4 * count], rest[-2], rest[-1]
     me = lax.axis_index("ctx")
     odd = me % 2
-    rows = q_ref.shape[0]
 
     def run(pairs):
-        copies = [
-            pltpu.make_async_copy(source, target, sems.at[index])
-            for index, (source, target) in enumerate(pairs)
+        loads = [
+            pltpu.make_async_copy(source, stage, in_sems.at[index])
+            for index, ((source, _), stage) in enumerate(zip(pairs, stages))
         ]
-        for copy in copies:
-            copy.start()
-        for copy in copies:
-            copy.wait()
+        stores = [
+            pltpu.make_async_copy(stage, target, out_sems.at[index])
+            for index, ((_, target), stage) in enumerate(zip(pairs, stages))
+        ]
+        for load in loads:
+            load.start()
+        for load, store in zip(loads, stores):
+            load.wait()
+            store.start()
+        for store in stores:
+            store.wait()
 
     def cut(ref, chunk):
         return ref.at[:, pl.ds(starts[chunk], widths[chunk])]
@@ -286,12 +300,17 @@
         )
 
 
-def spread(rows_of_heads, count):
-    lanes = lax.broadcasted_iota(jnp.int32, rows_of_heads[0].shape, 1)
-    sums = jnp.zeros_like(rows_of_heads[0])
-    for index, column in enumerate(rows_of_heads):
+def as_rows(columns):
+    lanes = lax.broadcasted_iota(jnp.int32, columns[0].shape, 1)
+    sums = jnp.zeros_like(columns[0])
+    for index, column in enumerate(columns):
         sums = jnp.where(lanes == index, column, sums)
-    return jnp.transpose(sums)[:count]
+    return jnp.transpose(sums)[:SUBLANES]
+
+
+def as_columns(part):
+    fill = jnp.zeros((LANES - part.shape[0], part.shape[1]), jnp.float32)
+    return jnp.transpose(jnp.concatenate([part, fill], 0))
 
 
 def partial_kernel(transfers, upper, *refs):
@@ -328,7 +347,7 @@
             mixed, lse = soft(q_ref[:, block_lanes(head)], keys, values, mask)
             own_ref[:, block_lanes(head)] = mixed
             sums.append(lse)
-        lse_ref[...] = spread(sums, SUBLANES)
+        lse_ref[...] = as_rows(sums)
 
         def answer(index):
             sums = [[], []]
@@ -336,17 +355,19 @@
                 keys, values = key_value(head, with_quad)
                 query = ask_refs[index][:, :, block_lanes(head)].reshape(2 * rows, HEAD_DIM)
                 mixed, lse = soft(query, keys, values)
-                first = lse.astype(jnp.bfloat16).astype(jnp.float32)
-                second = (lse - first).astype(jnp.bfloat16).astype(jnp.float32)
                 for half in range(2):
                     cut = slice(half * rows, (half + 1) * rows)
                     start = half * half_rows + head * rows
                     answer_refs[index][start : start + rows, :] = mixed[cut].astype(jnp.bfloat16)
-                    sums[half] += [first[cut], second[cut], (lse - first - second)[cut]]
+                    sums[half].append(lse[cut])
             for half in range(2):
                 start = half * half_rows + heads * rows
-                tail = spread(sums[half], TAIL).astype(jnp.bfloat16)
-                answer_refs[index][start : start + TAIL, :] = tail
+                lse = as_rows(sums[half])
+                first = lse.astype(jnp.bfloat16).astype(jnp.float32)
+                second = (lse - first).astype(jnp.bfloat16).astype(jnp.float32)
+                third = lse - first - second
+                tail = jnp.concatenate([first, second, third, jnp.zeros_like(lse)], 0)
+                answer_refs[index][start : start + TAIL, :] = tail.astype(jnp.bfloat16)
 
         for index, pairs in enumerate(transfers):
             asked = [target for _, target in pairs if (target in upper) == with_quad]
@@ -372,28 +393,25 @@
         returned += [members, [member ^ 1 for member in members]]
     answered = among(me, sorted(set(sum(returned, []))))
 
-    def columns(part):
-        fill = jnp.zeros((LANES - part.shape[0], rows), jnp.float32)
-        return jnp.transpose(jnp.concatenate([part, fill], 0))
-
     @pl.when(answered)
     def _():
-        own_sums = columns(lse_ref[...])
         valid = [among(me, members) for members in returned]
-        sums = [columns(ref[heads * rows :, :].astype(jnp.float32)) for ref in others]
+        logs = [lse_ref[...]]
+        for index, ref in enumerate(others):
+            tail = ref[heads * rows :, :].astype(jnp.float32)
+            tail = tail[:SUBLANES] + tail[SUBLANES : 2 * SUBLANES] + tail[2 * SUBLANES : 3 * SUBLANES]
+            logs.append(jnp.where(valid[index], tail, NEGATIVE))
+        top = functools.reduce(jnp.maximum, logs)
+        weights = [jnp.exp2(part - top) for part in logs]
+        total = functools.reduce(jnp.add, weights)
+        shares = [as_columns(weight / total) for weight in weights]
         for head in range(heads):
             cut = block_lanes(head)
-            logs = [own_sums[:, head : head + 1]]
             mixed = [own_ref[:, cut]]
             for index, ref in enumerate(others):
-                parts = [sums[index][:, 3 * head + part : 3 * head + part + 1] for part in range(3)]
-                logs.append(jnp.where(valid[index], parts[0] + parts[1] + parts[2], NEGATIVE))
                 part = ref[head * rows : (head + 1) * rows, :].astype(jnp.float32)
                 mixed.append(jnp.where(valid[index], part, 0.0))
-            top = functools.reduce(jnp.maximum, logs)
-            weights = [jnp.exp2(part - top) for part in logs]
-            total = functools.reduce(jnp.add, weights)
-            terms = [part * (weight / total) for part, weight in zip(mixed, weights)]
+            terms = [part * share[:, head : head + 1] for part, share in zip(mixed, shares)]
             out_ref[:, cut] = functools.reduce(jnp.add, terms).astype(out_ref.dtype)
 
     @pl.when(jnp.logical_not(answered))
@@ -405,7 +423,7 @@
     return lax.optimization_barrier((array, *others))[0]
 
 
-def attend(query, key, value):
+def attend(query, key, value, conv):
     rows, columns = query.shape
     devices = lax.axis_size("ctx")
     quads = devices // 4
@@ -441,27 +459,44 @@
             in_specs=[hbm] * 4,
             out_specs=[hbm] * (2 * len(members)),
             out_shape=shapes * 2,
-            scratch_shapes=[pltpu.SemaphoreType.DMA((2 * len(members),))],
+            scratch_shapes=[
+                pltpu.VMEM((rows, widths[chunk]), jnp.bfloat16)
+                for chunk in members
+                for _ in range(2)
+            ]
+            + [pltpu.SemaphoreType.DMA((2 * len(members),))] * 2,
             compiler_params=params(),
             cost_estimate=cost(1),
             name="att_pack",
         )(query, query_swapped, key, value)
         return list(zip(outs[: len(members)], outs[len(members) :]))
 
-    packs = pack([0]) + (pack(list(range(1, chunks))) if chunks > 1 else [])
-    asks, quad_kv = [], []
-    for chunk in range(chunks):
+    packs = pack([0])
+    conv_state, conv_output = conv
+    local_result, state, *conv_shared = conv_state(packs[0][1])
+    packs += pack(list(range(1, chunks))) if chunks > 1 else []
+    asks, quad_kv, all_answers = [], [], []
+
+    def send(chunk):
         key_pack, query_pack = packs[chunk]
         if chunk:
             key_pack = after(key_pack, quad_kv[-1][0])
             query_pack = after(query_pack, *asks[-1])
+        if chunk > 1:
+            key_pack = after(key_pack, all_answers[chunk - 2][0])
+            query_pack = after(query_pack, all_answers[chunk - 2][0])
         arrived = lax.ppermute(key_pack, "ctx", gathers)
         asks.append([lax.ppermute(query_pack, "ctx", pairs) for pairs in transfers])
         quad_kv.append([arrived, lax.ppermute(arrived, "ctx", swap)])
 
+    send(0)
     half_rows = HEADS_PER_STEP * rows + TAIL
     result = None
     for chunk in range(chunks):
+        if chunk + 1 < chunks:
+            send(chunk + 1)
+        if chunk == 0:
+            asks[0] = [after(asked, state) for asked in asks[0]]
         steps, first = CHUNK_STEPS[chunk], first_steps[chunk]
         whole_spec = pl.BlockSpec((rows, step_width), lambda step, first=first: (0, first + step))
         chunk_spec = pl.BlockSpec((rows, step_width), lambda step: (0, step))
@@ -483,6 +518,7 @@
             cost_estimate=cost(4),
             name="att_partial",
         )(query, key, value, key_swapped, value_swapped, *quad_kv[chunk], *asks[chunk])
+        all_answers.append(answers)
         operands = [me, own, lse]
         for answer, pairs in zip(answers, transfers):
             back = lax.ppermute(answer, "ctx", [(target, source) for source, target in pairs])
@@ -517,15 +553,15 @@
             cost_estimate=cost(2),
             name="att_merge",
         )(*operands)
-    return result
+    shared = [after(part, all_answers[-1][0]) for part in conv_shared]
+    return conv_output(local_result, state, *shared), result
 
 
 def local(
     hyena_q, hyena_k, hyena_v, short_filter, residue, decay_rate, att_query, att_key, att_value
 ):
-    att_out = attend(att_query, att_key, att_value)
-    hyena_out = convolve(hyena_q, hyena_k, hyena_v, short_filter, residue, decay_rate)
-    return (hyena_out, att_out)
+    conv = convolution(hyena_q, hyena_k, hyena_v, short_filter, residue, decay_rate)
+    return attend(att_query, att_key, att_value, conv)
 
 
 def solution(mesh):

time: 232 us -> 186 us (0.80)
  starting transfers between devices: 127 us -> 109 us
  waiting for transfers between devices: 29.3 us -> 13.5 us
  local copies, waits for them, and re-layouts: 6.9 us -> 0.01 us
  Pallas kernels: 54.3 us -> 48.1 us
    ppermute x1, starting transfers between devices: 59.1 us -> 0.36 us  [attend(): key_swapped = lax.ppermute(key, 'ctx', swap)]
    ppermute x13, starting transfers between devices: 18.9 us -> 66.2 us  [the longest x4 51.9 us: send(): quad_kv.append([arrived, lax.ppermute(arrived, 'ctx', swap)])]
    ppermute x13, waiting for transfers between devices: 26.2 us -> 0.32 us  [the longest x1 0.29 us: first_part(): lax.ppermute(rim, 'ctx', [(index, index + 1) for index in range(devices -...]
    ppermute x4, starting transfers between devices: 37.6 us -> 26.4 us  [attend(): operands += [back, lax.ppermute(back, 'ctx', swap)]]
    ppermute x4, waiting for transfers between devices: 0.01 us -> 10.5 us  [attend(): lax.ppermute(answer, 'ctx', [(target, source) for source, target in pairs])]
    unnamed x38 -> x2, local copies, waits for them, and re-layouts: 6.9 us -> 0.01 us
    pallas_call x4, Pallas kernels: 16.6 us -> 10.8 us  [attend(): pl.pallas_call(functools.partial(merge_kernel, transfers), grid_spec=pltp...]
    all_to_all x1, waiting for transfers between devices: 3.04 us -> 0.01 us  [first_part(): lax.all_to_all(own_par, 'ctx', split_axis=0, concat_axis=0, tiled=True)]
  transfers between devices with their start and end apart: 26 -> 26, of which waited for: 4 -> 5; matrix products, arithmetic and copies ran while one was open for 0% -> 0% of each run, Pallas kernels for 22% -> 21%
where the time goes in v4:
time: 186 us; the launch traced here: 185 us
  starting transfers between devices  109 us (59%)
  Pallas kernels  48.1 us (26%)
  between operations  14.1 us (8%)
  waiting for transfers between devices  13.5 us (7%)
    ppermute x4, starting transfers between devices, send(): quad_kv.append([arrived, lax.ppermute(arrived, 'ctx', swap)])  51.9 us
    ppermute x4, starting transfers between devices, attend(): operands += [back, lax.ppermute(back, 'ctx', swap)]  26.4 us
    pallas_call x4, Pallas kernels, attend(): pl.pallas_call(functools.partial(partial_kernel, transfers, upper), grid=...  18.8 us
    pallas_call x4, Pallas kernels, attend(): pl.pallas_call(functools.partial(merge_kernel, transfers), grid_spec=pltp...  10.8 us
    ppermute x4, waiting for transfers between devices, attend(): lax.ppermute(answer, 'ctx', [(target, source) for source, target in pairs])  10.5 us
    pallas_call x1, Pallas kernels, first_part(): pl.pallas_call(functools.partial(state_kernel, modes), grid=(groups,), in...  9.66 us
    ppermute x4, starting transfers between devices, attend(): lax.ppermute(answer, 'ctx', [(target, source) for source, target in pairs])  8.4 us
    all_to_all x1, starting transfers between devices, first_part(): lax.all_to_all(own_par, 'ctx', split_axis=0, concat_axis=0, tiled=True)  6.97 us
  transfers between devices with their start and end apart: 26, of which 5 were waited for; matrix products, arithmetic and copies ran while one was open for 0% of the time, Pallas kernels for 21%

profile of v4, /device:TPU:17, one launch (start us, length us, event | category | flops | bytes accessed | tf_op | source)
XLA Modules:
  0.0 185.0 jit_solution(6151065383073923493)
XLA Ops:
  7.2 0.7 collective-permute-start
  7.9 2.6 %collective-permute-done.qs_ref = bf16[128,4096]{1,0:T(8,128)(2,1)} collective-permute-done((bf16[128,4096]{1,0:T(8,128)(2,1)}, bf16[128,4096]{1,0:T(8,128)(2,1)}, u32[]{:S(2)}, u32[]{:S(2)}) %collective-permute-start) | collective-permute-done | bytes 1048608 | tf_op jit(solution)/shard_map/ppermute | solution.py:442
  10.6 2.0 %conv_pack.1 = (f32[8,128,128]{2,1,0:T(8,128)}, f32[8,4096]{1,0:T(8,128)}) custom-call(f32[16,512]{1,0:T(8,128)} %bitcast.6, f32[16,512]{1,0:T(8,128)} %bitcast.7, bf16[128,4096]{1,0:T(8,128)(2,1)} %q_ref.7, bf16[128,4096]{1,0:T(8,128)(2,1)} %k_ref.6, bf16[128,4096]{1,0:T(8,128)(2,1)} %v_ref.6), custom_call_target="tpu_custom_call" | custom-call | flops 1000000000 | bytes 1048576 | tf_op jit(solution)/shard_map/conv_pack/pallas_call | solution.py:161
  12.5 7.0 %all-to-all-start = ((f32[8,128,128]{2,1,0:T(8,128)}), f32[8,128,128]{2,1,0:T(8,128)}, u32[]{:S(2)}, u32[]{:S(2)}) async-start(f32[8,128,128]{2,1,0:T(8,128)} %get-tuple-element.43), calls=%async_computation | async-start | bytes 1048576 | tf_op jit(solution)/shard_map/all_to_all | solution.py:178
  19.5 1.5 collective-permute-start.4
  21.0 0.4 collective-permute-start.2
  21.3 0.1 collective-permute-start.3
  21.5 3.3 %collective-permute-start.1 = (f32[8,4096]{1,0:T(8,128)}, f32[8,4096]{1,0:T(8,128)S(1)}, u32[]{:S(2)}, u32[]{:S(2)}) collective-permute-start(f32[8,4096]{1,0:T(8,128)} %get-tuple-element.42), channel_id=1, source_target_pairs={{0,1},{1,2},{2,3},{3,4},{4,5},{5,6},{6,7},{8,9},{9,10},{10,11},{11... | collective-permute-start | bytes 393224 | tf_op jit(solution)/shard_map/ppermute | solution.py:180
  24.8 1.3 collective-permute-start.7
  26.1 0.2 att_pack.3
  26.3 0.0 collective-permute-done.4.refs_5_
  26.3 1.5 collective-permute-start.5
  27.8 0.3 collective-permute-done.1.rim_ref
  28.0 6.0 %collective-permute-start.6 = (bf16[2,128,1024]{2,1,0:T(8,128)(2,1)}, bf16[2,128,1024]{2,1,0:T(8,128)(2,1)}, u32[]{:S(2)}, u32[]{:S(2)}) collective-permute-start(bf16[2,128,1024]{2,1,0:T(8,128)(2,1)} %collective-permute-done.4.refs_5_), channel_id=1, source_target_pairs={{0,1},{1,0},{2,3},{3,2},{4,5},{5,4},{6,7},{7,6},{8,9},{9,8},{10,11... | collective-permute-start | bytes 1572872 | tf_op jit(solution)/shard_map/ppermute | solution.py:490
  34.1 9.7 %conv_state.1 = (f32[128,4096]{1,0:T(8,128)}, f32[512,128]{1,0:T(8,128)}) custom-call(bf16[128,4096]{1,0:T(8,128)(2,1)} %k_ref.6, bf16[128,4096]{1,0:T(8,128)(2,1)} %v_ref.6, f32[8,4096]{1,0:T(8,128)} %copy-done, f32[1024,128]{1,0:T(8,128)} %bitcast.2.par_ref, f32[3,3,4096]{2,1,0:T(4,128)} %taps_ref.3), custom_call_target="tpu_custom_call" | custom-call | flops 8999999488 | bytes 1048576 | tf_op jit(solution)/shard_map/conv_state/pallas_call | solution.py:181
  43.7 0.0 all-gather.2.cloned.1.call-update
  43.8 1.3 collective-permute-start.10
  45.1 0.0 collective-permute-done.5.refs_5_
  45.1 11.2 %collective-permute-start.9 = (bf16[2,128,1024]{2,1,0:T(8,128)(2,1)}, bf16[2,128,1024]{2,1,0:T(8,128)(2,1)}, u32[]{:S(2)}, u32[]{:S(2)}) collective-permute-start(bf16[2,128,1024]{2,1,0:T(8,128)(2,1)} %collective-permute-done.5.refs_5_), channel_id=1, source_target_pairs={{0,1},{1,0},{2,3},{3,2},{4,5},{5,4},{6,7},{7,6},{8,9},{9,8},{10,11... | collective-permute-start | bytes 1572872 | tf_op jit(solution)/shard_map/ppermute | solution.py:490
  56.3 0.0 collective-permute-done.2.refs_3_
  56.3 0.0 collective-permute-done.3.refs_4_
  56.3 0.0 collective-permute-done.6.refs_6_
  56.3 4.7 %att_partial.4 = (f32[128,1024]{1,0:T(8,128)}, f32[16,128]{1,0:T(8,128)}, bf16[2176,128]{1,0:T(8,128)(2,1)}) custom-call(bf16[128,4096]{1,0:T(8,128)(2,1)} %refs_0_.7, bf16[128,4096]{1,0:T(8,128)(2,1)} %refs_1_.7, bf16[128,4096]{1,0:T(8,128)(2,1)} %refs_2_.7, bf16[128,4096]{1,0:T(8,128)(2,1)} %collective-permute-done.2.refs_3_, ...), custom_call_target="tpu_custom_call" | custom-call | flops 4000000000 | bytes 1048576 | tf_op jit(solution)/shard_map/att_partial/pallas_call | solution.py:507
  61.0 1.5 collective-permute-start.8
  62.5 1.3 collective-permute-start.13
  63.8 4.7 %att_partial.5 = (f32[128,1024]{1,0:T(8,128)}, f32[16,128]{1,0:T(8,128)}, bf16[2176,128]{1,0:T(8,128)(2,1)}) custom-call(bf16[128,4096]{1,0:T(8,128)(2,1)} %refs_0_.7, bf16[128,4096]{1,0:T(8,128)(2,1)} %refs_1_.7, bf16[128,4096]{1,0:T(8,128)(2,1)} %refs_2_.7, bf16[128,4096]{1,0:T(8,128)(2,1)} %collective-permute-done.2.refs_3_, ...), custom_call_target="tpu_custom_call" | custom-call | flops 4000000000 | bytes 1048576 | tf_op jit(solution)/shard_map/att_partial/pallas_call | solution.py:507
  68.5 1.5 collective-permute-start.11
  70.0 29.4 %collective-permute-start.17 = (bf16[2,128,1024]{2,1,0:T(8,128)(2,1)}, bf16[2,128,1024]{2,1,0:T(8,128)(2,1)}, u32[]{:S(2)}, u32[]{:S(2)}) collective-permute-start(bf16[2,128,1024]{2,1,0:T(8,128)(2,1)} %collective-permute-done.8.refs_5_), channel_id=1, source_target_pairs={{0,1},{1,0},{2,3},{3,2},{4,5},{5,4},{6,7},{7,6},{8,9},{9,8},{10,11... | collective-permute-start | bytes 1572872 | tf_op jit(solution)/shard_map/ppermute | solution.py:490
  99.4 1.3 collective-permute-start.14
  100.7 5.3 %collective-permute-start.12 = (bf16[2,128,1024]{2,1,0:T(8,128)(2,1)}, bf16[2,128,1024]{2,1,0:T(8,128)(2,1)}, u32[]{:S(2)}, u32[]{:S(2)}) collective-permute-start(bf16[2,128,1024]{2,1,0:T(8,128)(2,1)} %collective-permute-done.11.refs_5_), channel_id=1, source_target_pairs={{0,1},{1,0},{2,3},{3,2},{4,5},{5,4},{6,7},{7,6},{8,9},{9,8},{10,11... | collective-permute-start | bytes 1572872 | tf_op jit(solution)/shard_map/ppermute | solution.py:490
  106.0 2.1 %collective-permute-start.22 = (bf16[2176,128]{1,0:T(8,128)(2,1)}, bf16[2176,128]{1,0:T(8,128)(2,1)}, u32[]{:S(2)}, u32[]{:S(2)}) collective-permute-start(bf16[2176,128]{1,0:T(8,128)(2,1)} %get-tuple-element.53), channel_id=1, source_target_pairs={{5,7},{2,4},{3,6},{13,15},{10,12},{11,14},{21,23},{18,20},{19,22},... | collective-permute-start | bytes 1671176 | tf_op jit(solution)/shard_map/ppermute | solution.py:524
  108.1 2.1 %collective-permute-start.20 = (bf16[2176,128]{1,0:T(8,128)(2,1)}, bf16[2176,128]{1,0:T(8,128)(2,1)}, u32[]{:S(2)}, u32[]{:S(2)}) collective-permute-start(bf16[2176,128]{1,0:T(8,128)(2,1)} %get-tuple-element.58), channel_id=1, source_target_pairs={{5,7},{2,4},{3,6},{13,15},{10,12},{11,14},{21,23},{18,20},{19,22},... | collective-permute-start | bytes 1671176 | tf_op jit(solution)/shard_map/ppermute | solution.py:524
  110.2 4.7 %att_partial.7 = (f32[128,1024]{1,0:T(8,128)}, f32[16,128]{1,0:T(8,128)}, bf16[2176,128]{1,0:T(8,128)(2,1)}) custom-call(bf16[128,4096]{1,0:T(8,128)(2,1)} %refs_0_.7, bf16[128,4096]{1,0:T(8,128)(2,1)} %refs_1_.7, bf16[128,4096]{1,0:T(8,128)(2,1)} %refs_2_.7, bf16[128,4096]{1,0:T(8,128)(2,1)} %collective-permute-done.2.refs_3_, ...), custom_call_target="tpu_custom_call" | custom-call | flops 4000000000 | bytes 1048576 | tf_op jit(solution)/shard_map/att_partial/pallas_call | solution.py:507
  114.8 2.1 %collective-permute-start.18 = (bf16[2176,128]{1,0:T(8,128)(2,1)}, bf16[2176,128]{1,0:T(8,128)(2,1)}, u32[]{:S(2)}, u32[]{:S(2)}) collective-permute-start(bf16[2176,128]{1,0:T(8,128)(2,1)} %get-tuple-element.73), channel_id=1, source_target_pairs={{5,7},{2,4},{3,6},{13,15},{10,12},{11,14},{21,23},{18,20},{19,22},... | collective-permute-start | bytes 1671176 | tf_op jit(solution)/shard_map/ppermute | solution.py:524
  117.0 4.7 %att_partial.6 = (f32[128,1024]{1,0:T(8,128)}, f32[16,128]{1,0:T(8,128)}, bf16[2176,128]{1,0:T(8,128)(2,1)}) custom-call(bf16[128,4096]{1,0:T(8,128)(2,1)} %refs_0_.7, bf16[128,4096]{1,0:T(8,128)(2,1)} %refs_1_.7, bf16[128,4096]{1,0:T(8,128)(2,1)} %refs_2_.7, bf16[128,4096]{1,0:T(8,128)(2,1)} %collective-permute-done.2.refs_3_, ...), custom_call_target="tpu_custom_call" | custom-call | flops 4000000000 | bytes 1048576 | tf_op jit(solution)/shard_map/att_partial/pallas_call | solution.py:507
  121.6 2.1 %collective-permute-start.15 = (bf16[2176,128]{1,0:T(8,128)(2,1)}, bf16[2176,128]{1,0:T(8,128)(2,1)}, u32[]{:S(2)}, u32[]{:S(2)}) collective-permute-start(bf16[2176,128]{1,0:T(8,128)(2,1)} %get-tuple-element.66), channel_id=1, source_target_pairs={{5,7},{2,4},{3,6},{13,15},{10,12},{11,14},{21,23},{18,20},{19,22},... | collective-permute-start | bytes 1671176 | tf_op jit(solution)/shard_map/ppermute | solution.py:524
  123.7 1.3 collective-permute-start.23
  125.0 3.5 %collective-permute-done.20.refs_0_ = bf16[2176,128]{1,0:T(8,128)(2,1)} collective-permute-done((bf16[2176,128]{1,0:T(8,128)(2,1)}, bf16[2176,128]{1,0:T(8,128)(2,1)}, u32[]{:S(2)}, u32[]{:S(2)}) %collective-permute-start.20) | collective-permute-done | bytes 557088 | tf_op jit(solution)/shard_map/ppermute | solution.py:524
  128.5 8.4 %collective-permute-start.21 = (bf16[2176,128]{1,0:T(8,128)(2,1)}, bf16[2176,128]{1,0:T(8,128)(2,1)}, u32[]{:S(2)}, u32[]{:S(2)}) collective-permute-start(bf16[2176,128]{1,0:T(8,128)(2,1)} %collective-permute-done.20.refs_0_), channel_id=1, source_target_pairs={{0,1},{1,0},{2,3},{3,2},{4,5},{5,4},{6,7},{7,6},{8,9},{9,8},{10,11... | collective-permute-start | bytes 1671176 | tf_op jit(solution)/shard_map/ppermute | solution.py:525
  137.0 3.5 %collective-permute-done.18.refs_0_ = bf16[2176,128]{1,0:T(8,128)(2,1)} collective-permute-done((bf16[2176,128]{1,0:T(8,128)(2,1)}, bf16[2176,128]{1,0:T(8,128)(2,1)}, u32[]{:S(2)}, u32[]{:S(2)}) %collective-permute-start.18) | collective-permute-done | bytes 557088 | tf_op jit(solution)/shard_map/ppermute | solution.py:524
  140.5 8.4 %collective-permute-start.19 = (bf16[2176,128]{1,0:T(8,128)(2,1)}, bf16[2176,128]{1,0:T(8,128)(2,1)}, u32[]{:S(2)}, u32[]{:S(2)}) collective-permute-start(bf16[2176,128]{1,0:T(8,128)(2,1)} %collective-permute-done.18.refs_0_), channel_id=1, source_target_pairs={{0,1},{1,0},{2,3},{3,2},{4,5},{5,4},{6,7},{7,6},{8,9},{9,8},{10,11... | collective-permute-start | bytes 1671176 | tf_op jit(solution)/shard_map/ppermute | solution.py:525
  148.9 3.5 %collective-permute-done.15.refs_0_ = bf16[2176,128]{1,0:T(8,128)(2,1)} collective-permute-done((bf16[2176,128]{1,0:T(8,128)(2,1)}, bf16[2176,128]{1,0:T(8,128)(2,1)}, u32[]{:S(2)}, u32[]{:S(2)}) %collective-permute-start.15) | collective-permute-done | bytes 557088 | tf_op jit(solution)/shard_map/ppermute | solution.py:524
  152.4 8.2 %collective-permute-start.16 = (bf16[2176,128]{1,0:T(8,128)(2,1)}, bf16[2176,128]{1,0:T(8,128)(2,1)}, u32[]{:S(2)}, u32[]{:S(2)}) collective-permute-start(bf16[2176,128]{1,0:T(8,128)(2,1)} %collective-permute-done.15.refs_0_), channel_id=1, source_target_pairs={{0,1},{1,0},{2,3},{3,2},{4,5},{5,4},{6,7},{7,6},{8,9},{9,8},{10,11... | collective-permute-start | bytes 1671176 | tf_op jit(solution)/shard_map/ppermute | solution.py:525
  160.7 2.7 %att_merge.4.refs_2_ = bf16[128,4096]{1,0:T(8,128)(2,1)} custom-call(s32[1]{0:T(128)} %bitcast.4.me_ref, f32[128,1024]{1,0:T(8,128)} %get-tuple-element.76.own_ref, f32[16,128]{1,0:T(8,128)} %get-tuple-element.77.lse_ref, bf16[2176,128]{1,0:T(8,128)(2,1)} %collective-permute-done.22.refs_0_, bf16[2176,128]{1,0:T(8,128)(2,1)} %collective-permute-done.23.refs_1_), custom_call_target="tpu_custom_call" | custom-call | flops 2000000000 | bytes 1048576 | tf_op jit(solution)/shard_map/att_merge/pallas_call | solution.py:542
  163.4 2.7 %att_merge.5.refs_2_ = bf16[128,4096]{1,0:T(8,128)(2,1)} custom-call(s32[1]{0:T(128)} %bitcast.4.me_ref, f32[128,1024]{1,0:T(8,128)} %get-tuple-element.74.own_ref, f32[16,128]{1,0:T(8,128)} %get-tuple-element.75.lse_ref, bf16[2176,128]{1,0:T(8,128)(2,1)} %collective-permute-done.20.refs_0_, ...), custom_call_target="tpu_custom_call", output_to_operand_aliasing={{}: (5, {})} | custom-call | flops 2000000000 | bytes 1048576 | tf_op jit(solution)/shard_map/att_merge/pallas_call | solution.py:542
  166.1 2.7 %att_merge.6.refs_2_ = bf16[128,4096]{1,0:T(8,128)(2,1)} custom-call(s32[1]{0:T(128)} %bitcast.4.me_ref, f32[128,1024]{1,0:T(8,128)} %get-tuple-element.71.own_ref, f32[16,128]{1,0:T(8,128)} %get-tuple-element.72.lse_ref, bf16[2176,128]{1,0:T(8,128)(2,1)} %collective-permute-done.18.refs_0_, ...), custom_call_target="tpu_custom_call", output_to_operand_aliasing={{}: (5, {})} | custom-call | flops 2000000000 | bytes 1048576 | tf_op jit(solution)/shard_map/att_merge/pallas_call | solution.py:542
  168.8 2.7 %att_merge.7 = bf16[128,4096]{1,0:T(8,128)(2,1)} custom-call(s32[1]{0:T(128)} %bitcast.4.me_ref, f32[128,1024]{1,0:T(8,128)} %get-tuple-element.69.own_ref, f32[16,128]{1,0:T(8,128)} %get-tuple-element.70.lse_ref, bf16[2176,128]{1,0:T(8,128)(2,1)} %collective-permute-done.15.refs_0_, ...), custom_call_target="tpu_custom_call", output_to_operand_aliasing={{}: (5, {})} | custom-call | flops 2000000000 | bytes 1048576 | tf_op jit(solution)/shard_map/att_merge/pallas_call | solution.py:542
  171.5 6.7 %conv_output.1 = bf16[128,4096]{1,0:T(8,128)(2,1)} custom-call(bf16[128,4096]{1,0:T(8,128)(2,1)} %q_ref.7, f32[128,4096]{1,0:T(8,128)} %get-tuple-element.44.y_ref, f32[8,4096]{1,0:T(8,128)} %copy-done, f32[1024,128]{1,0:T(8,128)} %bitcast.2.par_ref, f32[8,512,128]{2,1,0:T(8,128)} %bitcast.5, f32[3,3,4096]{2,1,0:T(4,128)} %taps_ref.3), custom_call_target="tpu_custom_call" | custom-call | flops 6000000000 | bytes 1048576 | tf_op jit(solution)/shard_map/conv_output/pallas_call | solution.py:203
  (20 shorter events, 0.1 us)
Async XLA Ops:
  7.2 3.4 %collective-permute-start = (bf16[128,4096]{1,0:T(8,128)(2,1)}, bf16[128,4096]{1,0:T(8,128)(2,1)}, u32[]{:S(2)}, u32[]{:S(2)}) collective-permute-start(bf16[128,4096]{1,0:T(8,128)(2,1)} %refs_0_.7), channel_id=1, source_target_pairs={{0,1},{1,0},{2,3},{3,2},{4,5},{5,4},{6,7},{7,6},{8,9},{9,8},{10,11... | collective-permute-start | bytes 3145736 | tf_op jit(solution)/shard_map/ppermute | solution.py:442
  12.5 21.5 %all-to-all-start = ((f32[8,128,128]{2,1,0:T(8,128)}), f32[8,128,128]{2,1,0:T(8,128)}, u32[]{:S(2)}, u32[]{:S(2)}) async-start(f32[8,128,128]{2,1,0:T(8,128)} %get-tuple-element.43), calls=%async_computation | async-start | bytes 1048576 | tf_op jit(solution)/shard_map/all_to_all | solution.py:178
  19.5 152.0 %all-gather.2.cloned.1.call-start = ((), (), s32[]{:S(2)}) async-start(), calls=%async_computation.1 | async-start | bytes 2359296 | tf_op jit(solution)/shard_map/all_gather | solution.py:201
  19.5 6.8 %collective-permute-start.4 = (bf16[2,128,1024]{2,1,0:T(8,128)(2,1)}, bf16[2,128,1024]{2,1,0:T(8,128)(2,1)}, u32[]{:S(2)}, u32[]{:S(2)}) collective-permute-start(bf16[2,128,1024]{2,1,0:T(8,128)(2,1)} %get-tuple-element.48), channel_id=1, source_target_pairs={{0,2},{1,3},{8,10},{9,11},{16,18},{17,19},{24,26},{25,27}} | collective-permute-start | bytes 1572872 | tf_op jit(solution)/shard_map/ppermute | solution.py:488
  21.0 35.3 %collective-permute-start.2 = (bf16[128,4096]{1,0:T(8,128)(2,1)}, bf16[128,4096]{1,0:T(8,128)(2,1)}, u32[]{:S(2)}, u32[]{:S(2)}) collective-permute-start(bf16[128,4096]{1,0:T(8,128)(2,1)} %refs_1_.7), channel_id=1, source_target_pairs={{0,1},{1,0},{2,3},{3,2},{4,5},{5,4},{6,7},{7,6},{8,9},{9,8},{10,11... | collective-permute-start | bytes 3145736 | tf_op jit(solution)/shard_map/ppermute | solution.py:443
  21.3 35.0 %collective-permute-start.3 = (bf16[128,4096]{1,0:T(8,128)(2,1)}, bf16[128,4096]{1,0:T(8,128)(2,1)}, u32[]{:S(2)}, u32[]{:S(2)}) collective-permute-start(bf16[128,4096]{1,0:T(8,128)(2,1)} %refs_2_.7), channel_id=1, source_target_pairs={{0,1},{1,0},{2,3},{3,2},{4,5},{5,4},{6,7},{7,6},{8,9},{9,8},{10,11... | collective-permute-start | bytes 3145736 | tf_op jit(solution)/shard_map/ppermute | solution.py:444
  21.5 6.6 %collective-permute-start.1 = (f32[8,4096]{1,0:T(8,128)}, f32[8,4096]{1,0:T(8,128)S(1)}, u32[]{:S(2)}, u32[]{:S(2)}) collective-permute-start(f32[8,4096]{1,0:T(8,128)} %get-tuple-element.42), channel_id=1, source_target_pairs={{0,1},{1,2},{2,3},{3,4},{4,5},{5,6},{6,7},{8,9},{9,10},{10,11},{11... | collective-permute-start | bytes 393224 | tf_op jit(solution)/shard_map/ppermute | solution.py:180
  24.8 19.0 %collective-permute-start.7 = (bf16[2,128,1024]{2,1,0:T(8,128)(2,1)}, bf16[2,128,1024]{2,1,0:T(8,128)(2,1)}, u32[]{:S(2)}, u32[]{:S(2)}) collective-permute-start(bf16[2,128,1024]{2,1,0:T(8,128)(2,1)} %get-tuple-element.40), channel_id=1, source_target_pairs={{7,5},{4,2},{6,3},{15,13},{12,10},{14,11},{23,21},{20,18},{22,19},... | collective-permute-start | bytes 1572872 | tf_op jit(solution)/shard_map/ppermute | solution.py:489
  26.3 18.8 %collective-permute-start.5 = (bf16[2,128,1024]{2,1,0:T(8,128)(2,1)}, bf16[2,128,1024]{2,1,0:T(8,128)(2,1)}, u32[]{:S(2)}, u32[]{:S(2)}) collective-permute-start(bf16[2,128,1024]{2,1,0:T(8,128)(2,1)} %get-tuple-element.49), channel_id=1, source_target_pairs={{0,2},{1,3},{8,10},{9,11},{16,18},{17,19},{24,26},{25,27}} | collective-permute-start | bytes 1572872 | tf_op jit(solution)/shard_map/ppermute | solution.py:488
  28.0 6.0 %copy-start = (f32[8,4096]{1,0:T(8,128)}, f32[8,4096]{1,0:T(8,128)S(1)}, u32[]{:S(2)}) copy-start(f32[8,4096]{1,0:T(8,128)S(1)} %collective-permute-done.1.rim_ref) | copy-start | bytes 393220
  28.0 28.3 %collective-permute-start.6 = (bf16[2,128,1024]{2,1,0:T(8,128)(2,1)}, bf16[2,128,1024]{2,1,0:T(8,128)(2,1)}, u32[]{:S(2)}, u32[]{:S(2)}) collective-permute-start(bf16[2,128,1024]{2,1,0:T(8,128)(2,1)} %collective-permute-done.4.refs_5_), channel_id=1, source_target_pairs={{0,1},{1,0},{2,3},{3,2},{4,5},{5,4},{6,7},{7,6},{8,9},{9,8},{10,11... | collective-permute-start | bytes 1572872 | tf_op jit(solution)/shard_map/ppermute | solution.py:490
  43.8 18.7 %collective-permute-start.10 = (bf16[2,128,1024]{2,1,0:T(8,128)(2,1)}, bf16[2,128,1024]{2,1,0:T(8,128)(2,1)}, u32[]{:S(2)}, u32[]{:S(2)}) collective-permute-start(bf16[2,128,1024]{2,1,0:T(8,128)(2,1)} %get-tuple-element.57), channel_id=1, source_target_pairs={{7,5},{4,2},{6,3},{15,13},{12,10},{14,11},{23,21},{20,18},{22,19},... | collective-permute-start | bytes 1572872 | tf_op jit(solution)/shard_map/ppermute | solution.py:489
  45.1 18.7 %collective-permute-start.9 = (bf16[2,128,1024]{2,1,0:T(8,128)(2,1)}, bf16[2,128,1024]{2,1,0:T(8,128)(2,1)}, u32[]{:S(2)}, u32[]{:S(2)}) collective-permute-start(bf16[2,128,1024]{2,1,0:T(8,128)(2,1)} %collective-permute-done.5.refs_5_), channel_id=1, source_target_pairs={{0,1},{1,0},{2,3},{3,2},{4,5},{5,4},{6,7},{7,6},{8,9},{9,8},{10,11... | collective-permute-start | bytes 1572872 | tf_op jit(solution)/shard_map/ppermute | solution.py:490
  61.0 7.5 %collective-permute-start.8 = (bf16[2,128,1024]{2,1,0:T(8,128)(2,1)}, bf16[2,128,1024]{2,1,0:T(8,128)(2,1)}, u32[]{:S(2)}, u32[]{:S(2)}) collective-permute-start(bf16[2,128,1024]{2,1,0:T(8,128)(2,1)} %get-tuple-element.54), channel_id=1, source_target_pairs={{0,2},{1,3},{8,10},{9,11},{16,18},{17,19},{24,26},{25,27}} | collective-permute-start | bytes 1572872 | tf_op jit(solution)/shard_map/ppermute | solution.py:488
  62.5 36.9 %collective-permute-start.13 = (bf16[2,128,1024]{2,1,0:T(8,128)(2,1)}, bf16[2,128,1024]{2,1,0:T(8,128)(2,1)}, u32[]{:S(2)}, u32[]{:S(2)}) collective-permute-start(bf16[2,128,1024]{2,1,0:T(8,128)(2,1)} %get-tuple-element.63), channel_id=1, source_target_pairs={{7,5},{4,2},{6,3},{15,13},{12,10},{14,11},{23,21},{20,18},{22,19},... | collective-permute-start | bytes 1572872 | tf_op jit(solution)/shard_map/ppermute | solution.py:489
  68.5 32.2 %collective-permute-start.11 = (bf16[2,128,1024]{2,1,0:T(8,128)(2,1)}, bf16[2,128,1024]{2,1,0:T(8,128)(2,1)}, u32[]{:S(2)}, u32[]{:S(2)}) collective-permute-start(bf16[2,128,1024]{2,1,0:T(8,128)(2,1)} %get-tuple-element.59), channel_id=1, source_target_pairs={{0,2},{1,3},{8,10},{9,11},{16,18},{17,19},{24,26},{25,27}} | collective-permute-start | bytes 1572872 | tf_op jit(solution)/shard_map/ppermute | solution.py:488
  70.0 40.2 %collective-permute-start.17 = (bf16[2,128,1024]{2,1,0:T(8,128)(2,1)}, bf16[2,128,1024]{2,1,0:T(8,128)(2,1)}, u32[]{:S(2)}, u32[]{:S(2)}) collective-permute-start(bf16[2,128,1024]{2,1,0:T(8,128)(2,1)} %collective-permute-done.8.refs_5_), channel_id=1, source_target_pairs={{0,1},{1,0},{2,3},{3,2},{4,5},{5,4},{6,7},{7,6},{8,9},{9,8},{10,11... | collective-permute-start | bytes 1572872 | tf_op jit(solution)/shard_map/ppermute | solution.py:490
  99.4 17.5 %collective-permute-start.14 = (bf16[2,128,1024]{2,1,0:T(8,128)(2,1)}, bf16[2,128,1024]{2,1,0:T(8,128)(2,1)}, u32[]{:S(2)}, u32[]{:S(2)}) collective-permute-start(bf16[2,128,1024]{2,1,0:T(8,128)(2,1)} %get-tuple-element.65), channel_id=1, source_target_pairs={{7,5},{4,2},{6,3},{15,13},{12,10},{14,11},{23,21},{20,18},{22,19},... | collective-permute-start | bytes 1572872 | tf_op jit(solution)/shard_map/ppermute | solution.py:489
  100.7 16.2 %collective-permute-start.12 = (bf16[2,128,1024]{2,1,0:T(8,128)(2,1)}, bf16[2,128,1024]{2,1,0:T(8,128)(2,1)}, u32[]{:S(2)}, u32[]{:S(2)}) collective-permute-start(bf16[2,128,1024]{2,1,0:T(8,128)(2,1)} %collective-permute-done.11.refs_5_), channel_id=1, source_target_pairs={{0,1},{1,0},{2,3},{3,2},{4,5},{5,4},{6,7},{7,6},{8,9},{9,8},{10,11... | collective-permute-start | bytes 1572872 | tf_op jit(solution)/shard_map/ppermute | solution.py:490
  106.0 17.8 %collective-permute-start.22 = (bf16[2176,128]{1,0:T(8,128)(2,1)}, bf16[2176,128]{1,0:T(8,128)(2,1)}, u32[]{:S(2)}, u32[]{:S(2)}) collective-permute-start(bf16[2176,128]{1,0:T(8,128)(2,1)} %get-tuple-element.53), channel_id=1, source_target_pairs={{5,7},{2,4},{3,6},{13,15},{10,12},{11,14},{21,23},{18,20},{19,22},... | collective-permute-start | bytes 1671176 | tf_op jit(solution)/shard_map/ppermute | solution.py:524
  108.1 20.5 %collective-permute-start.20 = (bf16[2176,128]{1,0:T(8,128)(2,1)}, bf16[2176,128]{1,0:T(8,128)(2,1)}, u32[]{:S(2)}, u32[]{:S(2)}) collective-permute-start(bf16[2176,128]{1,0:T(8,128)(2,1)} %get-tuple-element.58), channel_id=1, source_target_pairs={{5,7},{2,4},{3,6},{13,15},{10,12},{11,14},{21,23},{18,20},{19,22},... | collective-permute-start | bytes 1671176 | tf_op jit(solution)/shard_map/ppermute | solution.py:524
  114.8 25.6 %collective-permute-start.18 = (bf16[2176,128]{1,0:T(8,128)(2,1)}, bf16[2176,128]{1,0:T(8,128)(2,1)}, u32[]{:S(2)}, u32[]{:S(2)}) collective-permute-start(bf16[2176,128]{1,0:T(8,128)(2,1)} %get-tuple-element.73), channel_id=1, source_target_pairs={{5,7},{2,4},{3,6},{13,15},{10,12},{11,14},{21,23},{18,20},{19,22},... | collective-permute-start | bytes 1671176 | tf_op jit(solution)/shard_map/ppermute | solution.py:524
  121.6 30.8 %collective-permute-start.15 = (bf16[2176,128]{1,0:T(8,128)(2,1)}, bf16[2176,128]{1,0:T(8,128)(2,1)}, u32[]{:S(2)}, u32[]{:S(2)}) collective-permute-start(bf16[2176,128]{1,0:T(8,128)(2,1)} %get-tuple-element.66), channel_id=1, source_target_pairs={{5,7},{2,4},{3,6},{13,15},{10,12},{11,14},{21,23},{18,20},{19,22},... | collective-permute-start | bytes 1671176 | tf_op jit(solution)/shard_map/ppermute | solution.py:524
  123.7 36.9 %collective-permute-start.23 = (bf16[2176,128]{1,0:T(8,128)(2,1)}, bf16[2176,128]{1,0:T(8,128)(2,1)}, u32[]{:S(2)}, u32[]{:S(2)}) collective-permute-start(bf16[2176,128]{1,0:T(8,128)(2,1)} %collective-permute-done.22.refs_0_), channel_id=1, source_target_pairs={{0,1},{1,0},{2,3},{3,2},{4,5},{5,4},{6,7},{7,6},{8,9},{9,8},{10,11... | collective-permute-start | bytes 1671176 | tf_op jit(solution)/shard_map/ppermute | solution.py:525
  128.5 34.8 %collective-permute-start.21 = (bf16[2176,128]{1,0:T(8,128)(2,1)}, bf16[2176,128]{1,0:T(8,128)(2,1)}, u32[]{:S(2)}, u32[]{:S(2)}) collective-permute-start(bf16[2176,128]{1,0:T(8,128)(2,1)} %collective-permute-done.20.refs_0_), channel_id=1, source_target_pairs={{0,1},{1,0},{2,3},{3,2},{4,5},{5,4},{6,7},{7,6},{8,9},{9,8},{10,11... | collective-permute-start | bytes 1671176 | tf_op jit(solution)/shard_map/ppermute | solution.py:525
  140.5 25.6 %collective-permute-start.19 = (bf16[2176,128]{1,0:T(8,128)(2,1)}, bf16[2176,128]{1,0:T(8,128)(2,1)}, u32[]{:S(2)}, u32[]{:S(2)}) collective-permute-start(bf16[2176,128]{1,0:T(8,128)(2,1)} %collective-permute-done.18.refs_0_), channel_id=1, source_target_pairs={{0,1},{1,0},{2,3},{3,2},{4,5},{5,4},{6,7},{7,6},{8,9},{9,8},{10,11... | collective-permute-start | bytes 1671176 | tf_op jit(solution)/shard_map/ppermute | solution.py:525
  152.4 16.3 %collective-permute-start.16 = (bf16[2176,128]{1,0:T(8,128)(2,1)}, bf16[2176,128]{1,0:T(8,128)(2,1)}, u32[]{:S(2)}, u32[]{:S(2)}) collective-permute-start(bf16[2176,128]{1,0:T(8,128)(2,1)} %collective-permute-done.15.refs_0_), channel_id=1, source_target_pairs={{0,1},{1,0},{2,3},{3,2},{4,5},{5,4},{6,7},{7,6},{8,9},{9,8},{10,11... | collective-permute-start | bytes 1671176 | tf_op jit(solution)/shard_map/ppermute | solution.py:525
Sparse Core Ops, SparseCore 0:
  43.9 49.9 all-gather.1

commit v5 on v4

--- a/solution.py
+++ b/solution.py
@@ -26,7 +26,7 @@
 
 def cost(microseconds):
     return pl.CostEstimate(
-        flops=microseconds * 10**9, bytes_accessed=2**20, transcendentals=0
+        flops=microseconds * 10**8, bytes_accessed=2**16, transcendentals=0
     )
 
 
@@ -98,8 +98,7 @@
         y_ref[:, block_lanes(block)] = y_scr[pl.ds(block, rows, SUBLANES), :]
 
 
-def output_kernel(modes, q_ref, y_ref, rim_ref, par_ref, state_ref, taps_ref, out_ref):
-    me = lax.axis_index("ctx")
+def output_kernel(modes, q_ref, y_ref, rim_ref, par_ref, enter_ref, taps_ref, out_ref):
     rows = q_ref.shape[0]
     step = lax.broadcasted_iota(jnp.int32, (SUBLANES, LANES), 0).astype(jnp.float32) + 1.0
 
@@ -107,12 +106,7 @@
         lanes = pl.ds(pl.multiple_of(block * LANES, LANES), LANES)
         rate = par_ref[pl.ds(pl.multiple_of(2 * block * modes, SUBLANES), modes), :]
         residue = par_ref[pl.ds(pl.multiple_of((2 * block + 1) * modes, SUBLANES), modes), :]
-        chunk_decay = jnp.exp(-rate * rows)
-        entering = jnp.zeros((modes, LANES), jnp.float32)
-        for device in range(state_ref.shape[0] - 1):
-            start = pl.multiple_of(block * modes, SUBLANES)
-            after = entering * chunk_decay + state_ref[device, pl.ds(start, modes), :]
-            entering = jnp.where(device < me, after, entering)
+        entering = enter_ref[pl.ds(pl.multiple_of(block * modes, SUBLANES), modes), :]
         weighted = residue * entering
         eight = jnp.exp(-rate * SUBLANES)
         terms = [
@@ -174,10 +168,10 @@
             compiler_params=params(),
             cost_estimate=cost(1),
             name="conv_pack",
-        )(after(decay_rate.T, token), residue.T, hyena_q, hyena_k, hyena_v)
-        par = lax.all_to_all(own_par, "ctx", split_axis=0, concat_axis=0, tiled=True)
+        )(decay_rate.T, residue.T, hyena_q, hyena_k, hyena_v)
+        par = lax.all_to_all(after(own_par, token), "ctx", split_axis=0, concat_axis=0, tiled=True)
         par = par.reshape(devices * par_rows, LANES)
-        rim = lax.ppermute(rim, "ctx", [(index, index + 1) for index in range(devices - 1)])
+        rim = lax.ppermute(after(rim, token), "ctx", [(index, index + 1) for index in range(devices - 1)])
         local_result, state = pl.pallas_call(
             functools.partial(state_kernel, modes),
             grid=(groups,),
@@ -195,11 +189,26 @@
             cost_estimate=cost(9),
             name="conv_state",
         )(hyena_k, hyena_v, rim, par, short_filter)
-        return local_result, state, rim, par
-
-    def last_part(local_result, state, rim, par):
-        states = lax.all_gather(state, "ctx", axis=0, tiled=True)
-        states = states.reshape(devices, blocks * modes, LANES)
+        return local_result, entering_state(state, par), rim, par
+
+    def entering_state(state, par):
+        me = lax.axis_index("ctx")
+        swap = [(index, index ^ 1) for index in range(devices)]
+        rate = par.reshape(blocks, 2 * modes, LANES)[:, :modes].reshape(blocks * modes, LANES)
+        other = lax.ppermute(state, "ctx", swap)
+        total = state + jnp.exp(-rows * rate) * other
+        entering = jnp.zeros_like(state)
+        reach = 1
+        while 2 * reach < devices:
+            moves = [(index, index + 2 * reach) for index in range(1, devices - 2 * reach, 2)]
+            arrived = lax.ppermute(total, "ctx", moves)
+            entering = entering + jnp.exp(-2.0 * rows * (reach - 1) * rate) * arrived
+            total = total + jnp.exp(-2.0 * rows * reach * rate) * arrived
+            reach *= 2
+        from_second = lax.ppermute(entering, "ctx", swap)
+        return jnp.where(me % 2 == 1, jnp.exp(-rows * rate) * entering + other, from_second)
+
+    def last_part(local_result, entering, rim, par):
         return pl.pallas_call(
             functools.partial(output_kernel, modes),
             grid=(groups,),
@@ -208,7 +217,7 @@
                 feature_spec,
                 rim_spec,
                 par_spec,
-                pl.BlockSpec((devices, SUBLANES * modes, LANES), lambda group: (0, group, 0)),
+                pl.BlockSpec((SUBLANES * modes, LANES), lambda group: (group, 0)),
                 taps_spec,
             ],
             out_specs=feature_spec,
@@ -216,7 +225,7 @@
             compiler_params=params(),
             cost_estimate=cost(6),
             name="conv_output",
-        )(hyena_q, local_result, rim, par, states, short_filter)
+        )(hyena_q, local_result, rim, par, entering, short_filter)
 
     return first_part, last_part
 
@@ -313,12 +322,13 @@
     return jnp.transpose(jnp.concatenate([part, fill], 0))
 
 
-def partial_kernel(transfers, upper, *refs):
+def partial_kernel(transfers, upper, onto, *refs):
     count = len(transfers)
+    out_ref = refs[-1]
     q_ref, k_ref, v_ref, kp_ref, vp_ref, g_ref, gp_ref = refs[:7]
     ask_refs = refs[7 : 7 + count]
-    own_ref, lse_ref = refs[7 + count : 9 + count]
-    answer_refs = refs[9 + count :]
+    own_ref, lse_ref = refs[7 + count + onto : 9 + count + onto]
+    answer_refs = refs[9 + count + onto : -1]
     me = lax.axis_index("ctx")
     rows = q_ref.shape[0]
     heads = q_ref.shape[1] // HEAD_DIM
@@ -346,6 +356,7 @@
             keys, values = key_value(head, with_quad)
             mixed, lse = soft(q_ref[:, block_lanes(head)], keys, values, mask)
             own_ref[:, block_lanes(head)] = mixed
+            out_ref[:, block_lanes(head)] = mixed.astype(out_ref.dtype)
             sums.append(lse)
         lse_ref[...] = as_rows(sums)
 
@@ -381,42 +392,60 @@
         run(False)
 
 
-def merge_kernel(transfers, me_ref, own_ref, lse_ref, *refs):
-    others = refs[: 2 * len(transfers)]
-    out_ref = refs[-1]
-    me = me_ref[0]
-    rows, width = out_ref.shape
-    heads = width // HEAD_DIM
+def merge_kernel(transfers, steps, start, own_hbm, lse_hbm, *refs):
+    count = 2 * len(transfers)
+    others_hbm, out_hbm = refs[:count], refs[count + 1]
+    own_ref, lse_ref, *other_refs = refs[count + 2 : 2 * count + 4]
+    out_ref, sems = refs[-2:]
+    me = lax.axis_index("ctx")
+    odd = me % 2
+    rows, width = own_ref.shape
+    heads = HEADS_PER_STEP
+    half_rows = heads * rows + TAIL
     returned = []
     for pairs in transfers:
         members = [source for source, _ in pairs]
         returned += [members, [member ^ 1 for member in members]]
-    answered = among(me, sorted(set(sum(returned, []))))
-
-    @pl.when(answered)
+
+    @pl.when(among(me, sorted(set(sum(returned, [])))))
     def _():
+        loads = [(own_hbm, own_ref), (lse_hbm, lse_ref)]
+        for hbm, ref in zip(others_hbm, other_refs):
+            for step in range(steps):
+                half = pl.ds(pl.multiple_of((2 * step + odd) * half_rows, TAIL), half_rows)
+                loads.append((hbm.at[half, :], ref.at[step]))
+        copies = [
+            pltpu.make_async_copy(source, target, sems.at[index])
+            for index, (source, target) in enumerate(loads)
+        ]
+        for copy in copies:
+            copy.start()
+        for copy in copies:
+            copy.wait()
         valid = [among(me, members) for members in returned]
-        logs = [lse_ref[...]]
-        for index, ref in enumerate(others):
-            tail = ref[heads * rows :, :].astype(jnp.float32)
-            tail = tail[:SUBLANES] + tail[SUBLANES : 2 * SUBLANES] + tail[2 * SUBLANES : 3 * SUBLANES]
-            logs.append(jnp.where(valid[index], tail, NEGATIVE))
-        top = functools.reduce(jnp.maximum, logs)
-        weights = [jnp.exp2(part - top) for part in logs]
-        total = functools.reduce(jnp.add, weights)
-        shares = [as_columns(weight / total) for weight in weights]
-        for head in range(heads):
-            cut = block_lanes(head)
-            mixed = [own_ref[:, cut]]
-            for index, ref in enumerate(others):
-                part = ref[head * rows : (head + 1) * rows, :].astype(jnp.float32)
-                mixed.append(jnp.where(valid[index], part, 0.0))
-            terms = [part * share[:, head : head + 1] for part, share in zip(mixed, shares)]
-            out_ref[:, cut] = functools.reduce(jnp.add, terms).astype(out_ref.dtype)
-
-    @pl.when(jnp.logical_not(answered))
-    def _():
-        out_ref[...] = own_ref[...].astype(out_ref.dtype)
+        for step in range(steps):
+            logs = [lse_ref[step * SUBLANES : (step + 1) * SUBLANES, :]]
+            for index, ref in enumerate(other_refs):
+                tail = ref[step, heads * rows :, :].astype(jnp.float32)
+                parts = [tail[part * SUBLANES : (part + 1) * SUBLANES] for part in range(3)]
+                logs.append(jnp.where(valid[index], parts[0] + parts[1] + parts[2], NEGATIVE))
+            top = functools.reduce(jnp.maximum, logs)
+            weights = [jnp.exp2(part - top) for part in logs]
+            total = functools.reduce(jnp.add, weights)
+            shares = [as_columns(weight / total) for weight in weights]
+            for head in range(heads):
+                cut = block_lanes(step * heads + head)
+                mixed = [own_ref[:, cut]]
+                for index, ref in enumerate(other_refs):
+                    part = ref[step, head * rows : (head + 1) * rows, :].astype(jnp.float32)
+                    mixed.append(jnp.where(valid[index], part, 0.0))
+                terms = [part * share[:, head : head + 1] for part, share in zip(mixed, shares)]
+                out_ref[:, cut] = functools.reduce(jnp.add, terms).astype(out_ref.dtype)
+        store = pltpu.make_async_copy(
+            out_ref, out_hbm.at[:, pl.ds(start, width)], sems.at[len(copies)]
+        )
+        store.start()
+        store.wait()
 
 
 def after(array, *others):
@@ -437,7 +466,6 @@
     gathers = [(who - 2, who) for who in upper]
     askers = sorted({source for pairs in transfers for source, _ in pairs})
     swap = [(index, index ^ 1) for index in range(devices)]
-    me = lax.axis_index("ctx").astype(jnp.int32).reshape(1)
 
     query_swapped = lax.ppermute(query, "ctx", swap)
     key_swapped = lax.ppermute(key, "ctx", swap)
@@ -471,32 +499,32 @@
         )(query, query_swapped, key, value)
         return list(zip(outs[: len(members)], outs[len(members) :]))
 
-    packs = pack([0])
-    conv_state, conv_output = conv
-    local_result, state, *conv_shared = conv_state(packs[0][1])
-    packs += pack(list(range(1, chunks))) if chunks > 1 else []
+    packs = pack(list(range(chunks)))
+    conv_first, conv_last = conv
+    local_result, *conv_shared = conv_first(packs[0][1])
     asks, quad_kv, all_answers = [], [], []
 
     def send(chunk):
         key_pack, query_pack = packs[chunk]
-        if chunk:
-            key_pack = after(key_pack, quad_kv[-1][0])
-            query_pack = after(query_pack, *asks[-1])
         if chunk > 1:
-            key_pack = after(key_pack, all_answers[chunk - 2][0])
-            query_pack = after(query_pack, all_answers[chunk - 2][0])
+            key_pack = after(key_pack, quad_kv[chunk - 2][0], all_answers[chunk - 2][0])
+            query_pack = after(query_pack, *asks[chunk - 2], all_answers[chunk - 2][0])
         arrived = lax.ppermute(key_pack, "ctx", gathers)
         asks.append([lax.ppermute(query_pack, "ctx", pairs) for pairs in transfers])
-        quad_kv.append([arrived, lax.ppermute(arrived, "ctx", swap)])
-
+        quad_kv.append([arrived])
+
+    half_rows = HEADS_PER_STEP * rows + TAIL
+    hbm = pl.BlockSpec(memory_space=pl.ANY)
     send(0)
-    half_rows = HEADS_PER_STEP * rows + TAIL
     result = None
+    returned = []
     for chunk in range(chunks):
         if chunk + 1 < chunks:
             send(chunk + 1)
         if chunk == 0:
-            asks[0] = [after(asked, state) for asked in asks[0]]
+            quad_kv[0] = [after(quad_kv[0][0], local_result)]
+            asks[0] = [after(asked, local_result) for asked in asks[0]]
+        quad_kv[chunk].append(lax.ppermute(quad_kv[chunk][0], "ctx", swap))
         steps, first = CHUNK_STEPS[chunk], first_steps[chunk]
         whole_spec = pl.BlockSpec((rows, step_width), lambda step, first=first: (0, first + step))
         chunk_spec = pl.BlockSpec((rows, step_width), lambda step: (0, step))
@@ -504,57 +532,59 @@
         lse_spec = pl.BlockSpec((SUBLANES, LANES), lambda step: (step, 0))
         answer_spec = pl.BlockSpec((2 * half_rows, LANES), lambda step: (step, 0))
         answer_shape = jax.ShapeDtypeStruct((2 * half_rows * steps, LANES), jnp.bfloat16)
-        own, lse, *answers = pl.pallas_call(
-            functools.partial(partial_kernel, transfers, upper),
+        operands = [query, key, value, key_swapped, value_swapped, *quad_kv[chunk], *asks[chunk]]
+        specs = [whole_spec] * 5 + [pair_spec] * (2 + len(transfers))
+        aliases = {}
+        if result is not None:
+            aliases = {len(operands): 2 + len(transfers)}
+            operands.append(result)
+            specs.append(hbm)
+        own, lse, *answers, result = pl.pallas_call(
+            functools.partial(partial_kernel, transfers, upper, len(aliases)),
             grid=(steps,),
-            in_specs=[whole_spec] * 5 + [pair_spec] * (2 + len(transfers)),
-            out_specs=[chunk_spec, lse_spec] + [answer_spec] * len(transfers),
+            in_specs=specs,
+            out_specs=[chunk_spec, lse_spec] + [answer_spec] * len(transfers) + [whole_spec],
             out_shape=[
                 jax.ShapeDtypeStruct((rows, widths[chunk]), jnp.float32),
                 jax.ShapeDtypeStruct((SUBLANES * steps, LANES), jnp.float32),
             ]
-            + [answer_shape] * len(transfers),
+            + [answer_shape] * len(transfers)
+            + [jax.ShapeDtypeStruct((rows, columns), jnp.bfloat16)],
+            input_output_aliases=aliases,
             compiler_params=params(),
             cost_estimate=cost(4),
             name="att_partial",
-        )(query, key, value, key_swapped, value_swapped, *quad_kv[chunk], *asks[chunk])
+        )(*operands)
         all_answers.append(answers)
-        operands = [me, own, lse]
+        parts = [own, lse]
         for answer, pairs in zip(answers, transfers):
             back = lax.ppermute(answer, "ctx", [(target, source) for source, target in pairs])
-            operands += [back, lax.ppermute(back, "ctx", swap)]
-
-        def shifted(step, me_ref, first=first):
-            return (0, first + step)
-
-        half_spec = pl.BlockSpec(
-            (half_rows, LANES), lambda step, me_ref: (2 * step + me_ref[0] % 2, 0)
-        )
-        specs = [
-            pl.BlockSpec((rows, step_width), lambda step, me_ref: (0, step)),
-            pl.BlockSpec((SUBLANES, LANES), lambda step, me_ref: (step, 0)),
-        ] + [half_spec] * (2 * len(transfers))
-        aliases = {}
-        if result is not None:
-            aliases = {len(operands): 0}
-            operands.append(result)
-            specs.append(pl.BlockSpec(memory_space=pl.ANY))
+            parts += [back, lax.ppermute(back, "ctx", swap)]
+        returned.append(parts)
+    conv_shared = [after(part, all_answers[-1][0]) for part in conv_shared]
+    for chunk, parts in enumerate(returned):
+        steps = CHUNK_STEPS[chunk]
+        count = 2 * len(transfers)
         result = pl.pallas_call(
-            functools.partial(merge_kernel, transfers),
-            grid_spec=pltpu.PrefetchScalarGridSpec(
-                num_scalar_prefetch=1,
-                grid=(steps,),
-                in_specs=specs,
-                out_specs=pl.BlockSpec((rows, step_width), shifted),
-            ),
+            functools.partial(merge_kernel, transfers, steps, starts[chunk]),
+            in_specs=[hbm] * (len(parts) + 1),
+            out_specs=hbm,
             out_shape=jax.ShapeDtypeStruct((rows, columns), jnp.bfloat16),
-            input_output_aliases=aliases,
+            input_output_aliases={len(parts): 0},
+            scratch_shapes=[
+                pltpu.VMEM((rows, widths[chunk]), jnp.float32),
+                pltpu.VMEM((SUBLANES * steps, LANES), jnp.float32),
+            ]
+            + [pltpu.VMEM((steps, half_rows, LANES), jnp.bfloat16)] * count
+            + [
+                pltpu.VMEM((rows, widths[chunk]), jnp.bfloat16),
+                pltpu.SemaphoreType.DMA((3 + count * steps,)),
+            ],
             compiler_params=params(),
             cost_estimate=cost(2),
             name="att_merge",
-        )(*operands)
-    shared = [after(part, all_answers[-1][0]) for part in conv_shared]
-    return conv_output(local_result, state, *shared), result
+        )(*parts, result)
+    return conv_last(local_result, *conv_shared), result
 
 
 def local(

time: 186 us -> 164 us (0.88)
  the two profiles are of different devices: /device:TPU:17 before, /device:TPU:25 now
where the time goes in v5:
time: 164 us
  starting transfers between devices  91.5 us (56%)
  Pallas kernels  44.2 us (27%)
  waiting for transfers between devices  20.3 us (12%)
  other arithmetic  6.65 us (4%)
    ppermute x4, starting transfers between devices, attend(): parts += [back, lax.ppermute(back, 'ctx', swap)]  32 us
    ppermute x4, starting transfers between devices, send(): asks.append([lax.ppermute(query_pack, 'ctx', pairs) for pairs in transfers])  30.6 us
    pallas_call x4, Pallas kernels, attend(): pl.pallas_call(functools.partial(partial_kernel, transfers, upper, len(al...  13.5 us
    pallas_call x4, Pallas kernels, attend(): pl.pallas_call(functools.partial(merge_kernel, transfers, steps, starts[c...  10.6 us
    pallas_call x1, Pallas kernels, first_part(): pl.pallas_call(functools.partial(state_kernel, modes), grid=(groups,), in...  9.62 us
    ppermute x4, waiting for transfers between devices, send(): asks.append([lax.ppermute(query_pack, 'ctx', pairs) for pairs in transfers])  8.82 us
    ppermute x4, waiting for transfers between devices, attend(): lax.ppermute(answer, 'ctx', [(target, source) for source, target in pairs])  8.16 us
    pallas_call x1, Pallas kernels, last_part(): pl.pallas_call(functools.partial(output_kernel, modes), grid=(groups,), i...  6.11 us
  transfers between devices with their start and end apart: 29, of which 8 were waited for; matrix products, arithmetic and copies ran while one was open for 4% of the time, Pallas kernels for 24%

profile of v5, /device:TPU:25, one launch (start us, length us, event | category | flops | bytes accessed | tf_op | source)
XLA Modules:
  0.0 163.6 jit_solution(14758477346240228701)
XLA Ops:
  0.6 0.7 collective-permute-start
  1.4 1.9 %conv_pack.1 = (f32[8,128,128]{2,1,0:T(8,128)}, f32[8,4096]{1,0:T(8,128)}) custom-call(f32[16,512]{1,0:T(8,128)} %bitcast.24, f32[16,512]{1,0:T(8,128)} %bitcast.25, bf16[128,4096]{1,0:T(8,128)(2,1)} %q_ref.5, bf16[128,4096]{1,0:T(8,128)(2,1)} %k_ref.5, bf16[128,4096]{1,0:T(8,128)(2,1)} %v_ref.5), custom_call_target="tpu_custom_call" | custom-call | flops 100000000 | bytes 65536 | tf_op jit(solution)/shard_map/conv_pack/pallas_call | solution.py:155
  3.3 0.7 collective-permute-done.qs_ref
  4.0 2.4 %att_pack.1 = (bf16[2,128,1024]{2,1,0:T(8,128)(2,1)}, bf16[2,128,1024]{2,1,0:T(8,128)(2,1)}, bf16[2,128,1024]{2,1,0:T(8,128)(2,1)}, bf16[2,128,1024]{2,1,0:T(8,1...) custom-call(bf16[128,4096]{1,0:T(8,128)(2,1)} %refs_0_.7, ...), custom_call_target="tpu_custom_call" | custom-call | flops 100000000 | bytes 65536 | tf_op jit(solution)/shard_map/att_pack/pallas_call | solution.py:479
  6.4 5.1 %all-to-all-start = ((f32[8,128,128]{2,1,0:T(8,128)}), f32[8,128,128]{2,1,0:T(8,128)}, u32[]{:S(2)}, u32[]{:S(2)}) async-start(f32[8,128,128]{2,1,0:T(8,128)} %get-tuple-element.45), calls=%async_computation | async-start | bytes 1048576 | tf_op jit(solution)/shard_map/all_to_all | solution.py:172
  11.6 1.5 collective-permute-start.7
  13.5 1.3 collective-permute-start.1
  14.8 1.5 collective-permute-start.4
  16.3 1.3 collective-permute-done.1.rim_ref
  17.6 5.5 %collective-permute-start.9 = (bf16[2,128,1024]{2,1,0:T(8,128)(2,1)}, bf16[2,128,1024]{2,1,0:T(8,128)(2,1)}, u32[]{:S(2)}, u32[]{:S(2)}) collective-permute-start(bf16[2,128,1024]{2,1,0:T(8,128)(2,1)} %get-tuple-element.42), channel_id=1, source_target_pairs={{7,5},{4,2},{6,3},{15,13},{12,10},{14,11},{23,21},{20,18},{22,19},... | collective-permute-start | bytes 1572872 | tf_op jit(solution)/shard_map/ppermute | solution.py:513
  23.1 1.3 all-to-all-done
  24.4 9.6 %conv_state.1 = (f32[128,4096]{1,0:T(8,128)}, f32[512,128]{1,0:T(8,128)}) custom-call(bf16[128,4096]{1,0:T(8,128)(2,1)} %k_ref.5, bf16[128,4096]{1,0:T(8,128)(2,1)} %v_ref.5, f32[8,4096]{1,0:T(8,128)} %copy-done.3, f32[1024,128]{1,0:T(8,128)} %bitcast.2.par_ref, f32[3,3,4096]{2,1,0:T(4,128)} %taps_ref.3), custom_call_target="tpu_custom_call" | custom-call | flops 900000000 | bytes 65536 | tf_op jit(solution)/shard_map/conv_state/pallas_call | solution.py:175
  34.0 3.9 %collective-permute-start.8 = (bf16[2,128,1024]{2,1,0:T(8,128)(2,1)}, bf16[2,128,1024]{2,1,0:T(8,128)(2,1)}, u32[]{:S(2)}, u32[]{:S(2)}) collective-permute-start(bf16[2,128,1024]{2,1,0:T(8,128)(2,1)} %collective-permute-done.7.refs_5_), channel_id=1, source_target_pairs={{0,1},{1,0},{2,3},{3,2},{4,5},{5,4},{6,7},{7,6},{8,9},{9,8},{10,11... | collective-permute-start | bytes 1572872 | tf_op jit(solution)/shard_map/ppermute | solution.py:527
  37.9 13.8 %collective-permute-start.6 = (bf16[2,128,1024]{2,1,0:T(8,128)(2,1)}, bf16[2,128,1024]{2,1,0:T(8,128)(2,1)}, u32[]{:S(2)}, u32[]{:S(2)}) collective-permute-start(bf16[2,128,1024]{2,1,0:T(8,128)(2,1)} %get-tuple-element.49), channel_id=1, source_target_pairs={{7,5},{4,2},{6,3},{15,13},{12,10},{14,11},{23,21},{20,18},{22,19},... | collective-permute-start | bytes 1572872 | tf_op jit(solution)/shard_map/ppermute | solution.py:513
  51.8 3.3 %att_partial.4 = (f32[128,1024]{1,0:T(8,128)}, f32[16,128]{1,0:T(8,128)}, bf16[2176,128]{1,0:T(8,128)(2,1)}, bf16[128,4096]{1,0:T(8,128)(2,1)}) custom-call(bf16[128,4096]{1,0:T(8,128)(2,1)} %refs_0_.7, bf16[128,4096]{1,0:T(8,128)(2,1)} %refs_1_.7, bf16[128,4096]{1,0:T(8,128)(2,1)} %refs_2_.7, bf16[128,4096]{1,0:T(8,128)(2,1)} %collective-permute-done.2.refs_3_, ...), custom_call_target="tpu_custom_call" | custom-call | flops 400000000 | bytes 65536 | tf_op jit(solution)/shard_map/att_partial/pallas_call | solution.py:542
  55.1 1.5 collective-permute-start.13
  56.6 0.5 collective-permute-start.16
  57.1 4.5 %collective-permute-done.6.refs_7_ = bf16[2,128,1024]{2,1,0:T(8,128)(2,1)} collective-permute-done((bf16[2,128,1024]{2,1,0:T(8,128)(2,1)}, bf16[2,128,1024]{2,1,0:T(8,128)(2,1)}, u32[]{:S(2)}, u32[]{:S(2)}) %collective-permute-start.6) | collective-permute-done | bytes 524320 | tf_op jit(solution)/shard_map/ppermute | solution.py:513
  61.6 3.4 %att_partial.5 = (f32[128,1024]{1,0:T(8,128)}, f32[16,128]{1,0:T(8,128)}, bf16[2176,128]{1,0:T(8,128)(2,1)}, bf16[128,4096]{1,0:T(8,128)(2,1)}) custom-call(bf16[128,4096]{1,0:T(8,128)(2,1)} %refs_0_.7, bf16[128,4096]{1,0:T(8,128)(2,1)} %refs_1_.7, bf16[128,4096]{1,0:T(8,128)(2,1)} %refs_2_.7, ...), custom_call_target="tpu_custom_call", output_to_operand_aliasing={{3}: (8, {})} | custom-call | flops 400000000 | bytes 65536 | tf_op jit(solution)/shard_map/att_partial/pallas_call | solution.py:542
  65.0 1.5 collective-permute-start.10
  66.5 1.8 %multiply_exponential_fusion.1 = (f32[32,16,128]{2,1,0:T(8,128)}, f32[32,16,128]{2,1,0:T(8,128)S(1)}, f32[32,16,128]{2,1,0:T(8,128)S(1)}) fusion(f32[32,32,128]{2,1,0:T(8,128)} %bitcast.3), kind=kLoop, calls=%fused_computation.11 | loop fusion | flops 196608 | bytes 1048576 | tf_op jit(solution)/shard_map/exp | solution.py:205
  68.3 6.0 %collective-permute-start.15 = (bf16[2,128,1024]{2,1,0:T(8,128)(2,1)}, bf16[2,128,1024]{2,1,0:T(8,128)(2,1)}, u32[]{:S(2)}, u32[]{:S(2)}) collective-permute-start(bf16[2,128,1024]{2,1,0:T(8,128)(2,1)} %get-tuple-element.62), channel_id=1, source_target_pairs={{7,5},{4,2},{6,3},{15,13},{12,10},{14,11},{23,21},{20,18},{22,19},... | collective-permute-start | bytes 1572872 | tf_op jit(solution)/shard_map/ppermute | solution.py:513
  74.6 1.1 fusion.2
  75.7 1.3 collective-permute-start.17
  77.0 5.3 %collective-permute-start.12 = (bf16[2,128,1024]{2,1,0:T(8,128)(2,1)}, bf16[2,128,1024]{2,1,0:T(8,128)(2,1)}, u32[]{:S(2)}, u32[]{:S(2)}) collective-permute-start(bf16[2,128,1024]{2,1,0:T(8,128)(2,1)} %get-tuple-element.57), channel_id=1, source_target_pairs={{7,5},{4,2},{6,3},{15,13},{12,10},{14,11},{23,21},{20,18},{22,19},... | collective-permute-start | bytes 1572872 | tf_op jit(solution)/shard_map/ppermute | solution.py:513
  82.3 1.6 collective-permute-start.11
  83.9 0.8 fusion
  84.7 1.3 collective-permute-start.18
  86.0 1.3 collective-permute-start.24
  87.3 1.3 collective-permute-start.26
  88.6 3.4 %att_partial.6 = (f32[128,1024]{1,0:T(8,128)}, f32[16,128]{1,0:T(8,128)}, bf16[2176,128]{1,0:T(8,128)(2,1)}, bf16[128,4096]{1,0:T(8,128)(2,1)}) custom-call(bf16[128,4096]{1,0:T(8,128)(2,1)} %refs_0_.7, bf16[128,4096]{1,0:T(8,128)(2,1)} %refs_1_.7, bf16[128,4096]{1,0:T(8,128)(2,1)} %refs_2_.7, ...), custom_call_target="tpu_custom_call", output_to_operand_aliasing={{3}: (8, {})} | custom-call | flops 400000000 | bytes 65536 | tf_op jit(solution)/shard_map/att_partial/pallas_call | solution.py:542
  92.0 4.3 %collective-permute-done.12.refs_7_ = bf16[2,128,1024]{2,1,0:T(8,128)(2,1)} collective-permute-done((bf16[2,128,1024]{2,1,0:T(8,128)(2,1)}, bf16[2,128,1024]{2,1,0:T(8,128)(2,1)}, u32[]{:S(2)}, u32[]{:S(2)}) %collective-permute-start.12) | collective-permute-done | bytes 524320 | tf_op jit(solution)/shard_map/ppermute | solution.py:513
  96.2 1.5 collective-permute-start.22
  97.7 3.4 %att_partial.7 = (f32[128,1024]{1,0:T(8,128)}, f32[16,128]{1,0:T(8,128)}, bf16[2176,128]{1,0:T(8,128)(2,1)}, bf16[128,4096]{1,0:T(8,128)(2,1)}) custom-call(bf16[128,4096]{1,0:T(8,128)(2,1)} %refs_0_.7, bf16[128,4096]{1,0:T(8,128)(2,1)} %refs_1_.7, bf16[128,4096]{1,0:T(8,128)(2,1)} %refs_2_.7, ...), custom_call_target="tpu_custom_call", output_to_operand_aliasing={{3}: (8, {})} | custom-call | flops 400000000 | bytes 65536 | tf_op jit(solution)/shard_map/att_partial/pallas_call | solution.py:542
  101.1 1.3 collective-permute-start.20
  102.4 1.2 fusion.1
  103.7 1.0 collective-permute-start.19
  104.6 7.4 %collective-permute-done.26.refs_0_ = bf16[2176,128]{1,0:T(8,128)(2,1)} collective-permute-done((bf16[2176,128]{1,0:T(8,128)(2,1)}, bf16[2176,128]{1,0:T(8,128)(2,1)}, u32[]{:S(2)}, u32[]{:S(2)}) %collective-permute-start.26) | collective-permute-done | bytes 557088 | tf_op jit(solution)/shard_map/ppermute | solution.py:561
  112.0 11.6 %collective-permute-start.27 = (bf16[2176,128]{1,0:T(8,128)(2,1)}, bf16[2176,128]{1,0:T(8,128)(2,1)}, u32[]{:S(2)}, u32[]{:S(2)}) collective-permute-start(bf16[2176,128]{1,0:T(8,128)(2,1)} %collective-permute-done.26.refs_0_), channel_id=1, source_target_pairs={{0,1},{1,0},{2,3},{3,2},{4,5},{5,4},{6,7},{7,6},{8,9},{9,8},{10,11... | collective-permute-start | bytes 1671176 | tf_op jit(solution)/shard_map/ppermute | solution.py:562
  123.9 11.6 %collective-permute-start.23 = (bf16[2176,128]{1,0:T(8,128)(2,1)}, bf16[2176,128]{1,0:T(8,128)(2,1)}, u32[]{:S(2)}, u32[]{:S(2)}) collective-permute-start(bf16[2176,128]{1,0:T(8,128)(2,1)} %collective-permute-done.22.refs_0_), channel_id=1, source_target_pairs={{0,1},{1,0},{2,3},{3,2},{4,5},{5,4},{6,7},{7,6},{8,9},{9,8},{10,11... | collective-permute-start | bytes 1671176 | tf_op jit(solution)/shard_map/ppermute | solution.py:562
  135.5 0.4 collective-permute-done.20.refs_0_
  135.9 8.9 %collective-permute-start.21 = (bf16[2176,128]{1,0:T(8,128)(2,1)}, bf16[2176,128]{1,0:T(8,128)(2,1)}, u32[]{:S(2)}, u32[]{:S(2)}) collective-permute-start(bf16[2176,128]{1,0:T(8,128)(2,1)} %collective-permute-done.20.refs_0_), channel_id=1, source_target_pairs={{0,1},{1,0},{2,3},{3,2},{4,5},{5,4},{6,7},{7,6},{8,9},{9,8},{10,11... | collective-permute-start | bytes 1671176 | tf_op jit(solution)/shard_map/ppermute | solution.py:562
  144.8 1.8 %fusion.4.enter_ref = f32[512,128]{1,0:T(8,128)} fusion(f32[512,128]{1,0:T(8,128)S(1)} %collective-permute-done.19, f32[512,128]{1,0:T(8,128)} %collective-permute-done.16, f32[512,128]{1,0:T(8,128)S(1)} %fusion.1, f32[32,16,128]{2,1,0:T(8,128)} %copy-done, pred[]{:T(512)S(6)} %eq.5), kind=kLoop, calls=%fused_computation.9 | loop fusion | flops 196608 | bytes 1310721 | tf_op jit(solution)/shard_map/jit(_where)/select_n | solution.py:209
  146.6 6.1 %conv_output.1 = bf16[128,4096]{1,0:T(8,128)(2,1)} custom-call(bf16[128,4096]{1,0:T(8,128)(2,1)} %q_ref.5, f32[128,4096]{1,0:T(8,128)} %get-tuple-element.46.y_ref, f32[8,4096]{1,0:T(8,128)} %copy-done.3, f32[1024,128]{1,0:T(8,128)} %bitcast.2.par_ref, f32[512,128]{1,0:T(8,128)} %fusion.4.enter_ref, f32[3,3,4096]{2,1,0:T(4,128)} %taps_ref.3), custom_call_target="tpu_custom_call" | custom-call | flops 600000000 | bytes 65536 | tf_op jit(solution)/shard_map/conv_output/pallas_call | solution.py:212
  152.7 2.7 %att_merge.4.refs_2_ = bf16[128,4096]{1,0:T(8,128)(2,1)} custom-call(f32[128,1024]{1,0:T(8,128)} %get-tuple-element.77.own_hbm, f32[16,128]{1,0:T(8,128)} %get-tuple-element.78.lse_hbm, bf16[2176,128]{1,0:T(8,128)(2,1)} %collective-permute-done.26.refs_0_, bf16[2176,128]{1,0:T(8,128)(2,1)} %collective-permute-done.27.refs_1_, ...), custom_call_target="tpu_custom_call", output_to_operand_aliasing={{}: (4, {})} | custom-call | flops 200000000 | bytes 65536 | tf_op jit(solution)/shard_map/att_merge/pallas_call | solution.py:568
  155.4 2.7 %att_merge.5.refs_2_ = bf16[128,4096]{1,0:T(8,128)(2,1)} custom-call(f32[128,1024]{1,0:T(8,128)} %get-tuple-element.75.own_hbm, f32[16,128]{1,0:T(8,128)} %get-tuple-element.76.lse_hbm, bf16[2176,128]{1,0:T(8,128)(2,1)} %collective-permute-done.24.refs_0_, bf16[2176,128]{1,0:T(8,128)(2,1)} %collective-permute-done.25.refs_1_, ...), custom_call_target="tpu_custom_call", output_to_operand_aliasing={{}: (4, {})} | custom-call | flops 200000000 | bytes 65536 | tf_op jit(solution)/shard_map/att_merge/pallas_call | solution.py:568
  158.1 2.7 %att_merge.6.refs_2_ = bf16[128,4096]{1,0:T(8,128)(2,1)} custom-call(f32[128,1024]{1,0:T(8,128)} %get-tuple-element.72.own_hbm, f32[16,128]{1,0:T(8,128)} %get-tuple-element.73.lse_hbm, bf16[2176,128]{1,0:T(8,128)(2,1)} %collective-permute-done.22.refs_0_, bf16[2176,128]{1,0:T(8,128)(2,1)} %collective-permute-done.23.refs_1_, ...), custom_call_target="tpu_custom_call", output_to_operand_aliasing={{}: (4, {})} | custom-call | flops 200000000 | bytes 65536 | tf_op jit(solution)/shard_map/att_merge/pallas_call | solution.py:568
  160.7 2.7 %att_merge.7 = bf16[128,4096]{1,0:T(8,128)(2,1)} custom-call(f32[128,1024]{1,0:T(8,128)} %get-tuple-element.70.own_hbm, f32[16,128]{1,0:T(8,128)} %get-tuple-element.71.lse_hbm, bf16[2176,128]{1,0:T(8,128)(2,1)} %collective-permute-done.20.refs_0_, bf16[2176,128]{1,0:T(8,128)(2,1)} %collective-permute-done.21.refs_1_, ...), custom_call_target="tpu_custom_call", output_to_operand_aliasing={{}: (4, {})} | custom-call | flops 200000000 | bytes 65536 | tf_op jit(solution)/shard_map/att_merge/pallas_call | solution.py:568
  (35 shorter events, 1.3 us)
Async XLA Ops:
  0.6 3.4 %collective-permute-start = (bf16[128,4096]{1,0:T(8,128)(2,1)}, bf16[128,4096]{1,0:T(8,128)(2,1)}, u32[]{:S(2)}, u32[]{:S(2)}) collective-permute-start(bf16[128,4096]{1,0:T(8,128)(2,1)} %refs_0_.7), channel_id=1, source_target_pairs={{0,1},{1,0},{2,3},{3,2},{4,5},{5,4},{6,7},{7,6},{8,9},{9,8},{10,11... | collective-permute-start | bytes 3145736 | tf_op jit(solution)/shard_map/ppermute | solution.py:470
  6.4 18.0 %all-to-all-start = ((f32[8,128,128]{2,1,0:T(8,128)}), f32[8,128,128]{2,1,0:T(8,128)}, u32[]{:S(2)}, u32[]{:S(2)}) async-start(f32[8,128,128]{2,1,0:T(8,128)} %get-tuple-element.45), calls=%async_computation | async-start | bytes 1048576 | tf_op jit(solution)/shard_map/all_to_all | solution.py:172
  11.6 22.4 %collective-permute-start.7 = (bf16[2,128,1024]{2,1,0:T(8,128)(2,1)}, bf16[2,128,1024]{2,1,0:T(8,128)(2,1)}, u32[]{:S(2)}, u32[]{:S(2)}) collective-permute-start(bf16[2,128,1024]{2,1,0:T(8,128)(2,1)} %get-tuple-element.50), channel_id=1, source_target_pairs={{0,2},{1,3},{8,10},{9,11},{16,18},{17,19},{24,26},{25,27}} | collective-permute-start | bytes 1572872 | tf_op jit(solution)/shard_map/ppermute | solution.py:512
  13.0 38.7 %collective-permute-start.2 = (bf16[128,4096]{1,0:T(8,128)(2,1)}, bf16[128,4096]{1,0:T(8,128)(2,1)}, u32[]{:S(2)}, u32[]{:S(2)}) collective-permute-start(bf16[128,4096]{1,0:T(8,128)(2,1)} %refs_1_.7), channel_id=1, source_target_pairs={{0,1},{1,0},{2,3},{3,2},{4,5},{5,4},{6,7},{7,6},{8,9},{9,8},{10,11... | collective-permute-start | bytes 3145736 | tf_op jit(solution)/shard_map/ppermute | solution.py:471
  13.4 38.4 %collective-permute-start.3 = (bf16[128,4096]{1,0:T(8,128)(2,1)}, bf16[128,4096]{1,0:T(8,128)(2,1)}, u32[]{:S(2)}, u32[]{:S(2)}) collective-permute-start(bf16[128,4096]{1,0:T(8,128)(2,1)} %refs_2_.7), channel_id=1, source_target_pairs={{0,1},{1,0},{2,3},{3,2},{4,5},{5,4},{6,7},{7,6},{8,9},{9,8},{10,11... | collective-permute-start | bytes 3145736 | tf_op jit(solution)/shard_map/ppermute | solution.py:472
  13.5 4.0 %collective-permute-start.1 = (f32[8,4096]{1,0:T(8,128)}, f32[8,4096]{1,0:T(8,128)S(1)}, u32[]{:S(2)}, u32[]{:S(2)}) collective-permute-start(f32[8,4096]{1,0:T(8,128)} %get-tuple-element.43), channel_id=1, source_target_pairs={{0,1},{1,2},{2,3},{3,4},{4,5},{5,6},{6,7},{8,9},{9,10},{10,11},{11... | collective-permute-start | bytes 393224 | tf_op jit(solution)/shard_map/ppermute | solution.py:174
  14.8 23.1 %collective-permute-start.4 = (bf16[2,128,1024]{2,1,0:T(8,128)(2,1)}, bf16[2,128,1024]{2,1,0:T(8,128)(2,1)}, u32[]{:S(2)}, u32[]{:S(2)}) collective-permute-start(bf16[2,128,1024]{2,1,0:T(8,128)(2,1)} %get-tuple-element.48), channel_id=1, source_target_pairs={{0,2},{1,3},{8,10},{9,11},{16,18},{17,19},{24,26},{25,27}} | collective-permute-start | bytes 1572872 | tf_op jit(solution)/shard_map/ppermute | solution.py:512
  17.6 6.8 %copy-start.3 = (f32[8,4096]{1,0:T(8,128)}, f32[8,4096]{1,0:T(8,128)S(1)}, u32[]{:S(2)}) copy-start(f32[8,4096]{1,0:T(8,128)S(1)} %collective-permute-done.1.rim_ref) | copy-start | bytes 393220
  17.6 34.2 %collective-permute-start.9 = (bf16[2,128,1024]{2,1,0:T(8,128)(2,1)}, bf16[2,128,1024]{2,1,0:T(8,128)(2,1)}, u32[]{:S(2)}, u32[]{:S(2)}) collective-permute-start(bf16[2,128,1024]{2,1,0:T(8,128)(2,1)} %get-tuple-element.42), channel_id=1, source_target_pairs={{7,5},{4,2},{6,3},{15,13},{12,10},{14,11},{23,21},{20,18},{22,19},... | collective-permute-start | bytes 1572872 | tf_op jit(solution)/shard_map/ppermute | solution.py:513
  34.0 17.8 %collective-permute-start.8 = (bf16[2,128,1024]{2,1,0:T(8,128)(2,1)}, bf16[2,128,1024]{2,1,0:T(8,128)(2,1)}, u32[]{:S(2)}, u32[]{:S(2)}) collective-permute-start(bf16[2,128,1024]{2,1,0:T(8,128)(2,1)} %collective-permute-done.7.refs_5_), channel_id=1, source_target_pairs={{0,1},{1,0},{2,3},{3,2},{4,5},{5,4},{6,7},{7,6},{8,9},{9,8},{10,11... | collective-permute-start | bytes 1572872 | tf_op jit(solution)/shard_map/ppermute | solution.py:527
  37.9 23.7 %collective-permute-start.6 = (bf16[2,128,1024]{2,1,0:T(8,128)(2,1)}, bf16[2,128,1024]{2,1,0:T(8,128)(2,1)}, u32[]{:S(2)}, u32[]{:S(2)}) collective-permute-start(bf16[2,128,1024]{2,1,0:T(8,128)(2,1)} %get-tuple-element.49), channel_id=1, source_target_pairs={{7,5},{4,2},{6,3},{15,13},{12,10},{14,11},{23,21},{20,18},{22,19},... | collective-permute-start | bytes 1572872 | tf_op jit(solution)/shard_map/ppermute | solution.py:513
  51.7 9.9 %collective-permute-start.5 = (bf16[2,128,1024]{2,1,0:T(8,128)(2,1)}, bf16[2,128,1024]{2,1,0:T(8,128)(2,1)}, u32[]{:S(2)}, u32[]{:S(2)}) collective-permute-start(bf16[2,128,1024]{2,1,0:T(8,128)(2,1)} %collective-permute-done.4.refs_5_), channel_id=1, source_target_pairs={{0,1},{1,0},{2,3},{3,2},{4,5},{5,4},{6,7},{7,6},{8,9},{9,8},{10,11... | collective-permute-start | bytes 1572872 | tf_op jit(solution)/shard_map/ppermute | solution.py:527
  55.1 19.1 %collective-permute-start.13 = (bf16[2,128,1024]{2,1,0:T(8,128)(2,1)}, bf16[2,128,1024]{2,1,0:T(8,128)(2,1)}, u32[]{:S(2)}, u32[]{:S(2)}) collective-permute-start(bf16[2,128,1024]{2,1,0:T(8,128)(2,1)} %get-tuple-element.60), channel_id=1, source_target_pairs={{0,2},{1,3},{8,10},{9,11},{16,18},{17,19},{24,26},{25,27}} | collective-permute-start | bytes 1572872 | tf_op jit(solution)/shard_map/ppermute | solution.py:512
  56.6 18.1 %collective-permute-start.16 = (f32[512,128]{1,0:T(8,128)}, f32[512,128]{1,0:T(8,128)}, u32[]{:S(2)}, u32[]{:S(2)}) collective-permute-start(f32[512,128]{1,0:T(8,128)} %get-tuple-element.68), channel_id=1, source_target_pairs={{0,1},{1,0},{2,3},{3,2},{4,5},{5,4},{6,7},{7,6},{8,9},{9,8},{10,11... | collective-permute-start | bytes 786440 | tf_op jit(solution)/shard_map/ppermute | solution.py:198
  65.0 17.3 %collective-permute-start.10 = (bf16[2,128,1024]{2,1,0:T(8,128)(2,1)}, bf16[2,128,1024]{2,1,0:T(8,128)(2,1)}, u32[]{:S(2)}, u32[]{:S(2)}) collective-permute-start(bf16[2,128,1024]{2,1,0:T(8,128)(2,1)} %get-tuple-element.55), channel_id=1, source_target_pairs={{0,2},{1,3},{8,10},{9,11},{16,18},{17,19},{24,26},{25,27}} | collective-permute-start | bytes 1572872 | tf_op jit(solution)/shard_map/ppermute | solution.py:512
  68.3 6.4 %copy-start = (f32[32,16,128]{2,1,0:T(8,128)}, f32[32,16,128]{2,1,0:T(8,128)S(1)}, u32[]{:S(2)}) copy-start(f32[32,16,128]{2,1,0:T(8,128)S(1)} %get-tuple-element.82) | copy-start | bytes 786436
  68.3 15.6 %copy-start.1 = (f32[32,16,128]{2,1,0:T(8,128)}, f32[32,16,128]{2,1,0:T(8,128)S(1)}, u32[]{:S(2)}) copy-start(f32[32,16,128]{2,1,0:T(8,128)S(1)} %get-tuple-element.81) | copy-start | bytes 786436
  68.3 17.7 %collective-permute-start.15 = (bf16[2,128,1024]{2,1,0:T(8,128)(2,1)}, bf16[2,128,1024]{2,1,0:T(8,128)(2,1)}, u32[]{:S(2)}, u32[]{:S(2)}) collective-permute-start(bf16[2,128,1024]{2,1,0:T(8,128)(2,1)} %get-tuple-element.62), channel_id=1, source_target_pairs={{7,5},{4,2},{6,3},{15,13},{12,10},{14,11},{23,21},{20,18},{22,19},... | collective-permute-start | bytes 1572872 | tf_op jit(solution)/shard_map/ppermute | solution.py:513
  74.3 13.0 %collective-permute-start.14 = (bf16[2,128,1024]{2,1,0:T(8,128)(2,1)}, bf16[2,128,1024]{2,1,0:T(8,128)(2,1)}, u32[]{:S(2)}, u32[]{:S(2)}) collective-permute-start(bf16[2,128,1024]{2,1,0:T(8,128)(2,1)} %collective-permute-done.13.refs_5_), channel_id=1, source_target_pairs={{0,1},{1,0},{2,3},{3,2},{4,5},{5,4},{6,7},{7,6},{8,9},{9,8},{10,11... | collective-permute-start | bytes 1572872 | tf_op jit(solution)/shard_map/ppermute | solution.py:527
  75.7 8.2 %collective-permute-start.17 = (f32[512,128]{1,0:T(8,128)S(1)}, f32[512,128]{1,0:T(8,128)S(1)}, u32[]{:S(2)}, u32[]{:S(2)}) collective-permute-start(f32[512,128]{1,0:T(8,128)S(1)} %fusion.2), channel_id=1, source_target_pairs={{1,3},{3,5},{5,7},{9,11},{11,13},{13,15},{17,19},{19,21},{21,23},{... | collective-permute-start | bytes 786440 | tf_op jit(solution)/shard_map/ppermute | solution.py:204
  77.0 19.2 %collective-permute-start.12 = (bf16[2,128,1024]{2,1,0:T(8,128)(2,1)}, bf16[2,128,1024]{2,1,0:T(8,128)(2,1)}, u32[]{:S(2)}, u32[]{:S(2)}) collective-permute-start(bf16[2,128,1024]{2,1,0:T(8,128)(2,1)} %get-tuple-element.57), channel_id=1, source_target_pairs={{7,5},{4,2},{6,3},{15,13},{12,10},{14,11},{23,21},{20,18},{22,19},... | collective-permute-start | bytes 1572872 | tf_op jit(solution)/shard_map/ppermute | solution.py:513
  82.3 15.4 %collective-permute-start.11 = (bf16[2,128,1024]{2,1,0:T(8,128)(2,1)}, bf16[2,128,1024]{2,1,0:T(8,128)(2,1)}, u32[]{:S(2)}, u32[]{:S(2)}) collective-permute-start(bf16[2,128,1024]{2,1,0:T(8,128)(2,1)} %collective-permute-done.10.refs_5_), channel_id=1, source_target_pairs={{0,1},{1,0},{2,3},{3,2},{4,5},{5,4},{6,7},{7,6},{8,9},{9,8},{10,11... | collective-permute-start | bytes 1572872 | tf_op jit(solution)/shard_map/ppermute | solution.py:527
  83.9 0.8 copy-start.2
  84.7 17.7 %collective-permute-start.18 = (f32[512,128]{1,0:T(8,128)}, f32[512,128]{1,0:T(8,128)}, u32[]{:S(2)}, u32[]{:S(2)}) collective-permute-start(f32[512,128]{1,0:T(8,128)} %fusion), channel_id=1, source_target_pairs={{1,5},{3,7},{9,13},{11,15},{17,21},{19,23},{25,29},{27,31}} | collective-permute-start | bytes 786440 | tf_op jit(solution)/shard_map/ppermute | solution.py:204
  86.0 37.6 %collective-permute-start.24 = (bf16[2176,128]{1,0:T(8,128)(2,1)}, bf16[2176,128]{1,0:T(8,128)(2,1)}, u32[]{:S(2)}, u32[]{:S(2)}) collective-permute-start(bf16[2176,128]{1,0:T(8,128)(2,1)} %get-tuple-element.54), channel_id=1, source_target_pairs={{5,7},{2,4},{3,6},{13,15},{10,12},{11,14},{21,23},{18,20},{19,22},... | collective-permute-start | bytes 1671176 | tf_op jit(solution)/shard_map/ppermute | solution.py:561
  87.3 24.7 %collective-permute-start.26 = (bf16[2176,128]{1,0:T(8,128)(2,1)}, bf16[2176,128]{1,0:T(8,128)(2,1)}, u32[]{:S(2)}, u32[]{:S(2)}) collective-permute-start(bf16[2176,128]{1,0:T(8,128)(2,1)} %get-tuple-element.59), channel_id=1, source_target_pairs={{5,7},{2,4},{3,6},{13,15},{10,12},{11,14},{21,23},{18,20},{19,22},... | collective-permute-start | bytes 1671176 | tf_op jit(solution)/shard_map/ppermute | solution.py:561
  96.2 27.7 %collective-permute-start.22 = (bf16[2176,128]{1,0:T(8,128)(2,1)}, bf16[2176,128]{1,0:T(8,128)(2,1)}, u32[]{:S(2)}, u32[]{:S(2)}) collective-permute-start(bf16[2176,128]{1,0:T(8,128)(2,1)} %get-tuple-element.74), channel_id=1, source_target_pairs={{5,7},{2,4},{3,6},{13,15},{10,12},{11,14},{21,23},{18,20},{19,22},... | collective-permute-start | bytes 1671176 | tf_op jit(solution)/shard_map/ppermute | solution.py:561
  101.1 34.8 %collective-permute-start.20 = (bf16[2176,128]{1,0:T(8,128)(2,1)}, bf16[2176,128]{1,0:T(8,128)(2,1)}, u32[]{:S(2)}, u32[]{:S(2)}) collective-permute-start(bf16[2176,128]{1,0:T(8,128)(2,1)} %get-tuple-element.65), channel_id=1, source_target_pairs={{5,7},{2,4},{3,6},{13,15},{10,12},{11,14},{21,23},{18,20},{19,22},... | collective-permute-start | bytes 1671176 | tf_op jit(solution)/shard_map/ppermute | solution.py:561
  103.7 41.2 %collective-permute-start.19 = (f32[512,128]{1,0:T(8,128)S(1)}, f32[512,128]{1,0:T(8,128)S(1)}, u32[]{:S(2)}, u32[]{:S(2)}) collective-permute-start(f32[512,128]{1,0:T(8,128)S(1)} %fusion.1), channel_id=1, source_target_pairs={{0,1},{1,0},{2,3},{3,2},{4,5},{5,4},{6,7},{7,6},{8,9},{9,8},{10,11... | collective-permute-start | bytes 786440 | tf_op jit(solution)/shard_map/ppermute | solution.py:208
  112.0 40.7 %collective-permute-start.27 = (bf16[2176,128]{1,0:T(8,128)(2,1)}, bf16[2176,128]{1,0:T(8,128)(2,1)}, u32[]{:S(2)}, u32[]{:S(2)}) collective-permute-start(bf16[2176,128]{1,0:T(8,128)(2,1)} %collective-permute-done.26.refs_0_), channel_id=1, source_target_pairs={{0,1},{1,0},{2,3},{3,2},{4,5},{5,4},{6,7},{7,6},{8,9},{9,8},{10,11... | collective-permute-start | bytes 1671176 | tf_op jit(solution)/shard_map/ppermute | solution.py:562
  123.6 31.8 %collective-permute-start.25 = (bf16[2176,128]{1,0:T(8,128)(2,1)}, bf16[2176,128]{1,0:T(8,128)(2,1)}, u32[]{:S(2)}, u32[]{:S(2)}) collective-permute-start(bf16[2176,128]{1,0:T(8,128)(2,1)} %collective-permute-done.24.refs_0_), channel_id=1, source_target_pairs={{0,1},{1,0},{2,3},{3,2},{4,5},{5,4},{6,7},{7,6},{8,9},{9,8},{10,11... | collective-permute-start | bytes 1671176 | tf_op jit(solution)/shard_map/ppermute | solution.py:562
  123.9 34.1 %collective-permute-start.23 = (bf16[2176,128]{1,0:T(8,128)(2,1)}, bf16[2176,128]{1,0:T(8,128)(2,1)}, u32[]{:S(2)}, u32[]{:S(2)}) collective-permute-start(bf16[2176,128]{1,0:T(8,128)(2,1)} %collective-permute-done.22.refs_0_), channel_id=1, source_target_pairs={{0,1},{1,0},{2,3},{3,2},{4,5},{5,4},{6,7},{7,6},{8,9},{9,8},{10,11... | collective-permute-start | bytes 1671176 | tf_op jit(solution)/shard_map/ppermute | solution.py:562
  135.9 24.8 %collective-permute-start.21 = (bf16[2176,128]{1,0:T(8,128)(2,1)}, bf16[2176,128]{1,0:T(8,128)(2,1)}, u32[]{:S(2)}, u32[]{:S(2)}) collective-permute-start(bf16[2176,128]{1,0:T(8,128)(2,1)} %collective-permute-done.20.refs_0_), channel_id=1, source_target_pairs={{0,1},{1,0},{2,3},{3,2},{4,5},{5,4},{6,7},{7,6},{8,9},{9,8},{10,11... | collective-permute-start | bytes 1671176 | tf_op jit(solution)/shard_map/ppermute | solution.py:562

commit v6 on v5

--- a/solution.py
+++ b/solution.py
@@ -15,6 +15,7 @@
 TAPS = 3
 HEADS_PER_STEP = 4
 CHUNK_STEPS = (2, 2, 2, 2)
+LAG = 2
 NEGATIVE = -1e30
 EXP_SCALE = HEAD_DIM**-0.5 * math.log2(math.e)
 VMEM_LIMIT = 255 * 1024 * 256
@@ -63,7 +64,9 @@
     return [taps_ref[feature, pl.ds(tap, 1), lanes] for tap in range(TAPS)]
 
 
-def state_kernel(modes, k_ref, v_ref, rim_ref, par_ref, taps_ref, y_ref, s_ref, p_scr, y_scr):
+def state_kernel(
+    modes, k_ref, v_ref, rim_ref, par_ref, taps_ref, y_ref, s_ref, d_ref, p_scr, y_scr
+):
     rows = k_ref.shape[0]
     for block in range(SUBLANES):
         lanes = block_lanes(block)
@@ -95,10 +98,26 @@
     for mode in range(modes):
         s_ref[pl.ds(mode, SUBLANES, modes), :] = states[mode]
     for block in range(SUBLANES):
+        rate = par_ref[2 * block * modes : (2 * block + 1) * modes, :]
+        d_ref[block * modes : (block + 1) * modes, :] = jnp.exp(-rate * rows)
+    for block in range(SUBLANES):
         y_ref[:, block_lanes(block)] = y_scr[pl.ds(block, rows, SUBLANES), :]
 
 
-def output_kernel(modes, q_ref, y_ref, rim_ref, par_ref, enter_ref, taps_ref, out_ref):
+def output_kernel(
+    modes,
+    q_ref,
+    y_ref,
+    rim_ref,
+    par_ref,
+    decay_ref,
+    enter_ref,
+    enter_first_ref,
+    other_ref,
+    taps_ref,
+    out_ref,
+):
+    second = lax.axis_index("ctx") % 2 == 1
     rows = q_ref.shape[0]
     step = lax.broadcasted_iota(jnp.int32, (SUBLANES, LANES), 0).astype(jnp.float32) + 1.0
 
@@ -106,7 +125,9 @@
         lanes = pl.ds(pl.multiple_of(block * LANES, LANES), LANES)
         rate = par_ref[pl.ds(pl.multiple_of(2 * block * modes, SUBLANES), modes), :]
         residue = par_ref[pl.ds(pl.multiple_of((2 * block + 1) * modes, SUBLANES), modes), :]
-        entering = enter_ref[pl.ds(pl.multiple_of(block * modes, SUBLANES), modes), :]
+        here = pl.ds(pl.multiple_of(block * modes, SUBLANES), modes)
+        after_first = decay_ref[here, :] * enter_ref[here, :] + other_ref[here, :]
+        entering = jnp.where(second, after_first, enter_first_ref[here, :])
         weighted = residue * entering
         eight = jnp.exp(-rate * SUBLANES)
         terms = [
@@ -169,19 +190,19 @@
             cost_estimate=cost(1),
             name="conv_pack",
         )(decay_rate.T, residue.T, hyena_q, hyena_k, hyena_v)
-        par = lax.all_to_all(after(own_par, token), "ctx", split_axis=0, concat_axis=0, tiled=True)
+        rim = lax.ppermute(rim, "ctx", [(index, index + 1) for index in range(devices - 1)])
+        own_par = after(own_par, rim, token)
+        par = lax.all_to_all(own_par, "ctx", split_axis=0, concat_axis=0, tiled=True)
         par = par.reshape(devices * par_rows, LANES)
-        rim = lax.ppermute(after(rim, token), "ctx", [(index, index + 1) for index in range(devices - 1)])
-        local_result, state = pl.pallas_call(
+        state_spec = pl.BlockSpec((SUBLANES * modes, LANES), lambda group: (group, 0))
+        local_result, state, decay = pl.pallas_call(
             functools.partial(state_kernel, modes),
             grid=(groups,),
             in_specs=[feature_spec, feature_spec, rim_spec, par_spec, taps_spec],
-            out_specs=[
-                feature_spec,
-                pl.BlockSpec((SUBLANES * modes, LANES), lambda group: (group, 0)),
-            ],
+            out_specs=[feature_spec, state_spec, state_spec],
             out_shape=[
                 jax.ShapeDtypeStruct((rows, channels), jnp.float32),
+                jax.ShapeDtypeStruct((blocks * modes, LANES), jnp.float32),
                 jax.ShapeDtypeStruct((blocks * modes, LANES), jnp.float32),
             ],
             scratch_shapes=[positions, positions],
@@ -189,43 +210,50 @@
             cost_estimate=cost(9),
             name="conv_state",
         )(hyena_k, hyena_v, rim, par, short_filter)
-        return local_result, entering_state(state, par), rim, par
-
-    def entering_state(state, par):
-        me = lax.axis_index("ctx")
+        return local_result, rim, par, decay, *entering_state(state, decay)
+
+    def entering_state(state, decay):
         swap = [(index, index ^ 1) for index in range(devices)]
-        rate = par.reshape(blocks, 2 * modes, LANES)[:, :modes].reshape(blocks * modes, LANES)
         other = lax.ppermute(state, "ctx", swap)
-        total = state + jnp.exp(-rows * rate) * other
-        entering = jnp.zeros_like(state)
+        total = state + decay * other
+        entering = None
         reach = 1
         while 2 * reach < devices:
             moves = [(index, index + 2 * reach) for index in range(1, devices - 2 * reach, 2)]
             arrived = lax.ppermute(total, "ctx", moves)
-            entering = entering + jnp.exp(-2.0 * rows * (reach - 1) * rate) * arrived
-            total = total + jnp.exp(-2.0 * rows * reach * rate) * arrived
+            if reach == 1:
+                entering = arrived
+            else:
+                entering = entering + decay ** (2 * (reach - 1)) * arrived
+            if 4 * reach < devices:
+                total = total + decay ** (2 * reach) * arrived
             reach *= 2
-        from_second = lax.ppermute(entering, "ctx", swap)
-        return jnp.where(me % 2 == 1, jnp.exp(-rows * rate) * entering + other, from_second)
-
-    def last_part(local_result, entering, rim, par):
+        return entering, lax.ppermute(entering, "ctx", swap), other
+
+    def last_part(local_result, rim, par, decay, entering, entering_first, other):
+        state_spec = pl.BlockSpec((SUBLANES * modes, LANES), lambda group: (group, 0))
         return pl.pallas_call(
             functools.partial(output_kernel, modes),
             grid=(groups,),
-            in_specs=[
-                feature_spec,
-                feature_spec,
-                rim_spec,
-                par_spec,
-                pl.BlockSpec((SUBLANES * modes, LANES), lambda group: (group, 0)),
-                taps_spec,
-            ],
+            in_specs=[feature_spec, feature_spec, rim_spec, par_spec]
+            + [state_spec] * 4
+            + [taps_spec],
             out_specs=feature_spec,
             out_shape=jax.ShapeDtypeStruct((rows, channels), jnp.bfloat16),
             compiler_params=params(),
             cost_estimate=cost(6),
             name="conv_output",
-        )(hyena_q, local_result, rim, par, entering, short_filter)
+        )(
+            hyena_q,
+            local_result,
+            rim,
+            par,
+            decay,
+            entering,
+            entering_first,
+            other,
+            short_filter,
+        )
 
     return first_part, last_part
 
@@ -259,10 +287,10 @@
     return mixed[:, :HEAD_DIM] / total, top + jnp.log2(total)
 
 
-def pack_kernel(gathers, askers, widths, starts, q_ref, qs_ref, k_ref, v_ref, *rest):
+def pack_kernel(gathers, askers, asked, widths, starts, q_ref, qs_ref, k_ref, v_ref, *rest):
     count = len(widths)
-    key_outs, query_outs = rest[:count], rest[count : 2 * count]
-    stages, in_sems, out_sems = rest[2 * count : 4 * count], rest[-2], rest[-1]
+    key_outs, query_outs = rest[:count], rest[count : count + asked]
+    stages, in_sems, out_sems = rest[count + asked : -2], rest[-2], rest[-1]
     me = lax.axis_index("ctx")
     odd = me % 2
 
@@ -303,7 +331,7 @@
         run(
             [
                 (cut(ref, chunk), query_outs[chunk].at[half])
-                for chunk in range(count)
+                for chunk in range(asked)
                 for ref, half in ((q_ref, odd), (qs_ref, 1 - odd))
             ]
         )
@@ -322,9 +350,12 @@
     return jnp.transpose(jnp.concatenate([part, fill], 0))
 
 
-def partial_kernel(transfers, upper, onto, *refs):
+def partial_kernel(transfers, upper, natural, asking, onto, *refs):
     count = len(transfers)
     out_ref = refs[-1]
+    if asking:
+        next_refs = refs[7 + count : 9 + count]
+        refs = refs[: 7 + count] + refs[9 + count :]
     q_ref, k_ref, v_ref, kp_ref, vp_ref, g_ref, gp_ref = refs[:7]
     ask_refs = refs[7 : 7 + count]
     own_ref, lse_ref = refs[7 + count + onto : 9 + count + onto]
@@ -364,7 +395,13 @@
             sums = [[], []]
             for head in range(heads):
                 keys, values = key_value(head, with_quad)
-                query = ask_refs[index][:, :, block_lanes(head)].reshape(2 * rows, HEAD_DIM)
+                if natural:
+                    query = ask_refs[index][:, :, block_lanes(head)].reshape(2 * rows, HEAD_DIM)
+                else:
+                    halves = [half * half_rows + head * rows for half in range(2)]
+                    query = jnp.concatenate(
+                        [ask_refs[index][start : start + rows, :] for start in halves], 0
+                    )
                 mixed, lse = soft(query, keys, values)
                 for half in range(2):
                     cut = slice(half * rows, (half + 1) * rows)
@@ -390,6 +427,16 @@
         pl.when(jnp.logical_not(among(me, upper)))(functools.partial(run, False))
     else:
         run(False)
+
+    if asking:
+        for index, pairs in enumerate(transfers):
+
+            @pl.when(among(me, [source for source, _ in pairs]))
+            def _():
+                for ref, half in zip(next_refs, (me % 2, 1 - me % 2)):
+                    for head in range(heads):
+                        start = pl.multiple_of(half * half_rows + head * rows, TAIL)
+                        answer_refs[index][pl.ds(start, rows), :] = ref[:, block_lanes(head)]
 
 
 def merge_kernel(transfers, steps, start, own_hbm, lse_hbm, *refs):
@@ -471,56 +518,60 @@
     key_swapped = lax.ppermute(key, "ctx", swap)
     value_swapped = lax.ppermute(value, "ctx", swap)
 
-    def pack(members):
+    both_ways = chunks > LAG and all(
+        not {source for source, _ in pairs} & {target for _, target in pairs}
+        for pairs in transfers
+    )
+    asked = LAG if both_ways else chunks
+
+    def pack():
         hbm = pl.BlockSpec(memory_space=pl.ANY)
-        shapes = [
-            jax.ShapeDtypeStruct((2, rows, widths[chunk]), jnp.bfloat16) for chunk in members
-        ]
+        shapes = [jax.ShapeDtypeStruct((2, rows, width), jnp.bfloat16) for width in widths]
         outs = pl.pallas_call(
             functools.partial(
                 pack_kernel,
                 [source for source, _ in gathers],
                 askers,
-                [widths[chunk] for chunk in members],
-                [starts[chunk] for chunk in members],
+                asked,
+                widths,
+                starts,
             ),
             in_specs=[hbm] * 4,
-            out_specs=[hbm] * (2 * len(members)),
-            out_shape=shapes * 2,
+            out_specs=[hbm] * (chunks + asked),
+            out_shape=shapes + shapes[:asked],
             scratch_shapes=[
-                pltpu.VMEM((rows, widths[chunk]), jnp.bfloat16)
-                for chunk in members
-                for _ in range(2)
+                pltpu.VMEM((rows, width), jnp.bfloat16) for width in widths for _ in range(2)
             ]
-            + [pltpu.SemaphoreType.DMA((2 * len(members),))] * 2,
+            + [pltpu.SemaphoreType.DMA((2 * chunks,))] * 2,
             compiler_params=params(),
             cost_estimate=cost(1),
             name="att_pack",
         )(query, query_swapped, key, value)
-        return list(zip(outs[: len(members)], outs[len(members) :]))
-
-    packs = pack(list(range(chunks)))
+        return outs[:chunks], outs[chunks:]
+
+    key_packs, query_packs = pack()
     conv_first, conv_last = conv
-    local_result, *conv_shared = conv_first(packs[0][1])
-    asks, quad_kv, all_answers = [], [], []
+    local_result, *conv_shared = conv_first(query_packs[0])
+    asks, quad_kv, all_answers = {}, [], []
 
     def send(chunk):
-        key_pack, query_pack = packs[chunk]
-        if chunk > 1:
-            key_pack = after(key_pack, quad_kv[chunk - 2][0], all_answers[chunk - 2][0])
-            query_pack = after(query_pack, *asks[chunk - 2], all_answers[chunk - 2][0])
-        arrived = lax.ppermute(key_pack, "ctx", gathers)
-        asks.append([lax.ppermute(query_pack, "ctx", pairs) for pairs in transfers])
-        quad_kv.append([arrived])
+        key_pack = key_packs[chunk]
+        if chunk >= LAG:
+            key_pack = after(key_pack, quad_kv[chunk - LAG][0], all_answers[chunk - LAG][0])
+        quad_kv.append([lax.ppermute(key_pack, "ctx", gathers)])
+        if chunk < asked:
+            query_pack = query_packs[chunk]
+            if chunk >= LAG:
+                query_pack = after(query_pack, *asks[chunk - LAG], all_answers[chunk - LAG][0])
+            asks[chunk] = [lax.ppermute(query_pack, "ctx", pairs) for pairs in transfers]
 
     half_rows = HEADS_PER_STEP * rows + TAIL
     hbm = pl.BlockSpec(memory_space=pl.ANY)
-    send(0)
+    for chunk in range(min(LAG, chunks)):
+        send(chunk)
     result = None
     returned = []
     for chunk in range(chunks):
-        if chunk + 1 < chunks:
-            send(chunk + 1)
         if chunk == 0:
             quad_kv[0] = [after(quad_kv[0][0], local_result)]
             asks[0] = [after(asked, local_result) for asked in asks[0]]
@@ -532,15 +583,24 @@
         lse_spec = pl.BlockSpec((SUBLANES, LANES), lambda step: (step, 0))
         answer_spec = pl.BlockSpec((2 * half_rows, LANES), lambda step: (step, 0))
         answer_shape = jax.ShapeDtypeStruct((2 * half_rows * steps, LANES), jnp.bfloat16)
+        asking = both_ways and chunk + LAG < chunks
+        natural = chunk < asked
         operands = [query, key, value, key_swapped, value_swapped, *quad_kv[chunk], *asks[chunk]]
-        specs = [whole_spec] * 5 + [pair_spec] * (2 + len(transfers))
+        specs = [whole_spec] * 5 + [pair_spec] * 2
+        specs += [pair_spec if natural else answer_spec] * len(transfers)
+        if asking:
+            later = first_steps[chunk + LAG]
+            operands += [query, query_swapped]
+            specs += [
+                pl.BlockSpec((rows, step_width), lambda step, later=later: (0, later + step))
+            ] * 2
         aliases = {}
         if result is not None:
             aliases = {len(operands): 2 + len(transfers)}
             operands.append(result)
             specs.append(hbm)
         own, lse, *answers, result = pl.pallas_call(
-            functools.partial(partial_kernel, transfers, upper, len(aliases)),
+            functools.partial(partial_kernel, transfers, upper, natural, asking, len(aliases)),
             grid=(steps,),
             in_specs=specs,
             out_specs=[chunk_spec, lse_spec] + [answer_spec] * len(transfers) + [whole_spec],
@@ -557,12 +617,25 @@
         )(*operands)
         all_answers.append(answers)
         parts = [own, lse]
+        arrivals = []
         for answer, pairs in zip(answers, transfers):
-            back = lax.ppermute(answer, "ctx", [(target, source) for source, target in pairs])
-            parts += [back, lax.ppermute(back, "ctx", swap)]
-        returned.append(parts)
+            moves = [(target, source) for source, target in pairs]
+            if asking:
+                moves += pairs
+            arrivals.append(lax.ppermute(answer, "ctx", moves))
+        if asking:
+            asks[chunk + LAG] = arrivals
+        returned.append([own, lse, arrivals])
+        if chunk + LAG < chunks:
+            send(chunk + LAG)
     conv_shared = [after(part, all_answers[-1][0]) for part in conv_shared]
-    for chunk, parts in enumerate(returned):
+    hyena_out = conv_last(local_result, *conv_shared)
+    for chunk, (own, lse, arrivals) in enumerate(returned):
+        parts = [own, lse]
+        for arrival in arrivals:
+            if chunk == chunks - 1:
+                arrival = after(arrival, hyena_out, result)
+            parts += [arrival, lax.ppermute(arrival, "ctx", swap)]
         steps = CHUNK_STEPS[chunk]
         count = 2 * len(transfers)
         result = pl.pallas_call(
@@ -584,7 +657,7 @@
             cost_estimate=cost(2),
             name="att_merge",
         )(*parts, result)
-    return conv_last(local_result, *conv_shared), result
+    return hyena_out, result
 
 
 def local(

time: 164 us -> 134 us (0.82)
  the two profiles are of different devices: /device:TPU:25 before, /device:TPU:29 now
where the time goes in v6:
time: 134 us
  starting transfers between devices  67.2 us (50%)
  Pallas kernels  44.6 us (33%)
  waiting for transfers between devices  15.2 us (11%)
  other arithmetic  4.88 us (4%)
    ppermute x4, starting transfers between devices, attend(): parts += [arrival, lax.ppermute(arrival, 'ctx', swap)]  16.9 us
    pallas_call x4, Pallas kernels, attend(): pl.pallas_call(functools.partial(partial_kernel, transfers, upper, natura...  13.9 us
    ppermute x4, starting transfers between devices, attend(): quad_kv[chunk].append(lax.ppermute(quad_kv[chunk][0], 'ctx', swap))  12.8 us
    ppermute x4, starting transfers between devices, attend(): arrivals.append(lax.ppermute(answer, 'ctx', moves))  11.9 us
    pallas_call x4, Pallas kernels, attend(): pl.pallas_call(functools.partial(merge_kernel, transfers, steps, starts[c...  10.6 us
    pallas_call x1, Pallas kernels, first_part(): pl.pallas_call(functools.partial(state_kernel, modes), grid=(groups,), in...  9.72 us
    all_to_all x1, starting transfers between devices, first_part(): lax.all_to_all(own_par, 'ctx', split_axis=0, concat_axis=0, tiled=True)  7.74 us
    all_to_all x1, waiting for transfers between devices, first_part(): lax.all_to_all(own_par, 'ctx', split_axis=0, concat_axis=0, tiled=True)  6.36 us
  transfers between devices with their start and end apart: 27, of which 5 were waited for; matrix products, arithmetic and copies ran while one was open for 4% of the time, Pallas kernels for 31%

profile of v6, /device:TPU:29, one launch (start us, length us, event | category | flops | bytes accessed | tf_op | source)
XLA Modules:
  0.0 133.7 jit_solution(18157087740874538720)
XLA Ops:
  0.6 0.7 collective-permute-start.1
  1.4 1.9 %conv_pack.1 = (f32[8,128,128]{2,1,0:T(8,128)}, f32[8,4096]{1,0:T(8,128)}) custom-call(f32[16,512]{1,0:T(8,128)} %bitcast.3, f32[16,512]{1,0:T(8,128)} %bitcast.4, bf16[128,4096]{1,0:T(8,128)(2,1)} %q_ref.5, bf16[128,4096]{1,0:T(8,128)(2,1)} %k_ref.5, bf16[128,4096]{1,0:T(8,128)(2,1)} %v_ref.5), custom_call_target="tpu_custom_call" | custom-call | flops 100000000 | bytes 65536 | tf_op jit(solution)/shard_map/conv_pack/pallas_call | solution.py:176
  3.3 1.3 collective-permute-start
  4.6 2.2 %att_pack.1 = (bf16[2,128,1024]{2,1,0:T(8,128)(2,1)}, bf16[2,128,1024]{2,1,0:T(8,128)(2,1)}, bf16[2,128,1024]{2,1,0:T(8,128)(2,1)}, bf16[2,128,1024]{2,1,0:T(8,1...) custom-call(bf16[128,4096]{1,0:T(8,128)(2,1)} %refs_0_.7, ...), custom_call_target="tpu_custom_call" | custom-call | flops 100000000 | bytes 65536 | tf_op jit(solution)/shard_map/att_pack/pallas_call | solution.py:530
  6.8 7.7 %all-to-all-start = ((f32[8,128,128]{2,1,0:T(8,128)}), f32[8,128,128]{2,1,0:T(8,128)}, u32[]{:S(2)}, u32[]{:S(2)}) async-start(f32[8,128,128]{2,1,0:T(8,128)} %get-tuple-element.44), calls=%async_computation | async-start | bytes 1048576 | tf_op jit(solution)/shard_map/all_to_all | solution.py:195
  14.6 1.5 %collective-permute-start.7 = (bf16[2,128,1024]{2,1,0:T(8,128)(2,1)}, bf16[2,128,1024]{2,1,0:T(8,128)(2,1)}, u32[]{:S(2)}, u32[]{:S(2)}) collective-permute-start(bf16[2,128,1024]{2,1,0:T(8,128)(2,1)} %get-tuple-element.49), channel_id=1, source_target_pairs={{0,2},{1,3},{8,10},{9,11},{16,18},{17,19},{24,26},{25,27}} | collective-permute-start | bytes 1572872 | tf_op jit(solution)/shard_map/ppermute | solution.py:561
  16.0 0.4 collective-permute-start.2
  16.4 0.1 collective-permute-start.3
  16.5 3.0 %collective-permute-start.9 = (bf16[2,128,1024]{2,1,0:T(8,128)(2,1)}, bf16[2,128,1024]{2,1,0:T(8,128)(2,1)}, u32[]{:S(2)}, u32[]{:S(2)}) collective-permute-start(bf16[2,128,1024]{2,1,0:T(8,128)(2,1)} %get-tuple-element.43), channel_id=1, source_target_pairs={{7,5},{4,2},{6,3},{15,13},{12,10},{14,11},{23,21},{20,18},{22,19},... | collective-permute-start | bytes 1572872 | tf_op jit(solution)/shard_map/ppermute | solution.py:566
  19.5 1.5 %collective-permute-start.4 = (bf16[2,128,1024]{2,1,0:T(8,128)(2,1)}, bf16[2,128,1024]{2,1,0:T(8,128)(2,1)}, u32[]{:S(2)}, u32[]{:S(2)}) collective-permute-start(bf16[2,128,1024]{2,1,0:T(8,128)(2,1)} %get-tuple-element.47), channel_id=1, source_target_pairs={{0,2},{1,3},{8,10},{9,11},{16,18},{17,19},{24,26},{25,27}} | collective-permute-start | bytes 1572872 | tf_op jit(solution)/shard_map/ppermute | solution.py:561
  21.0 6.4 %all-to-all-done = f32[8,128,128]{2,1,0:T(8,128)} async-done(((f32[8,128,128]{2,1,0:T(8,128)}), f32[8,128,128]{2,1,0:T(8,128)}, u32[]{:S(2)}, u32[]{:S(2)}) %all-to-all-start) | async-done | bytes 524320 | tf_op jit(solution)/shard_map/all_to_all | solution.py:195
  27.4 9.7 %conv_state.1 = (f32[128,4096]{1,0:T(8,128)}, f32[512,128]{1,0:T(8,128)}, f32[512,128]{1,0:T(8,128)}) custom-call(bf16[128,4096]{1,0:T(8,128)(2,1)} %k_ref.5, bf16[128,4096]{1,0:T(8,128)(2,1)} %v_ref.5, f32[8,4096]{1,0:T(8,128)} %copy-done.1, f32[1024,128]{1,0:T(8,128)} %bitcast.2.par_ref, f32[3,3,4096]{2,1,0:T(4,128)} %taps_ref.3), custom_call_target="tpu_custom_call" | custom-call | flops 900000000 | bytes 65536 | tf_op jit(solution)/shard_map/conv_state/pallas_call | solution.py:198
  37.1 0.0 collective-permute-done.7.refs_5_
  37.1 0.5 collective-permute-start.8
  37.6 3.4 %collective-permute-start.6 = (bf16[2,128,1024]{2,1,0:T(8,128)(2,1)}, bf16[2,128,1024]{2,1,0:T(8,128)(2,1)}, u32[]{:S(2)}, u32[]{:S(2)}) collective-permute-start(bf16[2,128,1024]{2,1,0:T(8,128)(2,1)} %get-tuple-element.48), channel_id=1, source_target_pairs={{7,5},{4,2},{6,3},{15,13},{12,10},{14,11},{23,21},{20,18},{22,19},... | collective-permute-start | bytes 1572872 | tf_op jit(solution)/shard_map/ppermute | solution.py:566
  41.0 0.1 collective-permute-start.5
  41.1 3.6 %att_partial.4 = (f32[128,1024]{1,0:T(8,128)}, f32[16,128]{1,0:T(8,128)}, bf16[2176,128]{1,0:T(8,128)(2,1)}, bf16[128,4096]{1,0:T(8,128)(2,1)}) custom-call(bf16[128,4096]{1,0:T(8,128)(2,1)} %refs_0_.7, bf16[128,4096]{1,0:T(8,128)(2,1)} %refs_1_.7, bf16[128,4096]{1,0:T(8,128)(2,1)} %refs_2_.7, bf16[128,4096]{1,0:T(8,128)(2,1)} %collective-permute-done.2.refs_3_, ...), custom_call_target="tpu_custom_call" | custom-call | flops 400000000 | bytes 65536 | tf_op jit(solution)/shard_map/att_partial/pallas_call | solution.py:602
  44.6 1.5 %collective-permute-start.13 = (bf16[2,128,1024]{2,1,0:T(8,128)(2,1)}, bf16[2,128,1024]{2,1,0:T(8,128)(2,1)}, u32[]{:S(2)}, u32[]{:S(2)}) collective-permute-start(bf16[2,128,1024]{2,1,0:T(8,128)(2,1)} %get-tuple-element.57), channel_id=1, source_target_pairs={{0,2},{1,3},{8,10},{9,11},{16,18},{17,19},{24,26},{25,27}} | collective-permute-start | bytes 1572872 | tf_op jit(solution)/shard_map/ppermute | solution.py:561
  46.1 0.4 collective-permute-start.16
  46.6 5.4 %collective-permute-start.15 = (bf16[2176,128]{1,0:T(8,128)(2,1)}, bf16[2176,128]{1,0:T(8,128)(2,1)}, u32[]{:S(2)}, u32[]{:S(2)}) collective-permute-start(bf16[2176,128]{1,0:T(8,128)(2,1)} %get-tuple-element.56), channel_id=1, source_target_pairs={{5,7},{2,4},{3,6},{7,5},{4,2},{6,3},{13,15},{10,12},{11,14},{15,13... | collective-permute-start | bytes 1671176 | tf_op jit(solution)/shard_map/ppermute | solution.py:625
  51.9 0.1 collective-permute-done.6.refs_7_
  52.0 3.6 %att_partial.5 = (f32[128,1024]{1,0:T(8,128)}, f32[16,128]{1,0:T(8,128)}, bf16[2176,128]{1,0:T(8,128)(2,1)}, bf16[128,4096]{1,0:T(8,128)(2,1)}) custom-call(bf16[128,4096]{1,0:T(8,128)(2,1)} %refs_0_.7, bf16[128,4096]{1,0:T(8,128)(2,1)} %refs_1_.7, bf16[128,4096]{1,0:T(8,128)(2,1)} %refs_2_.7, ...), custom_call_target="tpu_custom_call", output_to_operand_aliasing={{3}: (10, {})} | custom-call | flops 400000000 | bytes 65536 | tf_op jit(solution)/shard_map/att_partial/pallas_call | solution.py:602
  55.6 1.5 %collective-permute-start.10 = (bf16[2,128,1024]{2,1,0:T(8,128)(2,1)}, bf16[2,128,1024]{2,1,0:T(8,128)(2,1)}, u32[]{:S(2)}, u32[]{:S(2)}) collective-permute-start(bf16[2,128,1024]{2,1,0:T(8,128)(2,1)} %get-tuple-element.54), channel_id=1, source_target_pairs={{0,2},{1,3},{8,10},{9,11},{16,18},{17,19},{24,26},{25,27}} | collective-permute-start | bytes 1572872 | tf_op jit(solution)/shard_map/ppermute | solution.py:561
  57.0 5.0 %collective-permute-start.14 = (bf16[2,128,1024]{2,1,0:T(8,128)(2,1)}, bf16[2,128,1024]{2,1,0:T(8,128)(2,1)}, u32[]{:S(2)}, u32[]{:S(2)}) collective-permute-start(bf16[2,128,1024]{2,1,0:T(8,128)(2,1)} %collective-permute-done.13.refs_5_), channel_id=1, source_target_pairs={{0,1},{1,0},{2,3},{3,2},{4,5},{5,4},{6,7},{7,6},{8,9},{9,8},{10,11... | collective-permute-start | bytes 1572872 | tf_op jit(solution)/shard_map/ppermute | solution.py:578
  62.0 1.9 %multiply_add_fusion.2 = f32[512,128]{1,0:T(8,128)} fusion(f32[512,128]{1,0:T(8,128)} %get-tuple-element.65, f32[512,128]{1,0:T(8,128)} %get-tuple-element.64.decay_ref, f32[512,128]{1,0:T(8,128)} %collective-permute-done.16.other_ref), kind=kLoop, calls=%fused_computation.2 | loop fusion | flops 131072 | bytes 1048576 | tf_op jit(solution)/shard_map/add | solution.py:218
  63.9 1.3 collective-permute-start.17
  65.2 4.0 %collective-permute-start.12 = (bf16[2176,128]{1,0:T(8,128)(2,1)}, bf16[2176,128]{1,0:T(8,128)(2,1)}, u32[]{:S(2)}, u32[]{:S(2)}) collective-permute-start(bf16[2176,128]{1,0:T(8,128)(2,1)} %get-tuple-element.53), channel_id=1, source_target_pairs={{5,7},{2,4},{3,6},{7,5},{4,2},{6,3},{13,15},{10,12},{11,14},{15,13... | collective-permute-start | bytes 1671176 | tf_op jit(solution)/shard_map/ppermute | solution.py:625
  69.2 7.2 %collective-permute-start.11 = (bf16[2,128,1024]{2,1,0:T(8,128)(2,1)}, bf16[2,128,1024]{2,1,0:T(8,128)(2,1)}, u32[]{:S(2)}, u32[]{:S(2)}) collective-permute-start(bf16[2,128,1024]{2,1,0:T(8,128)(2,1)} %collective-permute-done.10.refs_5_), channel_id=1, source_target_pairs={{0,1},{1,0},{2,3},{3,2},{4,5},{5,4},{6,7},{7,6},{8,9},{9,8},{10,11... | collective-permute-start | bytes 1572872 | tf_op jit(solution)/shard_map/ppermute | solution.py:578
  76.4 3.4 %att_partial.6 = (f32[128,1024]{1,0:T(8,128)}, f32[16,128]{1,0:T(8,128)}, bf16[2176,128]{1,0:T(8,128)(2,1)}, bf16[128,4096]{1,0:T(8,128)(2,1)}) custom-call(bf16[128,4096]{1,0:T(8,128)(2,1)} %refs_0_.7, bf16[128,4096]{1,0:T(8,128)(2,1)} %refs_1_.7, bf16[128,4096]{1,0:T(8,128)(2,1)} %refs_2_.7, ...), custom_call_target="tpu_custom_call", output_to_operand_aliasing={{3}: (8, {})} | custom-call | flops 400000000 | bytes 65536 | tf_op jit(solution)/shard_map/att_partial/pallas_call | solution.py:602
  79.8 1.3 collective-permute-start.21
  81.1 1.9 %multiply_add_fusion.1 = f32[512,128]{1,0:T(8,128)} fusion(f32[512,128]{1,0:T(8,128)} %multiply_add_fusion.2, f32[512,128]{1,0:T(8,128)} %collective-permute-done.17, f32[512,128]{1,0:T(8,128)} %get-tuple-element.64.decay_ref), kind=kLoop, calls=%fused_computation.1 | loop fusion | flops 196608 | bytes 1048576 | tf_op jit(solution)/shard_map/add | solution.py:229
  82.9 1.5 %collective-permute-start.18 = (f32[512,128]{1,0:T(8,128)}, f32[512,128]{1,0:T(8,128)}, u32[]{:S(2)}, u32[]{:S(2)}) collective-permute-start(f32[512,128]{1,0:T(8,128)} %multiply_add_fusion.1), channel_id=1, source_target_pairs={{1,5},{3,7},{9,13},{11,15},{17,21},{19,23},{25,29},{27,31}} | collective-permute-start | bytes 786440 | tf_op jit(solution)/shard_map/ppermute | solution.py:223
  84.4 0.1 collective-permute-start.24
  84.5 6.5 %collective-permute-start.23 = (bf16[2176,128]{1,0:T(8,128)(2,1)}, bf16[2176,128]{1,0:T(8,128)(2,1)}, u32[]{:S(2)}, u32[]{:S(2)}) collective-permute-start(bf16[2176,128]{1,0:T(8,128)(2,1)} %collective-permute-done.12.refs_7_.refs_0_), channel_id=1, source_target_pairs={{0,1},{1,0},{2,3},{3,2},{4,5},{5,4},{6,7},{7,6},{8,9},{9,8},{10,11... | collective-permute-start | bytes 1671176 | tf_op jit(solution)/shard_map/ppermute | solution.py:638
  91.0 3.4 %att_partial.7 = (f32[128,1024]{1,0:T(8,128)}, f32[16,128]{1,0:T(8,128)}, bf16[2176,128]{1,0:T(8,128)(2,1)}, bf16[128,4096]{1,0:T(8,128)(2,1)}) custom-call(bf16[128,4096]{1,0:T(8,128)(2,1)} %refs_0_.7, bf16[128,4096]{1,0:T(8,128)(2,1)} %refs_1_.7, bf16[128,4096]{1,0:T(8,128)(2,1)} %refs_2_.7, ...), custom_call_target="tpu_custom_call", output_to_operand_aliasing={{3}: (8, {})} | custom-call | flops 400000000 | bytes 65536 | tf_op jit(solution)/shard_map/att_partial/pallas_call | solution.py:602
  94.4 1.3 collective-permute-start.20
  95.7 10.1 %collective-permute-start.22 = (bf16[2176,128]{1,0:T(8,128)(2,1)}, bf16[2176,128]{1,0:T(8,128)(2,1)}, u32[]{:S(2)}, u32[]{:S(2)}) collective-permute-start(bf16[2176,128]{1,0:T(8,128)(2,1)} %collective-permute-done.21.refs_0_), channel_id=1, source_target_pairs={{0,1},{1,0},{2,3},{3,2},{4,5},{5,4},{6,7},{7,6},{8,9},{9,8},{10,11... | collective-permute-start | bytes 1671176 | tf_op jit(solution)/shard_map/ppermute | solution.py:638
  105.7 4.9 %collective-permute-done.18 = f32[512,128]{1,0:T(8,128)} collective-permute-done((f32[512,128]{1,0:T(8,128)}, f32[512,128]{1,0:T(8,128)}, u32[]{:S(2)}, u32[]{:S(2)}) %collective-permute-start.18) | collective-permute-done | bytes 262176 | tf_op jit(solution)/shard_map/ppermute | solution.py:223
  110.7 1.1 multiply_add_fusion.enter_ref
  111.8 0.7 copy-done
  112.5 1.7 %collective-permute-done.19.enter_first_ref = f32[512,128]{1,0:T(8,128)} collective-permute-done((f32[512,128]{1,0:T(8,128)S(1)}, f32[512,128]{1,0:T(8,128)}, u32[]{:S(2)}, u32[]{:S(2)}) %collective-permute-start.19) | collective-permute-done | bytes 262176 | tf_op jit(solution)/shard_map/ppermute | solution.py:231
  114.2 6.3 %conv_output.1 = bf16[128,4096]{1,0:T(8,128)(2,1)} custom-call(bf16[128,4096]{1,0:T(8,128)(2,1)} %q_ref.5, f32[128,4096]{1,0:T(8,128)} %get-tuple-element.45.y_ref, f32[8,4096]{1,0:T(8,128)} %copy-done.1, f32[1024,128]{1,0:T(8,128)} %bitcast.2.par_ref, f32[512,128]{1,0:T(8,128)} %get-tuple-element.64.decay_ref, f32[512,128]{1,0:T(8,128)} %copy-done, ...), custom_call_target="tpu_custom_call" | custom-call | flops 600000000 | bytes 65536 | tf_op jit(solution)/shard_map/conv_output/pallas_call | solution.py:235
  120.5 2.7 %att_merge.4.refs_2_ = bf16[128,4096]{1,0:T(8,128)(2,1)} custom-call(f32[128,1024]{1,0:T(8,128)} %get-tuple-element.76.own_hbm, f32[16,128]{1,0:T(8,128)} %get-tuple-element.77.lse_hbm, bf16[2176,128]{1,0:T(8,128)(2,1)} %collective-permute-done.15.refs_7_.refs_0_, bf16[2176,128]{1,0:T(8,128)(2,1)} %collective-permute-done.24.refs_1_, ...), custom_call_target="tpu_custom_call", output_to_operand_aliasing={{}: (4, {})} | custom-call | flops 200000000 | bytes 65536 | tf_op jit(solution)/shard_map/att_merge/pallas_call | solution.py:641
  123.2 2.7 %att_merge.5.refs_2_ = bf16[128,4096]{1,0:T(8,128)(2,1)} custom-call(f32[128,1024]{1,0:T(8,128)} %get-tuple-element.74.own_hbm, f32[16,128]{1,0:T(8,128)} %get-tuple-element.75.lse_hbm, bf16[2176,128]{1,0:T(8,128)(2,1)} %collective-permute-done.12.refs_7_.refs_0_, bf16[2176,128]{1,0:T(8,128)(2,1)} %collective-permute-done.23.refs_1_, ...), custom_call_target="tpu_custom_call", output_to_operand_aliasing={{}: (4, {})} | custom-call | flops 200000000 | bytes 65536 | tf_op jit(solution)/shard_map/att_merge/pallas_call | solution.py:641
  125.8 2.7 %att_merge.6.refs_2_ = bf16[128,4096]{1,0:T(8,128)(2,1)} custom-call(f32[128,1024]{1,0:T(8,128)} %get-tuple-element.71.own_hbm, f32[16,128]{1,0:T(8,128)} %get-tuple-element.72.lse_hbm, bf16[2176,128]{1,0:T(8,128)(2,1)} %collective-permute-done.21.refs_0_, bf16[2176,128]{1,0:T(8,128)(2,1)} %collective-permute-done.22.refs_1_, ...), custom_call_target="tpu_custom_call", output_to_operand_aliasing={{}: (4, {})} | custom-call | flops 200000000 | bytes 65536 | tf_op jit(solution)/shard_map/att_merge/pallas_call | solution.py:641
  128.5 0.2 collective-permute-start.25
  128.7 2.2 %collective-permute-done.25.refs_1_ = bf16[2176,128]{1,0:T(8,128)(2,1)} collective-permute-done((bf16[2176,128]{1,0:T(8,128)(2,1)}, bf16[2176,128]{1,0:T(8,128)(2,1)}, u32[]{:S(2)}, u32[]{:S(2)}) %collective-permute-start.25) | collective-permute-done | bytes 557088 | tf_op jit(solution)/shard_map/ppermute | solution.py:638
  130.9 2.6 %att_merge.7 = bf16[128,4096]{1,0:T(8,128)(2,1)} custom-call(f32[128,1024]{1,0:T(8,128)} %get-tuple-element.69.own_hbm, f32[16,128]{1,0:T(8,128)} %get-tuple-element.70.lse_hbm, bf16[2176,128]{1,0:T(8,128)(2,1)} %collective-permute-done.20.refs_0_, bf16[2176,128]{1,0:T(8,128)(2,1)} %collective-permute-done.25.refs_1_, ...), custom_call_target="tpu_custom_call", output_to_operand_aliasing={{}: (4, {})} | custom-call | flops 200000000 | bytes 65536 | tf_op jit(solution)/shard_map/att_merge/pallas_call | solution.py:641
  (25 shorter events, 0.1 us)
Async XLA Ops:
  0.6 4.0 %collective-permute-start.1 = (bf16[128,4096]{1,0:T(8,128)(2,1)}, bf16[128,4096]{1,0:T(8,128)(2,1)}, u32[]{:S(2)}, u32[]{:S(2)}) collective-permute-start(bf16[128,4096]{1,0:T(8,128)(2,1)} %refs_0_.7), channel_id=1, source_target_pairs={{0,1},{1,0},{2,3},{3,2},{4,5},{5,4},{6,7},{7,6},{8,9},{9,8},{10,11... | collective-permute-start | bytes 3145736 | tf_op jit(solution)/shard_map/ppermute | solution.py:517
  3.3 3.5 %collective-permute-start = (f32[8,4096]{1,0:T(8,128)}, f32[8,4096]{1,0:T(8,128)S(1)}, u32[]{:S(2)}, u32[]{:S(2)}) collective-permute-start(f32[8,4096]{1,0:T(8,128)} %get-tuple-element.41), channel_id=1, source_target_pairs={{0,1},{1,2},{2,3},{3,4},{4,5},{5,6},{6,7},{8,9},{9,10},{10,11},{11... | collective-permute-start | bytes 393224 | tf_op jit(solution)/shard_map/ppermute | solution.py:193
  6.8 20.6 %copy-start.1 = (f32[8,4096]{1,0:T(8,128)}, f32[8,4096]{1,0:T(8,128)S(1)}, u32[]{:S(2)}) copy-start(f32[8,4096]{1,0:T(8,128)S(1)} %collective-permute-done.rim_ref) | copy-start | bytes 393220
  6.8 20.6 %all-to-all-start = ((f32[8,128,128]{2,1,0:T(8,128)}), f32[8,128,128]{2,1,0:T(8,128)}, u32[]{:S(2)}, u32[]{:S(2)}) async-start(f32[8,128,128]{2,1,0:T(8,128)} %get-tuple-element.44), calls=%async_computation | async-start | bytes 1048576 | tf_op jit(solution)/shard_map/all_to_all | solution.py:195
  14.6 22.5 %collective-permute-start.7 = (bf16[2,128,1024]{2,1,0:T(8,128)(2,1)}, bf16[2,128,1024]{2,1,0:T(8,128)(2,1)}, u32[]{:S(2)}, u32[]{:S(2)}) collective-permute-start(bf16[2,128,1024]{2,1,0:T(8,128)(2,1)} %get-tuple-element.49), channel_id=1, source_target_pairs={{0,2},{1,3},{8,10},{9,11},{16,18},{17,19},{24,26},{25,27}} | collective-permute-start | bytes 1572872 | tf_op jit(solution)/shard_map/ppermute | solution.py:561
  16.0 25.1 %collective-permute-start.2 = (bf16[128,4096]{1,0:T(8,128)(2,1)}, bf16[128,4096]{1,0:T(8,128)(2,1)}, u32[]{:S(2)}, u32[]{:S(2)}) collective-permute-start(bf16[128,4096]{1,0:T(8,128)(2,1)} %refs_1_.7), channel_id=1, source_target_pairs={{0,1},{1,0},{2,3},{3,2},{4,5},{5,4},{6,7},{7,6},{8,9},{9,8},{10,11... | collective-permute-start | bytes 3145736 | tf_op jit(solution)/shard_map/ppermute | solution.py:518
  16.4 24.7 %collective-permute-start.3 = (bf16[128,4096]{1,0:T(8,128)(2,1)}, bf16[128,4096]{1,0:T(8,128)(2,1)}, u32[]{:S(2)}, u32[]{:S(2)}) collective-permute-start(bf16[128,4096]{1,0:T(8,128)(2,1)} %refs_2_.7), channel_id=1, source_target_pairs={{0,1},{1,0},{2,3},{3,2},{4,5},{5,4},{6,7},{7,6},{8,9},{9,8},{10,11... | collective-permute-start | bytes 3145736 | tf_op jit(solution)/shard_map/ppermute | solution.py:519
  16.5 21.1 %collective-permute-start.9 = (bf16[2,128,1024]{2,1,0:T(8,128)(2,1)}, bf16[2,128,1024]{2,1,0:T(8,128)(2,1)}, u32[]{:S(2)}, u32[]{:S(2)}) collective-permute-start(bf16[2,128,1024]{2,1,0:T(8,128)(2,1)} %get-tuple-element.43), channel_id=1, source_target_pairs={{7,5},{4,2},{6,3},{15,13},{12,10},{14,11},{23,21},{20,18},{22,19},... | collective-permute-start | bytes 1572872 | tf_op jit(solution)/shard_map/ppermute | solution.py:566
  19.5 21.5 %collective-permute-start.4 = (bf16[2,128,1024]{2,1,0:T(8,128)(2,1)}, bf16[2,128,1024]{2,1,0:T(8,128)(2,1)}, u32[]{:S(2)}, u32[]{:S(2)}) collective-permute-start(bf16[2,128,1024]{2,1,0:T(8,128)(2,1)} %get-tuple-element.47), channel_id=1, source_target_pairs={{0,2},{1,3},{8,10},{9,11},{16,18},{17,19},{24,26},{25,27}} | collective-permute-start | bytes 1572872 | tf_op jit(solution)/shard_map/ppermute | solution.py:561
  37.1 4.0 %collective-permute-start.8 = (bf16[2,128,1024]{2,1,0:T(8,128)(2,1)}, bf16[2,128,1024]{2,1,0:T(8,128)(2,1)}, u32[]{:S(2)}, u32[]{:S(2)}) collective-permute-start(bf16[2,128,1024]{2,1,0:T(8,128)(2,1)} %collective-permute-done.7.refs_5_), channel_id=1, source_target_pairs={{0,1},{1,0},{2,3},{3,2},{4,5},{5,4},{6,7},{7,6},{8,9},{9,8},{10,11... | collective-permute-start | bytes 1572872 | tf_op jit(solution)/shard_map/ppermute | solution.py:578
  37.6 14.4 %collective-permute-start.6 = (bf16[2,128,1024]{2,1,0:T(8,128)(2,1)}, bf16[2,128,1024]{2,1,0:T(8,128)(2,1)}, u32[]{:S(2)}, u32[]{:S(2)}) collective-permute-start(bf16[2,128,1024]{2,1,0:T(8,128)(2,1)} %get-tuple-element.48), channel_id=1, source_target_pairs={{7,5},{4,2},{6,3},{15,13},{12,10},{14,11},{23,21},{20,18},{22,19},... | collective-permute-start | bytes 1572872 | tf_op jit(solution)/shard_map/ppermute | solution.py:566
  41.0 11.0 %collective-permute-start.5 = (bf16[2,128,1024]{2,1,0:T(8,128)(2,1)}, bf16[2,128,1024]{2,1,0:T(8,128)(2,1)}, u32[]{:S(2)}, u32[]{:S(2)}) collective-permute-start(bf16[2,128,1024]{2,1,0:T(8,128)(2,1)} %collective-permute-done.4.refs_5_), channel_id=1, source_target_pairs={{0,1},{1,0},{2,3},{3,2},{4,5},{5,4},{6,7},{7,6},{8,9},{9,8},{10,11... | collective-permute-start | bytes 1572872 | tf_op jit(solution)/shard_map/ppermute | solution.py:578
  44.6 12.4 %collective-permute-start.13 = (bf16[2,128,1024]{2,1,0:T(8,128)(2,1)}, bf16[2,128,1024]{2,1,0:T(8,128)(2,1)}, u32[]{:S(2)}, u32[]{:S(2)}) collective-permute-start(bf16[2,128,1024]{2,1,0:T(8,128)(2,1)} %get-tuple-element.57), channel_id=1, source_target_pairs={{0,2},{1,3},{8,10},{9,11},{16,18},{17,19},{24,26},{25,27}} | collective-permute-start | bytes 1572872 | tf_op jit(solution)/shard_map/ppermute | solution.py:561
  46.1 15.9 %collective-permute-start.16 = (f32[512,128]{1,0:T(8,128)}, f32[512,128]{1,0:T(8,128)}, u32[]{:S(2)}, u32[]{:S(2)}) collective-permute-start(f32[512,128]{1,0:T(8,128)} %get-tuple-element.65), channel_id=1, source_target_pairs={{0,1},{1,0},{2,3},{3,2},{4,5},{5,4},{6,7},{7,6},{8,9},{9,8},{10,11... | collective-permute-start | bytes 786440 | tf_op jit(solution)/shard_map/ppermute | solution.py:217
  46.6 29.8 %collective-permute-start.15 = (bf16[2176,128]{1,0:T(8,128)(2,1)}, bf16[2176,128]{1,0:T(8,128)(2,1)}, u32[]{:S(2)}, u32[]{:S(2)}) collective-permute-start(bf16[2176,128]{1,0:T(8,128)(2,1)} %get-tuple-element.56), channel_id=1, source_target_pairs={{5,7},{2,4},{3,6},{7,5},{4,2},{6,3},{13,15},{10,12},{11,14},{15,13... | collective-permute-start | bytes 1671176 | tf_op jit(solution)/shard_map/ppermute | solution.py:625
  55.6 13.6 %collective-permute-start.10 = (bf16[2,128,1024]{2,1,0:T(8,128)(2,1)}, bf16[2,128,1024]{2,1,0:T(8,128)(2,1)}, u32[]{:S(2)}, u32[]{:S(2)}) collective-permute-start(bf16[2,128,1024]{2,1,0:T(8,128)(2,1)} %get-tuple-element.54), channel_id=1, source_target_pairs={{0,2},{1,3},{8,10},{9,11},{16,18},{17,19},{24,26},{25,27}} | collective-permute-start | bytes 1572872 | tf_op jit(solution)/shard_map/ppermute | solution.py:561
  57.0 19.4 %collective-permute-start.14 = (bf16[2,128,1024]{2,1,0:T(8,128)(2,1)}, bf16[2,128,1024]{2,1,0:T(8,128)(2,1)}, u32[]{:S(2)}, u32[]{:S(2)}) collective-permute-start(bf16[2,128,1024]{2,1,0:T(8,128)(2,1)} %collective-permute-done.13.refs_5_), channel_id=1, source_target_pairs={{0,1},{1,0},{2,3},{3,2},{4,5},{5,4},{6,7},{7,6},{8,9},{9,8},{10,11... | collective-permute-start | bytes 1572872 | tf_op jit(solution)/shard_map/ppermute | solution.py:578
  63.9 17.1 %collective-permute-start.17 = (f32[512,128]{1,0:T(8,128)}, f32[512,128]{1,0:T(8,128)}, u32[]{:S(2)}, u32[]{:S(2)}) collective-permute-start(f32[512,128]{1,0:T(8,128)} %multiply_add_fusion.2), channel_id=1, source_target_pairs={{1,3},{3,5},{5,7},{9,11},{11,13},{13,15},{17,19},{19,21},{21,23},{... | collective-permute-start | bytes 786440 | tf_op jit(solution)/shard_map/ppermute | solution.py:223
  65.2 19.3 %collective-permute-start.12 = (bf16[2176,128]{1,0:T(8,128)(2,1)}, bf16[2176,128]{1,0:T(8,128)(2,1)}, u32[]{:S(2)}, u32[]{:S(2)}) collective-permute-start(bf16[2176,128]{1,0:T(8,128)(2,1)} %get-tuple-element.53), channel_id=1, source_target_pairs={{5,7},{2,4},{3,6},{7,5},{4,2},{6,3},{13,15},{10,12},{11,14},{15,13... | collective-permute-start | bytes 1671176 | tf_op jit(solution)/shard_map/ppermute | solution.py:625
  69.2 21.8 %collective-permute-start.11 = (bf16[2,128,1024]{2,1,0:T(8,128)(2,1)}, bf16[2,128,1024]{2,1,0:T(8,128)(2,1)}, u32[]{:S(2)}, u32[]{:S(2)}) collective-permute-start(bf16[2,128,1024]{2,1,0:T(8,128)(2,1)} %collective-permute-done.10.refs_5_), channel_id=1, source_target_pairs={{0,1},{1,0},{2,3},{3,2},{4,5},{5,4},{6,7},{7,6},{8,9},{9,8},{10,11... | collective-permute-start | bytes 1572872 | tf_op jit(solution)/shard_map/ppermute | solution.py:578
  79.8 15.9 %collective-permute-start.21 = (bf16[2176,128]{1,0:T(8,128)(2,1)}, bf16[2176,128]{1,0:T(8,128)(2,1)}, u32[]{:S(2)}, u32[]{:S(2)}) collective-permute-start(bf16[2176,128]{1,0:T(8,128)(2,1)} %get-tuple-element.73), channel_id=1, source_target_pairs={{5,7},{2,4},{3,6},{13,15},{10,12},{11,14},{21,23},{18,20},{19,22},... | collective-permute-start | bytes 1671176 | tf_op jit(solution)/shard_map/ppermute | solution.py:625
  82.9 27.7 %collective-permute-start.18 = (f32[512,128]{1,0:T(8,128)}, f32[512,128]{1,0:T(8,128)}, u32[]{:S(2)}, u32[]{:S(2)}) collective-permute-start(f32[512,128]{1,0:T(8,128)} %multiply_add_fusion.1), channel_id=1, source_target_pairs={{1,5},{3,7},{9,13},{11,15},{17,21},{19,23},{25,29},{27,31}} | collective-permute-start | bytes 786440 | tf_op jit(solution)/shard_map/ppermute | solution.py:223
  84.4 36.1 %collective-permute-start.24 = (bf16[2176,128]{1,0:T(8,128)(2,1)}, bf16[2176,128]{1,0:T(8,128)(2,1)}, u32[]{:S(2)}, u32[]{:S(2)}) collective-permute-start(bf16[2176,128]{1,0:T(8,128)(2,1)} %collective-permute-done.15.refs_7_.refs_0_), channel_id=1, source_target_pairs={{0,1},{1,0},{2,3},{3,2},{4,5},{5,4},{6,7},{7,6},{8,9},{9,8},{10,11... | collective-permute-start | bytes 1671176 | tf_op jit(solution)/shard_map/ppermute | solution.py:638
  84.5 38.7 %collective-permute-start.23 = (bf16[2176,128]{1,0:T(8,128)(2,1)}, bf16[2176,128]{1,0:T(8,128)(2,1)}, u32[]{:S(2)}, u32[]{:S(2)}) collective-permute-start(bf16[2176,128]{1,0:T(8,128)(2,1)} %collective-permute-done.12.refs_7_.refs_0_), channel_id=1, source_target_pairs={{0,1},{1,0},{2,3},{3,2},{4,5},{5,4},{6,7},{7,6},{8,9},{9,8},{10,11... | collective-permute-start | bytes 1671176 | tf_op jit(solution)/shard_map/ppermute | solution.py:638
  94.4 34.1 %collective-permute-start.20 = (bf16[2176,128]{1,0:T(8,128)(2,1)}, bf16[2176,128]{1,0:T(8,128)(2,1)}, u32[]{:S(2)}, u32[]{:S(2)}) collective-permute-start(bf16[2176,128]{1,0:T(8,128)(2,1)} %get-tuple-element.60), channel_id=1, source_target_pairs={{5,7},{2,4},{3,6},{13,15},{10,12},{11,14},{21,23},{18,20},{19,22},... | collective-permute-start | bytes 1671176 | tf_op jit(solution)/shard_map/ppermute | solution.py:625
  95.7 30.2 %collective-permute-start.22 = (bf16[2176,128]{1,0:T(8,128)(2,1)}, bf16[2176,128]{1,0:T(8,128)(2,1)}, u32[]{:S(2)}, u32[]{:S(2)}) collective-permute-start(bf16[2176,128]{1,0:T(8,128)(2,1)} %collective-permute-done.21.refs_0_), channel_id=1, source_target_pairs={{0,1},{1,0},{2,3},{3,2},{4,5},{5,4},{6,7},{7,6},{8,9},{9,8},{10,11... | collective-permute-start | bytes 1671176 | tf_op jit(solution)/shard_map/ppermute | solution.py:638
  111.8 0.7 copy-start
  112.5 1.7 %collective-permute-start.19 = (f32[512,128]{1,0:T(8,128)S(1)}, f32[512,128]{1,0:T(8,128)}, u32[]{:S(2)}, u32[]{:S(2)}) collective-permute-start(f32[512,128]{1,0:T(8,128)S(1)} %multiply_add_fusion.enter_ref), channel_id=1, source_target_pairs={{0,1},{1,0},{2,3},{3,2},{4,5},{5,4},{6,7},{7,6},{8,9},{9,8},{10,11... | collective-permute-start | bytes 786440 | tf_op jit(solution)/shard_map/ppermute | solution.py:231
  128.5 2.4 %collective-permute-start.25 = (bf16[2176,128]{1,0:T(8,128)(2,1)}, bf16[2176,128]{1,0:T(8,128)(2,1)}, u32[]{:S(2)}, u32[]{:S(2)}) collective-permute-start(bf16[2176,128]{1,0:T(8,128)(2,1)} %collective-permute-done.20.refs_0_), channel_id=1, source_target_pairs={{0,1},{1,0},{2,3},{3,2},{4,5},{5,4},{6,7},{7,6},{8,9},{9,8},{10,11... | collective-permute-start | bytes 1671176 | tf_op jit(solution)/shard_map/ppermute | solution.py:638

commit v7 on v6

--- a/solution.py
+++ b/solution.py
@@ -27,7 +27,7 @@
 
 def cost(microseconds):
     return pl.CostEstimate(
-        flops=microseconds * 10**8, bytes_accessed=2**16, transcendentals=0
+        flops=microseconds * 10**9, bytes_accessed=2**20, transcendentals=0
     )
 
 
@@ -172,7 +172,7 @@
     taps_spec = pl.BlockSpec((TAPS, TAPS, width), lambda group: (0, 0, group))
     positions = pltpu.VMEM((rows * SUBLANES, LANES), jnp.float32)
 
-    def first_part(token):
+    def first_part(token, state_token):
         own_par, rim = pl.pallas_call(
             conv_pack_kernel,
             grid=(1,),
@@ -190,8 +190,9 @@
             cost_estimate=cost(1),
             name="conv_pack",
         )(decay_rate.T, residue.T, hyena_q, hyena_k, hyena_v)
+        rim = after(rim, token)
         rim = lax.ppermute(rim, "ctx", [(index, index + 1) for index in range(devices - 1)])
-        own_par = after(own_par, rim, token)
+        own_par = after(own_par, rim)
         par = lax.all_to_all(own_par, "ctx", split_axis=0, concat_axis=0, tiled=True)
         par = par.reshape(devices * par_rows, LANES)
         state_spec = pl.BlockSpec((SUBLANES * modes, LANES), lambda group: (group, 0))
@@ -209,7 +210,7 @@
             compiler_params=params(),
             cost_estimate=cost(9),
             name="conv_state",
-        )(hyena_k, hyena_v, rim, par, short_filter)
+        )(hyena_k, hyena_v, after(rim, state_token), par, short_filter)
         return local_result, rim, par, decay, *entering_state(state, decay)
 
     def entering_state(state, decay):
@@ -287,14 +288,16 @@
     return mixed[:, :HEAD_DIM] / total, top + jnp.log2(total)
 
 
-def pack_kernel(gathers, askers, asked, widths, starts, q_ref, qs_ref, k_ref, v_ref, *rest):
-    count = len(widths)
-    key_outs, query_outs = rest[:count], rest[count : count + asked]
-    stages, in_sems, out_sems = rest[count + asked : -2], rest[-2], rest[-1]
+def pack_kernel(gathers, askers, key_cuts, query_cuts, q_ref, qs_ref, k_ref, v_ref, *rest):
+    count = len(key_cuts)
+    total = count + len(query_cuts)
+    key_outs, query_outs = rest[:count], rest[count:total]
+    key_stages, query_stages = rest[total : total + 2 * count], rest[total + 2 * count : -2]
+    in_sems, out_sems = rest[-2:]
     me = lax.axis_index("ctx")
     odd = me % 2
 
-    def run(pairs):
+    def run(pairs, stages):
         loads = [
             pltpu.make_async_copy(source, stage, in_sems.at[index])
             for index, ((source, _), stage) in enumerate(zip(pairs, stages))
@@ -311,30 +314,28 @@
         for store in stores:
             store.wait()
 
-    def cut(ref, chunk):
-        return ref.at[:, pl.ds(starts[chunk], widths[chunk])]
+    def cut(ref, columns):
+        return ref.at[:, pl.ds(*columns)]
 
     if gathers:
 
         @pl.when(among(me, gathers))
         def _():
-            run(
-                [
-                    (cut(ref, chunk), key_outs[chunk].at[which])
-                    for chunk in range(count)
-                    for which, ref in enumerate((k_ref, v_ref))
-                ]
-            )
+            pairs = [
+                (cut(ref, columns), out.at[which])
+                for columns, out in zip(key_cuts, key_outs)
+                for which, ref in enumerate((k_ref, v_ref))
+            ]
+            run(pairs, key_stages)
 
     @pl.when(among(me, askers))
     def _():
-        run(
-            [
-                (cut(ref, chunk), query_outs[chunk].at[half])
-                for chunk in range(asked)
-                for ref, half in ((q_ref, odd), (qs_ref, 1 - odd))
-            ]
-        )
+        pairs = [
+            (cut(ref, columns), out.at[half])
+            for columns, out in zip(query_cuts, query_outs)
+            for ref, half in ((q_ref, odd), (qs_ref, 1 - odd))
+        ]
+        run(pairs, query_stages)
 
 
 def as_rows(columns):
@@ -526,21 +527,26 @@
 
     def pack():
         hbm = pl.BlockSpec(memory_space=pl.ANY)
-        shapes = [jax.ShapeDtypeStruct((2, rows, width), jnp.bfloat16) for width in widths]
+        key_cuts = list(zip(starts, widths))
+        query_cuts = key_cuts[:asked]
         outs = pl.pallas_call(
             functools.partial(
                 pack_kernel,
                 [source for source, _ in gathers],
                 askers,
-                asked,
-                widths,
-                starts,
+                key_cuts,
+                query_cuts,
             ),
             in_specs=[hbm] * 4,
             out_specs=[hbm] * (chunks + asked),
-            out_shape=shapes + shapes[:asked],
+            out_shape=[
+                jax.ShapeDtypeStruct((2, rows, width), jnp.bfloat16)
+                for _, width in key_cuts + query_cuts
+            ],
             scratch_shapes=[
-                pltpu.VMEM((rows, width), jnp.bfloat16) for width in widths for _ in range(2)
+                pltpu.VMEM((rows, width), jnp.bfloat16)
+                for _, width in key_cuts + query_cuts
+                for _ in range(2)
             ]
             + [pltpu.SemaphoreType.DMA((2 * chunks,))] * 2,
             compiler_params=params(),
@@ -551,31 +557,61 @@
 
     key_packs, query_packs = pack()
     conv_first, conv_last = conv
-    local_result, *conv_shared = conv_first(query_packs[0])
     asks, quad_kv, all_answers = {}, [], []
-
-    def send(chunk):
+    for chunk in range(chunks):
         key_pack = key_packs[chunk]
-        if chunk >= LAG:
-            key_pack = after(key_pack, quad_kv[chunk - LAG][0], all_answers[chunk - LAG][0])
+        if chunk:
+            key_pack = after(key_pack, quad_kv[-1][0])
         quad_kv.append([lax.ppermute(key_pack, "ctx", gathers)])
-        if chunk < asked:
-            query_pack = query_packs[chunk]
-            if chunk >= LAG:
-                query_pack = after(query_pack, *asks[chunk - LAG], all_answers[chunk - LAG][0])
-            asks[chunk] = [lax.ppermute(query_pack, "ctx", pairs) for pairs in transfers]
+    for chunk in range(asked):
+        query_pack = query_packs[chunk]
+        if chunk:
+            query_pack = after(query_pack, *asks[chunk - 1])
+        asks[chunk] = [lax.ppermute(query_pack, "ctx", pairs) for pairs in transfers]
 
     half_rows = HEADS_PER_STEP * rows + TAIL
     hbm = pl.BlockSpec(memory_space=pl.ANY)
-    for chunk in range(min(LAG, chunks)):
-        send(chunk)
     result = None
     returned = []
+
+    def merged(result, chunk, *earlier):
+        own, lse, arrivals = returned[chunk]
+        parts = [own, lse]
+        for arrival in arrivals:
+            if earlier:
+                arrival = after(arrival, *earlier)
+            parts += [arrival, lax.ppermute(arrival, "ctx", swap)]
+        steps = CHUNK_STEPS[chunk]
+        count = 2 * len(transfers)
+        return pl.pallas_call(
+            functools.partial(merge_kernel, transfers, steps, starts[chunk]),
+            in_specs=[hbm] * (len(parts) + 1),
+            out_specs=hbm,
+            out_shape=jax.ShapeDtypeStruct((rows, columns), jnp.bfloat16),
+            input_output_aliases={len(parts): 0},
+            scratch_shapes=[
+                pltpu.VMEM((rows, widths[chunk]), jnp.float32),
+                pltpu.VMEM((SUBLANES * steps, LANES), jnp.float32),
+            ]
+            + [pltpu.VMEM((steps, half_rows, LANES), jnp.bfloat16)] * count
+            + [
+                pltpu.VMEM((rows, widths[chunk]), jnp.bfloat16),
+                pltpu.SemaphoreType.DMA((3 + count * steps,)),
+            ],
+            compiler_params=params(),
+            cost_estimate=cost(2),
+            name="att_merge",
+        )(*parts, result)
+
+    merged_count = 0
     for chunk in range(chunks):
-        if chunk == 0:
-            quad_kv[0] = [after(quad_kv[0][0], local_result)]
-            asks[0] = [after(asked, local_result) for asked in asks[0]]
-        quad_kv[chunk].append(lax.ppermute(quad_kv[chunk][0], "ctx", swap))
+        arrived = quad_kv[chunk][0]
+        if chunk:
+            arrived = after(arrived, all_answers[-1][0])
+        quad_kv[chunk] = [arrived, lax.ppermute(arrived, "ctx", swap)]
+        if chunk > LAG:
+            result = merged(result, merged_count)
+            merged_count += 1
         steps, first = CHUNK_STEPS[chunk], first_steps[chunk]
         whole_spec = pl.BlockSpec((rows, step_width), lambda step, first=first: (0, first + step))
         chunk_spec = pl.BlockSpec((rows, step_width), lambda step: (0, step))
@@ -616,7 +652,6 @@
             name="att_partial",
         )(*operands)
         all_answers.append(answers)
-        parts = [own, lse]
         arrivals = []
         for answer, pairs in zip(answers, transfers):
             moves = [(target, source) for source, target in pairs]
@@ -626,37 +661,13 @@
         if asking:
             asks[chunk + LAG] = arrivals
         returned.append([own, lse, arrivals])
-        if chunk + LAG < chunks:
-            send(chunk + LAG)
+        if chunk == 0:
+            local_result, *conv_shared = conv_first(query_packs[0], answers[0])
     conv_shared = [after(part, all_answers[-1][0]) for part in conv_shared]
     hyena_out = conv_last(local_result, *conv_shared)
-    for chunk, (own, lse, arrivals) in enumerate(returned):
-        parts = [own, lse]
-        for arrival in arrivals:
-            if chunk == chunks - 1:
-                arrival = after(arrival, hyena_out, result)
-            parts += [arrival, lax.ppermute(arrival, "ctx", swap)]
-        steps = CHUNK_STEPS[chunk]
-        count = 2 * len(transfers)
-        result = pl.pallas_call(
-            functools.partial(merge_kernel, transfers, steps, starts[chunk]),
-            in_specs=[hbm] * (len(parts) + 1),
-            out_specs=hbm,
-            out_shape=jax.ShapeDtypeStruct((rows, columns), jnp.bfloat16),
-            input_output_aliases={len(parts): 0},
-            scratch_shapes=[
-                pltpu.VMEM((rows, widths[chunk]), jnp.float32),
-                pltpu.VMEM((SUBLANES * steps, LANES), jnp.float32),
-            ]
-            + [pltpu.VMEM((steps, half_rows, LANES), jnp.bfloat16)] * count
-            + [
-                pltpu.VMEM((rows, widths[chunk]), jnp.bfloat16),
-                pltpu.SemaphoreType.DMA((3 + count * steps,)),
-            ],
-            compiler_params=params(),
-            cost_estimate=cost(2),
-            name="att_merge",
-        )(*parts, result)
+    for chunk in range(merged_count, chunks):
+        last = chunk == chunks - 1
+        result = merged(result, chunk, *((hyena_out, result) if last else ()))
     return hyena_out, result
 
 

time: 134 us -> 138 us (1.030)
  the two profiles are of different devices: /device:TPU:29 before, /device:TPU:17 now
where the time goes in v7:
time: 138 us; the launch traced here: 136 us
  Pallas kernels  47.9 us (35%)
  starting transfers between devices  47 us (34%)
  waiting for transfers between devices  34.9 us (25%)
  other arithmetic  4.72 us (3%)
    pallas_call x4, Pallas kernels, attend(): pl.pallas_call(functools.partial(partial_kernel, transfers, upper, natura...  19.2 us
    ppermute x2, waiting for transfers between devices, attend(): lax.ppermute(query_pack, 'ctx', pairs)  15.8 us
    ppermute x4, starting transfers between devices, attend(): arrivals.append(lax.ppermute(answer, 'ctx', moves))  11.6 us
    pallas_call x4, Pallas kernels, merged(): pl.pallas_call(functools.partial(merge_kernel, transfers, steps, starts[c...  10.6 us
    pallas_call x1, Pallas kernels, first_part(): pl.pallas_call(functools.partial(state_kernel, modes), grid=(groups,), in...  9.72 us
    all_to_all x1, starting transfers between devices, first_part(): lax.all_to_all(own_par, 'ctx', split_axis=0, concat_axis=0, tiled=True)  9.6 us
    ppermute x2, waiting for transfers between devices, entering_state(): arrived = lax.ppermute(total, 'ctx', moves)  9.27 us
    ppermute x4, starting transfers between devices, attend(): quad_kv[chunk] = [arrived, lax.ppermute(arrived, 'ctx', swap)]  6.85 us
  transfers between devices with their start and end apart: 27, of which 7 were waited for; matrix products, arithmetic and copies ran while one was open for 3% of the time, Pallas kernels for 33%

profile of v7, /device:TPU:17, one launch (start us, length us, event | category | flops | bytes accessed | tf_op | source)
XLA Modules:
  0.0 136.3 jit_solution(10796933125159077407)
XLA Ops:
  0.6 0.7 collective-permute-start
  1.4 0.1 collective-permute-start.2
  1.5 0.4 collective-permute-start.3
  1.9 2.1 %collective-permute-done.qs_ref.refs_9_ = bf16[128,4096]{1,0:T(8,128)(2,1)} collective-permute-done((bf16[128,4096]{1,0:T(8,128)(2,1)}, bf16[128,4096]{1,0:T(8,128)(2,1)}, u32[]{:S(2)}, u32[]{:S(2)}) %collective-permute-start) | collective-permute-done | bytes 1048608 | tf_op jit(solution)/shard_map/ppermute | solution.py:518
  4.0 0.1 att_pack.1
  4.2 1.5 %collective-permute-start.4 = (bf16[2,128,1024]{2,1,0:T(8,128)(2,1)}, bf16[2,128,1024]{2,1,0:T(8,128)(2,1)}, u32[]{:S(2)}, u32[]{:S(2)}) collective-permute-start(bf16[2,128,1024]{2,1,0:T(8,128)(2,1)} %get-tuple-element.49), channel_id=1, source_target_pairs={{0,2},{1,3},{8,10},{9,11},{16,18},{17,19},{24,26},{25,27}} | collective-permute-start | bytes 1572872 | tf_op jit(solution)/shard_map/ppermute | solution.py:565
  5.6 2.0 %conv_pack.1 = (f32[8,128,128]{2,1,0:T(8,128)}, f32[8,4096]{1,0:T(8,128)}) custom-call(f32[16,512]{1,0:T(8,128)} %bitcast.3, f32[16,512]{1,0:T(8,128)} %bitcast.4, bf16[128,4096]{1,0:T(8,128)(2,1)} %q_ref.5, bf16[128,4096]{1,0:T(8,128)(2,1)} %k_ref.5, bf16[128,4096]{1,0:T(8,128)(2,1)} %v_ref.5), custom_call_target="tpu_custom_call" | custom-call | flops 1000000000 | bytes 1048576 | tf_op jit(solution)/shard_map/conv_pack/pallas_call | solution.py:176
  7.6 5.4 %collective-permute-start.1 = (f32[8,4096]{1,0:T(8,128)}, f32[8,4096]{1,0:T(8,128)S(1)}, u32[]{:S(2)}, u32[]{:S(2)}) collective-permute-start(f32[8,4096]{1,0:T(8,128)} %get-tuple-element.48), channel_id=1, source_target_pairs={{0,1},{1,2},{2,3},{3,4},{4,5},{5,6},{6,7},{8,9},{9,10},{10,11},{11... | collective-permute-start | bytes 393224 | tf_op jit(solution)/shard_map/ppermute | solution.py:194
  13.0 2.2 %collective-permute-done.1.rim_ref = f32[8,4096]{1,0:T(8,128)S(1)} collective-permute-done((f32[8,4096]{1,0:T(8,128)}, f32[8,4096]{1,0:T(8,128)S(1)}, u32[]{:S(2)}, u32[]{:S(2)}) %collective-permute-start.1) | collective-permute-done | bytes 131104 | tf_op jit(solution)/shard_map/ppermute | solution.py:194
  15.2 9.6 %all-to-all-start = ((f32[8,128,128]{2,1,0:T(8,128)}), f32[8,128,128]{2,1,0:T(8,128)}, u32[]{:S(2)}, u32[]{:S(2)}) async-start(f32[8,128,128]{2,1,0:T(8,128)} %get-tuple-element.53), calls=%async_computation | async-start | bytes 1048576 | tf_op jit(solution)/shard_map/all_to_all | solution.py:196
  24.8 1.3 collective-permute-start.6
  26.1 0.0 collective-permute-done.4.refs_5_
  26.1 3.1 %collective-permute-start.5 = (bf16[2,128,1024]{2,1,0:T(8,128)(2,1)}, bf16[2,128,1024]{2,1,0:T(8,128)(2,1)}, u32[]{:S(2)}, u32[]{:S(2)}) collective-permute-start(bf16[2,128,1024]{2,1,0:T(8,128)(2,1)} %collective-permute-done.4.refs_5_), channel_id=1, source_target_pairs={{0,1},{1,0},{2,3},{3,2},{4,5},{5,4},{6,7},{7,6},{8,9},{9,8},{10,11... | collective-permute-start | bytes 1572872 | tf_op jit(solution)/shard_map/ppermute | solution.py:611
  29.3 1.5 %collective-permute-start.7 = (bf16[2,128,1024]{2,1,0:T(8,128)(2,1)}, bf16[2,128,1024]{2,1,0:T(8,128)(2,1)}, u32[]{:S(2)}, u32[]{:S(2)}) collective-permute-start(bf16[2,128,1024]{2,1,0:T(8,128)(2,1)} %get-tuple-element.58), channel_id=1, source_target_pairs={{0,2},{1,3},{8,10},{9,11},{16,18},{17,19},{24,26},{25,27}} | collective-permute-start | bytes 1572872 | tf_op jit(solution)/shard_map/ppermute | solution.py:565
  30.7 15.8 %collective-permute-done.6.refs_7_ = bf16[2,128,1024]{2,1,0:T(8,128)(2,1)} collective-permute-done((bf16[2,128,1024]{2,1,0:T(8,128)(2,1)}, bf16[2,128,1024]{2,1,0:T(8,128)(2,1)}, u32[]{:S(2)}, u32[]{:S(2)}) %collective-permute-start.6) | collective-permute-done | bytes 524320 | tf_op jit(solution)/shard_map/ppermute | solution.py:570
  46.5 1.3 collective-permute-start.11
  47.9 4.8 %att_partial.4 = (f32[128,1024]{1,0:T(8,128)}, f32[16,128]{1,0:T(8,128)}, bf16[2176,128]{1,0:T(8,128)(2,1)}, bf16[128,4096]{1,0:T(8,128)(2,1)}) custom-call(bf16[128,4096]{1,0:T(8,128)(2,1)} %refs_0_.7, bf16[128,4096]{1,0:T(8,128)(2,1)} %refs_1_.7, bf16[128,4096]{1,0:T(8,128)(2,1)} %refs_2_.7, bf16[128,4096]{1,0:T(8,128)(2,1)} %collective-permute-done.2.refs_3_, ...), custom_call_target="tpu_custom_call" | custom-call | flops 4000000000 | bytes 1048576 | tf_op jit(solution)/shard_map/att_partial/pallas_call | solution.py:638
  52.7 3.5 %collective-permute-start.13 = (bf16[2176,128]{1,0:T(8,128)(2,1)}, bf16[2176,128]{1,0:T(8,128)(2,1)}, u32[]{:S(2)}, u32[]{:S(2)}) collective-permute-start(bf16[2176,128]{1,0:T(8,128)(2,1)} %get-tuple-element.50), channel_id=1, source_target_pairs={{5,7},{2,4},{3,6},{7,5},{4,2},{6,3},{13,15},{10,12},{11,14},{15,13... | collective-permute-start | bytes 1671176 | tf_op jit(solution)/shard_map/ppermute | solution.py:660
  56.2 3.6 %collective-permute-start.10 = (bf16[2,128,1024]{2,1,0:T(8,128)(2,1)}, bf16[2,128,1024]{2,1,0:T(8,128)(2,1)}, u32[]{:S(2)}, u32[]{:S(2)}) collective-permute-start(bf16[2,128,1024]{2,1,0:T(8,128)(2,1)} %collective-permute-done.7.refs_5_), channel_id=1, source_target_pairs={{0,1},{1,0},{2,3},{3,2},{4,5},{5,4},{6,7},{7,6},{8,9},{9,8},{10,11... | collective-permute-start | bytes 1572872 | tf_op jit(solution)/shard_map/ppermute | solution.py:611
  59.8 1.5 %collective-permute-start.8 = (bf16[2,128,1024]{2,1,0:T(8,128)(2,1)}, bf16[2,128,1024]{2,1,0:T(8,128)(2,1)}, u32[]{:S(2)}, u32[]{:S(2)}) collective-permute-start(bf16[2,128,1024]{2,1,0:T(8,128)(2,1)} %get-tuple-element.59), channel_id=1, source_target_pairs={{0,2},{1,3},{8,10},{9,11},{16,18},{17,19},{24,26},{25,27}} | collective-permute-start | bytes 1572872 | tf_op jit(solution)/shard_map/ppermute | solution.py:565
  61.3 9.7 %conv_state.1 = (f32[128,4096]{1,0:T(8,128)}, f32[512,128]{1,0:T(8,128)}, f32[512,128]{1,0:T(8,128)}) custom-call(bf16[128,4096]{1,0:T(8,128)(2,1)} %k_ref.5, bf16[128,4096]{1,0:T(8,128)(2,1)} %v_ref.5, f32[8,4096]{1,0:T(8,128)} %copy-done.1, f32[1024,128]{1,0:T(8,128)} %bitcast.2.par_ref, f32[3,3,4096]{2,1,0:T(4,128)} %taps_ref.3), custom_call_target="tpu_custom_call" | custom-call | flops 8999999488 | bytes 1048576 | tf_op jit(solution)/shard_map/conv_state/pallas_call | solution.py:199
  71.0 0.0 collective-permute-start.17
  71.0 4.9 %att_partial.5 = (f32[128,1024]{1,0:T(8,128)}, f32[16,128]{1,0:T(8,128)}, bf16[2176,128]{1,0:T(8,128)(2,1)}, bf16[128,4096]{1,0:T(8,128)(2,1)}) custom-call(bf16[128,4096]{1,0:T(8,128)(2,1)} %refs_0_.7, bf16[128,4096]{1,0:T(8,128)(2,1)} %refs_1_.7, bf16[128,4096]{1,0:T(8,128)(2,1)} %refs_2_.7, ...), custom_call_target="tpu_custom_call", output_to_operand_aliasing={{3}: (10, {})} | custom-call | flops 4000000000 | bytes 1048576 | tf_op jit(solution)/shard_map/att_partial/pallas_call | solution.py:638
  75.9 0.1 collective-permute-start.12
  76.0 1.2 multiply_add_fusion.2
  77.1 1.9 %collective-permute-start.18 = (f32[512,128]{1,0:T(8,128)S(1)}, f32[512,128]{1,0:T(8,128)S(1)}, u32[]{:S(2)}, u32[]{:S(2)}) collective-permute-start(f32[512,128]{1,0:T(8,128)S(1)} %multiply_add_fusion.2), channel_id=1, source_target_pairs={{1,3},{3,5},{5,7},{9,11},{11,13},{13,15},{17,19},{19,21},{21,23},{... | collective-permute-start | bytes 786440 | tf_op jit(solution)/shard_map/ppermute | solution.py:224
  79.1 1.5 %collective-permute-start.9 = (bf16[2,128,1024]{2,1,0:T(8,128)(2,1)}, bf16[2,128,1024]{2,1,0:T(8,128)(2,1)}, u32[]{:S(2)}, u32[]{:S(2)}) collective-permute-start(bf16[2,128,1024]{2,1,0:T(8,128)(2,1)} %get-tuple-element.60), channel_id=1, source_target_pairs={{0,2},{1,3},{8,10},{9,11},{16,18},{17,19},{24,26},{25,27}} | collective-permute-start | bytes 1572872 | tf_op jit(solution)/shard_map/ppermute | solution.py:565
  80.5 4.4 %collective-permute-done.18 = f32[512,128]{1,0:T(8,128)S(1)} collective-permute-done((f32[512,128]{1,0:T(8,128)S(1)}, f32[512,128]{1,0:T(8,128)S(1)}, u32[]{:S(2)}, u32[]{:S(2)}) %collective-permute-start.18) | collective-permute-done | bytes 262176 | tf_op jit(solution)/shard_map/ppermute | solution.py:224
  85.0 0.7 copy-done
  85.7 1.7 %multiply_add_fusion.1 = f32[512,128]{1,0:T(8,128)} fusion(f32[512,128]{1,0:T(8,128)S(1)} %multiply_add_fusion.2, f32[512,128]{1,0:T(8,128)S(1)} %collective-permute-done.18, f32[512,128]{1,0:T(8,128)} %get-tuple-element.77.decay_ref), kind=kLoop, calls=%fused_computation.1 | loop fusion | flops 196608 | bytes 1048576 | tf_op jit(solution)/shard_map/add | solution.py:230
  87.4 1.3 collective-permute-start.19
  88.7 1.9 %collective-permute-start.15 = (bf16[2176,128]{1,0:T(8,128)(2,1)}, bf16[2176,128]{1,0:T(8,128)(2,1)}, u32[]{:S(2)}, u32[]{:S(2)}) collective-permute-start(bf16[2176,128]{1,0:T(8,128)(2,1)} %get-tuple-element.65), channel_id=1, source_target_pairs={{5,7},{2,4},{3,6},{7,5},{4,2},{6,3},{13,15},{10,12},{11,14},{15,13... | collective-permute-start | bytes 1671176 | tf_op jit(solution)/shard_map/ppermute | solution.py:660
  90.6 0.1 collective-permute-start.16
  90.7 4.8 %att_partial.6 = (f32[128,1024]{1,0:T(8,128)}, f32[16,128]{1,0:T(8,128)}, bf16[2176,128]{1,0:T(8,128)(2,1)}, bf16[128,4096]{1,0:T(8,128)(2,1)}) custom-call(bf16[128,4096]{1,0:T(8,128)(2,1)} %refs_0_.7, bf16[128,4096]{1,0:T(8,128)(2,1)} %refs_1_.7, bf16[128,4096]{1,0:T(8,128)(2,1)} %refs_2_.7, ...), custom_call_target="tpu_custom_call", output_to_operand_aliasing={{3}: (8, {})} | custom-call | flops 4000000000 | bytes 1048576 | tf_op jit(solution)/shard_map/att_partial/pallas_call | solution.py:638
  95.5 0.1 collective-permute-start.14
  95.6 4.8 %collective-permute-done.19 = f32[512,128]{1,0:T(8,128)} collective-permute-done((f32[512,128]{1,0:T(8,128)}, f32[512,128]{1,0:T(8,128)}, u32[]{:S(2)}, u32[]{:S(2)}) %collective-permute-start.19) | collective-permute-done | bytes 262176 | tf_op jit(solution)/shard_map/ppermute | solution.py:224
  100.4 1.8 %multiply_add_fusion.enter_ref = f32[512,128]{1,0:T(8,128)} fusion(f32[512,128]{1,0:T(8,128)} %copy-done, f32[512,128]{1,0:T(8,128)} %collective-permute-done.19, f32[512,128]{1,0:T(8,128)} %get-tuple-element.77.decay_ref), kind=kLoop, calls=%fused_computation | loop fusion | flops 196608 | bytes 1048576 | tf_op jit(solution)/shard_map/add | solution.py:228
  102.3 2.4 %collective-permute-start.22 = (bf16[2176,128]{1,0:T(8,128)(2,1)}, bf16[2176,128]{1,0:T(8,128)(2,1)}, u32[]{:S(2)}, u32[]{:S(2)}) collective-permute-start(bf16[2176,128]{1,0:T(8,128)(2,1)} %get-tuple-element.68), channel_id=1, source_target_pairs={{5,7},{2,4},{3,6},{13,15},{10,12},{11,14},{21,23},{18,20},{19,22},... | collective-permute-start | bytes 1671176 | tf_op jit(solution)/shard_map/ppermute | solution.py:660
  104.7 3.5 %collective-permute-done.15.refs_7_.refs_0_ = bf16[2176,128]{1,0:T(8,128)(2,1)} collective-permute-done((bf16[2176,128]{1,0:T(8,128)(2,1)}, bf16[2176,128]{1,0:T(8,128)(2,1)}, u32[]{:S(2)}, u32[]{:S(2)}) %collective-permute-start.15) | collective-permute-done | bytes 557088 | tf_op jit(solution)/shard_map/ppermute | solution.py:660
  108.2 2.6 %att_merge.4.refs_8_ = bf16[128,4096]{1,0:T(8,128)(2,1)} custom-call(f32[128,1024]{1,0:T(8,128)} %get-tuple-element.70.own_hbm, f32[16,128]{1,0:T(8,128)} %get-tuple-element.71.lse_hbm, bf16[2176,128]{1,0:T(8,128)(2,1)} %collective-permute-done.13.refs_7_.refs_0_, bf16[2176,128]{1,0:T(8,128)(2,1)} %collective-permute-done.16.refs_1_, ...), custom_call_target="tpu_custom_call", output_to_operand_aliasing={{}: (4, {})} | custom-call | flops 2000000000 | bytes 1048576 | tf_op jit(solution)/shard_map/att_merge/pallas_call | solution.py:586
  110.9 4.8 %att_partial.7 = (f32[128,1024]{1,0:T(8,128)}, f32[16,128]{1,0:T(8,128)}, bf16[2176,128]{1,0:T(8,128)(2,1)}, bf16[128,4096]{1,0:T(8,128)(2,1)}) custom-call(bf16[128,4096]{1,0:T(8,128)(2,1)} %refs_0_.7, bf16[128,4096]{1,0:T(8,128)(2,1)} %refs_1_.7, bf16[128,4096]{1,0:T(8,128)(2,1)} %refs_2_.7, ...), custom_call_target="tpu_custom_call", output_to_operand_aliasing={{3}: (8, {})} | custom-call | flops 4000000000 | bytes 1048576 | tf_op jit(solution)/shard_map/att_partial/pallas_call | solution.py:638
  115.7 3.7 %collective-permute-start.21 = (bf16[2176,128]{1,0:T(8,128)(2,1)}, bf16[2176,128]{1,0:T(8,128)(2,1)}, u32[]{:S(2)}, u32[]{:S(2)}) collective-permute-start(bf16[2176,128]{1,0:T(8,128)(2,1)} %get-tuple-element.73), channel_id=1, source_target_pairs={{5,7},{2,4},{3,6},{13,15},{10,12},{11,14},{21,23},{18,20},{19,22},... | collective-permute-start | bytes 1671176 | tf_op jit(solution)/shard_map/ppermute | solution.py:660
  119.4 6.3 %conv_output.1 = bf16[128,4096]{1,0:T(8,128)(2,1)} custom-call(bf16[128,4096]{1,0:T(8,128)(2,1)} %q_ref.5, f32[128,4096]{1,0:T(8,128)} %get-tuple-element.54.y_ref, f32[8,4096]{1,0:T(8,128)} %copy-done.1, f32[1024,128]{1,0:T(8,128)} %bitcast.2.par_ref, f32[512,128]{1,0:T(8,128)} %get-tuple-element.77.decay_ref, f32[512,128]{1,0:T(8,128)} %multiply_add_fusion.enter_ref, ...), custom_call_target="tpu_custom_call" | custom-call | flops 6000000000 | bytes 1048576 | tf_op jit(solution)/shard_map/conv_output/pallas_call | solution.py:236
  125.7 2.7 %att_merge.5.refs_2_ = bf16[128,4096]{1,0:T(8,128)(2,1)} custom-call(f32[128,1024]{1,0:T(8,128)} %get-tuple-element.86.own_hbm, f32[16,128]{1,0:T(8,128)} %get-tuple-element.87.lse_hbm, bf16[2176,128]{1,0:T(8,128)(2,1)} %collective-permute-done.15.refs_7_.refs_0_, bf16[2176,128]{1,0:T(8,128)(2,1)} %collective-permute-done.24.refs_1_, ...), custom_call_target="tpu_custom_call", output_to_operand_aliasing={{}: (4, {})} | custom-call | flops 2000000000 | bytes 1048576 | tf_op jit(solution)/shard_map/att_merge/pallas_call | solution.py:586
  128.4 2.7 %att_merge.6.refs_2_ = bf16[128,4096]{1,0:T(8,128)(2,1)} custom-call(f32[128,1024]{1,0:T(8,128)} %get-tuple-element.84.own_hbm, f32[16,128]{1,0:T(8,128)} %get-tuple-element.85.lse_hbm, bf16[2176,128]{1,0:T(8,128)(2,1)} %collective-permute-done.22.refs_0_, bf16[2176,128]{1,0:T(8,128)(2,1)} %collective-permute-done.23.refs_1_, ...), custom_call_target="tpu_custom_call", output_to_operand_aliasing={{}: (4, {})} | custom-call | flops 2000000000 | bytes 1048576 | tf_op jit(solution)/shard_map/att_merge/pallas_call | solution.py:586
  131.0 0.6 collective-permute-start.25
  131.6 1.9 %collective-permute-done.25.refs_1_ = bf16[2176,128]{1,0:T(8,128)(2,1)} collective-permute-done((bf16[2176,128]{1,0:T(8,128)(2,1)}, bf16[2176,128]{1,0:T(8,128)(2,1)}, u32[]{:S(2)}, u32[]{:S(2)}) %collective-permute-start.25) | collective-permute-done | bytes 557088 | tf_op jit(solution)/shard_map/ppermute | solution.py:583
  133.5 2.6 %att_merge.7 = bf16[128,4096]{1,0:T(8,128)(2,1)} custom-call(f32[128,1024]{1,0:T(8,128)} %get-tuple-element.82.own_hbm, f32[16,128]{1,0:T(8,128)} %get-tuple-element.83.lse_hbm, bf16[2176,128]{1,0:T(8,128)(2,1)} %collective-permute-done.21.refs_0_, bf16[2176,128]{1,0:T(8,128)(2,1)} %collective-permute-done.25.refs_1_, ...), custom_call_target="tpu_custom_call", output_to_operand_aliasing={{}: (4, {})} | custom-call | flops 2000000000 | bytes 1048576 | tf_op jit(solution)/shard_map/att_merge/pallas_call | solution.py:586
  (25 shorter events, 0.1 us)
Async XLA Ops:
  0.6 3.4 %collective-permute-start = (bf16[128,4096]{1,0:T(8,128)(2,1)}, bf16[128,4096]{1,0:T(8,128)(2,1)}, u32[]{:S(2)}, u32[]{:S(2)}) collective-permute-start(bf16[128,4096]{1,0:T(8,128)(2,1)} %refs_0_.7), channel_id=1, source_target_pairs={{0,1},{1,0},{2,3},{3,2},{4,5},{5,4},{6,7},{7,6},{8,9},{9,8},{10,11... | collective-permute-start | bytes 3145736 | tf_op jit(solution)/shard_map/ppermute | solution.py:518
  1.4 46.5 %collective-permute-start.2 = (bf16[128,4096]{1,0:T(8,128)(2,1)}, bf16[128,4096]{1,0:T(8,128)(2,1)}, u32[]{:S(2)}, u32[]{:S(2)}) collective-permute-start(bf16[128,4096]{1,0:T(8,128)(2,1)} %refs_1_.7), channel_id=1, source_target_pairs={{0,1},{1,0},{2,3},{3,2},{4,5},{5,4},{6,7},{7,6},{8,9},{9,8},{10,11... | collective-permute-start | bytes 3145736 | tf_op jit(solution)/shard_map/ppermute | solution.py:519
  1.5 46.4 %collective-permute-start.3 = (bf16[128,4096]{1,0:T(8,128)(2,1)}, bf16[128,4096]{1,0:T(8,128)(2,1)}, u32[]{:S(2)}, u32[]{:S(2)}) collective-permute-start(bf16[128,4096]{1,0:T(8,128)(2,1)} %refs_2_.7), channel_id=1, source_target_pairs={{0,1},{1,0},{2,3},{3,2},{4,5},{5,4},{6,7},{7,6},{8,9},{9,8},{10,11... | collective-permute-start | bytes 3145736 | tf_op jit(solution)/shard_map/ppermute | solution.py:520
  4.2 22.0 %collective-permute-start.4 = (bf16[2,128,1024]{2,1,0:T(8,128)(2,1)}, bf16[2,128,1024]{2,1,0:T(8,128)(2,1)}, u32[]{:S(2)}, u32[]{:S(2)}) collective-permute-start(bf16[2,128,1024]{2,1,0:T(8,128)(2,1)} %get-tuple-element.49), channel_id=1, source_target_pairs={{0,2},{1,3},{8,10},{9,11},{16,18},{17,19},{24,26},{25,27}} | collective-permute-start | bytes 1572872 | tf_op jit(solution)/shard_map/ppermute | solution.py:565
  7.6 7.6 %collective-permute-start.1 = (f32[8,4096]{1,0:T(8,128)}, f32[8,4096]{1,0:T(8,128)S(1)}, u32[]{:S(2)}, u32[]{:S(2)}) collective-permute-start(f32[8,4096]{1,0:T(8,128)} %get-tuple-element.48), channel_id=1, source_target_pairs={{0,1},{1,2},{2,3},{3,4},{4,5},{5,6},{6,7},{8,9},{9,10},{10,11},{11... | collective-permute-start | bytes 393224 | tf_op jit(solution)/shard_map/ppermute | solution.py:194
  15.2 37.5 %copy-start.1 = (f32[8,4096]{1,0:T(8,128)}, f32[8,4096]{1,0:T(8,128)S(1)}, u32[]{:S(2)}) copy-start(f32[8,4096]{1,0:T(8,128)S(1)} %collective-permute-done.1.rim_ref) | copy-start | bytes 393220
  15.2 46.0 %all-to-all-start = ((f32[8,128,128]{2,1,0:T(8,128)}), f32[8,128,128]{2,1,0:T(8,128)}, u32[]{:S(2)}, u32[]{:S(2)}) async-start(f32[8,128,128]{2,1,0:T(8,128)} %get-tuple-element.53), calls=%async_computation | async-start | bytes 1048576 | tf_op jit(solution)/shard_map/all_to_all | solution.py:196
  24.8 21.7 %collective-permute-start.6 = (bf16[2,128,1024]{2,1,0:T(8,128)(2,1)}, bf16[2,128,1024]{2,1,0:T(8,128)(2,1)}, u32[]{:S(2)}, u32[]{:S(2)}) collective-permute-start(bf16[2,128,1024]{2,1,0:T(8,128)(2,1)} %get-tuple-element.47), channel_id=1, source_target_pairs={{7,5},{4,2},{6,3},{15,13},{12,10},{14,11},{23,21},{20,18},{22,19},... | collective-permute-start | bytes 1572872 | tf_op jit(solution)/shard_map/ppermute | solution.py:570
  26.1 21.7 %collective-permute-start.5 = (bf16[2,128,1024]{2,1,0:T(8,128)(2,1)}, bf16[2,128,1024]{2,1,0:T(8,128)(2,1)}, u32[]{:S(2)}, u32[]{:S(2)}) collective-permute-start(bf16[2,128,1024]{2,1,0:T(8,128)(2,1)} %collective-permute-done.4.refs_5_), channel_id=1, source_target_pairs={{0,1},{1,0},{2,3},{3,2},{4,5},{5,4},{6,7},{7,6},{8,9},{9,8},{10,11... | collective-permute-start | bytes 1572872 | tf_op jit(solution)/shard_map/ppermute | solution.py:611
  29.3 27.0 %collective-permute-start.7 = (bf16[2,128,1024]{2,1,0:T(8,128)(2,1)}, bf16[2,128,1024]{2,1,0:T(8,128)(2,1)}, u32[]{:S(2)}, u32[]{:S(2)}) collective-permute-start(bf16[2,128,1024]{2,1,0:T(8,128)(2,1)} %get-tuple-element.58), channel_id=1, source_target_pairs={{0,2},{1,3},{8,10},{9,11},{16,18},{17,19},{24,26},{25,27}} | collective-permute-start | bytes 1572872 | tf_op jit(solution)/shard_map/ppermute | solution.py:565
  46.5 24.5 %collective-permute-start.11 = (bf16[2,128,1024]{2,1,0:T(8,128)(2,1)}, bf16[2,128,1024]{2,1,0:T(8,128)(2,1)}, u32[]{:S(2)}, u32[]{:S(2)}) collective-permute-start(bf16[2,128,1024]{2,1,0:T(8,128)(2,1)} %get-tuple-element.63), channel_id=1, source_target_pairs={{7,5},{4,2},{6,3},{15,13},{12,10},{14,11},{23,21},{20,18},{22,19},... | collective-permute-start | bytes 1572872 | tf_op jit(solution)/shard_map/ppermute | solution.py:570
  52.7 37.9 %collective-permute-start.13 = (bf16[2176,128]{1,0:T(8,128)(2,1)}, bf16[2176,128]{1,0:T(8,128)(2,1)}, u32[]{:S(2)}, u32[]{:S(2)}) collective-permute-start(bf16[2176,128]{1,0:T(8,128)(2,1)} %get-tuple-element.50), channel_id=1, source_target_pairs={{5,7},{2,4},{3,6},{7,5},{4,2},{6,3},{13,15},{10,12},{11,14},{15,13... | collective-permute-start | bytes 1671176 | tf_op jit(solution)/shard_map/ppermute | solution.py:660
  56.2 14.8 %collective-permute-start.10 = (bf16[2,128,1024]{2,1,0:T(8,128)(2,1)}, bf16[2,128,1024]{2,1,0:T(8,128)(2,1)}, u32[]{:S(2)}, u32[]{:S(2)}) collective-permute-start(bf16[2,128,1024]{2,1,0:T(8,128)(2,1)} %collective-permute-done.7.refs_5_), channel_id=1, source_target_pairs={{0,1},{1,0},{2,3},{3,2},{4,5},{5,4},{6,7},{7,6},{8,9},{9,8},{10,11... | collective-permute-start | bytes 1572872 | tf_op jit(solution)/shard_map/ppermute | solution.py:611
  59.8 16.1 %collective-permute-start.8 = (bf16[2,128,1024]{2,1,0:T(8,128)(2,1)}, bf16[2,128,1024]{2,1,0:T(8,128)(2,1)}, u32[]{:S(2)}, u32[]{:S(2)}) collective-permute-start(bf16[2,128,1024]{2,1,0:T(8,128)(2,1)} %get-tuple-element.59), channel_id=1, source_target_pairs={{0,2},{1,3},{8,10},{9,11},{16,18},{17,19},{24,26},{25,27}} | collective-permute-start | bytes 1572872 | tf_op jit(solution)/shard_map/ppermute | solution.py:565
  71.0 5.0 %collective-permute-start.17 = (f32[512,128]{1,0:T(8,128)}, f32[512,128]{1,0:T(8,128)}, u32[]{:S(2)}, u32[]{:S(2)}) collective-permute-start(f32[512,128]{1,0:T(8,128)} %get-tuple-element.78), channel_id=1, source_target_pairs={{0,1},{1,0},{2,3},{3,2},{4,5},{5,4},{6,7},{7,6},{8,9},{9,8},{10,11... | collective-permute-start | bytes 786440 | tf_op jit(solution)/shard_map/ppermute | solution.py:218
  75.9 14.8 %collective-permute-start.12 = (bf16[2,128,1024]{2,1,0:T(8,128)(2,1)}, bf16[2,128,1024]{2,1,0:T(8,128)(2,1)}, u32[]{:S(2)}, u32[]{:S(2)}) collective-permute-start(bf16[2,128,1024]{2,1,0:T(8,128)(2,1)} %collective-permute-done.8.refs_5_), channel_id=1, source_target_pairs={{0,1},{1,0},{2,3},{3,2},{4,5},{5,4},{6,7},{7,6},{8,9},{9,8},{10,11... | collective-permute-start | bytes 1572872 | tf_op jit(solution)/shard_map/ppermute | solution.py:611
  77.1 7.8 %collective-permute-start.18 = (f32[512,128]{1,0:T(8,128)S(1)}, f32[512,128]{1,0:T(8,128)S(1)}, u32[]{:S(2)}, u32[]{:S(2)}) collective-permute-start(f32[512,128]{1,0:T(8,128)S(1)} %multiply_add_fusion.2), channel_id=1, source_target_pairs={{1,3},{3,5},{5,7},{9,11},{11,13},{13,15},{17,19},{19,21},{21,23},{... | collective-permute-start | bytes 786440 | tf_op jit(solution)/shard_map/ppermute | solution.py:224
  79.1 16.4 %collective-permute-start.9 = (bf16[2,128,1024]{2,1,0:T(8,128)(2,1)}, bf16[2,128,1024]{2,1,0:T(8,128)(2,1)}, u32[]{:S(2)}, u32[]{:S(2)}) collective-permute-start(bf16[2,128,1024]{2,1,0:T(8,128)(2,1)} %get-tuple-element.60), channel_id=1, source_target_pairs={{0,2},{1,3},{8,10},{9,11},{16,18},{17,19},{24,26},{25,27}} | collective-permute-start | bytes 1572872 | tf_op jit(solution)/shard_map/ppermute | solution.py:565
  85.0 0.7 copy-start
  87.4 13.0 %collective-permute-start.19 = (f32[512,128]{1,0:T(8,128)}, f32[512,128]{1,0:T(8,128)}, u32[]{:S(2)}, u32[]{:S(2)}) collective-permute-start(f32[512,128]{1,0:T(8,128)} %multiply_add_fusion.1), channel_id=1, source_target_pairs={{1,5},{3,7},{9,13},{11,15},{17,21},{19,23},{25,29},{27,31}} | collective-permute-start | bytes 786440 | tf_op jit(solution)/shard_map/ppermute | solution.py:224
  88.7 19.5 %collective-permute-start.15 = (bf16[2176,128]{1,0:T(8,128)(2,1)}, bf16[2176,128]{1,0:T(8,128)(2,1)}, u32[]{:S(2)}, u32[]{:S(2)}) collective-permute-start(bf16[2176,128]{1,0:T(8,128)(2,1)} %get-tuple-element.65), channel_id=1, source_target_pairs={{5,7},{2,4},{3,6},{7,5},{4,2},{6,3},{13,15},{10,12},{11,14},{15,13... | collective-permute-start | bytes 1671176 | tf_op jit(solution)/shard_map/ppermute | solution.py:660
  90.6 17.6 %collective-permute-start.16 = (bf16[2176,128]{1,0:T(8,128)(2,1)}, bf16[2176,128]{1,0:T(8,128)(2,1)}, u32[]{:S(2)}, u32[]{:S(2)}) collective-permute-start(bf16[2176,128]{1,0:T(8,128)(2,1)} %collective-permute-done.13.refs_7_.refs_0_), channel_id=1, source_target_pairs={{0,1},{1,0},{2,3},{3,2},{4,5},{5,4},{6,7},{7,6},{8,9},{9,8},{10,11... | collective-permute-start | bytes 1671176 | tf_op jit(solution)/shard_map/ppermute | solution.py:583
  95.5 15.4 %collective-permute-start.14 = (bf16[2,128,1024]{2,1,0:T(8,128)(2,1)}, bf16[2,128,1024]{2,1,0:T(8,128)(2,1)}, u32[]{:S(2)}, u32[]{:S(2)}) collective-permute-start(bf16[2,128,1024]{2,1,0:T(8,128)(2,1)} %collective-permute-done.9.refs_5_), channel_id=1, source_target_pairs={{0,1},{1,0},{2,3},{3,2},{4,5},{5,4},{6,7},{7,6},{8,9},{9,8},{10,11... | collective-permute-start | bytes 1572872 | tf_op jit(solution)/shard_map/ppermute | solution.py:611
  102.3 17.1 %collective-permute-start.20 = (f32[512,128]{1,0:T(8,128)}, f32[512,128]{1,0:T(8,128)}, u32[]{:S(2)}, u32[]{:S(2)}) collective-permute-start(f32[512,128]{1,0:T(8,128)} %multiply_add_fusion.enter_ref), channel_id=1, source_target_pairs={{0,1},{1,0},{2,3},{3,2},{4,5},{5,4},{6,7},{7,6},{8,9},{9,8},{10,11... | collective-permute-start | bytes 786440 | tf_op jit(solution)/shard_map/ppermute | solution.py:232
  102.3 17.1 %collective-permute-start.22 = (bf16[2176,128]{1,0:T(8,128)(2,1)}, bf16[2176,128]{1,0:T(8,128)(2,1)}, u32[]{:S(2)}, u32[]{:S(2)}) collective-permute-start(bf16[2176,128]{1,0:T(8,128)(2,1)} %get-tuple-element.68), channel_id=1, source_target_pairs={{5,7},{2,4},{3,6},{13,15},{10,12},{11,14},{21,23},{18,20},{19,22},... | collective-permute-start | bytes 1671176 | tf_op jit(solution)/shard_map/ppermute | solution.py:660
  108.2 17.4 %collective-permute-start.24 = (bf16[2176,128]{1,0:T(8,128)(2,1)}, bf16[2176,128]{1,0:T(8,128)(2,1)}, u32[]{:S(2)}, u32[]{:S(2)}) collective-permute-start(bf16[2176,128]{1,0:T(8,128)(2,1)} %collective-permute-done.15.refs_7_.refs_0_), channel_id=1, source_target_pairs={{0,1},{1,0},{2,3},{3,2},{4,5},{5,4},{6,7},{7,6},{8,9},{9,8},{10,11... | collective-permute-start | bytes 1671176 | tf_op jit(solution)/shard_map/ppermute | solution.py:583
  115.7 15.4 %collective-permute-start.21 = (bf16[2176,128]{1,0:T(8,128)(2,1)}, bf16[2176,128]{1,0:T(8,128)(2,1)}, u32[]{:S(2)}, u32[]{:S(2)}) collective-permute-start(bf16[2176,128]{1,0:T(8,128)(2,1)} %get-tuple-element.73), channel_id=1, source_target_pairs={{5,7},{2,4},{3,6},{13,15},{10,12},{11,14},{21,23},{18,20},{19,22},... | collective-permute-start | bytes 1671176 | tf_op jit(solution)/shard_map/ppermute | solution.py:660
  119.4 9.0 %collective-permute-start.23 = (bf16[2176,128]{1,0:T(8,128)(2,1)}, bf16[2176,128]{1,0:T(8,128)(2,1)}, u32[]{:S(2)}, u32[]{:S(2)}) collective-permute-start(bf16[2176,128]{1,0:T(8,128)(2,1)} %collective-permute-done.22.refs_0_), channel_id=1, source_target_pairs={{0,1},{1,0},{2,3},{3,2},{4,5},{5,4},{6,7},{7,6},{8,9},{9,8},{10,11... | collective-permute-start | bytes 1671176 | tf_op jit(solution)/shard_map/ppermute | solution.py:583
  131.0 2.5 %collective-permute-start.25 = (bf16[2176,128]{1,0:T(8,128)(2,1)}, bf16[2176,128]{1,0:T(8,128)(2,1)}, u32[]{:S(2)}, u32[]{:S(2)}) collective-permute-start(bf16[2176,128]{1,0:T(8,128)(2,1)} %collective-permute-done.21.refs_0_), channel_id=1, source_target_pairs={{0,1},{1,0},{2,3},{3,2},{4,5},{5,4},{6,7},{7,6},{8,9},{9,8},{10,11... | collective-permute-start | bytes 1671176 | tf_op jit(solution)/shard_map/ppermute | solution.py:583

commit v8 on v7

--- a/solution.py
+++ b/solution.py
@@ -16,6 +16,7 @@
 HEADS_PER_STEP = 4
 CHUNK_STEPS = (2, 2, 2, 2)
 LAG = 2
+PARTS = 2
 NEGATIVE = -1e30
 EXP_SCALE = HEAD_DIM**-0.5 * math.log2(math.e)
 VMEM_LIMIT = 255 * 1024 * 256
@@ -27,7 +28,7 @@
 
 def cost(microseconds):
     return pl.CostEstimate(
-        flops=microseconds * 10**9, bytes_accessed=2**20, transcendentals=0
+        flops=microseconds * 10**8, bytes_accessed=2**16, transcendentals=0
     )
 
 
@@ -64,9 +65,8 @@
     return [taps_ref[feature, pl.ds(tap, 1), lanes] for tap in range(TAPS)]
 
 
-def state_kernel(
-    modes, k_ref, v_ref, rim_ref, par_ref, taps_ref, y_ref, s_ref, d_ref, p_scr, y_scr
-):
+def state_kernel(modes, k_ref, v_ref, rim_ref, par_ref, taps_ref, *rest):
+    y_ref, s_ref, d_ref, p_scr, y_scr = rest[-5:]
     rows = k_ref.shape[0]
     for block in range(SUBLANES):
         lanes = block_lanes(block)
@@ -172,7 +172,7 @@
     taps_spec = pl.BlockSpec((TAPS, TAPS, width), lambda group: (0, 0, group))
     positions = pltpu.VMEM((rows * SUBLANES, LANES), jnp.float32)
 
-    def first_part(token, state_token):
+    def first_part(token):
         own_par, rim = pl.pallas_call(
             conv_pack_kernel,
             grid=(1,),
@@ -192,46 +192,61 @@
         )(decay_rate.T, residue.T, hyena_q, hyena_k, hyena_v)
         rim = after(rim, token)
         rim = lax.ppermute(rim, "ctx", [(index, index + 1) for index in range(devices - 1)])
-        own_par = after(own_par, rim)
         par = lax.all_to_all(own_par, "ctx", split_axis=0, concat_axis=0, tiled=True)
         par = par.reshape(devices * par_rows, LANES)
-        state_spec = pl.BlockSpec((SUBLANES * modes, LANES), lambda group: (group, 0))
-        local_result, state, decay = pl.pallas_call(
+        return rim, par
+
+    def state_part(rim, par, part, earlier, *tokens):
+        count = groups // PARTS
+        first = part * count
+        blocked = [
+            pl.BlockSpec((rows, width), lambda group: (0, first + group)),
+            pl.BlockSpec((SUBLANES * modes, LANES), lambda group: (first + group, 0)),
+            pl.BlockSpec((SUBLANES * modes, LANES), lambda group: (first + group, 0)),
+        ]
+        return pl.pallas_call(
             functools.partial(state_kernel, modes),
-            grid=(groups,),
-            in_specs=[feature_spec, feature_spec, rim_spec, par_spec, taps_spec],
-            out_specs=[feature_spec, state_spec, state_spec],
+            grid=(count,),
+            in_specs=[
+                blocked[0],
+                blocked[0],
+                pl.BlockSpec((8, width), lambda group: (0, first + group)),
+                pl.BlockSpec((2 * SUBLANES * modes, LANES), lambda group: (first + group, 0)),
+                pl.BlockSpec((TAPS, TAPS, width), lambda group: (0, 0, first + group)),
+            ]
+            + [pl.BlockSpec(memory_space=pl.ANY)] * len(earlier),
+            out_specs=blocked,
             out_shape=[
                 jax.ShapeDtypeStruct((rows, channels), jnp.float32),
                 jax.ShapeDtypeStruct((blocks * modes, LANES), jnp.float32),
                 jax.ShapeDtypeStruct((blocks * modes, LANES), jnp.float32),
             ],
             scratch_shapes=[positions, positions],
+            input_output_aliases={5 + index: index for index in range(len(earlier))},
             compiler_params=params(),
-            cost_estimate=cost(9),
+            cost_estimate=cost(5),
             name="conv_state",
-        )(hyena_k, hyena_v, after(rim, state_token), par, short_filter)
-        return local_result, rim, par, decay, *entering_state(state, decay)
-
-    def entering_state(state, decay):
+        )(hyena_k, hyena_v, after(rim, *tokens) if tokens else rim, par, short_filter, *earlier)
+
+    def entering_state(state, decay, token):
         swap = [(index, index ^ 1) for index in range(devices)]
         other = lax.ppermute(state, "ctx", swap)
-        total = state + decay * other
+        total = after(state, token) + decay * other
         entering = None
-        reach = 1
-        while 2 * reach < devices:
-            moves = [(index, index + 2 * reach) for index in range(1, devices - 2 * reach, 2)]
+        for distance in range(1, devices // 2):
+            reach = 2 * distance
+            moves = [(index, index + reach) for index in range(1, devices - reach, 2)]
             arrived = lax.ppermute(total, "ctx", moves)
-            if reach == 1:
+            if distance == 1:
                 entering = arrived
             else:
-                entering = entering + decay ** (2 * (reach - 1)) * arrived
-            if 4 * reach < devices:
-                total = total + decay ** (2 * reach) * arrived
-            reach *= 2
+                entering = entering + decay ** (2 * (distance - 1)) * arrived
         return entering, lax.ppermute(entering, "ctx", swap), other
 
-    def last_part(local_result, rim, par, decay, entering, entering_first, other):
+    def last_part(parts, rim, par, token, last_token):
+        local_result, state, decay = parts
+        entering, entering_first, other = entering_state(state, decay, token)
+        entering = after(entering, last_token)
         state_spec = pl.BlockSpec((SUBLANES * modes, LANES), lambda group: (group, 0))
         return pl.pallas_call(
             functools.partial(output_kernel, modes),
@@ -256,7 +271,7 @@
             short_filter,
         )
 
-    return first_part, last_part
+    return first_part, state_part, last_part
 
 
 def among(me, members):
@@ -556,7 +571,7 @@
         return outs[:chunks], outs[chunks:]
 
     key_packs, query_packs = pack()
-    conv_first, conv_last = conv
+    conv_first, conv_state, conv_last = conv
     asks, quad_kv, all_answers = {}, [], []
     for chunk in range(chunks):
         key_pack = key_packs[chunk]
@@ -568,6 +583,8 @@
         if chunk:
             query_pack = after(query_pack, *asks[chunk - 1])
         asks[chunk] = [lax.ppermute(query_pack, "ctx", pairs) for pairs in transfers]
+    rim, par = conv_first(query_packs[0])
+    conv_parts = conv_state(rim, par, 0, ())
 
     half_rows = HEADS_PER_STEP * rows + TAIL
     hbm = pl.BlockSpec(memory_space=pl.ANY)
@@ -578,8 +595,7 @@
         own, lse, arrivals = returned[chunk]
         parts = [own, lse]
         for arrival in arrivals:
-            if earlier:
-                arrival = after(arrival, *earlier)
+            arrival = after(arrival, *earlier)
             parts += [arrival, lax.ppermute(arrival, "ctx", swap)]
         steps = CHUNK_STEPS[chunk]
         count = 2 * len(transfers)
@@ -605,12 +621,10 @@
 
     merged_count = 0
     for chunk in range(chunks):
-        arrived = quad_kv[chunk][0]
-        if chunk:
-            arrived = after(arrived, all_answers[-1][0])
+        arrived = after(quad_kv[chunk][0], all_answers[-1][0] if chunk else conv_parts[1])
         quad_kv[chunk] = [arrived, lax.ppermute(arrived, "ctx", swap)]
         if chunk > LAG:
-            result = merged(result, merged_count)
+            result = merged(result, merged_count, all_answers[-1][0])
             merged_count += 1
         steps, first = CHUNK_STEPS[chunk], first_steps[chunk]
         whole_spec = pl.BlockSpec((rows, step_width), lambda step, first=first: (0, first + step))
@@ -661,13 +675,14 @@
         if asking:
             asks[chunk + LAG] = arrivals
         returned.append([own, lse, arrivals])
-        if chunk == 0:
-            local_result, *conv_shared = conv_first(query_packs[0], answers[0])
-    conv_shared = [after(part, all_answers[-1][0]) for part in conv_shared]
-    hyena_out = conv_last(local_result, *conv_shared)
+        if chunk < PARTS - 1:
+            conv_parts = conv_state(rim, par, chunk + 1, conv_parts, answers[0])
+            asks[chunk + 1] = [after(ask, conv_parts[1]) for ask in asks[chunk + 1]]
+    tokens = [all_answers[min(LAG, chunks - 1)][0], all_answers[-1][0]]
+    hyena_out = conv_last(conv_parts, rim, par, *tokens)
     for chunk in range(merged_count, chunks):
         last = chunk == chunks - 1
-        result = merged(result, chunk, *((hyena_out, result) if last else ()))
+        result = merged(result, chunk, *((hyena_out, result) if last else all_answers[-1][:1]))
     return hyena_out, result
 
 

time: 138 us -> 141 us (1.022)
  starting transfers between devices: 47 us -> 66 us
  waiting for transfers between devices: 34.9 us -> 17.3 us
  Pallas kernels: 47.9 us -> 50 us
  local copies, waits for them, and re-layouts: 0.71 us -> 2.74 us
  other arithmetic: 4.72 us -> 3.02 us
    ppermute x2, waiting for transfers between devices: 15.8 us -> 0.27 us  [attend(): lax.ppermute(query_pack, 'ctx', pairs)]
    ppermute x4, starting transfers between devices: 6.85 us -> 18.5 us  [attend(): quad_kv[chunk] = [arrived, lax.ppermute(arrived, 'ctx', swap)]]
    ppermute x4, starting transfers between devices: 0.63 us -> 10.4 us  [merged(): parts += [arrival, lax.ppermute(arrival, 'ctx', swap)]]
    all_to_all x1, starting transfers between devices: 9.6 us -> 4.96 us  [first_part(): lax.all_to_all(own_par, 'ctx', split_axis=0, concat_axis=0, tiled=True)]
    ppermute x4, waiting for transfers between devices: 3.54 us -> 0.01 us  [attend(): arrivals.append(lax.ppermute(answer, 'ctx', moves))]
    all_to_all x1, waiting for transfers between devices: 0.01 us -> 2.83 us  [first_part(): lax.all_to_all(own_par, 'ctx', split_axis=0, concat_axis=0, tiled=True)]
    ppermute x1, starting transfers between devices: 0.08 us -> 2.32 us  [attend(): key_swapped = lax.ppermute(key, 'ctx', swap)]
    ppermute x1, waiting for transfers between devices: 2.24 us -> 0.01 us  [first_part(): lax.ppermute(rim, 'ctx', [(index, index + 1) for index in range(devices -...]
  transfers between devices with their start and end apart: 27 -> 28, of which waited for: 7 -> 5; matrix products, arithmetic and copies ran while one was open for 3% -> 2% of each run, Pallas kernels for 33% -> 34%
where the time goes in v8:
time: 141 us; the launch traced here: 140 us
  starting transfers between devices  66 us (47%)
  Pallas kernels  50 us (35%)
  waiting for transfers between devices  17.3 us (12%)
  other arithmetic  3.02 us (2%)
  local copies, waits for them, and re-layouts  2.74 us (2%)
    pallas_call x4, Pallas kernels, attend(): pl.pallas_call(functools.partial(partial_kernel, transfers, upper, natura...  19.2 us
    ppermute x4, starting transfers between devices, attend(): quad_kv[chunk] = [arrived, lax.ppermute(arrived, 'ctx', swap)]  18.5 us
    ppermute x4, starting transfers between devices, attend(): arrivals.append(lax.ppermute(answer, 'ctx', moves))  12.5 us
    pallas_call x2, Pallas kernels, state_part(): pl.pallas_call(functools.partial(state_kernel, modes), grid=(count,), in_...  11.6 us
    pallas_call x4, Pallas kernels, merged(): pl.pallas_call(functools.partial(merge_kernel, transfers, steps, starts[c...  10.8 us
    ppermute x3, waiting for transfers between devices, entering_state(): arrived = lax.ppermute(total, 'ctx', moves)  10.5 us
    ppermute x4, starting transfers between devices, merged(): parts += [arrival, lax.ppermute(arrival, 'ctx', swap)]  10.4 us
    pallas_call x1, Pallas kernels, last_part(): pl.pallas_call(functools.partial(output_kernel, modes), grid=(groups,), i...  6.28 us
  transfers between devices with their start and end apart: 28, of which 5 were waited for; matrix products, arithmetic and copies ran while one was open for 2% of the time, Pallas kernels for 34%

profile of v8, /device:TPU:17, one launch (start us, length us, event | category | flops | bytes accessed | tf_op | source)
XLA Modules:
  0.0 140.1 jit_solution(13874076097552888797)
XLA Ops:
  0.6 0.7 collective-permute-start
  1.4 1.9 %conv_pack.1 = (f32[8,128,128]{2,1,0:T(8,128)}, f32[8,4096]{1,0:T(8,128)}) custom-call(f32[16,512]{1,0:T(8,128)} %bitcast.3, f32[16,512]{1,0:T(8,128)} %bitcast.4, bf16[128,4096]{1,0:T(8,128)(2,1)} %q_ref.5, bf16[128,4096]{1,0:T(8,128)(2,1)} %k_ref.7, bf16[128,4096]{1,0:T(8,128)(2,1)} %v_ref.7), custom_call_target="tpu_custom_call" | custom-call | flops 100000000 | bytes 65536 | tf_op jit(solution)/shard_map/conv_pack/pallas_call | solution.py:176
  3.3 5.0 %all-to-all-start = ((f32[8,128,128]{2,1,0:T(8,128)}), f32[8,128,128]{2,1,0:T(8,128)}, u32[]{:S(2)}, u32[]{:S(2)}) async-start(f32[8,128,128]{2,1,0:T(8,128)} %get-tuple-element.53), calls=%async_computation | async-start | bytes 1048576 | tf_op jit(solution)/shard_map/all_to_all | solution.py:195
  8.3 0.1 att_pack.1
  8.4 1.5 %collective-permute-start.4 = (bf16[2,128,1024]{2,1,0:T(8,128)(2,1)}, bf16[2,128,1024]{2,1,0:T(8,128)(2,1)}, u32[]{:S(2)}, u32[]{:S(2)}) collective-permute-start(bf16[2,128,1024]{2,1,0:T(8,128)(2,1)} %get-tuple-element.52), channel_id=1, source_target_pairs={{0,2},{1,3},{8,10},{9,11},{16,18},{17,19},{24,26},{25,27}} | collective-permute-start | bytes 1572872 | tf_op jit(solution)/shard_map/ppermute | solution.py:580
  9.9 2.3 %collective-permute-start.2 = (bf16[128,4096]{1,0:T(8,128)(2,1)}, bf16[128,4096]{1,0:T(8,128)(2,1)}, u32[]{:S(2)}, u32[]{:S(2)}) collective-permute-start(bf16[128,4096]{1,0:T(8,128)(2,1)} %refs_1_.7), channel_id=1, source_target_pairs={{0,1},{1,0},{2,3},{3,2},{4,5},{5,4},{6,7},{7,6},{8,9},{9,8},{10,11... | collective-permute-start | bytes 3145736 | tf_op jit(solution)/shard_map/ppermute | solution.py:534
  12.2 3.5 %collective-permute-start.1 = (f32[8,4096]{1,0:T(8,128)}, f32[8,4096]{1,0:T(8,128)S(1)}, u32[]{:S(2)}, u32[]{:S(2)}) collective-permute-start(f32[8,4096]{1,0:T(8,128)} %get-tuple-element.51), channel_id=1, source_target_pairs={{0,1},{1,2},{2,3},{3,4},{4,5},{5,6},{6,7},{8,9},{9,10},{10,11},{11... | collective-permute-start | bytes 393224 | tf_op jit(solution)/shard_map/ppermute | solution.py:194
  15.7 1.3 collective-permute-start.6
  17.0 2.8 %all-to-all-done = f32[8,128,128]{2,1,0:T(8,128)} async-done(((f32[8,128,128]{2,1,0:T(8,128)}), f32[8,128,128]{2,1,0:T(8,128)}, u32[]{:S(2)}, u32[]{:S(2)}) %all-to-all-start) | async-done | bytes 524320 | tf_op jit(solution)/shard_map/all_to_all | solution.py:195
  19.9 0.6 copy-done
  20.5 5.8 %conv_state.2 = (f32[128,4096]{1,0:T(8,128)}, f32[512,128]{1,0:T(8,128)}, f32[512,128]{1,0:T(8,128)}) custom-call(bf16[128,4096]{1,0:T(8,128)(2,1)} %k_ref.7, bf16[128,4096]{1,0:T(8,128)(2,1)} %v_ref.7, f32[8,4096]{1,0:T(8,128)} %copy-done, f32[1024,128]{1,0:T(8,128)} %bitcast.2.par_ref, f32[3,3,4096]{2,1,0:T(4,128)} %taps_ref.5), custom_call_target="tpu_custom_call" | custom-call | flops 500000000 | bytes 65536 | tf_op jit(solution)/shard_map/conv_state/pallas_call | solution.py:207
  26.3 3.0 %collective-permute-start.5 = (bf16[2,128,1024]{2,1,0:T(8,128)(2,1)}, bf16[2,128,1024]{2,1,0:T(8,128)(2,1)}, u32[]{:S(2)}, u32[]{:S(2)}) collective-permute-start(bf16[2,128,1024]{2,1,0:T(8,128)(2,1)} %collective-permute-done.4.refs_5_), channel_id=1, source_target_pairs={{0,1},{1,0},{2,3},{3,2},{4,5},{5,4},{6,7},{7,6},{8,9},{9,8},{10,11... | collective-permute-start | bytes 1572872 | tf_op jit(solution)/shard_map/ppermute | solution.py:625
  29.3 1.4 %collective-permute-start.7 = (bf16[2,128,1024]{2,1,0:T(8,128)(2,1)}, bf16[2,128,1024]{2,1,0:T(8,128)(2,1)}, u32[]{:S(2)}, u32[]{:S(2)}) collective-permute-start(bf16[2,128,1024]{2,1,0:T(8,128)(2,1)} %get-tuple-element.65), channel_id=1, source_target_pairs={{0,2},{1,3},{8,10},{9,11},{16,18},{17,19},{24,26},{25,27}} | collective-permute-start | bytes 1572872 | tf_op jit(solution)/shard_map/ppermute | solution.py:580
  30.8 0.3 collective-permute-done.6.refs_7_
  31.1 1.3 collective-permute-start.10
  32.4 4.8 %att_partial.4 = (f32[128,1024]{1,0:T(8,128)}, f32[16,128]{1,0:T(8,128)}, bf16[2176,128]{1,0:T(8,128)(2,1)}, bf16[128,4096]{1,0:T(8,128)(2,1)}) custom-call(bf16[128,4096]{1,0:T(8,128)(2,1)} %refs_0_.7, bf16[128,4096]{1,0:T(8,128)(2,1)} %refs_1_.7, bf16[128,4096]{1,0:T(8,128)(2,1)} %refs_2_.7, bf16[128,4096]{1,0:T(8,128)(2,1)} %collective-permute-done.2.refs_3_, ...), custom_call_target="tpu_custom_call" | custom-call | flops 400000000 | bytes 65536 | tf_op jit(solution)/shard_map/att_partial/pallas_call | solution.py:652
  37.2 8.8 %collective-permute-start.9 = (bf16[2,128,1024]{2,1,0:T(8,128)(2,1)}, bf16[2,128,1024]{2,1,0:T(8,128)(2,1)}, u32[]{:S(2)}, u32[]{:S(2)}) collective-permute-start(bf16[2,128,1024]{2,1,0:T(8,128)(2,1)} %collective-permute-done.7.refs_5_), channel_id=1, source_target_pairs={{0,1},{1,0},{2,3},{3,2},{4,5},{5,4},{6,7},{7,6},{8,9},{9,8},{10,11... | collective-permute-start | bytes 1572872 | tf_op jit(solution)/shard_map/ppermute | solution.py:625
  46.0 1.5 %collective-permute-start.8 = (bf16[2,128,1024]{2,1,0:T(8,128)(2,1)}, bf16[2,128,1024]{2,1,0:T(8,128)(2,1)}, u32[]{:S(2)}, u32[]{:S(2)}) collective-permute-start(bf16[2,128,1024]{2,1,0:T(8,128)(2,1)} %get-tuple-element.66), channel_id=1, source_target_pairs={{0,2},{1,3},{8,10},{9,11},{16,18},{17,19},{24,26},{25,27}} | collective-permute-start | bytes 1572872 | tf_op jit(solution)/shard_map/ppermute | solution.py:580
  47.5 3.2 %collective-permute-start.12 = (bf16[2176,128]{1,0:T(8,128)(2,1)}, bf16[2176,128]{1,0:T(8,128)(2,1)}, u32[]{:S(2)}, u32[]{:S(2)}) collective-permute-start(bf16[2176,128]{1,0:T(8,128)(2,1)} %get-tuple-element.56), channel_id=1, source_target_pairs={{5,7},{2,4},{3,6},{7,5},{4,2},{6,3},{13,15},{10,12},{11,14},{15,13... | collective-permute-start | bytes 1671176 | tf_op jit(solution)/shard_map/ppermute | solution.py:674
  50.6 5.8 %conv_state.3 = (f32[128,4096]{1,0:T(8,128)}, f32[512,128]{1,0:T(8,128)}, f32[512,128]{1,0:T(8,128)}) custom-call(bf16[128,4096]{1,0:T(8,128)(2,1)} %k_ref.7, bf16[128,4096]{1,0:T(8,128)(2,1)} %v_ref.7, f32[8,4096]{1,0:T(8,128)} %copy-done, f32[1024,128]{1,0:T(8,128)} %bitcast.2.par_ref, ...), custom_call_target="tpu_custom_call", output_to_operand_aliasing={{0}: (5, {}), {1}: (6, {}), {2}: (7, {})} | custom-call | flops 500000000 | bytes 65536 | tf_op jit(solution)/shard_map/conv_state/pallas_call | solution.py:207
  56.5 4.8 %att_partial.5 = (f32[128,1024]{1,0:T(8,128)}, f32[16,128]{1,0:T(8,128)}, bf16[2176,128]{1,0:T(8,128)(2,1)}, bf16[128,4096]{1,0:T(8,128)(2,1)}) custom-call(bf16[128,4096]{1,0:T(8,128)(2,1)} %refs_0_.7, bf16[128,4096]{1,0:T(8,128)(2,1)} %refs_1_.7, bf16[128,4096]{1,0:T(8,128)(2,1)} %refs_2_.7, ...), custom_call_target="tpu_custom_call", output_to_operand_aliasing={{3}: (10, {})} | custom-call | flops 400000000 | bytes 65536 | tf_op jit(solution)/shard_map/att_partial/pallas_call | solution.py:652
  61.3 6.3 %collective-permute-start.11 = (bf16[2,128,1024]{2,1,0:T(8,128)(2,1)}, bf16[2,128,1024]{2,1,0:T(8,128)(2,1)}, u32[]{:S(2)}, u32[]{:S(2)}) collective-permute-start(bf16[2,128,1024]{2,1,0:T(8,128)(2,1)} %collective-permute-done.8.refs_5_), channel_id=1, source_target_pairs={{0,1},{1,0},{2,3},{3,2},{4,5},{5,4},{6,7},{7,6},{8,9},{9,8},{10,11... | collective-permute-start | bytes 1572872 | tf_op jit(solution)/shard_map/ppermute | solution.py:625
  67.6 1.4 %collective-permute-start.17 = (bf16[2,128,1024]{2,1,0:T(8,128)(2,1)}, bf16[2,128,1024]{2,1,0:T(8,128)(2,1)}, u32[]{:S(2)}, u32[]{:S(2)}) collective-permute-start(bf16[2,128,1024]{2,1,0:T(8,128)(2,1)} %get-tuple-element.78), channel_id=1, source_target_pairs={{0,2},{1,3},{8,10},{9,11},{16,18},{17,19},{24,26},{25,27}} | collective-permute-start | bytes 1572872 | tf_op jit(solution)/shard_map/ppermute | solution.py:580
  69.0 3.2 %collective-permute-start.19 = (bf16[2176,128]{1,0:T(8,128)(2,1)}, bf16[2176,128]{1,0:T(8,128)(2,1)}, u32[]{:S(2)}, u32[]{:S(2)}) collective-permute-start(bf16[2176,128]{1,0:T(8,128)(2,1)} %get-tuple-element.72), channel_id=1, source_target_pairs={{5,7},{2,4},{3,6},{7,5},{4,2},{6,3},{13,15},{10,12},{11,14},{15,13... | collective-permute-start | bytes 1671176 | tf_op jit(solution)/shard_map/ppermute | solution.py:674
  72.3 4.8 %att_partial.6 = (f32[128,1024]{1,0:T(8,128)}, f32[16,128]{1,0:T(8,128)}, bf16[2176,128]{1,0:T(8,128)(2,1)}, bf16[128,4096]{1,0:T(8,128)(2,1)}) custom-call(bf16[128,4096]{1,0:T(8,128)(2,1)} %refs_0_.7, bf16[128,4096]{1,0:T(8,128)(2,1)} %refs_1_.7, bf16[128,4096]{1,0:T(8,128)(2,1)} %refs_2_.7, ...), custom_call_target="tpu_custom_call", output_to_operand_aliasing={{3}: (8, {})} | custom-call | flops 400000000 | bytes 65536 | tf_op jit(solution)/shard_map/att_partial/pallas_call | solution.py:652
  77.0 1.1 collective-permute-start.20
  78.2 0.4 collective-permute-start.18
  78.6 4.1 %collective-permute-start.23 = (bf16[2176,128]{1,0:T(8,128)(2,1)}, bf16[2176,128]{1,0:T(8,128)(2,1)}, u32[]{:S(2)}, u32[]{:S(2)}) collective-permute-start(bf16[2176,128]{1,0:T(8,128)(2,1)} %get-tuple-element.75), channel_id=1, source_target_pairs={{5,7},{2,4},{3,6},{13,15},{10,12},{11,14},{21,23},{18,20},{19,22},... | collective-permute-start | bytes 1671176 | tf_op jit(solution)/shard_map/ppermute | solution.py:674
  82.7 0.7 copy-done.2
  83.4 1.8 %multiply_add_fusion.1 = f32[512,128]{1,0:T(8,128)} fusion(f32[512,128]{1,0:T(8,128)} %get-tuple-element.76, f32[512,128]{1,0:T(8,128)} %get-tuple-element.61.decay_ref, f32[512,128]{1,0:T(8,128)S(1)} %collective-permute-done.13.other_ref), kind=kLoop, calls=%fused_computation.1 | loop fusion | flops 131072 | bytes 1048576 | tf_op jit(solution)/shard_map/add | solution.py:234
  85.1 1.4 collective-permute-start.16
  86.5 1.3 collective-permute-start.15
  87.8 1.9 %collective-permute-start.14 = (f32[512,128]{1,0:T(8,128)}, f32[512,128]{1,0:T(8,128)}, u32[]{:S(2)}, u32[]{:S(2)}) collective-permute-start(f32[512,128]{1,0:T(8,128)} %multiply_add_fusion.1), channel_id=1, source_target_pairs={{1,3},{3,5},{5,7},{9,11},{11,13},{13,15},{17,19},{19,21},{21,23},{... | collective-permute-start | bytes 786440 | tf_op jit(solution)/shard_map/ppermute | solution.py:239
  89.7 2.8 %att_merge.4.refs_8_ = bf16[128,4096]{1,0:T(8,128)(2,1)} custom-call(f32[128,1024]{1,0:T(8,128)} %get-tuple-element.80.own_hbm, f32[16,128]{1,0:T(8,128)} %get-tuple-element.81.lse_hbm, bf16[2176,128]{1,0:T(8,128)(2,1)} %collective-permute-done.12.refs_7_.refs_0_, bf16[2176,128]{1,0:T(8,128)(2,1)} %collective-permute-done.20.refs_1_, ...), custom_call_target="tpu_custom_call", output_to_operand_aliasing={{}: (4, {})} | custom-call | flops 200000000 | bytes 65536 | tf_op jit(solution)/shard_map/att_merge/pallas_call | solution.py:602
  92.6 4.8 %att_partial.7 = (f32[128,1024]{1,0:T(8,128)}, f32[16,128]{1,0:T(8,128)}, bf16[2176,128]{1,0:T(8,128)(2,1)}, bf16[128,4096]{1,0:T(8,128)(2,1)}) custom-call(bf16[128,4096]{1,0:T(8,128)(2,1)} %refs_0_.7, bf16[128,4096]{1,0:T(8,128)(2,1)} %refs_1_.7, bf16[128,4096]{1,0:T(8,128)(2,1)} %refs_2_.7, ...), custom_call_target="tpu_custom_call", output_to_operand_aliasing={{3}: (8, {})} | custom-call | flops 400000000 | bytes 65536 | tf_op jit(solution)/shard_map/att_partial/pallas_call | solution.py:652
  97.4 2.1 %collective-permute-start.22 = (bf16[2176,128]{1,0:T(8,128)(2,1)}, bf16[2176,128]{1,0:T(8,128)(2,1)}, u32[]{:S(2)}, u32[]{:S(2)}) collective-permute-start(bf16[2176,128]{1,0:T(8,128)(2,1)} %get-tuple-element.84), channel_id=1, source_target_pairs={{5,7},{2,4},{3,6},{13,15},{10,12},{11,14},{21,23},{18,20},{19,22},... | collective-permute-start | bytes 1671176 | tf_op jit(solution)/shard_map/ppermute | solution.py:674
  99.5 9.1 %collective-permute-start.25 = (bf16[2176,128]{1,0:T(8,128)(2,1)}, bf16[2176,128]{1,0:T(8,128)(2,1)}, u32[]{:S(2)}, u32[]{:S(2)}) collective-permute-start(bf16[2176,128]{1,0:T(8,128)(2,1)} %collective-permute-done.19.refs_7_.refs_0_), channel_id=1, source_target_pairs={{0,1},{1,0},{2,3},{3,2},{4,5},{5,4},{6,7},{7,6},{8,9},{9,8},{10,11... | collective-permute-start | bytes 1671176 | tf_op jit(solution)/shard_map/ppermute | solution.py:599
  108.6 10.5 %collective-permute-done.14 = f32[512,128]{1,0:T(8,128)} collective-permute-done((f32[512,128]{1,0:T(8,128)}, f32[512,128]{1,0:T(8,128)}, u32[]{:S(2)}, u32[]{:S(2)}) %collective-permute-start.14) | collective-permute-done | bytes 262176 | tf_op jit(solution)/shard_map/ppermute | solution.py:239
  119.1 1.2 multiply_add_fusion.enter_ref
  120.3 0.7 copy-done.1
  121.0 1.5 %collective-permute-done.21.enter_first_ref = f32[512,128]{1,0:T(8,128)S(1)} collective-permute-done((f32[512,128]{1,0:T(8,128)S(1)}, f32[512,128]{1,0:T(8,128)S(1)}, u32[]{:S(2)}, u32[]{:S(2)}) %collective-permute-start.21) | collective-permute-done | bytes 262176 | tf_op jit(solution)/shard_map/ppermute | solution.py:244
  122.6 0.7 copy-done.3
  123.3 6.3 %conv_output.1 = bf16[128,4096]{1,0:T(8,128)(2,1)} custom-call(bf16[128,4096]{1,0:T(8,128)(2,1)} %q_ref.5, f32[128,4096]{1,0:T(8,128)} %get-tuple-element.60.y_ref, f32[8,4096]{1,0:T(8,128)} %copy-done, f32[1024,128]{1,0:T(8,128)} %bitcast.2.par_ref, f32[512,128]{1,0:T(8,128)} %get-tuple-element.61.decay_ref, f32[512,128]{1,0:T(8,128)} %copy-done.1, ...), custom_call_target="tpu_custom_call" | custom-call | flops 600000000 | bytes 65536 | tf_op jit(solution)/shard_map/conv_output/pallas_call | solution.py:251
  129.6 2.7 %att_merge.5.refs_2_ = bf16[128,4096]{1,0:T(8,128)(2,1)} custom-call(f32[128,1024]{1,0:T(8,128)} %get-tuple-element.91.own_hbm, f32[16,128]{1,0:T(8,128)} %get-tuple-element.92.lse_hbm, bf16[2176,128]{1,0:T(8,128)(2,1)} %collective-permute-done.19.refs_7_.refs_0_, bf16[2176,128]{1,0:T(8,128)(2,1)} %collective-permute-done.25.refs_1_, ...), custom_call_target="tpu_custom_call", output_to_operand_aliasing={{}: (4, {})} | custom-call | flops 200000000 | bytes 65536 | tf_op jit(solution)/shard_map/att_merge/pallas_call | solution.py:602
  132.2 2.7 %att_merge.6.refs_2_ = bf16[128,4096]{1,0:T(8,128)(2,1)} custom-call(f32[128,1024]{1,0:T(8,128)} %get-tuple-element.88.own_hbm, f32[16,128]{1,0:T(8,128)} %get-tuple-element.89.lse_hbm, bf16[2176,128]{1,0:T(8,128)(2,1)} %collective-permute-done.23.refs_0_, bf16[2176,128]{1,0:T(8,128)(2,1)} %collective-permute-done.24.refs_1_, ...), custom_call_target="tpu_custom_call", output_to_operand_aliasing={{}: (4, {})} | custom-call | flops 200000000 | bytes 65536 | tf_op jit(solution)/shard_map/att_merge/pallas_call | solution.py:602
  134.9 0.2 collective-permute-start.26
  135.1 2.2 %collective-permute-done.26.refs_1_ = bf16[2176,128]{1,0:T(8,128)(2,1)} collective-permute-done((bf16[2176,128]{1,0:T(8,128)(2,1)}, bf16[2176,128]{1,0:T(8,128)(2,1)}, u32[]{:S(2)}, u32[]{:S(2)}) %collective-permute-start.26) | collective-permute-done | bytes 557088 | tf_op jit(solution)/shard_map/ppermute | solution.py:599
  137.3 2.6 %att_merge.7 = bf16[128,4096]{1,0:T(8,128)(2,1)} custom-call(f32[128,1024]{1,0:T(8,128)} %get-tuple-element.86.own_hbm, f32[16,128]{1,0:T(8,128)} %get-tuple-element.87.lse_hbm, bf16[2176,128]{1,0:T(8,128)(2,1)} %collective-permute-done.22.refs_0_, bf16[2176,128]{1,0:T(8,128)(2,1)} %collective-permute-done.26.refs_1_, ...), custom_call_target="tpu_custom_call", output_to_operand_aliasing={{}: (4, {})} | custom-call | flops 200000000 | bytes 65536 | tf_op jit(solution)/shard_map/att_merge/pallas_call | solution.py:602
  (31 shorter events, 0.2 us)
Async XLA Ops:
  0.6 7.6 %collective-permute-start = (bf16[128,4096]{1,0:T(8,128)(2,1)}, bf16[128,4096]{1,0:T(8,128)(2,1)}, u32[]{:S(2)}, u32[]{:S(2)}) collective-permute-start(bf16[128,4096]{1,0:T(8,128)(2,1)} %refs_0_.7), channel_id=1, source_target_pairs={{0,1},{1,0},{2,3},{3,2},{4,5},{5,4},{6,7},{7,6},{8,9},{9,8},{10,11... | collective-permute-start | bytes 3145736 | tf_op jit(solution)/shard_map/ppermute | solution.py:533
  3.3 16.5 %all-to-all-start = ((f32[8,128,128]{2,1,0:T(8,128)}), f32[8,128,128]{2,1,0:T(8,128)}, u32[]{:S(2)}, u32[]{:S(2)}) async-start(f32[8,128,128]{2,1,0:T(8,128)} %get-tuple-element.53), calls=%async_computation | async-start | bytes 1048576 | tf_op jit(solution)/shard_map/all_to_all | solution.py:195
  8.4 17.9 %collective-permute-start.4 = (bf16[2,128,1024]{2,1,0:T(8,128)(2,1)}, bf16[2,128,1024]{2,1,0:T(8,128)(2,1)}, u32[]{:S(2)}, u32[]{:S(2)}) collective-permute-start(bf16[2,128,1024]{2,1,0:T(8,128)(2,1)} %get-tuple-element.52), channel_id=1, source_target_pairs={{0,2},{1,3},{8,10},{9,11},{16,18},{17,19},{24,26},{25,27}} | collective-permute-start | bytes 1572872 | tf_op jit(solution)/shard_map/ppermute | solution.py:580
  9.9 22.4 %collective-permute-start.2 = (bf16[128,4096]{1,0:T(8,128)(2,1)}, bf16[128,4096]{1,0:T(8,128)(2,1)}, u32[]{:S(2)}, u32[]{:S(2)}) collective-permute-start(bf16[128,4096]{1,0:T(8,128)(2,1)} %refs_1_.7), channel_id=1, source_target_pairs={{0,1},{1,0},{2,3},{3,2},{4,5},{5,4},{6,7},{7,6},{8,9},{9,8},{10,11... | collective-permute-start | bytes 3145736 | tf_op jit(solution)/shard_map/ppermute | solution.py:534
  12.2 20.1 %collective-permute-start.3 = (bf16[128,4096]{1,0:T(8,128)(2,1)}, bf16[128,4096]{1,0:T(8,128)(2,1)}, u32[]{:S(2)}, u32[]{:S(2)}) collective-permute-start(bf16[128,4096]{1,0:T(8,128)(2,1)} %refs_2_.7), channel_id=1, source_target_pairs={{0,1},{1,0},{2,3},{3,2},{4,5},{5,4},{6,7},{7,6},{8,9},{9,8},{10,11... | collective-permute-start | bytes 3145736 | tf_op jit(solution)/shard_map/ppermute | solution.py:535
  12.2 7.6 %collective-permute-start.1 = (f32[8,4096]{1,0:T(8,128)}, f32[8,4096]{1,0:T(8,128)S(1)}, u32[]{:S(2)}, u32[]{:S(2)}) collective-permute-start(f32[8,4096]{1,0:T(8,128)} %get-tuple-element.51), channel_id=1, source_target_pairs={{0,1},{1,2},{2,3},{3,4},{4,5},{5,6},{6,7},{8,9},{9,10},{10,11},{11... | collective-permute-start | bytes 393224 | tf_op jit(solution)/shard_map/ppermute | solution.py:194
  15.7 15.3 %collective-permute-start.6 = (bf16[2,128,1024]{2,1,0:T(8,128)(2,1)}, bf16[2,128,1024]{2,1,0:T(8,128)(2,1)}, u32[]{:S(2)}, u32[]{:S(2)}) collective-permute-start(bf16[2,128,1024]{2,1,0:T(8,128)(2,1)} %get-tuple-element.50), channel_id=1, source_target_pairs={{7,5},{4,2},{6,3},{15,13},{12,10},{14,11},{23,21},{20,18},{22,19},... | collective-permute-start | bytes 1572872 | tf_op jit(solution)/shard_map/ppermute | solution.py:585
  19.8 0.6 copy-start
  26.3 6.1 %collective-permute-start.5 = (bf16[2,128,1024]{2,1,0:T(8,128)(2,1)}, bf16[2,128,1024]{2,1,0:T(8,128)(2,1)}, u32[]{:S(2)}, u32[]{:S(2)}) collective-permute-start(bf16[2,128,1024]{2,1,0:T(8,128)(2,1)} %collective-permute-done.4.refs_5_), channel_id=1, source_target_pairs={{0,1},{1,0},{2,3},{3,2},{4,5},{5,4},{6,7},{7,6},{8,9},{9,8},{10,11... | collective-permute-start | bytes 1572872 | tf_op jit(solution)/shard_map/ppermute | solution.py:625
  29.3 7.9 %collective-permute-start.7 = (bf16[2,128,1024]{2,1,0:T(8,128)(2,1)}, bf16[2,128,1024]{2,1,0:T(8,128)(2,1)}, u32[]{:S(2)}, u32[]{:S(2)}) collective-permute-start(bf16[2,128,1024]{2,1,0:T(8,128)(2,1)} %get-tuple-element.65), channel_id=1, source_target_pairs={{0,2},{1,3},{8,10},{9,11},{16,18},{17,19},{24,26},{25,27}} | collective-permute-start | bytes 1572872 | tf_op jit(solution)/shard_map/ppermute | solution.py:580
  31.1 25.4 %collective-permute-start.10 = (bf16[2,128,1024]{2,1,0:T(8,128)(2,1)}, bf16[2,128,1024]{2,1,0:T(8,128)(2,1)}, u32[]{:S(2)}, u32[]{:S(2)}) collective-permute-start(bf16[2,128,1024]{2,1,0:T(8,128)(2,1)} %get-tuple-element.69), channel_id=1, source_target_pairs={{7,5},{4,2},{6,3},{15,13},{12,10},{14,11},{23,21},{20,18},{22,19},... | collective-permute-start | bytes 1572872 | tf_op jit(solution)/shard_map/ppermute | solution.py:585
  37.2 19.3 %collective-permute-start.9 = (bf16[2,128,1024]{2,1,0:T(8,128)(2,1)}, bf16[2,128,1024]{2,1,0:T(8,128)(2,1)}, u32[]{:S(2)}, u32[]{:S(2)}) collective-permute-start(bf16[2,128,1024]{2,1,0:T(8,128)(2,1)} %collective-permute-done.7.refs_5_), channel_id=1, source_target_pairs={{0,1},{1,0},{2,3},{3,2},{4,5},{5,4},{6,7},{7,6},{8,9},{9,8},{10,11... | collective-permute-start | bytes 1572872 | tf_op jit(solution)/shard_map/ppermute | solution.py:625
  46.0 15.3 %collective-permute-start.8 = (bf16[2,128,1024]{2,1,0:T(8,128)(2,1)}, bf16[2,128,1024]{2,1,0:T(8,128)(2,1)}, u32[]{:S(2)}, u32[]{:S(2)}) collective-permute-start(bf16[2,128,1024]{2,1,0:T(8,128)(2,1)} %get-tuple-element.66), channel_id=1, source_target_pairs={{0,2},{1,3},{8,10},{9,11},{16,18},{17,19},{24,26},{25,27}} | collective-permute-start | bytes 1572872 | tf_op jit(solution)/shard_map/ppermute | solution.py:580
  47.5 24.8 %collective-permute-start.12 = (bf16[2176,128]{1,0:T(8,128)(2,1)}, bf16[2176,128]{1,0:T(8,128)(2,1)}, u32[]{:S(2)}, u32[]{:S(2)}) collective-permute-start(bf16[2176,128]{1,0:T(8,128)(2,1)} %get-tuple-element.56), channel_id=1, source_target_pairs={{5,7},{2,4},{3,6},{7,5},{4,2},{6,3},{13,15},{10,12},{11,14},{15,13... | collective-permute-start | bytes 1671176 | tf_op jit(solution)/shard_map/ppermute | solution.py:674
  61.3 10.9 %collective-permute-start.11 = (bf16[2,128,1024]{2,1,0:T(8,128)(2,1)}, bf16[2,128,1024]{2,1,0:T(8,128)(2,1)}, u32[]{:S(2)}, u32[]{:S(2)}) collective-permute-start(bf16[2,128,1024]{2,1,0:T(8,128)(2,1)} %collective-permute-done.8.refs_5_), channel_id=1, source_target_pairs={{0,1},{1,0},{2,3},{3,2},{4,5},{5,4},{6,7},{7,6},{8,9},{9,8},{10,11... | collective-permute-start | bytes 1572872 | tf_op jit(solution)/shard_map/ppermute | solution.py:625
  67.6 10.6 %collective-permute-start.17 = (bf16[2,128,1024]{2,1,0:T(8,128)(2,1)}, bf16[2,128,1024]{2,1,0:T(8,128)(2,1)}, u32[]{:S(2)}, u32[]{:S(2)}) collective-permute-start(bf16[2,128,1024]{2,1,0:T(8,128)(2,1)} %get-tuple-element.78), channel_id=1, source_target_pairs={{0,2},{1,3},{8,10},{9,11},{16,18},{17,19},{24,26},{25,27}} | collective-permute-start | bytes 1572872 | tf_op jit(solution)/shard_map/ppermute | solution.py:580
  69.0 17.5 %collective-permute-start.19 = (bf16[2176,128]{1,0:T(8,128)(2,1)}, bf16[2176,128]{1,0:T(8,128)(2,1)}, u32[]{:S(2)}, u32[]{:S(2)}) collective-permute-start(bf16[2176,128]{1,0:T(8,128)(2,1)} %get-tuple-element.72), channel_id=1, source_target_pairs={{5,7},{2,4},{3,6},{7,5},{4,2},{6,3},{13,15},{10,12},{11,14},{15,13... | collective-permute-start | bytes 1671176 | tf_op jit(solution)/shard_map/ppermute | solution.py:674
  77.0 10.8 %collective-permute-start.20 = (bf16[2176,128]{1,0:T(8,128)(2,1)}, bf16[2176,128]{1,0:T(8,128)(2,1)}, u32[]{:S(2)}, u32[]{:S(2)}) collective-permute-start(bf16[2176,128]{1,0:T(8,128)(2,1)} %collective-permute-done.12.refs_7_.refs_0_), channel_id=1, source_target_pairs={{0,1},{1,0},{2,3},{3,2},{4,5},{5,4},{6,7},{7,6},{8,9},{9,8},{10,11... | collective-permute-start | bytes 1671176 | tf_op jit(solution)/shard_map/ppermute | solution.py:599
  78.1 4.6 %collective-permute-start.13 = (f32[512,128]{1,0:T(8,128)}, f32[512,128]{1,0:T(8,128)S(1)}, u32[]{:S(2)}, u32[]{:S(2)}) collective-permute-start(f32[512,128]{1,0:T(8,128)} %get-tuple-element.76), channel_id=1, source_target_pairs={{0,1},{1,0},{2,3},{3,2},{4,5},{5,4},{6,7},{7,6},{8,9},{9,8},{10,11... | collective-permute-start | bytes 786440 | tf_op jit(solution)/shard_map/ppermute | solution.py:233
  78.2 14.4 %collective-permute-start.18 = (bf16[2,128,1024]{2,1,0:T(8,128)(2,1)}, bf16[2,128,1024]{2,1,0:T(8,128)(2,1)}, u32[]{:S(2)}, u32[]{:S(2)}) collective-permute-start(bf16[2,128,1024]{2,1,0:T(8,128)(2,1)} %collective-permute-done.17.refs_5_), channel_id=1, source_target_pairs={{0,1},{1,0},{2,3},{3,2},{4,5},{5,4},{6,7},{7,6},{8,9},{9,8},{10,11... | collective-permute-start | bytes 1572872 | tf_op jit(solution)/shard_map/ppermute | solution.py:625
  78.6 20.9 %collective-permute-start.23 = (bf16[2176,128]{1,0:T(8,128)(2,1)}, bf16[2176,128]{1,0:T(8,128)(2,1)}, u32[]{:S(2)}, u32[]{:S(2)}) collective-permute-start(bf16[2176,128]{1,0:T(8,128)(2,1)} %get-tuple-element.75), channel_id=1, source_target_pairs={{5,7},{2,4},{3,6},{13,15},{10,12},{11,14},{21,23},{18,20},{19,22},... | collective-permute-start | bytes 1671176 | tf_op jit(solution)/shard_map/ppermute | solution.py:674
  82.7 0.7 copy-start.2
  85.1 23.5 %collective-permute-start.16 = (f32[512,128]{1,0:T(8,128)}, f32[512,128]{1,0:T(8,128)}, u32[]{:S(2)}, u32[]{:S(2)}) collective-permute-start(f32[512,128]{1,0:T(8,128)} %multiply_add_fusion.1), channel_id=1, source_target_pairs={{1,7},{9,15},{17,23},{25,31}} | collective-permute-start | bytes 786440 | tf_op jit(solution)/shard_map/ppermute | solution.py:239
  86.5 22.1 %collective-permute-start.15 = (f32[512,128]{1,0:T(8,128)}, f32[512,128]{1,0:T(8,128)}, u32[]{:S(2)}, u32[]{:S(2)}) collective-permute-start(f32[512,128]{1,0:T(8,128)} %multiply_add_fusion.1), channel_id=1, source_target_pairs={{1,5},{3,7},{9,13},{11,15},{17,21},{19,23},{25,29},{27,31}} | collective-permute-start | bytes 786440 | tf_op jit(solution)/shard_map/ppermute | solution.py:239
  87.8 31.3 %collective-permute-start.14 = (f32[512,128]{1,0:T(8,128)}, f32[512,128]{1,0:T(8,128)}, u32[]{:S(2)}, u32[]{:S(2)}) collective-permute-start(f32[512,128]{1,0:T(8,128)} %multiply_add_fusion.1), channel_id=1, source_target_pairs={{1,3},{3,5},{5,7},{9,11},{11,13},{13,15},{17,19},{19,21},{21,23},{... | collective-permute-start | bytes 786440 | tf_op jit(solution)/shard_map/ppermute | solution.py:239
  97.4 37.5 %collective-permute-start.22 = (bf16[2176,128]{1,0:T(8,128)(2,1)}, bf16[2176,128]{1,0:T(8,128)(2,1)}, u32[]{:S(2)}, u32[]{:S(2)}) collective-permute-start(bf16[2176,128]{1,0:T(8,128)(2,1)} %get-tuple-element.84), channel_id=1, source_target_pairs={{5,7},{2,4},{3,6},{13,15},{10,12},{11,14},{21,23},{18,20},{19,22},... | collective-permute-start | bytes 1671176 | tf_op jit(solution)/shard_map/ppermute | solution.py:674
  99.5 30.1 %collective-permute-start.25 = (bf16[2176,128]{1,0:T(8,128)(2,1)}, bf16[2176,128]{1,0:T(8,128)(2,1)}, u32[]{:S(2)}, u32[]{:S(2)}) collective-permute-start(bf16[2176,128]{1,0:T(8,128)(2,1)} %collective-permute-done.19.refs_7_.refs_0_), channel_id=1, source_target_pairs={{0,1},{1,0},{2,3},{3,2},{4,5},{5,4},{6,7},{7,6},{8,9},{9,8},{10,11... | collective-permute-start | bytes 1671176 | tf_op jit(solution)/shard_map/ppermute | solution.py:599
  108.6 23.6 %collective-permute-start.24 = (bf16[2176,128]{1,0:T(8,128)(2,1)}, bf16[2176,128]{1,0:T(8,128)(2,1)}, u32[]{:S(2)}, u32[]{:S(2)}) collective-permute-start(bf16[2176,128]{1,0:T(8,128)(2,1)} %collective-permute-done.23.refs_0_), channel_id=1, source_target_pairs={{0,1},{1,0},{2,3},{3,2},{4,5},{5,4},{6,7},{7,6},{8,9},{9,8},{10,11... | collective-permute-start | bytes 1671176 | tf_op jit(solution)/shard_map/ppermute | solution.py:599
  120.3 0.7 copy-start.1
  121.0 1.5 %collective-permute-start.21 = (f32[512,128]{1,0:T(8,128)S(1)}, f32[512,128]{1,0:T(8,128)S(1)}, u32[]{:S(2)}, u32[]{:S(2)}) collective-permute-start(f32[512,128]{1,0:T(8,128)S(1)} %multiply_add_fusion.enter_ref), channel_id=1, source_target_pairs={{0,1},{1,0},{2,3},{3,2},{4,5},{5,4},{6,7},{7,6},{8,9},{9,8},{10,11... | collective-permute-start | bytes 786440 | tf_op jit(solution)/shard_map/ppermute | solution.py:244
  122.6 0.7 copy-start.3
  134.9 2.4 %collective-permute-start.26 = (bf16[2176,128]{1,0:T(8,128)(2,1)}, bf16[2176,128]{1,0:T(8,128)(2,1)}, u32[]{:S(2)}, u32[]{:S(2)}) collective-permute-start(bf16[2176,128]{1,0:T(8,128)(2,1)} %collective-permute-done.22.refs_0_), channel_id=1, source_target_pairs={{0,1},{1,0},{2,3},{3,2},{4,5},{5,4},{6,7},{7,6},{8,9},{9,8},{10,11... | collective-permute-start | bytes 1671176 | tf_op jit(solution)/shard_map/ppermute | solution.py:599

commit v9 on v6

--- a/solution.py
+++ b/solution.py
@@ -27,7 +27,7 @@
 
 def cost(microseconds):
     return pl.CostEstimate(
-        flops=microseconds * 10**8, bytes_accessed=2**16, transcendentals=0
+        flops=microseconds * 10**9, bytes_accessed=2**20, transcendentals=0
     )
 
 
@@ -191,7 +191,7 @@
             name="conv_pack",
         )(decay_rate.T, residue.T, hyena_q, hyena_k, hyena_v)
         rim = lax.ppermute(rim, "ctx", [(index, index + 1) for index in range(devices - 1)])
-        own_par = after(own_par, rim, token)
+        own_par = after(own_par, rim)
         par = lax.all_to_all(own_par, "ctx", split_axis=0, concat_axis=0, tiled=True)
         par = par.reshape(devices * par_rows, LANES)
         state_spec = pl.BlockSpec((SUBLANES * modes, LANES), lambda group: (group, 0))
@@ -210,7 +210,7 @@
             cost_estimate=cost(9),
             name="conv_state",
         )(hyena_k, hyena_v, rim, par, short_filter)
-        return local_result, rim, par, decay, *entering_state(state, decay)
+        return local_result, rim, par, decay, state
 
     def entering_state(state, decay):
         swap = [(index, index ^ 1) for index in range(devices)]
@@ -230,7 +230,9 @@
             reach *= 2
         return entering, lax.ppermute(entering, "ctx", swap), other
 
-    def last_part(local_result, rim, par, decay, entering, entering_first, other):
+    def last_part(local_result, rim, par, decay, state, last_token):
+        entering, entering_first, other = entering_state(state, decay)
+        entering = after(entering, last_token)
         state_spec = pl.BlockSpec((SUBLANES * modes, LANES), lambda group: (group, 0))
         return pl.pallas_call(
             functools.partial(output_kernel, modes),
@@ -557,7 +559,7 @@
     def send(chunk):
         key_pack = key_packs[chunk]
         if chunk >= LAG:
-            key_pack = after(key_pack, quad_kv[chunk - LAG][0], all_answers[chunk - LAG][0])
+            key_pack = after(key_pack, quad_kv[chunk - LAG][0], *all_answers[chunk - LAG][:1])
         quad_kv.append([lax.ppermute(key_pack, "ctx", gathers)])
         if chunk < asked:
             query_pack = query_packs[chunk]
@@ -575,6 +577,8 @@
         if chunk == 0:
             quad_kv[0] = [after(quad_kv[0][0], local_result)]
             asks[0] = [after(asked, local_result) for asked in asks[0]]
+        else:
+            quad_kv[chunk] = [after(quad_kv[chunk][0], all_answers[-1][0])]
         quad_kv[chunk].append(lax.ppermute(quad_kv[chunk][0], "ctx", swap))
         steps, first = CHUNK_STEPS[chunk], first_steps[chunk]
         whole_spec = pl.BlockSpec((rows, step_width), lambda step, first=first: (0, first + step))
@@ -628,13 +632,15 @@
         returned.append([own, lse, arrivals])
         if chunk + LAG < chunks:
             send(chunk + LAG)
-    conv_shared = [after(part, all_answers[-1][0]) for part in conv_shared]
-    hyena_out = conv_last(local_result, *conv_shared)
+    tokens = [all_answers[-1][0]]
+    hyena_out = conv_last(local_result, *conv_shared, *tokens)
     for chunk, (own, lse, arrivals) in enumerate(returned):
         parts = [own, lse]
         for arrival in arrivals:
             if chunk == chunks - 1:
                 arrival = after(arrival, hyena_out, result)
+            elif chunk == chunks - 2:
+                arrival = after(arrival, hyena_out)
             parts += [arrival, lax.ppermute(arrival, "ctx", swap)]
         steps = CHUNK_STEPS[chunk]
         count = 2 * len(transfers)

time: 134 us -> 142 us (1.060)
  the two profiles are of different devices: /device:TPU:29 before, /device:TPU:17 now
where the time goes in v9:
time: 142 us; the launch traced here: 141 us
  starting transfers between devices  55.2 us (39%)
  Pallas kernels  47.8 us (34%)
  waiting for transfers between devices  31.1 us (22%)
  other arithmetic  4.71 us (3%)
    pallas_call x4, Pallas kernels, attend(): pl.pallas_call(functools.partial(partial_kernel, transfers, upper, natura...  19.1 us
    ppermute x4, starting transfers between devices, attend(): arrivals.append(lax.ppermute(answer, 'ctx', moves))  16.2 us
    ppermute x4, starting transfers between devices, attend(): quad_kv[chunk].append(lax.ppermute(quad_kv[chunk][0], 'ctx', swap))  13 us
    pallas_call x4, Pallas kernels, attend(): pl.pallas_call(functools.partial(merge_kernel, transfers, steps, starts[c...  10.6 us
    ppermute x2, waiting for transfers between devices, entering_state(): arrived = lax.ppermute(total, 'ctx', moves)  10.1 us
    pallas_call x1, Pallas kernels, first_part(): pl.pallas_call(functools.partial(state_kernel, modes), grid=(groups,), in...  9.65 us
    all_to_all x1, waiting for transfers between devices, first_part(): lax.all_to_all(own_par, 'ctx', split_axis=0, concat_axis=0, tiled=True)  8.53 us
    pallas_call x1, Pallas kernels, last_part(): pl.pallas_call(functools.partial(output_kernel, modes), grid=(groups,), i...  6.3 us
  transfers between devices with their start and end apart: 27, of which 9 were waited for; matrix products, arithmetic and copies ran while one was open for 3% of the time, Pallas kernels for 32%

profile of v9, /device:TPU:17, one launch (start us, length us, event | category | flops | bytes accessed | tf_op | source)
XLA Modules:
  0.0 140.5 jit_solution(6827669367449637765)
XLA Ops:
  0.6 0.7 collective-permute-start.6
  1.4 1.9 %conv_pack.1 = (f32[8,128,128]{2,1,0:T(8,128)}, f32[8,4096]{1,0:T(8,128)}) custom-call(f32[16,512]{1,0:T(8,128)} %bitcast.3, f32[16,512]{1,0:T(8,128)} %bitcast.4, bf16[128,4096]{1,0:T(8,128)(2,1)} %q_ref.5, bf16[128,4096]{1,0:T(8,128)(2,1)} %k_ref.4, bf16[128,4096]{1,0:T(8,128)(2,1)} %v_ref.4), custom_call_target="tpu_custom_call" | custom-call | flops 1000000000 | bytes 1048576 | tf_op jit(solution)/shard_map/conv_pack/pallas_call | solution.py:176
  3.3 3.1 %collective-permute-start = (f32[8,4096]{1,0:T(8,128)}, f32[8,4096]{1,0:T(8,128)S(1)}, u32[]{:S(2)}, u32[]{:S(2)}) collective-permute-start(f32[8,4096]{1,0:T(8,128)} %get-tuple-element.40), channel_id=1, source_target_pairs={{0,1},{1,2},{2,3},{3,4},{4,5},{5,6},{6,7},{8,9},{9,10},{10,11},{11... | collective-permute-start | bytes 393224 | tf_op jit(solution)/shard_map/ppermute | solution.py:193
  6.4 2.2 %collective-permute-done.rim_ref = f32[8,4096]{1,0:T(8,128)S(1)} collective-permute-done((f32[8,4096]{1,0:T(8,128)}, f32[8,4096]{1,0:T(8,128)S(1)}, u32[]{:S(2)}, u32[]{:S(2)}) %collective-permute-start) | collective-permute-done | bytes 131104 | tf_op jit(solution)/shard_map/ppermute | solution.py:193
  8.7 6.0 %all-to-all-start = ((f32[8,128,128]{2,1,0:T(8,128)}), f32[8,128,128]{2,1,0:T(8,128)}, u32[]{:S(2)}, u32[]{:S(2)}) async-start(f32[8,128,128]{2,1,0:T(8,128)} %get-tuple-element.42), calls=%async_computation | async-start | bytes 1048576 | tf_op jit(solution)/shard_map/all_to_all | solution.py:195
  14.7 0.4 collective-permute-start.4
  15.0 0.1 collective-permute-start.5
  15.2 0.1 att_pack.1
  15.3 1.5 %collective-permute-start.8 = (bf16[2,128,1024]{2,1,0:T(8,128)(2,1)}, bf16[2,128,1024]{2,1,0:T(8,128)(2,1)}, u32[]{:S(2)}, u32[]{:S(2)}) collective-permute-start(bf16[2,128,1024]{2,1,0:T(8,128)(2,1)} %get-tuple-element.48), channel_id=1, source_target_pairs={{0,2},{1,3},{8,10},{9,11},{16,18},{17,19},{24,26},{25,27}} | collective-permute-start | bytes 1572872 | tf_op jit(solution)/shard_map/ppermute | solution.py:563
  16.8 1.3 collective-permute-start.10
  18.1 8.5 %all-to-all-done = f32[8,128,128]{2,1,0:T(8,128)} async-done(((f32[8,128,128]{2,1,0:T(8,128)}), f32[8,128,128]{2,1,0:T(8,128)}, u32[]{:S(2)}, u32[]{:S(2)}) %all-to-all-start) | async-done | bytes 524320 | tf_op jit(solution)/shard_map/all_to_all | solution.py:195
  26.6 9.7 %conv_state.1 = (f32[128,4096]{1,0:T(8,128)}, f32[512,128]{1,0:T(8,128)}, f32[512,128]{1,0:T(8,128)}) custom-call(bf16[128,4096]{1,0:T(8,128)(2,1)} %k_ref.4, bf16[128,4096]{1,0:T(8,128)(2,1)} %v_ref.4, f32[8,4096]{1,0:T(8,128)} %copy-done.1, f32[1024,128]{1,0:T(8,128)} %bitcast.2.par_ref, f32[3,3,4096]{2,1,0:T(4,128)} %taps_ref.3), custom_call_target="tpu_custom_call" | custom-call | flops 8999999488 | bytes 1048576 | tf_op jit(solution)/shard_map/conv_state/pallas_call | solution.py:198
  36.3 1.8 %collective-permute-start.9 = (bf16[2,128,1024]{2,1,0:T(8,128)(2,1)}, bf16[2,128,1024]{2,1,0:T(8,128)(2,1)}, u32[]{:S(2)}, u32[]{:S(2)}) collective-permute-start(bf16[2,128,1024]{2,1,0:T(8,128)(2,1)} %collective-permute-done.8.refs_5_), channel_id=1, source_target_pairs={{0,1},{1,0},{2,3},{3,2},{4,5},{5,4},{6,7},{7,6},{8,9},{9,8},{10,11... | collective-permute-start | bytes 1572872 | tf_op jit(solution)/shard_map/ppermute | solution.py:582
  38.1 1.5 %collective-permute-start.7 = (bf16[2,128,1024]{2,1,0:T(8,128)(2,1)}, bf16[2,128,1024]{2,1,0:T(8,128)(2,1)}, u32[]{:S(2)}, u32[]{:S(2)}) collective-permute-start(bf16[2,128,1024]{2,1,0:T(8,128)(2,1)} %get-tuple-element.47), channel_id=1, source_target_pairs={{0,2},{1,3},{8,10},{9,11},{16,18},{17,19},{24,26},{25,27}} | collective-permute-start | bytes 1572872 | tf_op jit(solution)/shard_map/ppermute | solution.py:563
  39.5 1.3 collective-permute-start.12
  40.9 4.8 %att_partial.4 = (f32[128,1024]{1,0:T(8,128)}, f32[16,128]{1,0:T(8,128)}, bf16[2176,128]{1,0:T(8,128)(2,1)}, bf16[128,4096]{1,0:T(8,128)(2,1)}) custom-call(bf16[128,4096]{1,0:T(8,128)(2,1)} %refs_0_.7, bf16[128,4096]{1,0:T(8,128)(2,1)} %refs_1_.7, bf16[128,4096]{1,0:T(8,128)(2,1)} %refs_2_.7, bf16[128,4096]{1,0:T(8,128)(2,1)} %collective-permute-done.4.refs_3_, ...), custom_call_target="tpu_custom_call" | custom-call | flops 4000000000 | bytes 1048576 | tf_op jit(solution)/shard_map/att_partial/pallas_call | solution.py:606
  45.7 1.5 %collective-permute-start.11 = (bf16[2,128,1024]{2,1,0:T(8,128)(2,1)}, bf16[2,128,1024]{2,1,0:T(8,128)(2,1)}, u32[]{:S(2)}, u32[]{:S(2)}) collective-permute-start(bf16[2,128,1024]{2,1,0:T(8,128)(2,1)} %collective-permute-done.7.refs_5_), channel_id=1, source_target_pairs={{0,1},{1,0},{2,3},{3,2},{4,5},{5,4},{6,7},{7,6},{8,9},{9,8},{10,11... | collective-permute-start | bytes 1572872 | tf_op jit(solution)/shard_map/ppermute | solution.py:582
  47.2 1.5 %collective-permute-start.14 = (bf16[2,128,1024]{2,1,0:T(8,128)(2,1)}, bf16[2,128,1024]{2,1,0:T(8,128)(2,1)}, u32[]{:S(2)}, u32[]{:S(2)}) collective-permute-start(bf16[2,128,1024]{2,1,0:T(8,128)(2,1)} %get-tuple-element.59), channel_id=1, source_target_pairs={{0,2},{1,3},{8,10},{9,11},{16,18},{17,19},{24,26},{25,27}} | collective-permute-start | bytes 1572872 | tf_op jit(solution)/shard_map/ppermute | solution.py:563
  48.6 2.1 %collective-permute-start.16 = (bf16[2176,128]{1,0:T(8,128)(2,1)}, bf16[2176,128]{1,0:T(8,128)(2,1)}, u32[]{:S(2)}, u32[]{:S(2)}) collective-permute-start(bf16[2176,128]{1,0:T(8,128)(2,1)} %get-tuple-element.52), channel_id=1, source_target_pairs={{5,7},{2,4},{3,6},{7,5},{4,2},{6,3},{13,15},{10,12},{11,14},{15,13... | collective-permute-start | bytes 1671176 | tf_op jit(solution)/shard_map/ppermute | solution.py:629
  50.7 4.4 %collective-permute-done.12.refs_7_ = bf16[2,128,1024]{2,1,0:T(8,128)(2,1)} collective-permute-done((bf16[2,128,1024]{2,1,0:T(8,128)(2,1)}, bf16[2,128,1024]{2,1,0:T(8,128)(2,1)}, u32[]{:S(2)}, u32[]{:S(2)}) %collective-permute-start.12) | collective-permute-done | bytes 524320 | tf_op jit(solution)/shard_map/ppermute | solution.py:568
  55.1 4.8 %att_partial.5 = (f32[128,1024]{1,0:T(8,128)}, f32[16,128]{1,0:T(8,128)}, bf16[2176,128]{1,0:T(8,128)(2,1)}, bf16[128,4096]{1,0:T(8,128)(2,1)}) custom-call(bf16[128,4096]{1,0:T(8,128)(2,1)} %refs_0_.7, bf16[128,4096]{1,0:T(8,128)(2,1)} %refs_1_.7, bf16[128,4096]{1,0:T(8,128)(2,1)} %refs_2_.7, ...), custom_call_target="tpu_custom_call", output_to_operand_aliasing={{3}: (10, {})} | custom-call | flops 4000000000 | bytes 1048576 | tf_op jit(solution)/shard_map/att_partial/pallas_call | solution.py:606
  60.0 3.2 %collective-permute-start.15 = (bf16[2,128,1024]{2,1,0:T(8,128)(2,1)}, bf16[2,128,1024]{2,1,0:T(8,128)(2,1)}, u32[]{:S(2)}, u32[]{:S(2)}) collective-permute-start(bf16[2,128,1024]{2,1,0:T(8,128)(2,1)} %collective-permute-done.14.refs_5_), channel_id=1, source_target_pairs={{0,1},{1,0},{2,3},{3,2},{4,5},{5,4},{6,7},{7,6},{8,9},{9,8},{10,11... | collective-permute-start | bytes 1572872 | tf_op jit(solution)/shard_map/ppermute | solution.py:582
  63.2 0.1 collective-permute-start.1
  63.3 1.5 %collective-permute-start.13 = (bf16[2,128,1024]{2,1,0:T(8,128)(2,1)}, bf16[2,128,1024]{2,1,0:T(8,128)(2,1)}, u32[]{:S(2)}, u32[]{:S(2)}) collective-permute-start(bf16[2,128,1024]{2,1,0:T(8,128)(2,1)} %get-tuple-element.57), channel_id=1, source_target_pairs={{0,2},{1,3},{8,10},{9,11},{16,18},{17,19},{24,26},{25,27}} | collective-permute-start | bytes 1572872 | tf_op jit(solution)/shard_map/ppermute | solution.py:563
  64.8 0.6 collective-permute-done.1.other_ref
  65.3 0.7 copy-done
  66.1 1.8 %multiply_add_fusion.2 = f32[512,128]{1,0:T(8,128)} fusion(f32[512,128]{1,0:T(8,128)} %get-tuple-element.45, f32[512,128]{1,0:T(8,128)} %get-tuple-element.44.decay_ref, f32[512,128]{1,0:T(8,128)S(1)} %collective-permute-done.1.other_ref), kind=kLoop, calls=%fused_computation.2 | loop fusion | flops 131072 | bytes 1048576 | tf_op jit(solution)/shard_map/add | solution.py:218
  67.8 3.2 %collective-permute-start.2 = (f32[512,128]{1,0:T(8,128)}, f32[512,128]{1,0:T(8,128)}, u32[]{:S(2)}, u32[]{:S(2)}) collective-permute-start(f32[512,128]{1,0:T(8,128)} %multiply_add_fusion.2), channel_id=1, source_target_pairs={{1,3},{3,5},{5,7},{9,11},{11,13},{13,15},{17,19},{19,21},{21,23},{... | collective-permute-start | bytes 786440 | tf_op jit(solution)/shard_map/ppermute | solution.py:223
  71.0 1.9 %collective-permute-start.18 = (bf16[2176,128]{1,0:T(8,128)(2,1)}, bf16[2176,128]{1,0:T(8,128)(2,1)}, u32[]{:S(2)}, u32[]{:S(2)}) collective-permute-start(bf16[2176,128]{1,0:T(8,128)(2,1)} %get-tuple-element.56), channel_id=1, source_target_pairs={{5,7},{2,4},{3,6},{7,5},{4,2},{6,3},{13,15},{10,12},{11,14},{15,13... | collective-permute-start | bytes 1671176 | tf_op jit(solution)/shard_map/ppermute | solution.py:629
  73.0 4.8 %att_partial.6 = (f32[128,1024]{1,0:T(8,128)}, f32[16,128]{1,0:T(8,128)}, bf16[2176,128]{1,0:T(8,128)(2,1)}, bf16[128,4096]{1,0:T(8,128)(2,1)}) custom-call(bf16[128,4096]{1,0:T(8,128)(2,1)} %refs_0_.7, bf16[128,4096]{1,0:T(8,128)(2,1)} %refs_1_.7, bf16[128,4096]{1,0:T(8,128)(2,1)} %refs_2_.7, ...), custom_call_target="tpu_custom_call", output_to_operand_aliasing={{3}: (8, {})} | custom-call | flops 4000000000 | bytes 1048576 | tf_op jit(solution)/shard_map/att_partial/pallas_call | solution.py:606
  77.7 6.5 %collective-permute-start.17 = (bf16[2,128,1024]{2,1,0:T(8,128)(2,1)}, bf16[2,128,1024]{2,1,0:T(8,128)(2,1)}, u32[]{:S(2)}, u32[]{:S(2)}) collective-permute-start(bf16[2,128,1024]{2,1,0:T(8,128)(2,1)} %collective-permute-done.13.refs_5_), channel_id=1, source_target_pairs={{0,1},{1,0},{2,3},{3,2},{4,5},{5,4},{6,7},{7,6},{8,9},{9,8},{10,11... | collective-permute-start | bytes 1572872 | tf_op jit(solution)/shard_map/ppermute | solution.py:582
  84.3 1.1 multiply_add_fusion.1
  85.5 1.3 collective-permute-start.3
  86.8 10.0 %collective-permute-done.3 = f32[512,128]{1,0:T(8,128)S(1)} collective-permute-done((f32[512,128]{1,0:T(8,128)S(1)}, f32[512,128]{1,0:T(8,128)S(1)}, u32[]{:S(2)}, u32[]{:S(2)}) %collective-permute-start.3) | collective-permute-done | bytes 262176 | tf_op jit(solution)/shard_map/ppermute | solution.py:223
  96.8 1.8 %multiply_add_fusion.enter_ref = f32[512,128]{1,0:T(8,128)} fusion(f32[512,128]{1,0:T(8,128)} %collective-permute-done.2, f32[512,128]{1,0:T(8,128)S(1)} %collective-permute-done.3, f32[512,128]{1,0:T(8,128)} %get-tuple-element.44.decay_ref), kind=kLoop, calls=%fused_computation | loop fusion | flops 196608 | bytes 1048576 | tf_op jit(solution)/shard_map/add | solution.py:227
  98.6 0.5 collective-permute-start.24
  99.1 7.6 %collective-permute-start.21 = (bf16[2176,128]{1,0:T(8,128)(2,1)}, bf16[2176,128]{1,0:T(8,128)(2,1)}, u32[]{:S(2)}, u32[]{:S(2)}) collective-permute-start(bf16[2176,128]{1,0:T(8,128)(2,1)} %get-tuple-element.62), channel_id=1, source_target_pairs={{5,7},{2,4},{3,6},{13,15},{10,12},{11,14},{21,23},{18,20},{19,22},... | collective-permute-start | bytes 1671176 | tf_op jit(solution)/shard_map/ppermute | solution.py:629
  106.7 4.8 %att_partial.7 = (f32[128,1024]{1,0:T(8,128)}, f32[16,128]{1,0:T(8,128)}, bf16[2176,128]{1,0:T(8,128)(2,1)}, bf16[128,4096]{1,0:T(8,128)(2,1)}) custom-call(bf16[128,4096]{1,0:T(8,128)(2,1)} %refs_0_.7, bf16[128,4096]{1,0:T(8,128)(2,1)} %refs_1_.7, bf16[128,4096]{1,0:T(8,128)(2,1)} %refs_2_.7, ...), custom_call_target="tpu_custom_call", output_to_operand_aliasing={{3}: (8, {})} | custom-call | flops 4000000000 | bytes 1048576 | tf_op jit(solution)/shard_map/att_partial/pallas_call | solution.py:606
  111.5 6.3 %conv_output.1 = bf16[128,4096]{1,0:T(8,128)(2,1)} custom-call(bf16[128,4096]{1,0:T(8,128)(2,1)} %q_ref.5, f32[128,4096]{1,0:T(8,128)} %get-tuple-element.43.y_ref, f32[8,4096]{1,0:T(8,128)} %copy-done.1, f32[1024,128]{1,0:T(8,128)} %bitcast.2.par_ref, f32[512,128]{1,0:T(8,128)} %get-tuple-element.44.decay_ref, f32[512,128]{1,0:T(8,128)} %multiply_add_fusion.enter_ref, ...), custom_call_target="tpu_custom_call" | custom-call | flops 6000000000 | bytes 1048576 | tf_op jit(solution)/shard_map/conv_output/pallas_call | solution.py:237
  117.8 0.8 collective-permute-done.21.refs_0_
  118.6 4.6 %collective-permute-start.20 = (bf16[2176,128]{1,0:T(8,128)(2,1)}, bf16[2176,128]{1,0:T(8,128)(2,1)}, u32[]{:S(2)}, u32[]{:S(2)}) collective-permute-start(bf16[2176,128]{1,0:T(8,128)(2,1)} %get-tuple-element.65), channel_id=1, source_target_pairs={{5,7},{2,4},{3,6},{13,15},{10,12},{11,14},{21,23},{18,20},{19,22},... | collective-permute-start | bytes 1671176 | tf_op jit(solution)/shard_map/ppermute | solution.py:629
  123.2 2.6 %att_merge.4.refs_2_ = bf16[128,4096]{1,0:T(8,128)(2,1)} custom-call(f32[128,1024]{1,0:T(8,128)} %get-tuple-element.74.own_hbm, f32[16,128]{1,0:T(8,128)} %get-tuple-element.75.lse_hbm, bf16[2176,128]{1,0:T(8,128)(2,1)} %collective-permute-done.16.refs_7_.refs_0_, bf16[2176,128]{1,0:T(8,128)(2,1)} %collective-permute-done.24.refs_1_, ...), custom_call_target="tpu_custom_call", output_to_operand_aliasing={{}: (4, {})} | custom-call | flops 2000000000 | bytes 1048576 | tf_op jit(solution)/shard_map/att_merge/pallas_call | solution.py:647
  125.9 2.7 %att_merge.5.refs_2_ = bf16[128,4096]{1,0:T(8,128)(2,1)} custom-call(f32[128,1024]{1,0:T(8,128)} %get-tuple-element.72.own_hbm, f32[16,128]{1,0:T(8,128)} %get-tuple-element.73.lse_hbm, bf16[2176,128]{1,0:T(8,128)(2,1)} %collective-permute-done.18.refs_7_.refs_0_, bf16[2176,128]{1,0:T(8,128)(2,1)} %collective-permute-done.23.refs_1_, ...), custom_call_target="tpu_custom_call", output_to_operand_aliasing={{}: (4, {})} | custom-call | flops 2000000000 | bytes 1048576 | tf_op jit(solution)/shard_map/att_merge/pallas_call | solution.py:647
  128.6 2.7 %att_merge.6.refs_2_ = bf16[128,4096]{1,0:T(8,128)(2,1)} custom-call(f32[128,1024]{1,0:T(8,128)} %get-tuple-element.69.own_hbm, f32[16,128]{1,0:T(8,128)} %get-tuple-element.70.lse_hbm, bf16[2176,128]{1,0:T(8,128)(2,1)} %collective-permute-done.21.refs_0_, bf16[2176,128]{1,0:T(8,128)(2,1)} %collective-permute-done.22.refs_1_, ...), custom_call_target="tpu_custom_call", output_to_operand_aliasing={{}: (4, {})} | custom-call | flops 2000000000 | bytes 1048576 | tf_op jit(solution)/shard_map/att_merge/pallas_call | solution.py:647
  131.2 2.5 %collective-permute-done.20.refs_0_ = bf16[2176,128]{1,0:T(8,128)(2,1)} collective-permute-done((bf16[2176,128]{1,0:T(8,128)(2,1)}, bf16[2176,128]{1,0:T(8,128)(2,1)}, u32[]{:S(2)}, u32[]{:S(2)}) %collective-permute-start.20) | collective-permute-done | bytes 557088 | tf_op jit(solution)/shard_map/ppermute | solution.py:629
  133.7 2.0 %collective-permute-start.25 = (bf16[2176,128]{1,0:T(8,128)(2,1)}, bf16[2176,128]{1,0:T(8,128)(2,1)}, u32[]{:S(2)}, u32[]{:S(2)}) collective-permute-start(bf16[2176,128]{1,0:T(8,128)(2,1)} %collective-permute-done.20.refs_0_), channel_id=1, source_target_pairs={{0,1},{1,0},{2,3},{3,2},{4,5},{5,4},{6,7},{7,6},{8,9},{9,8},{10,11... | collective-permute-start | bytes 1671176 | tf_op jit(solution)/shard_map/ppermute | solution.py:644
  135.8 1.9 %collective-permute-done.25.refs_1_ = bf16[2176,128]{1,0:T(8,128)(2,1)} collective-permute-done((bf16[2176,128]{1,0:T(8,128)(2,1)}, bf16[2176,128]{1,0:T(8,128)(2,1)}, u32[]{:S(2)}, u32[]{:S(2)}) %collective-permute-start.25) | collective-permute-done | bytes 557088 | tf_op jit(solution)/shard_map/ppermute | solution.py:644
  137.7 2.6 %att_merge.7 = bf16[128,4096]{1,0:T(8,128)(2,1)} custom-call(f32[128,1024]{1,0:T(8,128)} %get-tuple-element.67.own_hbm, f32[16,128]{1,0:T(8,128)} %get-tuple-element.68.lse_hbm, bf16[2176,128]{1,0:T(8,128)(2,1)} %collective-permute-done.20.refs_0_, bf16[2176,128]{1,0:T(8,128)(2,1)} %collective-permute-done.25.refs_1_, ...), custom_call_target="tpu_custom_call", output_to_operand_aliasing={{}: (4, {})} | custom-call | flops 2000000000 | bytes 1048576 | tf_op jit(solution)/shard_map/att_merge/pallas_call | solution.py:647
  (25 shorter events, 0.1 us)
Async XLA Ops:
  0.6 14.6 %collective-permute-start.6 = (bf16[128,4096]{1,0:T(8,128)(2,1)}, bf16[128,4096]{1,0:T(8,128)(2,1)}, u32[]{:S(2)}, u32[]{:S(2)}) collective-permute-start(bf16[128,4096]{1,0:T(8,128)(2,1)} %refs_0_.7), channel_id=1, source_target_pairs={{0,1},{1,0},{2,3},{3,2},{4,5},{5,4},{6,7},{7,6},{8,9},{9,8},{10,11... | collective-permute-start | bytes 3145736 | tf_op jit(solution)/shard_map/ppermute | solution.py:519
  3.3 5.3 %collective-permute-start = (f32[8,4096]{1,0:T(8,128)}, f32[8,4096]{1,0:T(8,128)S(1)}, u32[]{:S(2)}, u32[]{:S(2)}) collective-permute-start(f32[8,4096]{1,0:T(8,128)} %get-tuple-element.40), channel_id=1, source_target_pairs={{0,1},{1,2},{2,3},{3,4},{4,5},{5,6},{6,7},{8,9},{9,10},{10,11},{11... | collective-permute-start | bytes 393224 | tf_op jit(solution)/shard_map/ppermute | solution.py:193
  8.7 6.7 %copy-start.1 = (f32[8,4096]{1,0:T(8,128)}, f32[8,4096]{1,0:T(8,128)S(1)}, u32[]{:S(2)}) copy-start(f32[8,4096]{1,0:T(8,128)S(1)} %collective-permute-done.rim_ref) | copy-start | bytes 393220
  8.7 18.0 %all-to-all-start = ((f32[8,128,128]{2,1,0:T(8,128)}), f32[8,128,128]{2,1,0:T(8,128)}, u32[]{:S(2)}, u32[]{:S(2)}) async-start(f32[8,128,128]{2,1,0:T(8,128)} %get-tuple-element.42), calls=%async_computation | async-start | bytes 1048576 | tf_op jit(solution)/shard_map/all_to_all | solution.py:195
  14.7 26.2 %collective-permute-start.4 = (bf16[128,4096]{1,0:T(8,128)(2,1)}, bf16[128,4096]{1,0:T(8,128)(2,1)}, u32[]{:S(2)}, u32[]{:S(2)}) collective-permute-start(bf16[128,4096]{1,0:T(8,128)(2,1)} %refs_1_.7), channel_id=1, source_target_pairs={{0,1},{1,0},{2,3},{3,2},{4,5},{5,4},{6,7},{7,6},{8,9},{9,8},{10,11... | collective-permute-start | bytes 3145736 | tf_op jit(solution)/shard_map/ppermute | solution.py:520
  15.0 25.8 %collective-permute-start.5 = (bf16[128,4096]{1,0:T(8,128)(2,1)}, bf16[128,4096]{1,0:T(8,128)(2,1)}, u32[]{:S(2)}, u32[]{:S(2)}) collective-permute-start(bf16[128,4096]{1,0:T(8,128)(2,1)} %refs_2_.7), channel_id=1, source_target_pairs={{0,1},{1,0},{2,3},{3,2},{4,5},{5,4},{6,7},{7,6},{8,9},{9,8},{10,11... | collective-permute-start | bytes 3145736 | tf_op jit(solution)/shard_map/ppermute | solution.py:521
  15.3 20.9 %collective-permute-start.8 = (bf16[2,128,1024]{2,1,0:T(8,128)(2,1)}, bf16[2,128,1024]{2,1,0:T(8,128)(2,1)}, u32[]{:S(2)}, u32[]{:S(2)}) collective-permute-start(bf16[2,128,1024]{2,1,0:T(8,128)(2,1)} %get-tuple-element.48), channel_id=1, source_target_pairs={{0,2},{1,3},{8,10},{9,11},{16,18},{17,19},{24,26},{25,27}} | collective-permute-start | bytes 1572872 | tf_op jit(solution)/shard_map/ppermute | solution.py:563
  16.8 22.7 %collective-permute-start.10 = (bf16[2,128,1024]{2,1,0:T(8,128)(2,1)}, bf16[2,128,1024]{2,1,0:T(8,128)(2,1)}, u32[]{:S(2)}, u32[]{:S(2)}) collective-permute-start(bf16[2,128,1024]{2,1,0:T(8,128)(2,1)} %get-tuple-element.50), channel_id=1, source_target_pairs={{7,5},{4,2},{6,3},{15,13},{12,10},{14,11},{23,21},{20,18},{22,19},... | collective-permute-start | bytes 1572872 | tf_op jit(solution)/shard_map/ppermute | solution.py:568
  36.3 4.6 %collective-permute-start.9 = (bf16[2,128,1024]{2,1,0:T(8,128)(2,1)}, bf16[2,128,1024]{2,1,0:T(8,128)(2,1)}, u32[]{:S(2)}, u32[]{:S(2)}) collective-permute-start(bf16[2,128,1024]{2,1,0:T(8,128)(2,1)} %collective-permute-done.8.refs_5_), channel_id=1, source_target_pairs={{0,1},{1,0},{2,3},{3,2},{4,5},{5,4},{6,7},{7,6},{8,9},{9,8},{10,11... | collective-permute-start | bytes 1572872 | tf_op jit(solution)/shard_map/ppermute | solution.py:582
  38.1 7.6 %collective-permute-start.7 = (bf16[2,128,1024]{2,1,0:T(8,128)(2,1)}, bf16[2,128,1024]{2,1,0:T(8,128)(2,1)}, u32[]{:S(2)}, u32[]{:S(2)}) collective-permute-start(bf16[2,128,1024]{2,1,0:T(8,128)(2,1)} %get-tuple-element.47), channel_id=1, source_target_pairs={{0,2},{1,3},{8,10},{9,11},{16,18},{17,19},{24,26},{25,27}} | collective-permute-start | bytes 1572872 | tf_op jit(solution)/shard_map/ppermute | solution.py:563
  39.5 15.6 %collective-permute-start.12 = (bf16[2,128,1024]{2,1,0:T(8,128)(2,1)}, bf16[2,128,1024]{2,1,0:T(8,128)(2,1)}, u32[]{:S(2)}, u32[]{:S(2)}) collective-permute-start(bf16[2,128,1024]{2,1,0:T(8,128)(2,1)} %get-tuple-element.54), channel_id=1, source_target_pairs={{7,5},{4,2},{6,3},{15,13},{12,10},{14,11},{23,21},{20,18},{22,19},... | collective-permute-start | bytes 1572872 | tf_op jit(solution)/shard_map/ppermute | solution.py:568
  45.7 9.4 %collective-permute-start.11 = (bf16[2,128,1024]{2,1,0:T(8,128)(2,1)}, bf16[2,128,1024]{2,1,0:T(8,128)(2,1)}, u32[]{:S(2)}, u32[]{:S(2)}) collective-permute-start(bf16[2,128,1024]{2,1,0:T(8,128)(2,1)} %collective-permute-done.7.refs_5_), channel_id=1, source_target_pairs={{0,1},{1,0},{2,3},{3,2},{4,5},{5,4},{6,7},{7,6},{8,9},{9,8},{10,11... | collective-permute-start | bytes 1572872 | tf_op jit(solution)/shard_map/ppermute | solution.py:582
  47.2 12.8 %collective-permute-start.14 = (bf16[2,128,1024]{2,1,0:T(8,128)(2,1)}, bf16[2,128,1024]{2,1,0:T(8,128)(2,1)}, u32[]{:S(2)}, u32[]{:S(2)}) collective-permute-start(bf16[2,128,1024]{2,1,0:T(8,128)(2,1)} %get-tuple-element.59), channel_id=1, source_target_pairs={{0,2},{1,3},{8,10},{9,11},{16,18},{17,19},{24,26},{25,27}} | collective-permute-start | bytes 1572872 | tf_op jit(solution)/shard_map/ppermute | solution.py:563
  48.6 24.3 %collective-permute-start.16 = (bf16[2176,128]{1,0:T(8,128)(2,1)}, bf16[2176,128]{1,0:T(8,128)(2,1)}, u32[]{:S(2)}, u32[]{:S(2)}) collective-permute-start(bf16[2176,128]{1,0:T(8,128)(2,1)} %get-tuple-element.52), channel_id=1, source_target_pairs={{5,7},{2,4},{3,6},{7,5},{4,2},{6,3},{13,15},{10,12},{11,14},{15,13... | collective-permute-start | bytes 1671176 | tf_op jit(solution)/shard_map/ppermute | solution.py:629
  60.0 13.0 %collective-permute-start.15 = (bf16[2,128,1024]{2,1,0:T(8,128)(2,1)}, bf16[2,128,1024]{2,1,0:T(8,128)(2,1)}, u32[]{:S(2)}, u32[]{:S(2)}) collective-permute-start(bf16[2,128,1024]{2,1,0:T(8,128)(2,1)} %collective-permute-done.14.refs_5_), channel_id=1, source_target_pairs={{0,1},{1,0},{2,3},{3,2},{4,5},{5,4},{6,7},{7,6},{8,9},{9,8},{10,11... | collective-permute-start | bytes 1572872 | tf_op jit(solution)/shard_map/ppermute | solution.py:582
  63.2 2.1 %collective-permute-start.1 = (f32[512,128]{1,0:T(8,128)}, f32[512,128]{1,0:T(8,128)S(1)}, u32[]{:S(2)}, u32[]{:S(2)}) collective-permute-start(f32[512,128]{1,0:T(8,128)} %get-tuple-element.45), channel_id=1, source_target_pairs={{0,1},{1,0},{2,3},{3,2},{4,5},{5,4},{6,7},{7,6},{8,9},{9,8},{10,11... | collective-permute-start | bytes 786440 | tf_op jit(solution)/shard_map/ppermute | solution.py:217
  63.3 14.4 %collective-permute-start.13 = (bf16[2,128,1024]{2,1,0:T(8,128)(2,1)}, bf16[2,128,1024]{2,1,0:T(8,128)(2,1)}, u32[]{:S(2)}, u32[]{:S(2)}) collective-permute-start(bf16[2,128,1024]{2,1,0:T(8,128)(2,1)} %get-tuple-element.57), channel_id=1, source_target_pairs={{0,2},{1,3},{8,10},{9,11},{16,18},{17,19},{24,26},{25,27}} | collective-permute-start | bytes 1572872 | tf_op jit(solution)/shard_map/ppermute | solution.py:563
  65.3 0.7 copy-start
  67.8 16.5 %collective-permute-start.2 = (f32[512,128]{1,0:T(8,128)}, f32[512,128]{1,0:T(8,128)}, u32[]{:S(2)}, u32[]{:S(2)}) collective-permute-start(f32[512,128]{1,0:T(8,128)} %multiply_add_fusion.2), channel_id=1, source_target_pairs={{1,3},{3,5},{5,7},{9,11},{11,13},{13,15},{17,19},{19,21},{21,23},{... | collective-permute-start | bytes 786440 | tf_op jit(solution)/shard_map/ppermute | solution.py:223
  71.0 35.7 %collective-permute-start.18 = (bf16[2176,128]{1,0:T(8,128)(2,1)}, bf16[2176,128]{1,0:T(8,128)(2,1)}, u32[]{:S(2)}, u32[]{:S(2)}) collective-permute-start(bf16[2176,128]{1,0:T(8,128)(2,1)} %get-tuple-element.56), channel_id=1, source_target_pairs={{5,7},{2,4},{3,6},{7,5},{4,2},{6,3},{13,15},{10,12},{11,14},{15,13... | collective-permute-start | bytes 1671176 | tf_op jit(solution)/shard_map/ppermute | solution.py:629
  77.7 29.0 %collective-permute-start.17 = (bf16[2,128,1024]{2,1,0:T(8,128)(2,1)}, bf16[2,128,1024]{2,1,0:T(8,128)(2,1)}, u32[]{:S(2)}, u32[]{:S(2)}) collective-permute-start(bf16[2,128,1024]{2,1,0:T(8,128)(2,1)} %collective-permute-done.13.refs_5_), channel_id=1, source_target_pairs={{0,1},{1,0},{2,3},{3,2},{4,5},{5,4},{6,7},{7,6},{8,9},{9,8},{10,11... | collective-permute-start | bytes 1572872 | tf_op jit(solution)/shard_map/ppermute | solution.py:582
  85.5 11.3 %collective-permute-start.3 = (f32[512,128]{1,0:T(8,128)S(1)}, f32[512,128]{1,0:T(8,128)S(1)}, u32[]{:S(2)}, u32[]{:S(2)}) collective-permute-start(f32[512,128]{1,0:T(8,128)S(1)} %multiply_add_fusion.1), channel_id=1, source_target_pairs={{1,5},{3,7},{9,13},{11,15},{17,21},{19,23},{25,29},{27,31}} | collective-permute-start | bytes 786440 | tf_op jit(solution)/shard_map/ppermute | solution.py:223
  98.6 12.9 %collective-permute-start.19 = (f32[512,128]{1,0:T(8,128)}, f32[512,128]{1,0:T(8,128)}, u32[]{:S(2)}, u32[]{:S(2)}) collective-permute-start(f32[512,128]{1,0:T(8,128)} %multiply_add_fusion.enter_ref), channel_id=1, source_target_pairs={{0,1},{1,0},{2,3},{3,2},{4,5},{5,4},{6,7},{7,6},{8,9},{9,8},{10,11... | collective-permute-start | bytes 786440 | tf_op jit(solution)/shard_map/ppermute | solution.py:231
  98.6 24.6 %collective-permute-start.24 = (bf16[2176,128]{1,0:T(8,128)(2,1)}, bf16[2176,128]{1,0:T(8,128)(2,1)}, u32[]{:S(2)}, u32[]{:S(2)}) collective-permute-start(bf16[2176,128]{1,0:T(8,128)(2,1)} %collective-permute-done.16.refs_7_.refs_0_), channel_id=1, source_target_pairs={{0,1},{1,0},{2,3},{3,2},{4,5},{5,4},{6,7},{7,6},{8,9},{9,8},{10,11... | collective-permute-start | bytes 1671176 | tf_op jit(solution)/shard_map/ppermute | solution.py:644
  99.1 19.5 %collective-permute-start.21 = (bf16[2176,128]{1,0:T(8,128)(2,1)}, bf16[2176,128]{1,0:T(8,128)(2,1)}, u32[]{:S(2)}, u32[]{:S(2)}) collective-permute-start(bf16[2176,128]{1,0:T(8,128)(2,1)} %get-tuple-element.62), channel_id=1, source_target_pairs={{5,7},{2,4},{3,6},{13,15},{10,12},{11,14},{21,23},{18,20},{19,22},... | collective-permute-start | bytes 1671176 | tf_op jit(solution)/shard_map/ppermute | solution.py:629
  106.7 19.2 %collective-permute-start.23 = (bf16[2176,128]{1,0:T(8,128)(2,1)}, bf16[2176,128]{1,0:T(8,128)(2,1)}, u32[]{:S(2)}, u32[]{:S(2)}) collective-permute-start(bf16[2176,128]{1,0:T(8,128)(2,1)} %collective-permute-done.18.refs_7_.refs_0_), channel_id=1, source_target_pairs={{0,1},{1,0},{2,3},{3,2},{4,5},{5,4},{6,7},{7,6},{8,9},{9,8},{10,11... | collective-permute-start | bytes 1671176 | tf_op jit(solution)/shard_map/ppermute | solution.py:644
  118.6 10.0 %collective-permute-start.22 = (bf16[2176,128]{1,0:T(8,128)(2,1)}, bf16[2176,128]{1,0:T(8,128)(2,1)}, u32[]{:S(2)}, u32[]{:S(2)}) collective-permute-start(bf16[2176,128]{1,0:T(8,128)(2,1)} %collective-permute-done.21.refs_0_), channel_id=1, source_target_pairs={{0,1},{1,0},{2,3},{3,2},{4,5},{5,4},{6,7},{7,6},{8,9},{9,8},{10,11... | collective-permute-start | bytes 1671176 | tf_op jit(solution)/shard_map/ppermute | solution.py:644
  118.6 15.1 %collective-permute-start.20 = (bf16[2176,128]{1,0:T(8,128)(2,1)}, bf16[2176,128]{1,0:T(8,128)(2,1)}, u32[]{:S(2)}, u32[]{:S(2)}) collective-permute-start(bf16[2176,128]{1,0:T(8,128)(2,1)} %get-tuple-element.65), channel_id=1, source_target_pairs={{5,7},{2,4},{3,6},{13,15},{10,12},{11,14},{21,23},{18,20},{19,22},... | collective-permute-start | bytes 1671176 | tf_op jit(solution)/shard_map/ppermute | solution.py:629
  133.7 4.0 %collective-permute-start.25 = (bf16[2176,128]{1,0:T(8,128)(2,1)}, bf16[2176,128]{1,0:T(8,128)(2,1)}, u32[]{:S(2)}, u32[]{:S(2)}) collective-permute-start(bf16[2176,128]{1,0:T(8,128)(2,1)} %collective-permute-done.20.refs_0_), channel_id=1, source_target_pairs={{0,1},{1,0},{2,3},{3,2},{4,5},{5,4},{6,7},{7,6},{8,9},{9,8},{10,11... | collective-permute-start | bytes 1671176 | tf_op jit(solution)/shard_map/ppermute | solution.py:644

commit v10 on v6

--- a/solution.py
+++ b/solution.py
@@ -27,7 +27,7 @@
 
 def cost(microseconds):
     return pl.CostEstimate(
-        flops=microseconds * 10**8, bytes_accessed=2**16, transcendentals=0
+        flops=microseconds * 10**9, bytes_accessed=2**20, transcendentals=0
     )
 
 
@@ -172,7 +172,7 @@
     taps_spec = pl.BlockSpec((TAPS, TAPS, width), lambda group: (0, 0, group))
     positions = pltpu.VMEM((rows * SUBLANES, LANES), jnp.float32)
 
-    def first_part(token):
+    def first_part():
         own_par, rim = pl.pallas_call(
             conv_pack_kernel,
             grid=(1,),
@@ -191,11 +191,13 @@
             name="conv_pack",
         )(decay_rate.T, residue.T, hyena_q, hyena_k, hyena_v)
         rim = lax.ppermute(rim, "ctx", [(index, index + 1) for index in range(devices - 1)])
-        own_par = after(own_par, rim, token)
+        own_par = after(own_par, rim)
         par = lax.all_to_all(own_par, "ctx", split_axis=0, concat_axis=0, tiled=True)
-        par = par.reshape(devices * par_rows, LANES)
+        return rim, par.reshape(devices * par_rows, LANES)
+
+    def state_part(rim, par):
         state_spec = pl.BlockSpec((SUBLANES * modes, LANES), lambda group: (group, 0))
-        local_result, state, decay = pl.pallas_call(
+        return pl.pallas_call(
             functools.partial(state_kernel, modes),
             grid=(groups,),
             in_specs=[feature_spec, feature_spec, rim_spec, par_spec, taps_spec],
@@ -210,26 +212,6 @@
             cost_estimate=cost(9),
             name="conv_state",
         )(hyena_k, hyena_v, rim, par, short_filter)
-        return local_result, rim, par, decay, *entering_state(state, decay)
-
-    def entering_state(state, decay):
-        swap = [(index, index ^ 1) for index in range(devices)]
-        other = lax.ppermute(state, "ctx", swap)
-        total = state + decay * other
-        entering = None
-        reach = 1
-        while 2 * reach < devices:
-            moves = [(index, index + 2 * reach) for index in range(1, devices - 2 * reach, 2)]
-            arrived = lax.ppermute(total, "ctx", moves)
-            if reach == 1:
-                entering = arrived
-            else:
-                entering = entering + decay ** (2 * (reach - 1)) * arrived
-            if 4 * reach < devices:
-                total = total + decay ** (2 * reach) * arrived
-            reach *= 2
-        return entering, lax.ppermute(entering, "ctx", swap), other
-
     def last_part(local_result, rim, par, decay, entering, entering_first, other):
         state_spec = pl.BlockSpec((SUBLANES * modes, LANES), lambda group: (group, 0))
         return pl.pallas_call(
@@ -255,7 +237,7 @@
             short_filter,
         )
 
-    return first_part, last_part
+    return first_part, state_part, last_part
 
 
 def among(me, members):
@@ -549,33 +531,9 @@
         )(query, query_swapped, key, value)
         return outs[:chunks], outs[chunks:]
 
-    key_packs, query_packs = pack()
-    conv_first, conv_last = conv
-    local_result, *conv_shared = conv_first(query_packs[0])
-    asks, quad_kv, all_answers = {}, [], []
-
-    def send(chunk):
-        key_pack = key_packs[chunk]
-        if chunk >= LAG:
-            key_pack = after(key_pack, quad_kv[chunk - LAG][0], all_answers[chunk - LAG][0])
-        quad_kv.append([lax.ppermute(key_pack, "ctx", gathers)])
-        if chunk < asked:
-            query_pack = query_packs[chunk]
-            if chunk >= LAG:
-                query_pack = after(query_pack, *asks[chunk - LAG], all_answers[chunk - LAG][0])
-            asks[chunk] = [lax.ppermute(query_pack, "ctx", pairs) for pairs in transfers]
-
     half_rows = HEADS_PER_STEP * rows + TAIL
     hbm = pl.BlockSpec(memory_space=pl.ANY)
-    for chunk in range(min(LAG, chunks)):
-        send(chunk)
-    result = None
-    returned = []
-    for chunk in range(chunks):
-        if chunk == 0:
-            quad_kv[0] = [after(quad_kv[0][0], local_result)]
-            asks[0] = [after(asked, local_result) for asked in asks[0]]
-        quad_kv[chunk].append(lax.ppermute(quad_kv[chunk][0], "ctx", swap))
+    def partial(chunk, ask, quad, result):
         steps, first = CHUNK_STEPS[chunk], first_steps[chunk]
         whole_spec = pl.BlockSpec((rows, step_width), lambda step, first=first: (0, first + step))
         chunk_spec = pl.BlockSpec((rows, step_width), lambda step: (0, step))
@@ -585,7 +543,7 @@
         answer_shape = jax.ShapeDtypeStruct((2 * half_rows * steps, LANES), jnp.bfloat16)
         asking = both_ways and chunk + LAG < chunks
         natural = chunk < asked
-        operands = [query, key, value, key_swapped, value_swapped, *quad_kv[chunk], *asks[chunk]]
+        operands = [query, key, value, key_swapped, value_swapped, *quad, *ask]
         specs = [whole_spec] * 5 + [pair_spec] * 2
         specs += [pair_spec if natural else answer_spec] * len(transfers)
         if asking:
@@ -599,7 +557,7 @@
             aliases = {len(operands): 2 + len(transfers)}
             operands.append(result)
             specs.append(hbm)
-        own, lse, *answers, result = pl.pallas_call(
+        return pl.pallas_call(
             functools.partial(partial_kernel, transfers, upper, natural, asking, len(aliases)),
             grid=(steps,),
             in_specs=specs,
@@ -615,30 +573,11 @@
             cost_estimate=cost(4),
             name="att_partial",
         )(*operands)
-        all_answers.append(answers)
-        parts = [own, lse]
-        arrivals = []
-        for answer, pairs in zip(answers, transfers):
-            moves = [(target, source) for source, target in pairs]
-            if asking:
-                moves += pairs
-            arrivals.append(lax.ppermute(answer, "ctx", moves))
-        if asking:
-            asks[chunk + LAG] = arrivals
-        returned.append([own, lse, arrivals])
-        if chunk + LAG < chunks:
-            send(chunk + LAG)
-    conv_shared = [after(part, all_answers[-1][0]) for part in conv_shared]
-    hyena_out = conv_last(local_result, *conv_shared)
-    for chunk, (own, lse, arrivals) in enumerate(returned):
-        parts = [own, lse]
-        for arrival in arrivals:
-            if chunk == chunks - 1:
-                arrival = after(arrival, hyena_out, result)
-            parts += [arrival, lax.ppermute(arrival, "ctx", swap)]
+
+    def merge(chunk, parts, result):
         steps = CHUNK_STEPS[chunk]
         count = 2 * len(transfers)
-        result = pl.pallas_call(
+        return pl.pallas_call(
             functools.partial(merge_kernel, transfers, steps, starts[chunk]),
             in_specs=[hbm] * (len(parts) + 1),
             out_specs=hbm,
@@ -657,6 +596,85 @@
             cost_estimate=cost(2),
             name="att_merge",
         )(*parts, result)
+    def exchange(operands, ways):
+        moved = []
+        for operand, pairs in zip(operands, transfers):
+            back = [(target, source) for source, target in pairs]
+            moves = pairs if ways == 1 else back if ways == -1 else pairs + back
+            moved.append(lax.ppermute(operand, "ctx", moves))
+        return moved
+
+    def swapped(array):
+        return lax.ppermute(array, "ctx", swap)
+
+    def with_swapped(arrays):
+        return [item for array in arrays for item in (array, swapped(array))]
+
+    conv_first, conv_state, conv_last = conv
+    rim, par = conv_first()
+    key_packs, query_packs = pack()
+    rim, key_packs, query_packs = lax.optimization_barrier((rim, key_packs, query_packs))
+
+    asks = [exchange([query_packs[0]] * len(transfers), 1)]
+    quad = lax.ppermute(key_packs[0], "ctx", gathers)
+    local_result, state, decay = conv_state(rim, par)
+    live = (asks[0], quad, local_result, state, decay, key_packs[1:], query_packs[1:])
+    asks[0], quad, local_result, state, decay, key_packs, query_packs = (
+        lax.optimization_barrier(live)
+    )
+
+    other = total = entering = answers = result = None
+    hops = devices // 2 - 1
+    hop_pairs = [(index, index + 2) for index in range(1, devices - 2, 2)]
+
+    def hop(entering):
+        leaving = total if entering is None else total + decay * decay * entering
+        return lax.ppermute(leaving, "ctx", hop_pairs)
+
+    owns, waiting = [], []
+    for chunk in range(chunks):
+        last = chunk == chunks - 1
+        next_ask = next_quad = back = None
+        if not last:
+            next_quad = lax.ppermute(key_packs[chunk], "ctx", gathers)
+        if not last and chunk + 1 < asked:
+            next_ask = exchange([query_packs[chunk]] * len(transfers), 1)
+        if chunk:
+            both = next_ask is None and not last
+            back = exchange(answers, 0 if both else -1)
+            if both:
+                next_ask = back
+        if chunk == 0:
+            other = swapped(state)
+            total = state + decay * other
+        if hops:
+            entering = hop(entering)
+            hops -= 1
+        parts = with_swapped(waiting[0]) if waiting else None
+        quad_swapped = swapped(quad)
+        own, lse, *answers, result = partial(chunk, asks[chunk], (quad, quad_swapped), result)
+        owns.append([own, lse])
+        if parts:
+            result = merge(chunk - 2, owns[chunk - 2] + parts, result)
+            waiting = waiting[1:]
+        if back:
+            waiting.append(back)
+        live = (next_ask, next_quad, waiting, answers, result, total, entering, owns[chunk])
+        next_ask, quad, waiting, answers, result, total, entering, owns[chunk] = (
+            lax.optimization_barrier(live)
+        )
+        asks.append(next_ask)
+
+    back = exchange(answers, -1)
+    for _ in range(hops):
+        entering = hop(entering)
+    hyena_out = conv_last(
+        local_result, rim, par, decay, entering, swapped(entering), other
+    )
+    for chunk, arrivals in zip(range(chunks - 1 - len(waiting), chunks - 1), waiting):
+        result = merge(chunk, owns[chunk] + with_swapped(arrivals), result)
+    back, hyena_out, result = lax.optimization_barrier((back, hyena_out, result))
+    result = merge(chunks - 1, owns[-1] + with_swapped(back), result)
     return hyena_out, result
 
 

time: 134 us -> 144 us (1.075)
  the two profiles are of different devices: /device:TPU:29 before, /device:TPU:17 now
where the time goes in v10:
time: 144 us; the launch traced here: 143 us
  starting transfers between devices  51.6 us (36%)
  Pallas kernels  47.8 us (33%)
  waiting for transfers between devices  36.6 us (25%)
  other arithmetic  5.49 us (4%)
    pallas_call x4, Pallas kernels, partial(): pl.pallas_call(functools.partial(partial_kernel, transfers, upper, natura...  19.2 us
    ppermute x6, starting transfers between devices, exchange(): moved.append(lax.ppermute(operand, 'ctx', moves))  16.4 us
    ppermute x6, waiting for transfers between devices, exchange(): moved.append(lax.ppermute(operand, 'ctx', moves))  11.7 us
    ppermute x3, waiting for transfers between devices, hop(): return lax.ppermute(leaving, 'ctx', hop_pairs)  11.1 us
    pallas_call x4, Pallas kernels, merge(): pl.pallas_call(functools.partial(merge_kernel, transfers, steps, starts[c...  10.6 us
    pallas_call x1, Pallas kernels, state_part(): pl.pallas_call(functools.partial(state_kernel, modes), grid=(groups,), in...  9.68 us
    ppermute x10, starting transfers between devices, swapped(): return lax.ppermute(array, 'ctx', swap)  9.62 us
    ppermute x3, starting transfers between devices, hop(): return lax.ppermute(leaving, 'ctx', hop_pairs)  9.34 us
  transfers between devices with their start and end apart: 28, of which 9 were waited for; matrix products, arithmetic and copies ran while one was open for 4% of the time, Pallas kernels for 32%

profile of v10, /device:TPU:17, one launch (start us, length us, event | category | flops | bytes accessed | tf_op | source)
XLA Modules:
  0.0 142.5 jit_solution(14942706640006707049)
XLA Ops:
  0.6 0.7 collective-permute-start.1
  1.4 1.9 %conv_pack.1 = (f32[8,128,128]{2,1,0:T(8,128)}, f32[8,4096]{1,0:T(8,128)}) custom-call(f32[16,512]{1,0:T(8,128)} %bitcast.3, f32[16,512]{1,0:T(8,128)} %bitcast.4, bf16[128,4096]{1,0:T(8,128)(2,1)} %q_ref.5, bf16[128,4096]{1,0:T(8,128)(2,1)} %k_ref.5, bf16[128,4096]{1,0:T(8,128)(2,1)} %v_ref.5), custom_call_target="tpu_custom_call" | custom-call | flops 1000000000 | bytes 1048576 | tf_op jit(solution)/shard_map/conv_pack/pallas_call | solution.py:176
  3.3 3.1 %collective-permute-start = (f32[8,4096]{1,0:T(8,128)}, f32[8,4096]{1,0:T(8,128)S(1)}, u32[]{:S(2)}, u32[]{:S(2)}) collective-permute-start(f32[8,4096]{1,0:T(8,128)} %get-tuple-element.80), channel_id=1, source_target_pairs={{0,1},{1,2},{2,3},{3,4},{4,5},{5,6},{6,7},{8,9},{9,10},{10,11},{11... | collective-permute-start | bytes 393224 | tf_op jit(solution)/shard_map/ppermute | solution.py:193
  6.4 2.2 %collective-permute-done.rim_ref = f32[8,4096]{1,0:T(8,128)S(1)} collective-permute-done((f32[8,4096]{1,0:T(8,128)}, f32[8,4096]{1,0:T(8,128)S(1)}, u32[]{:S(2)}, u32[]{:S(2)}) %collective-permute-start) | collective-permute-done | bytes 131104 | tf_op jit(solution)/shard_map/ppermute | solution.py:193
  8.7 6.0 %all-to-all-start = ((f32[8,128,128]{2,1,0:T(8,128)}), f32[8,128,128]{2,1,0:T(8,128)}, u32[]{:S(2)}, u32[]{:S(2)}) async-start(f32[8,128,128]{2,1,0:T(8,128)} %get-tuple-element.91), calls=%async_computation | async-start | bytes 1048576 | tf_op jit(solution)/shard_map/all_to_all | solution.py:195
  14.7 0.4 collective-permute-start.6
  15.0 0.1 collective-permute-start.7
  15.2 0.1 att_pack.1
  15.3 1.3 collective-permute-start.2
  16.6 1.5 %collective-permute-start.3 = (bf16[2,128,1024]{2,1,0:T(8,128)(2,1)}, bf16[2,128,1024]{2,1,0:T(8,128)(2,1)}, u32[]{:S(2)}, u32[]{:S(2)}) collective-permute-start(bf16[2,128,1024]{2,1,0:T(8,128)(2,1)} %get-tuple-element.88), channel_id=1, source_target_pairs={{0,2},{1,3},{8,10},{9,11},{16,18},{17,19},{24,26},{25,27}} | collective-permute-start | bytes 1572872 | tf_op jit(solution)/shard_map/ppermute | solution.py:619
  18.1 8.5 %all-to-all-done = f32[8,128,128]{2,1,0:T(8,128)} async-done(((f32[8,128,128]{2,1,0:T(8,128)}), f32[8,128,128]{2,1,0:T(8,128)}, u32[]{:S(2)}, u32[]{:S(2)}) %all-to-all-start) | async-done | bytes 524320 | tf_op jit(solution)/shard_map/all_to_all | solution.py:195
  26.6 9.7 %conv_state.1 = (f32[128,4096]{1,0:T(8,128)}, f32[512,128]{1,0:T(8,128)}, f32[512,128]{1,0:T(8,128)}) custom-call(bf16[128,4096]{1,0:T(8,128)(2,1)} %k_ref.5, bf16[128,4096]{1,0:T(8,128)(2,1)} %v_ref.5, f32[8,4096]{1,0:T(8,128)} %copy-done.1, f32[1024,128]{1,0:T(8,128)} %bitcast.2.par_ref, f32[3,3,4096]{2,1,0:T(4,128)} %taps_ref.3), custom_call_target="tpu_custom_call" | custom-call | flops 8999999488 | bytes 1048576 | tf_op jit(solution)/shard_map/conv_state/pallas_call | solution.py:200
  36.3 0.1 collective-permute-done.2.refs_7_
  36.4 2.0 %collective-permute-start.8 = (bf16[2,128,1024]{2,1,0:T(8,128)(2,1)}, bf16[2,128,1024]{2,1,0:T(8,128)(2,1)}, u32[]{:S(2)}, u32[]{:S(2)}) collective-permute-start(bf16[2,128,1024]{2,1,0:T(8,128)(2,1)} %collective-permute-done.3.refs_5_), channel_id=1, source_target_pairs={{0,1},{1,0},{2,3},{3,2},{4,5},{5,4},{6,7},{7,6},{8,9},{9,8},{10,11... | collective-permute-start | bytes 1572872 | tf_op jit(solution)/shard_map/ppermute | solution.py:608
  38.4 0.0 collective-permute-start.9
  38.4 1.3 collective-permute-start.4
  39.7 0.7 collective-permute-done.9.other_ref
  40.4 1.5 %collective-permute-start.5 = (bf16[2,128,1024]{2,1,0:T(8,128)(2,1)}, bf16[2,128,1024]{2,1,0:T(8,128)(2,1)}, u32[]{:S(2)}, u32[]{:S(2)}) collective-permute-start(bf16[2,128,1024]{2,1,0:T(8,128)(2,1)} %get-tuple-element.100), channel_id=1, source_target_pairs={{0,2},{1,3},{8,10},{9,11},{16,18},{17,19},{24,26},{25,27}} | collective-permute-start | bytes 1572872 | tf_op jit(solution)/shard_map/ppermute | solution.py:639
  41.8 1.8 %multiply_add_fusion.2 = f32[512,128]{1,0:T(8,128)} fusion(f32[512,128]{1,0:T(8,128)} %get-tuple-element.105, f32[512,128]{1,0:T(8,128)} %get-tuple-element.106.decay_ref, f32[512,128]{1,0:T(8,128)S(1)} %collective-permute-done.9.other_ref), kind=kLoop, calls=%fused_computation.2 | loop fusion | flops 131072 | bytes 1048576 | tf_op jit(solution)/shard_map/add | solution.py:649
  43.6 4.1 %collective-permute-start.10 = (f32[512,128]{1,0:T(8,128)}, f32[512,128]{1,0:T(8,128)}, u32[]{:S(2)}, u32[]{:S(2)}) collective-permute-start(f32[512,128]{1,0:T(8,128)} %multiply_add_fusion.2), channel_id=1, source_target_pairs={{1,3},{3,5},{5,7},{9,11},{11,13},{13,15},{17,19},{19,21},{21,23},{... | collective-permute-start | bytes 786440 | tf_op jit(solution)/shard_map/ppermute | solution.py:632
  47.7 4.8 %att_partial.4 = (f32[128,1024]{1,0:T(8,128)}, f32[16,128]{1,0:T(8,128)}, bf16[2176,128]{1,0:T(8,128)(2,1)}, bf16[128,4096]{1,0:T(8,128)(2,1)}) custom-call(bf16[128,4096]{1,0:T(8,128)(2,1)} %refs_0_.7, bf16[128,4096]{1,0:T(8,128)(2,1)} %refs_1_.7, bf16[128,4096]{1,0:T(8,128)(2,1)} %refs_2_.7, bf16[128,4096]{1,0:T(8,128)(2,1)} %collective-permute-done.6.refs_3_, ...), custom_call_target="tpu_custom_call" | custom-call | flops 4000000000 | bytes 1048576 | tf_op jit(solution)/shard_map/att_partial/pallas_call | solution.py:560
  52.6 3.3 %collective-permute-start.13 = (bf16[2,128,1024]{2,1,0:T(8,128)(2,1)}, bf16[2,128,1024]{2,1,0:T(8,128)(2,1)}, u32[]{:S(2)}, u32[]{:S(2)}) collective-permute-start(bf16[2,128,1024]{2,1,0:T(8,128)(2,1)} %collective-permute-done.5.refs_5_), channel_id=1, source_target_pairs={{0,1},{1,0},{2,3},{3,2},{4,5},{5,4},{6,7},{7,6},{8,9},{9,8},{10,11... | collective-permute-start | bytes 1572872 | tf_op jit(solution)/shard_map/ppermute | solution.py:608
  55.9 1.5 %collective-permute-start.12 = (bf16[2,128,1024]{2,1,0:T(8,128)(2,1)}, bf16[2,128,1024]{2,1,0:T(8,128)(2,1)}, u32[]{:S(2)}, u32[]{:S(2)}) collective-permute-start(bf16[2,128,1024]{2,1,0:T(8,128)(2,1)} %get-tuple-element.110), channel_id=1, source_target_pairs={{0,2},{1,3},{8,10},{9,11},{16,18},{17,19},{24,26},{25,27}} | collective-permute-start | bytes 1572872 | tf_op jit(solution)/shard_map/ppermute | solution.py:639
  57.3 1.9 %collective-permute-start.11 = (bf16[2176,128]{1,0:T(8,128)(2,1)}, bf16[2176,128]{1,0:T(8,128)(2,1)}, u32[]{:S(2)}, u32[]{:S(2)}) collective-permute-start(bf16[2176,128]{1,0:T(8,128)(2,1)} %get-tuple-element.109), channel_id=1, source_target_pairs={{7,5},{4,2},{6,3},{5,7},{2,4},{3,6},{15,13},{12,10},{14,11},{13,15... | collective-permute-start | bytes 1671176 | tf_op jit(solution)/shard_map/ppermute | solution.py:604
  59.3 1.9 %multiply_add_fusion.1 = f32[512,128]{1,0:T(8,128)} fusion(f32[512,128]{1,0:T(8,128)} %multiply_add_fusion.2, f32[512,128]{1,0:T(8,128)} %collective-permute-done.10, f32[512,128]{1,0:T(8,128)} %get-tuple-element.106.decay_ref), kind=kLoop, calls=%fused_computation.1 | loop fusion | flops 196608 | bytes 1048576 | tf_op jit(solution)/shard_map/add | solution.py:631
  61.1 3.4 %collective-permute-start.14 = (f32[512,128]{1,0:T(8,128)}, f32[512,128]{1,0:T(8,128)}, u32[]{:S(2)}, u32[]{:S(2)}) collective-permute-start(f32[512,128]{1,0:T(8,128)} %multiply_add_fusion.1), channel_id=1, source_target_pairs={{1,3},{3,5},{5,7},{9,11},{11,13},{13,15},{17,19},{19,21},{21,23},{... | collective-permute-start | bytes 786440 | tf_op jit(solution)/shard_map/ppermute | solution.py:632
  64.5 4.8 %att_partial.5 = (f32[128,1024]{1,0:T(8,128)}, f32[16,128]{1,0:T(8,128)}, bf16[2176,128]{1,0:T(8,128)(2,1)}, bf16[128,4096]{1,0:T(8,128)(2,1)}) custom-call(bf16[128,4096]{1,0:T(8,128)(2,1)} %refs_0_.7, bf16[128,4096]{1,0:T(8,128)(2,1)} %refs_1_.7, bf16[128,4096]{1,0:T(8,128)(2,1)} %refs_2_.7, ...), custom_call_target="tpu_custom_call", output_to_operand_aliasing={{3}: (10, {})} | custom-call | flops 4000000000 | bytes 1048576 | tf_op jit(solution)/shard_map/att_partial/pallas_call | solution.py:560
  69.3 11.1 %collective-permute-done.14 = f32[512,128]{1,0:T(8,128)} collective-permute-done((f32[512,128]{1,0:T(8,128)}, f32[512,128]{1,0:T(8,128)}, u32[]{:S(2)}, u32[]{:S(2)}) %collective-permute-start.14) | collective-permute-done | bytes 262176 | tf_op jit(solution)/shard_map/ppermute | solution.py:632
  80.5 1.5 %collective-permute-start.16 = (bf16[2,128,1024]{2,1,0:T(8,128)(2,1)}, bf16[2,128,1024]{2,1,0:T(8,128)(2,1)}, u32[]{:S(2)}, u32[]{:S(2)}) collective-permute-start(bf16[2,128,1024]{2,1,0:T(8,128)(2,1)} %get-tuple-element.121), channel_id=1, source_target_pairs={{0,2},{1,3},{8,10},{9,11},{16,18},{17,19},{24,26},{25,27}} | collective-permute-start | bytes 1572872 | tf_op jit(solution)/shard_map/ppermute | solution.py:639
  81.9 0.5 collective-permute-start.18
  82.4 1.9 %multiply_add_fusion = f32[512,128]{1,0:T(8,128)} fusion(f32[512,128]{1,0:T(8,128)} %multiply_add_fusion.2, f32[512,128]{1,0:T(8,128)} %collective-permute-done.14, f32[512,128]{1,0:T(8,128)} %get-tuple-element.106.decay_ref), kind=kLoop, calls=%fused_computation | loop fusion | flops 196608 | bytes 1048576 | tf_op jit(solution)/shard_map/add | solution.py:631
  84.3 1.9 %collective-permute-start.19 = (f32[512,128]{1,0:T(8,128)}, f32[512,128]{1,0:T(8,128)}, u32[]{:S(2)}, u32[]{:S(2)}) collective-permute-start(f32[512,128]{1,0:T(8,128)} %multiply_add_fusion), channel_id=1, source_target_pairs={{1,3},{3,5},{5,7},{9,11},{11,13},{13,15},{17,19},{19,21},{21,23},{... | collective-permute-start | bytes 786440 | tf_op jit(solution)/shard_map/ppermute | solution.py:632
  86.2 1.9 %collective-permute-start.15 = (bf16[2176,128]{1,0:T(8,128)(2,1)}, bf16[2176,128]{1,0:T(8,128)(2,1)}, u32[]{:S(2)}, u32[]{:S(2)}) collective-permute-start(bf16[2176,128]{1,0:T(8,128)(2,1)} %get-tuple-element.120), channel_id=1, source_target_pairs={{7,5},{4,2},{6,3},{5,7},{2,4},{3,6},{15,13},{12,10},{14,11},{13,15... | collective-permute-start | bytes 1671176 | tf_op jit(solution)/shard_map/ppermute | solution.py:604
  88.1 4.8 %att_partial.6 = (f32[128,1024]{1,0:T(8,128)}, f32[16,128]{1,0:T(8,128)}, bf16[2176,128]{1,0:T(8,128)(2,1)}, bf16[128,4096]{1,0:T(8,128)(2,1)}) custom-call(bf16[128,4096]{1,0:T(8,128)(2,1)} %refs_0_.7, bf16[128,4096]{1,0:T(8,128)(2,1)} %refs_1_.7, bf16[128,4096]{1,0:T(8,128)(2,1)} %refs_2_.7, ...), custom_call_target="tpu_custom_call", output_to_operand_aliasing={{3}: (8, {})} | custom-call | flops 4000000000 | bytes 1048576 | tf_op jit(solution)/shard_map/att_partial/pallas_call | solution.py:560
  92.9 2.7 %att_merge.4.refs_8_ = bf16[128,4096]{1,0:T(8,128)(2,1)} custom-call(f32[128,1024]{1,0:T(8,128)} %get-tuple-element.126.own_hbm, f32[16,128]{1,0:T(8,128)} %get-tuple-element.127.lse_hbm, bf16[2176,128]{1,0:T(8,128)(2,1)} %collective-permute-done.11.refs_7_.refs_0_, ...), custom_call_target="tpu_custom_call", output_to_operand_aliasing={{}: (4, {})} | custom-call | flops 2000000000 | bytes 1048576 | tf_op jit(solution)/shard_map/att_merge/pallas_call | solution.py:580
  95.6 5.6 %collective-permute-done.15.refs_7_.refs_0_ = bf16[2176,128]{1,0:T(8,128)(2,1)} collective-permute-done((bf16[2176,128]{1,0:T(8,128)(2,1)}, bf16[2176,128]{1,0:T(8,128)(2,1)}, u32[]{:S(2)}, u32[]{:S(2)}) %collective-permute-start.15) | collective-permute-done | bytes 557088 | tf_op jit(solution)/shard_map/ppermute | solution.py:604
  101.2 2.2 %collective-permute-start.21 = (bf16[2,128,1024]{2,1,0:T(8,128)(2,1)}, bf16[2,128,1024]{2,1,0:T(8,128)(2,1)}, u32[]{:S(2)}, u32[]{:S(2)}) collective-permute-start(bf16[2,128,1024]{2,1,0:T(8,128)(2,1)} %collective-permute-done.16.refs_5_), channel_id=1, source_target_pairs={{0,1},{1,0},{2,3},{3,2},{4,5},{5,4},{6,7},{7,6},{8,9},{9,8},{10,11... | collective-permute-start | bytes 1572872 | tf_op jit(solution)/shard_map/ppermute | solution.py:608
  103.4 4.8 %collective-permute-start.20 = (bf16[2176,128]{1,0:T(8,128)(2,1)}, bf16[2176,128]{1,0:T(8,128)(2,1)}, u32[]{:S(2)}, u32[]{:S(2)}) collective-permute-start(bf16[2176,128]{1,0:T(8,128)(2,1)} %get-tuple-element.134), channel_id=1, source_target_pairs={{5,7},{2,4},{3,6},{13,15},{10,12},{11,14},{21,23},{18,20},{19,22},... | collective-permute-start | bytes 1671176 | tf_op jit(solution)/shard_map/ppermute | solution.py:604
  108.2 4.8 %att_partial.7 = (f32[128,1024]{1,0:T(8,128)}, f32[16,128]{1,0:T(8,128)}, bf16[2176,128]{1,0:T(8,128)(2,1)}, bf16[128,4096]{1,0:T(8,128)(2,1)}) custom-call(bf16[128,4096]{1,0:T(8,128)(2,1)} %refs_0_.7, bf16[128,4096]{1,0:T(8,128)(2,1)} %refs_1_.7, bf16[128,4096]{1,0:T(8,128)(2,1)} %refs_2_.7, ...), custom_call_target="tpu_custom_call", output_to_operand_aliasing={{3}: (8, {})} | custom-call | flops 4000000000 | bytes 1048576 | tf_op jit(solution)/shard_map/att_partial/pallas_call | solution.py:560
  113.0 2.7 %att_merge.5.refs_2_ = bf16[128,4096]{1,0:T(8,128)(2,1)} custom-call(f32[128,1024]{1,0:T(8,128)} %get-tuple-element.139.own_hbm, f32[16,128]{1,0:T(8,128)} %get-tuple-element.140.lse_hbm, bf16[2176,128]{1,0:T(8,128)(2,1)} %collective-permute-done.15.refs_7_.refs_0_, ...), custom_call_target="tpu_custom_call", output_to_operand_aliasing={{}: (4, {})} | custom-call | flops 2000000000 | bytes 1048576 | tf_op jit(solution)/shard_map/att_merge/pallas_call | solution.py:580
  115.7 3.0 %collective-permute-done.20.refs_0_ = bf16[2176,128]{1,0:T(8,128)(2,1)} collective-permute-done((bf16[2176,128]{1,0:T(8,128)(2,1)}, bf16[2176,128]{1,0:T(8,128)(2,1)}, u32[]{:S(2)}, u32[]{:S(2)}) %collective-permute-start.20) | collective-permute-done | bytes 557088 | tf_op jit(solution)/shard_map/ppermute | solution.py:604
  118.7 1.6 %collective-permute-start.24 = (f32[512,128]{1,0:T(8,128)}, f32[512,128]{1,0:T(8,128)}, u32[]{:S(2)}, u32[]{:S(2)}) collective-permute-start(f32[512,128]{1,0:T(8,128)} %collective-permute-done.19.enter_ref), channel_id=1, source_target_pairs={{0,1},{1,0},{2,3},{3,2},{4,5},{5,4},{6,7},{7,6},{8,9},{9,8},{10,11... | collective-permute-start | bytes 786440 | tf_op jit(solution)/shard_map/ppermute | solution.py:608
  120.3 5.2 %collective-permute-start.23 = (bf16[2176,128]{1,0:T(8,128)(2,1)}, bf16[2176,128]{1,0:T(8,128)(2,1)}, u32[]{:S(2)}, u32[]{:S(2)}) collective-permute-start(bf16[2176,128]{1,0:T(8,128)(2,1)} %get-tuple-element.146), channel_id=1, source_target_pairs={{5,7},{2,4},{3,6},{13,15},{10,12},{11,14},{21,23},{18,20},{19,22},... | collective-permute-start | bytes 1671176 | tf_op jit(solution)/shard_map/ppermute | solution.py:604
  125.5 6.3 %conv_output.1 = bf16[128,4096]{1,0:T(8,128)(2,1)} custom-call(bf16[128,4096]{1,0:T(8,128)(2,1)} %q_ref.5, f32[128,4096]{1,0:T(8,128)} %get-tuple-element.147.y_ref, f32[8,4096]{1,0:T(8,128)} %copy-done.1, f32[1024,128]{1,0:T(8,128)} %bitcast.2.par_ref, f32[512,128]{1,0:T(8,128)} %get-tuple-element.106.decay_ref, ...), custom_call_target="tpu_custom_call" | custom-call | flops 6000000000 | bytes 1048576 | tf_op jit(solution)/shard_map/conv_output/pallas_call | solution.py:217
  131.8 2.7 %att_merge.6.refs_2_ = bf16[128,4096]{1,0:T(8,128)(2,1)} custom-call(f32[128,1024]{1,0:T(8,128)} %get-tuple-element.149.own_hbm, f32[16,128]{1,0:T(8,128)} %get-tuple-element.150.lse_hbm, bf16[2176,128]{1,0:T(8,128)(2,1)} %collective-permute-done.20.refs_0_, bf16[2176,128]{1,0:T(8,128)(2,1)} %collective-permute-done.25.refs_1_, ...), custom_call_target="tpu_custom_call", output_to_operand_aliasing={{}: (4, {})} | custom-call | flops 2000000000 | bytes 1048576 | tf_op jit(solution)/shard_map/att_merge/pallas_call | solution.py:580
  134.5 3.0 %collective-permute-done.23.refs_0_ = bf16[2176,128]{1,0:T(8,128)(2,1)} collective-permute-done((bf16[2176,128]{1,0:T(8,128)(2,1)}, bf16[2176,128]{1,0:T(8,128)(2,1)}, u32[]{:S(2)}, u32[]{:S(2)}) %collective-permute-start.23) | collective-permute-done | bytes 557088 | tf_op jit(solution)/shard_map/ppermute | solution.py:604
  137.4 2.3 %collective-permute-done.26.refs_1_ = bf16[2176,128]{1,0:T(8,128)(2,1)} collective-permute-done((bf16[2176,128]{1,0:T(8,128)(2,1)}, bf16[2176,128]{1,0:T(8,128)(2,1)}, u32[]{:S(2)}, u32[]{:S(2)}) %collective-permute-start.26) | collective-permute-done | bytes 557088 | tf_op jit(solution)/shard_map/ppermute | solution.py:608
  139.7 2.6 %att_merge.7 = bf16[128,4096]{1,0:T(8,128)(2,1)} custom-call(f32[128,1024]{1,0:T(8,128)} %get-tuple-element.154.own_hbm, f32[16,128]{1,0:T(8,128)} %get-tuple-element.155.lse_hbm, bf16[2176,128]{1,0:T(8,128)(2,1)} %collective-permute-done.23.refs_0_, bf16[2176,128]{1,0:T(8,128)(2,1)} %collective-permute-done.26.refs_1_, ...), custom_call_target="tpu_custom_call", output_to_operand_aliasing={{}: (4, {})} | custom-call | flops 2000000000 | bytes 1048576 | tf_op jit(solution)/shard_map/att_merge/pallas_call | solution.py:580
  (27 shorter events, 0.1 us)
Async XLA Ops:
  0.6 14.6 %collective-permute-start.1 = (bf16[128,4096]{1,0:T(8,128)(2,1)}, bf16[128,4096]{1,0:T(8,128)(2,1)}, u32[]{:S(2)}, u32[]{:S(2)}) collective-permute-start(bf16[128,4096]{1,0:T(8,128)(2,1)} %refs_0_.7), channel_id=1, source_target_pairs={{0,1},{1,0},{2,3},{3,2},{4,5},{5,4},{6,7},{7,6},{8,9},{9,8},{10,11... | collective-permute-start | bytes 3145736 | tf_op jit(solution)/shard_map/ppermute | solution.py:499
  3.3 5.3 %collective-permute-start = (f32[8,4096]{1,0:T(8,128)}, f32[8,4096]{1,0:T(8,128)S(1)}, u32[]{:S(2)}, u32[]{:S(2)}) collective-permute-start(f32[8,4096]{1,0:T(8,128)} %get-tuple-element.80), channel_id=1, source_target_pairs={{0,1},{1,2},{2,3},{3,4},{4,5},{5,6},{6,7},{8,9},{9,10},{10,11},{11... | collective-permute-start | bytes 393224 | tf_op jit(solution)/shard_map/ppermute | solution.py:193
  8.7 6.7 %copy-start.1 = (f32[8,4096]{1,0:T(8,128)}, f32[8,4096]{1,0:T(8,128)S(1)}, u32[]{:S(2)}) copy-start(f32[8,4096]{1,0:T(8,128)S(1)} %collective-permute-done.rim_ref) | copy-start | bytes 393220
  8.7 18.0 %all-to-all-start = ((f32[8,128,128]{2,1,0:T(8,128)}), f32[8,128,128]{2,1,0:T(8,128)}, u32[]{:S(2)}, u32[]{:S(2)}) async-start(f32[8,128,128]{2,1,0:T(8,128)} %get-tuple-element.91), calls=%async_computation | async-start | bytes 1048576 | tf_op jit(solution)/shard_map/all_to_all | solution.py:195
  14.7 28.9 %collective-permute-start.6 = (bf16[128,4096]{1,0:T(8,128)(2,1)}, bf16[128,4096]{1,0:T(8,128)(2,1)}, u32[]{:S(2)}, u32[]{:S(2)}) collective-permute-start(bf16[128,4096]{1,0:T(8,128)(2,1)} %refs_1_.7), channel_id=1, source_target_pairs={{0,1},{1,0},{2,3},{3,2},{4,5},{5,4},{6,7},{7,6},{8,9},{9,8},{10,11... | collective-permute-start | bytes 3145736 | tf_op jit(solution)/shard_map/ppermute | solution.py:500
  15.0 32.7 %collective-permute-start.7 = (bf16[128,4096]{1,0:T(8,128)(2,1)}, bf16[128,4096]{1,0:T(8,128)(2,1)}, u32[]{:S(2)}, u32[]{:S(2)}) collective-permute-start(bf16[128,4096]{1,0:T(8,128)(2,1)} %refs_2_.7), channel_id=1, source_target_pairs={{0,1},{1,0},{2,3},{3,2},{4,5},{5,4},{6,7},{7,6},{8,9},{9,8},{10,11... | collective-permute-start | bytes 3145736 | tf_op jit(solution)/shard_map/ppermute | solution.py:501
  15.3 21.0 %collective-permute-start.2 = (bf16[2,128,1024]{2,1,0:T(8,128)(2,1)}, bf16[2,128,1024]{2,1,0:T(8,128)(2,1)}, u32[]{:S(2)}, u32[]{:S(2)}) collective-permute-start(bf16[2,128,1024]{2,1,0:T(8,128)(2,1)} %get-tuple-element.87), channel_id=1, source_target_pairs={{7,5},{4,2},{6,3},{15,13},{12,10},{14,11},{23,21},{20,18},{22,19},... | collective-permute-start | bytes 1572872 | tf_op jit(solution)/shard_map/ppermute | solution.py:604
  16.6 19.7 %collective-permute-start.3 = (bf16[2,128,1024]{2,1,0:T(8,128)(2,1)}, bf16[2,128,1024]{2,1,0:T(8,128)(2,1)}, u32[]{:S(2)}, u32[]{:S(2)}) collective-permute-start(bf16[2,128,1024]{2,1,0:T(8,128)(2,1)} %get-tuple-element.88), channel_id=1, source_target_pairs={{0,2},{1,3},{8,10},{9,11},{16,18},{17,19},{24,26},{25,27}} | collective-permute-start | bytes 1572872 | tf_op jit(solution)/shard_map/ppermute | solution.py:619
  36.4 11.3 %collective-permute-start.8 = (bf16[2,128,1024]{2,1,0:T(8,128)(2,1)}, bf16[2,128,1024]{2,1,0:T(8,128)(2,1)}, u32[]{:S(2)}, u32[]{:S(2)}) collective-permute-start(bf16[2,128,1024]{2,1,0:T(8,128)(2,1)} %collective-permute-done.3.refs_5_), channel_id=1, source_target_pairs={{0,1},{1,0},{2,3},{3,2},{4,5},{5,4},{6,7},{7,6},{8,9},{9,8},{10,11... | collective-permute-start | bytes 1572872 | tf_op jit(solution)/shard_map/ppermute | solution.py:608
  38.4 2.0 %collective-permute-start.9 = (f32[512,128]{1,0:T(8,128)}, f32[512,128]{1,0:T(8,128)S(1)}, u32[]{:S(2)}, u32[]{:S(2)}) collective-permute-start(f32[512,128]{1,0:T(8,128)} %get-tuple-element.105), channel_id=1, source_target_pairs={{0,1},{1,0},{2,3},{3,2},{4,5},{5,4},{6,7},{7,6},{8,9},{9,8},{10,11... | collective-permute-start | bytes 786440 | tf_op jit(solution)/shard_map/ppermute | solution.py:608
  38.4 14.2 %collective-permute-start.4 = (bf16[2,128,1024]{2,1,0:T(8,128)(2,1)}, bf16[2,128,1024]{2,1,0:T(8,128)(2,1)}, u32[]{:S(2)}, u32[]{:S(2)}) collective-permute-start(bf16[2,128,1024]{2,1,0:T(8,128)(2,1)} %get-tuple-element.99), channel_id=1, source_target_pairs={{7,5},{4,2},{6,3},{15,13},{12,10},{14,11},{23,21},{20,18},{22,19},... | collective-permute-start | bytes 1572872 | tf_op jit(solution)/shard_map/ppermute | solution.py:604
  40.3 1.5 %copy-start = (f32[512,128]{1,0:T(8,128)}, f32[512,128]{1,0:T(8,128)S(1)}, u32[]{:S(2)}) copy-start(f32[512,128]{1,0:T(8,128)S(1)} %collective-permute-done.9.other_ref) | copy-start | bytes 786436
  40.4 12.2 %collective-permute-start.5 = (bf16[2,128,1024]{2,1,0:T(8,128)(2,1)}, bf16[2,128,1024]{2,1,0:T(8,128)(2,1)}, u32[]{:S(2)}, u32[]{:S(2)}) collective-permute-start(bf16[2,128,1024]{2,1,0:T(8,128)(2,1)} %get-tuple-element.100), channel_id=1, source_target_pairs={{0,2},{1,3},{8,10},{9,11},{16,18},{17,19},{24,26},{25,27}} | collective-permute-start | bytes 1572872 | tf_op jit(solution)/shard_map/ppermute | solution.py:639
  43.6 8.9 %collective-permute-start.10 = (f32[512,128]{1,0:T(8,128)}, f32[512,128]{1,0:T(8,128)}, u32[]{:S(2)}, u32[]{:S(2)}) collective-permute-start(f32[512,128]{1,0:T(8,128)} %multiply_add_fusion.2), channel_id=1, source_target_pairs={{1,3},{3,5},{5,7},{9,11},{11,13},{13,15},{17,19},{19,21},{21,23},{... | collective-permute-start | bytes 786440 | tf_op jit(solution)/shard_map/ppermute | solution.py:632
  52.6 11.9 %collective-permute-start.13 = (bf16[2,128,1024]{2,1,0:T(8,128)(2,1)}, bf16[2,128,1024]{2,1,0:T(8,128)(2,1)}, u32[]{:S(2)}, u32[]{:S(2)}) collective-permute-start(bf16[2,128,1024]{2,1,0:T(8,128)(2,1)} %collective-permute-done.5.refs_5_), channel_id=1, source_target_pairs={{0,1},{1,0},{2,3},{3,2},{4,5},{5,4},{6,7},{7,6},{8,9},{9,8},{10,11... | collective-permute-start | bytes 1572872 | tf_op jit(solution)/shard_map/ppermute | solution.py:608
  55.9 13.5 %collective-permute-start.12 = (bf16[2,128,1024]{2,1,0:T(8,128)(2,1)}, bf16[2,128,1024]{2,1,0:T(8,128)(2,1)}, u32[]{:S(2)}, u32[]{:S(2)}) collective-permute-start(bf16[2,128,1024]{2,1,0:T(8,128)(2,1)} %get-tuple-element.110), channel_id=1, source_target_pairs={{0,2},{1,3},{8,10},{9,11},{16,18},{17,19},{24,26},{25,27}} | collective-permute-start | bytes 1572872 | tf_op jit(solution)/shard_map/ppermute | solution.py:639
  57.3 23.1 %collective-permute-start.11 = (bf16[2176,128]{1,0:T(8,128)(2,1)}, bf16[2176,128]{1,0:T(8,128)(2,1)}, u32[]{:S(2)}, u32[]{:S(2)}) collective-permute-start(bf16[2176,128]{1,0:T(8,128)(2,1)} %get-tuple-element.109), channel_id=1, source_target_pairs={{7,5},{4,2},{6,3},{5,7},{2,4},{3,6},{15,13},{12,10},{14,11},{13,15... | collective-permute-start | bytes 1671176 | tf_op jit(solution)/shard_map/ppermute | solution.py:604
  61.1 19.3 %collective-permute-start.14 = (f32[512,128]{1,0:T(8,128)}, f32[512,128]{1,0:T(8,128)}, u32[]{:S(2)}, u32[]{:S(2)}) collective-permute-start(f32[512,128]{1,0:T(8,128)} %multiply_add_fusion.1), channel_id=1, source_target_pairs={{1,3},{3,5},{5,7},{9,11},{11,13},{13,15},{17,19},{19,21},{21,23},{... | collective-permute-start | bytes 786440 | tf_op jit(solution)/shard_map/ppermute | solution.py:632
  80.4 7.7 %collective-permute-start.17 = (bf16[2,128,1024]{2,1,0:T(8,128)(2,1)}, bf16[2,128,1024]{2,1,0:T(8,128)(2,1)}, u32[]{:S(2)}, u32[]{:S(2)}) collective-permute-start(bf16[2,128,1024]{2,1,0:T(8,128)(2,1)} %collective-permute-done.12.refs_5_), channel_id=1, source_target_pairs={{0,1},{1,0},{2,3},{3,2},{4,5},{5,4},{6,7},{7,6},{8,9},{9,8},{10,11... | collective-permute-start | bytes 1572872 | tf_op jit(solution)/shard_map/ppermute | solution.py:608
  80.5 15.1 %collective-permute-start.16 = (bf16[2,128,1024]{2,1,0:T(8,128)(2,1)}, bf16[2,128,1024]{2,1,0:T(8,128)(2,1)}, u32[]{:S(2)}, u32[]{:S(2)}) collective-permute-start(bf16[2,128,1024]{2,1,0:T(8,128)(2,1)} %get-tuple-element.121), channel_id=1, source_target_pairs={{0,2},{1,3},{8,10},{9,11},{16,18},{17,19},{24,26},{25,27}} | collective-permute-start | bytes 1572872 | tf_op jit(solution)/shard_map/ppermute | solution.py:639
  81.9 11.0 %collective-permute-start.18 = (bf16[2176,128]{1,0:T(8,128)(2,1)}, bf16[2176,128]{1,0:T(8,128)(2,1)}, u32[]{:S(2)}, u32[]{:S(2)}) collective-permute-start(bf16[2176,128]{1,0:T(8,128)(2,1)} %collective-permute-done.11.refs_7_.refs_0_), channel_id=1, source_target_pairs={{0,1},{1,0},{2,3},{3,2},{4,5},{5,4},{6,7},{7,6},{8,9},{9,8},{10,11... | collective-permute-start | bytes 1671176 | tf_op jit(solution)/shard_map/ppermute | solution.py:608
  84.3 11.3 %collective-permute-start.19 = (f32[512,128]{1,0:T(8,128)}, f32[512,128]{1,0:T(8,128)}, u32[]{:S(2)}, u32[]{:S(2)}) collective-permute-start(f32[512,128]{1,0:T(8,128)} %multiply_add_fusion), channel_id=1, source_target_pairs={{1,3},{3,5},{5,7},{9,11},{11,13},{13,15},{17,19},{19,21},{21,23},{... | collective-permute-start | bytes 786440 | tf_op jit(solution)/shard_map/ppermute | solution.py:632
  86.2 15.0 %collective-permute-start.15 = (bf16[2176,128]{1,0:T(8,128)(2,1)}, bf16[2176,128]{1,0:T(8,128)(2,1)}, u32[]{:S(2)}, u32[]{:S(2)}) collective-permute-start(bf16[2176,128]{1,0:T(8,128)(2,1)} %get-tuple-element.120), channel_id=1, source_target_pairs={{7,5},{4,2},{6,3},{5,7},{2,4},{3,6},{15,13},{12,10},{14,11},{13,15... | collective-permute-start | bytes 1671176 | tf_op jit(solution)/shard_map/ppermute | solution.py:604
  101.2 7.0 %collective-permute-start.21 = (bf16[2,128,1024]{2,1,0:T(8,128)(2,1)}, bf16[2,128,1024]{2,1,0:T(8,128)(2,1)}, u32[]{:S(2)}, u32[]{:S(2)}) collective-permute-start(bf16[2,128,1024]{2,1,0:T(8,128)(2,1)} %collective-permute-done.16.refs_5_), channel_id=1, source_target_pairs={{0,1},{1,0},{2,3},{3,2},{4,5},{5,4},{6,7},{7,6},{8,9},{9,8},{10,11... | collective-permute-start | bytes 1572872 | tf_op jit(solution)/shard_map/ppermute | solution.py:608
  103.4 9.6 %collective-permute-start.22 = (bf16[2176,128]{1,0:T(8,128)(2,1)}, bf16[2176,128]{1,0:T(8,128)(2,1)}, u32[]{:S(2)}, u32[]{:S(2)}) collective-permute-start(bf16[2176,128]{1,0:T(8,128)(2,1)} %collective-permute-done.15.refs_7_.refs_0_), channel_id=1, source_target_pairs={{0,1},{1,0},{2,3},{3,2},{4,5},{5,4},{6,7},{7,6},{8,9},{9,8},{10,11... | collective-permute-start | bytes 1671176 | tf_op jit(solution)/shard_map/ppermute | solution.py:608
  103.4 15.3 %collective-permute-start.20 = (bf16[2176,128]{1,0:T(8,128)(2,1)}, bf16[2176,128]{1,0:T(8,128)(2,1)}, u32[]{:S(2)}, u32[]{:S(2)}) collective-permute-start(bf16[2176,128]{1,0:T(8,128)(2,1)} %get-tuple-element.134), channel_id=1, source_target_pairs={{5,7},{2,4},{3,6},{13,15},{10,12},{11,14},{21,23},{18,20},{19,22},... | collective-permute-start | bytes 1671176 | tf_op jit(solution)/shard_map/ppermute | solution.py:604
  118.7 6.8 %collective-permute-start.24 = (f32[512,128]{1,0:T(8,128)}, f32[512,128]{1,0:T(8,128)}, u32[]{:S(2)}, u32[]{:S(2)}) collective-permute-start(f32[512,128]{1,0:T(8,128)} %collective-permute-done.19.enter_ref), channel_id=1, source_target_pairs={{0,1},{1,0},{2,3},{3,2},{4,5},{5,4},{6,7},{7,6},{8,9},{9,8},{10,11... | collective-permute-start | bytes 786440 | tf_op jit(solution)/shard_map/ppermute | solution.py:608
  120.3 17.1 %collective-permute-start.23 = (bf16[2176,128]{1,0:T(8,128)(2,1)}, bf16[2176,128]{1,0:T(8,128)(2,1)}, u32[]{:S(2)}, u32[]{:S(2)}) collective-permute-start(bf16[2176,128]{1,0:T(8,128)(2,1)} %get-tuple-element.146), channel_id=1, source_target_pairs={{5,7},{2,4},{3,6},{13,15},{10,12},{11,14},{21,23},{18,20},{19,22},... | collective-permute-start | bytes 1671176 | tf_op jit(solution)/shard_map/ppermute | solution.py:604
  125.5 6.3 %collective-permute-start.25 = (bf16[2176,128]{1,0:T(8,128)(2,1)}, bf16[2176,128]{1,0:T(8,128)(2,1)}, u32[]{:S(2)}, u32[]{:S(2)}) collective-permute-start(bf16[2176,128]{1,0:T(8,128)(2,1)} %collective-permute-done.20.refs_0_), channel_id=1, source_target_pairs={{0,1},{1,0},{2,3},{3,2},{4,5},{5,4},{6,7},{7,6},{8,9},{9,8},{10,11... | collective-permute-start | bytes 1671176 | tf_op jit(solution)/shard_map/ppermute | solution.py:608
  137.4 2.3 %collective-permute-start.26 = (bf16[2176,128]{1,0:T(8,128)(2,1)}, bf16[2176,128]{1,0:T(8,128)(2,1)}, u32[]{:S(2)}, u32[]{:S(2)}) collective-permute-start(bf16[2176,128]{1,0:T(8,128)(2,1)} %collective-permute-done.23.refs_0_), channel_id=1, source_target_pairs={{0,1},{1,0},{2,3},{3,2},{4,5},{5,4},{6,7},{7,6},{8,9},{9,8},{10,11... | collective-permute-start | bytes 1671176 | tf_op jit(solution)/shard_map/ppermute | solution.py:608

commit v11 on v10

--- a/solution.py
+++ b/solution.py
@@ -191,9 +191,11 @@
             name="conv_pack",
         )(decay_rate.T, residue.T, hyena_q, hyena_k, hyena_v)
         rim = lax.ppermute(rim, "ctx", [(index, index + 1) for index in range(devices - 1)])
-        own_par = after(own_par, rim)
+        return rim, own_par
+
+    def shared_part(own_par):
         par = lax.all_to_all(own_par, "ctx", split_axis=0, concat_axis=0, tiled=True)
-        return rim, par.reshape(devices * par_rows, LANES)
+        return par.reshape(devices * par_rows, LANES)
 
     def state_part(rim, par):
         state_spec = pl.BlockSpec((SUBLANES * modes, LANES), lambda group: (group, 0))
@@ -237,7 +239,7 @@
             short_filter,
         )
 
-    return first_part, state_part, last_part
+    return first_part, shared_part, state_part, last_part
 
 
 def among(me, members):
@@ -610,19 +612,19 @@
     def with_swapped(arrays):
         return [item for array in arrays for item in (array, swapped(array))]
 
-    conv_first, conv_state, conv_last = conv
-    rim, par = conv_first()
+    conv_first, conv_shared, conv_state, conv_last = conv
+    rim, own_par = conv_first()
     key_packs, query_packs = pack()
-    rim, key_packs, query_packs = lax.optimization_barrier((rim, key_packs, query_packs))
+    live = (rim, own_par, key_packs, query_packs)
+    rim, own_par, key_packs, query_packs = lax.optimization_barrier(live)
 
     asks = [exchange([query_packs[0]] * len(transfers), 1)]
     quad = lax.ppermute(key_packs[0], "ctx", gathers)
-    local_result, state, decay = conv_state(rim, par)
-    live = (asks[0], quad, local_result, state, decay, key_packs[1:], query_packs[1:])
-    asks[0], quad, local_result, state, decay, key_packs, query_packs = (
-        lax.optimization_barrier(live)
-    )
-
+    par = conv_shared(own_par)
+    live = (asks[0], quad, rim, par, key_packs[1:], query_packs[1:])
+    asks[0], quad, rim, par, key_packs, query_packs = lax.optimization_barrier(live)
+
+    local_result = state = decay = None
     other = total = entering = answers = result = None
     hops = devices // 2 - 1
     hop_pairs = [(index, index + 2) for index in range(1, devices - 2, 2)]
@@ -645,9 +647,11 @@
             if both:
                 next_ask = back
         if chunk == 0:
+            local_result, state, decay = conv_state(rim, par)
+        if chunk == 1:
             other = swapped(state)
             total = state + decay * other
-        if hops:
+        if chunk and hops:
             entering = hop(entering)
             hops -= 1
         parts = with_swapped(waiting[0]) if waiting else None
@@ -659,10 +663,12 @@
             waiting = waiting[1:]
         if back:
             waiting.append(back)
-        live = (next_ask, next_quad, waiting, answers, result, total, entering, owns[chunk])
-        next_ask, quad, waiting, answers, result, total, entering, owns[chunk] = (
+        convolved = (local_result, state, decay, total, entering)
+        live = (next_ask, next_quad, waiting, answers, result, convolved, owns[chunk])
+        next_ask, quad, waiting, answers, result, convolved, owns[chunk] = (
             lax.optimization_barrier(live)
         )
+        local_result, state, decay, total, entering = convolved
         asks.append(next_ask)
 
     back = exchange(answers, -1)

time: 144 us -> 143 us (level)
  starting transfers between devices: 51.6 us -> 49.2 us
    all_to_all x1, waiting for transfers between devices: 8.51 us -> 0.01 us  [shared_part(): lax.all_to_all(own_par, 'ctx', split_axis=0, concat_axis=0, tiled=True)]
    ppermute x6, waiting for transfers between devices: 11.7 us -> 19.1 us  [exchange(): moved.append(lax.ppermute(operand, 'ctx', moves))]
    ppermute x6, starting transfers between devices: 16.4 us -> 12.2 us  [exchange(): moved.append(lax.ppermute(operand, 'ctx', moves))]
    ppermute x3, waiting for transfers between devices: 11.1 us -> 14.3 us  [hop(): return lax.ppermute(leaving, 'ctx', hop_pairs)]
    ppermute x1, starting transfers between devices: 0.36 us -> 2.33 us  [attend(): key_swapped = lax.ppermute(key, 'ctx', swap)]
  transfers between devices with their start and end apart: 28 -> 28, of which waited for: 9 -> 7; matrix products, arithmetic and copies ran while one was open for 4% -> 4% of each run, Pallas kernels for 32% -> 32%
where the time goes in v11:
time: 143 us; the launch traced here: 142 us
  starting transfers between devices  49.2 us (34%)
  Pallas kernels  47.9 us (33%)
  waiting for transfers between devices  37.3 us (26%)
  other arithmetic  5.47 us (4%)
    pallas_call x4, Pallas kernels, partial(): pl.pallas_call(functools.partial(partial_kernel, transfers, upper, natura...  19.2 us
    ppermute x6, waiting for transfers between devices, exchange(): moved.append(lax.ppermute(operand, 'ctx', moves))  19.1 us
    ppermute x3, waiting for transfers between devices, hop(): return lax.ppermute(leaving, 'ctx', hop_pairs)  14.3 us
    ppermute x6, starting transfers between devices, exchange(): moved.append(lax.ppermute(operand, 'ctx', moves))  12.2 us
    ppermute x10, starting transfers between devices, swapped(): return lax.ppermute(array, 'ctx', swap)  10.7 us
    pallas_call x4, Pallas kernels, merge(): pl.pallas_call(functools.partial(merge_kernel, transfers, steps, starts[c...  10.6 us
    pallas_call x1, Pallas kernels, state_part(): pl.pallas_call(functools.partial(state_kernel, modes), grid=(groups,), in...  9.69 us
    ppermute x3, starting transfers between devices, hop(): return lax.ppermute(leaving, 'ctx', hop_pairs)  8.36 us
  transfers between devices with their start and end apart: 28, of which 7 were waited for; matrix products, arithmetic and copies ran while one was open for 4% of the time, Pallas kernels for 32%

profile of v11, /device:TPU:17, one launch (start us, length us, event | category | flops | bytes accessed | tf_op | source)
XLA Modules:
  0.0 141.7 jit_solution(7907691318800653608)
XLA Ops:
  0.6 0.7 collective-permute-start.1
  1.4 1.9 %conv_pack.1 = (f32[8,128,128]{2,1,0:T(8,128)}, f32[8,4096]{1,0:T(8,128)}) custom-call(f32[16,512]{1,0:T(8,128)} %bitcast.3, f32[16,512]{1,0:T(8,128)} %bitcast.4, bf16[128,4096]{1,0:T(8,128)(2,1)} %q_ref.5, bf16[128,4096]{1,0:T(8,128)(2,1)} %k_ref.5, bf16[128,4096]{1,0:T(8,128)(2,1)} %v_ref.5), custom_call_target="tpu_custom_call" | custom-call | flops 1000000000 | bytes 1048576 | tf_op jit(solution)/shard_map/conv_pack/pallas_call | solution.py:176
  3.3 3.1 %collective-permute-start = (f32[8,4096]{1,0:T(8,128)}, f32[8,4096]{1,0:T(8,128)S(1)}, u32[]{:S(2)}, u32[]{:S(2)}) collective-permute-start(f32[8,4096]{1,0:T(8,128)} %get-tuple-element.87), channel_id=1, source_target_pairs={{0,1},{1,2},{2,3},{3,4},{4,5},{5,6},{6,7},{8,9},{9,10},{10,11},{11... | collective-permute-start | bytes 393224 | tf_op jit(solution)/shard_map/ppermute | solution.py:193
  6.4 0.0 collective-permute-done.1.qs_ref.refs_9_
  6.4 0.2 att_pack.1
  6.6 2.0 %collective-permute-done.rim_ref = f32[8,4096]{1,0:T(8,128)S(1)} collective-permute-done((f32[8,4096]{1,0:T(8,128)}, f32[8,4096]{1,0:T(8,128)S(1)}, u32[]{:S(2)}, u32[]{:S(2)}) %collective-permute-start) | collective-permute-done | bytes 131104 | tf_op jit(solution)/shard_map/ppermute | solution.py:193
  8.7 6.0 %all-to-all-start = ((f32[8,128,128]{2,1,0:T(8,128)}), f32[8,128,128]{2,1,0:T(8,128)}, u32[]{:S(2)}, u32[]{:S(2)}) async-start(f32[8,128,128]{2,1,0:T(8,128)} %get-tuple-element.98), calls=%async_computation | async-start | bytes 1048576 | tf_op jit(solution)/shard_map/all_to_all | solution.py:197
  14.7 1.3 collective-permute-start.2
  16.0 1.5 %collective-permute-start.3 = (bf16[2,128,1024]{2,1,0:T(8,128)(2,1)}, bf16[2,128,1024]{2,1,0:T(8,128)(2,1)}, u32[]{:S(2)}, u32[]{:S(2)}) collective-permute-start(bf16[2,128,1024]{2,1,0:T(8,128)(2,1)} %get-tuple-element.96), channel_id=1, source_target_pairs={{0,2},{1,3},{8,10},{9,11},{16,18},{17,19},{24,26},{25,27}} | collective-permute-start | bytes 1572872 | tf_op jit(solution)/shard_map/ppermute | solution.py:622
  17.4 2.3 %collective-permute-start.6 = (bf16[128,4096]{1,0:T(8,128)(2,1)}, bf16[128,4096]{1,0:T(8,128)(2,1)}, u32[]{:S(2)}, u32[]{:S(2)}) collective-permute-start(bf16[128,4096]{1,0:T(8,128)(2,1)} %refs_1_.7), channel_id=1, source_target_pairs={{0,1},{1,0},{2,3},{3,2},{4,5},{5,4},{6,7},{7,6},{8,9},{9,8},{10,11... | collective-permute-start | bytes 3145736 | tf_op jit(solution)/shard_map/ppermute | solution.py:502
  19.8 0.0 collective-permute-start.7
  19.8 16.6 %collective-permute-done.2.refs_7_ = bf16[2,128,1024]{2,1,0:T(8,128)(2,1)} collective-permute-done((bf16[2,128,1024]{2,1,0:T(8,128)(2,1)}, bf16[2,128,1024]{2,1,0:T(8,128)(2,1)}, u32[]{:S(2)}, u32[]{:S(2)}) %collective-permute-start.2) | collective-permute-done | bytes 524320 | tf_op jit(solution)/shard_map/ppermute | solution.py:606
  36.4 1.3 collective-permute-start.4
  37.7 1.5 %collective-permute-start.5 = (bf16[2,128,1024]{2,1,0:T(8,128)(2,1)}, bf16[2,128,1024]{2,1,0:T(8,128)(2,1)}, u32[]{:S(2)}, u32[]{:S(2)}) collective-permute-start(bf16[2,128,1024]{2,1,0:T(8,128)(2,1)} %get-tuple-element.104), channel_id=1, source_target_pairs={{0,2},{1,3},{8,10},{9,11},{16,18},{17,19},{24,26},{25,27}} | collective-permute-start | bytes 1572872 | tf_op jit(solution)/shard_map/ppermute | solution.py:641
  39.1 5.9 %collective-permute-start.8 = (bf16[2,128,1024]{2,1,0:T(8,128)(2,1)}, bf16[2,128,1024]{2,1,0:T(8,128)(2,1)}, u32[]{:S(2)}, u32[]{:S(2)}) collective-permute-start(bf16[2,128,1024]{2,1,0:T(8,128)(2,1)} %collective-permute-done.3.refs_5_), channel_id=1, source_target_pairs={{0,1},{1,0},{2,3},{3,2},{4,5},{5,4},{6,7},{7,6},{8,9},{9,8},{10,11... | collective-permute-start | bytes 1572872 | tf_op jit(solution)/shard_map/ppermute | solution.py:610
  45.0 9.7 %conv_state.1 = (f32[128,4096]{1,0:T(8,128)}, f32[512,128]{1,0:T(8,128)}, f32[512,128]{1,0:T(8,128)}) custom-call(bf16[128,4096]{1,0:T(8,128)(2,1)} %k_ref.5, bf16[128,4096]{1,0:T(8,128)(2,1)} %v_ref.5, f32[8,4096]{1,0:T(8,128)} %copy-done.1, f32[1024,128]{1,0:T(8,128)} %bitcast.2.par_ref, f32[3,3,4096]{2,1,0:T(4,128)} %taps_ref.3), custom_call_target="tpu_custom_call" | custom-call | flops 8999999488 | bytes 1048576 | tf_op jit(solution)/shard_map/conv_state/pallas_call | solution.py:202
  54.7 4.8 %att_partial.4 = (f32[128,1024]{1,0:T(8,128)}, f32[16,128]{1,0:T(8,128)}, bf16[2176,128]{1,0:T(8,128)(2,1)}, bf16[128,4096]{1,0:T(8,128)(2,1)}) custom-call(bf16[128,4096]{1,0:T(8,128)(2,1)} %refs_0_.7, bf16[128,4096]{1,0:T(8,128)(2,1)} %refs_1_.7, bf16[128,4096]{1,0:T(8,128)(2,1)} %refs_2_.7, bf16[128,4096]{1,0:T(8,128)(2,1)} %collective-permute-done.6.refs_3_, ...), custom_call_target="tpu_custom_call" | custom-call | flops 4000000000 | bytes 1048576 | tf_op jit(solution)/shard_map/att_partial/pallas_call | solution.py:562
  59.6 0.1 collective-permute-start.11
  59.6 0.5 collective-permute-start.12
  60.1 1.5 %collective-permute-start.10 = (bf16[2,128,1024]{2,1,0:T(8,128)(2,1)}, bf16[2,128,1024]{2,1,0:T(8,128)(2,1)}, u32[]{:S(2)}, u32[]{:S(2)}) collective-permute-start(bf16[2,128,1024]{2,1,0:T(8,128)(2,1)} %get-tuple-element.117), channel_id=1, source_target_pairs={{0,2},{1,3},{8,10},{9,11},{16,18},{17,19},{24,26},{25,27}} | collective-permute-start | bytes 1572872 | tf_op jit(solution)/shard_map/ppermute | solution.py:641
  61.6 1.9 %collective-permute-start.9 = (bf16[2176,128]{1,0:T(8,128)(2,1)}, bf16[2176,128]{1,0:T(8,128)(2,1)}, u32[]{:S(2)}, u32[]{:S(2)}) collective-permute-start(bf16[2176,128]{1,0:T(8,128)(2,1)} %get-tuple-element.116), channel_id=1, source_target_pairs={{7,5},{4,2},{6,3},{5,7},{2,4},{3,6},{15,13},{12,10},{14,11},{13,15... | collective-permute-start | bytes 1671176 | tf_op jit(solution)/shard_map/ppermute | solution.py:606
  63.5 0.7 copy-done
  64.2 1.8 %multiply_add_fusion.2 = f32[512,128]{1,0:T(8,128)} fusion(f32[512,128]{1,0:T(8,128)} %get-tuple-element.124, f32[512,128]{1,0:T(8,128)} %get-tuple-element.161.decay_ref, f32[512,128]{1,0:T(8,128)S(1)} %collective-permute-done.12.other_ref), kind=kLoop, calls=%fused_computation.2 | loop fusion | flops 131072 | bytes 1048576 | tf_op jit(solution)/shard_map/add | solution.py:653
  66.0 3.4 %collective-permute-start.13 = (f32[512,128]{1,0:T(8,128)}, f32[512,128]{1,0:T(8,128)}, u32[]{:S(2)}, u32[]{:S(2)}) collective-permute-start(f32[512,128]{1,0:T(8,128)} %multiply_add_fusion.2), channel_id=1, source_target_pairs={{1,3},{3,5},{5,7},{9,11},{11,13},{13,15},{17,19},{19,21},{21,23},{... | collective-permute-start | bytes 786440 | tf_op jit(solution)/shard_map/ppermute | solution.py:634
  69.4 4.8 %att_partial.5 = (f32[128,1024]{1,0:T(8,128)}, f32[16,128]{1,0:T(8,128)}, bf16[2176,128]{1,0:T(8,128)(2,1)}, bf16[128,4096]{1,0:T(8,128)(2,1)}) custom-call(bf16[128,4096]{1,0:T(8,128)(2,1)} %refs_0_.7, bf16[128,4096]{1,0:T(8,128)(2,1)} %refs_1_.7, bf16[128,4096]{1,0:T(8,128)(2,1)} %refs_2_.7, ...), custom_call_target="tpu_custom_call", output_to_operand_aliasing={{3}: (10, {})} | custom-call | flops 4000000000 | bytes 1048576 | tf_op jit(solution)/shard_map/att_partial/pallas_call | solution.py:562
  74.2 3.8 %collective-permute-done.13 = f32[512,128]{1,0:T(8,128)} collective-permute-done((f32[512,128]{1,0:T(8,128)}, f32[512,128]{1,0:T(8,128)}, u32[]{:S(2)}, u32[]{:S(2)}) %collective-permute-start.13) | collective-permute-done | bytes 262176 | tf_op jit(solution)/shard_map/ppermute | solution.py:634
  78.0 0.9 collective-permute-start.16
  78.9 1.5 %collective-permute-start.15 = (bf16[2,128,1024]{2,1,0:T(8,128)(2,1)}, bf16[2,128,1024]{2,1,0:T(8,128)(2,1)}, u32[]{:S(2)}, u32[]{:S(2)}) collective-permute-start(bf16[2,128,1024]{2,1,0:T(8,128)(2,1)} %get-tuple-element.129), channel_id=1, source_target_pairs={{0,2},{1,3},{8,10},{9,11},{16,18},{17,19},{24,26},{25,27}} | collective-permute-start | bytes 1572872 | tf_op jit(solution)/shard_map/ppermute | solution.py:641
  80.4 2.4 %collective-permute-start.14 = (bf16[2176,128]{1,0:T(8,128)(2,1)}, bf16[2176,128]{1,0:T(8,128)(2,1)}, u32[]{:S(2)}, u32[]{:S(2)}) collective-permute-start(bf16[2176,128]{1,0:T(8,128)(2,1)} %get-tuple-element.128), channel_id=1, source_target_pairs={{7,5},{4,2},{6,3},{5,7},{2,4},{3,6},{15,13},{12,10},{14,11},{13,15... | collective-permute-start | bytes 1671176 | tf_op jit(solution)/shard_map/ppermute | solution.py:606
  82.8 0.1 collective-permute-start.17
  82.8 1.9 %multiply_add_fusion.1 = f32[512,128]{1,0:T(8,128)} fusion(f32[512,128]{1,0:T(8,128)} %multiply_add_fusion.2, f32[512,128]{1,0:T(8,128)} %collective-permute-done.13, f32[512,128]{1,0:T(8,128)} %get-tuple-element.161.decay_ref), kind=kLoop, calls=%fused_computation.1 | loop fusion | flops 196608 | bytes 1048576 | tf_op jit(solution)/shard_map/add | solution.py:633
  84.7 2.9 %collective-permute-start.18 = (f32[512,128]{1,0:T(8,128)}, f32[512,128]{1,0:T(8,128)}, u32[]{:S(2)}, u32[]{:S(2)}) collective-permute-start(f32[512,128]{1,0:T(8,128)} %multiply_add_fusion.1), channel_id=1, source_target_pairs={{1,3},{3,5},{5,7},{9,11},{11,13},{13,15},{17,19},{19,21},{21,23},{... | collective-permute-start | bytes 786440 | tf_op jit(solution)/shard_map/ppermute | solution.py:634
  87.6 4.8 %att_partial.6 = (f32[128,1024]{1,0:T(8,128)}, f32[16,128]{1,0:T(8,128)}, bf16[2176,128]{1,0:T(8,128)(2,1)}, bf16[128,4096]{1,0:T(8,128)(2,1)}) custom-call(bf16[128,4096]{1,0:T(8,128)(2,1)} %refs_0_.7, bf16[128,4096]{1,0:T(8,128)(2,1)} %refs_1_.7, bf16[128,4096]{1,0:T(8,128)(2,1)} %refs_2_.7, ...), custom_call_target="tpu_custom_call", output_to_operand_aliasing={{3}: (8, {})} | custom-call | flops 4000000000 | bytes 1048576 | tf_op jit(solution)/shard_map/att_partial/pallas_call | solution.py:562
  92.4 2.7 %att_merge.4.refs_8_ = bf16[128,4096]{1,0:T(8,128)(2,1)} custom-call(f32[128,1024]{1,0:T(8,128)} %get-tuple-element.134.own_hbm, f32[16,128]{1,0:T(8,128)} %get-tuple-element.135.lse_hbm, bf16[2176,128]{1,0:T(8,128)(2,1)} %collective-permute-done.9.refs_7_.refs_0_, ...), custom_call_target="tpu_custom_call", output_to_operand_aliasing={{}: (4, {})} | custom-call | flops 2000000000 | bytes 1048576 | tf_op jit(solution)/shard_map/att_merge/pallas_call | solution.py:582
  95.1 5.1 %collective-permute-done.18 = f32[512,128]{1,0:T(8,128)} collective-permute-done((f32[512,128]{1,0:T(8,128)}, f32[512,128]{1,0:T(8,128)}, u32[]{:S(2)}, u32[]{:S(2)}) %collective-permute-start.18) | collective-permute-done | bytes 262176 | tf_op jit(solution)/shard_map/ppermute | solution.py:634
  100.2 2.7 %collective-permute-start.19 = (bf16[2176,128]{1,0:T(8,128)(2,1)}, bf16[2176,128]{1,0:T(8,128)(2,1)}, u32[]{:S(2)}, u32[]{:S(2)}) collective-permute-start(bf16[2176,128]{1,0:T(8,128)(2,1)} %get-tuple-element.144), channel_id=1, source_target_pairs={{5,7},{2,4},{3,6},{13,15},{10,12},{11,14},{21,23},{18,20},{19,22},... | collective-permute-start | bytes 1671176 | tf_op jit(solution)/shard_map/ppermute | solution.py:606
  103.0 1.8 %multiply_add_fusion = f32[512,128]{1,0:T(8,128)} fusion(f32[512,128]{1,0:T(8,128)} %multiply_add_fusion.2, f32[512,128]{1,0:T(8,128)} %collective-permute-done.18, f32[512,128]{1,0:T(8,128)} %get-tuple-element.161.decay_ref), kind=kLoop, calls=%fused_computation | loop fusion | flops 196608 | bytes 1048576 | tf_op jit(solution)/shard_map/add | solution.py:633
  104.8 2.1 %collective-permute-start.22 = (f32[512,128]{1,0:T(8,128)}, f32[512,128]{1,0:T(8,128)}, u32[]{:S(2)}, u32[]{:S(2)}) collective-permute-start(f32[512,128]{1,0:T(8,128)} %multiply_add_fusion), channel_id=1, source_target_pairs={{1,3},{3,5},{5,7},{9,11},{11,13},{13,15},{17,19},{19,21},{21,23},{... | collective-permute-start | bytes 786440 | tf_op jit(solution)/shard_map/ppermute | solution.py:634
  106.9 4.8 %att_partial.7 = (f32[128,1024]{1,0:T(8,128)}, f32[16,128]{1,0:T(8,128)}, bf16[2176,128]{1,0:T(8,128)(2,1)}, bf16[128,4096]{1,0:T(8,128)(2,1)}) custom-call(bf16[128,4096]{1,0:T(8,128)(2,1)} %refs_0_.7, bf16[128,4096]{1,0:T(8,128)(2,1)} %refs_1_.7, bf16[128,4096]{1,0:T(8,128)(2,1)} %refs_2_.7, ...), custom_call_target="tpu_custom_call", output_to_operand_aliasing={{3}: (8, {})} | custom-call | flops 4000000000 | bytes 1048576 | tf_op jit(solution)/shard_map/att_partial/pallas_call | solution.py:562
  111.7 2.7 %att_merge.5.refs_2_ = bf16[128,4096]{1,0:T(8,128)(2,1)} custom-call(f32[128,1024]{1,0:T(8,128)} %get-tuple-element.149.own_hbm, f32[16,128]{1,0:T(8,128)} %get-tuple-element.150.lse_hbm, bf16[2176,128]{1,0:T(8,128)(2,1)} %collective-permute-done.14.refs_7_.refs_0_, ...), custom_call_target="tpu_custom_call", output_to_operand_aliasing={{}: (4, {})} | custom-call | flops 2000000000 | bytes 1048576 | tf_op jit(solution)/shard_map/att_merge/pallas_call | solution.py:582
  114.4 5.3 %collective-permute-done.22.enter_ref = f32[512,128]{1,0:T(8,128)} collective-permute-done((f32[512,128]{1,0:T(8,128)}, f32[512,128]{1,0:T(8,128)}, u32[]{:S(2)}, u32[]{:S(2)}) %collective-permute-start.22) | collective-permute-done | bytes 262176 | tf_op jit(solution)/shard_map/ppermute | solution.py:634
  119.7 2.6 %collective-permute-start.23 = (bf16[2176,128]{1,0:T(8,128)(2,1)}, bf16[2176,128]{1,0:T(8,128)(2,1)}, u32[]{:S(2)}, u32[]{:S(2)}) collective-permute-start(bf16[2176,128]{1,0:T(8,128)(2,1)} %get-tuple-element.159), channel_id=1, source_target_pairs={{5,7},{2,4},{3,6},{13,15},{10,12},{11,14},{21,23},{18,20},{19,22},... | collective-permute-start | bytes 1671176 | tf_op jit(solution)/shard_map/ppermute | solution.py:606
  122.3 6.3 %conv_output.1 = bf16[128,4096]{1,0:T(8,128)(2,1)} custom-call(bf16[128,4096]{1,0:T(8,128)(2,1)} %q_ref.5, f32[128,4096]{1,0:T(8,128)} %get-tuple-element.160.y_ref, f32[8,4096]{1,0:T(8,128)} %copy-done.1, f32[1024,128]{1,0:T(8,128)} %bitcast.2.par_ref, f32[512,128]{1,0:T(8,128)} %get-tuple-element.161.decay_ref, ...), custom_call_target="tpu_custom_call" | custom-call | flops 6000000000 | bytes 1048576 | tf_op jit(solution)/shard_map/conv_output/pallas_call | solution.py:219
  128.6 2.7 %att_merge.6.refs_2_ = bf16[128,4096]{1,0:T(8,128)(2,1)} custom-call(f32[128,1024]{1,0:T(8,128)} %get-tuple-element.163.own_hbm, f32[16,128]{1,0:T(8,128)} %get-tuple-element.164.lse_hbm, bf16[2176,128]{1,0:T(8,128)(2,1)} %collective-permute-done.19.refs_0_, bf16[2176,128]{1,0:T(8,128)(2,1)} %collective-permute-done.25.refs_1_, ...), custom_call_target="tpu_custom_call", output_to_operand_aliasing={{}: (4, {})} | custom-call | flops 2000000000 | bytes 1048576 | tf_op jit(solution)/shard_map/att_merge/pallas_call | solution.py:582
  131.3 2.4 %collective-permute-done.23.refs_0_ = bf16[2176,128]{1,0:T(8,128)(2,1)} collective-permute-done((bf16[2176,128]{1,0:T(8,128)(2,1)}, bf16[2176,128]{1,0:T(8,128)(2,1)}, u32[]{:S(2)}, u32[]{:S(2)}) %collective-permute-start.23) | collective-permute-done | bytes 557088 | tf_op jit(solution)/shard_map/ppermute | solution.py:606
  133.7 3.3 %collective-permute-start.26 = (bf16[2176,128]{1,0:T(8,128)(2,1)}, bf16[2176,128]{1,0:T(8,128)(2,1)}, u32[]{:S(2)}, u32[]{:S(2)}) collective-permute-start(bf16[2176,128]{1,0:T(8,128)(2,1)} %collective-permute-done.23.refs_0_), channel_id=1, source_target_pairs={{0,1},{1,0},{2,3},{3,2},{4,5},{5,4},{6,7},{7,6},{8,9},{9,8},{10,11... | collective-permute-start | bytes 1671176 | tf_op jit(solution)/shard_map/ppermute | solution.py:610
  137.0 1.9 %collective-permute-done.26.refs_1_ = bf16[2176,128]{1,0:T(8,128)(2,1)} collective-permute-done((bf16[2176,128]{1,0:T(8,128)(2,1)}, bf16[2176,128]{1,0:T(8,128)(2,1)}, u32[]{:S(2)}, u32[]{:S(2)}) %collective-permute-start.26) | collective-permute-done | bytes 557088 | tf_op jit(solution)/shard_map/ppermute | solution.py:610
  138.9 2.6 %att_merge.7 = bf16[128,4096]{1,0:T(8,128)(2,1)} custom-call(f32[128,1024]{1,0:T(8,128)} %get-tuple-element.168.own_hbm, f32[16,128]{1,0:T(8,128)} %get-tuple-element.169.lse_hbm, bf16[2176,128]{1,0:T(8,128)(2,1)} %collective-permute-done.23.refs_0_, bf16[2176,128]{1,0:T(8,128)(2,1)} %collective-permute-done.26.refs_1_, ...), custom_call_target="tpu_custom_call", output_to_operand_aliasing={{}: (4, {})} | custom-call | flops 2000000000 | bytes 1048576 | tf_op jit(solution)/shard_map/att_merge/pallas_call | solution.py:582
  (27 shorter events, 0.1 us)
Async XLA Ops:
  0.6 5.8 %collective-permute-start.1 = (bf16[128,4096]{1,0:T(8,128)(2,1)}, bf16[128,4096]{1,0:T(8,128)(2,1)}, u32[]{:S(2)}, u32[]{:S(2)}) collective-permute-start(bf16[128,4096]{1,0:T(8,128)(2,1)} %refs_0_.7), channel_id=1, source_target_pairs={{0,1},{1,0},{2,3},{3,2},{4,5},{5,4},{6,7},{7,6},{8,9},{9,8},{10,11... | collective-permute-start | bytes 3145736 | tf_op jit(solution)/shard_map/ppermute | solution.py:501
  3.3 5.3 %collective-permute-start = (f32[8,4096]{1,0:T(8,128)}, f32[8,4096]{1,0:T(8,128)S(1)}, u32[]{:S(2)}, u32[]{:S(2)}) collective-permute-start(f32[8,4096]{1,0:T(8,128)} %get-tuple-element.87), channel_id=1, source_target_pairs={{0,1},{1,2},{2,3},{3,4},{4,5},{5,6},{6,7},{8,9},{9,10},{10,11},{11... | collective-permute-start | bytes 393224 | tf_op jit(solution)/shard_map/ppermute | solution.py:193
  8.7 36.3 %copy-start.1 = (f32[8,4096]{1,0:T(8,128)}, f32[8,4096]{1,0:T(8,128)S(1)}, u32[]{:S(2)}) copy-start(f32[8,4096]{1,0:T(8,128)S(1)} %collective-permute-done.rim_ref) | copy-start | bytes 393220
  8.7 27.7 %all-to-all-start = ((f32[8,128,128]{2,1,0:T(8,128)}), f32[8,128,128]{2,1,0:T(8,128)}, u32[]{:S(2)}, u32[]{:S(2)}) async-start(f32[8,128,128]{2,1,0:T(8,128)} %get-tuple-element.98), calls=%async_computation | async-start | bytes 1048576 | tf_op jit(solution)/shard_map/all_to_all | solution.py:197
  14.7 21.7 %collective-permute-start.2 = (bf16[2,128,1024]{2,1,0:T(8,128)(2,1)}, bf16[2,128,1024]{2,1,0:T(8,128)(2,1)}, u32[]{:S(2)}, u32[]{:S(2)}) collective-permute-start(bf16[2,128,1024]{2,1,0:T(8,128)(2,1)} %get-tuple-element.95), channel_id=1, source_target_pairs={{7,5},{4,2},{6,3},{15,13},{12,10},{14,11},{23,21},{20,18},{22,19},... | collective-permute-start | bytes 1572872 | tf_op jit(solution)/shard_map/ppermute | solution.py:606
  16.0 20.4 %collective-permute-start.3 = (bf16[2,128,1024]{2,1,0:T(8,128)(2,1)}, bf16[2,128,1024]{2,1,0:T(8,128)(2,1)}, u32[]{:S(2)}, u32[]{:S(2)}) collective-permute-start(bf16[2,128,1024]{2,1,0:T(8,128)(2,1)} %get-tuple-element.96), channel_id=1, source_target_pairs={{0,2},{1,3},{8,10},{9,11},{16,18},{17,19},{24,26},{25,27}} | collective-permute-start | bytes 1572872 | tf_op jit(solution)/shard_map/ppermute | solution.py:622
  17.4 37.3 %collective-permute-start.6 = (bf16[128,4096]{1,0:T(8,128)(2,1)}, bf16[128,4096]{1,0:T(8,128)(2,1)}, u32[]{:S(2)}, u32[]{:S(2)}) collective-permute-start(bf16[128,4096]{1,0:T(8,128)(2,1)} %refs_1_.7), channel_id=1, source_target_pairs={{0,1},{1,0},{2,3},{3,2},{4,5},{5,4},{6,7},{7,6},{8,9},{9,8},{10,11... | collective-permute-start | bytes 3145736 | tf_op jit(solution)/shard_map/ppermute | solution.py:502
  19.8 34.9 %collective-permute-start.7 = (bf16[128,4096]{1,0:T(8,128)(2,1)}, bf16[128,4096]{1,0:T(8,128)(2,1)}, u32[]{:S(2)}, u32[]{:S(2)}) collective-permute-start(bf16[128,4096]{1,0:T(8,128)(2,1)} %refs_2_.7), channel_id=1, source_target_pairs={{0,1},{1,0},{2,3},{3,2},{4,5},{5,4},{6,7},{7,6},{8,9},{9,8},{10,11... | collective-permute-start | bytes 3145736 | tf_op jit(solution)/shard_map/ppermute | solution.py:503
  36.4 23.2 %collective-permute-start.4 = (bf16[2,128,1024]{2,1,0:T(8,128)(2,1)}, bf16[2,128,1024]{2,1,0:T(8,128)(2,1)}, u32[]{:S(2)}, u32[]{:S(2)}) collective-permute-start(bf16[2,128,1024]{2,1,0:T(8,128)(2,1)} %get-tuple-element.103), channel_id=1, source_target_pairs={{7,5},{4,2},{6,3},{15,13},{12,10},{14,11},{23,21},{20,18},{22,19},... | collective-permute-start | bytes 1572872 | tf_op jit(solution)/shard_map/ppermute | solution.py:606
  37.7 21.9 %collective-permute-start.5 = (bf16[2,128,1024]{2,1,0:T(8,128)(2,1)}, bf16[2,128,1024]{2,1,0:T(8,128)(2,1)}, u32[]{:S(2)}, u32[]{:S(2)}) collective-permute-start(bf16[2,128,1024]{2,1,0:T(8,128)(2,1)} %get-tuple-element.104), channel_id=1, source_target_pairs={{0,2},{1,3},{8,10},{9,11},{16,18},{17,19},{24,26},{25,27}} | collective-permute-start | bytes 1572872 | tf_op jit(solution)/shard_map/ppermute | solution.py:641
  39.1 15.6 %collective-permute-start.8 = (bf16[2,128,1024]{2,1,0:T(8,128)(2,1)}, bf16[2,128,1024]{2,1,0:T(8,128)(2,1)}, u32[]{:S(2)}, u32[]{:S(2)}) collective-permute-start(bf16[2,128,1024]{2,1,0:T(8,128)(2,1)} %collective-permute-done.3.refs_5_), channel_id=1, source_target_pairs={{0,1},{1,0},{2,3},{3,2},{4,5},{5,4},{6,7},{7,6},{8,9},{9,8},{10,11... | collective-permute-start | bytes 1572872 | tf_op jit(solution)/shard_map/ppermute | solution.py:610
  59.6 9.8 %collective-permute-start.11 = (bf16[2,128,1024]{2,1,0:T(8,128)(2,1)}, bf16[2,128,1024]{2,1,0:T(8,128)(2,1)}, u32[]{:S(2)}, u32[]{:S(2)}) collective-permute-start(bf16[2,128,1024]{2,1,0:T(8,128)(2,1)} %collective-permute-done.5.refs_5_), channel_id=1, source_target_pairs={{0,1},{1,0},{2,3},{3,2},{4,5},{5,4},{6,7},{7,6},{8,9},{9,8},{10,11... | collective-permute-start | bytes 1572872 | tf_op jit(solution)/shard_map/ppermute | solution.py:610
  59.6 3.9 %collective-permute-start.12 = (f32[512,128]{1,0:T(8,128)}, f32[512,128]{1,0:T(8,128)S(1)}, u32[]{:S(2)}, u32[]{:S(2)}) collective-permute-start(f32[512,128]{1,0:T(8,128)} %get-tuple-element.124), channel_id=1, source_target_pairs={{0,1},{1,0},{2,3},{3,2},{4,5},{5,4},{6,7},{7,6},{8,9},{9,8},{10,11... | collective-permute-start | bytes 786440 | tf_op jit(solution)/shard_map/ppermute | solution.py:610
  60.1 14.1 %collective-permute-start.10 = (bf16[2,128,1024]{2,1,0:T(8,128)(2,1)}, bf16[2,128,1024]{2,1,0:T(8,128)(2,1)}, u32[]{:S(2)}, u32[]{:S(2)}) collective-permute-start(bf16[2,128,1024]{2,1,0:T(8,128)(2,1)} %get-tuple-element.117), channel_id=1, source_target_pairs={{0,2},{1,3},{8,10},{9,11},{16,18},{17,19},{24,26},{25,27}} | collective-permute-start | bytes 1572872 | tf_op jit(solution)/shard_map/ppermute | solution.py:641
  61.6 16.5 %collective-permute-start.9 = (bf16[2176,128]{1,0:T(8,128)(2,1)}, bf16[2176,128]{1,0:T(8,128)(2,1)}, u32[]{:S(2)}, u32[]{:S(2)}) collective-permute-start(bf16[2176,128]{1,0:T(8,128)(2,1)} %get-tuple-element.116), channel_id=1, source_target_pairs={{7,5},{4,2},{6,3},{5,7},{2,4},{3,6},{15,13},{12,10},{14,11},{13,15... | collective-permute-start | bytes 1671176 | tf_op jit(solution)/shard_map/ppermute | solution.py:606
  63.5 0.7 copy-start
  66.0 12.0 %collective-permute-start.13 = (f32[512,128]{1,0:T(8,128)}, f32[512,128]{1,0:T(8,128)}, u32[]{:S(2)}, u32[]{:S(2)}) collective-permute-start(f32[512,128]{1,0:T(8,128)} %multiply_add_fusion.2), channel_id=1, source_target_pairs={{1,3},{3,5},{5,7},{9,11},{11,13},{13,15},{17,19},{19,21},{21,23},{... | collective-permute-start | bytes 786440 | tf_op jit(solution)/shard_map/ppermute | solution.py:634
  78.0 9.6 %collective-permute-start.16 = (bf16[2,128,1024]{2,1,0:T(8,128)(2,1)}, bf16[2,128,1024]{2,1,0:T(8,128)(2,1)}, u32[]{:S(2)}, u32[]{:S(2)}) collective-permute-start(bf16[2,128,1024]{2,1,0:T(8,128)(2,1)} %collective-permute-done.10.refs_5_), channel_id=1, source_target_pairs={{0,1},{1,0},{2,3},{3,2},{4,5},{5,4},{6,7},{7,6},{8,9},{9,8},{10,11... | collective-permute-start | bytes 1572872 | tf_op jit(solution)/shard_map/ppermute | solution.py:610
  78.9 16.1 %collective-permute-start.15 = (bf16[2,128,1024]{2,1,0:T(8,128)(2,1)}, bf16[2,128,1024]{2,1,0:T(8,128)(2,1)}, u32[]{:S(2)}, u32[]{:S(2)}) collective-permute-start(bf16[2,128,1024]{2,1,0:T(8,128)(2,1)} %get-tuple-element.129), channel_id=1, source_target_pairs={{0,2},{1,3},{8,10},{9,11},{16,18},{17,19},{24,26},{25,27}} | collective-permute-start | bytes 1572872 | tf_op jit(solution)/shard_map/ppermute | solution.py:641
  80.4 19.8 %collective-permute-start.14 = (bf16[2176,128]{1,0:T(8,128)(2,1)}, bf16[2176,128]{1,0:T(8,128)(2,1)}, u32[]{:S(2)}, u32[]{:S(2)}) collective-permute-start(bf16[2176,128]{1,0:T(8,128)(2,1)} %get-tuple-element.128), channel_id=1, source_target_pairs={{7,5},{4,2},{6,3},{5,7},{2,4},{3,6},{15,13},{12,10},{14,11},{13,15... | collective-permute-start | bytes 1671176 | tf_op jit(solution)/shard_map/ppermute | solution.py:606
  82.8 9.6 %collective-permute-start.17 = (bf16[2176,128]{1,0:T(8,128)(2,1)}, bf16[2176,128]{1,0:T(8,128)(2,1)}, u32[]{:S(2)}, u32[]{:S(2)}) collective-permute-start(bf16[2176,128]{1,0:T(8,128)(2,1)} %collective-permute-done.9.refs_7_.refs_0_), channel_id=1, source_target_pairs={{0,1},{1,0},{2,3},{3,2},{4,5},{5,4},{6,7},{7,6},{8,9},{9,8},{10,11... | collective-permute-start | bytes 1671176 | tf_op jit(solution)/shard_map/ppermute | solution.py:610
  84.7 15.5 %collective-permute-start.18 = (f32[512,128]{1,0:T(8,128)}, f32[512,128]{1,0:T(8,128)}, u32[]{:S(2)}, u32[]{:S(2)}) collective-permute-start(f32[512,128]{1,0:T(8,128)} %multiply_add_fusion.1), channel_id=1, source_target_pairs={{1,3},{3,5},{5,7},{9,11},{11,13},{13,15},{17,19},{19,21},{21,23},{... | collective-permute-start | bytes 786440 | tf_op jit(solution)/shard_map/ppermute | solution.py:634
  100.2 6.7 %collective-permute-start.20 = (bf16[2,128,1024]{2,1,0:T(8,128)(2,1)}, bf16[2,128,1024]{2,1,0:T(8,128)(2,1)}, u32[]{:S(2)}, u32[]{:S(2)}) collective-permute-start(bf16[2,128,1024]{2,1,0:T(8,128)(2,1)} %collective-permute-done.15.refs_5_), channel_id=1, source_target_pairs={{0,1},{1,0},{2,3},{3,2},{4,5},{5,4},{6,7},{7,6},{8,9},{9,8},{10,11... | collective-permute-start | bytes 1572872 | tf_op jit(solution)/shard_map/ppermute | solution.py:610
  100.2 19.5 %collective-permute-start.19 = (bf16[2176,128]{1,0:T(8,128)(2,1)}, bf16[2176,128]{1,0:T(8,128)(2,1)}, u32[]{:S(2)}, u32[]{:S(2)}) collective-permute-start(bf16[2176,128]{1,0:T(8,128)(2,1)} %get-tuple-element.144), channel_id=1, source_target_pairs={{5,7},{2,4},{3,6},{13,15},{10,12},{11,14},{21,23},{18,20},{19,22},... | collective-permute-start | bytes 1671176 | tf_op jit(solution)/shard_map/ppermute | solution.py:606
  103.0 8.7 %collective-permute-start.21 = (bf16[2176,128]{1,0:T(8,128)(2,1)}, bf16[2176,128]{1,0:T(8,128)(2,1)}, u32[]{:S(2)}, u32[]{:S(2)}) collective-permute-start(bf16[2176,128]{1,0:T(8,128)(2,1)} %collective-permute-done.14.refs_7_.refs_0_), channel_id=1, source_target_pairs={{0,1},{1,0},{2,3},{3,2},{4,5},{5,4},{6,7},{7,6},{8,9},{9,8},{10,11... | collective-permute-start | bytes 1671176 | tf_op jit(solution)/shard_map/ppermute | solution.py:610
  104.8 14.9 %collective-permute-start.22 = (f32[512,128]{1,0:T(8,128)}, f32[512,128]{1,0:T(8,128)}, u32[]{:S(2)}, u32[]{:S(2)}) collective-permute-start(f32[512,128]{1,0:T(8,128)} %multiply_add_fusion), channel_id=1, source_target_pairs={{1,3},{3,5},{5,7},{9,11},{11,13},{13,15},{17,19},{19,21},{21,23},{... | collective-permute-start | bytes 786440 | tf_op jit(solution)/shard_map/ppermute | solution.py:634
  119.7 2.6 %collective-permute-start.24 = (f32[512,128]{1,0:T(8,128)}, f32[512,128]{1,0:T(8,128)}, u32[]{:S(2)}, u32[]{:S(2)}) collective-permute-start(f32[512,128]{1,0:T(8,128)} %collective-permute-done.22.enter_ref), channel_id=1, source_target_pairs={{0,1},{1,0},{2,3},{3,2},{4,5},{5,4},{6,7},{7,6},{8,9},{9,8},{10,11... | collective-permute-start | bytes 786440 | tf_op jit(solution)/shard_map/ppermute | solution.py:610
  119.7 14.0 %collective-permute-start.23 = (bf16[2176,128]{1,0:T(8,128)(2,1)}, bf16[2176,128]{1,0:T(8,128)(2,1)}, u32[]{:S(2)}, u32[]{:S(2)}) collective-permute-start(bf16[2176,128]{1,0:T(8,128)(2,1)} %get-tuple-element.159), channel_id=1, source_target_pairs={{5,7},{2,4},{3,6},{13,15},{10,12},{11,14},{21,23},{18,20},{19,22},... | collective-permute-start | bytes 1671176 | tf_op jit(solution)/shard_map/ppermute | solution.py:606
  122.3 6.3 %collective-permute-start.25 = (bf16[2176,128]{1,0:T(8,128)(2,1)}, bf16[2176,128]{1,0:T(8,128)(2,1)}, u32[]{:S(2)}, u32[]{:S(2)}) collective-permute-start(bf16[2176,128]{1,0:T(8,128)(2,1)} %collective-permute-done.19.refs_0_), channel_id=1, source_target_pairs={{0,1},{1,0},{2,3},{3,2},{4,5},{5,4},{6,7},{7,6},{8,9},{9,8},{10,11... | collective-permute-start | bytes 1671176 | tf_op jit(solution)/shard_map/ppermute | solution.py:610
  133.7 5.2 %collective-permute-start.26 = (bf16[2176,128]{1,0:T(8,128)(2,1)}, bf16[2176,128]{1,0:T(8,128)(2,1)}, u32[]{:S(2)}, u32[]{:S(2)}) collective-permute-start(bf16[2176,128]{1,0:T(8,128)(2,1)} %collective-permute-done.23.refs_0_), channel_id=1, source_target_pairs={{0,1},{1,0},{2,3},{3,2},{4,5},{5,4},{6,7},{7,6},{8,9},{9,8},{10,11... | collective-permute-start | bytes 1671176 | tf_op jit(solution)/shard_map/ppermute | solution.py:610

commit v12 on v6

--- a/solution.py
+++ b/solution.py
@@ -64,9 +64,31 @@
     return [taps_ref[feature, pl.ds(tap, 1), lanes] for tap in range(TAPS)]
 
 
+def join_parameters(same_ref, other_ref, par_ref):
+    odd = lax.axis_index("ctx") % 2
+    chips, rows, _ = same_ref.shape
+    for chip in range(chips):
+        for ref, core in ((same_ref, odd), (other_ref, 1 - odd)):
+            start = pl.multiple_of((2 * chip + core) * rows, SUBLANES)
+            par_ref[pl.ds(start, rows), :] = ref[chip]
+
+
 def state_kernel(
-    modes, k_ref, v_ref, rim_ref, par_ref, taps_ref, y_ref, s_ref, d_ref, p_scr, y_scr
+    modes,
+    k_ref,
+    v_ref,
+    rim_ref,
+    same_ref,
+    other_ref,
+    taps_ref,
+    y_ref,
+    s_ref,
+    d_ref,
+    par_ref,
+    p_scr,
+    y_scr,
 ):
+    join_parameters(same_ref, other_ref, par_ref)
     rows = k_ref.shape[0]
     for block in range(SUBLANES):
         lanes = block_lanes(block)
@@ -109,14 +131,17 @@
     q_ref,
     y_ref,
     rim_ref,
-    par_ref,
+    same_ref,
+    other_par_ref,
     decay_ref,
     enter_ref,
     enter_first_ref,
     other_ref,
     taps_ref,
     out_ref,
+    par_ref,
 ):
+    join_parameters(same_ref, other_par_ref, par_ref)
     second = lax.axis_index("ctx") % 2 == 1
     rows = q_ref.shape[0]
     step = lax.broadcasted_iota(jnp.int32, (SUBLANES, LANES), 0).astype(jnp.float32) + 1.0
@@ -168,7 +193,9 @@
     par_rows = 2 * own_blocks * modes
     feature_spec = pl.BlockSpec((rows, width), lambda group: (0, group))
     rim_spec = pl.BlockSpec((8, width), lambda group: (0, group))
-    par_spec = pl.BlockSpec((2 * SUBLANES * modes, LANES), lambda group: (group, 0))
+    chips = SUBLANES // (2 * own_blocks)
+    par_spec = pl.BlockSpec((chips, par_rows, LANES), lambda group: (group, 0, 0))
+    par_scratch = pltpu.VMEM((2 * SUBLANES * modes, LANES), jnp.float32)
     taps_spec = pl.BlockSpec((TAPS, TAPS, width), lambda group: (0, 0, group))
     positions = pltpu.VMEM((rows * SUBLANES, LANES), jnp.float32)
 
@@ -179,11 +206,11 @@
             in_specs=[pl.BlockSpec((modes, residue.shape[0]), lambda step: (0, 0))] * 2
             + [pl.BlockSpec((16, channels), lambda step: (end, 0))] * 3,
             out_specs=[
-                pl.BlockSpec((devices, par_rows, LANES), lambda step: (0, 0, 0)),
+                pl.BlockSpec((devices // 2, par_rows, LANES), lambda step: (0, 0, 0)),
                 pl.BlockSpec((8, channels), lambda step: (0, 0)),
             ],
             out_shape=[
-                jax.ShapeDtypeStruct((devices, par_rows, LANES), jnp.float32),
+                jax.ShapeDtypeStruct((devices // 2, par_rows, LANES), jnp.float32),
                 jax.ShapeDtypeStruct((8, channels), jnp.float32),
             ],
             compiler_params=params(),
@@ -192,24 +219,31 @@
         )(decay_rate.T, residue.T, hyena_q, hyena_k, hyena_v)
         rim = lax.ppermute(rim, "ctx", [(index, index + 1) for index in range(devices - 1)])
         own_par = after(own_par, rim, token)
-        par = lax.all_to_all(own_par, "ctx", split_axis=0, concat_axis=0, tiled=True)
-        par = par.reshape(devices * par_rows, LANES)
+        same = lax.all_to_all(
+            own_par,
+            "ctx",
+            split_axis=0,
+            concat_axis=0,
+            axis_index_groups=[list(range(core, devices, 2)) for core in range(2)],
+            tiled=True,
+        )
+        par = (same, lax.ppermute(same, "ctx", [(index, index ^ 1) for index in range(devices)]))
         state_spec = pl.BlockSpec((SUBLANES * modes, LANES), lambda group: (group, 0))
         local_result, state, decay = pl.pallas_call(
             functools.partial(state_kernel, modes),
             grid=(groups,),
-            in_specs=[feature_spec, feature_spec, rim_spec, par_spec, taps_spec],
+            in_specs=[feature_spec, feature_spec, rim_spec, par_spec, par_spec, taps_spec],
             out_specs=[feature_spec, state_spec, state_spec],
             out_shape=[
                 jax.ShapeDtypeStruct((rows, channels), jnp.float32),
                 jax.ShapeDtypeStruct((blocks * modes, LANES), jnp.float32),
                 jax.ShapeDtypeStruct((blocks * modes, LANES), jnp.float32),
             ],
-            scratch_shapes=[positions, positions],
+            scratch_shapes=[par_scratch, positions, positions],
             compiler_params=params(),
             cost_estimate=cost(9),
             name="conv_state",
-        )(hyena_k, hyena_v, rim, par, short_filter)
+        )(hyena_k, hyena_v, rim, *par, short_filter)
         return local_result, rim, par, decay, *entering_state(state, decay)
 
     def entering_state(state, decay):
@@ -235,11 +269,12 @@
         return pl.pallas_call(
             functools.partial(output_kernel, modes),
             grid=(groups,),
-            in_specs=[feature_spec, feature_spec, rim_spec, par_spec]
+            in_specs=[feature_spec, feature_spec, rim_spec, par_spec, par_spec]
             + [state_spec] * 4
             + [taps_spec],
             out_specs=feature_spec,
             out_shape=jax.ShapeDtypeStruct((rows, channels), jnp.bfloat16),
+            scratch_shapes=[par_scratch],
             compiler_params=params(),
             cost_estimate=cost(6),
             name="conv_output",
@@ -247,7 +282,7 @@
             hyena_q,
             local_result,
             rim,
-            par,
+            *par,
             decay,
             entering,
             entering_first,
@@ -557,7 +592,7 @@
     def send(chunk):
         key_pack = key_packs[chunk]
         if chunk >= LAG:
-            key_pack = after(key_pack, quad_kv[chunk - LAG][0], all_answers[chunk - LAG][0])
+            key_pack = after(key_pack, quad_kv[chunk - LAG][0], *all_answers[chunk - LAG][:1])
         quad_kv.append([lax.ppermute(key_pack, "ctx", gathers)])
         if chunk < asked:
             query_pack = query_packs[chunk]
@@ -622,19 +657,23 @@
             moves = [(target, source) for source, target in pairs]
             if asking:
                 moves += pairs
+            if chunk == chunks - 1:
+                live = (answer, conv_shared, [part[2] for part in returned], result)
+                answer, conv_shared, early, result = lax.optimization_barrier(live)
+                returned = [part[:2] + [back] for part, back in zip(returned, early)]
             arrivals.append(lax.ppermute(answer, "ctx", moves))
         if asking:
             asks[chunk + LAG] = arrivals
         returned.append([own, lse, arrivals])
         if chunk + LAG < chunks:
             send(chunk + LAG)
-    conv_shared = [after(part, all_answers[-1][0]) for part in conv_shared]
     hyena_out = conv_last(local_result, *conv_shared)
     for chunk, (own, lse, arrivals) in enumerate(returned):
+        if chunk == chunks - 1:
+            live = (arrivals, hyena_out, result)
+            arrivals, hyena_out, result = lax.optimization_barrier(live)
         parts = [own, lse]
         for arrival in arrivals:
-            if chunk == chunks - 1:
-                arrival = after(arrival, hyena_out, result)
             parts += [arrival, lax.ppermute(arrival, "ctx", swap)]
         steps = CHUNK_STEPS[chunk]
         count = 2 * len(transfers)

time: 134 us -> 127 us (0.948)
  the two profiles are of different devices: /device:TPU:29 before, /device:TPU:17 now
where the time goes in v12:
time: 127 us; the launch traced here: 126 us
  starting transfers between devices  59.9 us (47%)
  Pallas kernels  47.9 us (38%)
  waiting for transfers between devices  10.3 us (8%)
  other arithmetic  5.54 us (4%)
  local copies, waits for them, and re-layouts  1.4 us (1%)
    pallas_call x4, Pallas kernels, attend(): pl.pallas_call(functools.partial(partial_kernel, transfers, upper, natura...  19.1 us
    ppermute x4, starting transfers between devices, attend(): arrivals.append(lax.ppermute(answer, 'ctx', moves))  17.3 us
    ppermute x4, starting transfers between devices, attend(): quad_kv[chunk].append(lax.ppermute(quad_kv[chunk][0], 'ctx', swap))  10.9 us
    pallas_call x4, Pallas kernels, attend(): pl.pallas_call(functools.partial(merge_kernel, transfers, steps, starts[c...  10.6 us
    pallas_call x1, Pallas kernels, first_part(): pl.pallas_call(functools.partial(state_kernel, modes), grid=(groups,), in...  9.78 us
    ppermute x4, starting transfers between devices, attend(): parts += [arrival, lax.ppermute(arrival, 'ctx', swap)]  6.73 us
    pallas_call x1, Pallas kernels, last_part(): pl.pallas_call(functools.partial(output_kernel, modes), grid=(groups,), i...  6.31 us
    ppermute x4, waiting for transfers between devices, attend(): arrivals.append(lax.ppermute(answer, 'ctx', moves))  5.94 us
  transfers between devices with their start and end apart: 28, of which 3 were waited for; matrix products, arithmetic and copies ran while one was open for 4% of the time, Pallas kernels for 36%

profile of v12, /device:TPU:17, one launch (start us, length us, event | category | flops | bytes accessed | tf_op | source)
XLA Modules:
  0.0 126.1 jit_solution(15234156496605431710)
XLA Ops:
  0.6 0.7 collective-permute-start.2
  1.4 1.8 %conv_pack.1 = (f32[4,128,128]{2,1,0:T(8,128)}, f32[8,4096]{1,0:T(8,128)}) custom-call(f32[16,512]{1,0:T(8,128)} %bitcast.2, f32[16,512]{1,0:T(8,128)} %bitcast.3, bf16[128,4096]{1,0:T(8,128)(2,1)} %q_ref.5, bf16[128,4096]{1,0:T(8,128)(2,1)} %k_ref.5, bf16[128,4096]{1,0:T(8,128)(2,1)} %v_ref.5), custom_call_target="tpu_custom_call" | custom-call | flops 100000000 | bytes 65536 | tf_op jit(solution)/shard_map/conv_pack/pallas_call | solution.py:203
  3.2 3.1 %collective-permute-start.7 = (f32[8,4096]{1,0:T(8,128)}, f32[8,4096]{1,0:T(8,128)S(1)}, u32[]{:S(2)}, u32[]{:S(2)}) collective-permute-start(f32[8,4096]{1,0:T(8,128)} %get-tuple-element.53), channel_id=1, source_target_pairs={{0,1},{1,2},{2,3},{3,4},{4,5},{5,6},{6,7},{8,9},{9,10},{10,11},{11... | collective-permute-start | bytes 393224 | tf_op jit(solution)/shard_map/ppermute | solution.py:220
  6.3 0.2 att_pack.1
  6.5 2.0 %collective-permute-done.7.rim_ref = f32[8,4096]{1,0:T(8,128)S(1)} collective-permute-done((f32[8,4096]{1,0:T(8,128)}, f32[8,4096]{1,0:T(8,128)S(1)}, u32[]{:S(2)}, u32[]{:S(2)}) %collective-permute-start.7) | collective-permute-done | bytes 131104 | tf_op jit(solution)/shard_map/ppermute | solution.py:220
  8.6 3.6 %all-to-all-start = ((f32[4,128,128]{2,1,0:T(8,128)}), f32[4,128,128]{2,1,0:T(8,128)S(1)}, u32[]{:S(2)}, u32[]{:S(2)}) async-start(f32[4,128,128]{2,1,0:T(8,128)} %get-tuple-element.56), calls=%async_computation | async-start | bytes 524288 | tf_op jit(solution)/shard_map/all_to_all | solution.py:222
  12.2 2.7 %collective-permute-start = (bf16[128,4096]{1,0:T(8,128)(2,1)}, bf16[128,4096]{1,0:T(8,128)(2,1)}, u32[]{:S(2)}, u32[]{:S(2)}) collective-permute-start(bf16[128,4096]{1,0:T(8,128)(2,1)} %refs_1_.7), channel_id=1, source_target_pairs={{0,1},{1,0},{2,3},{3,2},{4,5},{5,4},{6,7},{7,6},{8,9},{9,8},{10,11... | collective-permute-start | bytes 3145736 | tf_op jit(solution)/shard_map/ppermute | solution.py:553
  14.9 1.5 %collective-permute-start.6 = (bf16[2,128,1024]{2,1,0:T(8,128)(2,1)}, bf16[2,128,1024]{2,1,0:T(8,128)(2,1)}, u32[]{:S(2)}, u32[]{:S(2)}) collective-permute-start(bf16[2,128,1024]{2,1,0:T(8,128)(2,1)} %get-tuple-element.52), channel_id=1, source_target_pairs={{0,2},{1,3},{8,10},{9,11},{16,18},{17,19},{24,26},{25,27}} | collective-permute-start | bytes 1572872 | tf_op jit(solution)/shard_map/ppermute | solution.py:596
  16.4 0.0 collective-permute-start.1
  16.4 0.7 copy-done
  17.1 3.1 %collective-permute-start.8 = (f32[4,128,128]{2,1,0:T(8,128)S(1)}, f32[4,128,128]{2,1,0:T(8,128)S(1)}, u32[]{:S(2)}, u32[]{:S(2)}) collective-permute-start(f32[4,128,128]{2,1,0:T(8,128)S(1)} %all-to-all-done.same_ref), channel_id=1, source_target_pairs={{0,1},{1,0},{2,3},{3,2},{4,5},{5,4},{6,7},{7,6},{8,9},{9,8},{10,11... | collective-permute-start | bytes 786440 | tf_op jit(solution)/shard_map/ppermute | solution.py:230
  20.2 1.3 %collective-permute-start.10 = (bf16[2,128,1024]{2,1,0:T(8,128)(2,1)}, bf16[2,128,1024]{2,1,0:T(8,128)(2,1)}, u32[]{:S(2)}, u32[]{:S(2)}) collective-permute-start(bf16[2,128,1024]{2,1,0:T(8,128)(2,1)} %get-tuple-element.55), channel_id=1, source_target_pairs={{7,5},{4,2},{6,3},{15,13},{12,10},{14,11},{23,21},{20,18},{22,19},... | collective-permute-start | bytes 1572872 | tf_op jit(solution)/shard_map/ppermute | solution.py:601
  21.5 0.7 copy-done.1
  22.2 1.5 %collective-permute-start.3 = (bf16[2,128,1024]{2,1,0:T(8,128)(2,1)}, bf16[2,128,1024]{2,1,0:T(8,128)(2,1)}, u32[]{:S(2)}, u32[]{:S(2)}) collective-permute-start(bf16[2,128,1024]{2,1,0:T(8,128)(2,1)} %get-tuple-element.50), channel_id=1, source_target_pairs={{0,2},{1,3},{8,10},{9,11},{16,18},{17,19},{24,26},{25,27}} | collective-permute-start | bytes 1572872 | tf_op jit(solution)/shard_map/ppermute | solution.py:596
  23.7 9.8 %conv_state.1 = (f32[128,4096]{1,0:T(8,128)}, f32[512,128]{1,0:T(8,128)}, f32[512,128]{1,0:T(8,128)}) custom-call(bf16[128,4096]{1,0:T(8,128)(2,1)} %k_ref.5, bf16[128,4096]{1,0:T(8,128)(2,1)} %v_ref.5, f32[8,4096]{1,0:T(8,128)} %copy-done.2, f32[4,128,128]{2,1,0:T(8,128)} %copy-done, f32[4,128,128]{2,1,0:T(8,128)} %copy-done.1, f32[3,3,4096]{2,1,0:T(4,128)} %taps_ref.3), custom_call_target="tpu_custom_call" | custom-call | flops 900000000 | bytes 65536 | tf_op jit(solution)/shard_map/conv_state/pallas_call | solution.py:232
  33.5 3.6 %collective-permute-start.9 = (bf16[2,128,1024]{2,1,0:T(8,128)(2,1)}, bf16[2,128,1024]{2,1,0:T(8,128)(2,1)}, u32[]{:S(2)}, u32[]{:S(2)}) collective-permute-start(bf16[2,128,1024]{2,1,0:T(8,128)(2,1)} %collective-permute-done.6.refs_5_), channel_id=1, source_target_pairs={{0,1},{1,0},{2,3},{3,2},{4,5},{5,4},{6,7},{7,6},{8,9},{9,8},{10,11... | collective-permute-start | bytes 1572872 | tf_op jit(solution)/shard_map/ppermute | solution.py:613
  37.2 0.0 collective-permute-done.10.refs_7_
  37.2 0.1 collective-permute-start.17
  37.2 0.0 collective-permute-done.refs_3_
  37.2 1.3 %collective-permute-start.5 = (bf16[2,128,1024]{2,1,0:T(8,128)(2,1)}, bf16[2,128,1024]{2,1,0:T(8,128)(2,1)}, u32[]{:S(2)}, u32[]{:S(2)}) collective-permute-start(bf16[2,128,1024]{2,1,0:T(8,128)(2,1)} %get-tuple-element.51), channel_id=1, source_target_pairs={{7,5},{4,2},{6,3},{15,13},{12,10},{14,11},{23,21},{20,18},{22,19},... | collective-permute-start | bytes 1572872 | tf_op jit(solution)/shard_map/ppermute | solution.py:601
  38.5 3.6 %collective-permute-start.4 = (bf16[2,128,1024]{2,1,0:T(8,128)(2,1)}, bf16[2,128,1024]{2,1,0:T(8,128)(2,1)}, u32[]{:S(2)}, u32[]{:S(2)}) collective-permute-start(bf16[2,128,1024]{2,1,0:T(8,128)(2,1)} %collective-permute-done.3.refs_5_), channel_id=1, source_target_pairs={{0,1},{1,0},{2,3},{3,2},{4,5},{5,4},{6,7},{7,6},{8,9},{9,8},{10,11... | collective-permute-start | bytes 1572872 | tf_op jit(solution)/shard_map/ppermute | solution.py:613
  42.1 4.8 %att_partial.4 = (f32[128,1024]{1,0:T(8,128)}, f32[16,128]{1,0:T(8,128)}, bf16[2176,128]{1,0:T(8,128)(2,1)}, bf16[128,4096]{1,0:T(8,128)(2,1)}) custom-call(bf16[128,4096]{1,0:T(8,128)(2,1)} %refs_0_.7, bf16[128,4096]{1,0:T(8,128)(2,1)} %refs_1_.7, bf16[128,4096]{1,0:T(8,128)(2,1)} %refs_2_.7, bf16[128,4096]{1,0:T(8,128)(2,1)} %collective-permute-done.refs_3_, ...), custom_call_target="tpu_custom_call" | custom-call | flops 400000000 | bytes 65536 | tf_op jit(solution)/shard_map/att_partial/pallas_call | solution.py:637
  46.9 1.5 %collective-permute-start.14 = (bf16[2,128,1024]{2,1,0:T(8,128)(2,1)}, bf16[2,128,1024]{2,1,0:T(8,128)(2,1)}, u32[]{:S(2)}, u32[]{:S(2)}) collective-permute-start(bf16[2,128,1024]{2,1,0:T(8,128)(2,1)} %get-tuple-element.65), channel_id=1, source_target_pairs={{0,2},{1,3},{8,10},{9,11},{16,18},{17,19},{24,26},{25,27}} | collective-permute-start | bytes 1572872 | tf_op jit(solution)/shard_map/ppermute | solution.py:596
  48.4 1.8 %multiply_add_fusion.2 = f32[512,128]{1,0:T(8,128)} fusion(f32[512,128]{1,0:T(8,128)} %get-tuple-element.70, f32[512,128]{1,0:T(8,128)} %get-tuple-element.77.decay_ref, f32[512,128]{1,0:T(8,128)} %collective-permute-done.17.other_ref), kind=kLoop, calls=%fused_computation.2 | loop fusion | flops 131072 | bytes 1048576 | tf_op jit(solution)/shard_map/add | solution.py:252
  50.2 1.9 %collective-permute-start.18 = (f32[512,128]{1,0:T(8,128)}, f32[512,128]{1,0:T(8,128)}, u32[]{:S(2)}, u32[]{:S(2)}) collective-permute-start(f32[512,128]{1,0:T(8,128)} %multiply_add_fusion.2), channel_id=1, source_target_pairs={{1,3},{3,5},{5,7},{9,11},{11,13},{13,15},{17,19},{19,21},{21,23},{... | collective-permute-start | bytes 786440 | tf_op jit(solution)/shard_map/ppermute | solution.py:257
  52.2 1.9 %collective-permute-start.16 = (bf16[2176,128]{1,0:T(8,128)(2,1)}, bf16[2176,128]{1,0:T(8,128)(2,1)}, u32[]{:S(2)}, u32[]{:S(2)}) collective-permute-start(bf16[2176,128]{1,0:T(8,128)(2,1)} %get-tuple-element.64), channel_id=1, source_target_pairs={{5,7},{2,4},{3,6},{7,5},{4,2},{6,3},{13,15},{10,12},{11,14},{15,13... | collective-permute-start | bytes 1671176 | tf_op jit(solution)/shard_map/ppermute | solution.py:664
  54.1 4.8 %att_partial.5 = (f32[128,1024]{1,0:T(8,128)}, f32[16,128]{1,0:T(8,128)}, bf16[2176,128]{1,0:T(8,128)(2,1)}, bf16[128,4096]{1,0:T(8,128)(2,1)}) custom-call(bf16[128,4096]{1,0:T(8,128)(2,1)} %refs_0_.7, bf16[128,4096]{1,0:T(8,128)(2,1)} %refs_1_.7, bf16[128,4096]{1,0:T(8,128)(2,1)} %refs_2_.7, ...), custom_call_target="tpu_custom_call", output_to_operand_aliasing={{3}: (10, {})} | custom-call | flops 400000000 | bytes 65536 | tf_op jit(solution)/shard_map/att_partial/pallas_call | solution.py:637
  59.0 1.5 %collective-permute-start.11 = (bf16[2,128,1024]{2,1,0:T(8,128)(2,1)}, bf16[2,128,1024]{2,1,0:T(8,128)(2,1)}, u32[]{:S(2)}, u32[]{:S(2)}) collective-permute-start(bf16[2,128,1024]{2,1,0:T(8,128)(2,1)} %get-tuple-element.62), channel_id=1, source_target_pairs={{0,2},{1,3},{8,10},{9,11},{16,18},{17,19},{24,26},{25,27}} | collective-permute-start | bytes 1572872 | tf_op jit(solution)/shard_map/ppermute | solution.py:596
  60.5 1.8 %multiply_add_fusion.1 = f32[512,128]{1,0:T(8,128)} fusion(f32[512,128]{1,0:T(8,128)} %multiply_add_fusion.2, f32[512,128]{1,0:T(8,128)} %collective-permute-done.18, f32[512,128]{1,0:T(8,128)} %get-tuple-element.77.decay_ref), kind=kLoop, calls=%fused_computation.1 | loop fusion | flops 196608 | bytes 1048576 | tf_op jit(solution)/shard_map/add | solution.py:263
  62.3 1.3 %collective-permute-start.19 = (f32[512,128]{1,0:T(8,128)}, f32[512,128]{1,0:T(8,128)}, u32[]{:S(2)}, u32[]{:S(2)}) collective-permute-start(f32[512,128]{1,0:T(8,128)} %multiply_add_fusion.1), channel_id=1, source_target_pairs={{1,5},{3,7},{9,13},{11,15},{17,21},{19,23},{25,29},{27,31}} | collective-permute-start | bytes 786440 | tf_op jit(solution)/shard_map/ppermute | solution.py:257
  63.6 3.6 %collective-permute-start.13 = (bf16[2176,128]{1,0:T(8,128)(2,1)}, bf16[2176,128]{1,0:T(8,128)(2,1)}, u32[]{:S(2)}, u32[]{:S(2)}) collective-permute-start(bf16[2176,128]{1,0:T(8,128)(2,1)} %get-tuple-element.61), channel_id=1, source_target_pairs={{5,7},{2,4},{3,6},{7,5},{4,2},{6,3},{13,15},{10,12},{11,14},{15,13... | collective-permute-start | bytes 1671176 | tf_op jit(solution)/shard_map/ppermute | solution.py:664
  67.3 3.6 %collective-permute-start.12 = (bf16[2,128,1024]{2,1,0:T(8,128)(2,1)}, bf16[2,128,1024]{2,1,0:T(8,128)(2,1)}, u32[]{:S(2)}, u32[]{:S(2)}) collective-permute-start(bf16[2,128,1024]{2,1,0:T(8,128)(2,1)} %collective-permute-done.11.refs_5_), channel_id=1, source_target_pairs={{0,1},{1,0},{2,3},{3,2},{4,5},{5,4},{6,7},{7,6},{8,9},{9,8},{10,11... | collective-permute-start | bytes 1572872 | tf_op jit(solution)/shard_map/ppermute | solution.py:613
  70.9 4.7 %att_partial.6 = (f32[128,1024]{1,0:T(8,128)}, f32[16,128]{1,0:T(8,128)}, bf16[2176,128]{1,0:T(8,128)(2,1)}, bf16[128,4096]{1,0:T(8,128)(2,1)}) custom-call(bf16[128,4096]{1,0:T(8,128)(2,1)} %refs_0_.7, bf16[128,4096]{1,0:T(8,128)(2,1)} %refs_1_.7, bf16[128,4096]{1,0:T(8,128)(2,1)} %refs_2_.7, ...), custom_call_target="tpu_custom_call", output_to_operand_aliasing={{3}: (8, {})} | custom-call | flops 400000000 | bytes 65536 | tf_op jit(solution)/shard_map/att_partial/pallas_call | solution.py:637
  75.6 5.6 %collective-permute-start.21 = (bf16[2176,128]{1,0:T(8,128)(2,1)}, bf16[2176,128]{1,0:T(8,128)(2,1)}, u32[]{:S(2)}, u32[]{:S(2)}) collective-permute-start(bf16[2176,128]{1,0:T(8,128)(2,1)} %get-tuple-element.71), channel_id=1, source_target_pairs={{5,7},{2,4},{3,6},{13,15},{10,12},{11,14},{21,23},{18,20},{19,22},... | collective-permute-start | bytes 1671176 | tf_op jit(solution)/shard_map/ppermute | solution.py:664
  81.3 1.8 %multiply_add_fusion.enter_ref = f32[512,128]{1,0:T(8,128)} fusion(f32[512,128]{1,0:T(8,128)} %collective-permute-done.18, f32[512,128]{1,0:T(8,128)} %collective-permute-done.19, f32[512,128]{1,0:T(8,128)} %get-tuple-element.77.decay_ref), kind=kLoop, calls=%fused_computation | loop fusion | flops 196608 | bytes 1048576 | tf_op jit(solution)/shard_map/add | solution.py:261
  83.1 4.8 %att_partial.7 = (f32[128,1024]{1,0:T(8,128)}, f32[16,128]{1,0:T(8,128)}, bf16[2176,128]{1,0:T(8,128)(2,1)}, bf16[128,4096]{1,0:T(8,128)(2,1)}) custom-call(bf16[128,4096]{1,0:T(8,128)(2,1)} %refs_0_.7, bf16[128,4096]{1,0:T(8,128)(2,1)} %refs_1_.7, bf16[128,4096]{1,0:T(8,128)(2,1)} %refs_2_.7, ...), custom_call_target="tpu_custom_call", output_to_operand_aliasing={{3}: (8, {})} | custom-call | flops 400000000 | bytes 65536 | tf_op jit(solution)/shard_map/att_partial/pallas_call | solution.py:637
  87.9 5.9 %collective-permute-done.21.refs_0_ = bf16[2176,128]{1,0:T(8,128)(2,1)} collective-permute-done((bf16[2176,128]{1,0:T(8,128)(2,1)}, bf16[2176,128]{1,0:T(8,128)(2,1)}, u32[]{:S(2)}, u32[]{:S(2)}) %collective-permute-start.21) | collective-permute-done | bytes 557088 | tf_op jit(solution)/shard_map/ppermute | solution.py:664
  93.8 6.2 %collective-permute-start.25 = (bf16[2176,128]{1,0:T(8,128)(2,1)}, bf16[2176,128]{1,0:T(8,128)(2,1)}, u32[]{:S(2)}, u32[]{:S(2)}) collective-permute-start(bf16[2176,128]{1,0:T(8,128)(2,1)} %collective-permute-done.16.refs_7_.refs_0_), channel_id=1, source_target_pairs={{0,1},{1,0},{2,3},{3,2},{4,5},{5,4},{6,7},{7,6},{8,9},{9,8},{10,11... | collective-permute-start | bytes 1671176 | tf_op jit(solution)/shard_map/ppermute | solution.py:677
  100.0 0.0 collective-permute-start.24
  100.0 0.5 collective-permute-start.23
  100.5 6.1 %collective-permute-start.22 = (bf16[2176,128]{1,0:T(8,128)(2,1)}, bf16[2176,128]{1,0:T(8,128)(2,1)}, u32[]{:S(2)}, u32[]{:S(2)}) collective-permute-start(bf16[2176,128]{1,0:T(8,128)(2,1)} %get-tuple-element.73), channel_id=1, source_target_pairs={{5,7},{2,4},{3,6},{13,15},{10,12},{11,14},{21,23},{18,20},{19,22},... | collective-permute-start | bytes 1671176 | tf_op jit(solution)/shard_map/ppermute | solution.py:664
  106.6 6.3 %conv_output.1 = bf16[128,4096]{1,0:T(8,128)(2,1)} custom-call(bf16[128,4096]{1,0:T(8,128)(2,1)} %q_ref.5, f32[128,4096]{1,0:T(8,128)} %get-tuple-element.57.y_ref, f32[8,4096]{1,0:T(8,128)} %copy-done.2, f32[4,128,128]{2,1,0:T(8,128)} %copy-done, f32[4,128,128]{2,1,0:T(8,128)} %copy-done.1, f32[512,128]{1,0:T(8,128)} %get-tuple-element.77.decay_ref, ...), custom_call_target="tpu_custom_call" | custom-call | flops 600000000 | bytes 65536 | tf_op jit(solution)/shard_map/conv_output/pallas_call | solution.py:269
  112.9 2.7 %att_merge.4.refs_2_ = bf16[128,4096]{1,0:T(8,128)(2,1)} custom-call(f32[128,1024]{1,0:T(8,128)} %get-tuple-element.87.own_hbm, f32[16,128]{1,0:T(8,128)} %get-tuple-element.88.lse_hbm, bf16[2176,128]{1,0:T(8,128)(2,1)} %collective-permute-done.16.refs_7_.refs_0_, bf16[2176,128]{1,0:T(8,128)(2,1)} %collective-permute-done.25.refs_1_, ...), custom_call_target="tpu_custom_call", output_to_operand_aliasing={{}: (4, {})} | custom-call | flops 200000000 | bytes 65536 | tf_op jit(solution)/shard_map/att_merge/pallas_call | solution.py:680
  115.6 2.7 %att_merge.5.refs_2_ = bf16[128,4096]{1,0:T(8,128)(2,1)} custom-call(f32[128,1024]{1,0:T(8,128)} %get-tuple-element.84.own_hbm, f32[16,128]{1,0:T(8,128)} %get-tuple-element.85.lse_hbm, bf16[2176,128]{1,0:T(8,128)(2,1)} %collective-permute-done.13.refs_7_.refs_0_, bf16[2176,128]{1,0:T(8,128)(2,1)} %collective-permute-done.24.refs_1_, ...), custom_call_target="tpu_custom_call", output_to_operand_aliasing={{}: (4, {})} | custom-call | flops 200000000 | bytes 65536 | tf_op jit(solution)/shard_map/att_merge/pallas_call | solution.py:680
  118.2 2.7 %att_merge.6.refs_2_ = bf16[128,4096]{1,0:T(8,128)(2,1)} custom-call(f32[128,1024]{1,0:T(8,128)} %get-tuple-element.81.own_hbm, f32[16,128]{1,0:T(8,128)} %get-tuple-element.82.lse_hbm, bf16[2176,128]{1,0:T(8,128)(2,1)} %collective-permute-done.21.refs_0_, bf16[2176,128]{1,0:T(8,128)(2,1)} %collective-permute-done.23.refs_1_, ...), custom_call_target="tpu_custom_call", output_to_operand_aliasing={{}: (4, {})} | custom-call | flops 200000000 | bytes 65536 | tf_op jit(solution)/shard_map/att_merge/pallas_call | solution.py:680
  120.9 0.1 collective-permute-start.26
  121.0 2.3 %collective-permute-done.26.refs_1_ = bf16[2176,128]{1,0:T(8,128)(2,1)} collective-permute-done((bf16[2176,128]{1,0:T(8,128)(2,1)}, bf16[2176,128]{1,0:T(8,128)(2,1)}, u32[]{:S(2)}, u32[]{:S(2)}) %collective-permute-start.26) | collective-permute-done | bytes 557088 | tf_op jit(solution)/shard_map/ppermute | solution.py:677
  123.3 2.6 %att_merge.7 = bf16[128,4096]{1,0:T(8,128)(2,1)} custom-call(f32[128,1024]{1,0:T(8,128)} %get-tuple-element.92.own_hbm, f32[16,128]{1,0:T(8,128)} %get-tuple-element.93.lse_hbm, bf16[2176,128]{1,0:T(8,128)(2,1)} %collective-permute-done.22.refs_0_, bf16[2176,128]{1,0:T(8,128)(2,1)} %collective-permute-done.26.refs_1_, ...), custom_call_target="tpu_custom_call", output_to_operand_aliasing={{}: (4, {})} | custom-call | flops 200000000 | bytes 65536 | tf_op jit(solution)/shard_map/att_merge/pallas_call | solution.py:680
  (29 shorter events, 0.1 us)
Async XLA Ops:
  0.6 5.7 %collective-permute-start.2 = (bf16[128,4096]{1,0:T(8,128)(2,1)}, bf16[128,4096]{1,0:T(8,128)(2,1)}, u32[]{:S(2)}, u32[]{:S(2)}) collective-permute-start(bf16[128,4096]{1,0:T(8,128)(2,1)} %refs_0_.7), channel_id=1, source_target_pairs={{0,1},{1,0},{2,3},{3,2},{4,5},{5,4},{6,7},{7,6},{8,9},{9,8},{10,11... | collective-permute-start | bytes 3145736 | tf_op jit(solution)/shard_map/ppermute | solution.py:552
  3.2 5.3 %collective-permute-start.7 = (f32[8,4096]{1,0:T(8,128)}, f32[8,4096]{1,0:T(8,128)S(1)}, u32[]{:S(2)}, u32[]{:S(2)}) collective-permute-start(f32[8,4096]{1,0:T(8,128)} %get-tuple-element.53), channel_id=1, source_target_pairs={{0,1},{1,2},{2,3},{3,4},{4,5},{5,6},{6,7},{8,9},{9,10},{10,11},{11... | collective-permute-start | bytes 393224 | tf_op jit(solution)/shard_map/ppermute | solution.py:220
  8.6 15.2 %copy-start.2 = (f32[8,4096]{1,0:T(8,128)}, f32[8,4096]{1,0:T(8,128)S(1)}, u32[]{:S(2)}) copy-start(f32[8,4096]{1,0:T(8,128)S(1)} %collective-permute-done.7.rim_ref) | copy-start | bytes 393220
  8.6 7.8 %all-to-all-start = ((f32[4,128,128]{2,1,0:T(8,128)}), f32[4,128,128]{2,1,0:T(8,128)S(1)}, u32[]{:S(2)}, u32[]{:S(2)}) async-start(f32[4,128,128]{2,1,0:T(8,128)} %get-tuple-element.56), calls=%async_computation | async-start | bytes 524288 | tf_op jit(solution)/shard_map/all_to_all | solution.py:222
  12.2 25.0 %collective-permute-start = (bf16[128,4096]{1,0:T(8,128)(2,1)}, bf16[128,4096]{1,0:T(8,128)(2,1)}, u32[]{:S(2)}, u32[]{:S(2)}) collective-permute-start(bf16[128,4096]{1,0:T(8,128)(2,1)} %refs_1_.7), channel_id=1, source_target_pairs={{0,1},{1,0},{2,3},{3,2},{4,5},{5,4},{6,7},{7,6},{8,9},{9,8},{10,11... | collective-permute-start | bytes 3145736 | tf_op jit(solution)/shard_map/ppermute | solution.py:553
  14.9 18.6 %collective-permute-start.6 = (bf16[2,128,1024]{2,1,0:T(8,128)(2,1)}, bf16[2,128,1024]{2,1,0:T(8,128)(2,1)}, u32[]{:S(2)}, u32[]{:S(2)}) collective-permute-start(bf16[2,128,1024]{2,1,0:T(8,128)(2,1)} %get-tuple-element.52), channel_id=1, source_target_pairs={{0,2},{1,3},{8,10},{9,11},{16,18},{17,19},{24,26},{25,27}} | collective-permute-start | bytes 1572872 | tf_op jit(solution)/shard_map/ppermute | solution.py:596
  16.4 25.7 %collective-permute-start.1 = (bf16[128,4096]{1,0:T(8,128)(2,1)}, bf16[128,4096]{1,0:T(8,128)(2,1)}, u32[]{:S(2)}, u32[]{:S(2)}) collective-permute-start(bf16[128,4096]{1,0:T(8,128)(2,1)} %refs_2_.7), channel_id=1, source_target_pairs={{0,1},{1,0},{2,3},{3,2},{4,5},{5,4},{6,7},{7,6},{8,9},{9,8},{10,11... | collective-permute-start | bytes 3145736 | tf_op jit(solution)/shard_map/ppermute | solution.py:554
  16.4 0.7 copy-start
  17.1 4.4 %collective-permute-start.8 = (f32[4,128,128]{2,1,0:T(8,128)S(1)}, f32[4,128,128]{2,1,0:T(8,128)S(1)}, u32[]{:S(2)}, u32[]{:S(2)}) collective-permute-start(f32[4,128,128]{2,1,0:T(8,128)S(1)} %all-to-all-done.same_ref), channel_id=1, source_target_pairs={{0,1},{1,0},{2,3},{3,2},{4,5},{5,4},{6,7},{7,6},{8,9},{9,8},{10,11... | collective-permute-start | bytes 786440 | tf_op jit(solution)/shard_map/ppermute | solution.py:230
  20.2 16.9 %collective-permute-start.10 = (bf16[2,128,1024]{2,1,0:T(8,128)(2,1)}, bf16[2,128,1024]{2,1,0:T(8,128)(2,1)}, u32[]{:S(2)}, u32[]{:S(2)}) collective-permute-start(bf16[2,128,1024]{2,1,0:T(8,128)(2,1)} %get-tuple-element.55), channel_id=1, source_target_pairs={{7,5},{4,2},{6,3},{15,13},{12,10},{14,11},{23,21},{20,18},{22,19},... | collective-permute-start | bytes 1572872 | tf_op jit(solution)/shard_map/ppermute | solution.py:601
  21.5 0.7 copy-start.1
  22.2 16.3 %collective-permute-start.3 = (bf16[2,128,1024]{2,1,0:T(8,128)(2,1)}, bf16[2,128,1024]{2,1,0:T(8,128)(2,1)}, u32[]{:S(2)}, u32[]{:S(2)}) collective-permute-start(bf16[2,128,1024]{2,1,0:T(8,128)(2,1)} %get-tuple-element.50), channel_id=1, source_target_pairs={{0,2},{1,3},{8,10},{9,11},{16,18},{17,19},{24,26},{25,27}} | collective-permute-start | bytes 1572872 | tf_op jit(solution)/shard_map/ppermute | solution.py:596
  33.5 8.6 %collective-permute-start.9 = (bf16[2,128,1024]{2,1,0:T(8,128)(2,1)}, bf16[2,128,1024]{2,1,0:T(8,128)(2,1)}, u32[]{:S(2)}, u32[]{:S(2)}) collective-permute-start(bf16[2,128,1024]{2,1,0:T(8,128)(2,1)} %collective-permute-done.6.refs_5_), channel_id=1, source_target_pairs={{0,1},{1,0},{2,3},{3,2},{4,5},{5,4},{6,7},{7,6},{8,9},{9,8},{10,11... | collective-permute-start | bytes 1572872 | tf_op jit(solution)/shard_map/ppermute | solution.py:613
  37.2 11.2 %collective-permute-start.17 = (f32[512,128]{1,0:T(8,128)}, f32[512,128]{1,0:T(8,128)}, u32[]{:S(2)}, u32[]{:S(2)}) collective-permute-start(f32[512,128]{1,0:T(8,128)} %get-tuple-element.70), channel_id=1, source_target_pairs={{0,1},{1,0},{2,3},{3,2},{4,5},{5,4},{6,7},{7,6},{8,9},{9,8},{10,11... | collective-permute-start | bytes 786440 | tf_op jit(solution)/shard_map/ppermute | solution.py:251
  37.2 16.9 %collective-permute-start.5 = (bf16[2,128,1024]{2,1,0:T(8,128)(2,1)}, bf16[2,128,1024]{2,1,0:T(8,128)(2,1)}, u32[]{:S(2)}, u32[]{:S(2)}) collective-permute-start(bf16[2,128,1024]{2,1,0:T(8,128)(2,1)} %get-tuple-element.51), channel_id=1, source_target_pairs={{7,5},{4,2},{6,3},{15,13},{12,10},{14,11},{23,21},{20,18},{22,19},... | collective-permute-start | bytes 1572872 | tf_op jit(solution)/shard_map/ppermute | solution.py:601
  38.5 15.6 %collective-permute-start.4 = (bf16[2,128,1024]{2,1,0:T(8,128)(2,1)}, bf16[2,128,1024]{2,1,0:T(8,128)(2,1)}, u32[]{:S(2)}, u32[]{:S(2)}) collective-permute-start(bf16[2,128,1024]{2,1,0:T(8,128)(2,1)} %collective-permute-done.3.refs_5_), channel_id=1, source_target_pairs={{0,1},{1,0},{2,3},{3,2},{4,5},{5,4},{6,7},{7,6},{8,9},{9,8},{10,11... | collective-permute-start | bytes 1572872 | tf_op jit(solution)/shard_map/ppermute | solution.py:613
  46.9 13.5 %collective-permute-start.14 = (bf16[2,128,1024]{2,1,0:T(8,128)(2,1)}, bf16[2,128,1024]{2,1,0:T(8,128)(2,1)}, u32[]{:S(2)}, u32[]{:S(2)}) collective-permute-start(bf16[2,128,1024]{2,1,0:T(8,128)(2,1)} %get-tuple-element.65), channel_id=1, source_target_pairs={{0,2},{1,3},{8,10},{9,11},{16,18},{17,19},{24,26},{25,27}} | collective-permute-start | bytes 1572872 | tf_op jit(solution)/shard_map/ppermute | solution.py:596
  50.2 10.2 %collective-permute-start.18 = (f32[512,128]{1,0:T(8,128)}, f32[512,128]{1,0:T(8,128)}, u32[]{:S(2)}, u32[]{:S(2)}) collective-permute-start(f32[512,128]{1,0:T(8,128)} %multiply_add_fusion.2), channel_id=1, source_target_pairs={{1,3},{3,5},{5,7},{9,11},{11,13},{13,15},{17,19},{19,21},{21,23},{... | collective-permute-start | bytes 786440 | tf_op jit(solution)/shard_map/ppermute | solution.py:257
  52.2 18.7 %collective-permute-start.16 = (bf16[2176,128]{1,0:T(8,128)(2,1)}, bf16[2176,128]{1,0:T(8,128)(2,1)}, u32[]{:S(2)}, u32[]{:S(2)}) collective-permute-start(bf16[2176,128]{1,0:T(8,128)(2,1)} %get-tuple-element.64), channel_id=1, source_target_pairs={{5,7},{2,4},{3,6},{7,5},{4,2},{6,3},{13,15},{10,12},{11,14},{15,13... | collective-permute-start | bytes 1671176 | tf_op jit(solution)/shard_map/ppermute | solution.py:664
  59.0 8.3 %collective-permute-start.11 = (bf16[2,128,1024]{2,1,0:T(8,128)(2,1)}, bf16[2,128,1024]{2,1,0:T(8,128)(2,1)}, u32[]{:S(2)}, u32[]{:S(2)}) collective-permute-start(bf16[2,128,1024]{2,1,0:T(8,128)(2,1)} %get-tuple-element.62), channel_id=1, source_target_pairs={{0,2},{1,3},{8,10},{9,11},{16,18},{17,19},{24,26},{25,27}} | collective-permute-start | bytes 1572872 | tf_op jit(solution)/shard_map/ppermute | solution.py:596
  60.5 10.5 %collective-permute-start.15 = (bf16[2,128,1024]{2,1,0:T(8,128)(2,1)}, bf16[2,128,1024]{2,1,0:T(8,128)(2,1)}, u32[]{:S(2)}, u32[]{:S(2)}) collective-permute-start(bf16[2,128,1024]{2,1,0:T(8,128)(2,1)} %collective-permute-done.14.refs_5_), channel_id=1, source_target_pairs={{0,1},{1,0},{2,3},{3,2},{4,5},{5,4},{6,7},{7,6},{8,9},{9,8},{10,11... | collective-permute-start | bytes 1572872 | tf_op jit(solution)/shard_map/ppermute | solution.py:613
  62.3 19.0 %collective-permute-start.19 = (f32[512,128]{1,0:T(8,128)}, f32[512,128]{1,0:T(8,128)}, u32[]{:S(2)}, u32[]{:S(2)}) collective-permute-start(f32[512,128]{1,0:T(8,128)} %multiply_add_fusion.1), channel_id=1, source_target_pairs={{1,5},{3,7},{9,13},{11,15},{17,21},{19,23},{25,29},{27,31}} | collective-permute-start | bytes 786440 | tf_op jit(solution)/shard_map/ppermute | solution.py:257
  63.6 19.5 %collective-permute-start.13 = (bf16[2176,128]{1,0:T(8,128)(2,1)}, bf16[2176,128]{1,0:T(8,128)(2,1)}, u32[]{:S(2)}, u32[]{:S(2)}) collective-permute-start(bf16[2176,128]{1,0:T(8,128)(2,1)} %get-tuple-element.61), channel_id=1, source_target_pairs={{5,7},{2,4},{3,6},{7,5},{4,2},{6,3},{13,15},{10,12},{11,14},{15,13... | collective-permute-start | bytes 1671176 | tf_op jit(solution)/shard_map/ppermute | solution.py:664
  67.3 15.9 %collective-permute-start.12 = (bf16[2,128,1024]{2,1,0:T(8,128)(2,1)}, bf16[2,128,1024]{2,1,0:T(8,128)(2,1)}, u32[]{:S(2)}, u32[]{:S(2)}) collective-permute-start(bf16[2,128,1024]{2,1,0:T(8,128)(2,1)} %collective-permute-done.11.refs_5_), channel_id=1, source_target_pairs={{0,1},{1,0},{2,3},{3,2},{4,5},{5,4},{6,7},{7,6},{8,9},{9,8},{10,11... | collective-permute-start | bytes 1572872 | tf_op jit(solution)/shard_map/ppermute | solution.py:613
  75.6 18.2 %collective-permute-start.21 = (bf16[2176,128]{1,0:T(8,128)(2,1)}, bf16[2176,128]{1,0:T(8,128)(2,1)}, u32[]{:S(2)}, u32[]{:S(2)}) collective-permute-start(bf16[2176,128]{1,0:T(8,128)(2,1)} %get-tuple-element.71), channel_id=1, source_target_pairs={{5,7},{2,4},{3,6},{13,15},{10,12},{11,14},{21,23},{18,20},{19,22},... | collective-permute-start | bytes 1671176 | tf_op jit(solution)/shard_map/ppermute | solution.py:664
  83.1 4.8 %collective-permute-start.20 = (f32[512,128]{1,0:T(8,128)}, f32[512,128]{1,0:T(8,128)}, u32[]{:S(2)}, u32[]{:S(2)}) collective-permute-start(f32[512,128]{1,0:T(8,128)} %multiply_add_fusion.enter_ref), channel_id=1, source_target_pairs={{0,1},{1,0},{2,3},{3,2},{4,5},{5,4},{6,7},{7,6},{8,9},{9,8},{10,11... | collective-permute-start | bytes 786440 | tf_op jit(solution)/shard_map/ppermute | solution.py:265
  93.8 19.1 %collective-permute-start.25 = (bf16[2176,128]{1,0:T(8,128)(2,1)}, bf16[2176,128]{1,0:T(8,128)(2,1)}, u32[]{:S(2)}, u32[]{:S(2)}) collective-permute-start(bf16[2176,128]{1,0:T(8,128)(2,1)} %collective-permute-done.16.refs_7_.refs_0_), channel_id=1, source_target_pairs={{0,1},{1,0},{2,3},{3,2},{4,5},{5,4},{6,7},{7,6},{8,9},{9,8},{10,11... | collective-permute-start | bytes 1671176 | tf_op jit(solution)/shard_map/ppermute | solution.py:677
  100.0 15.6 %collective-permute-start.24 = (bf16[2176,128]{1,0:T(8,128)(2,1)}, bf16[2176,128]{1,0:T(8,128)(2,1)}, u32[]{:S(2)}, u32[]{:S(2)}) collective-permute-start(bf16[2176,128]{1,0:T(8,128)(2,1)} %collective-permute-done.13.refs_7_.refs_0_), channel_id=1, source_target_pairs={{0,1},{1,0},{2,3},{3,2},{4,5},{5,4},{6,7},{7,6},{8,9},{9,8},{10,11... | collective-permute-start | bytes 1671176 | tf_op jit(solution)/shard_map/ppermute | solution.py:677
  100.0 18.2 %collective-permute-start.23 = (bf16[2176,128]{1,0:T(8,128)(2,1)}, bf16[2176,128]{1,0:T(8,128)(2,1)}, u32[]{:S(2)}, u32[]{:S(2)}) collective-permute-start(bf16[2176,128]{1,0:T(8,128)(2,1)} %collective-permute-done.21.refs_0_), channel_id=1, source_target_pairs={{0,1},{1,0},{2,3},{3,2},{4,5},{5,4},{6,7},{7,6},{8,9},{9,8},{10,11... | collective-permute-start | bytes 1671176 | tf_op jit(solution)/shard_map/ppermute | solution.py:677
  100.5 20.4 %collective-permute-start.22 = (bf16[2176,128]{1,0:T(8,128)(2,1)}, bf16[2176,128]{1,0:T(8,128)(2,1)}, u32[]{:S(2)}, u32[]{:S(2)}) collective-permute-start(bf16[2176,128]{1,0:T(8,128)(2,1)} %get-tuple-element.73), channel_id=1, source_target_pairs={{5,7},{2,4},{3,6},{13,15},{10,12},{11,14},{21,23},{18,20},{19,22},... | collective-permute-start | bytes 1671176 | tf_op jit(solution)/shard_map/ppermute | solution.py:664
  120.9 2.4 %collective-permute-start.26 = (bf16[2176,128]{1,0:T(8,128)(2,1)}, bf16[2176,128]{1,0:T(8,128)(2,1)}, u32[]{:S(2)}, u32[]{:S(2)}) collective-permute-start(bf16[2176,128]{1,0:T(8,128)(2,1)} %collective-permute-done.22.refs_0_), channel_id=1, source_target_pairs={{0,1},{1,0},{2,3},{3,2},{4,5},{5,4},{6,7},{7,6},{8,9},{9,8},{10,11... | collective-permute-start | bytes 1671176 | tf_op jit(solution)/shard_map/ppermute | solution.py:677

commit v13 on v12

--- a/solution.py
+++ b/solution.py
@@ -592,7 +592,8 @@
     def send(chunk):
         key_pack = key_packs[chunk]
         if chunk >= LAG:
-            key_pack = after(key_pack, quad_kv[chunk - LAG][0], *all_answers[chunk - LAG][:1])
+            earlier = all_answers[chunk - LAG - 1] if chunk > LAG else asks[0]
+            key_pack = after(key_pack, quad_kv[chunk - LAG][0], earlier[0])
         quad_kv.append([lax.ppermute(key_pack, "ctx", gathers)])
         if chunk < asked:
             query_pack = query_packs[chunk]

time: 127 us -> 131 us (1.031)
  starting transfers between devices: 59.9 us -> 64.8 us
    ppermute x4, starting transfers between devices: 10.9 us -> 17.2 us  [attend(): quad_kv[chunk].append(lax.ppermute(quad_kv[chunk][0], 'ctx', swap))]
    ppermute x4, starting transfers between devices: 17.3 us -> 11.1 us  [attend(): arrivals.append(lax.ppermute(answer, 'ctx', moves))]
    ppermute x1, starting transfers between devices: 0.09 us -> 3.44 us  [entering_state(): other = lax.ppermute(state, 'ctx', swap)]
  transfers between devices with their start and end apart: 28 -> 28, of which waited for: 3 -> 4; matrix products, arithmetic and copies ran while one was open for 4% -> 4% of each run, Pallas kernels for 36% -> 35%
where the time goes in v13:
time: 131 us; the launch traced here: 130 us
  starting transfers between devices  64.8 us (49%)
  Pallas kernels  47.9 us (37%)
  waiting for transfers between devices  10.5 us (8%)
  other arithmetic  5.52 us (4%)
    pallas_call x4, Pallas kernels, attend(): pl.pallas_call(functools.partial(partial_kernel, transfers, upper, natura...  19.1 us
    ppermute x4, starting transfers between devices, attend(): quad_kv[chunk].append(lax.ppermute(quad_kv[chunk][0], 'ctx', swap))  17.2 us
    ppermute x4, starting transfers between devices, attend(): arrivals.append(lax.ppermute(answer, 'ctx', moves))  11.1 us
    pallas_call x4, Pallas kernels, attend(): pl.pallas_call(functools.partial(merge_kernel, transfers, steps, starts[c...  10.6 us
    pallas_call x1, Pallas kernels, first_part(): pl.pallas_call(functools.partial(state_kernel, modes), grid=(groups,), in...  9.79 us
    ppermute x4, starting transfers between devices, attend(): parts += [arrival, lax.ppermute(arrival, 'ctx', swap)]  6.87 us
    pallas_call x1, Pallas kernels, last_part(): pl.pallas_call(functools.partial(output_kernel, modes), grid=(groups,), i...  6.31 us
    ppermute x4, starting transfers between devices, send(): quad_kv.append([lax.ppermute(key_pack, 'ctx', gathers)])  5.83 us
  transfers between devices with their start and end apart: 28, of which 4 were waited for; matrix products, arithmetic and copies ran while one was open for 4% of the time, Pallas kernels for 35%

profile of v13, /device:TPU:17, one launch (start us, length us, event | category | flops | bytes accessed | tf_op | source)
XLA Modules:
  0.0 130.4 jit_solution(17437621069952435773)
XLA Ops:
  0.6 0.7 collective-permute-start.2
  1.4 1.9 %conv_pack.1 = (f32[4,128,128]{2,1,0:T(8,128)}, f32[8,4096]{1,0:T(8,128)}) custom-call(f32[16,512]{1,0:T(8,128)} %bitcast.2, f32[16,512]{1,0:T(8,128)} %bitcast.3, bf16[128,4096]{1,0:T(8,128)(2,1)} %q_ref.5, bf16[128,4096]{1,0:T(8,128)(2,1)} %k_ref.5, bf16[128,4096]{1,0:T(8,128)(2,1)} %v_ref.5), custom_call_target="tpu_custom_call" | custom-call | flops 100000000 | bytes 65536 | tf_op jit(solution)/shard_map/conv_pack/pallas_call | solution.py:203
  3.2 3.1 %collective-permute-start.5 = (f32[8,4096]{1,0:T(8,128)}, f32[8,4096]{1,0:T(8,128)S(1)}, u32[]{:S(2)}, u32[]{:S(2)}) collective-permute-start(f32[8,4096]{1,0:T(8,128)} %get-tuple-element.52), channel_id=1, source_target_pairs={{0,1},{1,2},{2,3},{3,4},{4,5},{5,6},{6,7},{8,9},{9,10},{10,11},{11... | collective-permute-start | bytes 393224 | tf_op jit(solution)/shard_map/ppermute | solution.py:220
  6.3 0.2 att_pack.1
  6.5 2.0 %collective-permute-done.5.rim_ref = f32[8,4096]{1,0:T(8,128)S(1)} collective-permute-done((f32[8,4096]{1,0:T(8,128)}, f32[8,4096]{1,0:T(8,128)S(1)}, u32[]{:S(2)}, u32[]{:S(2)}) %collective-permute-start.5) | collective-permute-done | bytes 131104 | tf_op jit(solution)/shard_map/ppermute | solution.py:220
  8.6 3.7 %all-to-all-start = ((f32[4,128,128]{2,1,0:T(8,128)}), f32[4,128,128]{2,1,0:T(8,128)S(1)}, u32[]{:S(2)}, u32[]{:S(2)}) async-start(f32[4,128,128]{2,1,0:T(8,128)} %get-tuple-element.55), calls=%async_computation | async-start | bytes 524288 | tf_op jit(solution)/shard_map/all_to_all | solution.py:222
  12.2 2.7 %collective-permute-start = (bf16[128,4096]{1,0:T(8,128)(2,1)}, bf16[128,4096]{1,0:T(8,128)(2,1)}, u32[]{:S(2)}, u32[]{:S(2)}) collective-permute-start(bf16[128,4096]{1,0:T(8,128)(2,1)} %refs_1_.7), channel_id=1, source_target_pairs={{0,1},{1,0},{2,3},{3,2},{4,5},{5,4},{6,7},{7,6},{8,9},{9,8},{10,11... | collective-permute-start | bytes 3145736 | tf_op jit(solution)/shard_map/ppermute | solution.py:553
  14.9 0.0 collective-permute-start.1
  14.9 1.0 all-to-all-done.same_ref
  16.0 0.7 copy-done
  16.7 3.6 %collective-permute-start.6 = (f32[4,128,128]{2,1,0:T(8,128)S(1)}, f32[4,128,128]{2,1,0:T(8,128)}, u32[]{:S(2)}, u32[]{:S(2)}) collective-permute-start(f32[4,128,128]{2,1,0:T(8,128)S(1)} %all-to-all-done.same_ref), channel_id=1, source_target_pairs={{0,1},{1,0},{2,3},{3,2},{4,5},{5,4},{6,7},{7,6},{8,9},{9,8},{10,11... | collective-permute-start | bytes 786440 | tf_op jit(solution)/shard_map/ppermute | solution.py:230
  20.3 1.5 %collective-permute-start.4 = (bf16[2,128,1024]{2,1,0:T(8,128)(2,1)}, bf16[2,128,1024]{2,1,0:T(8,128)(2,1)}, u32[]{:S(2)}, u32[]{:S(2)}) collective-permute-start(bf16[2,128,1024]{2,1,0:T(8,128)(2,1)} %get-tuple-element.51), channel_id=1, source_target_pairs={{0,2},{1,3},{8,10},{9,11},{16,18},{17,19},{24,26},{25,27}} | collective-permute-start | bytes 1572872 | tf_op jit(solution)/shard_map/ppermute | solution.py:597
  21.7 1.3 collective-permute-start.8
  23.0 0.0 collective-permute-done.6.other_ref.other_par_ref
  23.0 9.8 %conv_state.1 = (f32[128,4096]{1,0:T(8,128)}, f32[512,128]{1,0:T(8,128)}, f32[512,128]{1,0:T(8,128)}) custom-call(bf16[128,4096]{1,0:T(8,128)(2,1)} %k_ref.5, bf16[128,4096]{1,0:T(8,128)(2,1)} %v_ref.5, f32[8,4096]{1,0:T(8,128)} %copy-done.2, f32[4,128,128]{2,1,0:T(8,128)} %copy-done, f32[4,128,128]{2,1,0:T(8,128)} %collective-permute-done.6.other_ref.other_par_ref, ...), custom_call_target="tpu_custom_call" | custom-call | flops 900000000 | bytes 65536 | tf_op jit(solution)/shard_map/conv_state/pallas_call | solution.py:232
  32.8 3.4 %collective-permute-start.17 = (f32[512,128]{1,0:T(8,128)}, f32[512,128]{1,0:T(8,128)S(1)}, u32[]{:S(2)}, u32[]{:S(2)}) collective-permute-start(f32[512,128]{1,0:T(8,128)} %get-tuple-element.70), channel_id=1, source_target_pairs={{0,1},{1,0},{2,3},{3,2},{4,5},{5,4},{6,7},{7,6},{8,9},{9,8},{10,11... | collective-permute-start | bytes 786440 | tf_op jit(solution)/shard_map/ppermute | solution.py:251
  36.3 1.5 %collective-permute-start.3 = (bf16[2,128,1024]{2,1,0:T(8,128)(2,1)}, bf16[2,128,1024]{2,1,0:T(8,128)(2,1)}, u32[]{:S(2)}, u32[]{:S(2)}) collective-permute-start(bf16[2,128,1024]{2,1,0:T(8,128)(2,1)} %get-tuple-element.50), channel_id=1, source_target_pairs={{0,2},{1,3},{8,10},{9,11},{16,18},{17,19},{24,26},{25,27}} | collective-permute-start | bytes 1572872 | tf_op jit(solution)/shard_map/ppermute | solution.py:597
  37.7 0.5 collective-permute-start.7
  38.3 1.5 %collective-permute-start.14 = (bf16[2,128,1024]{2,1,0:T(8,128)(2,1)}, bf16[2,128,1024]{2,1,0:T(8,128)(2,1)}, u32[]{:S(2)}, u32[]{:S(2)}) collective-permute-start(bf16[2,128,1024]{2,1,0:T(8,128)(2,1)} %get-tuple-element.65), channel_id=1, source_target_pairs={{0,2},{1,3},{8,10},{9,11},{16,18},{17,19},{24,26},{25,27}} | collective-permute-start | bytes 1572872 | tf_op jit(solution)/shard_map/ppermute | solution.py:597
  39.7 1.8 %multiply_add_fusion.2 = f32[512,128]{1,0:T(8,128)} fusion(f32[512,128]{1,0:T(8,128)} %get-tuple-element.70, f32[512,128]{1,0:T(8,128)} %get-tuple-element.77.decay_ref, f32[512,128]{1,0:T(8,128)S(1)} %collective-permute-done.17.other_ref), kind=kLoop, calls=%fused_computation.2 | loop fusion | flops 131072 | bytes 1048576 | tf_op jit(solution)/shard_map/add | solution.py:252
  41.5 2.7 %collective-permute-start.18 = (f32[512,128]{1,0:T(8,128)}, f32[512,128]{1,0:T(8,128)}, u32[]{:S(2)}, u32[]{:S(2)}) collective-permute-start(f32[512,128]{1,0:T(8,128)} %multiply_add_fusion.2), channel_id=1, source_target_pairs={{1,3},{3,5},{5,7},{9,11},{11,13},{13,15},{17,19},{19,21},{21,23},{... | collective-permute-start | bytes 786440 | tf_op jit(solution)/shard_map/ppermute | solution.py:257
  44.2 1.3 collective-permute-start.12
  45.5 2.4 %collective-permute-start.11 = (bf16[2,128,1024]{2,1,0:T(8,128)(2,1)}, bf16[2,128,1024]{2,1,0:T(8,128)(2,1)}, u32[]{:S(2)}, u32[]{:S(2)}) collective-permute-start(bf16[2,128,1024]{2,1,0:T(8,128)(2,1)} %collective-permute-done.3.refs_5_), channel_id=1, source_target_pairs={{0,1},{1,0},{2,3},{3,2},{4,5},{5,4},{6,7},{7,6},{8,9},{9,8},{10,11... | collective-permute-start | bytes 1572872 | tf_op jit(solution)/shard_map/ppermute | solution.py:614
  48.0 4.8 %att_partial.4 = (f32[128,1024]{1,0:T(8,128)}, f32[16,128]{1,0:T(8,128)}, bf16[2176,128]{1,0:T(8,128)(2,1)}, bf16[128,4096]{1,0:T(8,128)(2,1)}) custom-call(bf16[128,4096]{1,0:T(8,128)(2,1)} %refs_0_.7, bf16[128,4096]{1,0:T(8,128)(2,1)} %refs_1_.7, bf16[128,4096]{1,0:T(8,128)(2,1)} %refs_2_.7, bf16[128,4096]{1,0:T(8,128)(2,1)} %collective-permute-done.refs_3_, ...), custom_call_target="tpu_custom_call" | custom-call | flops 400000000 | bytes 65536 | tf_op jit(solution)/shard_map/att_partial/pallas_call | solution.py:638
  52.8 2.5 %collective-permute-start.16 = (bf16[2176,128]{1,0:T(8,128)(2,1)}, bf16[2176,128]{1,0:T(8,128)(2,1)}, u32[]{:S(2)}, u32[]{:S(2)}) collective-permute-start(bf16[2176,128]{1,0:T(8,128)(2,1)} %get-tuple-element.59), channel_id=1, source_target_pairs={{5,7},{2,4},{3,6},{7,5},{4,2},{6,3},{13,15},{10,12},{11,14},{15,13... | collective-permute-start | bytes 1671176 | tf_op jit(solution)/shard_map/ppermute | solution.py:665
  55.3 1.5 %collective-permute-start.9 = (bf16[2,128,1024]{2,1,0:T(8,128)(2,1)}, bf16[2,128,1024]{2,1,0:T(8,128)(2,1)}, u32[]{:S(2)}, u32[]{:S(2)}) collective-permute-start(bf16[2,128,1024]{2,1,0:T(8,128)(2,1)} %get-tuple-element.60), channel_id=1, source_target_pairs={{0,2},{1,3},{8,10},{9,11},{16,18},{17,19},{24,26},{25,27}} | collective-permute-start | bytes 1572872 | tf_op jit(solution)/shard_map/ppermute | solution.py:597
  56.8 8.1 %collective-permute-start.15 = (bf16[2,128,1024]{2,1,0:T(8,128)(2,1)}, bf16[2,128,1024]{2,1,0:T(8,128)(2,1)}, u32[]{:S(2)}, u32[]{:S(2)}) collective-permute-start(bf16[2,128,1024]{2,1,0:T(8,128)(2,1)} %collective-permute-done.14.refs_5_), channel_id=1, source_target_pairs={{0,1},{1,0},{2,3},{3,2},{4,5},{5,4},{6,7},{7,6},{8,9},{9,8},{10,11... | collective-permute-start | bytes 1572872 | tf_op jit(solution)/shard_map/ppermute | solution.py:614
  64.9 1.8 %multiply_add_fusion.1 = f32[512,128]{1,0:T(8,128)} fusion(f32[512,128]{1,0:T(8,128)} %multiply_add_fusion.2, f32[512,128]{1,0:T(8,128)} %collective-permute-done.18, f32[512,128]{1,0:T(8,128)} %get-tuple-element.77.decay_ref), kind=kLoop, calls=%fused_computation.1 | loop fusion | flops 196608 | bytes 1048576 | tf_op jit(solution)/shard_map/add | solution.py:263
  66.7 1.3 collective-permute-start.19
  68.0 4.8 %att_partial.5 = (f32[128,1024]{1,0:T(8,128)}, f32[16,128]{1,0:T(8,128)}, bf16[2176,128]{1,0:T(8,128)(2,1)}, bf16[128,4096]{1,0:T(8,128)(2,1)}) custom-call(bf16[128,4096]{1,0:T(8,128)(2,1)} %refs_0_.7, bf16[128,4096]{1,0:T(8,128)(2,1)} %refs_1_.7, bf16[128,4096]{1,0:T(8,128)(2,1)} %refs_2_.7, ...), custom_call_target="tpu_custom_call", output_to_operand_aliasing={{3}: (10, {})} | custom-call | flops 400000000 | bytes 65536 | tf_op jit(solution)/shard_map/att_partial/pallas_call | solution.py:638
  72.9 2.0 %collective-permute-start.13 = (bf16[2176,128]{1,0:T(8,128)(2,1)}, bf16[2176,128]{1,0:T(8,128)(2,1)}, u32[]{:S(2)}, u32[]{:S(2)}) collective-permute-start(bf16[2176,128]{1,0:T(8,128)(2,1)} %get-tuple-element.63), channel_id=1, source_target_pairs={{5,7},{2,4},{3,6},{7,5},{4,2},{6,3},{13,15},{10,12},{11,14},{15,13... | collective-permute-start | bytes 1671176 | tf_op jit(solution)/shard_map/ppermute | solution.py:665
  74.8 6.1 %collective-permute-start.10 = (bf16[2,128,1024]{2,1,0:T(8,128)(2,1)}, bf16[2,128,1024]{2,1,0:T(8,128)(2,1)}, u32[]{:S(2)}, u32[]{:S(2)}) collective-permute-start(bf16[2,128,1024]{2,1,0:T(8,128)(2,1)} %collective-permute-done.9.refs_5_), channel_id=1, source_target_pairs={{0,1},{1,0},{2,3},{3,2},{4,5},{5,4},{6,7},{7,6},{8,9},{9,8},{10,11... | collective-permute-start | bytes 1572872 | tf_op jit(solution)/shard_map/ppermute | solution.py:614
  80.9 4.7 %att_partial.6 = (f32[128,1024]{1,0:T(8,128)}, f32[16,128]{1,0:T(8,128)}, bf16[2176,128]{1,0:T(8,128)(2,1)}, bf16[128,4096]{1,0:T(8,128)(2,1)}) custom-call(bf16[128,4096]{1,0:T(8,128)(2,1)} %refs_0_.7, bf16[128,4096]{1,0:T(8,128)(2,1)} %refs_1_.7, bf16[128,4096]{1,0:T(8,128)(2,1)} %refs_2_.7, ...), custom_call_target="tpu_custom_call", output_to_operand_aliasing={{3}: (8, {})} | custom-call | flops 400000000 | bytes 65536 | tf_op jit(solution)/shard_map/att_partial/pallas_call | solution.py:638
  85.7 2.8 %collective-permute-start.21 = (bf16[2176,128]{1,0:T(8,128)(2,1)}, bf16[2176,128]{1,0:T(8,128)(2,1)}, u32[]{:S(2)}, u32[]{:S(2)}) collective-permute-start(bf16[2176,128]{1,0:T(8,128)(2,1)} %get-tuple-element.71), channel_id=1, source_target_pairs={{5,7},{2,4},{3,6},{13,15},{10,12},{11,14},{21,23},{18,20},{19,22},... | collective-permute-start | bytes 1671176 | tf_op jit(solution)/shard_map/ppermute | solution.py:665
  88.5 1.9 %multiply_add_fusion.enter_ref = f32[512,128]{1,0:T(8,128)} fusion(f32[512,128]{1,0:T(8,128)} %collective-permute-done.18, f32[512,128]{1,0:T(8,128)} %collective-permute-done.19, f32[512,128]{1,0:T(8,128)} %get-tuple-element.77.decay_ref), kind=kLoop, calls=%fused_computation | loop fusion | flops 196608 | bytes 1048576 | tf_op jit(solution)/shard_map/add | solution.py:261
  90.4 4.8 %att_partial.7 = (f32[128,1024]{1,0:T(8,128)}, f32[16,128]{1,0:T(8,128)}, bf16[2176,128]{1,0:T(8,128)(2,1)}, bf16[128,4096]{1,0:T(8,128)(2,1)}) custom-call(bf16[128,4096]{1,0:T(8,128)(2,1)} %refs_0_.7, bf16[128,4096]{1,0:T(8,128)(2,1)} %refs_1_.7, bf16[128,4096]{1,0:T(8,128)(2,1)} %refs_2_.7, ...), custom_call_target="tpu_custom_call", output_to_operand_aliasing={{3}: (8, {})} | custom-call | flops 400000000 | bytes 65536 | tf_op jit(solution)/shard_map/att_partial/pallas_call | solution.py:638
  95.2 5.1 %collective-permute-done.21.refs_0_ = bf16[2176,128]{1,0:T(8,128)(2,1)} collective-permute-done((bf16[2176,128]{1,0:T(8,128)(2,1)}, bf16[2176,128]{1,0:T(8,128)(2,1)}, u32[]{:S(2)}, u32[]{:S(2)}) %collective-permute-start.21) | collective-permute-done | bytes 557088 | tf_op jit(solution)/shard_map/ppermute | solution.py:665
  100.3 6.3 %collective-permute-start.25 = (bf16[2176,128]{1,0:T(8,128)(2,1)}, bf16[2176,128]{1,0:T(8,128)(2,1)}, u32[]{:S(2)}, u32[]{:S(2)}) collective-permute-start(bf16[2176,128]{1,0:T(8,128)(2,1)} %collective-permute-done.16.refs_7_.refs_0_), channel_id=1, source_target_pairs={{0,1},{1,0},{2,3},{3,2},{4,5},{5,4},{6,7},{7,6},{8,9},{9,8},{10,11... | collective-permute-start | bytes 1671176 | tf_op jit(solution)/shard_map/ppermute | solution.py:678
  106.5 0.0 collective-permute-start.24
  106.6 0.5 collective-permute-start.23
  107.1 3.9 %collective-permute-start.22 = (bf16[2176,128]{1,0:T(8,128)(2,1)}, bf16[2176,128]{1,0:T(8,128)(2,1)}, u32[]{:S(2)}, u32[]{:S(2)}) collective-permute-start(bf16[2176,128]{1,0:T(8,128)(2,1)} %get-tuple-element.73), channel_id=1, source_target_pairs={{5,7},{2,4},{3,6},{13,15},{10,12},{11,14},{21,23},{18,20},{19,22},... | collective-permute-start | bytes 1671176 | tf_op jit(solution)/shard_map/ppermute | solution.py:665
  110.9 6.3 %conv_output.1 = bf16[128,4096]{1,0:T(8,128)(2,1)} custom-call(bf16[128,4096]{1,0:T(8,128)(2,1)} %q_ref.5, f32[128,4096]{1,0:T(8,128)} %get-tuple-element.56.y_ref, f32[8,4096]{1,0:T(8,128)} %copy-done.2, f32[4,128,128]{2,1,0:T(8,128)} %copy-done, f32[4,128,128]{2,1,0:T(8,128)} %collective-permute-done.6.other_ref.other_par_ref, ...), custom_call_target="tpu_custom_call" | custom-call | flops 600000000 | bytes 65536 | tf_op jit(solution)/shard_map/conv_output/pallas_call | solution.py:269
  117.2 2.7 %att_merge.4.refs_2_ = bf16[128,4096]{1,0:T(8,128)(2,1)} custom-call(f32[128,1024]{1,0:T(8,128)} %get-tuple-element.87.own_hbm, f32[16,128]{1,0:T(8,128)} %get-tuple-element.88.lse_hbm, bf16[2176,128]{1,0:T(8,128)(2,1)} %collective-permute-done.16.refs_7_.refs_0_, bf16[2176,128]{1,0:T(8,128)(2,1)} %collective-permute-done.25.refs_1_, ...), custom_call_target="tpu_custom_call", output_to_operand_aliasing={{}: (4, {})} | custom-call | flops 200000000 | bytes 65536 | tf_op jit(solution)/shard_map/att_merge/pallas_call | solution.py:681
  119.9 2.7 %att_merge.5.refs_2_ = bf16[128,4096]{1,0:T(8,128)(2,1)} custom-call(f32[128,1024]{1,0:T(8,128)} %get-tuple-element.84.own_hbm, f32[16,128]{1,0:T(8,128)} %get-tuple-element.85.lse_hbm, bf16[2176,128]{1,0:T(8,128)(2,1)} %collective-permute-done.13.refs_7_.refs_0_, bf16[2176,128]{1,0:T(8,128)(2,1)} %collective-permute-done.24.refs_1_, ...), custom_call_target="tpu_custom_call", output_to_operand_aliasing={{}: (4, {})} | custom-call | flops 200000000 | bytes 65536 | tf_op jit(solution)/shard_map/att_merge/pallas_call | solution.py:681
  122.6 2.7 %att_merge.6.refs_2_ = bf16[128,4096]{1,0:T(8,128)(2,1)} custom-call(f32[128,1024]{1,0:T(8,128)} %get-tuple-element.81.own_hbm, f32[16,128]{1,0:T(8,128)} %get-tuple-element.82.lse_hbm, bf16[2176,128]{1,0:T(8,128)(2,1)} %collective-permute-done.21.refs_0_, bf16[2176,128]{1,0:T(8,128)(2,1)} %collective-permute-done.23.refs_1_, ...), custom_call_target="tpu_custom_call", output_to_operand_aliasing={{}: (4, {})} | custom-call | flops 200000000 | bytes 65536 | tf_op jit(solution)/shard_map/att_merge/pallas_call | solution.py:681
  125.3 0.1 collective-permute-start.26
  125.4 2.3 %collective-permute-done.26.refs_1_ = bf16[2176,128]{1,0:T(8,128)(2,1)} collective-permute-done((bf16[2176,128]{1,0:T(8,128)(2,1)}, bf16[2176,128]{1,0:T(8,128)(2,1)}, u32[]{:S(2)}, u32[]{:S(2)}) %collective-permute-start.26) | collective-permute-done | bytes 557088 | tf_op jit(solution)/shard_map/ppermute | solution.py:678
  127.6 2.6 %att_merge.7 = bf16[128,4096]{1,0:T(8,128)(2,1)} custom-call(f32[128,1024]{1,0:T(8,128)} %get-tuple-element.92.own_hbm, f32[16,128]{1,0:T(8,128)} %get-tuple-element.93.lse_hbm, bf16[2176,128]{1,0:T(8,128)(2,1)} %collective-permute-done.22.refs_0_, bf16[2176,128]{1,0:T(8,128)(2,1)} %collective-permute-done.26.refs_1_, ...), custom_call_target="tpu_custom_call", output_to_operand_aliasing={{}: (4, {})} | custom-call | flops 200000000 | bytes 65536 | tf_op jit(solution)/shard_map/att_merge/pallas_call | solution.py:681
  (29 shorter events, 0.1 us)
Async XLA Ops:
  0.6 5.7 %collective-permute-start.2 = (bf16[128,4096]{1,0:T(8,128)(2,1)}, bf16[128,4096]{1,0:T(8,128)(2,1)}, u32[]{:S(2)}, u32[]{:S(2)}) collective-permute-start(bf16[128,4096]{1,0:T(8,128)(2,1)} %refs_0_.7), channel_id=1, source_target_pairs={{0,1},{1,0},{2,3},{3,2},{4,5},{5,4},{6,7},{7,6},{8,9},{9,8},{10,11... | collective-permute-start | bytes 3145736 | tf_op jit(solution)/shard_map/ppermute | solution.py:552
  3.2 5.3 %collective-permute-start.5 = (f32[8,4096]{1,0:T(8,128)}, f32[8,4096]{1,0:T(8,128)S(1)}, u32[]{:S(2)}, u32[]{:S(2)}) collective-permute-start(f32[8,4096]{1,0:T(8,128)} %get-tuple-element.52), channel_id=1, source_target_pairs={{0,1},{1,2},{2,3},{3,4},{4,5},{5,6},{6,7},{8,9},{9,10},{10,11},{11... | collective-permute-start | bytes 393224 | tf_op jit(solution)/shard_map/ppermute | solution.py:220
  8.6 14.5 %copy-start.2 = (f32[8,4096]{1,0:T(8,128)}, f32[8,4096]{1,0:T(8,128)S(1)}, u32[]{:S(2)}) copy-start(f32[8,4096]{1,0:T(8,128)S(1)} %collective-permute-done.5.rim_ref) | copy-start | bytes 393220
  8.6 7.4 %all-to-all-start = ((f32[4,128,128]{2,1,0:T(8,128)}), f32[4,128,128]{2,1,0:T(8,128)S(1)}, u32[]{:S(2)}, u32[]{:S(2)}) async-start(f32[4,128,128]{2,1,0:T(8,128)} %get-tuple-element.55), calls=%async_computation | async-start | bytes 524288 | tf_op jit(solution)/shard_map/all_to_all | solution.py:222
  12.2 29.3 %collective-permute-start = (bf16[128,4096]{1,0:T(8,128)(2,1)}, bf16[128,4096]{1,0:T(8,128)(2,1)}, u32[]{:S(2)}, u32[]{:S(2)}) collective-permute-start(bf16[128,4096]{1,0:T(8,128)(2,1)} %refs_1_.7), channel_id=1, source_target_pairs={{0,1},{1,0},{2,3},{3,2},{4,5},{5,4},{6,7},{7,6},{8,9},{9,8},{10,11... | collective-permute-start | bytes 3145736 | tf_op jit(solution)/shard_map/ppermute | solution.py:553
  14.9 29.3 %collective-permute-start.1 = (bf16[128,4096]{1,0:T(8,128)(2,1)}, bf16[128,4096]{1,0:T(8,128)(2,1)}, u32[]{:S(2)}, u32[]{:S(2)}) collective-permute-start(bf16[128,4096]{1,0:T(8,128)(2,1)} %refs_2_.7), channel_id=1, source_target_pairs={{0,1},{1,0},{2,3},{3,2},{4,5},{5,4},{6,7},{7,6},{8,9},{9,8},{10,11... | collective-permute-start | bytes 3145736 | tf_op jit(solution)/shard_map/ppermute | solution.py:554
  16.0 0.7 copy-start
  16.7 6.3 %collective-permute-start.6 = (f32[4,128,128]{2,1,0:T(8,128)S(1)}, f32[4,128,128]{2,1,0:T(8,128)}, u32[]{:S(2)}, u32[]{:S(2)}) collective-permute-start(f32[4,128,128]{2,1,0:T(8,128)S(1)} %all-to-all-done.same_ref), channel_id=1, source_target_pairs={{0,1},{1,0},{2,3},{3,2},{4,5},{5,4},{6,7},{7,6},{8,9},{9,8},{10,11... | collective-permute-start | bytes 786440 | tf_op jit(solution)/shard_map/ppermute | solution.py:230
  20.3 16.0 %collective-permute-start.4 = (bf16[2,128,1024]{2,1,0:T(8,128)(2,1)}, bf16[2,128,1024]{2,1,0:T(8,128)(2,1)}, u32[]{:S(2)}, u32[]{:S(2)}) collective-permute-start(bf16[2,128,1024]{2,1,0:T(8,128)(2,1)} %get-tuple-element.51), channel_id=1, source_target_pairs={{0,2},{1,3},{8,10},{9,11},{16,18},{17,19},{24,26},{25,27}} | collective-permute-start | bytes 1572872 | tf_op jit(solution)/shard_map/ppermute | solution.py:597
  21.7 16.0 %collective-permute-start.8 = (bf16[2,128,1024]{2,1,0:T(8,128)(2,1)}, bf16[2,128,1024]{2,1,0:T(8,128)(2,1)}, u32[]{:S(2)}, u32[]{:S(2)}) collective-permute-start(bf16[2,128,1024]{2,1,0:T(8,128)(2,1)} %get-tuple-element.54), channel_id=1, source_target_pairs={{7,5},{4,2},{6,3},{15,13},{12,10},{14,11},{23,21},{20,18},{22,19},... | collective-permute-start | bytes 1572872 | tf_op jit(solution)/shard_map/ppermute | solution.py:602
  32.8 5.4 %collective-permute-start.17 = (f32[512,128]{1,0:T(8,128)}, f32[512,128]{1,0:T(8,128)S(1)}, u32[]{:S(2)}, u32[]{:S(2)}) collective-permute-start(f32[512,128]{1,0:T(8,128)} %get-tuple-element.70), channel_id=1, source_target_pairs={{0,1},{1,0},{2,3},{3,2},{4,5},{5,4},{6,7},{7,6},{8,9},{9,8},{10,11... | collective-permute-start | bytes 786440 | tf_op jit(solution)/shard_map/ppermute | solution.py:251
  36.3 9.2 %collective-permute-start.3 = (bf16[2,128,1024]{2,1,0:T(8,128)(2,1)}, bf16[2,128,1024]{2,1,0:T(8,128)(2,1)}, u32[]{:S(2)}, u32[]{:S(2)}) collective-permute-start(bf16[2,128,1024]{2,1,0:T(8,128)(2,1)} %get-tuple-element.50), channel_id=1, source_target_pairs={{0,2},{1,3},{8,10},{9,11},{16,18},{17,19},{24,26},{25,27}} | collective-permute-start | bytes 1572872 | tf_op jit(solution)/shard_map/ppermute | solution.py:597
  37.7 10.2 %collective-permute-start.7 = (bf16[2,128,1024]{2,1,0:T(8,128)(2,1)}, bf16[2,128,1024]{2,1,0:T(8,128)(2,1)}, u32[]{:S(2)}, u32[]{:S(2)}) collective-permute-start(bf16[2,128,1024]{2,1,0:T(8,128)(2,1)} %collective-permute-done.4.refs_5_), channel_id=1, source_target_pairs={{0,1},{1,0},{2,3},{3,2},{4,5},{5,4},{6,7},{7,6},{8,9},{9,8},{10,11... | collective-permute-start | bytes 1572872 | tf_op jit(solution)/shard_map/ppermute | solution.py:614
  38.3 1.5 %copy-start.1 = (f32[512,128]{1,0:T(8,128)}, f32[512,128]{1,0:T(8,128)S(1)}, u32[]{:S(2)}) copy-start(f32[512,128]{1,0:T(8,128)S(1)} %collective-permute-done.17.other_ref) | copy-start | bytes 786436
  38.3 18.5 %collective-permute-start.14 = (bf16[2,128,1024]{2,1,0:T(8,128)(2,1)}, bf16[2,128,1024]{2,1,0:T(8,128)(2,1)}, u32[]{:S(2)}, u32[]{:S(2)}) collective-permute-start(bf16[2,128,1024]{2,1,0:T(8,128)(2,1)} %get-tuple-element.65), channel_id=1, source_target_pairs={{0,2},{1,3},{8,10},{9,11},{16,18},{17,19},{24,26},{25,27}} | collective-permute-start | bytes 1572872 | tf_op jit(solution)/shard_map/ppermute | solution.py:597
  41.5 13.8 %collective-permute-start.18 = (f32[512,128]{1,0:T(8,128)}, f32[512,128]{1,0:T(8,128)}, u32[]{:S(2)}, u32[]{:S(2)}) collective-permute-start(f32[512,128]{1,0:T(8,128)} %multiply_add_fusion.2), channel_id=1, source_target_pairs={{1,3},{3,5},{5,7},{9,11},{11,13},{13,15},{17,19},{19,21},{21,23},{... | collective-permute-start | bytes 786440 | tf_op jit(solution)/shard_map/ppermute | solution.py:257
  44.2 22.5 %collective-permute-start.12 = (bf16[2,128,1024]{2,1,0:T(8,128)(2,1)}, bf16[2,128,1024]{2,1,0:T(8,128)(2,1)}, u32[]{:S(2)}, u32[]{:S(2)}) collective-permute-start(bf16[2,128,1024]{2,1,0:T(8,128)(2,1)} %get-tuple-element.61), channel_id=1, source_target_pairs={{7,5},{4,2},{6,3},{15,13},{12,10},{14,11},{23,21},{20,18},{22,19},... | collective-permute-start | bytes 1572872 | tf_op jit(solution)/shard_map/ppermute | solution.py:602
  45.5 22.5 %collective-permute-start.11 = (bf16[2,128,1024]{2,1,0:T(8,128)(2,1)}, bf16[2,128,1024]{2,1,0:T(8,128)(2,1)}, u32[]{:S(2)}, u32[]{:S(2)}) collective-permute-start(bf16[2,128,1024]{2,1,0:T(8,128)(2,1)} %collective-permute-done.3.refs_5_), channel_id=1, source_target_pairs={{0,1},{1,0},{2,3},{3,2},{4,5},{5,4},{6,7},{7,6},{8,9},{9,8},{10,11... | collective-permute-start | bytes 1572872 | tf_op jit(solution)/shard_map/ppermute | solution.py:614
  52.8 28.2 %collective-permute-start.16 = (bf16[2176,128]{1,0:T(8,128)(2,1)}, bf16[2176,128]{1,0:T(8,128)(2,1)}, u32[]{:S(2)}, u32[]{:S(2)}) collective-permute-start(bf16[2176,128]{1,0:T(8,128)(2,1)} %get-tuple-element.59), channel_id=1, source_target_pairs={{5,7},{2,4},{3,6},{7,5},{4,2},{6,3},{13,15},{10,12},{11,14},{15,13... | collective-permute-start | bytes 1671176 | tf_op jit(solution)/shard_map/ppermute | solution.py:665
  55.3 19.5 %collective-permute-start.9 = (bf16[2,128,1024]{2,1,0:T(8,128)(2,1)}, bf16[2,128,1024]{2,1,0:T(8,128)(2,1)}, u32[]{:S(2)}, u32[]{:S(2)}) collective-permute-start(bf16[2,128,1024]{2,1,0:T(8,128)(2,1)} %get-tuple-element.60), channel_id=1, source_target_pairs={{0,2},{1,3},{8,10},{9,11},{16,18},{17,19},{24,26},{25,27}} | collective-permute-start | bytes 1572872 | tf_op jit(solution)/shard_map/ppermute | solution.py:597
  56.8 24.2 %collective-permute-start.15 = (bf16[2,128,1024]{2,1,0:T(8,128)(2,1)}, bf16[2,128,1024]{2,1,0:T(8,128)(2,1)}, u32[]{:S(2)}, u32[]{:S(2)}) collective-permute-start(bf16[2,128,1024]{2,1,0:T(8,128)(2,1)} %collective-permute-done.14.refs_5_), channel_id=1, source_target_pairs={{0,1},{1,0},{2,3},{3,2},{4,5},{5,4},{6,7},{7,6},{8,9},{9,8},{10,11... | collective-permute-start | bytes 1572872 | tf_op jit(solution)/shard_map/ppermute | solution.py:614
  66.7 21.8 %collective-permute-start.19 = (f32[512,128]{1,0:T(8,128)}, f32[512,128]{1,0:T(8,128)}, u32[]{:S(2)}, u32[]{:S(2)}) collective-permute-start(f32[512,128]{1,0:T(8,128)} %multiply_add_fusion.1), channel_id=1, source_target_pairs={{1,5},{3,7},{9,13},{11,15},{17,21},{19,23},{25,29},{27,31}} | collective-permute-start | bytes 786440 | tf_op jit(solution)/shard_map/ppermute | solution.py:257
  72.9 17.5 %collective-permute-start.13 = (bf16[2176,128]{1,0:T(8,128)(2,1)}, bf16[2176,128]{1,0:T(8,128)(2,1)}, u32[]{:S(2)}, u32[]{:S(2)}) collective-permute-start(bf16[2176,128]{1,0:T(8,128)(2,1)} %get-tuple-element.63), channel_id=1, source_target_pairs={{5,7},{2,4},{3,6},{7,5},{4,2},{6,3},{13,15},{10,12},{11,14},{15,13... | collective-permute-start | bytes 1671176 | tf_op jit(solution)/shard_map/ppermute | solution.py:665
  74.8 15.6 %collective-permute-start.10 = (bf16[2,128,1024]{2,1,0:T(8,128)(2,1)}, bf16[2,128,1024]{2,1,0:T(8,128)(2,1)}, u32[]{:S(2)}, u32[]{:S(2)}) collective-permute-start(bf16[2,128,1024]{2,1,0:T(8,128)(2,1)} %collective-permute-done.9.refs_5_), channel_id=1, source_target_pairs={{0,1},{1,0},{2,3},{3,2},{4,5},{5,4},{6,7},{7,6},{8,9},{9,8},{10,11... | collective-permute-start | bytes 1572872 | tf_op jit(solution)/shard_map/ppermute | solution.py:614
  85.7 14.6 %collective-permute-start.21 = (bf16[2176,128]{1,0:T(8,128)(2,1)}, bf16[2176,128]{1,0:T(8,128)(2,1)}, u32[]{:S(2)}, u32[]{:S(2)}) collective-permute-start(bf16[2176,128]{1,0:T(8,128)(2,1)} %get-tuple-element.71), channel_id=1, source_target_pairs={{5,7},{2,4},{3,6},{13,15},{10,12},{11,14},{21,23},{18,20},{19,22},... | collective-permute-start | bytes 1671176 | tf_op jit(solution)/shard_map/ppermute | solution.py:665
  90.4 4.8 %collective-permute-start.20 = (f32[512,128]{1,0:T(8,128)}, f32[512,128]{1,0:T(8,128)}, u32[]{:S(2)}, u32[]{:S(2)}) collective-permute-start(f32[512,128]{1,0:T(8,128)} %multiply_add_fusion.enter_ref), channel_id=1, source_target_pairs={{0,1},{1,0},{2,3},{3,2},{4,5},{5,4},{6,7},{7,6},{8,9},{9,8},{10,11... | collective-permute-start | bytes 786440 | tf_op jit(solution)/shard_map/ppermute | solution.py:265
  100.3 17.0 %collective-permute-start.25 = (bf16[2176,128]{1,0:T(8,128)(2,1)}, bf16[2176,128]{1,0:T(8,128)(2,1)}, u32[]{:S(2)}, u32[]{:S(2)}) collective-permute-start(bf16[2176,128]{1,0:T(8,128)(2,1)} %collective-permute-done.16.refs_7_.refs_0_), channel_id=1, source_target_pairs={{0,1},{1,0},{2,3},{3,2},{4,5},{5,4},{6,7},{7,6},{8,9},{9,8},{10,11... | collective-permute-start | bytes 1671176 | tf_op jit(solution)/shard_map/ppermute | solution.py:678
  106.5 13.4 %collective-permute-start.24 = (bf16[2176,128]{1,0:T(8,128)(2,1)}, bf16[2176,128]{1,0:T(8,128)(2,1)}, u32[]{:S(2)}, u32[]{:S(2)}) collective-permute-start(bf16[2176,128]{1,0:T(8,128)(2,1)} %collective-permute-done.13.refs_7_.refs_0_), channel_id=1, source_target_pairs={{0,1},{1,0},{2,3},{3,2},{4,5},{5,4},{6,7},{7,6},{8,9},{9,8},{10,11... | collective-permute-start | bytes 1671176 | tf_op jit(solution)/shard_map/ppermute | solution.py:678
  106.6 16.0 %collective-permute-start.23 = (bf16[2176,128]{1,0:T(8,128)(2,1)}, bf16[2176,128]{1,0:T(8,128)(2,1)}, u32[]{:S(2)}, u32[]{:S(2)}) collective-permute-start(bf16[2176,128]{1,0:T(8,128)(2,1)} %collective-permute-done.21.refs_0_), channel_id=1, source_target_pairs={{0,1},{1,0},{2,3},{3,2},{4,5},{5,4},{6,7},{7,6},{8,9},{9,8},{10,11... | collective-permute-start | bytes 1671176 | tf_op jit(solution)/shard_map/ppermute | solution.py:678
  107.1 18.2 %collective-permute-start.22 = (bf16[2176,128]{1,0:T(8,128)(2,1)}, bf16[2176,128]{1,0:T(8,128)(2,1)}, u32[]{:S(2)}, u32[]{:S(2)}) collective-permute-start(bf16[2176,128]{1,0:T(8,128)(2,1)} %get-tuple-element.73), channel_id=1, source_target_pairs={{5,7},{2,4},{3,6},{13,15},{10,12},{11,14},{21,23},{18,20},{19,22},... | collective-permute-start | bytes 1671176 | tf_op jit(solution)/shard_map/ppermute | solution.py:665
  125.3 2.4 %collective-permute-start.26 = (bf16[2176,128]{1,0:T(8,128)(2,1)}, bf16[2176,128]{1,0:T(8,128)(2,1)}, u32[]{:S(2)}, u32[]{:S(2)}) collective-permute-start(bf16[2176,128]{1,0:T(8,128)(2,1)} %collective-permute-done.22.refs_0_), channel_id=1, source_target_pairs={{0,1},{1,0},{2,3},{3,2},{4,5},{5,4},{6,7},{7,6},{8,9},{9,8},{10,11... | collective-permute-start | bytes 1671176 | tf_op jit(solution)/shard_map/ppermute | solution.py:678

commit v14 on v13

--- a/solution.py
+++ b/solution.py
@@ -611,6 +611,8 @@
         if chunk == 0:
             quad_kv[0] = [after(quad_kv[0][0], local_result)]
             asks[0] = [after(asked, local_result) for asked in asks[0]]
+        elif chunk == 1:
+            quad_kv[1] = [after(quad_kv[1][0], all_answers[0][0])]
         quad_kv[chunk].append(lax.ppermute(quad_kv[chunk][0], "ctx", swap))
         steps, first = CHUNK_STEPS[chunk], first_steps[chunk]
         whole_spec = pl.BlockSpec((rows, step_width), lambda step, first=first: (0, first + step))

time: 131 us -> 133 us (1.015)
  starting transfers between devices: 64.8 us -> 66.4 us
    ppermute x4, starting transfers between devices: 17.2 us -> 18.6 us  [attend(): quad_kv[chunk].append(lax.ppermute(quad_kv[chunk][0], 'ctx', swap))]
  transfers between devices with their start and end apart: 28 -> 28, of which waited for: 4 -> 4; matrix products, arithmetic and copies ran while one was open for 4% -> 4% of each run, Pallas kernels for 35% -> 34%
where the time goes in v14:
time: 133 us; the launch traced here: 132 us
  starting transfers between devices  66.4 us (50%)
  Pallas kernels  47.9 us (36%)
  waiting for transfers between devices  10.5 us (8%)
  other arithmetic  5.52 us (4%)
    pallas_call x4, Pallas kernels, attend(): pl.pallas_call(functools.partial(partial_kernel, transfers, upper, natura...  19.2 us
    ppermute x4, starting transfers between devices, attend(): quad_kv[chunk].append(lax.ppermute(quad_kv[chunk][0], 'ctx', swap))  18.6 us
    ppermute x4, starting transfers between devices, attend(): arrivals.append(lax.ppermute(answer, 'ctx', moves))  10.8 us
    pallas_call x4, Pallas kernels, attend(): pl.pallas_call(functools.partial(merge_kernel, transfers, steps, starts[c...  10.6 us
    pallas_call x1, Pallas kernels, first_part(): pl.pallas_call(functools.partial(state_kernel, modes), grid=(groups,), in...  9.79 us
    ppermute x4, starting transfers between devices, attend(): parts += [arrival, lax.ppermute(arrival, 'ctx', swap)]  6.87 us
    pallas_call x1, Pallas kernels, last_part(): pl.pallas_call(functools.partial(output_kernel, modes), grid=(groups,), i...  6.31 us
    ppermute x4, starting transfers between devices, send(): quad_kv.append([lax.ppermute(key_pack, 'ctx', gathers)])  5.86 us
  transfers between devices with their start and end apart: 28, of which 4 were waited for; matrix products, arithmetic and copies ran while one was open for 4% of the time, Pallas kernels for 34%

profile of v14, /device:TPU:17, one launch (start us, length us, event | category | flops | bytes accessed | tf_op | source)
XLA Modules:
  0.0 132.1 jit_solution(10728337635888483830)
XLA Ops:
  0.6 0.7 collective-permute-start.2
  1.4 1.9 %conv_pack.1 = (f32[4,128,128]{2,1,0:T(8,128)}, f32[8,4096]{1,0:T(8,128)}) custom-call(f32[16,512]{1,0:T(8,128)} %bitcast.2, f32[16,512]{1,0:T(8,128)} %bitcast.3, bf16[128,4096]{1,0:T(8,128)(2,1)} %q_ref.5, bf16[128,4096]{1,0:T(8,128)(2,1)} %k_ref.5, bf16[128,4096]{1,0:T(8,128)(2,1)} %v_ref.5), custom_call_target="tpu_custom_call" | custom-call | flops 100000000 | bytes 65536 | tf_op jit(solution)/shard_map/conv_pack/pallas_call | solution.py:203
  3.2 3.1 %collective-permute-start.5 = (f32[8,4096]{1,0:T(8,128)}, f32[8,4096]{1,0:T(8,128)S(1)}, u32[]{:S(2)}, u32[]{:S(2)}) collective-permute-start(f32[8,4096]{1,0:T(8,128)} %get-tuple-element.53), channel_id=1, source_target_pairs={{0,1},{1,2},{2,3},{3,4},{4,5},{5,6},{6,7},{8,9},{9,10},{10,11},{11... | collective-permute-start | bytes 393224 | tf_op jit(solution)/shard_map/ppermute | solution.py:220
  6.3 0.0 collective-permute-done.2.qs_ref.refs_9_
  6.3 0.2 att_pack.1
  6.6 2.0 %collective-permute-done.5.rim_ref = f32[8,4096]{1,0:T(8,128)S(1)} collective-permute-done((f32[8,4096]{1,0:T(8,128)}, f32[8,4096]{1,0:T(8,128)S(1)}, u32[]{:S(2)}, u32[]{:S(2)}) %collective-permute-start.5) | collective-permute-done | bytes 131104 | tf_op jit(solution)/shard_map/ppermute | solution.py:220
  8.6 3.7 %all-to-all-start = ((f32[4,128,128]{2,1,0:T(8,128)}), f32[4,128,128]{2,1,0:T(8,128)S(1)}, u32[]{:S(2)}, u32[]{:S(2)}) async-start(f32[4,128,128]{2,1,0:T(8,128)} %get-tuple-element.56), calls=%async_computation | async-start | bytes 524288 | tf_op jit(solution)/shard_map/all_to_all | solution.py:222
  12.2 2.7 %collective-permute-start = (bf16[128,4096]{1,0:T(8,128)(2,1)}, bf16[128,4096]{1,0:T(8,128)(2,1)}, u32[]{:S(2)}, u32[]{:S(2)}) collective-permute-start(bf16[128,4096]{1,0:T(8,128)(2,1)} %refs_1_.7), channel_id=1, source_target_pairs={{0,1},{1,0},{2,3},{3,2},{4,5},{5,4},{6,7},{7,6},{8,9},{9,8},{10,11... | collective-permute-start | bytes 3145736 | tf_op jit(solution)/shard_map/ppermute | solution.py:553
  14.9 1.0 all-to-all-done.same_ref
  16.0 0.7 copy-done
  16.7 3.6 %collective-permute-start.6 = (f32[4,128,128]{2,1,0:T(8,128)S(1)}, f32[4,128,128]{2,1,0:T(8,128)}, u32[]{:S(2)}, u32[]{:S(2)}) collective-permute-start(f32[4,128,128]{2,1,0:T(8,128)S(1)} %all-to-all-done.same_ref), channel_id=1, source_target_pairs={{0,1},{1,0},{2,3},{3,2},{4,5},{5,4},{6,7},{7,6},{8,9},{9,8},{10,11... | collective-permute-start | bytes 786440 | tf_op jit(solution)/shard_map/ppermute | solution.py:230
  20.3 1.5 %collective-permute-start.4 = (bf16[2,128,1024]{2,1,0:T(8,128)(2,1)}, bf16[2,128,1024]{2,1,0:T(8,128)(2,1)}, u32[]{:S(2)}, u32[]{:S(2)}) collective-permute-start(bf16[2,128,1024]{2,1,0:T(8,128)(2,1)} %get-tuple-element.52), channel_id=1, source_target_pairs={{0,2},{1,3},{8,10},{9,11},{16,18},{17,19},{24,26},{25,27}} | collective-permute-start | bytes 1572872 | tf_op jit(solution)/shard_map/ppermute | solution.py:597
  21.7 1.3 collective-permute-start.8
  23.0 0.0 collective-permute-done.6.other_ref.other_par_ref
  23.0 9.8 %conv_state.1 = (f32[128,4096]{1,0:T(8,128)}, f32[512,128]{1,0:T(8,128)}, f32[512,128]{1,0:T(8,128)}) custom-call(bf16[128,4096]{1,0:T(8,128)(2,1)} %k_ref.5, bf16[128,4096]{1,0:T(8,128)(2,1)} %v_ref.5, f32[8,4096]{1,0:T(8,128)} %copy-done.2, f32[4,128,128]{2,1,0:T(8,128)} %copy-done, f32[4,128,128]{2,1,0:T(8,128)} %collective-permute-done.6.other_ref.other_par_ref, ...), custom_call_target="tpu_custom_call" | custom-call | flops 900000000 | bytes 65536 | tf_op jit(solution)/shard_map/conv_state/pallas_call | solution.py:232
  32.8 3.5 %collective-permute-start.17 = (f32[512,128]{1,0:T(8,128)}, f32[512,128]{1,0:T(8,128)S(1)}, u32[]{:S(2)}, u32[]{:S(2)}) collective-permute-start(f32[512,128]{1,0:T(8,128)} %get-tuple-element.72), channel_id=1, source_target_pairs={{0,1},{1,0},{2,3},{3,2},{4,5},{5,4},{6,7},{7,6},{8,9},{9,8},{10,11... | collective-permute-start | bytes 786440 | tf_op jit(solution)/shard_map/ppermute | solution.py:251
  36.3 0.1 collective-permute-start.7
  36.4 1.5 %collective-permute-start.3 = (bf16[2,128,1024]{2,1,0:T(8,128)(2,1)}, bf16[2,128,1024]{2,1,0:T(8,128)(2,1)}, u32[]{:S(2)}, u32[]{:S(2)}) collective-permute-start(bf16[2,128,1024]{2,1,0:T(8,128)(2,1)} %get-tuple-element.51), channel_id=1, source_target_pairs={{0,2},{1,3},{8,10},{9,11},{16,18},{17,19},{24,26},{25,27}} | collective-permute-start | bytes 1572872 | tf_op jit(solution)/shard_map/ppermute | solution.py:597
  37.9 1.5 %collective-permute-start.14 = (bf16[2,128,1024]{2,1,0:T(8,128)(2,1)}, bf16[2,128,1024]{2,1,0:T(8,128)(2,1)}, u32[]{:S(2)}, u32[]{:S(2)}) collective-permute-start(bf16[2,128,1024]{2,1,0:T(8,128)(2,1)} %get-tuple-element.67), channel_id=1, source_target_pairs={{0,2},{1,3},{8,10},{9,11},{16,18},{17,19},{24,26},{25,27}} | collective-permute-start | bytes 1572872 | tf_op jit(solution)/shard_map/ppermute | solution.py:597
  39.3 1.8 %multiply_add_fusion.2 = f32[512,128]{1,0:T(8,128)} fusion(f32[512,128]{1,0:T(8,128)} %get-tuple-element.72, f32[512,128]{1,0:T(8,128)} %get-tuple-element.79.decay_ref, f32[512,128]{1,0:T(8,128)S(1)} %collective-permute-done.17.other_ref), kind=kLoop, calls=%fused_computation.2 | loop fusion | flops 131072 | bytes 1048576 | tf_op jit(solution)/shard_map/add | solution.py:252
  41.1 3.2 %collective-permute-start.18 = (f32[512,128]{1,0:T(8,128)}, f32[512,128]{1,0:T(8,128)}, u32[]{:S(2)}, u32[]{:S(2)}) collective-permute-start(f32[512,128]{1,0:T(8,128)} %multiply_add_fusion.2), channel_id=1, source_target_pairs={{1,3},{3,5},{5,7},{9,11},{11,13},{13,15},{17,19},{19,21},{21,23},{... | collective-permute-start | bytes 786440 | tf_op jit(solution)/shard_map/ppermute | solution.py:257
  44.3 1.3 collective-permute-start.12
  45.6 4.8 %att_partial.4 = (f32[128,1024]{1,0:T(8,128)}, f32[16,128]{1,0:T(8,128)}, bf16[2176,128]{1,0:T(8,128)(2,1)}, bf16[128,4096]{1,0:T(8,128)(2,1)}) custom-call(bf16[128,4096]{1,0:T(8,128)(2,1)} %refs_0_.7, bf16[128,4096]{1,0:T(8,128)(2,1)} %refs_1_.7, bf16[128,4096]{1,0:T(8,128)(2,1)} %refs_2_.7, bf16[128,4096]{1,0:T(8,128)(2,1)} %collective-permute-done.refs_3_, ...), custom_call_target="tpu_custom_call" | custom-call | flops 400000000 | bytes 65536 | tf_op jit(solution)/shard_map/att_partial/pallas_call | solution.py:640
  50.4 2.4 %collective-permute-start.11 = (bf16[2,128,1024]{2,1,0:T(8,128)(2,1)}, bf16[2,128,1024]{2,1,0:T(8,128)(2,1)}, u32[]{:S(2)}, u32[]{:S(2)}) collective-permute-start(bf16[2,128,1024]{2,1,0:T(8,128)(2,1)} %collective-permute-done.3.refs_5_), channel_id=1, source_target_pairs={{0,1},{1,0},{2,3},{3,2},{4,5},{5,4},{6,7},{7,6},{8,9},{9,8},{10,11... | collective-permute-start | bytes 1572872 | tf_op jit(solution)/shard_map/ppermute | solution.py:616
  52.8 2.2 %collective-permute-start.16 = (bf16[2176,128]{1,0:T(8,128)(2,1)}, bf16[2176,128]{1,0:T(8,128)(2,1)}, u32[]{:S(2)}, u32[]{:S(2)}) collective-permute-start(bf16[2176,128]{1,0:T(8,128)(2,1)} %get-tuple-element.60), channel_id=1, source_target_pairs={{5,7},{2,4},{3,6},{7,5},{4,2},{6,3},{13,15},{10,12},{11,14},{15,13... | collective-permute-start | bytes 1671176 | tf_op jit(solution)/shard_map/ppermute | solution.py:667
  55.0 1.5 %collective-permute-start.9 = (bf16[2,128,1024]{2,1,0:T(8,128)(2,1)}, bf16[2,128,1024]{2,1,0:T(8,128)(2,1)}, u32[]{:S(2)}, u32[]{:S(2)}) collective-permute-start(bf16[2,128,1024]{2,1,0:T(8,128)(2,1)} %get-tuple-element.62), channel_id=1, source_target_pairs={{0,2},{1,3},{8,10},{9,11},{16,18},{17,19},{24,26},{25,27}} | collective-permute-start | bytes 1572872 | tf_op jit(solution)/shard_map/ppermute | solution.py:597
  56.5 4.7 %collective-permute-start.15 = (bf16[2,128,1024]{2,1,0:T(8,128)(2,1)}, bf16[2,128,1024]{2,1,0:T(8,128)(2,1)}, u32[]{:S(2)}, u32[]{:S(2)}) collective-permute-start(bf16[2,128,1024]{2,1,0:T(8,128)(2,1)} %collective-permute-done.14.refs_5_), channel_id=1, source_target_pairs={{0,1},{1,0},{2,3},{3,2},{4,5},{5,4},{6,7},{7,6},{8,9},{9,8},{10,11... | collective-permute-start | bytes 1572872 | tf_op jit(solution)/shard_map/ppermute | solution.py:616
  61.2 1.8 %multiply_add_fusion.1 = f32[512,128]{1,0:T(8,128)} fusion(f32[512,128]{1,0:T(8,128)} %multiply_add_fusion.2, f32[512,128]{1,0:T(8,128)} %collective-permute-done.18, f32[512,128]{1,0:T(8,128)} %get-tuple-element.79.decay_ref), kind=kLoop, calls=%fused_computation.1 | loop fusion | flops 196608 | bytes 1048576 | tf_op jit(solution)/shard_map/add | solution.py:263
  63.1 1.3 collective-permute-start.19
  64.4 4.8 %att_partial.5 = (f32[128,1024]{1,0:T(8,128)}, f32[16,128]{1,0:T(8,128)}, bf16[2176,128]{1,0:T(8,128)(2,1)}, bf16[128,4096]{1,0:T(8,128)(2,1)}) custom-call(bf16[128,4096]{1,0:T(8,128)(2,1)} %refs_0_.7, bf16[128,4096]{1,0:T(8,128)(2,1)} %refs_1_.7, bf16[128,4096]{1,0:T(8,128)(2,1)} %refs_2_.7, ...), custom_call_target="tpu_custom_call", output_to_operand_aliasing={{3}: (10, {})} | custom-call | flops 400000000 | bytes 65536 | tf_op jit(solution)/shard_map/att_partial/pallas_call | solution.py:640
  69.2 2.0 %collective-permute-start.13 = (bf16[2176,128]{1,0:T(8,128)(2,1)}, bf16[2176,128]{1,0:T(8,128)(2,1)}, u32[]{:S(2)}, u32[]{:S(2)}) collective-permute-start(bf16[2176,128]{1,0:T(8,128)(2,1)} %get-tuple-element.65), channel_id=1, source_target_pairs={{5,7},{2,4},{3,6},{7,5},{4,2},{6,3},{13,15},{10,12},{11,14},{15,13... | collective-permute-start | bytes 1671176 | tf_op jit(solution)/shard_map/ppermute | solution.py:667
  71.2 11.5 %collective-permute-start.10 = (bf16[2,128,1024]{2,1,0:T(8,128)(2,1)}, bf16[2,128,1024]{2,1,0:T(8,128)(2,1)}, u32[]{:S(2)}, u32[]{:S(2)}) collective-permute-start(bf16[2,128,1024]{2,1,0:T(8,128)(2,1)} %collective-permute-done.9.refs_5_), channel_id=1, source_target_pairs={{0,1},{1,0},{2,3},{3,2},{4,5},{5,4},{6,7},{7,6},{8,9},{9,8},{10,11... | collective-permute-start | bytes 1572872 | tf_op jit(solution)/shard_map/ppermute | solution.py:616
  82.6 4.7 %att_partial.6 = (f32[128,1024]{1,0:T(8,128)}, f32[16,128]{1,0:T(8,128)}, bf16[2176,128]{1,0:T(8,128)(2,1)}, bf16[128,4096]{1,0:T(8,128)(2,1)}) custom-call(bf16[128,4096]{1,0:T(8,128)(2,1)} %refs_0_.7, bf16[128,4096]{1,0:T(8,128)(2,1)} %refs_1_.7, bf16[128,4096]{1,0:T(8,128)(2,1)} %refs_2_.7, ...), custom_call_target="tpu_custom_call", output_to_operand_aliasing={{3}: (8, {})} | custom-call | flops 400000000 | bytes 65536 | tf_op jit(solution)/shard_map/att_partial/pallas_call | solution.py:640
  87.4 2.8 %collective-permute-start.21 = (bf16[2176,128]{1,0:T(8,128)(2,1)}, bf16[2176,128]{1,0:T(8,128)(2,1)}, u32[]{:S(2)}, u32[]{:S(2)}) collective-permute-start(bf16[2176,128]{1,0:T(8,128)(2,1)} %get-tuple-element.73), channel_id=1, source_target_pairs={{5,7},{2,4},{3,6},{13,15},{10,12},{11,14},{21,23},{18,20},{19,22},... | collective-permute-start | bytes 1671176 | tf_op jit(solution)/shard_map/ppermute | solution.py:667
  90.2 1.9 %multiply_add_fusion.enter_ref = f32[512,128]{1,0:T(8,128)} fusion(f32[512,128]{1,0:T(8,128)} %collective-permute-done.18, f32[512,128]{1,0:T(8,128)} %collective-permute-done.19, f32[512,128]{1,0:T(8,128)} %get-tuple-element.79.decay_ref), kind=kLoop, calls=%fused_computation | loop fusion | flops 196608 | bytes 1048576 | tf_op jit(solution)/shard_map/add | solution.py:261
  92.1 4.8 %att_partial.7 = (f32[128,1024]{1,0:T(8,128)}, f32[16,128]{1,0:T(8,128)}, bf16[2176,128]{1,0:T(8,128)(2,1)}, bf16[128,4096]{1,0:T(8,128)(2,1)}) custom-call(bf16[128,4096]{1,0:T(8,128)(2,1)} %refs_0_.7, bf16[128,4096]{1,0:T(8,128)(2,1)} %refs_1_.7, bf16[128,4096]{1,0:T(8,128)(2,1)} %refs_2_.7, ...), custom_call_target="tpu_custom_call", output_to_operand_aliasing={{3}: (8, {})} | custom-call | flops 400000000 | bytes 65536 | tf_op jit(solution)/shard_map/att_partial/pallas_call | solution.py:640
  96.9 5.1 %collective-permute-done.21.refs_0_ = bf16[2176,128]{1,0:T(8,128)(2,1)} collective-permute-done((bf16[2176,128]{1,0:T(8,128)(2,1)}, bf16[2176,128]{1,0:T(8,128)(2,1)}, u32[]{:S(2)}, u32[]{:S(2)}) %collective-permute-start.21) | collective-permute-done | bytes 557088 | tf_op jit(solution)/shard_map/ppermute | solution.py:667
  102.0 6.3 %collective-permute-start.25 = (bf16[2176,128]{1,0:T(8,128)(2,1)}, bf16[2176,128]{1,0:T(8,128)(2,1)}, u32[]{:S(2)}, u32[]{:S(2)}) collective-permute-start(bf16[2176,128]{1,0:T(8,128)(2,1)} %collective-permute-done.16.refs_7_.refs_0_), channel_id=1, source_target_pairs={{0,1},{1,0},{2,3},{3,2},{4,5},{5,4},{6,7},{7,6},{8,9},{9,8},{10,11... | collective-permute-start | bytes 1671176 | tf_op jit(solution)/shard_map/ppermute | solution.py:680
  108.2 0.0 collective-permute-start.24
  108.2 0.5 collective-permute-start.23
  108.8 3.9 %collective-permute-start.22 = (bf16[2176,128]{1,0:T(8,128)(2,1)}, bf16[2176,128]{1,0:T(8,128)(2,1)}, u32[]{:S(2)}, u32[]{:S(2)}) collective-permute-start(bf16[2176,128]{1,0:T(8,128)(2,1)} %get-tuple-element.75), channel_id=1, source_target_pairs={{5,7},{2,4},{3,6},{13,15},{10,12},{11,14},{21,23},{18,20},{19,22},... | collective-permute-start | bytes 1671176 | tf_op jit(solution)/shard_map/ppermute | solution.py:667
  112.6 6.3 %conv_output.1 = bf16[128,4096]{1,0:T(8,128)(2,1)} custom-call(bf16[128,4096]{1,0:T(8,128)(2,1)} %q_ref.5, f32[128,4096]{1,0:T(8,128)} %get-tuple-element.57.y_ref, f32[8,4096]{1,0:T(8,128)} %copy-done.2, f32[4,128,128]{2,1,0:T(8,128)} %copy-done, f32[4,128,128]{2,1,0:T(8,128)} %collective-permute-done.6.other_ref.other_par_ref, ...), custom_call_target="tpu_custom_call" | custom-call | flops 600000000 | bytes 65536 | tf_op jit(solution)/shard_map/conv_output/pallas_call | solution.py:269
  118.9 2.7 %att_merge.4.refs_2_ = bf16[128,4096]{1,0:T(8,128)(2,1)} custom-call(f32[128,1024]{1,0:T(8,128)} %get-tuple-element.89.own_hbm, f32[16,128]{1,0:T(8,128)} %get-tuple-element.90.lse_hbm, bf16[2176,128]{1,0:T(8,128)(2,1)} %collective-permute-done.16.refs_7_.refs_0_, bf16[2176,128]{1,0:T(8,128)(2,1)} %collective-permute-done.25.refs_1_, ...), custom_call_target="tpu_custom_call", output_to_operand_aliasing={{}: (4, {})} | custom-call | flops 200000000 | bytes 65536 | tf_op jit(solution)/shard_map/att_merge/pallas_call | solution.py:683
  121.6 2.7 %att_merge.5.refs_2_ = bf16[128,4096]{1,0:T(8,128)(2,1)} custom-call(f32[128,1024]{1,0:T(8,128)} %get-tuple-element.86.own_hbm, f32[16,128]{1,0:T(8,128)} %get-tuple-element.87.lse_hbm, bf16[2176,128]{1,0:T(8,128)(2,1)} %collective-permute-done.13.refs_7_.refs_0_, bf16[2176,128]{1,0:T(8,128)(2,1)} %collective-permute-done.24.refs_1_, ...), custom_call_target="tpu_custom_call", output_to_operand_aliasing={{}: (4, {})} | custom-call | flops 200000000 | bytes 65536 | tf_op jit(solution)/shard_map/att_merge/pallas_call | solution.py:683
  124.3 2.7 %att_merge.6.refs_2_ = bf16[128,4096]{1,0:T(8,128)(2,1)} custom-call(f32[128,1024]{1,0:T(8,128)} %get-tuple-element.83.own_hbm, f32[16,128]{1,0:T(8,128)} %get-tuple-element.84.lse_hbm, bf16[2176,128]{1,0:T(8,128)(2,1)} %collective-permute-done.21.refs_0_, bf16[2176,128]{1,0:T(8,128)(2,1)} %collective-permute-done.23.refs_1_, ...), custom_call_target="tpu_custom_call", output_to_operand_aliasing={{}: (4, {})} | custom-call | flops 200000000 | bytes 65536 | tf_op jit(solution)/shard_map/att_merge/pallas_call | solution.py:683
  127.0 0.1 collective-permute-start.26
  127.1 2.3 %collective-permute-done.26.refs_1_ = bf16[2176,128]{1,0:T(8,128)(2,1)} collective-permute-done((bf16[2176,128]{1,0:T(8,128)(2,1)}, bf16[2176,128]{1,0:T(8,128)(2,1)}, u32[]{:S(2)}, u32[]{:S(2)}) %collective-permute-start.26) | collective-permute-done | bytes 557088 | tf_op jit(solution)/shard_map/ppermute | solution.py:680
  129.3 2.6 %att_merge.7 = bf16[128,4096]{1,0:T(8,128)(2,1)} custom-call(f32[128,1024]{1,0:T(8,128)} %get-tuple-element.94.own_hbm, f32[16,128]{1,0:T(8,128)} %get-tuple-element.95.lse_hbm, bf16[2176,128]{1,0:T(8,128)(2,1)} %collective-permute-done.22.refs_0_, bf16[2176,128]{1,0:T(8,128)(2,1)} %collective-permute-done.26.refs_1_, ...), custom_call_target="tpu_custom_call", output_to_operand_aliasing={{}: (4, {})} | custom-call | flops 200000000 | bytes 65536 | tf_op jit(solution)/shard_map/att_merge/pallas_call | solution.py:683
  (29 shorter events, 0.1 us)
Async XLA Ops:
  0.6 5.7 %collective-permute-start.2 = (bf16[128,4096]{1,0:T(8,128)(2,1)}, bf16[128,4096]{1,0:T(8,128)(2,1)}, u32[]{:S(2)}, u32[]{:S(2)}) collective-permute-start(bf16[128,4096]{1,0:T(8,128)(2,1)} %refs_0_.7), channel_id=1, source_target_pairs={{0,1},{1,0},{2,3},{3,2},{4,5},{5,4},{6,7},{7,6},{8,9},{9,8},{10,11... | collective-permute-start | bytes 3145736 | tf_op jit(solution)/shard_map/ppermute | solution.py:552
  3.2 5.3 %collective-permute-start.5 = (f32[8,4096]{1,0:T(8,128)}, f32[8,4096]{1,0:T(8,128)S(1)}, u32[]{:S(2)}, u32[]{:S(2)}) collective-permute-start(f32[8,4096]{1,0:T(8,128)} %get-tuple-element.53), channel_id=1, source_target_pairs={{0,1},{1,2},{2,3},{3,4},{4,5},{5,6},{6,7},{8,9},{9,10},{10,11},{11... | collective-permute-start | bytes 393224 | tf_op jit(solution)/shard_map/ppermute | solution.py:220
  8.6 14.5 %copy-start.2 = (f32[8,4096]{1,0:T(8,128)}, f32[8,4096]{1,0:T(8,128)S(1)}, u32[]{:S(2)}) copy-start(f32[8,4096]{1,0:T(8,128)S(1)} %collective-permute-done.5.rim_ref) | copy-start | bytes 393220
  8.6 7.4 %all-to-all-start = ((f32[4,128,128]{2,1,0:T(8,128)}), f32[4,128,128]{2,1,0:T(8,128)S(1)}, u32[]{:S(2)}, u32[]{:S(2)}) async-start(f32[4,128,128]{2,1,0:T(8,128)} %get-tuple-element.56), calls=%async_computation | async-start | bytes 524288 | tf_op jit(solution)/shard_map/all_to_all | solution.py:222
  12.2 28.8 %collective-permute-start = (bf16[128,4096]{1,0:T(8,128)(2,1)}, bf16[128,4096]{1,0:T(8,128)(2,1)}, u32[]{:S(2)}, u32[]{:S(2)}) collective-permute-start(bf16[128,4096]{1,0:T(8,128)(2,1)} %refs_1_.7), channel_id=1, source_target_pairs={{0,1},{1,0},{2,3},{3,2},{4,5},{5,4},{6,7},{7,6},{8,9},{9,8},{10,11... | collective-permute-start | bytes 3145736 | tf_op jit(solution)/shard_map/ppermute | solution.py:553
  14.9 29.3 %collective-permute-start.1 = (bf16[128,4096]{1,0:T(8,128)(2,1)}, bf16[128,4096]{1,0:T(8,128)(2,1)}, u32[]{:S(2)}, u32[]{:S(2)}) collective-permute-start(bf16[128,4096]{1,0:T(8,128)(2,1)} %refs_2_.7), channel_id=1, source_target_pairs={{0,1},{1,0},{2,3},{3,2},{4,5},{5,4},{6,7},{7,6},{8,9},{9,8},{10,11... | collective-permute-start | bytes 3145736 | tf_op jit(solution)/shard_map/ppermute | solution.py:554
  16.0 0.7 copy-start
  16.7 6.3 %collective-permute-start.6 = (f32[4,128,128]{2,1,0:T(8,128)S(1)}, f32[4,128,128]{2,1,0:T(8,128)}, u32[]{:S(2)}, u32[]{:S(2)}) collective-permute-start(f32[4,128,128]{2,1,0:T(8,128)S(1)} %all-to-all-done.same_ref), channel_id=1, source_target_pairs={{0,1},{1,0},{2,3},{3,2},{4,5},{5,4},{6,7},{7,6},{8,9},{9,8},{10,11... | collective-permute-start | bytes 786440 | tf_op jit(solution)/shard_map/ppermute | solution.py:230
  20.3 16.0 %collective-permute-start.4 = (bf16[2,128,1024]{2,1,0:T(8,128)(2,1)}, bf16[2,128,1024]{2,1,0:T(8,128)(2,1)}, u32[]{:S(2)}, u32[]{:S(2)}) collective-permute-start(bf16[2,128,1024]{2,1,0:T(8,128)(2,1)} %get-tuple-element.52), channel_id=1, source_target_pairs={{0,2},{1,3},{8,10},{9,11},{16,18},{17,19},{24,26},{25,27}} | collective-permute-start | bytes 1572872 | tf_op jit(solution)/shard_map/ppermute | solution.py:597
  21.7 14.7 %collective-permute-start.8 = (bf16[2,128,1024]{2,1,0:T(8,128)(2,1)}, bf16[2,128,1024]{2,1,0:T(8,128)(2,1)}, u32[]{:S(2)}, u32[]{:S(2)}) collective-permute-start(bf16[2,128,1024]{2,1,0:T(8,128)(2,1)} %get-tuple-element.55), channel_id=1, source_target_pairs={{7,5},{4,2},{6,3},{15,13},{12,10},{14,11},{23,21},{20,18},{22,19},... | collective-permute-start | bytes 1572872 | tf_op jit(solution)/shard_map/ppermute | solution.py:602
  32.8 5.0 %collective-permute-start.17 = (f32[512,128]{1,0:T(8,128)}, f32[512,128]{1,0:T(8,128)S(1)}, u32[]{:S(2)}, u32[]{:S(2)}) collective-permute-start(f32[512,128]{1,0:T(8,128)} %get-tuple-element.72), channel_id=1, source_target_pairs={{0,1},{1,0},{2,3},{3,2},{4,5},{5,4},{6,7},{7,6},{8,9},{9,8},{10,11... | collective-permute-start | bytes 786440 | tf_op jit(solution)/shard_map/ppermute | solution.py:251
  36.3 9.3 %collective-permute-start.7 = (bf16[2,128,1024]{2,1,0:T(8,128)(2,1)}, bf16[2,128,1024]{2,1,0:T(8,128)(2,1)}, u32[]{:S(2)}, u32[]{:S(2)}) collective-permute-start(bf16[2,128,1024]{2,1,0:T(8,128)(2,1)} %collective-permute-done.4.refs_5_), channel_id=1, source_target_pairs={{0,1},{1,0},{2,3},{3,2},{4,5},{5,4},{6,7},{7,6},{8,9},{9,8},{10,11... | collective-permute-start | bytes 1572872 | tf_op jit(solution)/shard_map/ppermute | solution.py:616
  36.4 14.0 %collective-permute-start.3 = (bf16[2,128,1024]{2,1,0:T(8,128)(2,1)}, bf16[2,128,1024]{2,1,0:T(8,128)(2,1)}, u32[]{:S(2)}, u32[]{:S(2)}) collective-permute-start(bf16[2,128,1024]{2,1,0:T(8,128)(2,1)} %get-tuple-element.51), channel_id=1, source_target_pairs={{0,2},{1,3},{8,10},{9,11},{16,18},{17,19},{24,26},{25,27}} | collective-permute-start | bytes 1572872 | tf_op jit(solution)/shard_map/ppermute | solution.py:597
  37.8 1.5 %copy-start.1 = (f32[512,128]{1,0:T(8,128)}, f32[512,128]{1,0:T(8,128)S(1)}, u32[]{:S(2)}) copy-start(f32[512,128]{1,0:T(8,128)S(1)} %collective-permute-done.17.other_ref) | copy-start | bytes 786436
  37.9 18.7 %collective-permute-start.14 = (bf16[2,128,1024]{2,1,0:T(8,128)(2,1)}, bf16[2,128,1024]{2,1,0:T(8,128)(2,1)}, u32[]{:S(2)}, u32[]{:S(2)}) collective-permute-start(bf16[2,128,1024]{2,1,0:T(8,128)(2,1)} %get-tuple-element.67), channel_id=1, source_target_pairs={{0,2},{1,3},{8,10},{9,11},{16,18},{17,19},{24,26},{25,27}} | collective-permute-start | bytes 1572872 | tf_op jit(solution)/shard_map/ppermute | solution.py:597
  41.1 13.9 %collective-permute-start.18 = (f32[512,128]{1,0:T(8,128)}, f32[512,128]{1,0:T(8,128)}, u32[]{:S(2)}, u32[]{:S(2)}) collective-permute-start(f32[512,128]{1,0:T(8,128)} %multiply_add_fusion.2), channel_id=1, source_target_pairs={{1,3},{3,5},{5,7},{9,11},{11,13},{13,15},{17,19},{19,21},{21,23},{... | collective-permute-start | bytes 786440 | tf_op jit(solution)/shard_map/ppermute | solution.py:257
  44.3 18.8 %collective-permute-start.12 = (bf16[2,128,1024]{2,1,0:T(8,128)(2,1)}, bf16[2,128,1024]{2,1,0:T(8,128)(2,1)}, u32[]{:S(2)}, u32[]{:S(2)}) collective-permute-start(bf16[2,128,1024]{2,1,0:T(8,128)(2,1)} %get-tuple-element.63), channel_id=1, source_target_pairs={{7,5},{4,2},{6,3},{15,13},{12,10},{14,11},{23,21},{20,18},{22,19},... | collective-permute-start | bytes 1572872 | tf_op jit(solution)/shard_map/ppermute | solution.py:602
  50.4 13.9 %collective-permute-start.11 = (bf16[2,128,1024]{2,1,0:T(8,128)(2,1)}, bf16[2,128,1024]{2,1,0:T(8,128)(2,1)}, u32[]{:S(2)}, u32[]{:S(2)}) collective-permute-start(bf16[2,128,1024]{2,1,0:T(8,128)(2,1)} %collective-permute-done.3.refs_5_), channel_id=1, source_target_pairs={{0,1},{1,0},{2,3},{3,2},{4,5},{5,4},{6,7},{7,6},{8,9},{9,8},{10,11... | collective-permute-start | bytes 1572872 | tf_op jit(solution)/shard_map/ppermute | solution.py:616
  52.8 29.8 %collective-permute-start.16 = (bf16[2176,128]{1,0:T(8,128)(2,1)}, bf16[2176,128]{1,0:T(8,128)(2,1)}, u32[]{:S(2)}, u32[]{:S(2)}) collective-permute-start(bf16[2176,128]{1,0:T(8,128)(2,1)} %get-tuple-element.60), channel_id=1, source_target_pairs={{5,7},{2,4},{3,6},{7,5},{4,2},{6,3},{13,15},{10,12},{11,14},{15,13... | collective-permute-start | bytes 1671176 | tf_op jit(solution)/shard_map/ppermute | solution.py:667
  55.0 16.1 %collective-permute-start.9 = (bf16[2,128,1024]{2,1,0:T(8,128)(2,1)}, bf16[2,128,1024]{2,1,0:T(8,128)(2,1)}, u32[]{:S(2)}, u32[]{:S(2)}) collective-permute-start(bf16[2,128,1024]{2,1,0:T(8,128)(2,1)} %get-tuple-element.62), channel_id=1, source_target_pairs={{0,2},{1,3},{8,10},{9,11},{16,18},{17,19},{24,26},{25,27}} | collective-permute-start | bytes 1572872 | tf_op jit(solution)/shard_map/ppermute | solution.py:597
  56.5 26.1 %collective-permute-start.15 = (bf16[2,128,1024]{2,1,0:T(8,128)(2,1)}, bf16[2,128,1024]{2,1,0:T(8,128)(2,1)}, u32[]{:S(2)}, u32[]{:S(2)}) collective-permute-start(bf16[2,128,1024]{2,1,0:T(8,128)(2,1)} %collective-permute-done.14.refs_5_), channel_id=1, source_target_pairs={{0,1},{1,0},{2,3},{3,2},{4,5},{5,4},{6,7},{7,6},{8,9},{9,8},{10,11... | collective-permute-start | bytes 1572872 | tf_op jit(solution)/shard_map/ppermute | solution.py:616
  63.1 27.1 %collective-permute-start.19 = (f32[512,128]{1,0:T(8,128)}, f32[512,128]{1,0:T(8,128)}, u32[]{:S(2)}, u32[]{:S(2)}) collective-permute-start(f32[512,128]{1,0:T(8,128)} %multiply_add_fusion.1), channel_id=1, source_target_pairs={{1,5},{3,7},{9,13},{11,15},{17,21},{19,23},{25,29},{27,31}} | collective-permute-start | bytes 786440 | tf_op jit(solution)/shard_map/ppermute | solution.py:257
  69.2 22.9 %collective-permute-start.13 = (bf16[2176,128]{1,0:T(8,128)(2,1)}, bf16[2176,128]{1,0:T(8,128)(2,1)}, u32[]{:S(2)}, u32[]{:S(2)}) collective-permute-start(bf16[2176,128]{1,0:T(8,128)(2,1)} %get-tuple-element.65), channel_id=1, source_target_pairs={{5,7},{2,4},{3,6},{7,5},{4,2},{6,3},{13,15},{10,12},{11,14},{15,13... | collective-permute-start | bytes 1671176 | tf_op jit(solution)/shard_map/ppermute | solution.py:667
  71.2 20.9 %collective-permute-start.10 = (bf16[2,128,1024]{2,1,0:T(8,128)(2,1)}, bf16[2,128,1024]{2,1,0:T(8,128)(2,1)}, u32[]{:S(2)}, u32[]{:S(2)}) collective-permute-start(bf16[2,128,1024]{2,1,0:T(8,128)(2,1)} %collective-permute-done.9.refs_5_), channel_id=1, source_target_pairs={{0,1},{1,0},{2,3},{3,2},{4,5},{5,4},{6,7},{7,6},{8,9},{9,8},{10,11... | collective-permute-start | bytes 1572872 | tf_op jit(solution)/shard_map/ppermute | solution.py:616
  87.4 14.6 %collective-permute-start.21 = (bf16[2176,128]{1,0:T(8,128)(2,1)}, bf16[2176,128]{1,0:T(8,128)(2,1)}, u32[]{:S(2)}, u32[]{:S(2)}) collective-permute-start(bf16[2176,128]{1,0:T(8,128)(2,1)} %get-tuple-element.73), channel_id=1, source_target_pairs={{5,7},{2,4},{3,6},{13,15},{10,12},{11,14},{21,23},{18,20},{19,22},... | collective-permute-start | bytes 1671176 | tf_op jit(solution)/shard_map/ppermute | solution.py:667
  92.1 4.8 %collective-permute-start.20 = (f32[512,128]{1,0:T(8,128)}, f32[512,128]{1,0:T(8,128)}, u32[]{:S(2)}, u32[]{:S(2)}) collective-permute-start(f32[512,128]{1,0:T(8,128)} %multiply_add_fusion.enter_ref), channel_id=1, source_target_pairs={{0,1},{1,0},{2,3},{3,2},{4,5},{5,4},{6,7},{7,6},{8,9},{9,8},{10,11... | collective-permute-start | bytes 786440 | tf_op jit(solution)/shard_map/ppermute | solution.py:265
  102.0 17.0 %collective-permute-start.25 = (bf16[2176,128]{1,0:T(8,128)(2,1)}, bf16[2176,128]{1,0:T(8,128)(2,1)}, u32[]{:S(2)}, u32[]{:S(2)}) collective-permute-start(bf16[2176,128]{1,0:T(8,128)(2,1)} %collective-permute-done.16.refs_7_.refs_0_), channel_id=1, source_target_pairs={{0,1},{1,0},{2,3},{3,2},{4,5},{5,4},{6,7},{7,6},{8,9},{9,8},{10,11... | collective-permute-start | bytes 1671176 | tf_op jit(solution)/shard_map/ppermute | solution.py:680
  108.2 13.4 %collective-permute-start.24 = (bf16[2176,128]{1,0:T(8,128)(2,1)}, bf16[2176,128]{1,0:T(8,128)(2,1)}, u32[]{:S(2)}, u32[]{:S(2)}) collective-permute-start(bf16[2176,128]{1,0:T(8,128)(2,1)} %collective-permute-done.13.refs_7_.refs_0_), channel_id=1, source_target_pairs={{0,1},{1,0},{2,3},{3,2},{4,5},{5,4},{6,7},{7,6},{8,9},{9,8},{10,11... | collective-permute-start | bytes 1671176 | tf_op jit(solution)/shard_map/ppermute | solution.py:680
  108.2 16.0 %collective-permute-start.23 = (bf16[2176,128]{1,0:T(8,128)(2,1)}, bf16[2176,128]{1,0:T(8,128)(2,1)}, u32[]{:S(2)}, u32[]{:S(2)}) collective-permute-start(bf16[2176,128]{1,0:T(8,128)(2,1)} %collective-permute-done.21.refs_0_), channel_id=1, source_target_pairs={{0,1},{1,0},{2,3},{3,2},{4,5},{5,4},{6,7},{7,6},{8,9},{9,8},{10,11... | collective-permute-start | bytes 1671176 | tf_op jit(solution)/shard_map/ppermute | solution.py:680
  108.8 18.2 %collective-permute-start.22 = (bf16[2176,128]{1,0:T(8,128)(2,1)}, bf16[2176,128]{1,0:T(8,128)(2,1)}, u32[]{:S(2)}, u32[]{:S(2)}) collective-permute-start(bf16[2176,128]{1,0:T(8,128)(2,1)} %get-tuple-element.75), channel_id=1, source_target_pairs={{5,7},{2,4},{3,6},{13,15},{10,12},{11,14},{21,23},{18,20},{19,22},... | collective-permute-start | bytes 1671176 | tf_op jit(solution)/shard_map/ppermute | solution.py:667
  127.0 2.4 %collective-permute-start.26 = (bf16[2176,128]{1,0:T(8,128)(2,1)}, bf16[2176,128]{1,0:T(8,128)(2,1)}, u32[]{:S(2)}, u32[]{:S(2)}) collective-permute-start(bf16[2176,128]{1,0:T(8,128)(2,1)} %collective-permute-done.22.refs_0_), channel_id=1, source_target_pairs={{0,1},{1,0},{2,3},{3,2},{4,5},{5,4},{6,7},{7,6},{8,9},{9,8},{10,11... | collective-permute-start | bytes 1671176 | tf_op jit(solution)/shard_map/ppermute | solution.py:680

commit v15 on v12

--- a/solution.py
+++ b/solution.py
@@ -27,7 +27,7 @@
 
 def cost(microseconds):
     return pl.CostEstimate(
-        flops=microseconds * 10**8, bytes_accessed=2**16, transcendentals=0
+        flops=microseconds * 10**7, bytes_accessed=2**16, transcendentals=0
     )
 
 
@@ -610,6 +610,8 @@
         if chunk == 0:
             quad_kv[0] = [after(quad_kv[0][0], local_result)]
             asks[0] = [after(asked, local_result) for asked in asks[0]]
+        elif chunk == chunks - 1:
+            quad_kv[chunk] = [after(quad_kv[chunk][0], asks[3][0])]
         quad_kv[chunk].append(lax.ppermute(quad_kv[chunk][0], "ctx", swap))
         steps, first = CHUNK_STEPS[chunk], first_steps[chunk]
         whole_spec = pl.BlockSpec((rows, step_width), lambda step, first=first: (0, first + step))

time: 127 us -> 124 us (0.976)
  starting transfers between devices: 59.9 us -> 56.8 us
    ppermute x4, starting transfers between devices: 17.3 us -> 14.1 us  [attend(): arrivals.append(lax.ppermute(answer, 'ctx', moves))]
    ppermute x2, waiting for transfers between devices: 0.01 us -> 2.91 us  [entering_state(): arrived = lax.ppermute(total, 'ctx', moves)]
    ppermute x4, waiting for transfers between devices: 5.94 us -> 3.81 us  [attend(): arrivals.append(lax.ppermute(answer, 'ctx', moves))]
  transfers between devices with their start and end apart: 28 -> 28, of which waited for: 3 -> 4; matrix products, arithmetic and copies ran while one was open for 4% -> 4% of each run, Pallas kernels for 36% -> 37%
where the time goes in v15:
time: 124 us
  starting transfers between devices  56.8 us (46%)
  Pallas kernels  47.9 us (39%)
  waiting for transfers between devices  11.1 us (9%)
  other arithmetic  5.53 us (4%)
  local copies, waits for them, and re-layouts  1.4 us (1%)
    pallas_call x4, Pallas kernels, attend(): pl.pallas_call(functools.partial(partial_kernel, transfers, upper, natura...  19.1 us
    ppermute x4, starting transfers between devices, attend(): arrivals.append(lax.ppermute(answer, 'ctx', moves))  14.1 us
    ppermute x4, starting transfers between devices, attend(): quad_kv[chunk].append(lax.ppermute(quad_kv[chunk][0], 'ctx', swap))  11.8 us
    pallas_call x4, Pallas kernels, attend(): pl.pallas_call(functools.partial(merge_kernel, transfers, steps, starts[c...  10.6 us
    pallas_call x1, Pallas kernels, first_part(): pl.pallas_call(functools.partial(state_kernel, modes), grid=(groups,), in...  9.78 us
    pallas_call x1, Pallas kernels, last_part(): pl.pallas_call(functools.partial(output_kernel, modes), grid=(groups,), i...  6.31 us
    ppermute x4, starting transfers between devices, send(): quad_kv.append([lax.ppermute(key_pack, 'ctx', gathers)])  5.89 us
    ppermute x4, starting transfers between devices, attend(): parts += [arrival, lax.ppermute(arrival, 'ctx', swap)]  5.81 us
  transfers between devices with their start and end apart: 28, of which 4 were waited for; matrix products, arithmetic and copies ran while one was open for 4% of the time, Pallas kernels for 37%

profile of v15, /device:TPU:17, one launch (start us, length us, event | category | flops | bytes accessed | tf_op | source)
XLA Modules:
  0.0 123.7 jit_solution(3655789071714427586)
XLA Ops:
  0.6 0.7 collective-permute-start.2
  1.4 1.8 %conv_pack.1 = (f32[4,128,128]{2,1,0:T(8,128)}, f32[8,4096]{1,0:T(8,128)}) custom-call(f32[16,512]{1,0:T(8,128)} %bitcast.2, f32[16,512]{1,0:T(8,128)} %bitcast.3, bf16[128,4096]{1,0:T(8,128)(2,1)} %q_ref.5, bf16[128,4096]{1,0:T(8,128)(2,1)} %k_ref.5, bf16[128,4096]{1,0:T(8,128)(2,1)} %v_ref.5), custom_call_target="tpu_custom_call" | custom-call | flops 10000000 | bytes 65536 | tf_op jit(solution)/shard_map/conv_pack/pallas_call | solution.py:203
  3.2 3.1 %collective-permute-start.7 = (f32[8,4096]{1,0:T(8,128)}, f32[8,4096]{1,0:T(8,128)S(1)}, u32[]{:S(2)}, u32[]{:S(2)}) collective-permute-start(f32[8,4096]{1,0:T(8,128)} %get-tuple-element.54), channel_id=1, source_target_pairs={{0,1},{1,2},{2,3},{3,4},{4,5},{5,6},{6,7},{8,9},{9,10},{10,11},{11... | collective-permute-start | bytes 393224 | tf_op jit(solution)/shard_map/ppermute | solution.py:220
  6.3 0.2 att_pack.1
  6.5 2.0 %collective-permute-done.7.rim_ref = f32[8,4096]{1,0:T(8,128)S(1)} collective-permute-done((f32[8,4096]{1,0:T(8,128)}, f32[8,4096]{1,0:T(8,128)S(1)}, u32[]{:S(2)}, u32[]{:S(2)}) %collective-permute-start.7) | collective-permute-done | bytes 131104 | tf_op jit(solution)/shard_map/ppermute | solution.py:220
  8.6 3.6 %all-to-all-start = ((f32[4,128,128]{2,1,0:T(8,128)}), f32[4,128,128]{2,1,0:T(8,128)S(1)}, u32[]{:S(2)}, u32[]{:S(2)}) async-start(f32[4,128,128]{2,1,0:T(8,128)} %get-tuple-element.57), calls=%async_computation | async-start | bytes 524288 | tf_op jit(solution)/shard_map/all_to_all | solution.py:222
  12.2 2.7 %collective-permute-start = (bf16[128,4096]{1,0:T(8,128)(2,1)}, bf16[128,4096]{1,0:T(8,128)(2,1)}, u32[]{:S(2)}, u32[]{:S(2)}) collective-permute-start(bf16[128,4096]{1,0:T(8,128)(2,1)} %refs_1_.7), channel_id=1, source_target_pairs={{0,1},{1,0},{2,3},{3,2},{4,5},{5,4},{6,7},{7,6},{8,9},{9,8},{10,11... | collective-permute-start | bytes 3145736 | tf_op jit(solution)/shard_map/ppermute | solution.py:553
  14.9 1.5 %collective-permute-start.6 = (bf16[2,128,1024]{2,1,0:T(8,128)(2,1)}, bf16[2,128,1024]{2,1,0:T(8,128)(2,1)}, u32[]{:S(2)}, u32[]{:S(2)}) collective-permute-start(bf16[2,128,1024]{2,1,0:T(8,128)(2,1)} %get-tuple-element.53), channel_id=1, source_target_pairs={{0,2},{1,3},{8,10},{9,11},{16,18},{17,19},{24,26},{25,27}} | collective-permute-start | bytes 1572872 | tf_op jit(solution)/shard_map/ppermute | solution.py:596
  16.4 0.0 collective-permute-start.1
  16.4 0.7 copy-done
  17.1 3.1 %collective-permute-start.8 = (f32[4,128,128]{2,1,0:T(8,128)S(1)}, f32[4,128,128]{2,1,0:T(8,128)S(1)}, u32[]{:S(2)}, u32[]{:S(2)}) collective-permute-start(f32[4,128,128]{2,1,0:T(8,128)S(1)} %all-to-all-done.same_ref), channel_id=1, source_target_pairs={{0,1},{1,0},{2,3},{3,2},{4,5},{5,4},{6,7},{7,6},{8,9},{9,8},{10,11... | collective-permute-start | bytes 786440 | tf_op jit(solution)/shard_map/ppermute | solution.py:230
  20.2 1.3 %collective-permute-start.10 = (bf16[2,128,1024]{2,1,0:T(8,128)(2,1)}, bf16[2,128,1024]{2,1,0:T(8,128)(2,1)}, u32[]{:S(2)}, u32[]{:S(2)}) collective-permute-start(bf16[2,128,1024]{2,1,0:T(8,128)(2,1)} %get-tuple-element.56), channel_id=1, source_target_pairs={{7,5},{4,2},{6,3},{15,13},{12,10},{14,11},{23,21},{20,18},{22,19},... | collective-permute-start | bytes 1572872 | tf_op jit(solution)/shard_map/ppermute | solution.py:601
  21.5 0.7 copy-done.1
  22.2 1.5 %collective-permute-start.3 = (bf16[2,128,1024]{2,1,0:T(8,128)(2,1)}, bf16[2,128,1024]{2,1,0:T(8,128)(2,1)}, u32[]{:S(2)}, u32[]{:S(2)}) collective-permute-start(bf16[2,128,1024]{2,1,0:T(8,128)(2,1)} %get-tuple-element.51), channel_id=1, source_target_pairs={{0,2},{1,3},{8,10},{9,11},{16,18},{17,19},{24,26},{25,27}} | collective-permute-start | bytes 1572872 | tf_op jit(solution)/shard_map/ppermute | solution.py:596
  23.7 9.8 %conv_state.1 = (f32[128,4096]{1,0:T(8,128)}, f32[512,128]{1,0:T(8,128)}, f32[512,128]{1,0:T(8,128)}) custom-call(bf16[128,4096]{1,0:T(8,128)(2,1)} %k_ref.5, bf16[128,4096]{1,0:T(8,128)(2,1)} %v_ref.5, f32[8,4096]{1,0:T(8,128)} %copy-done.2, f32[4,128,128]{2,1,0:T(8,128)} %copy-done, f32[4,128,128]{2,1,0:T(8,128)} %copy-done.1, f32[3,3,4096]{2,1,0:T(4,128)} %taps_ref.3), custom_call_target="tpu_custom_call" | custom-call | flops 90000000 | bytes 65536 | tf_op jit(solution)/shard_map/conv_state/pallas_call | solution.py:232
  33.5 3.6 %collective-permute-start.9 = (bf16[2,128,1024]{2,1,0:T(8,128)(2,1)}, bf16[2,128,1024]{2,1,0:T(8,128)(2,1)}, u32[]{:S(2)}, u32[]{:S(2)}) collective-permute-start(bf16[2,128,1024]{2,1,0:T(8,128)(2,1)} %collective-permute-done.6.refs_5_), channel_id=1, source_target_pairs={{0,1},{1,0},{2,3},{3,2},{4,5},{5,4},{6,7},{7,6},{8,9},{9,8},{10,11... | collective-permute-start | bytes 1572872 | tf_op jit(solution)/shard_map/ppermute | solution.py:615
  37.2 0.1 collective-permute-start.17
  37.2 1.3 %collective-permute-start.5 = (bf16[2,128,1024]{2,1,0:T(8,128)(2,1)}, bf16[2,128,1024]{2,1,0:T(8,128)(2,1)}, u32[]{:S(2)}, u32[]{:S(2)}) collective-permute-start(bf16[2,128,1024]{2,1,0:T(8,128)(2,1)} %get-tuple-element.52), channel_id=1, source_target_pairs={{7,5},{4,2},{6,3},{15,13},{12,10},{14,11},{23,21},{20,18},{22,19},... | collective-permute-start | bytes 1572872 | tf_op jit(solution)/shard_map/ppermute | solution.py:601
  38.5 3.6 %collective-permute-start.4 = (bf16[2,128,1024]{2,1,0:T(8,128)(2,1)}, bf16[2,128,1024]{2,1,0:T(8,128)(2,1)}, u32[]{:S(2)}, u32[]{:S(2)}) collective-permute-start(bf16[2,128,1024]{2,1,0:T(8,128)(2,1)} %collective-permute-done.3.refs_5_), channel_id=1, source_target_pairs={{0,1},{1,0},{2,3},{3,2},{4,5},{5,4},{6,7},{7,6},{8,9},{9,8},{10,11... | collective-permute-start | bytes 1572872 | tf_op jit(solution)/shard_map/ppermute | solution.py:615
  42.1 4.8 %att_partial.4 = (f32[128,1024]{1,0:T(8,128)}, f32[16,128]{1,0:T(8,128)}, bf16[2176,128]{1,0:T(8,128)(2,1)}, bf16[128,4096]{1,0:T(8,128)(2,1)}) custom-call(bf16[128,4096]{1,0:T(8,128)(2,1)} %refs_0_.7, bf16[128,4096]{1,0:T(8,128)(2,1)} %refs_1_.7, bf16[128,4096]{1,0:T(8,128)(2,1)} %refs_2_.7, bf16[128,4096]{1,0:T(8,128)(2,1)} %collective-permute-done.refs_3_, ...), custom_call_target="tpu_custom_call" | custom-call | flops 40000000 | bytes 65536 | tf_op jit(solution)/shard_map/att_partial/pallas_call | solution.py:639
  46.9 1.5 %collective-permute-start.14 = (bf16[2,128,1024]{2,1,0:T(8,128)(2,1)}, bf16[2,128,1024]{2,1,0:T(8,128)(2,1)}, u32[]{:S(2)}, u32[]{:S(2)}) collective-permute-start(bf16[2,128,1024]{2,1,0:T(8,128)(2,1)} %get-tuple-element.67), channel_id=1, source_target_pairs={{0,2},{1,3},{8,10},{9,11},{16,18},{17,19},{24,26},{25,27}} | collective-permute-start | bytes 1572872 | tf_op jit(solution)/shard_map/ppermute | solution.py:596
  48.4 1.8 %multiply_add_fusion.2 = f32[512,128]{1,0:T(8,128)} fusion(f32[512,128]{1,0:T(8,128)} %get-tuple-element.72, f32[512,128]{1,0:T(8,128)} %get-tuple-element.79.decay_ref, f32[512,128]{1,0:T(8,128)} %collective-permute-done.17.other_ref), kind=kLoop, calls=%fused_computation.2 | loop fusion | flops 131072 | bytes 1048576 | tf_op jit(solution)/shard_map/add | solution.py:252
  50.2 1.9 %collective-permute-start.18 = (f32[512,128]{1,0:T(8,128)}, f32[512,128]{1,0:T(8,128)}, u32[]{:S(2)}, u32[]{:S(2)}) collective-permute-start(f32[512,128]{1,0:T(8,128)} %multiply_add_fusion.2), channel_id=1, source_target_pairs={{1,3},{3,5},{5,7},{9,11},{11,13},{13,15},{17,19},{19,21},{21,23},{... | collective-permute-start | bytes 786440 | tf_op jit(solution)/shard_map/ppermute | solution.py:257
  52.2 1.9 %collective-permute-start.16 = (bf16[2176,128]{1,0:T(8,128)(2,1)}, bf16[2176,128]{1,0:T(8,128)(2,1)}, u32[]{:S(2)}, u32[]{:S(2)}) collective-permute-start(bf16[2176,128]{1,0:T(8,128)(2,1)} %get-tuple-element.66), channel_id=1, source_target_pairs={{5,7},{2,4},{3,6},{7,5},{4,2},{6,3},{13,15},{10,12},{11,14},{15,13... | collective-permute-start | bytes 1671176 | tf_op jit(solution)/shard_map/ppermute | solution.py:666
  54.1 4.8 %att_partial.5 = (f32[128,1024]{1,0:T(8,128)}, f32[16,128]{1,0:T(8,128)}, bf16[2176,128]{1,0:T(8,128)(2,1)}, bf16[128,4096]{1,0:T(8,128)(2,1)}) custom-call(bf16[128,4096]{1,0:T(8,128)(2,1)} %refs_0_.7, bf16[128,4096]{1,0:T(8,128)(2,1)} %refs_1_.7, bf16[128,4096]{1,0:T(8,128)(2,1)} %refs_2_.7, ...), custom_call_target="tpu_custom_call", output_to_operand_aliasing={{3}: (10, {})} | custom-call | flops 40000000 | bytes 65536 | tf_op jit(solution)/shard_map/att_partial/pallas_call | solution.py:639
  59.0 2.1 %collective-permute-start.12 = (bf16[2176,128]{1,0:T(8,128)(2,1)}, bf16[2176,128]{1,0:T(8,128)(2,1)}, u32[]{:S(2)}, u32[]{:S(2)}) collective-permute-start(bf16[2176,128]{1,0:T(8,128)(2,1)} %get-tuple-element.62), channel_id=1, source_target_pairs={{5,7},{2,4},{3,6},{7,5},{4,2},{6,3},{13,15},{10,12},{11,14},{15,13... | collective-permute-start | bytes 1671176 | tf_op jit(solution)/shard_map/ppermute | solution.py:666
  61.1 2.8 %collective-permute-start.15 = (bf16[2,128,1024]{2,1,0:T(8,128)(2,1)}, bf16[2,128,1024]{2,1,0:T(8,128)(2,1)}, u32[]{:S(2)}, u32[]{:S(2)}) collective-permute-start(bf16[2,128,1024]{2,1,0:T(8,128)(2,1)} %collective-permute-done.14.refs_5_), channel_id=1, source_target_pairs={{0,1},{1,0},{2,3},{3,2},{4,5},{5,4},{6,7},{7,6},{8,9},{9,8},{10,11... | collective-permute-start | bytes 1572872 | tf_op jit(solution)/shard_map/ppermute | solution.py:615
  63.9 1.5 %collective-permute-start.11 = (bf16[2,128,1024]{2,1,0:T(8,128)(2,1)}, bf16[2,128,1024]{2,1,0:T(8,128)(2,1)}, u32[]{:S(2)}, u32[]{:S(2)}) collective-permute-start(bf16[2,128,1024]{2,1,0:T(8,128)(2,1)} %get-tuple-element.63), channel_id=1, source_target_pairs={{0,2},{1,3},{8,10},{9,11},{16,18},{17,19},{24,26},{25,27}} | collective-permute-start | bytes 1572872 | tf_op jit(solution)/shard_map/ppermute | solution.py:596
  65.4 1.8 %multiply_add_fusion.1 = f32[512,128]{1,0:T(8,128)} fusion(f32[512,128]{1,0:T(8,128)} %multiply_add_fusion.2, f32[512,128]{1,0:T(8,128)} %collective-permute-done.18, f32[512,128]{1,0:T(8,128)} %get-tuple-element.79.decay_ref), kind=kLoop, calls=%fused_computation.1 | loop fusion | flops 196608 | bytes 1048576 | tf_op jit(solution)/shard_map/add | solution.py:263
  67.2 1.3 %collective-permute-start.19 = (f32[512,128]{1,0:T(8,128)}, f32[512,128]{1,0:T(8,128)}, u32[]{:S(2)}, u32[]{:S(2)}) collective-permute-start(f32[512,128]{1,0:T(8,128)} %multiply_add_fusion.1), channel_id=1, source_target_pairs={{1,5},{3,7},{9,13},{11,15},{17,21},{19,23},{25,29},{27,31}} | collective-permute-start | bytes 786440 | tf_op jit(solution)/shard_map/ppermute | solution.py:257
  68.5 4.8 %att_partial.6 = (f32[128,1024]{1,0:T(8,128)}, f32[16,128]{1,0:T(8,128)}, bf16[2176,128]{1,0:T(8,128)(2,1)}, bf16[128,4096]{1,0:T(8,128)(2,1)}) custom-call(bf16[128,4096]{1,0:T(8,128)(2,1)} %refs_0_.7, bf16[128,4096]{1,0:T(8,128)(2,1)} %refs_1_.7, bf16[128,4096]{1,0:T(8,128)(2,1)} %refs_2_.7, ...), custom_call_target="tpu_custom_call", output_to_operand_aliasing={{3}: (8, {})} | custom-call | flops 40000000 | bytes 65536 | tf_op jit(solution)/shard_map/att_partial/pallas_call | solution.py:639
  73.3 2.1 %collective-permute-start.21 = (bf16[2176,128]{1,0:T(8,128)(2,1)}, bf16[2176,128]{1,0:T(8,128)(2,1)}, u32[]{:S(2)}, u32[]{:S(2)}) collective-permute-start(bf16[2176,128]{1,0:T(8,128)(2,1)} %get-tuple-element.73), channel_id=1, source_target_pairs={{5,7},{2,4},{3,6},{13,15},{10,12},{11,14},{21,23},{18,20},{19,22},... | collective-permute-start | bytes 1671176 | tf_op jit(solution)/shard_map/ppermute | solution.py:666
  75.4 3.8 %collective-permute-done.12.refs_7_.refs_0_ = bf16[2176,128]{1,0:T(8,128)(2,1)} collective-permute-done((bf16[2176,128]{1,0:T(8,128)(2,1)}, bf16[2176,128]{1,0:T(8,128)(2,1)}, u32[]{:S(2)}, u32[]{:S(2)}) %collective-permute-start.12) | collective-permute-done | bytes 557088 | tf_op jit(solution)/shard_map/ppermute | solution.py:666
  79.2 1.8 %collective-permute-start.13 = (bf16[2,128,1024]{2,1,0:T(8,128)(2,1)}, bf16[2,128,1024]{2,1,0:T(8,128)(2,1)}, u32[]{:S(2)}, u32[]{:S(2)}) collective-permute-start(bf16[2,128,1024]{2,1,0:T(8,128)(2,1)} %collective-permute-done.11.refs_5_), channel_id=1, source_target_pairs={{0,1},{1,0},{2,3},{3,2},{4,5},{5,4},{6,7},{7,6},{8,9},{9,8},{10,11... | collective-permute-start | bytes 1572872 | tf_op jit(solution)/shard_map/ppermute | solution.py:615
  81.0 2.9 %collective-permute-done.19 = f32[512,128]{1,0:T(8,128)} collective-permute-done((f32[512,128]{1,0:T(8,128)}, f32[512,128]{1,0:T(8,128)}, u32[]{:S(2)}, u32[]{:S(2)}) %collective-permute-start.19) | collective-permute-done | bytes 262176 | tf_op jit(solution)/shard_map/ppermute | solution.py:257
  83.9 1.8 %multiply_add_fusion.enter_ref = f32[512,128]{1,0:T(8,128)} fusion(f32[512,128]{1,0:T(8,128)} %collective-permute-done.18, f32[512,128]{1,0:T(8,128)} %collective-permute-done.19, f32[512,128]{1,0:T(8,128)} %get-tuple-element.79.decay_ref), kind=kLoop, calls=%fused_computation | loop fusion | flops 196608 | bytes 1048576 | tf_op jit(solution)/shard_map/add | solution.py:261
  85.7 4.7 %att_partial.7 = (f32[128,1024]{1,0:T(8,128)}, f32[16,128]{1,0:T(8,128)}, bf16[2176,128]{1,0:T(8,128)(2,1)}, bf16[128,4096]{1,0:T(8,128)(2,1)}) custom-call(bf16[128,4096]{1,0:T(8,128)(2,1)} %refs_0_.7, bf16[128,4096]{1,0:T(8,128)(2,1)} %refs_1_.7, bf16[128,4096]{1,0:T(8,128)(2,1)} %refs_2_.7, ...), custom_call_target="tpu_custom_call", output_to_operand_aliasing={{3}: (8, {})} | custom-call | flops 40000000 | bytes 65536 | tf_op jit(solution)/shard_map/att_partial/pallas_call | solution.py:639
  90.5 5.2 %collective-permute-start.25 = (bf16[2176,128]{1,0:T(8,128)(2,1)}, bf16[2176,128]{1,0:T(8,128)(2,1)}, u32[]{:S(2)}, u32[]{:S(2)}) collective-permute-start(bf16[2176,128]{1,0:T(8,128)(2,1)} %collective-permute-done.16.refs_7_.refs_0_), channel_id=1, source_target_pairs={{0,1},{1,0},{2,3},{3,2},{4,5},{5,4},{6,7},{7,6},{8,9},{9,8},{10,11... | collective-permute-start | bytes 1671176 | tf_op jit(solution)/shard_map/ppermute | solution.py:679
  95.7 0.0 collective-permute-start.24
  95.7 0.5 collective-permute-start.23
  96.2 8.0 %collective-permute-start.22 = (bf16[2176,128]{1,0:T(8,128)(2,1)}, bf16[2176,128]{1,0:T(8,128)(2,1)}, u32[]{:S(2)}, u32[]{:S(2)}) collective-permute-start(bf16[2176,128]{1,0:T(8,128)(2,1)} %get-tuple-element.75), channel_id=1, source_target_pairs={{5,7},{2,4},{3,6},{13,15},{10,12},{11,14},{21,23},{18,20},{19,22},... | collective-permute-start | bytes 1671176 | tf_op jit(solution)/shard_map/ppermute | solution.py:666
  104.2 6.3 %conv_output.1 = bf16[128,4096]{1,0:T(8,128)(2,1)} custom-call(bf16[128,4096]{1,0:T(8,128)(2,1)} %q_ref.5, f32[128,4096]{1,0:T(8,128)} %get-tuple-element.58.y_ref, f32[8,4096]{1,0:T(8,128)} %copy-done.2, f32[4,128,128]{2,1,0:T(8,128)} %copy-done, f32[4,128,128]{2,1,0:T(8,128)} %copy-done.1, f32[512,128]{1,0:T(8,128)} %get-tuple-element.79.decay_ref, ...), custom_call_target="tpu_custom_call" | custom-call | flops 60000000 | bytes 65536 | tf_op jit(solution)/shard_map/conv_output/pallas_call | solution.py:269
  110.5 2.7 %att_merge.4.refs_2_ = bf16[128,4096]{1,0:T(8,128)(2,1)} custom-call(f32[128,1024]{1,0:T(8,128)} %get-tuple-element.89.own_hbm, f32[16,128]{1,0:T(8,128)} %get-tuple-element.90.lse_hbm, bf16[2176,128]{1,0:T(8,128)(2,1)} %collective-permute-done.16.refs_7_.refs_0_, bf16[2176,128]{1,0:T(8,128)(2,1)} %collective-permute-done.25.refs_1_, ...), custom_call_target="tpu_custom_call", output_to_operand_aliasing={{}: (4, {})} | custom-call | flops 20000000 | bytes 65536 | tf_op jit(solution)/shard_map/att_merge/pallas_call | solution.py:682
  113.2 2.7 %att_merge.5.refs_2_ = bf16[128,4096]{1,0:T(8,128)(2,1)} custom-call(f32[128,1024]{1,0:T(8,128)} %get-tuple-element.86.own_hbm, f32[16,128]{1,0:T(8,128)} %get-tuple-element.87.lse_hbm, bf16[2176,128]{1,0:T(8,128)(2,1)} %collective-permute-done.12.refs_7_.refs_0_, bf16[2176,128]{1,0:T(8,128)(2,1)} %collective-permute-done.24.refs_1_, ...), custom_call_target="tpu_custom_call", output_to_operand_aliasing={{}: (4, {})} | custom-call | flops 20000000 | bytes 65536 | tf_op jit(solution)/shard_map/att_merge/pallas_call | solution.py:682
  115.9 2.7 %att_merge.6.refs_2_ = bf16[128,4096]{1,0:T(8,128)(2,1)} custom-call(f32[128,1024]{1,0:T(8,128)} %get-tuple-element.83.own_hbm, f32[16,128]{1,0:T(8,128)} %get-tuple-element.84.lse_hbm, bf16[2176,128]{1,0:T(8,128)(2,1)} %collective-permute-done.21.refs_0_, bf16[2176,128]{1,0:T(8,128)(2,1)} %collective-permute-done.23.refs_1_, ...), custom_call_target="tpu_custom_call", output_to_operand_aliasing={{}: (4, {})} | custom-call | flops 20000000 | bytes 65536 | tf_op jit(solution)/shard_map/att_merge/pallas_call | solution.py:682
  118.5 0.1 collective-permute-start.26
  118.6 2.3 %collective-permute-done.26.refs_1_ = bf16[2176,128]{1,0:T(8,128)(2,1)} collective-permute-done((bf16[2176,128]{1,0:T(8,128)(2,1)}, bf16[2176,128]{1,0:T(8,128)(2,1)}, u32[]{:S(2)}, u32[]{:S(2)}) %collective-permute-start.26) | collective-permute-done | bytes 557088 | tf_op jit(solution)/shard_map/ppermute | solution.py:679
  120.9 2.6 %att_merge.7 = bf16[128,4096]{1,0:T(8,128)(2,1)} custom-call(f32[128,1024]{1,0:T(8,128)} %get-tuple-element.94.own_hbm, f32[16,128]{1,0:T(8,128)} %get-tuple-element.95.lse_hbm, bf16[2176,128]{1,0:T(8,128)(2,1)} %collective-permute-done.22.refs_0_, bf16[2176,128]{1,0:T(8,128)(2,1)} %collective-permute-done.26.refs_1_, ...), custom_call_target="tpu_custom_call", output_to_operand_aliasing={{}: (4, {})} | custom-call | flops 20000000 | bytes 65536 | tf_op jit(solution)/shard_map/att_merge/pallas_call | solution.py:682
  (29 shorter events, 0.1 us)
Async XLA Ops:
  0.6 5.7 %collective-permute-start.2 = (bf16[128,4096]{1,0:T(8,128)(2,1)}, bf16[128,4096]{1,0:T(8,128)(2,1)}, u32[]{:S(2)}, u32[]{:S(2)}) collective-permute-start(bf16[128,4096]{1,0:T(8,128)(2,1)} %refs_0_.7), channel_id=1, source_target_pairs={{0,1},{1,0},{2,3},{3,2},{4,5},{5,4},{6,7},{7,6},{8,9},{9,8},{10,11... | collective-permute-start | bytes 3145736 | tf_op jit(solution)/shard_map/ppermute | solution.py:552
  3.2 5.3 %collective-permute-start.7 = (f32[8,4096]{1,0:T(8,128)}, f32[8,4096]{1,0:T(8,128)S(1)}, u32[]{:S(2)}, u32[]{:S(2)}) collective-permute-start(f32[8,4096]{1,0:T(8,128)} %get-tuple-element.54), channel_id=1, source_target_pairs={{0,1},{1,2},{2,3},{3,4},{4,5},{5,6},{6,7},{8,9},{9,10},{10,11},{11... | collective-permute-start | bytes 393224 | tf_op jit(solution)/shard_map/ppermute | solution.py:220
  8.6 15.2 %copy-start.2 = (f32[8,4096]{1,0:T(8,128)}, f32[8,4096]{1,0:T(8,128)S(1)}, u32[]{:S(2)}) copy-start(f32[8,4096]{1,0:T(8,128)S(1)} %collective-permute-done.7.rim_ref) | copy-start | bytes 393220
  8.6 7.8 %all-to-all-start = ((f32[4,128,128]{2,1,0:T(8,128)}), f32[4,128,128]{2,1,0:T(8,128)S(1)}, u32[]{:S(2)}, u32[]{:S(2)}) async-start(f32[4,128,128]{2,1,0:T(8,128)} %get-tuple-element.57), calls=%async_computation | async-start | bytes 524288 | tf_op jit(solution)/shard_map/all_to_all | solution.py:222
  12.2 25.0 %collective-permute-start = (bf16[128,4096]{1,0:T(8,128)(2,1)}, bf16[128,4096]{1,0:T(8,128)(2,1)}, u32[]{:S(2)}, u32[]{:S(2)}) collective-permute-start(bf16[128,4096]{1,0:T(8,128)(2,1)} %refs_1_.7), channel_id=1, source_target_pairs={{0,1},{1,0},{2,3},{3,2},{4,5},{5,4},{6,7},{7,6},{8,9},{9,8},{10,11... | collective-permute-start | bytes 3145736 | tf_op jit(solution)/shard_map/ppermute | solution.py:553
  14.9 18.6 %collective-permute-start.6 = (bf16[2,128,1024]{2,1,0:T(8,128)(2,1)}, bf16[2,128,1024]{2,1,0:T(8,128)(2,1)}, u32[]{:S(2)}, u32[]{:S(2)}) collective-permute-start(bf16[2,128,1024]{2,1,0:T(8,128)(2,1)} %get-tuple-element.53), channel_id=1, source_target_pairs={{0,2},{1,3},{8,10},{9,11},{16,18},{17,19},{24,26},{25,27}} | collective-permute-start | bytes 1572872 | tf_op jit(solution)/shard_map/ppermute | solution.py:596
  16.4 25.7 %collective-permute-start.1 = (bf16[128,4096]{1,0:T(8,128)(2,1)}, bf16[128,4096]{1,0:T(8,128)(2,1)}, u32[]{:S(2)}, u32[]{:S(2)}) collective-permute-start(bf16[128,4096]{1,0:T(8,128)(2,1)} %refs_2_.7), channel_id=1, source_target_pairs={{0,1},{1,0},{2,3},{3,2},{4,5},{5,4},{6,7},{7,6},{8,9},{9,8},{10,11... | collective-permute-start | bytes 3145736 | tf_op jit(solution)/shard_map/ppermute | solution.py:554
  16.4 0.7 copy-start
  17.1 4.4 %collective-permute-start.8 = (f32[4,128,128]{2,1,0:T(8,128)S(1)}, f32[4,128,128]{2,1,0:T(8,128)S(1)}, u32[]{:S(2)}, u32[]{:S(2)}) collective-permute-start(f32[4,128,128]{2,1,0:T(8,128)S(1)} %all-to-all-done.same_ref), channel_id=1, source_target_pairs={{0,1},{1,0},{2,3},{3,2},{4,5},{5,4},{6,7},{7,6},{8,9},{9,8},{10,11... | collective-permute-start | bytes 786440 | tf_op jit(solution)/shard_map/ppermute | solution.py:230
  20.2 16.9 %collective-permute-start.10 = (bf16[2,128,1024]{2,1,0:T(8,128)(2,1)}, bf16[2,128,1024]{2,1,0:T(8,128)(2,1)}, u32[]{:S(2)}, u32[]{:S(2)}) collective-permute-start(bf16[2,128,1024]{2,1,0:T(8,128)(2,1)} %get-tuple-element.56), channel_id=1, source_target_pairs={{7,5},{4,2},{6,3},{15,13},{12,10},{14,11},{23,21},{20,18},{22,19},... | collective-permute-start | bytes 1572872 | tf_op jit(solution)/shard_map/ppermute | solution.py:601
  21.5 0.7 copy-start.1
  22.2 16.3 %collective-permute-start.3 = (bf16[2,128,1024]{2,1,0:T(8,128)(2,1)}, bf16[2,128,1024]{2,1,0:T(8,128)(2,1)}, u32[]{:S(2)}, u32[]{:S(2)}) collective-permute-start(bf16[2,128,1024]{2,1,0:T(8,128)(2,1)} %get-tuple-element.51), channel_id=1, source_target_pairs={{0,2},{1,3},{8,10},{9,11},{16,18},{17,19},{24,26},{25,27}} | collective-permute-start | bytes 1572872 | tf_op jit(solution)/shard_map/ppermute | solution.py:596
  33.5 8.6 %collective-permute-start.9 = (bf16[2,128,1024]{2,1,0:T(8,128)(2,1)}, bf16[2,128,1024]{2,1,0:T(8,128)(2,1)}, u32[]{:S(2)}, u32[]{:S(2)}) collective-permute-start(bf16[2,128,1024]{2,1,0:T(8,128)(2,1)} %collective-permute-done.6.refs_5_), channel_id=1, source_target_pairs={{0,1},{1,0},{2,3},{3,2},{4,5},{5,4},{6,7},{7,6},{8,9},{9,8},{10,11... | collective-permute-start | bytes 1572872 | tf_op jit(solution)/shard_map/ppermute | solution.py:615
  37.2 11.2 %collective-permute-start.17 = (f32[512,128]{1,0:T(8,128)}, f32[512,128]{1,0:T(8,128)}, u32[]{:S(2)}, u32[]{:S(2)}) collective-permute-start(f32[512,128]{1,0:T(8,128)} %get-tuple-element.72), channel_id=1, source_target_pairs={{0,1},{1,0},{2,3},{3,2},{4,5},{5,4},{6,7},{7,6},{8,9},{9,8},{10,11... | collective-permute-start | bytes 786440 | tf_op jit(solution)/shard_map/ppermute | solution.py:251
  37.2 16.9 %collective-permute-start.5 = (bf16[2,128,1024]{2,1,0:T(8,128)(2,1)}, bf16[2,128,1024]{2,1,0:T(8,128)(2,1)}, u32[]{:S(2)}, u32[]{:S(2)}) collective-permute-start(bf16[2,128,1024]{2,1,0:T(8,128)(2,1)} %get-tuple-element.52), channel_id=1, source_target_pairs={{7,5},{4,2},{6,3},{15,13},{12,10},{14,11},{23,21},{20,18},{22,19},... | collective-permute-start | bytes 1572872 | tf_op jit(solution)/shard_map/ppermute | solution.py:601
  38.5 15.6 %collective-permute-start.4 = (bf16[2,128,1024]{2,1,0:T(8,128)(2,1)}, bf16[2,128,1024]{2,1,0:T(8,128)(2,1)}, u32[]{:S(2)}, u32[]{:S(2)}) collective-permute-start(bf16[2,128,1024]{2,1,0:T(8,128)(2,1)} %collective-permute-done.3.refs_5_), channel_id=1, source_target_pairs={{0,1},{1,0},{2,3},{3,2},{4,5},{5,4},{6,7},{7,6},{8,9},{9,8},{10,11... | collective-permute-start | bytes 1572872 | tf_op jit(solution)/shard_map/ppermute | solution.py:615
  46.9 14.2 %collective-permute-start.14 = (bf16[2,128,1024]{2,1,0:T(8,128)(2,1)}, bf16[2,128,1024]{2,1,0:T(8,128)(2,1)}, u32[]{:S(2)}, u32[]{:S(2)}) collective-permute-start(bf16[2,128,1024]{2,1,0:T(8,128)(2,1)} %get-tuple-element.67), channel_id=1, source_target_pairs={{0,2},{1,3},{8,10},{9,11},{16,18},{17,19},{24,26},{25,27}} | collective-permute-start | bytes 1572872 | tf_op jit(solution)/shard_map/ppermute | solution.py:596
  50.2 15.1 %collective-permute-start.18 = (f32[512,128]{1,0:T(8,128)}, f32[512,128]{1,0:T(8,128)}, u32[]{:S(2)}, u32[]{:S(2)}) collective-permute-start(f32[512,128]{1,0:T(8,128)} %multiply_add_fusion.2), channel_id=1, source_target_pairs={{1,3},{3,5},{5,7},{9,11},{11,13},{13,15},{17,19},{19,21},{21,23},{... | collective-permute-start | bytes 786440 | tf_op jit(solution)/shard_map/ppermute | solution.py:257
  52.2 16.3 %collective-permute-start.16 = (bf16[2176,128]{1,0:T(8,128)(2,1)}, bf16[2176,128]{1,0:T(8,128)(2,1)}, u32[]{:S(2)}, u32[]{:S(2)}) collective-permute-start(bf16[2176,128]{1,0:T(8,128)(2,1)} %get-tuple-element.66), channel_id=1, source_target_pairs={{5,7},{2,4},{3,6},{7,5},{4,2},{6,3},{13,15},{10,12},{11,14},{15,13... | collective-permute-start | bytes 1671176 | tf_op jit(solution)/shard_map/ppermute | solution.py:666
  59.0 20.2 %collective-permute-start.12 = (bf16[2176,128]{1,0:T(8,128)(2,1)}, bf16[2176,128]{1,0:T(8,128)(2,1)}, u32[]{:S(2)}, u32[]{:S(2)}) collective-permute-start(bf16[2176,128]{1,0:T(8,128)(2,1)} %get-tuple-element.62), channel_id=1, source_target_pairs={{5,7},{2,4},{3,6},{7,5},{4,2},{6,3},{13,15},{10,12},{11,14},{15,13... | collective-permute-start | bytes 1671176 | tf_op jit(solution)/shard_map/ppermute | solution.py:666
  61.1 7.4 %collective-permute-start.15 = (bf16[2,128,1024]{2,1,0:T(8,128)(2,1)}, bf16[2,128,1024]{2,1,0:T(8,128)(2,1)}, u32[]{:S(2)}, u32[]{:S(2)}) collective-permute-start(bf16[2,128,1024]{2,1,0:T(8,128)(2,1)} %collective-permute-done.14.refs_5_), channel_id=1, source_target_pairs={{0,1},{1,0},{2,3},{3,2},{4,5},{5,4},{6,7},{7,6},{8,9},{9,8},{10,11... | collective-permute-start | bytes 1572872 | tf_op jit(solution)/shard_map/ppermute | solution.py:615
  63.9 11.5 %collective-permute-start.11 = (bf16[2,128,1024]{2,1,0:T(8,128)(2,1)}, bf16[2,128,1024]{2,1,0:T(8,128)(2,1)}, u32[]{:S(2)}, u32[]{:S(2)}) collective-permute-start(bf16[2,128,1024]{2,1,0:T(8,128)(2,1)} %get-tuple-element.63), channel_id=1, source_target_pairs={{0,2},{1,3},{8,10},{9,11},{16,18},{17,19},{24,26},{25,27}} | collective-permute-start | bytes 1572872 | tf_op jit(solution)/shard_map/ppermute | solution.py:596
  67.2 16.7 %collective-permute-start.19 = (f32[512,128]{1,0:T(8,128)}, f32[512,128]{1,0:T(8,128)}, u32[]{:S(2)}, u32[]{:S(2)}) collective-permute-start(f32[512,128]{1,0:T(8,128)} %multiply_add_fusion.1), channel_id=1, source_target_pairs={{1,5},{3,7},{9,13},{11,15},{17,21},{19,23},{25,29},{27,31}} | collective-permute-start | bytes 786440 | tf_op jit(solution)/shard_map/ppermute | solution.py:257
  73.3 17.2 %collective-permute-start.21 = (bf16[2176,128]{1,0:T(8,128)(2,1)}, bf16[2176,128]{1,0:T(8,128)(2,1)}, u32[]{:S(2)}, u32[]{:S(2)}) collective-permute-start(bf16[2176,128]{1,0:T(8,128)(2,1)} %get-tuple-element.73), channel_id=1, source_target_pairs={{5,7},{2,4},{3,6},{13,15},{10,12},{11,14},{21,23},{18,20},{19,22},... | collective-permute-start | bytes 1671176 | tf_op jit(solution)/shard_map/ppermute | solution.py:666
  79.2 6.5 %collective-permute-start.13 = (bf16[2,128,1024]{2,1,0:T(8,128)(2,1)}, bf16[2,128,1024]{2,1,0:T(8,128)(2,1)}, u32[]{:S(2)}, u32[]{:S(2)}) collective-permute-start(bf16[2,128,1024]{2,1,0:T(8,128)(2,1)} %collective-permute-done.11.refs_5_), channel_id=1, source_target_pairs={{0,1},{1,0},{2,3},{3,2},{4,5},{5,4},{6,7},{7,6},{8,9},{9,8},{10,11... | collective-permute-start | bytes 1572872 | tf_op jit(solution)/shard_map/ppermute | solution.py:615
  85.7 4.7 %collective-permute-start.20 = (f32[512,128]{1,0:T(8,128)}, f32[512,128]{1,0:T(8,128)}, u32[]{:S(2)}, u32[]{:S(2)}) collective-permute-start(f32[512,128]{1,0:T(8,128)} %multiply_add_fusion.enter_ref), channel_id=1, source_target_pairs={{0,1},{1,0},{2,3},{3,2},{4,5},{5,4},{6,7},{7,6},{8,9},{9,8},{10,11... | collective-permute-start | bytes 786440 | tf_op jit(solution)/shard_map/ppermute | solution.py:265
  90.5 20.0 %collective-permute-start.25 = (bf16[2176,128]{1,0:T(8,128)(2,1)}, bf16[2176,128]{1,0:T(8,128)(2,1)}, u32[]{:S(2)}, u32[]{:S(2)}) collective-permute-start(bf16[2176,128]{1,0:T(8,128)(2,1)} %collective-permute-done.16.refs_7_.refs_0_), channel_id=1, source_target_pairs={{0,1},{1,0},{2,3},{3,2},{4,5},{5,4},{6,7},{7,6},{8,9},{9,8},{10,11... | collective-permute-start | bytes 1671176 | tf_op jit(solution)/shard_map/ppermute | solution.py:679
  95.7 17.5 %collective-permute-start.24 = (bf16[2176,128]{1,0:T(8,128)(2,1)}, bf16[2176,128]{1,0:T(8,128)(2,1)}, u32[]{:S(2)}, u32[]{:S(2)}) collective-permute-start(bf16[2176,128]{1,0:T(8,128)(2,1)} %collective-permute-done.12.refs_7_.refs_0_), channel_id=1, source_target_pairs={{0,1},{1,0},{2,3},{3,2},{4,5},{5,4},{6,7},{7,6},{8,9},{9,8},{10,11... | collective-permute-start | bytes 1671176 | tf_op jit(solution)/shard_map/ppermute | solution.py:679
  95.7 20.1 %collective-permute-start.23 = (bf16[2176,128]{1,0:T(8,128)(2,1)}, bf16[2176,128]{1,0:T(8,128)(2,1)}, u32[]{:S(2)}, u32[]{:S(2)}) collective-permute-start(bf16[2176,128]{1,0:T(8,128)(2,1)} %collective-permute-done.21.refs_0_), channel_id=1, source_target_pairs={{0,1},{1,0},{2,3},{3,2},{4,5},{5,4},{6,7},{7,6},{8,9},{9,8},{10,11... | collective-permute-start | bytes 1671176 | tf_op jit(solution)/shard_map/ppermute | solution.py:679
  96.2 22.3 %collective-permute-start.22 = (bf16[2176,128]{1,0:T(8,128)(2,1)}, bf16[2176,128]{1,0:T(8,128)(2,1)}, u32[]{:S(2)}, u32[]{:S(2)}) collective-permute-start(bf16[2176,128]{1,0:T(8,128)(2,1)} %get-tuple-element.75), channel_id=1, source_target_pairs={{5,7},{2,4},{3,6},{13,15},{10,12},{11,14},{21,23},{18,20},{19,22},... | collective-permute-start | bytes 1671176 | tf_op jit(solution)/shard_map/ppermute | solution.py:666
  118.5 2.4 %collective-permute-start.26 = (bf16[2176,128]{1,0:T(8,128)(2,1)}, bf16[2176,128]{1,0:T(8,128)(2,1)}, u32[]{:S(2)}, u32[]{:S(2)}) collective-permute-start(bf16[2176,128]{1,0:T(8,128)(2,1)} %collective-permute-done.22.refs_0_), channel_id=1, source_target_pairs={{0,1},{1,0},{2,3},{3,2},{4,5},{5,4},{6,7},{7,6},{8,9},{9,8},{10,11... | collective-permute-start | bytes 1671176 | tf_op jit(solution)/shard_map/ppermute | solution.py:679
